TPU v7x, 32 devices: a whole 2x2x4 slice. The times are simulated.
32 devices in a mesh: groups: 2 (over x), tensor: 8 (over z, y), dp: 2 (over core).
Axes of the slice: x: 2, y: 2, z: 4, core: 2. Of those that a mesh axis runs over, the one named last changes fastest.
Arguments:
- attention_result: bfloat16 [4, 768, 8192], P(None, ('groups', 'dp'), 'tensor'), parts along dimension 1, may hold values from -6 to 6
- tenant: int32 [768], P(('groups', 'dp')), parts along dimension 0, may hold values from 0 to 127, as said below
- projection_weight: bfloat16 [8192, 8192], P('tensor'), may hold values from -0.0625 to 0.0625
- adapter_down_maps: bfloat16 [256, 64, 8192], P(('groups', 'dp'), None, 'tensor'), parts along dimension 0, may hold values from -0.0625 to 0.0625
- adapter_up_maps: bfloat16 [256, 64, 8192], P(('groups', 'dp'), None, 'tensor'), parts along dimension 0, may hold values from -0.75 to 0.75
Outputs:
- projected: bfloat16 [4, 768, 8192], P(None, ('groups', 'dp'), 'tensor'), parts along dimension 1
There are 2 independent parts, one for each index of `groups`. A program takes and returns all parts, laid end to end along the dimension named above; an argument that names none is the same for every part. Nothing has to cross between parts.
Inputs may be any that keep to these rules, and one draw needn't show every extreme that they name: `tenant`: among the rows of one device (aligned blocks of 192 rows), at most 16 distinct adapters come from each owner's range of 64 consecutive ids; the first block names exactly 16 from every owner's range.
All inputs are finite; a program needn't handle non-finite values.
Results may differ from a plain program's by a relative error of at most 0.014.
Values may be sent and summed in bfloat16 or wider, within the bound.
No kernel may reach another device: no remote copies, remote signals or barrier semaphores. Data moves between devices by JAX's collectives and lax.ppermute only.
A program may use at most 128 MiB of HBM per device.

v0:
```python
import jax
import jax.numpy as jnp
from jax import lax
from jax.sharding import PartitionSpec as P

SLOTS = 16


def on_device(attention_result, tenant, projection_weight, adapter_down_maps, adapter_up_maps):
    decode_step_count, count_of_rows, shard_width = attention_result.shape
    local_tally = adapter_down_maps.shape[0]
    owners = lax.axis_size("dp")
    my_index = lax.axis_index("dp")
    total_adapters = local_tally * owners
    adapter_ids = jnp.arange(total_adapters, dtype=jnp.int32)
    tenants_all = lax.all_gather(tenant, "dp", axis=0, tiled=True)
    flat_rows = attention_result.reshape(decode_step_count * count_of_rows, shard_width)
    partial_value = jnp.dot(flat_rows, projection_weight, preferred_element_type=jnp.float32)
    base_projected = lax.psum_scatter(
        partial_value.astype(jnp.bfloat16), "tensor", scatter_dimension=1, tiled=True
    ).astype(jnp.float32)
    base_projected = base_projected.reshape(decode_step_count, count_of_rows, shard_width)
    hit_table = (
        tenants_all.reshape(owners, count_of_rows)[:, :, None] == adapter_ids[None, None, :]
    ).astype(jnp.int32)
    used_table = jnp.max(hit_table, axis=1).reshape(owners, owners, local_tally)
    slot_table = jnp.cumsum(used_table, axis=-1) - 1
    used_mine = lax.dynamic_index_in_dim(used_table, my_index, 1, keepdims=False)
    slot_mine = lax.dynamic_index_in_dim(slot_table, my_index, 1, keepdims=False)
    slot_range = jnp.arange(SLOTS, dtype=jnp.int32)
    adapter_picker = (used_mine[:, None, :] == 1) & (
        slot_mine[:, None, :] == slot_range[None, :, None]
    )
    adapter_picker = adapter_picker.astype(jnp.bfloat16)
    send_down = jnp.einsum(
        "xfo,ogi->xfgi", adapter_picker, adapter_down_maps, preferred_element_type=jnp.float32
    ).astype(jnp.bfloat16)
    send_up = jnp.einsum(
        "xfo,ogi->xfgi", adapter_picker, adapter_up_maps, preferred_element_type=jnp.float32
    ).astype(jnp.bfloat16)
    got_down, got_up = (
        lax.all_to_all(send_down, "dp", split_axis=0, concat_axis=0, tiled=True),
        lax.all_to_all(send_up, "dp", split_axis=0, concat_axis=0, tiled=True),
    )
    row_hot = (
        (tenant[:, None] == adapter_ids[None, :])
        .astype(jnp.int32)
        .reshape(count_of_rows, owners, local_tally)
    )
    own_used = jnp.max(row_hot, axis=0)
    own_slot = jnp.cumsum(own_used, axis=-1) - 1
    slot_hot = (
        (own_slot[:, :, None] == slot_range[None, None, :]) & (own_used[:, :, None] == 1)
    ).astype(jnp.float32)
    row_pick = jnp.einsum(
        "roa,oas->ros", row_hot.astype(jnp.float32), slot_hot, precision=lax.Precision.HIGHEST
    )
    scores = jnp.einsum(
        "trk,psnk->trpsn", attention_result, got_down, preferred_element_type=jnp.float32
    )
    low_part = jnp.sum(scores * row_pick[None, :, :, :, None], axis=(2, 3))
    low_rank = lax.psum(low_part.astype(jnp.bfloat16), "tensor")
    pick_bf = row_pick.astype(jnp.bfloat16)
    low_select = pick_bf[None, :, :, :, None] * low_rank[:, :, None, None, :]
    adapter_correction = jnp.einsum(
        "trpsn,psnk->trk", low_select, got_up, preferred_element_type=jnp.float32
    )
    return (base_projected + adapter_correction).astype(jnp.bfloat16)


def solution(mesh):
    placed = (
        P(None, ("groups", "dp"), "tensor"),
        P(("groups", "dp")),
        P("tensor", None),
        P(("groups", "dp"), None, "tensor"),
        P(("groups", "dp"), None, "tensor"),
    )
    return jax.shard_map(
        on_device,
        mesh=mesh,
        in_specs=placed,
        out_specs=P(None, ("groups", "dp"), "tensor"),
        check_vma=False,
    )
```

profile of v0, /device:TPU:0, one launch (start us, length us, event | category | flops | bytes accessed | tf_op | source)
XLA Modules:
  0.0 352.6 jit_solution(15821347649234854091)
XLA Ops:
  6.5 0.0 copy-start
  6.5 1.4 dynamic-slice
  8.6 0.9 dynamic-update-slice
  9.4 1.9 all-reduce
  11.4 0.1 eq.91
  11.4 0.1 convert_reduce_fusion
  11.6 0.1 reshape.46
  11.7 0.5 reduce_window_sum.23
  12.2 15.3 %fusion.13 = bf16[2,16,64,1024]{3,1,2,0:T(8,128)(2,1)} fusion(bf16[64,64,1024]{2,1,0:T(8,128)(2,1)} %param.8, s32[2,64]{1,0:T(2,128)S(1)} %bitcast.47, pred[2,64]{1,0:T(4,128)(4,1)S(1)} %bitcast.49), kind=kOutput, calls=%fused_computation.16 | convolution fusion | flops 270536704 | bytes 12583552 | tf_op jit(solution)/shard_map/xfo,ogi->xfgi/dot_general | solution.py:35
  27.5 0.0 copy-start.2
  27.5 5.7 %all-to-all-start = ((bf16[2,16,64,1024]{3,1,2,0:T(8,128)(2,1)}), bf16[2,16,64,1024]{3,1,2,0:T(8,128)(2,1)}, u32[]{:S(2)}, u32[]{:S(2)}) async-start(bf16[2,16,64,1024]{3,1,2,0:T(8,128)(2,1)} %fusion.13), calls=%async_computation.1 | async-start | bytes 8388608 | tf_op jit(solution)/shard_map/all_to_all | solution.py:42
  33.3 0.2 all-reduce.3.cloned.1.call-start
  33.5 0.0 copy-done.2
  33.5 0.2 convert_reduce_fusion.1
  33.7 0.2 reduce_window_sum.22
  34.0 0.2 fusion.42
  34.2 3.5 %all-to-all-done = bf16[2,16,64,1024]{3,1,2,0:T(8,128)(2,1)} async-done(((bf16[2,16,64,1024]{3,1,2,0:T(8,128)(2,1)}), bf16[2,16,64,1024]{3,1,2,0:T(8,128)(2,1)}, u32[]{:S(2)}, u32[]{:S(2)}) %all-to-all-start) | async-done | bytes 4194336 | tf_op jit(solution)/shard_map/all_to_all | solution.py:42
  37.8 0.0 copy-done
  37.8 10.4 %fusion.2 = bf16[4,192,64]{1,2,0:T(8,128)(2,1)} fusion(f32[192,2,16]{0,2,1:T(8,128)S(1)} %get-tuple-element.6, bf16[2,16,64,1024,1]{3,1,2,0,4:T(8,128)(2,1)} %bitcast.8, bf16[4,192,1024]{2,1,0:T(8,128)(2,1)S(1)} %copy-done), kind=kOutput, calls=%fused_computation.4 | convolution fusion | flops 3224322048 | bytes 5890048 | tf_op jit(solution)/shard_map/trk,psnk->trpsn/dot_general | solution.py:58
  48.2 0.0 all-reduce.3.cloned.1.call-update
  48.2 0.0 reduce-scatter.2.cloned.1.call-start
  48.3 21.2 %convolution_convert_fusion = bf16[768,8192]{1,0:T(8,128)(2,1)} fusion(bf16[768,1024]{1,0:T(8,128)(2,1)S(1)} %bitcast.45, bf16[1024,8192]{1,0:T(8,128)(2,1)} %param.7), kind=kOutput, calls=%fused_computation | convolution fusion | flops 12891193344 | bytes 30932992 | tf_op jit(solution)/shard_map/dot_general | solution.py:18
  69.5 0.0 reduce-scatter.2.cloned.1.call-update
  69.5 13.4 %fusion.16 = bf16[2,16,64,1024]{3,1,2,0:T(8,128)(2,1)S(1)} fusion(bf16[64,64,1024]{2,1,0:T(8,128)(2,1)} %param.9, s32[2,64]{1,0:T(2,128)S(1)} %bitcast.48, pred[2,64]{1,0:T(4,128)(4,1)S(1)} %bitcast.50), kind=kOutput, calls=%fused_computation.17 | convolution fusion | flops 270536704 | bytes 12583552 | tf_op jit(solution)/shard_map/xfo,ogi->xfgi/dot_general | solution.py:38
  82.9 8.2 %all_to_all.10 = bf16[2,16,64,1024]{3,1,2,0:T(8,128)(2,1)} all-to-all(bf16[2,16,64,1024]{3,1,2,0:T(8,128)(2,1)S(1)} %fusion.16), channel_id=1, replica_groups=mesh['groups'=2,'tensor'=8,'dp'=2] {'dp'}, dimensions={0} | all-to-all | bytes 8388608 | tf_op jit(solution)/shard_map/all_to_all | solution.py:43
  91.1 29.6 %all-reduce.3.cloned.1.call-done = bf16[4,192,64]{1,2,0:T(8,128)(2,1)} async-done(((bf16[4,192,64]{1,2,0:T(8,128)(2,1)}), bf16[4,192,64]{1,2,0:T(8,128)(2,1)}) %all-reduce.3.cloned.1.call-update) | async-done | bytes 98320 | tf_op jit(solution)/shard_map/psum | solution.py:62
  120.6 211.0 %reduce-scatter.2.cloned.1.call-done = bf16[768,1024]{1,0:T(8,128)(2,1)} async-done(((bf16[768,8192]{1,0:T(8,128)(2,1)}), bf16[768,1024]{1,0:T(8,128)(2,1)}) %reduce-scatter.2.cloned.1.call-update) | async-done | bytes 1572880 | tf_op jit(solution)/shard_map/reduce_scatter | solution.py:19
  331.7 0.0 copy-start.1
  331.7 14.1 %fusion.12 = bf16[4,192,1024]{2,1,0:T(8,128)(2,1)} fusion(bf16[4,192,1024]{2,1,0:T(8,128)(2,1)} %bitcast.51, bf16[2,16,64,1024,1]{3,1,2,0,4:T(8,128)(2,1)} %bitcast.46, bf16[4,192,64]{1,2,0:T(8,128)(2,1)} %all-reduce.3.cloned.1.call-done, bf16[192,2,16]{0,2,1:T(8,128)(2,1)S(1)} %get-tuple-element.5), kind=kOutput, calls=%fused_computation.15 | convolution fusion | flops 3225157632 | bytes 7450624 | tf_op jit(solution)/shard_map/trpsn,psnk->trk/dot_general | solution.py:65
  345.7 0.0 copy-done.1
  (7 shorter events, 0.0 us)
Async XLA Ops:
  6.5 31.2 %copy-start = (bf16[4,192,1024]{2,1,0:T(8,128)(2,1)S(1)}, bf16[4,192,1024]{2,1,0:T(8,128)(2,1)}, u32[]{:S(2)}) copy-start(bf16[4,192,1024]{2,1,0:T(8,128)(2,1)} %param.5) | copy-start | bytes 4718596
  27.5 6.0 %copy-start.2 = (s32[192]{0:T(256)S(1)}, s32[192]{0:T(256)}, u32[]{:S(2)}) copy-start(s32[192]{0:T(256)} %param.6) | copy-start | bytes 2308
  27.5 10.2 %all-to-all-start = ((bf16[2,16,64,1024]{3,1,2,0:T(8,128)(2,1)}), bf16[2,16,64,1024]{3,1,2,0:T(8,128)(2,1)}, u32[]{:S(2)}, u32[]{:S(2)}) async-start(bf16[2,16,64,1024]{3,1,2,0:T(8,128)(2,1)} %fusion.13), calls=%async_computation.1 | async-start | bytes 8388608 | tf_op jit(solution)/shard_map/all_to_all | solution.py:42
  33.3 87.3 %all-reduce.3.cloned.1.call-start = ((), (), s32[]{:S(2)}) async-start(), calls=%async_computation.4 | async-start | bytes 262144 | tf_op jit(solution)/shard_map/psum | solution.py:62
  48.2 283.4 %reduce-scatter.2.cloned.1.call-start = ((), (), s32[]{:S(2)}) async-start(), calls=%async_computation.3 | async-start | bytes 14155776 | tf_op jit(solution)/shard_map/reduce_scatter | solution.py:19
  331.7 14.1 %copy-start.1 = (bf16[4,192,1024]{2,1,0:T(8,128)(2,1)S(1)}, bf16[4,192,1024]{2,1,0:T(8,128)(2,1)}, u32[]{:S(2)}) copy-start(bf16[4,192,1024]{2,1,0:T(8,128)(2,1)} %param.5) | copy-start | bytes 4718596
Sparse Core Ops, SparseCore 0:
  48.3 72.2 all-reduce.2
  124.7 206.9 reduce-scatter.1
where the time goes:
time: 353 us
  waiting for transfers between devices  244 us (69%)
  matrix products  74.6 us (21%)
  between operations  14.1 us (4%)
  blocking collectives  10.1 us (3%)
  starting transfers between devices  6.01 us (2%)
    reduce_scatter x1, waiting for transfers between devices, on_device(): lax.psum_scatter(partial_value.astype(jnp.bfloat16), 'tensor', scatter_di...  211 us
    psum x1, waiting for transfers between devices, on_device(): low_rank = lax.psum(low_part.astype(jnp.bfloat16), 'tensor')  29.6 us
    dot_general x1, matrix products, on_device(): jnp.dot(flat_rows, projection_weight, preferred_element_type=jnp.float32)  21.2 us
    dot_general x1, matrix products, on_device(): jnp.einsum('xfo,ogi->xfgi', adapter_picker, adapter_down_maps, preferred_...  15.3 us
    dot_general x1, matrix products, on_device(): jnp.einsum('trpsn,psnk->trk', low_select, got_up, preferred_element_type=...  14.1 us
    dot_general x1, matrix products, on_device(): jnp.einsum('xfo,ogi->xfgi', adapter_picker, adapter_up_maps, preferred_el...  13.4 us
    dot_general x1, matrix products, on_device(): jnp.einsum('trk,psnk->trpsn', attention_result, got_down, preferred_eleme...  10.4 us
    all_to_all x1, blocking collectives, on_device(): lax.all_to_all(send_up, 'dp', split_axis=0, concat_axis=0, tiled=True)  8.18 us
  transfers between devices with their start and end apart: 3, of which 3 were waited for; matrix products, arithmetic and copies ran while one was open for 10% of the time, Pallas kernels for 0%

commit v1 on v0

v1 whole, which is shorter than its diff:
```python
import jax
import jax.numpy as jnp
import numpy as np
from jax import lax
from jax.experimental import pallas as pl
from jax.experimental.pallas import tpu as pltpu
from jax.sharding import PartitionSpec as P

SLOTS = 16
GROUP = 4


def copy_blocks(index, down, up):
    count = index.shape[0]

    def kernel(index_ref, down_ref, up_ref, down_out, up_out, sems):
        copies = []
        for s in range(count):
            for m, (src, dst) in enumerate(((down_ref, down_out), (up_ref, up_out))):
                copies.append(
                    pltpu.make_async_copy(src.at[index_ref[s]], dst.at[s], sems.at[m, s])
                )
        for copy in copies:
            copy.start()
        for copy in copies:
            copy.wait()

    shape = jax.ShapeDtypeStruct((count,) + down.shape[1:], down.dtype)
    return pl.pallas_call(
        kernel,
        out_shape=(shape, shape),
        in_specs=[
            pl.BlockSpec(memory_space=pltpu.SMEM),
            pl.BlockSpec(memory_space=pl.ANY),
            pl.BlockSpec(memory_space=pl.ANY),
        ],
        out_specs=(pl.BlockSpec(memory_space=pl.ANY), pl.BlockSpec(memory_space=pl.ANY)),
        scratch_shapes=[pltpu.SemaphoreType.DMA((2, count))],
        cost_estimate=pl.CostEstimate(
            flops=0, transcendentals=0, bytes_accessed=4 * count * down[0].size * 2
        ),
        name="copy_blocks",
    )(index, down, up)


def low_rank(rows, slot, maps):
    count, width = rows.shape
    rank = maps.shape[1]
    wide = GROUP * rank
    steps = maps.shape[0] // GROUP
    flat = maps.reshape(maps.shape[0] * rank, width)

    def kernel(rows_ref, slot_ref, maps_ref, out_ref, acc):
        i = pl.program_id(0)

        @pl.when(i == 0)
        def _():
            acc[...] = jnp.zeros_like(acc)

        scores = lax.dot_general(
            rows_ref[...], maps_ref[...], (((1,), (1,)), ((), ())),
            preferred_element_type=jnp.float32,
        )
        lane_slot = lax.broadcasted_iota(jnp.int32, (count, wide), 1) // rank + i * GROUP
        acc[...] += jnp.where(slot_ref[...] == lane_slot, scores, 0.0)

        @pl.when(i == steps - 1)
        def _():
            total = acc[:, 0:rank]
            for g in range(1, GROUP):
                total += acc[:, g * rank : (g + 1) * rank]
            out_ref[...] = total.astype(out_ref.dtype)

    return pl.pallas_call(
        kernel,
        grid=(steps,),
        out_shape=jax.ShapeDtypeStruct((count, rank), jnp.bfloat16),
        in_specs=[
            pl.BlockSpec((count, width), lambda i: (0, 0)),
            pl.BlockSpec((count, 1), lambda i: (0, 0)),
            pl.BlockSpec((wide, width), lambda i: (i, 0)),
        ],
        out_specs=pl.BlockSpec((count, rank), lambda i: (0, 0)),
        scratch_shapes=[pltpu.VMEM((count, wide), jnp.float32)],
        compiler_params=pltpu.CompilerParams(vmem_limit_bytes=32 * 2**20),
        cost_estimate=pl.CostEstimate(
            flops=2 * count * width * flat.shape[0],
            transcendentals=0,
            bytes_accessed=2 * (flat.size + rows.size),
        ),
        name="low_rank",
    )(rows, slot, flat)


def expand(low, slot, maps):
    count, rank = low.shape
    width = maps.shape[2]
    wide = GROUP * rank
    steps = maps.shape[0] // GROUP
    flat = maps.reshape(maps.shape[0] * rank, width)

    def kernel(low_ref, slot_ref, maps_ref, out_ref):
        i = pl.program_id(0)
        tiled = jnp.concatenate([low_ref[...]] * GROUP, axis=1)
        lane_slot = lax.broadcasted_iota(jnp.int32, (count, wide), 1) // rank + i * GROUP
        picked = jnp.where(slot_ref[...] == lane_slot, tiled, jnp.zeros_like(tiled))
        term = jnp.dot(picked, maps_ref[...], preferred_element_type=jnp.float32)

        @pl.when(i == 0)
        def _():
            out_ref[...] = term

        @pl.when(i > 0)
        def _():
            out_ref[...] += term

    return pl.pallas_call(
        kernel,
        grid=(steps,),
        out_shape=jax.ShapeDtypeStruct((count, width), jnp.float32),
        in_specs=[
            pl.BlockSpec((count, rank), lambda i: (0, 0)),
            pl.BlockSpec((count, 1), lambda i: (0, 0)),
            pl.BlockSpec((wide, width), lambda i: (i, 0)),
        ],
        out_specs=pl.BlockSpec((count, width), lambda i: (0, 0)),
        compiler_params=pltpu.CompilerParams(vmem_limit_bytes=32 * 2**20),
        cost_estimate=pl.CostEstimate(
            flops=2 * count * width * flat.shape[0],
            transcendentals=0,
            bytes_accessed=2 * flat.size + 4 * count * width,
        ),
        name="expand",
    )(low, slot, flat)


def line_plan(nz):
    order = np.zeros((nz, nz), np.int32)
    for z in range(nz):
        def need(j):
            if j == z:
                return (2 * nz, 0)
            return (nz - 1 - j + z, j) if j > z else (nz - 1 - z + j, nz - j)

        order[z] = sorted(range(nz), key=need)
    return order


def on_device(attention_result, tenant, projection_weight, adapter_down_maps, adapter_up_maps):
    steps, row_count, width = attention_result.shape
    local_adapters = adapter_down_maps.shape[0]
    owners = lax.axis_size("dp")
    me = lax.axis_index("dp")
    n = lax.axis_size("tensor")
    nz = n // 2
    place = lax.axis_index("tensor")
    z, y = place // 2, place % 2
    order = line_plan(nz)
    my_order = jnp.asarray(order)[z]
    out_width = projection_weight.shape[1] // n

    def swap_y(value):
        return lax.ppermute(value, "tensor", [(t, t ^ 1) for t in range(n)])

    def hop(value, h):
        pairs = []
        for side in range(2):
            pairs.append((h * 2 + side, (h + 1) * 2 + side))
            pairs.append(((nz - 1 - h) * 2 + side, (nz - 2 - h) * 2 + side))
        return lax.ppermute(value, "tensor", pairs)

    def slot_of(h, m):
        return list(order[h]).index(nz - 1 - m)

    def line_sum(blocks):
        arrived = {}
        for when in range(2 * nz - 3):
            for h in range(nz - 1):
                m = when - h
                if 0 <= m < nz - 1 - h:
                    value = blocks[slot_of(h, m)]
                    if h:
                        value = value.astype(jnp.float32) + arrived[h - 1, m].astype(jnp.float32)
                    arrived[h, m] = hop(value.astype(jnp.bfloat16), h)
        return [arrived[h, nz - 2 - h] for h in range(nz - 1)]

    rows = attention_result.reshape(steps * row_count, width)
    total_rows = steps * row_count
    first = total_rows // 6
    rows_a, rows_b = rows[:first], rows[first:]

    def weight_block(start, size):
        return lax.dynamic_slice(projection_weight, (0, start), (width, size))

    def dot(left, right):
        return jnp.dot(left, right, preferred_element_type=jnp.float32)

    sent_y = []
    for k in range(nz):
        partial = dot(rows_b, weight_block((my_order[k] * 2 + 1 - y) * out_width, out_width))
        sent_y.append(swap_y(partial.astype(jnp.bfloat16)))
    blocks_a = []
    for k in range(nz):
        blocks_a.append(dot(rows_a, weight_block(my_order[k] * 2 * out_width, 2 * out_width)))
        if k < nz - 1:
            blocks_a[k] = blocks_a[k].astype(jnp.bfloat16)
    arrived_a = line_sum(blocks_a)
    blocks_b = []
    for k in range(nz):
        partial = dot(rows_b, weight_block((my_order[k] * 2 + y) * out_width, out_width))
        partial = partial + sent_y[k].astype(jnp.float32)
        blocks_b.append(partial.astype(jnp.bfloat16) if k < nz - 1 else partial)
    arrived_b = line_sum(blocks_b)

    sum_a = blocks_a[nz - 1]
    for value in arrived_a:
        sum_a = sum_a + value.astype(jnp.float32)
    sum_a = sum_a.astype(jnp.bfloat16)
    away_a = lax.dynamic_slice(sum_a, (0, (1 - y) * out_width), (first, out_width))
    kept_a = lax.dynamic_slice(sum_a, (0, y * out_width), (first, out_width))
    other_a = swap_y(away_a)

    slot_range = jnp.arange(SLOTS, dtype=jnp.int32)
    ids = jnp.arange(local_adapters, dtype=jnp.int32)

    def slots(row_ids, owner):
        hit = row_ids[:, None] - owner * local_adapters == ids[None, :]
        used = jnp.any(hit, axis=0)
        position = jnp.sum(
            (used[None, :] & (ids[None, :] < ids[:, None])).astype(jnp.int32), axis=1
        )
        names = jnp.sum(
            jnp.where(used[None, :] & (position[None, :] == slot_range[:, None]), ids[None, :], 0),
            axis=1,
        )
        row_slot = jnp.sum(jnp.where(hit, position[None, :] + 1, 0), axis=1) - 1
        return names, row_slot

    downs, ups, row_slots = [], [], []
    for shift in range(owners):
        if shift == 0:
            names, row_slot = slots(tenant, me)
            down, up = copy_blocks(names, adapter_down_maps, adapter_up_maps)
        else:
            theirs = lax.ppermute(
                tenant, "dp", [(i, (i - shift) % owners) for i in range(owners)]
            )
            names, _ = slots(theirs, me)
            down, up = copy_blocks(names, adapter_down_maps, adapter_up_maps)
            onward = [(i, (i + shift) % owners) for i in range(owners)]
            down, up = lax.ppermute(down, "dp", onward), lax.ppermute(up, "dp", onward)
            _, row_slot = slots(tenant, (me - shift) % owners)
        downs.append(down)
        ups.append(up)
        row_slots.append(jnp.tile(row_slot, steps)[:, None])

    low = low_rank(rows, row_slots[0], downs[0]).astype(jnp.float32)
    for s in range(1, owners):
        low = low + low_rank(rows, row_slots[s], downs[s]).astype(jnp.float32)
    rank = low.shape[1]
    low = low.astype(jnp.bfloat16).reshape(total_rows * rank // 128, 128)
    bit = 1
    while bit < n:
        other = lax.ppermute(low, "tensor", [(t, t ^ bit) for t in range(n)])
        low = (low.astype(jnp.float32) + other.astype(jnp.float32)).astype(jnp.bfloat16)
        bit *= 2
    low = low.reshape(total_rows, rank)
    delta = expand(low, row_slots[0], ups[0])
    for s in range(1, owners):
        delta = delta + expand(low, row_slots[s], ups[s])

    head_b = lax.optimization_barrier(blocks_b[nz - 1] + delta[first:])
    out_b = head_b
    for value in arrived_b:
        out_b = out_b + value.astype(jnp.float32)
    out_a = kept_a.astype(jnp.float32) + other_a.astype(jnp.float32) + delta[:first]
    out = jnp.concatenate([out_a.astype(jnp.bfloat16), out_b.astype(jnp.bfloat16)], axis=0)
    return out.reshape(steps, row_count, out_width)


def solution(mesh):
    placed = (
        P(None, ("groups", "dp"), "tensor"),
        P(("groups", "dp")),
        P("tensor", None),
        P(("groups", "dp"), None, "tensor"),
        P(("groups", "dp"), None, "tensor"),
    )
    return jax.shard_map(
        on_device,
        mesh=mesh,
        in_specs=placed,
        out_specs=P(None, ("groups", "dp"), "tensor"),
        check_vma=False,
    )
```

time: 353 us -> 472 us (1.34)
  Pallas kernels: 0 us -> 272 us
  waiting for transfers between devices: 244 us -> 77.4 us
  starting transfers between devices: 6.01 us -> 40.5 us
  matrix products: 74.6 us -> 48.1 us
  other arithmetic: 1.07 us -> 22.1 us
  blocking collectives: 10.1 us -> 0 us
  between operations: 14.1 us -> 5.68 us
    pallas_call x0 -> x6, Pallas kernels: none -> 272 us  [the longest x2 258 us: copy_blocks(): pl.pallas_call(kernel, out_shape=(shape, shape), in_specs=[pl.BlockSpec(m...]
    reduce_scatter x1 -> x0, waiting for transfers between devices: 211 us -> none  [on_device(): lax.psum_scatter(partial_value.astype(jnp.bfloat16), 'tensor', scatter_di...]
    ppermute x0 -> x23, waiting for transfers between devices: none -> 77.4 us  [the longest x3 52.6 us: on_device(): other = lax.ppermute(low, 'tensor', [(t, t ^ bit) for t in range(n)])]
    ppermute x0 -> x23, starting transfers between devices: none -> 40.5 us  [the longest x12 32.5 us: hop(): return lax.ppermute(value, 'tensor', pairs)]
    psum x1 -> x0, waiting for transfers between devices: 29.6 us -> none  [on_device(): low_rank = lax.psum(low_part.astype(jnp.bfloat16), 'tensor')]
    dot_general x6 -> x12, matrix products: 74.6 us -> 48.1 us  [dot(): return jnp.dot(left, right, preferred_element_type=jnp.float32)]
    convert_element_type x0 -> x13, other arithmetic: none -> 17.8 us  [the longest x6 12.1 us: line_sum(): arrived[h, m] = hop(value.astype(jnp.bfloat16), h)]
    all_to_all x1 -> x0, blocking collectives: 8.18 us -> none  [on_device(): lax.all_to_all(send_up, 'dp', split_axis=0, concat_axis=0, tiled=True)]
  transfers between devices with their start and end apart: 3 -> 23, of which waited for: 3 -> 5; matrix products, arithmetic and copies ran while one was open for 10% -> 15% of each run, Pallas kernels for 0% -> 58%
where the time goes in v1:
time: 472 us; the launch traced here: 471 us
  Pallas kernels  272 us (58%)
  waiting for transfers between devices  77.4 us (16%)
  matrix products  48.1 us (10%)
  starting transfers between devices  40.5 us (9%)
  other arithmetic  22.1 us (5%)
  between operations  5.68 us (1%)
  local copies, waits for them, and re-layouts  4.82 us (1%)
    pallas_call x2, Pallas kernels, copy_blocks(): pl.pallas_call(kernel, out_shape=(shape, shape), in_specs=[pl.BlockSpec(m...  258 us
    ppermute x3, waiting for transfers between devices, on_device(): other = lax.ppermute(low, 'tensor', [(t, t ^ bit) for t in range(n)])  52.6 us
    dot_general x12, matrix products, dot(): return jnp.dot(left, right, preferred_element_type=jnp.float32)  48.1 us
    ppermute x12, starting transfers between devices, hop(): return lax.ppermute(value, 'tensor', pairs)  32.5 us
    ppermute x12, waiting for transfers between devices, hop(): return lax.ppermute(value, 'tensor', pairs)  13.5 us
    convert_element_type x6, other arithmetic, line_sum(): arrived[h, m] = hop(value.astype(jnp.bfloat16), h)  12.1 us
    ppermute x5, waiting for transfers between devices, swap_y(): return lax.ppermute(value, 'tensor', [(t, t ^ 1) for t in range(n)])  11.3 us
  transfers between devices with their start and end apart: 23, of which 5 were waited for; matrix products, arithmetic and copies ran while one was open for 15% of the time, Pallas kernels for 58%

profile of v1, /device:TPU:0, one launch (start us, length us, event | category | flops | bytes accessed | tf_op | source)
XLA Modules:
  0.0 471.1 jit_solution(178371945679598182)
XLA Ops:
  2.5 3.1 fusion.23
  5.6 5.3 %collective-permute-start.3 = (bf16[128,2048]{1,0:T(8,128)(2,1)S(1)}, bf16[128,2048]{1,0:T(8,128)(2,1)}, u32[]{:S(2)}, u32[]{:S(2)}) collective-permute-start(bf16[128,2048]{1,0:T(8,128)(2,1)S(1)} %fusion.23), channel_id=1, source_target_pairs={{0,4},{12,8},{2,6},{14,10},{1,5},{13,9},{3,7},{15,11},{16,20},{28,... | collective-permute-start | bytes 1572872 | tf_op jit(solution)/shard_map/ppermute | solution.py:170
  11.4 3.7 fusion.26
  15.2 2.1 collective-permute-start.1
  17.9 3.7 fusion.29
  21.7 2.1 collective-permute-start
  24.4 4.2 fusion.68
  28.6 1.5 collective-permute-start.19
  34.2 3.9 fusion.11
  38.1 4.2 fusion.77
  42.4 4.2 fusion.74
  46.6 4.2 fusion.71
  50.8 129.1 %copy_blocks.2 = (bf16[16,64,1024]{2,1,0:T(8,128)(2,1)}, bf16[16,64,1024]{2,1,0:T(8,128)(2,1)}) custom-call(s32[16]{0:T(128)} %select_reduce_fusion.3.index_ref, bf16[64,64,1024]{2,1,0:T(8,128)(2,1)} %down_ref.3, bf16[64,64,1024]{2,1,0:T(8,128)(2,1)} %up_ref.3), custom_call_target="tpu_custom_call" | custom-call | bytes 8388608 | tf_op jit(solution)/shard_map/copy_blocks/pallas_call | solution.py:29
  180.0 1.6 copy-done.2
  181.5 2.8 low_rank.2
  186.1 129.1 %copy_blocks.3 = (bf16[16,64,1024]{2,1,0:T(8,128)(2,1)}, bf16[16,64,1024]{2,1,0:T(8,128)(2,1)}) custom-call(s32[16]{0:T(128)} %select_reduce_fusion.2.index_ref, bf16[64,64,1024]{2,1,0:T(8,128)(2,1)} %down_ref.3, bf16[64,64,1024]{2,1,0:T(8,128)(2,1)} %up_ref.3), custom_call_target="tpu_custom_call" | custom-call | bytes 8388608 | tf_op jit(solution)/shard_map/copy_blocks/pallas_call | solution.py:29
  315.4 1.3 add_convert_fusion.6
  317.3 2.1 add_convert_fusion.7
  319.5 1.5 collective-permute-start.16
  321.0 4.5 fusion.8
  325.5 7.3 %collective-permute-start.20 = (bf16[640,1024]{1,0:T(8,128)(2,1)}, bf16[640,1024]{1,0:T(8,128)(2,1)}, u32[]{:S(2)}, u32[]{:S(2)}) collective-permute-start(bf16[640,1024]{1,0:T(8,128)(2,1)} %fusion.8), channel_id=1, source_target_pairs={{0,4},{12,8},{2,6},{14,10},{1,5},{13,9},{3,7},{15,11},{16,20},{28,... | collective-permute-start | bytes 3932168 | tf_op jit(solution)/shard_map/ppermute | solution.py:170
  332.8 2.0 add_convert_fusion.5
  334.8 4.6 fusion.10
  339.3 11.3 %collective-permute-done.16 = bf16[640,1024]{1,0:T(8,128)(2,1)S(1)} collective-permute-done((bf16[640,1024]{1,0:T(8,128)(2,1)S(1)}, bf16[640,1024]{1,0:T(8,128)(2,1)S(1)}, u32[]{:S(2)}, u32[]{:S(2)}) %collective-permute-start.16) | collective-permute-done | bytes 1310752 | tf_op jit(solution)/shard_map/ppermute | solution.py:163
  350.6 1.5 collective-permute-start.2
  352.0 4.2 fusion.9
  356.2 1.3 collective-permute-start.5
  357.5 2.8 low_rank.3
  361.1 1.2 reshape.76
  362.3 5.4 %collective-permute-start.17 = (bf16[640,1024]{1,0:T(8,128)(2,1)}, bf16[640,1024]{1,0:T(8,128)(2,1)S(1)}, u32[]{:S(2)}, u32[]{:S(2)}) collective-permute-start(bf16[640,1024]{1,0:T(8,128)(2,1)} %fusion.9), channel_id=1, source_target_pairs={{0,4},{12,8},{2,6},{14,10},{1,5},{13,9},{3,7},{15,11},{16,20},{28,... | collective-permute-start | bytes 3932168 | tf_op jit(solution)/shard_map/ppermute | solution.py:170
  367.7 2.2 add_convert_fusion.2
  369.9 1.6 collective-permute-start.13
  372.8 1.6 add_convert_fusion.4
  374.5 27.6 %collective-permute-done.9 = bf16[384,128]{1,0:T(8,128)(2,1)S(1)} collective-permute-done((bf16[384,128]{1,0:T(8,128)(2,1)S(1)}, bf16[384,128]{1,0:T(8,128)(2,1)S(1)}, u32[]{:S(2)}, u32[]{:S(2)}) %collective-permute-start.9) | collective-permute-done | bytes 98336 | tf_op jit(solution)/shard_map/ppermute | solution.py:264
  402.2 4.6 collective-permute-done.10
  406.8 3.0 collective-permute-start.15
  410.0 1.6 add_convert_fusion.3
  411.6 1.7 collective-permute-start.18
  413.3 2.9 add_convert_fusion.1
  416.2 20.4 %collective-permute-done.11 = bf16[384,128]{1,0:T(8,128)(2,1)S(1)} collective-permute-done((bf16[384,128]{1,0:T(8,128)(2,1)S(1)}, bf16[384,128]{1,0:T(8,128)(2,1)S(1)}, u32[]{:S(2)}, u32[]{:S(2)}) %collective-permute-start.11) | collective-permute-done | bytes 98336 | tf_op jit(solution)/shard_map/ppermute | solution.py:264
  436.7 1.5 collective-permute-start.22
  438.3 1.6 collective-permute-start.6
  439.9 5.0 %expand.3 = f32[768,1024]{1,0:T(8,128)S(1)} custom-call(bf16[768,64]{1,0:T(8,128)(2,1)S(1)} %reshape.77.low_ref, s32[768,1]{1,0:T(8,128)S(1)} %broadcast_in_dim_tile.9.slot_ref, bf16[1024,1024]{1,0:T(8,128)(2,1)} %bitcast.12.maps_ref), custom_call_target="tpu_custom_call" | custom-call | flops 1610612736 | bytes 5242880 | tf_op jit(solution)/shard_map/expand/pallas_call | solution.py:117
  444.9 3.6 expand.2
  449.5 3.5 slice_add_fusion
  453.2 13.5 %collective-permute-done.22 = bf16[640,1024]{1,0:T(8,128)(2,1)} collective-permute-done((bf16[640,1024]{1,0:T(8,128)(2,1)}, bf16[640,1024]{1,0:T(8,128)(2,1)}, u32[]{:S(2)}, u32[]{:S(2)}) %collective-permute-start.22) | collective-permute-done | bytes 1310752 | tf_op jit(solution)/shard_map/ppermute | solution.py:170
  466.8 3.1 add_convert_fusion
  469.8 1.3 pad_maximum_fusion
  (73 shorter events, 9.3 us)
Async XLA Ops:
  0.0 184.7 %collective-permute-start.7 = (s32[192]{0:T(256)}, s32[192]{0:T(256)S(1)}, u32[]{:S(2)}, u32[]{:S(2)}) collective-permute-start(s32[192]{0:T(256)} %param.7), channel_id=1, source_target_pairs={{0,1},{1,0},{2,3},{3,2},{4,5},{5,4},{6,7},{7,6},{8,9},{9,8},{10,11... | collective-permute-start | bytes 2312 | tf_op jit(solution)/shard_map/ppermute | solution.py:245
  2.5 9.0 %copy-start = (bf16[4,192,1024]{2,1,0:T(8,128)(2,1)S(1)}, bf16[4,192,1024]{2,1,0:T(8,128)(2,1)}, u32[]{:S(2)}) copy-start(bf16[4,192,1024]{2,1,0:T(8,128)(2,1)} %param.6) | copy-start | bytes 4718596
  5.6 309.7 %collective-permute-start.3 = (bf16[128,2048]{1,0:T(8,128)(2,1)S(1)}, bf16[128,2048]{1,0:T(8,128)(2,1)}, u32[]{:S(2)}, u32[]{:S(2)}) collective-permute-start(bf16[128,2048]{1,0:T(8,128)(2,1)S(1)} %fusion.23), channel_id=1, source_target_pairs={{0,4},{12,8},{2,6},{14,10},{1,5},{13,9},{3,7},{15,11},{16,20},{28,... | collective-permute-start | bytes 1572872 | tf_op jit(solution)/shard_map/ppermute | solution.py:170
  15.2 301.4 %collective-permute-start.1 = (bf16[128,2048]{1,0:T(8,128)(2,1)}, bf16[128,2048]{1,0:T(8,128)(2,1)}, u32[]{:S(2)}, u32[]{:S(2)}) collective-permute-start(bf16[128,2048]{1,0:T(8,128)(2,1)} %fusion.26), channel_id=1, source_target_pairs={{0,4},{12,8},{2,6},{14,10},{1,5},{13,9},{3,7},{15,11},{16,20},{28,... | collective-permute-start | bytes 1572872 | tf_op jit(solution)/shard_map/ppermute | solution.py:170
  21.7 348.3 %collective-permute-start = (bf16[128,2048]{1,0:T(8,128)(2,1)}, bf16[128,2048]{1,0:T(8,128)(2,1)}, u32[]{:S(2)}, u32[]{:S(2)}) collective-permute-start(bf16[128,2048]{1,0:T(8,128)(2,1)} %fusion.29), channel_id=1, source_target_pairs={{0,4},{12,8},{2,6},{14,10},{1,5},{13,9},{3,7},{15,11},{16,20},{28,... | collective-permute-start | bytes 1572872 | tf_op jit(solution)/shard_map/ppermute | solution.py:170
  24.4 5.7 %copy-start.7 = (s32[192]{0:T(256)S(1)}, s32[192]{0:T(256)}, u32[]{:S(2)}) copy-start(s32[192]{0:T(256)} %param.7) | copy-start | bytes 2308
  28.6 290.9 %collective-permute-start.19 = (bf16[640,1024]{1,0:T(8,128)(2,1)}, bf16[640,1024]{1,0:T(8,128)(2,1)}, u32[]{:S(2)}, u32[]{:S(2)}) collective-permute-start(bf16[640,1024]{1,0:T(8,128)(2,1)} %fusion.68), channel_id=1, source_target_pairs={{0,2},{2,0},{4,6},{6,4},{8,10},{10,8},{12,14},{14,12},{1,3},{3,1},... | collective-permute-start | bytes 3932168 | tf_op jit(solution)/shard_map/ppermute | solution.py:163
  179.9 1.6 copy-start.2
  184.7 150.1 %collective-permute-start.14 = (bf16[640,1024]{1,0:T(8,128)(2,1)}, bf16[640,1024]{1,0:T(8,128)(2,1)}, u32[]{:S(2)}, u32[]{:S(2)}) collective-permute-start(bf16[640,1024]{1,0:T(8,128)(2,1)} %fusion.74), channel_id=1, source_target_pairs={{0,2},{2,0},{4,6},{6,4},{8,10},{10,8},{12,14},{14,12},{1,3},{3,1},... | collective-permute-start | bytes 3932168 | tf_op jit(solution)/shard_map/ppermute | solution.py:163
  315.3 4.2 copy-start.8
  315.3 40.9 %collective-permute-start.8 = (bf16[16,64,1024]{2,1,0:T(8,128)(2,1)}, bf16[16,64,1024]{2,1,0:T(8,128)(2,1)S(1)}, u32[]{:S(2)}, u32[]{:S(2)}) collective-permute-start(bf16[16,64,1024]{2,1,0:T(8,128)(2,1)} %get-tuple-element.10), channel_id=1, source_target_pairs={{0,1},{1,0},{2,3},{3,2},{4,5},{5,4},{6,7},{7,6},{8,9},{9,8},{10,11... | collective-permute-start | bytes 6291464 | tf_op jit(solution)/shard_map/ppermute | solution.py:251
  316.6 8.9 %collective-permute-start.4 = (bf16[128,2048]{1,0:T(8,128)(2,1)S(1)}, bf16[128,2048]{1,0:T(8,128)(2,1)S(1)}, u32[]{:S(2)}, u32[]{:S(2)}) collective-permute-start(bf16[128,2048]{1,0:T(8,128)(2,1)S(1)} %add_convert_fusion.6), channel_id=1, source_target_pairs={{4,8},{8,4},{6,10},{10,6},{5,9},{9,5},{7,11},{11,7},{20,24},{24,20... | collective-permute-start | bytes 1572872 | tf_op jit(solution)/shard_map/ppermute | solution.py:170
  319.5 31.1 %collective-permute-start.16 = (bf16[640,1024]{1,0:T(8,128)(2,1)S(1)}, bf16[640,1024]{1,0:T(8,128)(2,1)S(1)}, u32[]{:S(2)}, u32[]{:S(2)}) collective-permute-start(bf16[640,1024]{1,0:T(8,128)(2,1)S(1)} %copy-done.8), channel_id=1, source_target_pairs={{0,2},{2,0},{4,6},{6,4},{8,10},{10,8},{12,14},{14,12},{1,3},{3,1},... | collective-permute-start | bytes 3932168 | tf_op jit(solution)/shard_map/ppermute | solution.py:163
  325.5 36.7 %collective-permute-start.20 = (bf16[640,1024]{1,0:T(8,128)(2,1)}, bf16[640,1024]{1,0:T(8,128)(2,1)}, u32[]{:S(2)}, u32[]{:S(2)}) collective-permute-start(bf16[640,1024]{1,0:T(8,128)(2,1)} %fusion.8), channel_id=1, source_target_pairs={{0,4},{12,8},{2,6},{14,10},{1,5},{13,9},{3,7},{15,11},{16,20},{28,... | collective-permute-start | bytes 3932168 | tf_op jit(solution)/shard_map/ppermute | solution.py:170
  334.8 103.6 %collective-permute-start.12 = (bf16[16,64,1024]{2,1,0:T(8,128)(2,1)}, bf16[16,64,1024]{2,1,0:T(8,128)(2,1)}, u32[]{:S(2)}, u32[]{:S(2)}) collective-permute-start(bf16[16,64,1024]{2,1,0:T(8,128)(2,1)} %get-tuple-element.12), channel_id=1, source_target_pairs={{0,1},{1,0},{2,3},{3,2},{4,5},{5,4},{6,7},{7,6},{8,9},{9,8},{10,11... | collective-permute-start | bytes 6291464 | tf_op jit(solution)/shard_map/ppermute | solution.py:251
  350.6 20.9 %collective-permute-start.2 = (bf16[128,2048]{1,0:T(8,128)(2,1)}, bf16[128,2048]{1,0:T(8,128)(2,1)}, u32[]{:S(2)}, u32[]{:S(2)}) collective-permute-start(bf16[128,2048]{1,0:T(8,128)(2,1)} %add_convert_fusion.7), channel_id=1, source_target_pairs={{4,8},{8,4},{6,10},{10,6},{5,9},{9,5},{7,11},{11,7},{20,24},{24,20... | collective-permute-start | bytes 1572872 | tf_op jit(solution)/shard_map/ppermute | solution.py:170
  356.2 15.8 %collective-permute-start.5 = (bf16[128,2048]{1,0:T(8,128)(2,1)}, bf16[128,2048]{1,0:T(8,128)(2,1)}, u32[]{:S(2)}, u32[]{:S(2)}) collective-permute-start(bf16[128,2048]{1,0:T(8,128)(2,1)} %add_convert_fusion.5), channel_id=1, source_target_pairs={{8,12},{4,0},{10,14},{6,2},{9,13},{5,1},{11,15},{7,3},{24,28},{20,... | collective-permute-start | bytes 1572872 | tf_op jit(solution)/shard_map/ppermute | solution.py:170
  361.1 11.7 %copy-start.3 = (f32[128,2048]{1,0:T(8,128)S(1)}, f32[128,2048]{1,0:T(8,128)}, u32[]{:S(2)}) copy-start(f32[128,2048]{1,0:T(8,128)} %fusion.11) | copy-start | bytes 3145732
  362.3 47.6 %collective-permute-start.17 = (bf16[640,1024]{1,0:T(8,128)(2,1)}, bf16[640,1024]{1,0:T(8,128)(2,1)S(1)}, u32[]{:S(2)}, u32[]{:S(2)}) collective-permute-start(bf16[640,1024]{1,0:T(8,128)(2,1)} %fusion.9), channel_id=1, source_target_pairs={{0,4},{12,8},{2,6},{14,10},{1,5},{13,9},{3,7},{15,11},{16,20},{28,... | collective-permute-start | bytes 3932168 | tf_op jit(solution)/shard_map/ppermute | solution.py:170
  369.9 40.0 %copy-start.6 = (bf16[640,1024]{1,0:T(8,128)(2,1)S(1)}, bf16[640,1024]{1,0:T(8,128)(2,1)}, u32[]{:S(2)}) copy-start(bf16[640,1024]{1,0:T(8,128)(2,1)} %fusion.9) | copy-start | bytes 3932164
  369.9 79.6 %collective-permute-start.13 = (bf16[640,1024]{1,0:T(8,128)(2,1)}, bf16[640,1024]{1,0:T(8,128)(2,1)}, u32[]{:S(2)}, u32[]{:S(2)}) collective-permute-start(bf16[640,1024]{1,0:T(8,128)(2,1)} %fusion.77), channel_id=1, source_target_pairs={{0,2},{2,0},{4,6},{6,4},{8,10},{10,8},{12,14},{14,12},{1,3},{3,1},... | collective-permute-start | bytes 3932168 | tf_op jit(solution)/shard_map/ppermute | solution.py:163
  371.5 30.6 %collective-permute-start.9 = (bf16[384,128]{1,0:T(8,128)(2,1)S(1)}, bf16[384,128]{1,0:T(8,128)(2,1)S(1)}, u32[]{:S(2)}, u32[]{:S(2)}) collective-permute-start(bf16[384,128]{1,0:T(8,128)(2,1)S(1)} %reshape.76), channel_id=1, source_target_pairs={{0,2},{2,0},{4,6},{6,4},{8,10},{10,8},{12,14},{14,12},{1,3},{3,1},... | collective-permute-start | bytes 294920 | tf_op jit(solution)/shard_map/ppermute | solution.py:264
  372.0 39.6 %collective-permute-start.21 = (bf16[640,1024]{1,0:T(8,128)(2,1)S(1)}, bf16[640,1024]{1,0:T(8,128)(2,1)S(1)}, u32[]{:S(2)}, u32[]{:S(2)}) collective-permute-start(bf16[640,1024]{1,0:T(8,128)(2,1)S(1)} %add_convert_fusion.2), channel_id=1, source_target_pairs={{4,8},{8,4},{6,10},{10,6},{5,9},{9,5},{7,11},{11,7},{20,24},{24,20... | collective-permute-start | bytes 3932168 | tf_op jit(solution)/shard_map/ppermute | solution.py:170
  374.4 27.8 %copy-start.4 = (bf16[128,2048]{1,0:T(8,128)(2,1)}, bf16[128,2048]{1,0:T(8,128)(2,1)S(1)}, u32[]{:S(2)}) copy-start(bf16[128,2048]{1,0:T(8,128)(2,1)S(1)} %add_convert_fusion.4) | copy-start | bytes 1572868
  402.1 4.7 collective-permute-start.10
  406.8 46.4 %collective-permute-start.15 = (bf16[640,1024]{1,0:T(8,128)(2,1)}, bf16[640,1024]{1,0:T(8,128)(2,1)}, u32[]{:S(2)}, u32[]{:S(2)}) collective-permute-start(bf16[640,1024]{1,0:T(8,128)(2,1)} %fusion.10), channel_id=1, source_target_pairs={{0,4},{12,8},{2,6},{14,10},{1,5},{13,9},{3,7},{15,11},{16,20},{28,... | collective-permute-start | bytes 3932168 | tf_op jit(solution)/shard_map/ppermute | solution.py:170
  409.9 26.8 %collective-permute-start.11 = (bf16[384,128]{1,0:T(8,128)(2,1)S(1)}, bf16[384,128]{1,0:T(8,128)(2,1)S(1)}, u32[]{:S(2)}, u32[]{:S(2)}) collective-permute-start(bf16[384,128]{1,0:T(8,128)(2,1)S(1)} %add_convert_fusion.10), channel_id=1, source_target_pairs={{0,8},{2,10},{4,12},{6,14},{8,0},{10,2},{12,4},{14,6},{1,9},{3,11}... | collective-permute-start | bytes 294920 | tf_op jit(solution)/shard_map/ppermute | solution.py:264
  411.6 41.6 %collective-permute-start.18 = (bf16[640,1024]{1,0:T(8,128)(2,1)}, bf16[640,1024]{1,0:T(8,128)(2,1)}, u32[]{:S(2)}, u32[]{:S(2)}) collective-permute-start(bf16[640,1024]{1,0:T(8,128)(2,1)} %add_convert_fusion.3), channel_id=1, source_target_pairs={{4,8},{8,4},{6,10},{10,6},{5,9},{9,5},{7,11},{11,7},{20,24},{24,20... | collective-permute-start | bytes 3932168 | tf_op jit(solution)/shard_map/ppermute | solution.py:170
  436.7 30.1 %collective-permute-start.22 = (bf16[640,1024]{1,0:T(8,128)(2,1)}, bf16[640,1024]{1,0:T(8,128)(2,1)}, u32[]{:S(2)}, u32[]{:S(2)}) collective-permute-start(bf16[640,1024]{1,0:T(8,128)(2,1)} %add_convert_fusion.1), channel_id=1, source_target_pairs={{8,12},{4,0},{10,14},{6,2},{9,13},{5,1},{11,15},{7,3},{24,28},{20,... | collective-permute-start | bytes 3932168 | tf_op jit(solution)/shard_map/ppermute | solution.py:170
  438.3 14.8 %collective-permute-start.6 = (bf16[128,1024]{1,0:T(8,128)(2,1)S(1)}, bf16[128,1024]{1,0:T(8,128)(2,1)S(1)}, u32[]{:S(2)}, u32[]{:S(2)}) collective-permute-start(bf16[128,1024]{1,0:T(8,128)(2,1)S(1)} %constant_dynamic-slice_fusion), channel_id=1, source_target_pairs={{0,2},{2,0},{4,6},{6,4},{8,10},{10,8},{12,14},{14,12},{1,3},{3,1},... | collective-permute-start | bytes 786440 | tf_op jit(solution)/shard_map/ppermute | solution.py:163
  439.9 5.0 %copy-start.1 = (bf16[16,64,1024]{2,1,0:T(8,128)(2,1)S(1)}, bf16[16,64,1024]{2,1,0:T(8,128)(2,1)}, u32[]{:S(2)}) copy-start(bf16[16,64,1024]{2,1,0:T(8,128)(2,1)} %get-tuple-element.11) | copy-start | bytes 6291460
  449.5 3.6 copy-start.5

commit v2 on v1

v2 whole, which is shorter than its diff:
```python
import jax
import jax.numpy as jnp
import numpy as np
from jax import lax
from jax.experimental import pallas as pl
from jax.experimental.pallas import tpu as pltpu
from jax.sharding import PartitionSpec as P

SLOTS = 16
GROUP = 4
VMEM = 32 * 2**20


def copy_blocks(index, down, up):
    count = index.shape[0]

    def kernel(index_ref, down_ref, up_ref, down_out, up_out, sems):
        copies = []
        for m, (src, dst) in enumerate(((down_ref, down_out), (up_ref, up_out))):
            for s in range(count):
                copies.append(
                    pltpu.make_async_copy(src.at[index_ref[s]], dst.at[s], sems.at[m, s])
                )
        for copy in copies:
            copy.start()
        for copy in copies:
            copy.wait()

    shape = jax.ShapeDtypeStruct((count,) + down.shape[1:], down.dtype)
    return pl.pallas_call(
        kernel,
        out_shape=(shape, shape),
        in_specs=[
            pl.BlockSpec(memory_space=pltpu.SMEM),
            pl.BlockSpec(memory_space=pl.ANY),
            pl.BlockSpec(memory_space=pl.ANY),
        ],
        out_specs=(pl.BlockSpec(memory_space=pltpu.VMEM), pl.BlockSpec(memory_space=pltpu.VMEM)),
        scratch_shapes=[pltpu.SemaphoreType.DMA((2, count))],
        compiler_params=pltpu.CompilerParams(vmem_limit_bytes=VMEM),
        cost_estimate=pl.CostEstimate(
            flops=0, transcendentals=0, bytes_accessed=4 * count * down[0].size * 2
        ),
        name="copy_blocks",
    )(index, down, up)


def low_rank(rows, slot, maps, index):
    count, width = rows.shape
    rank = maps.shape[1]
    wide = GROUP * rank
    steps = index.shape[0] // GROUP

    def kernel(index_ref, rows_ref, slot_ref, *refs):
        map_refs, out_ref, acc = refs[:GROUP], refs[GROUP], refs[GROUP + 1]
        i = pl.program_id(0)

        @pl.when(i == 0)
        def _():
            acc[...] = jnp.zeros_like(acc)

        blocks = jnp.concatenate([ref[0] for ref in map_refs], axis=0)
        scores = lax.dot_general(
            rows_ref[...], blocks, (((1,), (1,)), ((), ())),
            preferred_element_type=jnp.float32,
        )
        lane_slot = lax.broadcasted_iota(jnp.int32, (count, wide), 1) // rank + i * GROUP
        acc[...] += jnp.where(slot_ref[...] == lane_slot, scores, 0.0)

        @pl.when(i == steps - 1)
        def _():
            total = acc[:, 0:rank]
            for g in range(1, GROUP):
                total += acc[:, g * rank : (g + 1) * rank]
            out_ref[...] = total

    def map_spec(g):
        return pl.BlockSpec((1, rank, width), lambda i, index: (index[i * GROUP + g], 0, 0))

    return pl.pallas_call(
        kernel,
        grid_spec=pltpu.PrefetchScalarGridSpec(
            num_scalar_prefetch=1,
            grid=(steps,),
            in_specs=[
                pl.BlockSpec((count, width), lambda i, index: (0, 0)),
                pl.BlockSpec((count, 1), lambda i, index: (0, 0)),
            ]
            + [map_spec(g) for g in range(GROUP)],
            out_specs=pl.BlockSpec((count, rank), lambda i, index: (0, 0)),
            scratch_shapes=[pltpu.VMEM((count, wide), jnp.float32)],
        ),
        out_shape=jax.ShapeDtypeStruct((count, rank), jnp.float32),
        compiler_params=pltpu.CompilerParams(vmem_limit_bytes=VMEM),
        cost_estimate=pl.CostEstimate(
            flops=2 * count * width * rank * index.shape[0],
            transcendentals=0,
            bytes_accessed=2 * (index.shape[0] * rank * width + rows.size),
        ),
        name="low_rank",
    )(index, rows, slot, *[maps] * GROUP)


def expand(low, slot, maps, index, start=None):
    count, rank = low.shape
    width = maps.shape[2]
    wide = GROUP * rank
    steps = index.shape[0] // GROUP
    starts = [] if start is None else [start]

    def kernel(index_ref, low_ref, slot_ref, *refs):
        map_refs, out_ref = refs[:GROUP], refs[-1]
        i = pl.program_id(0)
        tiled = jnp.concatenate([low_ref[...]] * GROUP, axis=1)
        lane_slot = lax.broadcasted_iota(jnp.int32, (count, wide), 1) // rank + i * GROUP
        picked = jnp.where(slot_ref[...] == lane_slot, tiled, jnp.zeros_like(tiled))
        blocks = jnp.concatenate([ref[0] for ref in map_refs], axis=0)
        term = jnp.dot(picked, blocks, preferred_element_type=jnp.float32)

        @pl.when(i == 0)
        def _():
            out_ref[...] = term + refs[GROUP][...] if starts else term

        @pl.when(i > 0)
        def _():
            out_ref[...] += term

    def map_spec(g):
        return pl.BlockSpec((1, rank, width), lambda i, index: (index[i * GROUP + g], 0, 0))

    whole = pl.BlockSpec((count, width), lambda i, index: (0, 0))
    return pl.pallas_call(
        kernel,
        grid_spec=pltpu.PrefetchScalarGridSpec(
            num_scalar_prefetch=1,
            grid=(steps,),
            in_specs=[
                pl.BlockSpec((count, rank), lambda i, index: (0, 0)),
                pl.BlockSpec((count, 1), lambda i, index: (0, 0)),
            ]
            + [map_spec(g) for g in range(GROUP)]
            + [whole] * len(starts),
            out_specs=whole,
        ),
        out_shape=jax.ShapeDtypeStruct((count, width), jnp.float32),
        compiler_params=pltpu.CompilerParams(vmem_limit_bytes=VMEM),
        cost_estimate=pl.CostEstimate(
            flops=2 * count * width * rank * index.shape[0],
            transcendentals=0,
            bytes_accessed=2 * index.shape[0] * rank * width + 4 * count * width,
        ),
        name="expand",
    )(index, low, slot, *[maps] * GROUP, *starts)


def product(rows, row_at, row_tile, weight, at, size, adds=(), dtype=jnp.bfloat16):
    width = rows.shape[1]
    tile = min(512, size)
    steps = size // tile

    def kernel(at_ref, rows_ref, weight_ref, *refs):
        total = jnp.dot(rows_ref[...], weight_ref[...], preferred_element_type=jnp.float32)
        for ref in refs[:-1]:
            total += ref[...].astype(jnp.float32)
        refs[-1][...] = total.astype(dtype)

    return pl.pallas_call(
        kernel,
        grid_spec=pltpu.PrefetchScalarGridSpec(
            num_scalar_prefetch=1,
            grid=(steps,),
            in_specs=[
                pl.BlockSpec((row_tile, width), lambda i, at: (row_at, 0)),
                pl.BlockSpec((width, tile), lambda i, at: (0, at[0] * steps + i)),
            ]
            + [pl.BlockSpec((row_tile, tile), lambda i, at: (0, i)) for _ in adds],
            out_specs=pl.BlockSpec((row_tile, tile), lambda i, at: (0, i)),
        ),
        out_shape=jax.ShapeDtypeStruct((row_tile, size), dtype),
        compiler_params=pltpu.CompilerParams(vmem_limit_bytes=VMEM),
        cost_estimate=pl.CostEstimate(
            flops=2 * row_tile * width * size,
            transcendentals=0,
            bytes_accessed=2 * (row_tile * width + width * size + row_tile * size * (1 + len(adds))),
        ),
        name="product",
    )(jnp.reshape(at, (1,)), rows, weight, *adds)


def finish(head, arrived, tail):
    high, width = head.shape
    low = tail.shape[0]
    blocks = high // low

    def kernel(head_ref, *refs):
        tail_ref, out_ref = refs[-2], refs[-1]
        i = pl.program_id(0)

        @pl.when(i < blocks)
        def _():
            total = head_ref[...]
            for ref in refs[:-2]:
                total += ref[...].astype(jnp.float32)
            out_ref[...] = total.astype(out_ref.dtype)

        @pl.when(i == blocks)
        def _():
            out_ref[...] = tail_ref[...]

    spec = pl.BlockSpec((low, width), lambda i: (jnp.minimum(i, blocks - 1), 0))
    return pl.pallas_call(
        kernel,
        grid=(blocks + 1,),
        in_specs=[spec] * (1 + len(arrived)) + [pl.BlockSpec((low, width), lambda i: (0, 0))],
        out_specs=pl.BlockSpec((low, width), lambda i: (i, 0)),
        out_shape=jax.ShapeDtypeStruct((high + low, width), tail.dtype),
        compiler_params=pltpu.CompilerParams(vmem_limit_bytes=VMEM),
        cost_estimate=pl.CostEstimate(
            flops=high * width * len(arrived),
            transcendentals=0,
            bytes_accessed=high * width * (6 + 2 * len(arrived)),
        ),
        name="finish",
    )(head, *arrived, tail)


def line_plan(nz):
    order = np.zeros((nz, nz), np.int32)
    for z in range(nz):
        def need(j):
            if j == z:
                return (2 * nz, 0)
            return (nz - 1 - j + z, j) if j > z else (nz - 1 - z + j, nz - j)

        order[z] = sorted(range(nz), key=need)
    return order


def on_device(attention_result, tenant, projection_weight, adapter_down_maps, adapter_up_maps):
    steps, row_count, width = attention_result.shape
    local_adapters = adapter_down_maps.shape[0]
    owners = lax.axis_size("dp")
    me = lax.axis_index("dp")
    n = lax.axis_size("tensor")
    nz = n // 2
    place = lax.axis_index("tensor")
    z, y = place // 2, place % 2
    order = line_plan(nz)
    my_order = jnp.asarray(order)[z]
    out_width = projection_weight.shape[1] // n

    def swap_y(value):
        return lax.ppermute(value, "tensor", [(t, t ^ 1) for t in range(n)])

    def hop(value, h):
        pairs = []
        for side in range(2):
            pairs.append((h * 2 + side, (h + 1) * 2 + side))
            pairs.append(((nz - 1 - h) * 2 + side, (nz - 2 - h) * 2 + side))
        return lax.ppermute(value, "tensor", pairs)

    def slot_of(h, m):
        return list(order[h]).index(nz - 1 - m)

    def line_sum(blocks):
        arrived = {}
        for when in range(2 * nz - 3):
            for h in range(nz - 1):
                m = when - h
                if 0 <= m < nz - 1 - h:
                    value = blocks[slot_of(h, m)]
                    if h:
                        value = value.astype(jnp.float32) + arrived[h - 1, m].astype(jnp.float32)
                    arrived[h, m] = hop(value.astype(jnp.bfloat16), h)
        return [arrived[h, nz - 2 - h] for h in range(nz - 1)]

    rows = attention_result.reshape(steps * row_count, width)
    total_rows = steps * row_count
    few = total_rows // 6
    most = total_rows - few

    def product_a(at):
        return product(rows, most // few, few, projection_weight, at, 2 * out_width)

    def product_b(at, adds=(), dtype=jnp.bfloat16):
        return product(rows, 0, most, projection_weight, at, out_width, adds, dtype)

    sent_y = []
    for k in range(nz):
        sent_y.append(swap_y(product_b(my_order[k] * 2 + 1 - y)))
    blocks_a = [product_a(my_order[k]) for k in range(nz)]
    arrived_a = line_sum(blocks_a)
    blocks_b = [product_b(my_order[k] * 2 + y, [sent_y[k]]) for k in range(nz - 1)]
    arrived_b = line_sum(blocks_b)

    sum_a = blocks_a[nz - 1].astype(jnp.float32)
    for value in arrived_a:
        sum_a = sum_a + value.astype(jnp.float32)
    sum_a = sum_a.astype(jnp.bfloat16)
    away_a = lax.dynamic_slice(sum_a, (0, (1 - y) * out_width), (few, out_width))
    kept_a = lax.dynamic_slice(sum_a, (0, y * out_width), (few, out_width))
    other_a = swap_y(away_a)

    slot_range = jnp.arange(SLOTS, dtype=jnp.int32)
    ids = jnp.arange(local_adapters, dtype=jnp.int32)

    def slots(row_ids, owner):
        hit = row_ids[:, None] - owner * local_adapters == ids[None, :]
        used = jnp.any(hit, axis=0)
        position = jnp.sum(
            (used[None, :] & (ids[None, :] < ids[:, None])).astype(jnp.int32), axis=1
        )
        names = jnp.sum(
            jnp.where(used[None, :] & (position[None, :] == slot_range[:, None]), ids[None, :], 0),
            axis=1,
        )
        row_slot = jnp.sum(jnp.where(hit, position[None, :] + 1, 0), axis=1) - 1
        return names, row_slot

    held = []
    for shift in range(owners):
        names, row_slot = slots(tenant, (me - shift) % owners)
        if shift == 0:
            down, up = adapter_down_maps, adapter_up_maps
        else:
            theirs = lax.ppermute(
                tenant, "dp", [(i, (i - shift) % owners) for i in range(owners)]
            )
            down, up = copy_blocks(slots(theirs, me)[0], adapter_down_maps, adapter_up_maps)
            onward = [(i, (i + shift) % owners) for i in range(owners)]
            down, up = lax.ppermute(down, "dp", onward), lax.ppermute(up, "dp", onward)
            names = slot_range
        held.append((names, jnp.tile(row_slot, steps)[:, None], down, up))

    low = 0
    for names, row_slot, down, _ in held:
        low = low + low_rank(rows, row_slot, down, names)
    rank = low.shape[1]
    low = low.astype(jnp.bfloat16).reshape(total_rows * rank // 128, 128)
    bit = 1
    while bit < n:
        other = lax.ppermute(low, "tensor", [(t, t ^ bit) for t in range(n)])
        low = (low.astype(jnp.float32) + other.astype(jnp.float32)).astype(jnp.bfloat16)
        bit *= 2
    low = low.reshape(total_rows, rank)
    delta = None
    for names, row_slot, _, up in held:
        delta = expand(low, row_slot, up, names, delta)

    head_b = product_b(my_order[nz - 1] * 2 + y, [sent_y[nz - 1], delta], jnp.float32)
    out_a = kept_a.astype(jnp.float32) + other_a.astype(jnp.float32) + delta[most:]
    out = finish(head_b, arrived_b, out_a.astype(jnp.bfloat16))
    return out.reshape(steps, row_count, out_width)


def solution(mesh):
    placed = (
        P(None, ("groups", "dp"), "tensor"),
        P(("groups", "dp")),
        P("tensor", None),
        P(("groups", "dp"), None, "tensor"),
        P(("groups", "dp"), None, "tensor"),
    )
    return jax.shard_map(
        on_device,
        mesh=mesh,
        in_specs=placed,
        out_specs=P(None, ("groups", "dp"), "tensor"),
        check_vma=False,
    )
```

time: 472 us -> 233 us (0.49)
  Pallas kernels: 272 us -> 67.5 us
  local copies, waits for them, and re-layouts: 4.82 us -> 66.4 us
  waiting for transfers between devices: 77.4 us -> 29 us
  matrix products: 48.1 us -> 0 us
  starting transfers between devices: 40.5 us -> 50.1 us
  other arithmetic: 22.1 us -> 15.7 us
    pallas_call x2 -> x1, Pallas kernels: 258 us -> 8.34 us  [copy_blocks(): pl.pallas_call(kernel, out_shape=(shape, shape), in_specs=[pl.BlockSpec(m...]
    unnamed x18 -> x48, local copies, waits for them, and re-layouts: 1.62 us -> 61.2 us
    dot_general x12 -> x0, matrix products: 48.1 us -> none  [dot(): return jnp.dot(left, right, preferred_element_type=jnp.float32)]
    pallas_call x4 -> x17, Pallas kernels: 14.2 us -> 59.2 us  [the longest x12 36.1 us: product(): pl.pallas_call(kernel, grid_spec=pltpu.PrefetchScalarGridSpec(num_scalar_...]
    ppermute x3, waiting for transfers between devices: 52.6 us -> 11.4 us  [on_device(): other = lax.ppermute(low, 'tensor', [(t, t ^ bit) for t in range(n)])]
    ppermute x5, waiting for transfers between devices: 11.3 us -> 0.01 us  [swap_y(): return lax.ppermute(value, 'tensor', [(t, t ^ 1) for t in range(n)])]
    ppermute x3, starting transfers between devices: 0.65 us -> 10.8 us  [on_device(): other = lax.ppermute(low, 'tensor', [(t, t ^ bit) for t in range(n)])]
  transfers between devices with their start and end apart: 23 -> 23, of which waited for: 5 -> 5; matrix products, arithmetic and copies ran while one was open for 15% -> 9% of each run, Pallas kernels for 58% -> 27%
where the time goes in v2:
time: 233 us; the launch traced here: 232 us
  Pallas kernels  67.5 us (29%)
  local copies, waits for them, and re-layouts  66.4 us (28%)
  starting transfers between devices  50.1 us (22%)
  waiting for transfers between devices  29 us (12%)
  other arithmetic  15.7 us (7%)
  between operations  2.85 us (1%)
    unnamed x48, local copies, waits for them, and re-layouts  61.2 us
    pallas_call x12, Pallas kernels, product(): pl.pallas_call(kernel, grid_spec=pltpu.PrefetchScalarGridSpec(num_scalar_...  36.1 us
    ppermute x12, starting transfers between devices, hop(): return lax.ppermute(value, 'tensor', pairs)  33.3 us
    ppermute x12, waiting for transfers between devices, hop(): return lax.ppermute(value, 'tensor', pairs)  17.5 us
    convert_element_type x6, other arithmetic, line_sum(): arrived[h, m] = hop(value.astype(jnp.bfloat16), h)  12.4 us
    ppermute x3, waiting for transfers between devices, on_device(): other = lax.ppermute(low, 'tensor', [(t, t ^ bit) for t in range(n)])  11.4 us
    ppermute x3, starting transfers between devices, on_device(): other = lax.ppermute(low, 'tensor', [(t, t ^ bit) for t in range(n)])  10.8 us
    pallas_call x2, Pallas kernels, expand(): pl.pallas_call(kernel, grid_spec=pltpu.PrefetchScalarGridSpec(num_scalar_...  9.87 us
  transfers between devices with their start and end apart: 23, of which 5 were waited for; matrix products, arithmetic and copies ran while one was open for 9% of the time, Pallas kernels for 27%

profile of v2, /device:TPU:0, one launch (start us, length us, event | category | flops | bytes accessed | tf_op | source)
XLA Modules:
  0.0 231.5 jit_solution(17183855490867474397)
XLA Ops:
  1.7 5.8 %copy-done = bf16[1024,8192]{1,0:T(8,128)(2,1)S(1)} copy-done((bf16[1024,8192]{1,0:T(8,128)(2,1)S(1)}, bf16[1024,8192]{1,0:T(8,128)(2,1)}, u32[]{:S(2)}) %copy-start) | copy-done | bytes 16777240
  8.9 3.2 %product.23 = bf16[128,2048]{1,0:T(8,128)(2,1)} custom-call(s32[1]{0:T(128)} %bitcast.16.at_ref, bf16[768,1024]{1,0:T(8,128)(2,1)S(1)} %bitcast.18, bf16[1024,8192]{1,0:T(8,128)(2,1)S(1)} %copy-done), custom_call_target="tpu_custom_call" | custom-call | flops 536870912 | bytes 4980736 | tf_op jit(solution)/shard_map/product/pallas_call | solution.py:167
  12.1 5.3 %collective-permute-start.19 = (bf16[128,2048]{1,0:T(8,128)(2,1)}, bf16[128,2048]{1,0:T(8,128)(2,1)}, u32[]{:S(2)}, u32[]{:S(2)}) collective-permute-start(bf16[128,2048]{1,0:T(8,128)(2,1)} %product.23), channel_id=1, source_target_pairs={{0,4},{12,8},{2,6},{14,10},{1,5},{13,9},{3,7},{15,11},{16,20},{28,... | collective-permute-start | bytes 1572872 | tf_op jit(solution)/shard_map/ppermute | solution.py:260
  17.4 3.3 %product.22 = bf16[128,2048]{1,0:T(8,128)(2,1)} custom-call(s32[1]{0:T(128)} %bitcast.15.at_ref, bf16[768,1024]{1,0:T(8,128)(2,1)S(1)} %bitcast.19, bf16[1024,8192]{1,0:T(8,128)(2,1)S(1)} %copy-done), custom_call_target="tpu_custom_call" | custom-call | flops 536870912 | bytes 4980736 | tf_op jit(solution)/shard_map/product/pallas_call | solution.py:167
  20.7 2.1 collective-permute-start.17
  23.5 5.8 %copy-done.1 = bf16[1024,8192]{1,0:T(8,128)(2,1)S(1)} copy-done((bf16[1024,8192]{1,0:T(8,128)(2,1)S(1)}, bf16[1024,8192]{1,0:T(8,128)(2,1)}, u32[]{:S(2)}) %copy-start.1) | copy-done | bytes 16777240
  29.3 2.7 %product.18 = bf16[640,1024]{1,0:T(8,128)(2,1)} custom-call(s32[1]{0:T(128)} %bitcast.12.at_ref, bf16[768,1024]{1,0:T(8,128)(2,1)S(1)} %bitcast.20, bf16[1024,8192]{1,0:T(8,128)(2,1)S(1)} %copy-done.1), custom_call_target="tpu_custom_call" | custom-call | flops 1342177280 | bytes 4718592 | tf_op jit(solution)/shard_map/product/pallas_call | solution.py:167
  34.1 5.8 %copy-done.2 = bf16[1024,8192]{1,0:T(8,128)(2,1)S(1)} copy-done((bf16[1024,8192]{1,0:T(8,128)(2,1)S(1)}, bf16[1024,8192]{1,0:T(8,128)(2,1)}, u32[]{:S(2)}) %copy-start.2) | copy-done | bytes 16777240
  39.9 2.7 %product.16 = bf16[640,1024]{1,0:T(8,128)(2,1)} custom-call(s32[1]{0:T(128)} %bitcast.9.at_ref, bf16[768,1024]{1,0:T(8,128)(2,1)S(1)} %bitcast.21, bf16[1024,8192]{1,0:T(8,128)(2,1)S(1)} %copy-done.2), custom_call_target="tpu_custom_call" | custom-call | flops 1342177280 | bytes 4718592 | tf_op jit(solution)/shard_map/product/pallas_call | solution.py:167
  44.1 3.4 %copy-done.10 = bf16[64,64,1024]{2,1,0:T(8,128)(2,1)S(1)} copy-done((bf16[64,64,1024]{2,1,0:T(8,128)(2,1)S(1)}, bf16[64,64,1024]{2,1,0:T(8,128)(2,1)}, u32[]{:S(2)}) %copy-start.10) | copy-done | bytes 8388632
  47.5 3.4 %copy-done.12 = bf16[64,64,1024]{2,1,0:T(8,128)(2,1)S(1)} copy-done((bf16[64,64,1024]{2,1,0:T(8,128)(2,1)S(1)}, bf16[64,64,1024]{2,1,0:T(8,128)(2,1)}, u32[]{:S(2)}) %copy-start.12) | copy-done | bytes 8388632
  50.9 8.3 %copy_blocks.1 = (bf16[16,64,1024]{2,1,0:T(8,128)(2,1)}, bf16[16,64,1024]{2,1,0:T(8,128)(2,1)}) custom-call(s32[16]{0:T(128)S(1)} %select_reduce_fusion.2.index_ref, bf16[64,64,1024]{2,1,0:T(8,128)(2,1)S(1)} %copy-done.10, bf16[64,64,1024]{2,1,0:T(8,128)(2,1)S(1)} %copy-done.12), custom_call_target="tpu_custom_call" | custom-call | bytes 8388608 | tf_op jit(solution)/shard_map/copy_blocks/pallas_call | solution.py:30
  59.9 5.8 %copy-done.3 = bf16[1024,8192]{1,0:T(8,128)(2,1)S(1)} copy-done((bf16[1024,8192]{1,0:T(8,128)(2,1)S(1)}, bf16[1024,8192]{1,0:T(8,128)(2,1)}, u32[]{:S(2)}) %copy-start.3) | copy-done | bytes 16777240
  65.7 2.7 %product.12 = bf16[640,1024]{1,0:T(8,128)(2,1)} custom-call(s32[1]{0:T(128)} %bitcast.3.at_ref, bf16[768,1024]{1,0:T(8,128)(2,1)S(1)} %bitcast.22, bf16[1024,8192]{1,0:T(8,128)(2,1)S(1)} %copy-done.3), custom_call_target="tpu_custom_call" | custom-call | flops 1342177280 | bytes 4718592 | tf_op jit(solution)/shard_map/product/pallas_call | solution.py:167
  69.1 5.8 %copy-done.4 = bf16[1024,8192]{1,0:T(8,128)(2,1)S(1)} copy-done((bf16[1024,8192]{1,0:T(8,128)(2,1)S(1)}, bf16[1024,8192]{1,0:T(8,128)(2,1)}, u32[]{:S(2)}) %copy-start.4) | copy-done | bytes 16777240
  74.8 2.8 %product.14 = bf16[640,1024]{1,0:T(8,128)(2,1)} custom-call(s32[1]{0:T(128)} %bitcast.6.at_ref, bf16[768,1024]{1,0:T(8,128)(2,1)S(1)} %bitcast.23, bf16[1024,8192]{1,0:T(8,128)(2,1)S(1)} %copy-done.4), custom_call_target="tpu_custom_call" | custom-call | flops 1342177280 | bytes 4718592 | tf_op jit(solution)/shard_map/product/pallas_call | solution.py:167
  77.6 3.1 %product.21 = bf16[128,2048]{1,0:T(8,128)(2,1)} custom-call(s32[1]{0:T(128)} %bitcast.14.at_ref, bf16[768,1024]{1,0:T(8,128)(2,1)S(1)} %bitcast.24, bf16[1024,8192]{1,0:T(8,128)(2,1)S(1)} %copy-done.4), custom_call_target="tpu_custom_call" | custom-call | flops 536870912 | bytes 4980736 | tf_op jit(solution)/shard_map/product/pallas_call | solution.py:167
  82.1 5.8 %copy-done.5 = bf16[1024,8192]{1,0:T(8,128)(2,1)S(1)} copy-done((bf16[1024,8192]{1,0:T(8,128)(2,1)S(1)}, bf16[1024,8192]{1,0:T(8,128)(2,1)}, u32[]{:S(2)}) %copy-start.5) | copy-done | bytes 16777240
  87.9 2.3 product.20
  90.2 3.4 %copy-done.11 = bf16[64,64,1024]{2,1,0:T(8,128)(2,1)S(1)} copy-done((bf16[64,64,1024]{2,1,0:T(8,128)(2,1)S(1)}, bf16[64,64,1024]{2,1,0:T(8,128)(2,1)}, u32[]{:S(2)}) %copy-start.11) | copy-done | bytes 8388632
  93.6 3.4 %low_rank.2 = f32[768,64]{1,0:T(8,128)S(1)} custom-call(s32[16]{0:T(128)S(1)} %select_reduce_fusion.3.index_ref, bf16[768,1024]{1,0:T(8,128)(2,1)S(1)} %bitcast.26, s32[768,1]{1,0:T(8,128)S(1)} %broadcast_in_dim_tile.8.slot_ref, bf16[64,64,1024]{2,1,0:T(8,128)(2,1)S(1)} %copy-done.11, bf16[64,64,1024]{2,1,0:T(8,128)(2,1)S(1)} %copy-done.11, ...), custom_call_target="tpu_custom_call" | custom-call | flops 1610612736 | bytes 3670016 | tf_op jit(solution)/shard_map/low_rank/pallas_call | solution.py:80
  96.9 2.1 collective-permute-start.16
  99.1 5.8 %copy-done.6 = bf16[1024,8192]{1,0:T(8,128)(2,1)S(1)} copy-done((bf16[1024,8192]{1,0:T(8,128)(2,1)S(1)}, bf16[1024,8192]{1,0:T(8,128)(2,1)}, u32[]{:S(2)}) %copy-start.6) | copy-done | bytes 16777240
  104.8 3.0 %product.19 = bf16[640,1024]{1,0:T(8,128)(2,1)S(1)} custom-call(s32[1]{0:T(128)} %bitcast.11.at_ref, bf16[768,1024]{1,0:T(8,128)(2,1)S(1)} %bitcast.27, bf16[1024,8192]{1,0:T(8,128)(2,1)S(1)} %copy-done.6, bf16[640,1024]{1,0:T(8,128)(2,1)} %collective-permute-done.12.refs_0_), custom_call_target="tpu_custom_call" | custom-call | flops 1342177280 | bytes 6029312 | tf_op jit(solution)/shard_map/product/pallas_call | solution.py:167
  107.8 2.4 %collective-permute-start.13 = (bf16[640,1024]{1,0:T(8,128)(2,1)S(1)}, bf16[640,1024]{1,0:T(8,128)(2,1)}, u32[]{:S(2)}, u32[]{:S(2)}) collective-permute-start(bf16[640,1024]{1,0:T(8,128)(2,1)S(1)} %product.19), channel_id=1, source_target_pairs={{0,4},{12,8},{2,6},{14,10},{1,5},{13,9},{3,7},{15,11},{16,20},{28,... | collective-permute-start | bytes 3932168 | tf_op jit(solution)/shard_map/ppermute | solution.py:260
  110.2 2.1 add_convert_fusion.5
  112.3 1.5 collective-permute-start.7
  113.9 2.1 add_convert_fusion.6
  117.4 3.8 %product.17 = bf16[640,1024]{1,0:T(8,128)(2,1)} custom-call(s32[1]{0:T(128)} %bitcast.8.at_ref, bf16[768,1024]{1,0:T(8,128)(2,1)S(1)} %bitcast.28, bf16[1024,8192]{1,0:T(8,128)(2,1)S(1)} %copy-done.6, bf16[640,1024]{1,0:T(8,128)(2,1)} %collective-permute-done.9.refs_0_), custom_call_target="tpu_custom_call" | custom-call | flops 1342177280 | bytes 6029312 | tf_op jit(solution)/shard_map/product/pallas_call | solution.py:167
  121.2 2.4 %collective-permute-start.10 = (bf16[640,1024]{1,0:T(8,128)(2,1)}, bf16[640,1024]{1,0:T(8,128)(2,1)}, u32[]{:S(2)}, u32[]{:S(2)}) collective-permute-start(bf16[640,1024]{1,0:T(8,128)(2,1)} %product.17), channel_id=1, source_target_pairs={{0,4},{12,8},{2,6},{14,10},{1,5},{13,9},{3,7},{15,11},{16,20},{28,... | collective-permute-start | bytes 3932168 | tf_op jit(solution)/shard_map/ppermute | solution.py:260
  123.6 5.0 %low_rank.3 = f32[768,64]{1,0:T(8,128)S(1)} custom-call(s32[16]{0:T(128)S(1)} %iota.18.index_ref, bf16[768,1024]{1,0:T(8,128)(2,1)S(1)} %bitcast.29, s32[768,1]{1,0:T(8,128)S(1)} %copy-done.14, bf16[16,64,1024]{2,1,0:T(8,128)(2,1)} %collective-permute-done.2.refs_0_.refs_1_.refs_2_.refs_3_, ...), custom_call_target="tpu_custom_call" | custom-call | flops 1610612736 | bytes 3670016 | tf_op jit(solution)/shard_map/low_rank/pallas_call | solution.py:80
  129.4 9.4 %collective-permute-done.13 = bf16[640,1024]{1,0:T(8,128)(2,1)} collective-permute-done((bf16[640,1024]{1,0:T(8,128)(2,1)S(1)}, bf16[640,1024]{1,0:T(8,128)(2,1)}, u32[]{:S(2)}, u32[]{:S(2)}) %collective-permute-start.13) | collective-permute-done | bytes 1310752 | tf_op jit(solution)/shard_map/ppermute | solution.py:260
  140.4 1.8 add_convert_fusion.1
  145.9 4.1 %collective-permute-start.4 = (bf16[384,128]{1,0:T(8,128)(2,1)S(1)}, bf16[384,128]{1,0:T(8,128)(2,1)S(1)}, u32[]{:S(2)}, u32[]{:S(2)}) collective-permute-start(bf16[384,128]{1,0:T(8,128)(2,1)S(1)} %add_convert_fusion.10), channel_id=1, source_target_pairs={{0,4},{2,6},{4,0},{6,2},{8,12},{10,14},{12,8},{14,10},{1,5},{3,7},... | collective-permute-start | bytes 294920 | tf_op jit(solution)/shard_map/ppermute | solution.py:342
  150.0 5.8 %copy-done.7 = bf16[1024,8192]{1,0:T(8,128)(2,1)S(1)} copy-done((bf16[1024,8192]{1,0:T(8,128)(2,1)S(1)}, bf16[1024,8192]{1,0:T(8,128)(2,1)}, u32[]{:S(2)}) %copy-start.7) | copy-done | bytes 16777240
  155.8 3.0 %product.15 = bf16[640,1024]{1,0:T(8,128)(2,1)S(1)} custom-call(s32[1]{0:T(128)} %bitcast.5.at_ref, bf16[768,1024]{1,0:T(8,128)(2,1)S(1)} %bitcast.30, bf16[1024,8192]{1,0:T(8,128)(2,1)S(1)} %copy-done.7, bf16[640,1024]{1,0:T(8,128)(2,1)} %collective-permute-done.7.refs_0_), custom_call_target="tpu_custom_call" | custom-call | flops 1342177280 | bytes 6029312 | tf_op jit(solution)/shard_map/product/pallas_call | solution.py:167
  158.8 10.1 %collective-permute-done.4 = bf16[384,128]{1,0:T(8,128)(2,1)S(1)} collective-permute-done((bf16[384,128]{1,0:T(8,128)(2,1)S(1)}, bf16[384,128]{1,0:T(8,128)(2,1)S(1)}, u32[]{:S(2)}, u32[]{:S(2)}) %collective-permute-start.4) | collective-permute-done | bytes 98336 | tf_op jit(solution)/shard_map/ppermute | solution.py:342
  171.1 3.3 %add_convert_fusion.2 = bf16[640,1024]{1,0:T(8,128)(2,1)} fusion(bf16[640,1024]{1,0:T(8,128)(2,1)} %collective-permute-done.10, bf16[640,1024]{1,0:T(8,128)(2,1)} %product.17), kind=kLoop, calls=%fused_computation.2 | loop fusion | flops 2621440 | bytes 3932160 | tf_op jit(solution)/shard_map/convert_element_type | solution.py:274
  175.9 5.2 %collective-permute-start.5 = (bf16[384,128]{1,0:T(8,128)(2,1)S(1)}, bf16[384,128]{1,0:T(8,128)(2,1)S(1)}, u32[]{:S(2)}, u32[]{:S(2)}) collective-permute-start(bf16[384,128]{1,0:T(8,128)(2,1)S(1)} %add_convert_fusion.9), channel_id=1, source_target_pairs={{0,8},{2,10},{4,12},{6,14},{8,0},{10,2},{12,4},{14,6},{1,9},{3,11}... | collective-permute-start | bytes 294920 | tf_op jit(solution)/shard_map/ppermute | solution.py:342
  181.1 1.7 add_convert_fusion
  182.8 11.6 %collective-permute-start.8 = (bf16[640,1024]{1,0:T(8,128)(2,1)S(1)}, bf16[640,1024]{1,0:T(8,128)(2,1)}, u32[]{:S(2)}, u32[]{:S(2)}) collective-permute-start(bf16[640,1024]{1,0:T(8,128)(2,1)S(1)} %product.15), channel_id=1, source_target_pairs={{0,4},{12,8},{2,6},{14,10},{1,5},{13,9},{3,7},{15,11},{16,20},{28,... | collective-permute-start | bytes 3932168 | tf_op jit(solution)/shard_map/ppermute | solution.py:260
  194.4 1.7 collective-permute-start.11
  201.4 3.4 %copy-done.13 = bf16[64,64,1024]{2,1,0:T(8,128)(2,1)S(1)} copy-done((bf16[64,64,1024]{2,1,0:T(8,128)(2,1)S(1)}, bf16[64,64,1024]{2,1,0:T(8,128)(2,1)}, u32[]{:S(2)}) %copy-start.13) | copy-done | bytes 8388632
  204.8 4.2 %expand.2.refs_4_ = f32[768,1024]{1,0:T(8,128)S(1)} custom-call(s32[16]{0:T(128)S(1)} %select_reduce_fusion.3.index_ref, bf16[768,64]{1,0:T(8,128)(2,1)S(1)} %reshape.81.low_ref, s32[768,1]{1,0:T(8,128)S(1)} %broadcast_in_dim_tile.8.slot_ref, bf16[64,64,1024]{2,1,0:T(8,128)(2,1)S(1)} %copy-done.13, bf16[64,64,1024]{2,1,0:T(8,128)(2,1)S(1)} %copy-done.13, ...), custom_call_target="tpu_custom_call" | custom-call | flops 1610612736 | bytes 5242880 | tf_op jit(solution)/shard_map/expand/pallas_call | solution.py:132
  209.3 5.7 %expand.3.refs_1_ = f32[768,1024]{1,0:T(8,128)S(1)} custom-call(s32[16]{0:T(128)S(1)} %iota.17.index_ref, bf16[768,64]{1,0:T(8,128)(2,1)S(1)} %reshape.81.low_ref, s32[768,1]{1,0:T(8,128)S(1)} %copy-done.15, bf16[16,64,1024]{2,1,0:T(8,128)(2,1)} %collective-permute-done.6.refs_0_.refs_1_.refs_2_.refs_3_, ...), custom_call_target="tpu_custom_call" | custom-call | flops 1610612736 | bytes 5242880 | tf_op jit(solution)/shard_map/expand/pallas_call | solution.py:132
  215.0 3.4 %product.13.head_ref = f32[640,1024]{1,0:T(8,128)S(1)} custom-call(s32[1]{0:T(128)} %bitcast.1.at_ref, bf16[768,1024]{1,0:T(8,128)(2,1)S(1)} %bitcast.31, bf16[1024,8192]{1,0:T(8,128)(2,1)} %weight_ref.23, bf16[640,1024]{1,0:T(8,128)(2,1)} %collective-permute-done.refs_0_, f32[768,1024]{1,0:T(8,128)S(1)} %expand.3.refs_1_), custom_call_target="tpu_custom_call" | custom-call | flops 1342177280 | bytes 7340032 | tf_op jit(solution)/shard_map/product/pallas_call | solution.py:167
  219.5 7.2 %collective-permute-done.15.refs_2_ = bf16[640,1024]{1,0:T(8,128)(2,1)} collective-permute-done((bf16[640,1024]{1,0:T(8,128)(2,1)}, bf16[640,1024]{1,0:T(8,128)(2,1)}, u32[]{:S(2)}, u32[]{:S(2)}) %collective-permute-start.15) | collective-permute-done | bytes 1310752 | tf_op jit(solution)/shard_map/ppermute | solution.py:260
  226.7 4.9 %finish.1 = bf16[768,1024]{1,0:T(8,128)(2,1)} custom-call(f32[640,1024]{1,0:T(8,128)S(1)} %product.13.head_ref, bf16[640,1024]{1,0:T(8,128)(2,1)} %collective-permute-done.8.refs_0_, bf16[640,1024]{1,0:T(8,128)(2,1)} %collective-permute-done.11.refs_1_, bf16[640,1024]{1,0:T(8,128)(2,1)} %collective-permute-done.15.refs_2_, bf16[128,1024]{1,0:T(8,128)(2,1)S(1)} %fusion.refs_3_), custom_call_target="tpu_custom_call" | custom-call | flops 1966080 | bytes 7864320 | tf_op jit(solution)/shard_map/finish/pallas_call | solution.py:211
  (102 shorter events, 25.4 us)
Async XLA Ops:
  0.0 43.7 %collective-permute-start.1 = (s32[192]{0:T(256)}, s32[192]{0:T(256)S(1)}, u32[]{:S(2)}, u32[]{:S(2)}) collective-permute-start(s32[192]{0:T(256)} %param.7), channel_id=1, source_target_pairs={{0,1},{1,0},{2,3},{3,2},{4,5},{5,4},{6,7},{7,6},{8,9},{9,8},{10,11... | collective-permute-start | bytes 2312 | tf_op jit(solution)/shard_map/ppermute | solution.py:326
  1.7 5.8 %copy-start = (bf16[1024,8192]{1,0:T(8,128)(2,1)S(1)}, bf16[1024,8192]{1,0:T(8,128)(2,1)}, u32[]{:S(2)}) copy-start(bf16[1024,8192]{1,0:T(8,128)(2,1)} %weight_ref.23) | copy-start | bytes 50331652
  7.5 1.4 copy-start.8
  12.1 95.7 %collective-permute-start.19 = (bf16[128,2048]{1,0:T(8,128)(2,1)}, bf16[128,2048]{1,0:T(8,128)(2,1)}, u32[]{:S(2)}, u32[]{:S(2)}) collective-permute-start(bf16[128,2048]{1,0:T(8,128)(2,1)} %product.23), channel_id=1, source_target_pairs={{0,4},{12,8},{2,6},{14,10},{1,5},{13,9},{3,7},{15,11},{16,20},{28,... | collective-permute-start | bytes 1572872 | tf_op jit(solution)/shard_map/ppermute | solution.py:260
  17.4 6.1 %copy-start.9 = (bf16[4,192,1024]{2,1,0:T(8,128)(2,1)S(1)}, bf16[4,192,1024]{2,1,0:T(8,128)(2,1)}, u32[]{:S(2)}) copy-start(bf16[4,192,1024]{2,1,0:T(8,128)(2,1)} %param.6) | copy-start | bytes 4718596
  20.7 91.6 %collective-permute-start.17 = (bf16[128,2048]{1,0:T(8,128)(2,1)}, bf16[128,2048]{1,0:T(8,128)(2,1)}, u32[]{:S(2)}, u32[]{:S(2)}) collective-permute-start(bf16[128,2048]{1,0:T(8,128)(2,1)} %product.22), channel_id=1, source_target_pairs={{0,4},{12,8},{2,6},{14,10},{1,5},{13,9},{3,7},{15,11},{16,20},{28,... | collective-permute-start | bytes 1572872 | tf_op jit(solution)/shard_map/ppermute | solution.py:260
  23.5 5.8 %copy-start.1 = (bf16[1024,8192]{1,0:T(8,128)(2,1)S(1)}, bf16[1024,8192]{1,0:T(8,128)(2,1)}, u32[]{:S(2)}) copy-start(bf16[1024,8192]{1,0:T(8,128)(2,1)} %weight_ref.23) | copy-start | bytes 50331652
  32.0 64.9 %collective-permute-start.12 = (bf16[640,1024]{1,0:T(8,128)(2,1)}, bf16[640,1024]{1,0:T(8,128)(2,1)}, u32[]{:S(2)}, u32[]{:S(2)}) collective-permute-start(bf16[640,1024]{1,0:T(8,128)(2,1)} %product.18), channel_id=1, source_target_pairs={{0,2},{2,0},{4,6},{6,4},{8,10},{10,8},{12,14},{14,12},{1,3},{3,1},... | collective-permute-start | bytes 3932168 | tf_op jit(solution)/shard_map/ppermute | solution.py:253
  34.1 5.8 %copy-start.2 = (bf16[1024,8192]{1,0:T(8,128)(2,1)S(1)}, bf16[1024,8192]{1,0:T(8,128)(2,1)}, u32[]{:S(2)}) copy-start(bf16[1024,8192]{1,0:T(8,128)(2,1)} %weight_ref.23) | copy-start | bytes 50331652
  39.9 3.2 %copy-start.23 = (s32[192]{0:T(256)S(1)}, s32[192]{0:T(256)}, u32[]{:S(2)}) copy-start(s32[192]{0:T(256)} %param.7) | copy-start | bytes 2308
  42.6 73.4 %collective-permute-start.9 = (bf16[640,1024]{1,0:T(8,128)(2,1)}, bf16[640,1024]{1,0:T(8,128)(2,1)}, u32[]{:S(2)}, u32[]{:S(2)}) collective-permute-start(bf16[640,1024]{1,0:T(8,128)(2,1)} %product.16), channel_id=1, source_target_pairs={{0,2},{2,0},{4,6},{6,4},{8,10},{10,8},{12,14},{14,12},{1,3},{3,1},... | collective-permute-start | bytes 3932168 | tf_op jit(solution)/shard_map/ppermute | solution.py:253
  44.1 3.4 %copy-start.10 = (bf16[64,64,1024]{2,1,0:T(8,128)(2,1)S(1)}, bf16[64,64,1024]{2,1,0:T(8,128)(2,1)}, u32[]{:S(2)}) copy-start(bf16[64,64,1024]{2,1,0:T(8,128)(2,1)} %down_ref.1) | copy-start | bytes 25165828
  47.5 3.4 %copy-start.12 = (bf16[64,64,1024]{2,1,0:T(8,128)(2,1)S(1)}, bf16[64,64,1024]{2,1,0:T(8,128)(2,1)}, u32[]{:S(2)}) copy-start(bf16[64,64,1024]{2,1,0:T(8,128)(2,1)} %refs_3_.3) | copy-start | bytes 25165828
  59.2 62.0 %collective-permute-start.2 = (bf16[16,64,1024]{2,1,0:T(8,128)(2,1)}, bf16[16,64,1024]{2,1,0:T(8,128)(2,1)}, u32[]{:S(2)}, u32[]{:S(2)}) collective-permute-start(bf16[16,64,1024]{2,1,0:T(8,128)(2,1)} %get-tuple-element.7), channel_id=1, source_target_pairs={{0,1},{1,0},{2,3},{3,2},{4,5},{5,4},{6,7},{7,6},{8,9},{9,8},{10,11... | collective-permute-start | bytes 6291464 | tf_op jit(solution)/shard_map/ppermute | solution.py:331
  59.9 5.8 %copy-start.3 = (bf16[1024,8192]{1,0:T(8,128)(2,1)S(1)}, bf16[1024,8192]{1,0:T(8,128)(2,1)}, u32[]{:S(2)}) copy-start(bf16[1024,8192]{1,0:T(8,128)(2,1)} %weight_ref.23) | copy-start | bytes 50331652
  69.1 5.8 %copy-start.4 = (bf16[1024,8192]{1,0:T(8,128)(2,1)S(1)}, bf16[1024,8192]{1,0:T(8,128)(2,1)}, u32[]{:S(2)}) copy-start(bf16[1024,8192]{1,0:T(8,128)(2,1)} %weight_ref.23) | copy-start | bytes 50331652
  82.1 5.8 %copy-start.5 = (bf16[1024,8192]{1,0:T(8,128)(2,1)S(1)}, bf16[1024,8192]{1,0:T(8,128)(2,1)}, u32[]{:S(2)}) copy-start(bf16[1024,8192]{1,0:T(8,128)(2,1)} %weight_ref.23) | copy-start | bytes 50331652
  90.2 3.4 %copy-start.11 = (bf16[64,64,1024]{2,1,0:T(8,128)(2,1)S(1)}, bf16[64,64,1024]{2,1,0:T(8,128)(2,1)}, u32[]{:S(2)}) copy-start(bf16[64,64,1024]{2,1,0:T(8,128)(2,1)} %down_ref.1) | copy-start | bytes 25165828
  93.5 3.4 %copy-start.16 = (bf16[128,2048]{1,0:T(8,128)(2,1)}, bf16[128,2048]{1,0:T(8,128)(2,1)S(1)}, u32[]{:S(2)}) copy-start(bf16[128,2048]{1,0:T(8,128)(2,1)S(1)} %product.20) | copy-start | bytes 1572868
  96.9 77.4 %collective-permute-start.16 = (bf16[128,2048]{1,0:T(8,128)(2,1)}, bf16[128,2048]{1,0:T(8,128)(2,1)}, u32[]{:S(2)}, u32[]{:S(2)}) collective-permute-start(bf16[128,2048]{1,0:T(8,128)(2,1)} %product.21), channel_id=1, source_target_pairs={{0,4},{12,8},{2,6},{14,10},{1,5},{13,9},{3,7},{15,11},{16,20},{28,... | collective-permute-start | bytes 1572872 | tf_op jit(solution)/shard_map/ppermute | solution.py:260
  99.1 5.8 %copy-start.6 = (bf16[1024,8192]{1,0:T(8,128)(2,1)S(1)}, bf16[1024,8192]{1,0:T(8,128)(2,1)}, u32[]{:S(2)}) copy-start(bf16[1024,8192]{1,0:T(8,128)(2,1)} %weight_ref.23) | copy-start | bytes 50331652
  107.8 31.0 %collective-permute-start.13 = (bf16[640,1024]{1,0:T(8,128)(2,1)S(1)}, bf16[640,1024]{1,0:T(8,128)(2,1)}, u32[]{:S(2)}, u32[]{:S(2)}) collective-permute-start(bf16[640,1024]{1,0:T(8,128)(2,1)S(1)} %product.19), channel_id=1, source_target_pairs={{0,4},{12,8},{2,6},{14,10},{1,5},{13,9},{3,7},{15,11},{16,20},{28,... | collective-permute-start | bytes 3932168 | tf_op jit(solution)/shard_map/ppermute | solution.py:260
  112.3 33.5 %collective-permute-start.7 = (bf16[640,1024]{1,0:T(8,128)(2,1)}, bf16[640,1024]{1,0:T(8,128)(2,1)}, u32[]{:S(2)}, u32[]{:S(2)}) collective-permute-start(bf16[640,1024]{1,0:T(8,128)(2,1)} %product.14), channel_id=1, source_target_pairs={{0,2},{2,0},{4,6},{6,4},{8,10},{10,8},{12,14},{14,12},{1,3},{3,1},... | collective-permute-start | bytes 3932168 | tf_op jit(solution)/shard_map/ppermute | solution.py:253
  116.0 26.3 %collective-permute-start.20 = (bf16[128,2048]{1,0:T(8,128)(2,1)}, bf16[128,2048]{1,0:T(8,128)(2,1)}, u32[]{:S(2)}, u32[]{:S(2)}) collective-permute-start(bf16[128,2048]{1,0:T(8,128)(2,1)} %add_convert_fusion.5), channel_id=1, source_target_pairs={{4,8},{8,4},{6,10},{10,6},{5,9},{9,5},{7,11},{11,7},{20,24},{24,20... | collective-permute-start | bytes 1572872 | tf_op jit(solution)/shard_map/ppermute | solution.py:260
  117.4 6.1 %copy-start.14 = (s32[768,1]{1,0:T(8,128)S(1)}, s32[768,1]{1,0:T(8,128)}, u32[]{:S(2)}) copy-start(s32[768,1]{1,0:T(8,128)} %broadcast_in_dim_tile.9.slot_ref) | copy-start | bytes 9220
  121.2 48.4 %collective-permute-start.10 = (bf16[640,1024]{1,0:T(8,128)(2,1)}, bf16[640,1024]{1,0:T(8,128)(2,1)}, u32[]{:S(2)}, u32[]{:S(2)}) collective-permute-start(bf16[640,1024]{1,0:T(8,128)(2,1)} %product.17), channel_id=1, source_target_pairs={{0,4},{12,8},{2,6},{14,10},{1,5},{13,9},{3,7},{15,11},{16,20},{28,... | collective-permute-start | bytes 3932168 | tf_op jit(solution)/shard_map/ppermute | solution.py:260
  138.8 7.0 %collective-permute-start.3 = (bf16[384,128]{1,0:T(8,128)(2,1)}, bf16[384,128]{1,0:T(8,128)(2,1)S(1)}, u32[]{:S(2)}, u32[]{:S(2)}) collective-permute-start(bf16[384,128]{1,0:T(8,128)(2,1)} %reshape.80), channel_id=1, source_target_pairs={{0,2},{2,0},{4,6},{6,4},{8,10},{10,8},{12,14},{14,12},{1,3},{3,1},... | collective-permute-start | bytes 294920 | tf_op jit(solution)/shard_map/ppermute | solution.py:342
  142.2 3.6 %copy-start.21 = (bf16[384,128]{1,0:T(8,128)(2,1)S(1)}, bf16[384,128]{1,0:T(8,128)(2,1)}, u32[]{:S(2)}) copy-start(bf16[384,128]{1,0:T(8,128)(2,1)} %reshape.80) | copy-start | bytes 294916
  142.2 33.7 %collective-permute-start.14 = (bf16[640,1024]{1,0:T(8,128)(2,1)S(1)}, bf16[640,1024]{1,0:T(8,128)(2,1)S(1)}, u32[]{:S(2)}, u32[]{:S(2)}) collective-permute-start(bf16[640,1024]{1,0:T(8,128)(2,1)S(1)} %add_convert_fusion.1), channel_id=1, source_target_pairs={{4,8},{8,4},{6,10},{10,6},{5,9},{9,5},{7,11},{11,7},{20,24},{24,20... | collective-permute-start | bytes 3932168 | tf_op jit(solution)/shard_map/ppermute | solution.py:260
  145.8 63.2 %collective-permute-start.6 = (bf16[16,64,1024]{2,1,0:T(8,128)(2,1)}, bf16[16,64,1024]{2,1,0:T(8,128)(2,1)}, u32[]{:S(2)}, u32[]{:S(2)}) collective-permute-start(bf16[16,64,1024]{2,1,0:T(8,128)(2,1)} %get-tuple-element.8), channel_id=1, source_target_pairs={{0,1},{1,0},{2,3},{3,2},{4,5},{5,4},{6,7},{7,6},{8,9},{9,8},{10,11... | collective-permute-start | bytes 6291464 | tf_op jit(solution)/shard_map/ppermute | solution.py:331
  145.9 23.0 %collective-permute-start.4 = (bf16[384,128]{1,0:T(8,128)(2,1)S(1)}, bf16[384,128]{1,0:T(8,128)(2,1)S(1)}, u32[]{:S(2)}, u32[]{:S(2)}) collective-permute-start(bf16[384,128]{1,0:T(8,128)(2,1)S(1)} %add_convert_fusion.10), channel_id=1, source_target_pairs={{0,4},{2,6},{4,0},{6,2},{8,12},{10,14},{12,8},{14,10},{1,5},{3,7},... | collective-permute-start | bytes 294920 | tf_op jit(solution)/shard_map/ppermute | solution.py:342
  150.0 5.8 %copy-start.7 = (bf16[1024,8192]{1,0:T(8,128)(2,1)S(1)}, bf16[1024,8192]{1,0:T(8,128)(2,1)}, u32[]{:S(2)}) copy-start(bf16[1024,8192]{1,0:T(8,128)(2,1)} %weight_ref.23) | copy-start | bytes 50331652
  155.8 13.1 %copy-start.20 = (bf16[128,2048]{1,0:T(8,128)(2,1)S(1)}, bf16[128,2048]{1,0:T(8,128)(2,1)}, u32[]{:S(2)}) copy-start(bf16[128,2048]{1,0:T(8,128)(2,1)} %add_convert_fusion.6) | copy-start | bytes 1572868
  168.9 14.0 %collective-permute-start.18 = (bf16[128,2048]{1,0:T(8,128)(2,1)S(1)}, bf16[128,2048]{1,0:T(8,128)(2,1)S(1)}, u32[]{:S(2)}, u32[]{:S(2)}) collective-permute-start(bf16[128,2048]{1,0:T(8,128)(2,1)S(1)} %copy-done.20), channel_id=1, source_target_pairs={{4,8},{8,4},{6,10},{10,6},{5,9},{9,5},{7,11},{11,7},{20,24},{24,20... | collective-permute-start | bytes 1572872 | tf_op jit(solution)/shard_map/ppermute | solution.py:260
  169.6 24.8 %collective-permute-start.21 = (bf16[128,2048]{1,0:T(8,128)(2,1)S(1)}, bf16[128,2048]{1,0:T(8,128)(2,1)S(1)}, u32[]{:S(2)}, u32[]{:S(2)}) collective-permute-start(bf16[128,2048]{1,0:T(8,128)(2,1)S(1)} %add_convert_fusion.4), channel_id=1, source_target_pairs={{8,12},{4,0},{10,14},{6,2},{9,13},{5,1},{11,15},{7,3},{24,28},{20,... | collective-permute-start | bytes 1572872 | tf_op jit(solution)/shard_map/ppermute | solution.py:260
  174.4 23.0 %copy-start.17 = (bf16[128,2048]{1,0:T(8,128)(2,1)S(1)}, bf16[128,2048]{1,0:T(8,128)(2,1)}, u32[]{:S(2)}) copy-start(bf16[128,2048]{1,0:T(8,128)(2,1)} %copy-done.16) | copy-start | bytes 1572868
  174.4 40.6 %collective-permute-start = (bf16[640,1024]{1,0:T(8,128)(2,1)}, bf16[640,1024]{1,0:T(8,128)(2,1)}, u32[]{:S(2)}, u32[]{:S(2)}) collective-permute-start(bf16[640,1024]{1,0:T(8,128)(2,1)} %product.12), channel_id=1, source_target_pairs={{0,2},{2,0},{4,6},{6,4},{8,10},{10,8},{12,14},{14,12},{1,3},{3,1},... | collective-permute-start | bytes 3932168 | tf_op jit(solution)/shard_map/ppermute | solution.py:253
  175.9 20.2 %collective-permute-start.5 = (bf16[384,128]{1,0:T(8,128)(2,1)S(1)}, bf16[384,128]{1,0:T(8,128)(2,1)S(1)}, u32[]{:S(2)}, u32[]{:S(2)}) collective-permute-start(bf16[384,128]{1,0:T(8,128)(2,1)S(1)} %add_convert_fusion.9), channel_id=1, source_target_pairs={{0,8},{2,10},{4,12},{6,14},{8,0},{10,2},{12,4},{14,6},{1,9},{3,11}... | collective-permute-start | bytes 294920 | tf_op jit(solution)/shard_map/ppermute | solution.py:342
  182.8 36.6 %collective-permute-start.8 = (bf16[640,1024]{1,0:T(8,128)(2,1)S(1)}, bf16[640,1024]{1,0:T(8,128)(2,1)}, u32[]{:S(2)}, u32[]{:S(2)}) collective-permute-start(bf16[640,1024]{1,0:T(8,128)(2,1)S(1)} %product.15), channel_id=1, source_target_pairs={{0,4},{12,8},{2,6},{14,10},{1,5},{13,9},{3,7},{15,11},{16,20},{28,... | collective-permute-start | bytes 3932168 | tf_op jit(solution)/shard_map/ppermute | solution.py:260
  194.4 25.1 %collective-permute-start.11 = (bf16[640,1024]{1,0:T(8,128)(2,1)}, bf16[640,1024]{1,0:T(8,128)(2,1)}, u32[]{:S(2)}, u32[]{:S(2)}) collective-permute-start(bf16[640,1024]{1,0:T(8,128)(2,1)} %add_convert_fusion.2), channel_id=1, source_target_pairs={{4,8},{8,4},{6,10},{10,6},{5,9},{9,5},{7,11},{11,7},{20,24},{24,20... | collective-permute-start | bytes 3932168 | tf_op jit(solution)/shard_map/ppermute | solution.py:260
  196.1 30.6 %collective-permute-start.15 = (bf16[640,1024]{1,0:T(8,128)(2,1)}, bf16[640,1024]{1,0:T(8,128)(2,1)}, u32[]{:S(2)}, u32[]{:S(2)}) collective-permute-start(bf16[640,1024]{1,0:T(8,128)(2,1)} %add_convert_fusion), channel_id=1, source_target_pairs={{8,12},{4,0},{10,14},{6,2},{9,13},{5,1},{11,15},{7,3},{24,28},{20,... | collective-permute-start | bytes 3932168 | tf_op jit(solution)/shard_map/ppermute | solution.py:260
  198.8 0.9 copy-start.18
  201.4 3.4 %copy-start.13 = (bf16[64,64,1024]{2,1,0:T(8,128)(2,1)S(1)}, bf16[64,64,1024]{2,1,0:T(8,128)(2,1)}, u32[]{:S(2)}) copy-start(bf16[64,64,1024]{2,1,0:T(8,128)(2,1)} %refs_3_.3) | copy-start | bytes 25165828
  204.8 4.2 %copy-start.22 = (bf16[128,1024]{1,0:T(8,128)(2,1)S(1)}, bf16[128,1024]{1,0:T(8,128)(2,1)}, u32[]{:S(2)}) copy-start(bf16[128,1024]{1,0:T(8,128)(2,1)} %constant_dynamic-slice_fusion) | copy-start | bytes 786436
  204.8 4.6 %copy-start.15 = (s32[768,1]{1,0:T(8,128)S(1)}, s32[768,1]{1,0:T(8,128)}, u32[]{:S(2)}) copy-start(s32[768,1]{1,0:T(8,128)} %broadcast_in_dim_tile.9.slot_ref) | copy-start | bytes 9220
  209.0 9.4 %collective-permute-start.22 = (bf16[128,1024]{1,0:T(8,128)(2,1)S(1)}, bf16[128,1024]{1,0:T(8,128)(2,1)S(1)}, u32[]{:S(2)}, u32[]{:S(2)}) collective-permute-start(bf16[128,1024]{1,0:T(8,128)(2,1)S(1)} %copy-done.22), channel_id=1, source_target_pairs={{0,2},{2,0},{4,6},{6,4},{8,10},{10,8},{12,14},{14,12},{1,3},{3,1},... | collective-permute-start | bytes 786440 | tf_op jit(solution)/shard_map/ppermute | solution.py:253
  215.0 3.4 %copy-start.19 = (bf16[128,2048]{1,0:T(8,128)(2,1)S(1)}, bf16[128,2048]{1,0:T(8,128)(2,1)}, u32[]{:S(2)}) copy-start(bf16[128,2048]{1,0:T(8,128)(2,1)} %copy-done.18) | copy-start | bytes 1572868

commit v3 on v0

v3 whole, which is shorter than its diff:
```python
import jax
import jax.numpy as jnp
import numpy as np
from jax import lax
from jax.experimental import pallas as pl
from jax.experimental.pallas import tpu as pltpu
from jax.sharding import PartitionSpec as P

SLOTS = 16
GROUP = 4
VMEM = 60 * 2**20
ANY = pl.BlockSpec(memory_space=pl.ANY)


def call(kernel, operands, after, *, grid, in_specs, out_specs, out_shape, name, prefetch=0, scratch=(), alias=None):
    inputs, extra = len(operands), len(after)

    def body(*refs):
        kernel(*refs[:inputs], *refs[inputs + extra :])

    return pl.pallas_call(
        body,
        grid_spec=pltpu.PrefetchScalarGridSpec(
            num_scalar_prefetch=prefetch,
            grid=grid,
            in_specs=list(in_specs) + [ANY] * extra,
            out_specs=out_specs,
            scratch_shapes=list(scratch),
        ),
        out_shape=out_shape,
        input_output_aliases=alias or {},
        compiler_params=pltpu.CompilerParams(vmem_limit_bytes=VMEM),
        cost_estimate=pl.CostEstimate(flops=1, transcendentals=0, bytes_accessed=1),
        name=name,
    )(*operands, *after)


def hold(value, after):
    def kernel(value_ref, out_ref):
        pass

    return call(
        kernel, [value], after, grid=(), in_specs=[ANY], out_specs=ANY,
        out_shape=jax.ShapeDtypeStruct(value.shape, value.dtype), name="hold",
        alias={0: 0},
    )


def lane_pick(slot_ref, repeats, shape, rank, first):
    slot = jnp.concatenate([slot_ref[...]] * repeats, axis=0)
    return slot == lax.broadcasted_iota(jnp.int32, shape, 1) // rank + first


def low_rank(row_sets, slot_sets, maps, index, after=()):
    sets = len(row_sets)
    count, width = row_sets[0].shape
    rank = maps.shape[1]
    wide = GROUP * rank
    steps = index.shape[0] // sets // GROUP
    repeats = count // slot_sets[0].shape[0]
    half = count // 2

    def kernel(index_ref, *refs):
        row_refs, slot_refs, map_refs = refs[:sets], refs[sets : 2 * sets], refs[2 * sets : 2 * sets + GROUP]
        out_ref, acc = refs[-2], refs[-1]
        i = pl.program_id(1)
        blocks = jnp.concatenate([ref[0] for ref in map_refs], axis=0)
        for s in range(sets):

            @pl.when(pl.program_id(0) == s)
            def _():
                scores = lax.dot_general(
                    row_refs[s][...], blocks, (((1,), (1,)), ((), ())), preferred_element_type=jnp.float32
                )
                pick = lane_pick(slot_refs[s], repeats, (count, wide), rank, i * GROUP)
                term = jnp.where(pick, scores, 0.0)

                @pl.when(i == 0)
                def _():
                    acc[...] = term

                @pl.when(i > 0)
                def _():
                    acc[...] += term

        @pl.when(i == steps - 1)
        def _():
            summed = acc[:, 0:rank]
            for g in range(1, GROUP):
                summed += acc[:, g * rank : (g + 1) * rank]
            summed = jnp.concatenate([summed[:half], summed[half:]], axis=1)
            out_ref[...] = summed.astype(out_ref.dtype)

    def map_spec(g):
        return pl.BlockSpec((1, rank, width), lambda s, i, index: (index[(s * steps + i) * GROUP + g], 0, 0))

    def whole(array):
        return pl.BlockSpec(array.shape, lambda s, i, index: (0, 0))

    return call(
        kernel, [index, *row_sets, *slot_sets] + [maps] * GROUP, after, prefetch=1, grid=(sets, steps),
        in_specs=[whole(rows) for rows in row_sets]
        + [whole(slot) for slot in slot_sets]
        + [map_spec(g) for g in range(GROUP)],
        out_specs=pl.BlockSpec((half, 2 * rank), lambda s, i, index: (s, 0)),
        out_shape=jax.ShapeDtypeStruct((sets * half, 2 * rank), jnp.bfloat16),
        scratch=[pltpu.VMEM((count, wide), jnp.float32)],
        name="low_rank",
    )


def expand(low, slot_sets, maps, index, after=()):
    sets = len(slot_sets)
    rank, width = maps.shape[1:]
    half = low.shape[0] // sets
    count = 2 * half
    wide = GROUP * rank
    steps = index.shape[0] // sets // GROUP
    repeats = count // slot_sets[0].shape[0]

    def kernel(index_ref, low_ref, *refs):
        slot_refs, map_refs = refs[:sets], refs[sets : sets + GROUP]
        out_refs, acc = refs[sets + GROUP : -1], refs[-1]
        i = pl.program_id(1)
        blocks = jnp.concatenate([ref[0] for ref in map_refs], axis=0)
        packed = low_ref[...]
        tiled = jnp.concatenate([packed[:, :rank]] * GROUP, axis=1)
        tiled = jnp.concatenate([tiled, jnp.concatenate([packed[:, rank:]] * GROUP, axis=1)], axis=0)
        for s in range(sets):

            @pl.when(pl.program_id(0) == s)
            def _():
                pick = lane_pick(slot_refs[s], repeats, (count, wide), rank, i * GROUP)
                picked = jnp.where(pick, tiled, jnp.zeros_like(tiled))
                term = jnp.dot(picked, blocks, preferred_element_type=jnp.float32)

                @pl.when(i == 0)
                def _():
                    acc[...] = term

                @pl.when((i > 0) & (i < steps - 1))
                def _():
                    acc[...] += term

                @pl.when(i == steps - 1)
                def _():
                    out_refs[s][...] = (acc[...] + term).astype(out_refs[s].dtype)

    def map_spec(g):
        return pl.BlockSpec((1, rank, width), lambda s, i, index: (index[(s * steps + i) * GROUP + g], 0, 0))

    whole = pl.BlockSpec((count, width), lambda s, i, index: (0, 0))
    return call(
        kernel, [index, low, *slot_sets] + [maps] * GROUP, after, prefetch=1, grid=(sets, steps),
        in_specs=[pl.BlockSpec((half, 2 * rank), lambda s, i, index: (s, 0))]
        + [pl.BlockSpec(slot.shape, lambda s, i, index: (0, 0)) for slot in slot_sets]
        + [map_spec(g) for g in range(GROUP)],
        out_specs=[whole] * sets,
        out_shape=[
            jax.ShapeDtypeStruct((count, width), jnp.bfloat16 if s else jnp.float32) for s in range(sets)
        ],
        scratch=[pltpu.VMEM((count, width), jnp.float32)],
        name="expand",
    )


def products(rows, weight, at, after=()):
    width = rows.shape[1]
    count = first_rows(rows)
    blocks = at.shape[0]
    size = weight.shape[1] // lax.axis_size("tensor")
    tile = min(512, size)
    half = size // tile

    def kernel(at_ref, rows_ref, weight_ref, *out_refs):
        value = jnp.dot(rows_ref[...], weight_ref[...], preferred_element_type=jnp.float32)
        value = value.astype(rows.dtype)
        for b in range(blocks):

            @pl.when(pl.program_id(0) // half == b)
            def _():
                out_refs[b][...] = value

    def out_spec(b):
        return pl.BlockSpec((count, tile), lambda i, at: (0, jnp.clip(i - b * half, 0, half - 1)))

    return call(
        kernel, [at, rows, weight], after, prefetch=1, grid=(blocks * half,),
        in_specs=[
            pl.BlockSpec((count, width), lambda i, at: (0, 0)),
            pl.BlockSpec((width, tile), lambda i, at: (0, at[i // half] * half + i % half)),
        ],
        out_specs=[out_spec(b) for b in range(blocks)],
        out_shape=[jax.ShapeDtypeStruct((count, size), rows.dtype)] * blocks,
        name="products",
    )


def few_products(rows, weight, at, after=()):
    width = rows.shape[1]
    few = rows.shape[0] - first_rows(rows)
    pairs = at.shape[0]
    size = 2 * weight.shape[1] // lax.axis_size("tensor")
    tile = min(1024, size)
    half = size // tile

    def kernel(at_ref, rows_ref, weight_ref, sent_ref, kept_ref):
        value = jnp.dot(rows_ref[...], weight_ref[...], preferred_element_type=jnp.float32)
        value = value.astype(rows.dtype)

        @pl.when(pl.program_id(0) < pairs - 1)
        def _():
            sent_ref[...] = value

        @pl.when(pl.program_id(0) == pairs - 1)
        def _():
            kept_ref[...] = value

    def sent_at(b, i, at):
        done = b == pairs - 1
        return (jnp.where(done, pairs - 2, b), jnp.where(done, half - 1, i))

    return call(
        kernel, [at, rows, weight], after, prefetch=1, grid=(pairs, half),
        in_specs=[
            pl.BlockSpec((few, width), lambda b, i, at: (rows.shape[0] // few - 1, 0)),
            pl.BlockSpec((width, tile), lambda b, i, at: (0, at[b] * half + i)),
        ],
        out_specs=[
            pl.BlockSpec((few, tile), sent_at),
            pl.BlockSpec((few, tile), lambda b, i, at: (0, jnp.where(b == pairs - 1, i, 0))),
        ],
        out_shape=[
            jax.ShapeDtypeStruct(((pairs - 1) * few, size), rows.dtype),
            jax.ShapeDtypeStruct((few, size), rows.dtype),
        ],
        name="few_products",
    )


def first_rows(rows):
    return rows.shape[0] - rows.shape[0] // 6


def total(terms, tile=128, dtype=jnp.bfloat16, after=()):
    blocks = len(terms[0][1])
    width = terms[0][0].shape[1]
    table = np.asarray([list(places) for _, places in terms], np.int32)

    def kernel(table_ref, *refs):
        value = refs[0][...].astype(jnp.float32)
        for ref in refs[1:-1]:
            value += ref[...].astype(jnp.float32)
        refs[-1][...] = value.astype(dtype)

    def spec(t):
        return pl.BlockSpec((tile, width), lambda i, table: (table[t, i], 0))

    return call(
        kernel, [jnp.asarray(table)] + [term for term, _ in terms], after, prefetch=1, grid=(blocks,),
        in_specs=[spec(t) for t in range(len(terms))],
        out_specs=pl.BlockSpec((tile, width), lambda i, table: (i, 0)),
        out_shape=jax.ShapeDtypeStruct((blocks * tile, width), dtype),
        name="total",
    )


def finish(head, arrived, tail):
    high, width = head.shape
    low = tail.shape[0]
    blocks = high // low

    def kernel(head_ref, *refs):
        tail_ref, out_ref = refs[-2], refs[-1]
        i = pl.program_id(0)

        @pl.when(i < blocks)
        def _():
            value = head_ref[...]
            for ref in refs[:-2]:
                value += ref[...].astype(jnp.float32)
            out_ref[...] = value.astype(out_ref.dtype)

        @pl.when(i == blocks)
        def _():
            out_ref[...] = tail_ref[...]

    spec = pl.BlockSpec((low, width), lambda i: (jnp.minimum(i, blocks - 1), 0))
    return call(
        kernel, [head, *arrived, tail], (), grid=(blocks + 1,),
        in_specs=[spec] * (1 + len(arrived)) + [pl.BlockSpec((low, width), lambda i: (0, 0))],
        out_specs=pl.BlockSpec((low, width), lambda i: (i, 0)),
        out_shape=jax.ShapeDtypeStruct((high + low, width), tail.dtype),
        name="finish",
    )


def line_plan(nz):
    order = np.zeros((nz, nz), np.int32)
    for z in range(nz):
        def need(j):
            if j == z:
                return (2 * nz, 0)
            return (nz - 1 - j + z, j) if j > z else (nz - 1 - z + j, nz - j)

        order[z] = sorted(range(nz), key=need)
    return order


def on_device(attention_result, tenant, projection_weight, adapter_down_maps, adapter_up_maps):
    steps, row_count, width = attention_result.shape
    local_adapters = adapter_down_maps.shape[0]
    owners = lax.axis_size("dp")
    me = lax.axis_index("dp")
    n = lax.axis_size("tensor")
    nz = n // 2
    place = lax.axis_index("tensor")
    z, y = place // 2, place % 2
    order = line_plan(nz)
    my_order = jnp.asarray(order)[z]
    out_width = projection_weight.shape[1] // n

    def swap_y(value):
        return lax.ppermute(value, "tensor", [(t, t ^ 1) for t in range(n)])

    def hop(value, h):
        pairs = []
        for side in range(2):
            pairs.append((h * 2 + side, (h + 1) * 2 + side))
            pairs.append(((nz - 1 - h) * 2 + side, (nz - 2 - h) * 2 + side))
        return lax.ppermute(value, "tensor", pairs)

    def slot_of(h, m):
        return list(order[h]).index(nz - 1 - m)

    rows = attention_result.reshape(steps * row_count, width)
    total_rows = steps * row_count
    most = first_rows(rows)
    few = total_rows - most
    last = [()]

    def then(kernel, *operands, **options):
        out = kernel(*operands, after=last[0], **options)
        last[0] = (out[0] if isinstance(out, (tuple, list)) else out,)
        return out

    slot_range = jnp.arange(SLOTS, dtype=jnp.int32)
    ids = jnp.arange(local_adapters, dtype=jnp.int32)

    def slots(row_ids, owner):
        hit = row_ids[:, None] - owner * local_adapters == ids[None, :]
        used = jnp.any(hit, axis=0)
        position = jnp.sum(
            (used[None, :] & (ids[None, :] < ids[:, None])).astype(jnp.int32), axis=1
        )
        names = jnp.sum(
            jnp.where(used[None, :] & (position[None, :] == slot_range[:, None]), ids[None, :], 0),
            axis=1,
        )
        row_slot = jnp.sum(jnp.where(hit, position[None, :] + 1, 0), axis=1) - 1
        return names, row_slot[:, None]

    away = [my_order[k] * 2 + 1 - y for k in range(nz)]
    own = [my_order[k] * 2 + y for k in range(nz)]
    every = range(most // 128)
    held_y, own_part, from_y, arrived = {}, {}, {}, {}

    def multiply(aways, owns):
        at = jnp.stack([away[k] for k in aways] + [own[k] for k in owns])
        parts = then(products, rows, projection_weight, at)
        held_y.update(zip(aways, parts))
        own_part.update(zip(owns, parts[len(aways) :]))

    def line(h, m):
        k = slot_of(h, m)
        terms = [(own_part[k], every), (from_y[k], every)]
        if h:
            terms.append((arrived[h - 1, m], every))
        arrived[h, m] = hop(then(total, terms), h)

    few_arrived = []

    def few_line():
        h = len(few_arrived)
        if h == 0:
            few_arrived.append(hop(few_sent, 0))
        else:
            blocks = range(nz - 1 - h)
            terms = [(few_sent, [slot_of(h, m) for m in blocks]), (few_arrived[h - 1], blocks)]
            few_arrived.append(hop(then(total, terms, few), h))

    def pass_on(value, shift):
        return lax.ppermute(value, "dp", [(i, (i + shift) % owners) for i in range(owners)])

    row_ids = [tenant] + [pass_on(tenant, shift) for shift in range(1, owners)]
    row_sets = [rows] + [pass_on(rows, shift) for shift in range(1, owners)]
    multiply([0], [])
    from_y[0] = swap_y(held_y[0])
    few_sent, few_kept = then(few_products, rows, projection_weight, my_order)
    few_line()
    named = [slots(some_ids, me) for some_ids in row_ids]
    names = jnp.concatenate([which for which, _ in named])
    slot_sets = [row_slot for _, row_slot in named]
    low = then(low_rank, row_sets, slot_sets, adapter_down_maps, names)
    swaps = []
    while 1 << len(swaps) < n:
        swaps.append(1 << len(swaps))

    def low_step():
        nonlocal low
        if swaps:
            bit = swaps.pop(0)
            other = lax.ppermute(low, "tensor", [(t, t ^ bit) for t in range(n)])
            blocks = range(low.shape[0] // 128)
            low = then(total, [(low, blocks), (other, blocks)])

    multiply([1], [0])
    from_y[1] = swap_y(held_y[1])
    multiply(range(2, nz), range(1, nz))
    started = 2

    def start_y():
        nonlocal started
        if started < nz:
            from_y[started] = swap_y(hold(held_y[started], last[0]))
            started += 1

    low_step()
    line(0, 0)
    start_y()
    few_line()
    deltas = None
    for when in range(1, 2 * nz - 3):
        low_step()
        if not swaps and deltas is None:
            deltas = then(expand, low, slot_sets, adapter_up_maps, names)
        for h in range(nz - 1):
            if 0 <= when - h < nz - 1 - h:
                line(h, when - h)
                if h == 0:
                    start_y()
        if len(few_arrived) < nz - 1:
            few_line()
    while len(few_arrived) < nz - 1:
        few_line()
    while swaps:
        low_step()
    if deltas is None:
        deltas = then(expand, low, slot_sets, adapter_up_maps, names)
    delta = [deltas[0]] + [pass_on(deltas[shift], -shift) for shift in range(1, owners)]
    few_sum = then(
        total, [(few_kept, [0])] + [(few_arrived[h], [nz - 2 - h]) for h in range(nz - 1)], few
    )
    few_away = lax.dynamic_slice(few_sum, (0, (1 - y) * out_width), (few, out_width))
    few_own = lax.dynamic_slice(few_sum, (0, y * out_width), (few, out_width))
    few_other = swap_y(few_away)
    few_out = few_own.astype(jnp.float32) + few_other.astype(jnp.float32)
    for term in delta:
        few_out = few_out + term[most:].astype(jnp.float32)
    terms = [(own_part[nz - 1], every), (from_y[nz - 1], every)] + [(term, every) for term in delta]
    head = then(total, terms, 128, jnp.float32)
    out = finish(head, [arrived[h, nz - 2 - h] for h in range(nz - 1)], few_out.astype(jnp.bfloat16))
    return out.reshape(steps, row_count, out_width)


def solution(mesh):
    placed = (
        P(None, ("groups", "dp"), "tensor"),
        P(("groups", "dp")),
        P("tensor", None),
        P(("groups", "dp"), None, "tensor"),
        P(("groups", "dp"), None, "tensor"),
    )
    return jax.shard_map(
        on_device,
        mesh=mesh,
        in_specs=placed,
        out_specs=P(None, ("groups", "dp"), "tensor"),
        check_vma=False,
    )
```

time: 353 us -> 251 us (0.71)
  waiting for transfers between devices: 244 us -> 72 us
  Pallas kernels: 0 us -> 130 us
  matrix products: 74.6 us -> 0 us
  starting transfers between devices: 6.01 us -> 28.1 us
  between operations: 14.1 us -> 2.71 us
  blocking collectives: 10.1 us -> 0 us
  local copies, waits for them, and re-layouts: 2.43 us -> 11.8 us
    reduce_scatter x1 -> x0, waiting for transfers between devices: 211 us -> none  [on_device(): lax.psum_scatter(partial_value.astype(jnp.bfloat16), 'tensor', scatter_di...]
    pallas_call x0 -> x22, Pallas kernels: none -> 130 us  [call(): pl.pallas_call(body, grid_spec=pltpu.PrefetchScalarGridSpec(num_scalar_pr...]
    dot_general x6 -> x0, matrix products: 74.6 us -> none  [the longest x1 21.2 us: on_device(): jnp.dot(flat_rows, projection_weight, preferred_element_type=jnp.float32)]
    ppermute x0 -> x20, waiting for transfers between devices: none -> 72 us  [the longest x3 54.7 us: low_step(): other = lax.ppermute(low, 'tensor', [(t, t ^ bit) for t in range(n)])]
    psum x1 -> x0, waiting for transfers between devices: 29.6 us -> none  [on_device(): low_rank = lax.psum(low_part.astype(jnp.bfloat16), 'tensor')]
    ppermute x0 -> x20, starting transfers between devices: none -> 28.1 us  [the longest x9 19.9 us: hop(): return lax.ppermute(value, 'tensor', pairs)]
    all_to_all x1 -> x0, blocking collectives: 8.18 us -> none  [on_device(): lax.all_to_all(send_up, 'dp', split_axis=0, concat_axis=0, tiled=True)]
    all_to_all x1 -> x0, starting transfers between devices: 5.75 us -> none  [on_device(): lax.all_to_all(send_down, 'dp', split_axis=0, concat_axis=0, tiled=True)]
  transfers between devices with their start and end apart: 3 -> 20, of which waited for: 3 -> 4; matrix products, arithmetic and copies ran while one was open for 10% -> 4% of each run, Pallas kernels for 0% -> 50%
where the time goes in v3:
time: 251 us; the launch traced here: 248 us
  Pallas kernels  130 us (52%)
  waiting for transfers between devices  72 us (29%)
  starting transfers between devices  28.1 us (11%)
  local copies, waits for them, and re-layouts  11.8 us (5%)
  other arithmetic  4.03 us (2%)
  between operations  2.71 us (1%)
    pallas_call x22, Pallas kernels, call(): pl.pallas_call(body, grid_spec=pltpu.PrefetchScalarGridSpec(num_scalar_pr...  130 us
    ppermute x3, waiting for transfers between devices, low_step(): other = lax.ppermute(low, 'tensor', [(t, t ^ bit) for t in range(n)])  54.7 us
    ppermute x9, starting transfers between devices, hop(): return lax.ppermute(value, 'tensor', pairs)  19.9 us
    ppermute x9, waiting for transfers between devices, hop(): return lax.ppermute(value, 'tensor', pairs)  11.7 us
    unnamed x28, local copies, waits for them, and re-layouts  6.9 us
    ppermute x5, starting transfers between devices, swap_y(): return lax.ppermute(value, 'tensor', [(t, t ^ 1) for t in range(n)])  6.07 us
    ppermute x5, waiting for transfers between devices, swap_y(): return lax.ppermute(value, 'tensor', [(t, t ^ 1) for t in range(n)])  5.61 us
  transfers between devices with their start and end apart: 20, of which 4 were waited for; matrix products, arithmetic and copies ran while one was open for 4% of the time, Pallas kernels for 50%

profile of v3, /device:TPU:0, one launch (start us, length us, event | category | flops | bytes accessed | tf_op | source)
XLA Modules:
  0.0 248.4 jit_solution(16995455998851452198)
XLA Ops:
  0.5 1.2 fusion.6
  3.0 4.4 %products.3.refs_3_ = bf16[640,1024]{1,0:T(8,128)(2,1)} custom-call(s32[1]{0:T(128)} %bitcast.15.refs_0_, bf16[768,1024]{1,0:T(8,128)(2,1)} %bitcast.19, bf16[1024,8192]{1,0:T(8,128)(2,1)} %refs_2_.7), custom_call_target="tpu_custom_call" | custom-call | flops 1 | bytes 1 | tf_op jit(solution)/shard_map/products/pallas_call | solution.py:21
  7.5 3.0 %collective-permute-start.6 = (bf16[640,1024]{1,0:T(8,128)(2,1)}, bf16[640,1024]{1,0:T(8,128)(2,1)S(1)}, u32[]{:S(2)}, u32[]{:S(2)}) collective-permute-start(bf16[640,1024]{1,0:T(8,128)(2,1)} %products.3.refs_3_), channel_id=1, source_target_pairs={{0,2},{2,0},{4,6},{6,4},{8,10},{10,8},{12,14},{14,12},{1,3},{3,1},... | collective-permute-start | bytes 3932168 | tf_op jit(solution)/shard_map/ppermute | solution.py:324
  10.4 11.4 %few_products.1 = (bf16[384,2048]{1,0:T(8,128)(2,1)}, bf16[128,2048]{1,0:T(8,128)(2,1)}) custom-call(s32[4]{0:T(128)} %get-tuple-element.27.refs_0_, bf16[768,1024]{1,0:T(8,128)(2,1)} %bitcast.20, bf16[1024,8192]{1,0:T(8,128)(2,1)} %refs_2_.7, bf16[640,1024]{1,0:T(8,128)(2,1)} %products.3.refs_3_), custom_call_target="tpu_custom_call" | custom-call | flops 1 | bytes 1 | tf_op jit(solution)/shard_map/few_products/pallas_call | solution.py:21
  21.9 3.6 %collective-permute-start.5 = (bf16[384,2048]{1,0:T(8,128)(2,1)}, bf16[384,2048]{1,0:T(8,128)(2,1)S(1)}, u32[]{:S(2)}, u32[]{:S(2)}) collective-permute-start(bf16[384,2048]{1,0:T(8,128)(2,1)} %get-tuple-element.16.refs_9_.refs_1_), channel_id=1, source_target_pairs={{0,4},{12,8},{2,6},{14,10},{1,5},{13,9},{3,7},{15,11},{16,20},{28,... | collective-permute-start | bytes 4718600 | tf_op jit(solution)/shard_map/ppermute | solution.py:331
  25.8 0.8 copy.26.refs_3_.refs_2_
  26.9 0.8 copy.27.refs_4_.refs_3_
  28.5 11.2 %low_rank.1.refs_3_.refs_1_ = bf16[768,128]{1,0:T(8,128)(2,1)} custom-call(s32[32]{0:T(128)} %pad_add_fusion.1.refs_0_, bf16[768,1024]{1,0:T(8,128)(2,1)} %bitcast.21, bf16[768,1024]{1,0:T(8,128)(2,1)} %collective-permute-done.1.refs_2_, s32[192,1]{1,0:T(8,128)} %copy.26.refs_3_.refs_2_, s32[192,1]{1,0:T(8,128)} %copy.27.refs_4_.refs_3_, ...), custom_call_target="tpu_custom_call" | custom-call | flops 1 | bytes 1 | tf_op jit(solution)/shard_map/low_rank/pallas_call | solution.py:21
  43.1 7.8 %products.4 = (bf16[640,1024]{1,0:T(8,128)(2,1)}, bf16[640,1024]{1,0:T(8,128)(2,1)}) custom-call(s32[2]{0:T(128)} %pad_add_fusion.refs_0_, bf16[768,1024]{1,0:T(8,128)(2,1)} %bitcast.22, bf16[1024,8192]{1,0:T(8,128)(2,1)} %refs_2_.7, bf16[768,128]{1,0:T(8,128)(2,1)} %low_rank.1.refs_3_.refs_1_), custom_call_target="tpu_custom_call" | custom-call | flops 1 | bytes 1 | tf_op jit(solution)/shard_map/products/pallas_call | solution.py:21
  51.0 1.5 collective-permute-start.2
  52.5 15.8 %products.5 = (bf16[640,1024]{1,0:T(8,128)(2,1)}, bf16[640,1024]{1,0:T(8,128)(2,1)}, bf16[640,1024]{1,0:T(8,128)(2,1)}, bf16[640,1024]{1,0:T(8,128)(2,1)}, bf16[640,1024]{1,0:T(8,128)(2,1)}) custom-call(s32[5]{0:T(128)} %stack.35.refs_0_, bf16[768,1024]{1,0:T(8,128)(2,1)} %bitcast.23, bf16[1024,8192]{1,0:T(8,128)(2,1)} %refs_2_.7, ...), custom_call_target="tpu_custom_call" | custom-call | flops 1 | bytes 1 | tf_op jit(solution)/shard_map/products/pallas_call | solution.py:21
  68.3 0.7 copy-done.10
  69.0 4.3 %total.13.refs_3_.refs_1_ = bf16[768,128]{1,0:T(8,128)(2,1)} custom-call(s32[2,6]{1,0:T(2,128)} %constant.70.clone.refs_0_, bf16[768,128]{1,0:T(8,128)(2,1)} %low_rank.1.refs_3_.refs_1_, bf16[768,128]{1,0:T(8,128)(2,1)} %copy-done.10, bf16[640,1024]{1,0:T(8,128)(2,1)} %get-tuple-element.21.refs_3_.refs_0_), custom_call_target="tpu_custom_call" | custom-call | flops 1 | bytes 1 | tf_op jit(solution)/shard_map/total/pallas_call | solution.py:21
  73.3 1.1 copy-done.1
  74.4 5.1 %total.14.refs_3_.refs_1_ = bf16[640,1024]{1,0:T(8,128)(2,1)} custom-call(s32[2,5]{1,0:T(2,128)} %constant.71.clone.refs_0_, bf16[640,1024]{1,0:T(8,128)(2,1)} %get-tuple-element.22.refs_1_, bf16[640,1024]{1,0:T(8,128)(2,1)} %copy-done.1, bf16[768,128]{1,0:T(8,128)(2,1)} %total.13.refs_3_.refs_1_), custom_call_target="tpu_custom_call" | custom-call | flops 1 | bytes 1 | tf_op jit(solution)/shard_map/total/pallas_call | solution.py:21
  79.4 2.4 collective-permute-start.10
  82.3 1.2 copy-done
  83.5 3.2 %total.15.refs_3_ = bf16[256,2048]{1,0:T(8,128)(2,1)} custom-call(s32[2,2]{1,0:T(2,128)} %constant.72.clone.refs_0_, bf16[384,2048]{1,0:T(8,128)(2,1)} %get-tuple-element.16.refs_9_.refs_1_, bf16[384,2048]{1,0:T(8,128)(2,1)} %copy-done, bf16[640,1024]{1,0:T(8,128)(2,1)} %total.14.refs_3_.refs_1_), custom_call_target="tpu_custom_call" | custom-call | flops 1 | bytes 1 | tf_op jit(solution)/shard_map/total/pallas_call | solution.py:21
  86.6 0.7 collective-permute-start.9
  87.4 1.1 collective-permute-start.4
  88.5 24.2 %collective-permute-done.4.refs_2_ = bf16[768,128]{1,0:T(8,128)(2,1)S(1)} collective-permute-done((bf16[768,128]{1,0:T(8,128)(2,1)S(1)}, bf16[768,128]{1,0:T(8,128)(2,1)S(1)}, u32[]{:S(2)}, u32[]{:S(2)}) %collective-permute-start.4) | collective-permute-done | bytes 196640 | tf_op jit(solution)/shard_map/ppermute | solution.py:413
  112.7 0.7 copy-done.12
  113.4 4.3 %total.16.refs_3_.refs_1_ = bf16[768,128]{1,0:T(8,128)(2,1)} custom-call(s32[2,6]{1,0:T(2,128)} %constant.70.clone.refs_0_, bf16[768,128]{1,0:T(8,128)(2,1)} %total.13.refs_3_.refs_1_, bf16[768,128]{1,0:T(8,128)(2,1)} %copy-done.12, bf16[256,2048]{1,0:T(8,128)(2,1)} %total.15.refs_3_), custom_call_target="tpu_custom_call" | custom-call | flops 1 | bytes 1 | tf_op jit(solution)/shard_map/total/pallas_call | solution.py:21
  117.7 5.1 %total.17.refs_1_.refs_4_ = bf16[640,1024]{1,0:T(8,128)(2,1)} custom-call(s32[2,5]{1,0:T(2,128)} %constant.71.clone.refs_0_, bf16[640,1024]{1,0:T(8,128)(2,1)} %get-tuple-element.20.refs_1_, bf16[640,1024]{1,0:T(8,128)(2,1)} %collective-permute-done.2.refs_2_, bf16[768,128]{1,0:T(8,128)(2,1)} %total.16.refs_3_.refs_1_), custom_call_target="tpu_custom_call" | custom-call | flops 1 | bytes 1 | tf_op jit(solution)/shard_map/total/pallas_call | solution.py:21
  122.7 5.6 %collective-permute-start.15 = (bf16[640,1024]{1,0:T(8,128)(2,1)}, bf16[640,1024]{1,0:T(8,128)(2,1)}, u32[]{:S(2)}, u32[]{:S(2)}) collective-permute-start(bf16[640,1024]{1,0:T(8,128)(2,1)} %total.17.refs_1_.refs_4_), channel_id=1, source_target_pairs={{0,4},{12,8},{2,6},{14,10},{1,5},{13,9},{3,7},{15,11},{16,20},{28,... | collective-permute-start | bytes 3932168 | tf_op jit(solution)/shard_map/ppermute | solution.py:331
  128.4 5.4 %total.18.refs_3_ = bf16[640,1024]{1,0:T(8,128)(2,1)} custom-call(s32[3,5]{1,0:T(4,128)} %constant.73.clone.refs_0_, bf16[640,1024]{1,0:T(8,128)(2,1)} %get-tuple-element.22.refs_1_, bf16[640,1024]{1,0:T(8,128)(2,1)} %copy-done.1, bf16[640,1024]{1,0:T(8,128)(2,1)} %collective-permute-done.10.refs_3_, bf16[640,1024]{1,0:T(8,128)(2,1)} %total.17.refs_1_.refs_4_), custom_call_target="tpu_custom_call" | custom-call | flops 1 | bytes 1 | tf_op jit(solution)/shard_map/total/pallas_call | solution.py:21
  133.8 1.8 collective-permute-start.14
  135.6 1.0 copy-done.4
  136.6 2.8 %total.19.refs_3_ = bf16[128,2048]{1,0:T(8,128)(2,1)} custom-call(s32[2,1]{1,0:T(2,128)} %constant.74.clone.refs_0_, bf16[384,2048]{1,0:T(8,128)(2,1)} %get-tuple-element.16.refs_9_.refs_1_, bf16[256,2048]{1,0:T(8,128)(2,1)} %copy-done.4, bf16[640,1024]{1,0:T(8,128)(2,1)} %total.18.refs_3_), custom_call_target="tpu_custom_call" | custom-call | flops 1 | bytes 1 | tf_op jit(solution)/shard_map/total/pallas_call | solution.py:21
  139.4 1.3 collective-permute-start.12
  140.7 30.5 %collective-permute-done.8.refs_2_ = bf16[768,128]{1,0:T(8,128)(2,1)S(1)} collective-permute-done((bf16[768,128]{1,0:T(8,128)(2,1)S(1)}, bf16[768,128]{1,0:T(8,128)(2,1)S(1)}, u32[]{:S(2)}, u32[]{:S(2)}) %collective-permute-start.8) | collective-permute-done | bytes 196640 | tf_op jit(solution)/shard_map/ppermute | solution.py:413
  171.2 0.7 copy-done.11
  171.8 4.3 %total.20.refs_1_.refs_8_ = bf16[768,128]{1,0:T(8,128)(2,1)} custom-call(s32[2,6]{1,0:T(2,128)} %constant.70.clone.refs_0_, bf16[768,128]{1,0:T(8,128)(2,1)} %total.16.refs_3_.refs_1_, bf16[768,128]{1,0:T(8,128)(2,1)} %copy-done.11, bf16[128,2048]{1,0:T(8,128)(2,1)} %total.19.refs_3_), custom_call_target="tpu_custom_call" | custom-call | flops 1 | bytes 1 | tf_op jit(solution)/shard_map/total/pallas_call | solution.py:21
  176.1 13.0 %expand.1 = (f32[768,1024]{1,0:T(8,128)}, bf16[768,1024]{1,0:T(8,128)(2,1)}) custom-call(s32[32]{0:T(128)} %pad_add_fusion.1.refs_0_, bf16[768,128]{1,0:T(8,128)(2,1)} %total.20.refs_1_.refs_8_, s32[192,1]{1,0:T(8,128)} %copy.26.refs_3_.refs_2_, s32[192,1]{1,0:T(8,128)} %copy.27.refs_4_.refs_3_, bf16[64,64,1024]{2,1,0:T(8,128)(2,1)} %refs_7_.3, ...), custom_call_target="tpu_custom_call" | custom-call | flops 1 | bytes 1 | tf_op jit(solution)/shard_map/expand/pallas_call | solution.py:21
  190.3 5.1 %total.21.refs_4_ = bf16[640,1024]{1,0:T(8,128)(2,1)} custom-call(s32[2,5]{1,0:T(2,128)} %constant.71.clone.refs_0_, bf16[640,1024]{1,0:T(8,128)(2,1)} %get-tuple-element.26.refs_1_, bf16[640,1024]{1,0:T(8,128)(2,1)} %copy-done.2, f32[768,1024]{1,0:T(8,128)} %get-tuple-element.23.refs_3_), custom_call_target="tpu_custom_call" | custom-call | flops 1 | bytes 1 | tf_op jit(solution)/shard_map/total/pallas_call | solution.py:21
  195.3 1.6 collective-permute-start.16
  196.9 5.4 %total.22.refs_4_ = bf16[640,1024]{1,0:T(8,128)(2,1)} custom-call(s32[3,5]{1,0:T(4,128)} %constant.73.clone.refs_0_, bf16[640,1024]{1,0:T(8,128)(2,1)} %get-tuple-element.20.refs_1_, bf16[640,1024]{1,0:T(8,128)(2,1)} %collective-permute-done.2.refs_2_, bf16[640,1024]{1,0:T(8,128)(2,1)} %collective-permute-done.15.refs_3_, bf16[640,1024]{1,0:T(8,128)(2,1)} %total.21.refs_4_), custom_call_target="tpu_custom_call" | custom-call | flops 1 | bytes 1 | tf_op jit(solution)/shard_map/total/pallas_call | solution.py:21
  202.3 1.8 collective-permute-start.17
  204.1 5.4 %total.23.refs_5_ = bf16[640,1024]{1,0:T(8,128)(2,1)} custom-call(s32[3,5]{1,0:T(4,128)} %constant.73.clone.refs_0_, bf16[640,1024]{1,0:T(8,128)(2,1)} %get-tuple-element.26.refs_1_, bf16[640,1024]{1,0:T(8,128)(2,1)} %copy-done.2, bf16[640,1024]{1,0:T(8,128)(2,1)} %collective-permute-done.14.refs_3_, bf16[640,1024]{1,0:T(8,128)(2,1)} %total.22.refs_4_), custom_call_target="tpu_custom_call" | custom-call | flops 1 | bytes 1 | tf_op jit(solution)/shard_map/total/pallas_call | solution.py:21
  209.6 1.3 collective-permute-start.18
  210.9 3.3 %total.24.refs_5_ = bf16[128,2048]{1,0:T(8,128)(2,1)} custom-call(s32[4,1]{1,0:T(4,128)} %constant.75.clone.refs_0_, bf16[128,2048]{1,0:T(8,128)(2,1)} %get-tuple-element.25.refs_1_, bf16[384,2048]{1,0:T(8,128)(2,1)} %copy-done, bf16[256,2048]{1,0:T(8,128)(2,1)} %copy-done.4, bf16[128,2048]{1,0:T(8,128)(2,1)} %copy-done.9, bf16[640,1024]{1,0:T(8,128)(2,1)} %total.23.refs_5_), custom_call_target="tpu_custom_call" | custom-call | flops 1 | bytes 1 | tf_op jit(solution)/shard_map/total/pallas_call | solution.py:21
  214.1 1.0 constant_dynamic-slice_fusion
  215.1 5.6 %collective-permute-done.7.refs_2_ = bf16[640,1024]{1,0:T(8,128)(2,1)} collective-permute-done((bf16[640,1024]{1,0:T(8,128)(2,1)}, bf16[640,1024]{1,0:T(8,128)(2,1)}, u32[]{:S(2)}, u32[]{:S(2)}) %collective-permute-start.7) | collective-permute-done | bytes 1310752 | tf_op jit(solution)/shard_map/ppermute | solution.py:324
  221.2 1.1 copy-done.5
  222.4 6.7 %total.25.refs_0_ = f32[640,1024]{1,0:T(8,128)} custom-call(s32[4,5]{1,0:T(4,128)} %constant.76.clone.refs_0_, bf16[640,1024]{1,0:T(8,128)(2,1)} %get-tuple-element.18.refs_1_, bf16[640,1024]{1,0:T(8,128)(2,1)} %collective-permute-done.7.refs_2_, f32[768,1024]{1,0:T(8,128)} %get-tuple-element.23.refs_3_, bf16[768,1024]{1,0:T(8,128)(2,1)} %copy-done.5, ...), custom_call_target="tpu_custom_call" | custom-call | flops 1 | bytes 1 | tf_op jit(solution)/shard_map/total/pallas_call | solution.py:21
  229.1 2.0 add_convert_fusion.refs_4_
  231.1 11.7 %collective-permute-done.18.refs_3_ = bf16[640,1024]{1,0:T(8,128)(2,1)} collective-permute-done((bf16[640,1024]{1,0:T(8,128)(2,1)}, bf16[640,1024]{1,0:T(8,128)(2,1)}, u32[]{:S(2)}, u32[]{:S(2)}) %collective-permute-start.18) | collective-permute-done | bytes 1310752 | tf_op jit(solution)/shard_map/ppermute | solution.py:331
  242.7 5.7 %finish.1 = bf16[768,1024]{1,0:T(8,128)(2,1)} custom-call(f32[640,1024]{1,0:T(8,128)} %total.25.refs_0_, bf16[640,1024]{1,0:T(8,128)(2,1)} %copy-done.8, bf16[640,1024]{1,0:T(8,128)(2,1)} %collective-permute-done.17.refs_2_, bf16[640,1024]{1,0:T(8,128)(2,1)} %collective-permute-done.18.refs_3_, bf16[128,1024]{1,0:T(8,128)(2,1)} %add_convert_fusion.refs_4_), custom_call_target="tpu_custom_call" | custom-call | flops 1 | bytes 1 | tf_op jit(solution)/shard_map/finish/pallas_call | solution.py:21
  (64 shorter events, 6.4 us)
Async XLA Ops:
  0.0 26.6 %collective-permute-start = (s32[192]{0:T(256)}, s32[192]{0:T(256)S(1)}, u32[]{:S(2)}, u32[]{:S(2)}) collective-permute-start(s32[192]{0:T(256)} %param.20), channel_id=1, source_target_pairs={{0,1},{1,0},{2,3},{3,2},{4,5},{5,4},{6,7},{7,6},{8,9},{9,8},{10,11... | collective-permute-start | bytes 2312 | tf_op jit(solution)/shard_map/ppermute | solution.py:393
  0.5 28.0 %collective-permute-start.1 = (bf16[768,1024]{1,0:T(8,128)(2,1)}, bf16[768,1024]{1,0:T(8,128)(2,1)}, u32[]{:S(2)}, u32[]{:S(2)}) collective-permute-start(bf16[768,1024]{1,0:T(8,128)(2,1)} %bitcast.18), channel_id=1, source_target_pairs={{0,1},{1,0},{2,3},{3,2},{4,5},{5,4},{6,7},{7,6},{8,9},{9,8},{10,11... | collective-permute-start | bytes 4718600 | tf_op jit(solution)/shard_map/ppermute | solution.py:393
  7.5 65.8 %collective-permute-start.6 = (bf16[640,1024]{1,0:T(8,128)(2,1)}, bf16[640,1024]{1,0:T(8,128)(2,1)S(1)}, u32[]{:S(2)}, u32[]{:S(2)}) collective-permute-start(bf16[640,1024]{1,0:T(8,128)(2,1)} %products.3.refs_3_), channel_id=1, source_target_pairs={{0,2},{2,0},{4,6},{6,4},{8,10},{10,8},{12,14},{14,12},{1,3},{3,1},... | collective-permute-start | bytes 3932168 | tf_op jit(solution)/shard_map/ppermute | solution.py:324
  10.4 15.0 %copy-start.13 = (s32[192]{0:T(256)S(1)}, s32[192]{0:T(256)}, u32[]{:S(2)}) copy-start(s32[192]{0:T(256)} %param.20) | copy-start | bytes 2308
  21.9 60.5 %collective-permute-start.5 = (bf16[384,2048]{1,0:T(8,128)(2,1)}, bf16[384,2048]{1,0:T(8,128)(2,1)S(1)}, u32[]{:S(2)}, u32[]{:S(2)}) collective-permute-start(bf16[384,2048]{1,0:T(8,128)(2,1)} %get-tuple-element.16.refs_9_.refs_1_), channel_id=1, source_target_pairs={{0,4},{12,8},{2,6},{14,10},{1,5},{13,9},{3,7},{15,11},{16,20},{28,... | collective-permute-start | bytes 4718600 | tf_op jit(solution)/shard_map/ppermute | solution.py:331
  39.6 28.7 %collective-permute-start.3 = (bf16[768,128]{1,0:T(8,128)(2,1)}, bf16[768,128]{1,0:T(8,128)(2,1)S(1)}, u32[]{:S(2)}, u32[]{:S(2)}) collective-permute-start(bf16[768,128]{1,0:T(8,128)(2,1)} %low_rank.1.refs_3_.refs_1_), channel_id=1, source_target_pairs={{0,2},{2,0},{4,6},{6,4},{8,10},{10,8},{12,14},{14,12},{1,3},{3,1},... | collective-permute-start | bytes 589832 | tf_op jit(solution)/shard_map/ppermute | solution.py:413
  51.0 66.7 %collective-permute-start.2 = (bf16[640,1024]{1,0:T(8,128)(2,1)}, bf16[640,1024]{1,0:T(8,128)(2,1)}, u32[]{:S(2)}, u32[]{:S(2)}) collective-permute-start(bf16[640,1024]{1,0:T(8,128)(2,1)} %get-tuple-element.17.refs_3_), channel_id=1, source_target_pairs={{0,2},{2,0},{4,6},{6,4},{8,10},{10,8},{12,14},{14,12},{1,3},{3,1},... | collective-permute-start | bytes 3932168 | tf_op jit(solution)/shard_map/ppermute | solution.py:324
  68.3 0.7 copy-start.10
  73.3 1.1 copy-start.1
  79.4 48.9 %collective-permute-start.10 = (bf16[640,1024]{1,0:T(8,128)(2,1)}, bf16[640,1024]{1,0:T(8,128)(2,1)}, u32[]{:S(2)}, u32[]{:S(2)}) collective-permute-start(bf16[640,1024]{1,0:T(8,128)(2,1)} %total.14.refs_3_.refs_1_), channel_id=1, source_target_pairs={{0,4},{12,8},{2,6},{14,10},{1,5},{13,9},{3,7},{15,11},{16,20},{28,... | collective-permute-start | bytes 3932168 | tf_op jit(solution)/shard_map/ppermute | solution.py:331
  81.8 5.6 %copy-start.7 = (bf16[768,128]{1,0:T(8,128)(2,1)S(1)}, bf16[768,128]{1,0:T(8,128)(2,1)}, u32[]{:S(2)}) copy-start(bf16[768,128]{1,0:T(8,128)(2,1)} %total.13.refs_3_.refs_1_) | copy-start | bytes 589828
  81.8 107.4 %collective-permute-start.13 = (bf16[640,1024]{1,0:T(8,128)(2,1)}, bf16[640,1024]{1,0:T(8,128)(2,1)S(1)}, u32[]{:S(2)}, u32[]{:S(2)}) collective-permute-start(bf16[640,1024]{1,0:T(8,128)(2,1)} %hold.3), channel_id=1, source_target_pairs={{0,2},{2,0},{4,6},{6,4},{8,10},{10,8},{12,14},{14,12},{1,3},{3,1},... | collective-permute-start | bytes 3932168 | tf_op jit(solution)/shard_map/ppermute | solution.py:324
  82.3 1.2 copy-start
  86.6 48.9 %collective-permute-start.9 = (bf16[256,2048]{1,0:T(8,128)(2,1)}, bf16[256,2048]{1,0:T(8,128)(2,1)S(1)}, u32[]{:S(2)}, u32[]{:S(2)}) collective-permute-start(bf16[256,2048]{1,0:T(8,128)(2,1)} %total.15.refs_3_), channel_id=1, source_target_pairs={{4,8},{8,4},{6,10},{10,6},{5,9},{9,5},{7,11},{11,7},{20,24},{24,20... | collective-permute-start | bytes 3145736 | tf_op jit(solution)/shard_map/ppermute | solution.py:331
  87.4 25.3 %collective-permute-start.4 = (bf16[768,128]{1,0:T(8,128)(2,1)S(1)}, bf16[768,128]{1,0:T(8,128)(2,1)S(1)}, u32[]{:S(2)}, u32[]{:S(2)}) collective-permute-start(bf16[768,128]{1,0:T(8,128)(2,1)S(1)} %copy-done.7), channel_id=1, source_target_pairs={{0,4},{2,6},{4,0},{6,2},{8,12},{10,14},{12,8},{14,10},{1,5},{3,7},... | collective-permute-start | bytes 589832 | tf_op jit(solution)/shard_map/ppermute | solution.py:413
  112.7 0.7 copy-start.12
  122.7 12.8 %copy-start.6 = (bf16[768,128]{1,0:T(8,128)(2,1)S(1)}, bf16[768,128]{1,0:T(8,128)(2,1)}, u32[]{:S(2)}) copy-start(bf16[768,128]{1,0:T(8,128)(2,1)} %total.16.refs_3_.refs_1_) | copy-start | bytes 589828
  122.7 72.6 %collective-permute-start.15 = (bf16[640,1024]{1,0:T(8,128)(2,1)}, bf16[640,1024]{1,0:T(8,128)(2,1)}, u32[]{:S(2)}, u32[]{:S(2)}) collective-permute-start(bf16[640,1024]{1,0:T(8,128)(2,1)} %total.17.refs_1_.refs_4_), channel_id=1, source_target_pairs={{0,4},{12,8},{2,6},{14,10},{1,5},{13,9},{3,7},{15,11},{16,20},{28,... | collective-permute-start | bytes 3932168 | tf_op jit(solution)/shard_map/ppermute | solution.py:331
  133.8 68.5 %collective-permute-start.14 = (bf16[640,1024]{1,0:T(8,128)(2,1)}, bf16[640,1024]{1,0:T(8,128)(2,1)}, u32[]{:S(2)}, u32[]{:S(2)}) collective-permute-start(bf16[640,1024]{1,0:T(8,128)(2,1)} %total.18.refs_3_), channel_id=1, source_target_pairs={{4,8},{8,4},{6,10},{10,6},{5,9},{9,5},{7,11},{11,7},{20,24},{24,20... | collective-permute-start | bytes 3932168 | tf_op jit(solution)/shard_map/ppermute | solution.py:331
  135.6 35.6 %collective-permute-start.8 = (bf16[768,128]{1,0:T(8,128)(2,1)S(1)}, bf16[768,128]{1,0:T(8,128)(2,1)S(1)}, u32[]{:S(2)}, u32[]{:S(2)}) collective-permute-start(bf16[768,128]{1,0:T(8,128)(2,1)S(1)} %copy-done.6), channel_id=1, source_target_pairs={{0,8},{2,10},{4,12},{6,14},{8,0},{10,2},{12,4},{14,6},{1,9},{3,11}... | collective-permute-start | bytes 589832 | tf_op jit(solution)/shard_map/ppermute | solution.py:413
  135.6 1.0 copy-start.4
  139.4 70.2 %collective-permute-start.12 = (bf16[128,2048]{1,0:T(8,128)(2,1)}, bf16[128,2048]{1,0:T(8,128)(2,1)S(1)}, u32[]{:S(2)}, u32[]{:S(2)}) collective-permute-start(bf16[128,2048]{1,0:T(8,128)(2,1)} %total.19.refs_3_), channel_id=1, source_target_pairs={{8,12},{4,0},{10,14},{6,2},{9,13},{5,1},{11,15},{7,3},{24,28},{20,... | collective-permute-start | bytes 1572872 | tf_op jit(solution)/shard_map/ppermute | solution.py:331
  171.2 0.7 copy-start.11
  189.2 32.0 %collective-permute-start.11 = (bf16[768,1024]{1,0:T(8,128)(2,1)}, bf16[768,1024]{1,0:T(8,128)(2,1)S(1)}, u32[]{:S(2)}, u32[]{:S(2)}) collective-permute-start(bf16[768,1024]{1,0:T(8,128)(2,1)} %get-tuple-element.24), channel_id=1, source_target_pairs={{0,1},{1,0},{2,3},{3,2},{4,5},{5,4},{6,7},{7,6},{8,9},{9,8},{10,11... | collective-permute-start | bytes 4718600 | tf_op jit(solution)/shard_map/ppermute | solution.py:393
  189.2 1.1 copy-start.2
  189.2 31.5 %collective-permute-start.7 = (bf16[640,1024]{1,0:T(8,128)(2,1)}, bf16[640,1024]{1,0:T(8,128)(2,1)}, u32[]{:S(2)}, u32[]{:S(2)}) collective-permute-start(bf16[640,1024]{1,0:T(8,128)(2,1)} %hold.2), channel_id=1, source_target_pairs={{0,2},{2,0},{4,6},{6,4},{8,10},{10,8},{12,14},{14,12},{1,3},{3,1},... | collective-permute-start | bytes 3932168 | tf_op jit(solution)/shard_map/ppermute | solution.py:324
  195.3 35.7 %collective-permute-start.16 = (bf16[640,1024]{1,0:T(8,128)(2,1)}, bf16[640,1024]{1,0:T(8,128)(2,1)S(1)}, u32[]{:S(2)}, u32[]{:S(2)}) collective-permute-start(bf16[640,1024]{1,0:T(8,128)(2,1)} %total.21.refs_4_), channel_id=1, source_target_pairs={{0,4},{12,8},{2,6},{14,10},{1,5},{13,9},{3,7},{15,11},{16,20},{28,... | collective-permute-start | bytes 3932168 | tf_op jit(solution)/shard_map/ppermute | solution.py:331
  202.3 28.7 %collective-permute-start.17 = (bf16[640,1024]{1,0:T(8,128)(2,1)}, bf16[640,1024]{1,0:T(8,128)(2,1)}, u32[]{:S(2)}, u32[]{:S(2)}) collective-permute-start(bf16[640,1024]{1,0:T(8,128)(2,1)} %total.22.refs_4_), channel_id=1, source_target_pairs={{4,8},{8,4},{6,10},{10,6},{5,9},{9,5},{7,11},{11,7},{20,24},{24,20... | collective-permute-start | bytes 3932168 | tf_op jit(solution)/shard_map/ppermute | solution.py:331
  209.6 1.3 copy-start.9
  209.6 33.2 %collective-permute-start.18 = (bf16[640,1024]{1,0:T(8,128)(2,1)}, bf16[640,1024]{1,0:T(8,128)(2,1)}, u32[]{:S(2)}, u32[]{:S(2)}) collective-permute-start(bf16[640,1024]{1,0:T(8,128)(2,1)} %total.23.refs_5_), channel_id=1, source_target_pairs={{8,12},{4,0},{10,14},{6,2},{9,13},{5,1},{11,15},{7,3},{24,28},{20,... | collective-permute-start | bytes 3932168 | tf_op jit(solution)/shard_map/ppermute | solution.py:331
  220.7 8.4 %collective-permute-start.19 = (bf16[128,1024]{1,0:T(8,128)(2,1)S(1)}, bf16[128,1024]{1,0:T(8,128)(2,1)S(1)}, u32[]{:S(2)}, u32[]{:S(2)}) collective-permute-start(bf16[128,1024]{1,0:T(8,128)(2,1)S(1)} %constant_dynamic-slice_fusion), channel_id=1, source_target_pairs={{0,2},{2,0},{4,6},{6,4},{8,10},{10,8},{12,14},{14,12},{1,3},{3,1},... | collective-permute-start | bytes 786440 | tf_op jit(solution)/shard_map/ppermute | solution.py:324
  221.2 1.1 copy-start.5
  222.4 6.7 %copy-start.3 = (bf16[128,2048]{1,0:T(8,128)(2,1)S(1)}, bf16[128,2048]{1,0:T(8,128)(2,1)}, u32[]{:S(2)}) copy-start(bf16[128,2048]{1,0:T(8,128)(2,1)} %total.24.refs_5_) | copy-start | bytes 1572868
  231.1 11.7 %copy-start.8 = (bf16[640,1024]{1,0:T(8,128)(2,1)}, bf16[640,1024]{1,0:T(8,128)(2,1)S(1)}, u32[]{:S(2)}) copy-start(bf16[640,1024]{1,0:T(8,128)(2,1)S(1)} %collective-permute-done.16.refs_1_) | copy-start | bytes 3932164

commit v4 on v0

v4 whole, which is shorter than its diff:
```python
import jax
import jax.numpy as jnp
import numpy as np
from jax import lax
from jax.experimental import pallas as pl
from jax.experimental.pallas import tpu as pltpu
from jax.sharding import PartitionSpec as P

SLOTS = 16
LANES = 128
CHUNK = 256
PARTS = 2
LOW_WITH = (0, PARTS - 1)
VMEM = 50 * 2**20
ANY = pl.BlockSpec(memory_space=pl.ANY)


def call(kernel, operands, after, *, in_specs, out_specs, out_shape, name, prefetch=0, scratch=(), alias=None):
    inputs, extra = len(operands), len(after)

    def body(*refs):
        kernel(*refs[:inputs], *refs[inputs + extra :])

    return pl.pallas_call(
        body,
        grid_spec=pltpu.PrefetchScalarGridSpec(
            num_scalar_prefetch=prefetch,
            grid=(),
            in_specs=list(in_specs) + [ANY] * extra,
            out_specs=out_specs,
            scratch_shapes=list(scratch),
        ),
        out_shape=out_shape,
        input_output_aliases=alias or {},
        compiler_params=pltpu.CompilerParams(vmem_limit_bytes=VMEM),
        cost_estimate=pl.CostEstimate(flops=1, transcendentals=0, bytes_accessed=1),
        name=name,
    )(*operands, *after)


def hold(value, after):
    def kernel(value_ref, out_ref):
        pass

    return call(
        kernel, [value], after, in_specs=[ANY], out_specs=ANY,
        out_shape=jax.ShapeDtypeStruct(value.shape, value.dtype), name="hold", alias={0: 0},
    )


def products(rows, weight, starts, size, outs, tail=None, after=()):
    count, width = rows.shape
    blocks = starts.shape[0]
    chunks = [(at, min(CHUNK, size - at)) for at in range(0, size, CHUNK)]
    low = min(first for _, first, _ in outs)
    high = max(first + some for _, first, some in outs)
    upper = (high - low) // 32 * 16
    row_parts = [(0, upper), (upper, high - low - upper)]
    tails = [] if tail is None else [tail]
    heights = [some for _, _, some in outs]
    for array in tails:
        heights[-1] += array.shape[0]

    def kernel(starts_ref, rows_ref, weight_ref, *refs):
        tail_refs, refs = refs[: len(tails)], refs[len(tails) :]
        out_refs, (x, w, *refs) = refs[: len(outs)], refs[len(outs) :]
        stage, (x_sems, w_sems, out_sems, tail_sems) = refs[: len(outs)], refs[len(outs) :]
        x_copies = [
            pltpu.make_async_copy(
                rows_ref.at[pl.ds(low + at, some)], x.at[pl.ds(at, some)], x_sems.at[i]
            )
            for i, (at, some) in enumerate(row_parts)
        ]
        w_copies = [
            [
                pltpu.make_async_copy(
                    weight_ref.at[:, pl.ds(pl.multiple_of(starts_ref[b] + at, LANES), extent)],
                    w.at[b, :, pl.ds(at, extent)],
                    w_sems.at[b, c],
                )
                for c, (at, extent) in enumerate(chunks)
            ]
            for b in range(blocks)
        ]
        x_copies[0].start()
        w_copies[0][0].start()
        x_copies[1].start()
        for b in range(blocks):
            for c in range(len(chunks)):
                if b or c:
                    w_copies[b][c].start()
        stores = []
        for ref in tail_refs:
            below = pl.ds(outs[-1][2], ref.shape[0])
            read = pltpu.make_async_copy(ref, stage[-1].at[below], tail_sems.at[0])
            read.start()
            read.wait()
            stores.append(pltpu.make_async_copy(stage[-1].at[below], out_refs[-1].at[below], tail_sems.at[1]))
            stores[-1].start()
        for copy in x_copies:
            copy.wait()
        for b in range(blocks):
            for c, (at, extent) in enumerate(chunks):
                w_copies[b][c].wait()
                for o, (index, first, some) in enumerate(outs):
                    if index == b:
                        value = jnp.dot(
                            x[first - low : first - low + some, :], w[b, :, at : at + extent],
                            preferred_element_type=jnp.float32,
                        )
                        stage[o][:some, at : at + extent] = value.astype(rows.dtype)
                        store = pltpu.make_async_copy(
                            stage[o].at[pl.ds(0, some), pl.ds(at, extent)],
                            out_refs[o].at[pl.ds(0, some), pl.ds(at, extent)],
                            out_sems.at[o, c],
                        )
                        store.start()
                        stores.append(store)
        for store in stores:
            store.wait()

    shapes = [(height, size) for height in heights]
    return call(
        kernel, [starts, rows, weight] + tails, after, prefetch=1,
        in_specs=[ANY] * (2 + len(tails)),
        out_specs=[ANY] * len(outs),
        out_shape=[jax.ShapeDtypeStruct(shape, rows.dtype) for shape in shapes],
        scratch=[pltpu.VMEM((high - low, width), rows.dtype), pltpu.VMEM((blocks, width, size), rows.dtype)]
        + [pltpu.VMEM(shape, rows.dtype) for shape in shapes]
        + [
            pltpu.SemaphoreType.DMA((2,)),
            pltpu.SemaphoreType.DMA((blocks, len(chunks))),
            pltpu.SemaphoreType.DMA((len(outs), len(chunks))),
            pltpu.SemaphoreType.DMA((2,)),
        ],
        name="products",
    )


def total(runs, dtype=jnp.bfloat16, into=None, after=()):
    width = runs[0][1][0][0].shape[1]
    height = sum(some for some, _ in runs)
    rows_in_all, first, so_far = into or (height, 0, None)
    tiles = []
    at = 0
    for r, (some, terms) in enumerate(runs):
        size = -(-some // 32) * 16 if some * width > 2**17 else some
        for skip in range(0, some, size):
            tiles.append((r, skip, min(size, some - skip), at + skip))
        at += some
    operands = [term for _, terms in runs for term, _ in terms]
    before = [] if so_far is None else [so_far]
    most_terms = max(len(terms) for _, terms in runs)
    of_run = np.cumsum([0] + [len(terms) for _, terms in runs])

    def kernel(*refs):
        term_refs, out_ref = refs[: len(operands)], refs[len(operands) + len(before)]
        refs = refs[len(operands) + len(before) + 1 :]
        bufs, (stage, in_sems, out_sems) = refs[: len(operands)], refs[len(operands) :]
        reads, writes = [], []
        for n, (r, skip, size, place) in enumerate(tiles):
            reads.append(
                [
                    pltpu.make_async_copy(
                        term_refs[of_run[r] + t].at[pl.ds(start + skip, size)],
                        bufs[of_run[r] + t].at[pl.ds(skip, size)],
                        in_sems.at[t, n],
                    )
                    for t, (_, start) in enumerate(runs[r][1])
                ]
            )
            writes.append(
                pltpu.make_async_copy(
                    stage.at[pl.ds(place, size)], out_ref.at[pl.ds(first + place, size)], out_sems.at[n]
                )
            )
        for some in reads:
            for read in some:
                read.start()
        for n, (r, skip, size, place) in enumerate(tiles):
            for read in reads[n]:
                read.wait()
            value = None
            for t in range(len(runs[r][1])):
                part = bufs[of_run[r] + t][skip : skip + size, :].astype(jnp.float32)
                value = part if value is None else value + part
            stage[place : place + size, :] = value.astype(dtype)
            writes[n].start()
        for write in writes:
            write.wait()

    return call(
        kernel, operands + before, after,
        in_specs=[ANY] * (len(operands) + len(before)),
        out_specs=ANY,
        out_shape=jax.ShapeDtypeStruct((rows_in_all, width), dtype),
        scratch=[pltpu.VMEM((some, width), term.dtype) for some, terms in runs for term, _ in terms]
        + [
            pltpu.VMEM((height, width), dtype),
            pltpu.SemaphoreType.DMA((most_terms, len(tiles))),
            pltpu.SemaphoreType.DMA((len(tiles),)),
        ],
        alias={len(operands): 0} if before else None,
        name="total",
    )


def lane_pick(slot_ref, repeats, shape, rank, first):
    slot = jnp.concatenate([slot_ref[...]] * repeats, axis=0)
    return slot == lax.broadcasted_iota(jnp.int32, shape, 1) // rank + first


def block_copies(index_ref, maps_ref, buf, sems, sets, rank):
    each = index_ref.shape[0] // sets
    return [
        [
            pltpu.make_async_copy(
                maps_ref.at[index_ref[s * each + i]], buf.at[pl.ds((s * each + i) * rank, rank)],
                sems.at[s * each + i],
            )
            for i in range(each)
        ]
        for s in range(sets)
    ]


def low_rank(row_sets, slot_sets, maps, index, wide, after=()):
    sets = len(row_sets)
    count, width = row_sets[0].shape
    rank = maps.shape[1]
    span = index.shape[0] // sets * rank
    repeats = count // slot_sets[0].shape[0]
    half = count // 2
    group = 256
    tall = sets * half * 2 * rank // wide

    def kernel(index_ref, *refs):
        row_refs, slot_refs, maps_ref, out_ref = refs[:sets], refs[sets : 2 * sets], refs[2 * sets], refs[2 * sets + 1]
        rows_buf, maps_buf, row_sems, map_sems = refs[2 * sets + 2 :]
        row_copies = [
            pltpu.make_async_copy(row_refs[s], rows_buf.at[s], row_sems.at[s]) for s in range(sets)
        ]
        map_copies = block_copies(index_ref, maps_ref, maps_buf, map_sems, sets, rank)
        for s in range(sets):
            row_copies[s].start()
            for copy in map_copies[s]:
                copy.start()
        for s in range(sets):
            row_copies[s].wait()
            for copy in map_copies[s]:
                copy.wait()
            acc = None
            for at in range(0, span, group):
                scores = lax.dot_general(
                    rows_buf[s], maps_buf[s * span + at : s * span + at + group],
                    (((1,), (1,)), ((), ())), preferred_element_type=jnp.float32,
                )
                pick = lane_pick(slot_refs[s], repeats, (count, group), rank, at // rank)
                term = jnp.where(pick, scores, 0.0)
                acc = term if acc is None else acc + term
            summed = acc[:, 0:rank]
            for g in range(1, group // rank):
                summed += acc[:, g * rank : (g + 1) * rank]
            summed = summed.astype(out_ref.dtype)
            for b in range(half // tall):
                lanes = slice((s * half // tall + b) * 2 * rank, (s * half // tall + b + 1) * 2 * rank)
                both = [summed[start + b * tall : start + (b + 1) * tall] for start in (0, half)]
                out_ref[:, lanes] = jnp.concatenate(both, axis=1)

    return call(
        kernel, [index, *row_sets, *slot_sets, maps], after, prefetch=1,
        in_specs=[ANY] * sets + [pl.BlockSpec(memory_space=pltpu.VMEM)] * sets + [ANY],
        out_specs=pl.BlockSpec(memory_space=pltpu.VMEM),
        out_shape=jax.ShapeDtypeStruct((tall, wide), jnp.bfloat16),
        scratch=[
            pltpu.VMEM((sets, count, width), row_sets[0].dtype),
            pltpu.VMEM((sets * span, width), maps.dtype),
            pltpu.SemaphoreType.DMA((sets,)),
            pltpu.SemaphoreType.DMA((index.shape[0],)),
        ],
        name="low_rank",
    )


def expand(low, slot_sets, maps, index, parts, after=()):
    sets = len(slot_sets)
    rank, width = maps.shape[1:]
    tall = low.shape[0]
    half = low.size // sets // (2 * rank)
    count = 2 * half
    span = index.shape[0] // sets * rank
    repeats = count // slot_sets[0].shape[0]
    outs = [(s, first, some) for s in range(1, sets) for first, some in parts]
    outs.append((0, 0, count))

    def kernel(index_ref, low_ref, *refs):
        slot_refs, maps_ref, out_refs = refs[:sets], refs[sets], refs[sets + 1 : sets + 1 + len(outs)]
        stages, (maps_buf, map_sems, out_sems) = (
            refs[sets + 1 + len(outs) : sets + 1 + 2 * len(outs)], refs[sets + 1 + 2 * len(outs) :]
        )
        map_copies = block_copies(index_ref, maps_ref, maps_buf, map_sems, sets, rank)
        writes = [pltpu.make_async_copy(stages[o], out_refs[o], out_sems.at[o]) for o in range(len(outs))]
        order = list(range(1, sets)) + [0]
        for s in order:
            for copy in map_copies[s]:
                copy.start()
        for s in order:
            lanes = [(s * half // tall + b) * 2 * rank for b in range(half // tall)]
            mine = jnp.concatenate(
                [low_ref[:, at + side : at + side + rank] for side in (0, rank) for at in lanes], axis=0
            )
            tiled = jnp.concatenate([mine] * (span // rank), axis=1)
            pick = lane_pick(slot_refs[s], repeats, (count, span), rank, 0)
            picked = jnp.where(pick, tiled, jnp.zeros_like(tiled))
            for copy in map_copies[s]:
                copy.wait()
            for o, (which, first, some) in enumerate(outs):
                if which == s:
                    for at in range(0, width, CHUNK):
                        value = jnp.dot(
                            picked[first : first + some], maps_buf[s * span : (s + 1) * span, at : at + CHUNK],
                            preferred_element_type=jnp.float32,
                        )
                        stages[o][:, at : at + CHUNK] = value.astype(stages[o].dtype)
                    writes[o].start()
        for write in writes:
            write.wait()

    kinds = [jax.ShapeDtypeStruct((some, width), jnp.bfloat16 if s else jnp.float32) for s, _, some in outs]
    done = call(
        kernel, [index, low, *slot_sets, maps], after, prefetch=1,
        in_specs=[pl.BlockSpec(memory_space=pltpu.VMEM)] * (1 + sets) + [ANY],
        out_specs=[ANY] * len(outs),
        out_shape=kinds,
        scratch=[pltpu.VMEM(kind.shape, kind.dtype) for kind in kinds]
        + [
            pltpu.VMEM((sets * span, width), maps.dtype),
            pltpu.SemaphoreType.DMA((index.shape[0],)),
            pltpu.SemaphoreType.DMA((len(outs),)),
        ],
        name="expand",
    )
    return [done[-1]] + [done[s * len(parts) : (s + 1) * len(parts)] for s in range(sets - 1)]


def line_plan(nz):
    order = np.zeros((nz, nz), np.int32)
    for z in range(nz):
        def need(j):
            if j == z:
                return (2 * nz, 0)
            return (nz - 1 - j + z, j) if j > z else (nz - 1 - z + j, nz - j)

        order[z] = sorted(range(nz), key=need)
    return order


def on_device(attention_result, tenant, projection_weight, adapter_down_maps, adapter_up_maps):
    steps, row_count, width = attention_result.shape
    local_adapters = adapter_down_maps.shape[0]
    owners = lax.axis_size("dp")
    me = lax.axis_index("dp")
    n = lax.axis_size("tensor")
    nz = n // 2
    place = lax.axis_index("tensor")
    z, y = place // 2, place % 2
    order = line_plan(nz)
    my_order = jnp.asarray(order)[z]
    out_width = projection_weight.shape[1] // n

    def swap_y(value):
        return lax.ppermute(value, "tensor", [(t, t ^ 1) for t in range(n)])

    def hop(value, h):
        pairs = []
        for side in range(2):
            pairs.append((h * 2 + side, (h + 1) * 2 + side))
            pairs.append(((nz - 1 - h) * 2 + side, (nz - 2 - h) * 2 + side))
        return lax.ppermute(value, "tensor", pairs)

    def slot_of(h, m):
        return list(order[h]).index(nz - 1 - m)

    def pass_on(value, shift):
        return lax.ppermute(value, "dp", [(i, (i + shift) % owners) for i in range(owners)])

    rows = attention_result.reshape(steps * row_count, width)
    count = steps * row_count
    last = [()]

    def then(kernel, *operands, **options):
        out = kernel(*operands, after=last[0], **options)
        last[0] = (out[0] if isinstance(out, (tuple, list)) else out,)
        return out

    slot_range = jnp.arange(SLOTS, dtype=jnp.int32)
    ids = jnp.arange(local_adapters, dtype=jnp.int32)

    def slots(row_ids, owner):
        hit = row_ids[:, None] - owner * local_adapters == ids[None, :]
        used = jnp.any(hit, axis=0)
        position = jnp.sum(
            (used[None, :] & (ids[None, :] < ids[:, None])).astype(jnp.int32), axis=1
        )
        names = jnp.sum(
            jnp.where(used[None, :] & (position[None, :] == slot_range[:, None]), ids[None, :], 0),
            axis=1,
        )
        row_slot = jnp.sum(jnp.where(hit, position[None, :] + 1, 0), axis=1) - 1
        return names, row_slot[:, None]

    away = [(my_order[k] * 2 + 1 - y) * out_width for k in range(nz)]
    own = [(my_order[k] * 2 + y) * out_width for k in range(nz)]
    low_rows = 2 * (owners * count // 2) * adapter_down_maps.shape[1] // out_width
    even = [(p * count // PARTS, count // PARTS) for p in range(PARTS)]
    uneven = [(0, count // 2 + low_rows), (count // 2 + low_rows, count // 2 - low_rows)]
    away_part, own_all, from_y, sums, arrived = {}, {}, {}, {}, {}

    def split(k):
        return uneven if k == 0 else even

    def add_up(span, terms, extra=(), dtype=jnp.bfloat16, into=None):
        low_row, high_row = span[0], span[0] + span[1]
        cuts = {low_row, high_row}
        for term in terms:
            for at, some, _, _ in term:
                cuts.update(row for row in (at, at + some) if low_row < row < high_row)
        cuts = sorted(cuts)
        runs = []
        for begin, end in zip(cuts, cuts[1:]):
            here = [
                (array, row + begin - at) for term in terms for at, some, array, row in term if at <= begin < at + some
            ]
            runs.append((end - begin, here))
        return then(total, runs + list(extra), dtype, into)

    def whole(array):
        return [(0, count, array, 0)]

    def parts_of(arrays, cut):
        return [(at, some, array, 0) for (at, some), array in zip(cut, arrays)]

    def multiply(aways, owns, tail=None):
        ks = sorted({k for k, _ in aways})
        starts = jnp.stack([away[k] for k in ks] + [own[k] for k in owns])
        outs = [(ks.index(k), *split(k)[p]) for k, p in aways]
        outs += [(len(ks) + i, 0, count) for i in range(len(owns))]
        done = then(products, rows, projection_weight, starts, out_width, outs, tail)
        away_part.update(zip(aways, done))
        own_all.update(zip(owns, done[len(aways) :]))

    def start_y(i):
        k, p = divmod(i, PARTS)
        if k < nz:
            value = away_part[k, p]
            from_y[k, p] = swap_y(hold(value, last[0]) if i >= PARTS else value)

    def y_parts(k):
        return [(*split(k)[p], from_y[k, p], 0) for p in range(PARTS) if (k, p) in from_y]

    def sum_parts(k):
        return [(*split(k)[p], sums[k, p], 0) for p in range(PARTS) if (k, p) in sums]

    def cut_of(h, m):
        return uneven if m == 0 and h <= 1 else even

    def arrived_parts(h, m):
        return [(*cut_of(h, m)[p], arrived[h, m, p], 0) for p in range(PARTS) if (h, m, p) in arrived]

    def line(h, m, p):
        k = slot_of(h, m)
        span = cut_of(h, m)[p]
        low_too = m == 0 and h <= 1 and p == LOW_WITH[1]
        if h == 0:
            extra = [(low_rows, [(low, 0), (from_y[k, p], span[1])])] if low_too else []
            value = sums[k, p] = add_up(span, [whole(own_all[k]), y_parts(k)], extra)
        else:
            extra = [(low_rows, [(sums[k, p], span[1]), (arrived[h - 1, m, p], span[1])])] if low_too else []
            value = add_up(span, [sum_parts(k), arrived_parts(h - 1, m)], extra)
        arrived[h, m, p] = hop(value, h)

    def line_order():
        ready, free = {}, {}
        steps = [(h, m, p) for h in range(nz - 1) for m in range(nz - 1 - h) for p in range(PARTS)]
        for h, m, p in sorted(steps, key=lambda step: (step[0], step[1] * PARTS + step[2])):
            there = slot_of(h, m) * PARTS + p + 1.0
            if h:
                there = max(there, ready[h - 1, m, p, "end"])
            ready[h, m, p] = there
            free[h] = max(there, free.get(h, 0.0)) + 1.0
            ready[h, m, p, "end"] = free[h]
        return sorted(steps, key=lambda step: (ready[step], step[0]))

    row_ids = [tenant] + [pass_on(tenant, shift) for shift in range(1, owners)]
    row_sets = [rows] + [pass_on(rows, shift) for shift in range(1, owners)]
    multiply([(0, p) for p in range(PARTS - 1)], [])
    for i in range(PARTS - 1):
        start_y(i)
    named = [slots(some_ids, me) for some_ids in row_ids]
    names = jnp.concatenate([which for which, _ in named])
    slot_sets = [row_slot for _, row_slot in named]
    low = then(low_rank, row_sets, slot_sets, adapter_down_maps, names, out_width)
    multiply([LOW_WITH], [], low)
    start_y(PARTS - 1)
    multiply([(1, p) for p in range(PARTS)], [0])
    low_sum = None

    deltas = None
    started = PARTS
    for h, m, p in line_order():
        if h == 0 and (slot_of(0, m), p) == (2, 0) and nz > 2:
            low_at = uneven[LOW_WITH[1]][1]
            pieces = [(sums[LOW_WITH], low_at)]
            for step in range(nz - 1):
                if step >= 2:
                    prefix = then(total, [(low_rows, [pieces[0], pieces[-1]])])
                    pieces.append((hop(prefix, step), 0))
                else:
                    pieces.append((arrived[step, 0, LOW_WITH[1]], low_at))
            low_sum = then(total, [(low_rows, pieces)])
        line(h, m, p)
        if h == 0:
            start_y(started)
            started += 1
            if started == PARTS + 1:
                multiply([(k, q) for k in range(2, nz) for q in range(PARTS)], range(1, nz))
        if low_sum is not None and deltas is None:
            deltas = then(expand, low_sum, slot_sets, adapter_up_maps, names, even)
            back = {}
            for shift in range(1, owners):
                for q in range(PARTS):
                    back[shift, q] = pass_on(deltas[shift][q], -shift)
    head = [whole(own_all[nz - 1]), whole(deltas[0])]
    head += [parts_of([back[shift, q] for q in range(PARTS)], even) for shift in range(1, owners)]
    out = None
    for span in even:
        most = add_up(span, head + [arrived_parts(h, nz - 2 - h) for h in range(nz - 1)], dtype=jnp.float32)
        out = add_up(span, [[(*span, most, 0)], y_parts(nz - 1)], into=(count, span[0], out))
    return out.reshape(steps, row_count, out_width)


def solution(mesh):
    placed = (
        P(None, ("groups", "dp"), "tensor"),
        P(("groups", "dp")),
        P("tensor", None),
        P(("groups", "dp"), None, "tensor"),
        P(("groups", "dp"), None, "tensor"),
    )
    return jax.shard_map(
        on_device,
        mesh=mesh,
        in_specs=placed,
        out_specs=P(None, ("groups", "dp"), "tensor"),
        check_vma=False,
    )
```

time: 353 us -> 197 us (0.56)
  waiting for transfers between devices: 244 us -> 45.3 us
  Pallas kernels: 0 us -> 90.8 us
  matrix products: 74.6 us -> 0 us
  starting transfers between devices: 6.01 us -> 43.2 us
  between operations: 14.1 us -> 3.51 us
  blocking collectives: 10.1 us -> 0 us
  local copies, waits for them, and re-layouts: 2.43 us -> 11.8 us
    reduce_scatter x1 -> x0, waiting for transfers between devices: 211 us -> none  [on_device(): lax.psum_scatter(partial_value.astype(jnp.bfloat16), 'tensor', scatter_di...]
    pallas_call x0 -> x30, Pallas kernels: none -> 90.8 us  [call(): pl.pallas_call(body, grid_spec=pltpu.PrefetchScalarGridSpec(num_scalar_pr...]
    dot_general x6 -> x0, matrix products: 74.6 us -> none  [the longest x1 21.2 us: on_device(): jnp.dot(flat_rows, projection_weight, preferred_element_type=jnp.float32)]
    ppermute x0 -> x25, waiting for transfers between devices: none -> 45.3 us  [the longest x13 45.3 us: hop(): return lax.ppermute(value, 'tensor', pairs)]
    ppermute x0 -> x25, starting transfers between devices: none -> 43.2 us  [the longest x13 34.5 us: hop(): return lax.ppermute(value, 'tensor', pairs)]
    psum x1 -> x0, waiting for transfers between devices: 29.6 us -> none  [on_device(): low_rank = lax.psum(low_part.astype(jnp.bfloat16), 'tensor')]
    all_to_all x1 -> x0, blocking collectives: 8.18 us -> none  [on_device(): lax.all_to_all(send_up, 'dp', split_axis=0, concat_axis=0, tiled=True)]
    unnamed x10 -> x46, local copies, waits for them, and re-layouts: 2.26 us -> 10.1 us
  transfers between devices with their start and end apart: 3 -> 25, of which waited for: 3 -> 5; matrix products, arithmetic and copies ran while one was open for 10% -> 1% of each run, Pallas kernels for 0% -> 46%
where the time goes in v4:
time: 197 us; the launch traced here: 196 us
  Pallas kernels  90.8 us (46%)
  waiting for transfers between devices  45.3 us (23%)
  starting transfers between devices  43.2 us (22%)
  local copies, waits for them, and re-layouts  11.8 us (6%)
  between operations  3.51 us (2%)
    pallas_call x30, Pallas kernels, call(): pl.pallas_call(body, grid_spec=pltpu.PrefetchScalarGridSpec(num_scalar_pr...  90.8 us
    ppermute x13, waiting for transfers between devices, hop(): return lax.ppermute(value, 'tensor', pairs)  45.3 us
    ppermute x13, starting transfers between devices, hop(): return lax.ppermute(value, 'tensor', pairs)  34.5 us
    unnamed x46, local copies, waits for them, and re-layouts  10.1 us
    ppermute x8, starting transfers between devices, swap_y(): return lax.ppermute(value, 'tensor', [(t, t ^ 1) for t in range(n)])  8.12 us
  transfers between devices with their start and end apart: 25, of which 5 were waited for; matrix products, arithmetic and copies ran while one was open for 1% of the time, Pallas kernels for 46%

profile of v4, /device:TPU:0, one launch (start us, length us, event | category | flops | bytes accessed | tf_op | source)
XLA Modules:
  0.0 195.6 jit_solution(6877633372155797726)
XLA Ops:
  2.5 1.4 copy-done
  3.9 4.4 %products.4.refs_6_ = bf16[480,1024]{1,0:T(8,128)(2,1)S(1)} custom-call(s32[1]{0:T(128)} %bitcast.12.refs_0_, bf16[768,1024]{1,0:T(8,128)(2,1)S(1)} %bitcast.19, bf16[1024,8192]{1,0:T(8,128)(2,1)} %refs_2_.7), custom_call_target="tpu_custom_call" | custom-call | flops 1 | bytes 1 | tf_op jit(solution)/shard_map/products/pallas_call | solution.py:24
  8.3 3.0 %collective-permute-start.2 = (bf16[480,1024]{1,0:T(8,128)(2,1)S(1)}, bf16[480,1024]{1,0:T(8,128)(2,1)}, u32[]{:S(2)}, u32[]{:S(2)}) collective-permute-start(bf16[480,1024]{1,0:T(8,128)(2,1)S(1)} %products.4.refs_6_), channel_id=1, source_target_pairs={{0,2},{2,0},{4,6},{6,4},{8,10},{10,8},{12,14},{14,12},{1,3},{3,1},... | collective-permute-start | bytes 2949128 | tf_op jit(solution)/shard_map/ppermute | solution.py:372
  13.3 6.8 %low_rank.1.refs_3_.refs_4_.refs_2_ = bf16[96,1024]{1,0:T(8,128)(2,1)S(1)} custom-call(s32[32]{0:T(128)S(1)} %pad_add_fusion.1.refs_0_, bf16[768,1024]{1,0:T(8,128)(2,1)S(1)} %bitcast.20, bf16[768,1024]{1,0:T(8,128)(2,1)} %collective-permute-done.1.refs_2_, s32[192,1]{1,0:T(8,128)S(1)} %copy.18.refs_3_.refs_2_, s32[192,1]{1,0:T(8,128)S(1)} %copy.19.refs_4_.refs_3_, ...), custom_call_target="tpu_custom_call" | custom-call | flops 1 | bytes 1 | tf_op jit(solution)/shard_map/low_rank/pallas_call | solution.py:24
  20.1 3.1 %products.5.refs_3_ = bf16[384,1024]{1,0:T(8,128)(2,1)S(1)} custom-call(s32[1]{0:T(128)} %bitcast.12.refs_0_, bf16[768,1024]{1,0:T(8,128)(2,1)S(1)} %bitcast.21, bf16[1024,8192]{1,0:T(8,128)(2,1)} %refs_2_.7, bf16[96,1024]{1,0:T(8,128)(2,1)S(1)} %low_rank.1.refs_3_.refs_4_.refs_2_, bf16[96,1024]{1,0:T(8,128)(2,1)S(1)} %low_rank.1.refs_3_.refs_4_.refs_2_), custom_call_target="tpu_custom_call" | custom-call | flops 1 | bytes 1 | tf_op jit(solution)/shard_map/products/pallas_call | solution.py:24
  23.4 9.8 %products.6 = (bf16[384,1024]{1,0:T(8,128)(2,1)}, bf16[384,1024]{1,0:T(8,128)(2,1)S(1)}, bf16[768,1024]{1,0:T(8,128)(2,1)S(1)}) custom-call(s32[2]{0:T(128)S(1)} %pad_add_fusion.refs_0_, bf16[768,1024]{1,0:T(8,128)(2,1)} %bitcast.17, bf16[1024,8192]{1,0:T(8,128)(2,1)} %refs_2_.7, bf16[384,1024]{1,0:T(8,128)(2,1)S(1)} %products.5.refs_3_), custom_call_target="tpu_custom_call" | custom-call | flops 1 | bytes 1 | tf_op jit(solution)/shard_map/products/pallas_call | solution.py:24
  33.2 1.1 copy-done.7
  34.3 1.0 copy-done.16
  35.3 2.1 %total.18.refs_3_.refs_1_.refs_0_ = bf16[480,1024]{1,0:T(8,128)(2,1)S(1)} custom-call(bf16[768,1024]{1,0:T(8,128)(2,1)} %copy-done.7, bf16[480,1024]{1,0:T(8,128)(2,1)} %collective-permute-done.2.refs_1_, bf16[384,1024]{1,0:T(8,128)(2,1)} %get-tuple-element.19.refs_2_.refs_0_), custom_call_target="tpu_custom_call" | custom-call | flops 1 | bytes 1 | tf_op jit(solution)/shard_map/total/pallas_call | solution.py:24
  37.4 4.9 %collective-permute-start.6 = (bf16[480,1024]{1,0:T(8,128)(2,1)S(1)}, bf16[480,1024]{1,0:T(8,128)(2,1)}, u32[]{:S(2)}, u32[]{:S(2)}) collective-permute-start(bf16[480,1024]{1,0:T(8,128)(2,1)S(1)} %total.18.refs_3_.refs_1_.refs_0_), channel_id=1, source_target_pairs={{0,4},{12,8},{2,6},{14,10},{1,5},{13,9},{3,7},{15,11},{16,20},{28,... | collective-permute-start | bytes 2949128 | tf_op jit(solution)/shard_map/ppermute | solution.py:379
  42.3 1.5 collective-permute-start.5
  45.2 26.9 %products.7 = (bf16[384,1024]{1,0:T(8,128)(2,1)S(1)}, bf16[384,1024]{1,0:T(8,128)(2,1)}, bf16[384,1024]{1,0:T(8,128)(2,1)S(1)}, bf16[384,1024]{1,0:T(8,128)(2,1)...) custom-call(s32[5]{0:T(128)S(1)} %stack.36.refs_0_, ...), custom_call_target="tpu_custom_call" | custom-call | flops 1 | bytes 1 | tf_op jit(solution)/shard_map/products/pallas_call | solution.py:24
  72.1 0.9 copy-done.14
  73.0 1.7 total.19.refs_2_.refs_0_.refs_1_
  74.7 1.7 collective-permute-start.4
  77.0 2.2 %total.20.refs_2_ = bf16[480,1024]{1,0:T(8,128)(2,1)S(1)} custom-call(bf16[480,1024]{1,0:T(8,128)(2,1)S(1)} %copy-done.3, bf16[480,1024]{1,0:T(8,128)(2,1)} %collective-permute-done.6.refs_1_, bf16[384,1024]{1,0:T(8,128)(2,1)S(1)} %total.19.refs_2_.refs_0_.refs_1_), custom_call_target="tpu_custom_call" | custom-call | flops 1 | bytes 1 | tf_op jit(solution)/shard_map/total/pallas_call | solution.py:24
  79.3 1.4 total.21.refs_4_.refs_0_.refs_1_
  80.7 1.3 collective-permute-start.8
  82.0 12.0 %collective-permute-done.4.refs_1_.refs_3_ = bf16[384,1024]{1,0:T(8,128)(2,1)S(1)} collective-permute-done((bf16[384,1024]{1,0:T(8,128)(2,1)S(1)}, bf16[384,1024]{1,0:T(8,128)(2,1)S(1)}, u32[]{:S(2)}, u32[]{:S(2)}) %collective-permute-start.4) | collective-permute-done | bytes 786464 | tf_op jit(solution)/shard_map/ppermute | solution.py:379
  94.1 1.4 total.22.refs_2_
  97.5 0.9 copy-done.18
  98.4 1.1 copy-done.19
  99.5 1.4 total.23.refs_2_.refs_1_.refs_0_
  100.9 9.7 %collective-permute-start.15 = (bf16[384,1024]{1,0:T(8,128)(2,1)S(1)}, bf16[384,1024]{1,0:T(8,128)(2,1)}, u32[]{:S(2)}, u32[]{:S(2)}) collective-permute-start(bf16[384,1024]{1,0:T(8,128)(2,1)S(1)} %total.23.refs_2_.refs_1_.refs_0_), channel_id=1, source_target_pairs={{0,4},{12,8},{2,6},{14,10},{1,5},{13,9},{3,7},{15,11},{16,20},{28,... | collective-permute-start | bytes 2359304 | tf_op jit(solution)/shard_map/ppermute | solution.py:379
  110.9 1.2 collective-permute-start.13
  112.1 1.4 total.24.refs_2_
  114.3 1.4 collective-permute-start.10
  115.8 10.4 %collective-permute-done.10.refs_3_ = bf16[96,1024]{1,0:T(8,128)(2,1)S(1)} collective-permute-done((bf16[96,1024]{1,0:T(8,128)(2,1)S(1)}, bf16[96,1024]{1,0:T(8,128)(2,1)S(1)}, u32[]{:S(2)}, u32[]{:S(2)}) %collective-permute-start.10) | collective-permute-done | bytes 196640 | tf_op jit(solution)/shard_map/ppermute | solution.py:379
  126.9 1.4 total.26.refs_2_.refs_1_
  128.4 1.4 total.27.refs_5_.refs_0_.refs_1_
  129.7 4.3 %collective-permute-start.20 = (bf16[384,1024]{1,0:T(8,128)(2,1)S(1)}, bf16[384,1024]{1,0:T(8,128)(2,1)S(1)}, u32[]{:S(2)}, u32[]{:S(2)}) collective-permute-start(bf16[384,1024]{1,0:T(8,128)(2,1)S(1)} %total.27.refs_5_.refs_0_.refs_1_), channel_id=1, source_target_pairs={{0,4},{12,8},{2,6},{14,10},{1,5},{13,9},{3,7},{15,11},{16,20},{28,... | collective-permute-start | bytes 2359304 | tf_op jit(solution)/shard_map/ppermute | solution.py:379
  134.0 8.1 %expand.1 = (bf16[384,1024]{1,0:T(8,128)(2,1)}, bf16[384,1024]{1,0:T(8,128)(2,1)S(1)}, f32[768,1024]{1,0:T(8,128)}) custom-call(s32[32]{0:T(128)S(1)} %pad_add_fusion.1.refs_0_, bf16[96,1024]{1,0:T(8,128)(2,1)S(1)} %total.26.refs_2_.refs_1_, s32[192,1]{1,0:T(8,128)S(1)} %copy-done.11, s32[192,1]{1,0:T(8,128)S(1)} %copy-done.13, ...), custom_call_target="tpu_custom_call" | custom-call | flops 1 | bytes 1 | tf_op jit(solution)/shard_map/expand/pallas_call | solution.py:24
  142.2 0.9 copy-done.20
  143.1 1.8 total.28.refs_2_
  144.9 1.4 total.29.refs_2_
  146.3 1.3 collective-permute-start.22
  148.2 1.8 total.30.refs_0_.refs_2_.refs_4_.refs_1_
  150.0 1.4 total.31.refs_6_
  151.4 5.7 %collective-permute-start.16 = (bf16[384,1024]{1,0:T(8,128)(2,1)S(1)}, bf16[384,1024]{1,0:T(8,128)(2,1)S(1)}, u32[]{:S(2)}, u32[]{:S(2)}) collective-permute-start(bf16[384,1024]{1,0:T(8,128)(2,1)S(1)} %total.30.refs_0_.refs_2_.refs_4_.refs_1_), channel_id=1, source_target_pairs={{0,4},{12,8},{2,6},{14,10},{1,5},{13,9},{3,7},{15,11},{16,20},{28,... | collective-permute-start | bytes 2359304 | tf_op jit(solution)/shard_map/ppermute | solution.py:379
  158.0 10.1 %collective-permute-done.22.refs_5_ = bf16[384,1024]{1,0:T(8,128)(2,1)S(1)} collective-permute-done((bf16[384,1024]{1,0:T(8,128)(2,1)S(1)}, bf16[384,1024]{1,0:T(8,128)(2,1)S(1)}, u32[]{:S(2)}, u32[]{:S(2)}) %collective-permute-start.22) | collective-permute-done | bytes 786464 | tf_op jit(solution)/shard_map/ppermute | solution.py:379
  168.1 1.3 collective-permute-start.18
  170.0 3.3 %total.32.refs_0_.refs_2_ = f32[384,1024]{1,0:T(8,128)} custom-call(bf16[768,1024]{1,0:T(8,128)(2,1)} %get-tuple-element.20.refs_0_, f32[768,1024]{1,0:T(8,128)} %get-tuple-element.25.refs_2_.refs_1_, bf16[384,1024]{1,0:T(8,128)(2,1)S(1)} %collective-permute-done.19.refs_2_, bf16[384,1024]{1,0:T(8,128)(2,1)S(1)} %collective-permute-done.20.refs_3_, ...), custom_call_target="tpu_custom_call" | custom-call | flops 1 | bytes 1 | tf_op jit(solution)/shard_map/total/pallas_call | solution.py:24
  173.4 1.4 copy-done.5
  174.8 2.0 %total.33.refs_6_.refs_2_ = bf16[768,1024]{1,0:T(8,128)(2,1)} custom-call(f32[384,1024]{1,0:T(8,128)S(1)} %copy-done.5, bf16[384,1024]{1,0:T(8,128)(2,1)} %collective-permute-done.23.refs_1_, f32[384,1024]{1,0:T(8,128)S(1)} %copy-done.5), custom_call_target="tpu_custom_call" | custom-call | flops 1 | bytes 1 | tf_op jit(solution)/shard_map/total/pallas_call | solution.py:24
  176.8 12.3 %collective-permute-done.18.refs_5_ = bf16[384,1024]{1,0:T(8,128)(2,1)S(1)} collective-permute-done((bf16[384,1024]{1,0:T(8,128)(2,1)S(1)}, bf16[384,1024]{1,0:T(8,128)(2,1)S(1)}, u32[]{:S(2)}, u32[]{:S(2)}) %collective-permute-start.18) | collective-permute-done | bytes 786464 | tf_op jit(solution)/shard_map/ppermute | solution.py:379
  189.2 3.4 %total.34.refs_0_.refs_3_ = f32[384,1024]{1,0:T(8,128)} custom-call(bf16[768,1024]{1,0:T(8,128)(2,1)} %get-tuple-element.20.refs_0_, f32[768,1024]{1,0:T(8,128)} %get-tuple-element.25.refs_2_.refs_1_, bf16[384,1024]{1,0:T(8,128)(2,1)S(1)} %collective-permute-done.12.refs_2_, bf16[384,1024]{1,0:T(8,128)(2,1)S(1)} %collective-permute-done.16.refs_3_, ...), custom_call_target="tpu_custom_call" | custom-call | flops 1 | bytes 1 | tf_op jit(solution)/shard_map/total/pallas_call | solution.py:24
  192.6 1.4 copy-done.4
  194.0 1.5 total.35
  (98 shorter events, 9.7 us)
Async XLA Ops:
  0.0 12.6 %collective-permute-start = (s32[192]{0:T(256)}, s32[192]{0:T(256)S(1)}, u32[]{:S(2)}, u32[]{:S(2)}) collective-permute-start(s32[192]{0:T(256)} %param.7), channel_id=1, source_target_pairs={{0,1},{1,0},{2,3},{3,2},{4,5},{5,4},{6,7},{7,6},{8,9},{9,8},{10,11... | collective-permute-start | bytes 2312 | tf_op jit(solution)/shard_map/ppermute | solution.py:385
  0.5 12.8 %collective-permute-start.1 = (bf16[768,1024]{1,0:T(8,128)(2,1)}, bf16[768,1024]{1,0:T(8,128)(2,1)}, u32[]{:S(2)}, u32[]{:S(2)}) collective-permute-start(bf16[768,1024]{1,0:T(8,128)(2,1)} %bitcast.16), channel_id=1, source_target_pairs={{0,1},{1,0},{2,3},{3,2},{4,5},{5,4},{6,7},{7,6},{8,9},{9,8},{10,11... | collective-permute-start | bytes 4718600 | tf_op jit(solution)/shard_map/ppermute | solution.py:385
  2.5 1.4 copy-start
  3.9 7.4 %copy-start.22 = (s32[192]{0:T(256)S(1)}, s32[192]{0:T(256)}, u32[]{:S(2)}) copy-start(s32[192]{0:T(256)} %param.7) | copy-start | bytes 2308
  3.9 9.4 %copy-start.1 = (bf16[4,192,1024]{2,1,0:T(8,128)(2,1)S(1)}, bf16[4,192,1024]{2,1,0:T(8,128)(2,1)}, u32[]{:S(2)}) copy-start(bf16[4,192,1024]{2,1,0:T(8,128)(2,1)} %param.6) | copy-start | bytes 4718596
  8.3 26.9 %collective-permute-start.2 = (bf16[480,1024]{1,0:T(8,128)(2,1)S(1)}, bf16[480,1024]{1,0:T(8,128)(2,1)}, u32[]{:S(2)}, u32[]{:S(2)}) collective-permute-start(bf16[480,1024]{1,0:T(8,128)(2,1)S(1)} %products.4.refs_6_), channel_id=1, source_target_pairs={{0,2},{2,0},{4,6},{6,4},{8,10},{10,8},{12,14},{14,12},{1,3},{3,1},... | collective-permute-start | bytes 2949128 | tf_op jit(solution)/shard_map/ppermute | solution.py:372
  12.6 7.5 %copy-start.10 = (s32[192,1]{1,0:T(8,128)}, s32[192,1]{1,0:T(8,128)S(1)}, u32[]{:S(2)}) copy-start(s32[192,1]{1,0:T(8,128)S(1)} %copy.18.refs_3_.refs_2_) | copy-start | bytes 2308
  13.1 7.0 %copy-start.12 = (s32[192,1]{1,0:T(8,128)}, s32[192,1]{1,0:T(8,128)S(1)}, u32[]{:S(2)}) copy-start(s32[192,1]{1,0:T(8,128)S(1)} %copy.19.refs_4_.refs_3_) | copy-start | bytes 2308
  23.2 49.7 %collective-permute-start.3 = (bf16[384,1024]{1,0:T(8,128)(2,1)S(1)}, bf16[384,1024]{1,0:T(8,128)(2,1)}, u32[]{:S(2)}, u32[]{:S(2)}) collective-permute-start(bf16[384,1024]{1,0:T(8,128)(2,1)S(1)} %products.5.refs_3_), channel_id=1, source_target_pairs={{0,2},{2,0},{4,6},{6,4},{8,10},{10,8},{12,14},{14,12},{1,3},{3,1},... | collective-permute-start | bytes 2359304 | tf_op jit(solution)/shard_map/ppermute | solution.py:372
  33.2 1.1 copy-start.7
  34.3 1.0 copy-start.16
  37.4 7.8 %copy-start.2 = (bf16[480,1024]{1,0:T(8,128)(2,1)}, bf16[480,1024]{1,0:T(8,128)(2,1)S(1)}, u32[]{:S(2)}) copy-start(bf16[480,1024]{1,0:T(8,128)(2,1)S(1)} %total.18.refs_3_.refs_1_.refs_0_) | copy-start | bytes 2949124
  37.4 39.6 %collective-permute-start.6 = (bf16[480,1024]{1,0:T(8,128)(2,1)S(1)}, bf16[480,1024]{1,0:T(8,128)(2,1)}, u32[]{:S(2)}, u32[]{:S(2)}) collective-permute-start(bf16[480,1024]{1,0:T(8,128)(2,1)S(1)} %total.18.refs_3_.refs_1_.refs_0_), channel_id=1, source_target_pairs={{0,4},{12,8},{2,6},{14,10},{1,5},{13,9},{3,7},{15,11},{16,20},{28,... | collective-permute-start | bytes 2949128 | tf_op jit(solution)/shard_map/ppermute | solution.py:379
  42.3 37.0 %collective-permute-start.5 = (bf16[384,1024]{1,0:T(8,128)(2,1)}, bf16[384,1024]{1,0:T(8,128)(2,1)S(1)}, u32[]{:S(2)}, u32[]{:S(2)}) collective-permute-start(bf16[384,1024]{1,0:T(8,128)(2,1)} %hold.6), channel_id=1, source_target_pairs={{0,2},{2,0},{4,6},{6,4},{8,10},{10,8},{12,14},{14,12},{1,3},{3,1},... | collective-permute-start | bytes 2359304 | tf_op jit(solution)/shard_map/ppermute | solution.py:372
  45.2 27.8 %copy-start.8 = (bf16[768,1024]{1,0:T(8,128)(2,1)S(1)}, bf16[768,1024]{1,0:T(8,128)(2,1)}, u32[]{:S(2)}) copy-start(bf16[768,1024]{1,0:T(8,128)(2,1)} %copy-done.7) | copy-start | bytes 4718596
  72.1 0.9 copy-start.14
  73.0 3.4 %copy-start.17 = (bf16[384,1024]{1,0:T(8,128)(2,1)S(1)}, bf16[384,1024]{1,0:T(8,128)(2,1)}, u32[]{:S(2)}) copy-start(bf16[384,1024]{1,0:T(8,128)(2,1)} %copy-done.16) | copy-start | bytes 2359300
  74.7 2.3 %copy-start.3 = (bf16[480,1024]{1,0:T(8,128)(2,1)S(1)}, bf16[480,1024]{1,0:T(8,128)(2,1)}, u32[]{:S(2)}) copy-start(bf16[480,1024]{1,0:T(8,128)(2,1)} %copy-done.2) | copy-start | bytes 2949124
  74.7 19.4 %collective-permute-start.4 = (bf16[384,1024]{1,0:T(8,128)(2,1)S(1)}, bf16[384,1024]{1,0:T(8,128)(2,1)S(1)}, u32[]{:S(2)}, u32[]{:S(2)}) collective-permute-start(bf16[384,1024]{1,0:T(8,128)(2,1)S(1)} %total.19.refs_2_.refs_0_.refs_1_), channel_id=1, source_target_pairs={{0,4},{12,8},{2,6},{14,10},{1,5},{13,9},{3,7},{15,11},{16,20},{28,... | collective-permute-start | bytes 2359304 | tf_op jit(solution)/shard_map/ppermute | solution.py:379
  76.4 2.9 %copy-start.9 = (bf16[768,1024]{1,0:T(8,128)(2,1)S(1)}, bf16[768,1024]{1,0:T(8,128)(2,1)}, u32[]{:S(2)}) copy-start(bf16[768,1024]{1,0:T(8,128)(2,1)} %get-tuple-element.22.refs_0_) | copy-start | bytes 4718596
  76.4 21.1 %collective-permute-start.9 = (bf16[384,1024]{1,0:T(8,128)(2,1)S(1)}, bf16[384,1024]{1,0:T(8,128)(2,1)S(1)}, u32[]{:S(2)}, u32[]{:S(2)}) collective-permute-start(bf16[384,1024]{1,0:T(8,128)(2,1)S(1)} %hold.7), channel_id=1, source_target_pairs={{0,2},{2,0},{4,6},{6,4},{8,10},{10,8},{12,14},{14,12},{1,3},{3,1},... | collective-permute-start | bytes 2359304 | tf_op jit(solution)/shard_map/ppermute | solution.py:372
  80.7 30.2 %collective-permute-start.8 = (bf16[384,1024]{1,0:T(8,128)(2,1)S(1)}, bf16[384,1024]{1,0:T(8,128)(2,1)S(1)}, u32[]{:S(2)}, u32[]{:S(2)}) collective-permute-start(bf16[384,1024]{1,0:T(8,128)(2,1)S(1)} %total.21.refs_4_.refs_0_.refs_1_), channel_id=1, source_target_pairs={{0,4},{12,8},{2,6},{14,10},{1,5},{13,9},{3,7},{15,11},{16,20},{28,... | collective-permute-start | bytes 2359304 | tf_op jit(solution)/shard_map/ppermute | solution.py:379
  95.5 18.0 %collective-permute-start.7 = (bf16[384,1024]{1,0:T(8,128)(2,1)S(1)}, bf16[384,1024]{1,0:T(8,128)(2,1)S(1)}, u32[]{:S(2)}, u32[]{:S(2)}) collective-permute-start(bf16[384,1024]{1,0:T(8,128)(2,1)S(1)} %total.22.refs_2_), channel_id=1, source_target_pairs={{4,8},{8,4},{6,10},{10,6},{5,9},{9,5},{7,11},{11,7},{20,24},{24,20... | collective-permute-start | bytes 2359304 | tf_op jit(solution)/shard_map/ppermute | solution.py:379
  96.2 48.7 %collective-permute-start.14 = (bf16[480,1024]{1,0:T(8,128)(2,1)S(1)}, bf16[480,1024]{1,0:T(8,128)(2,1)S(1)}, u32[]{:S(2)}, u32[]{:S(2)}) collective-permute-start(bf16[480,1024]{1,0:T(8,128)(2,1)S(1)} %total.20.refs_2_), channel_id=1, source_target_pairs={{4,8},{8,4},{6,10},{10,6},{5,9},{9,5},{7,11},{11,7},{20,24},{24,20... | collective-permute-start | bytes 2949128 | tf_op jit(solution)/shard_map/ppermute | solution.py:379
  96.9 31.4 %collective-permute-start.11 = (bf16[384,1024]{1,0:T(8,128)(2,1)S(1)}, bf16[384,1024]{1,0:T(8,128)(2,1)S(1)}, u32[]{:S(2)}, u32[]{:S(2)}) collective-permute-start(bf16[384,1024]{1,0:T(8,128)(2,1)S(1)} %hold.8), channel_id=1, source_target_pairs={{0,2},{2,0},{4,6},{6,4},{8,10},{10,8},{12,14},{14,12},{1,3},{3,1},... | collective-permute-start | bytes 2359304 | tf_op jit(solution)/shard_map/ppermute | solution.py:372
  97.5 0.9 copy-start.18
  98.4 1.1 copy-start.19
  100.9 42.2 %collective-permute-start.15 = (bf16[384,1024]{1,0:T(8,128)(2,1)S(1)}, bf16[384,1024]{1,0:T(8,128)(2,1)}, u32[]{:S(2)}, u32[]{:S(2)}) collective-permute-start(bf16[384,1024]{1,0:T(8,128)(2,1)S(1)} %total.23.refs_2_.refs_1_.refs_0_), channel_id=1, source_target_pairs={{0,4},{12,8},{2,6},{14,10},{1,5},{13,9},{3,7},{15,11},{16,20},{28,... | collective-permute-start | bytes 2359304 | tf_op jit(solution)/shard_map/ppermute | solution.py:379
  110.9 36.7 %collective-permute-start.13 = (bf16[384,1024]{1,0:T(8,128)(2,1)}, bf16[384,1024]{1,0:T(8,128)(2,1)}, u32[]{:S(2)}, u32[]{:S(2)}) collective-permute-start(bf16[384,1024]{1,0:T(8,128)(2,1)} %hold.9), channel_id=1, source_target_pairs={{0,2},{2,0},{4,6},{6,4},{8,10},{10,8},{12,14},{14,12},{1,3},{3,1},... | collective-permute-start | bytes 2359304 | tf_op jit(solution)/shard_map/ppermute | solution.py:372
  114.3 14.0 %copy-start.6 = (bf16[768,1024]{1,0:T(8,128)(2,1)S(1)}, bf16[768,1024]{1,0:T(8,128)(2,1)}, u32[]{:S(2)}) copy-start(bf16[768,1024]{1,0:T(8,128)(2,1)} %get-tuple-element.24.refs_0_) | copy-start | bytes 4718596
  114.3 11.9 %collective-permute-start.10 = (bf16[96,1024]{1,0:T(8,128)(2,1)S(1)}, bf16[96,1024]{1,0:T(8,128)(2,1)S(1)}, u32[]{:S(2)}, u32[]{:S(2)}) collective-permute-start(bf16[96,1024]{1,0:T(8,128)(2,1)S(1)} %total.25.refs_4_), channel_id=1, source_target_pairs={{8,12},{4,0},{10,14},{6,2},{9,13},{5,1},{11,15},{7,3},{24,28},{20,... | collective-permute-start | bytes 589832 | tf_op jit(solution)/shard_map/ppermute | solution.py:379
  126.2 25.2 %collective-permute-start.21 = (bf16[384,1024]{1,0:T(8,128)(2,1)S(1)}, bf16[384,1024]{1,0:T(8,128)(2,1)S(1)}, u32[]{:S(2)}, u32[]{:S(2)}) collective-permute-start(bf16[384,1024]{1,0:T(8,128)(2,1)S(1)} %total.24.refs_2_), channel_id=1, source_target_pairs={{4,8},{8,4},{6,10},{10,6},{5,9},{9,5},{7,11},{11,7},{20,24},{24,20... | collective-permute-start | bytes 2359304 | tf_op jit(solution)/shard_map/ppermute | solution.py:379
  128.3 5.7 %copy-start.11 = (s32[192,1]{1,0:T(8,128)S(1)}, s32[192,1]{1,0:T(8,128)}, u32[]{:S(2)}) copy-start(s32[192,1]{1,0:T(8,128)} %copy-done.10) | copy-start | bytes 2308
  128.4 5.7 %copy-start.13 = (s32[192,1]{1,0:T(8,128)S(1)}, s32[192,1]{1,0:T(8,128)}, u32[]{:S(2)}) copy-start(s32[192,1]{1,0:T(8,128)} %copy-done.12) | copy-start | bytes 2308
  129.7 27.5 %collective-permute-start.20 = (bf16[384,1024]{1,0:T(8,128)(2,1)S(1)}, bf16[384,1024]{1,0:T(8,128)(2,1)S(1)}, u32[]{:S(2)}, u32[]{:S(2)}) collective-permute-start(bf16[384,1024]{1,0:T(8,128)(2,1)S(1)} %total.27.refs_5_.refs_0_.refs_1_), channel_id=1, source_target_pairs={{0,4},{12,8},{2,6},{14,10},{1,5},{13,9},{3,7},{15,11},{16,20},{28,... | collective-permute-start | bytes 2359304 | tf_op jit(solution)/shard_map/ppermute | solution.py:379
  142.2 0.9 copy-start.20
  143.1 14.1 %collective-permute-start.19 = (bf16[384,1024]{1,0:T(8,128)(2,1)}, bf16[384,1024]{1,0:T(8,128)(2,1)S(1)}, u32[]{:S(2)}, u32[]{:S(2)}) collective-permute-start(bf16[384,1024]{1,0:T(8,128)(2,1)} %get-tuple-element.28), channel_id=1, source_target_pairs={{0,1},{1,0},{2,3},{3,2},{4,5},{5,4},{6,7},{7,6},{8,9},{9,8},{10,11... | collective-permute-start | bytes 2359304 | tf_op jit(solution)/shard_map/ppermute | solution.py:385
  144.9 2.7 %copy-start.15 = (bf16[384,1024]{1,0:T(8,128)(2,1)S(1)}, bf16[384,1024]{1,0:T(8,128)(2,1)}, u32[]{:S(2)}) copy-start(bf16[384,1024]{1,0:T(8,128)(2,1)} %copy-done.14) | copy-start | bytes 2359300
  146.3 21.8 %collective-permute-start.22 = (bf16[384,1024]{1,0:T(8,128)(2,1)S(1)}, bf16[384,1024]{1,0:T(8,128)(2,1)S(1)}, u32[]{:S(2)}, u32[]{:S(2)}) collective-permute-start(bf16[384,1024]{1,0:T(8,128)(2,1)S(1)} %total.29.refs_2_), channel_id=1, source_target_pairs={{8,12},{4,0},{10,14},{6,2},{9,13},{5,1},{11,15},{7,3},{24,28},{20,... | collective-permute-start | bytes 2359304 | tf_op jit(solution)/shard_map/ppermute | solution.py:379
  147.6 21.8 %collective-permute-start.23 = (bf16[384,1024]{1,0:T(8,128)(2,1)S(1)}, bf16[384,1024]{1,0:T(8,128)(2,1)}, u32[]{:S(2)}, u32[]{:S(2)}) collective-permute-start(bf16[384,1024]{1,0:T(8,128)(2,1)S(1)} %hold.10), channel_id=1, source_target_pairs={{0,2},{2,0},{4,6},{6,4},{8,10},{10,8},{12,14},{14,12},{1,3},{3,1},... | collective-permute-start | bytes 2359304 | tf_op jit(solution)/shard_map/ppermute | solution.py:372
  150.0 7.2 %copy-start.21 = (bf16[384,1024]{1,0:T(8,128)(2,1)S(1)}, bf16[384,1024]{1,0:T(8,128)(2,1)}, u32[]{:S(2)}) copy-start(bf16[384,1024]{1,0:T(8,128)(2,1)} %copy-done.20) | copy-start | bytes 2359300
  151.4 25.4 %collective-permute-start.16 = (bf16[384,1024]{1,0:T(8,128)(2,1)S(1)}, bf16[384,1024]{1,0:T(8,128)(2,1)S(1)}, u32[]{:S(2)}, u32[]{:S(2)}) collective-permute-start(bf16[384,1024]{1,0:T(8,128)(2,1)S(1)} %total.30.refs_0_.refs_2_.refs_4_.refs_1_), channel_id=1, source_target_pairs={{0,4},{12,8},{2,6},{14,10},{1,5},{13,9},{3,7},{15,11},{16,20},{28,... | collective-permute-start | bytes 2359304 | tf_op jit(solution)/shard_map/ppermute | solution.py:379
  157.2 19.6 %collective-permute-start.12 = (bf16[384,1024]{1,0:T(8,128)(2,1)S(1)}, bf16[384,1024]{1,0:T(8,128)(2,1)S(1)}, u32[]{:S(2)}, u32[]{:S(2)}) collective-permute-start(bf16[384,1024]{1,0:T(8,128)(2,1)S(1)} %copy-done.21), channel_id=1, source_target_pairs={{0,1},{1,0},{2,3},{3,2},{4,5},{5,4},{6,7},{7,6},{8,9},{9,8},{10,11... | collective-permute-start | bytes 2359304 | tf_op jit(solution)/shard_map/ppermute | solution.py:385
  157.3 19.6 %collective-permute-start.17 = (bf16[384,1024]{1,0:T(8,128)(2,1)S(1)}, bf16[384,1024]{1,0:T(8,128)(2,1)S(1)}, u32[]{:S(2)}, u32[]{:S(2)}) collective-permute-start(bf16[384,1024]{1,0:T(8,128)(2,1)S(1)} %total.28.refs_2_), channel_id=1, source_target_pairs={{4,8},{8,4},{6,10},{10,6},{5,9},{9,5},{7,11},{11,7},{20,24},{24,20... | collective-permute-start | bytes 2359304 | tf_op jit(solution)/shard_map/ppermute | solution.py:379
  168.1 21.1 %collective-permute-start.18 = (bf16[384,1024]{1,0:T(8,128)(2,1)S(1)}, bf16[384,1024]{1,0:T(8,128)(2,1)S(1)}, u32[]{:S(2)}, u32[]{:S(2)}) collective-permute-start(bf16[384,1024]{1,0:T(8,128)(2,1)S(1)} %total.31.refs_6_), channel_id=1, source_target_pairs={{8,12},{4,0},{10,14},{6,2},{9,13},{5,1},{11,15},{7,3},{24,28},{20,... | collective-permute-start | bytes 2359304 | tf_op jit(solution)/shard_map/ppermute | solution.py:379
  169.4 23.1 %collective-permute-start.24 = (bf16[384,1024]{1,0:T(8,128)(2,1)}, bf16[384,1024]{1,0:T(8,128)(2,1)S(1)}, u32[]{:S(2)}, u32[]{:S(2)}) collective-permute-start(bf16[384,1024]{1,0:T(8,128)(2,1)} %hold.11), channel_id=1, source_target_pairs={{0,2},{2,0},{4,6},{6,4},{8,10},{10,8},{12,14},{14,12},{1,3},{3,1},... | collective-permute-start | bytes 2359304 | tf_op jit(solution)/shard_map/ppermute | solution.py:372
  173.3 1.4 copy-start.5
  192.6 1.4 copy-start.4

commit v5 on v4

--- a/solution.py
+++ b/solution.py
@@ -8,7 +8,7 @@
 
 SLOTS = 16
 LANES = 128
-CHUNK = 256
+CHUNK = 512
 PARTS = 2
 LOW_WITH = (0, PARTS - 1)
 VMEM = 50 * 2**20
@@ -48,10 +48,10 @@
     )
 
 
-def products(rows, weight, starts, size, outs, tail=None, after=()):
+def products(rows, weight, starts, size, outs, tail=None, chunk=1024, after=()):
     count, width = rows.shape
     blocks = starts.shape[0]
-    chunks = [(at, min(CHUNK, size - at)) for at in range(0, size, CHUNK)]
+    chunks = [(at, min(chunk, size - at)) for at in range(0, size, chunk)]
     low = min(first for _, first, _ in outs)
     high = max(first + some for _, first, some in outs)
     upper = (high - low) // 32 * 16
@@ -282,7 +282,7 @@
     )
 
 
-def expand(low, slot_sets, maps, index, parts, after=()):
+def expand(low, slot_sets, maps, index, after=()):
     sets = len(slot_sets)
     rank, width = maps.shape[1:]
     tall = low.shape[0]
@@ -290,16 +290,19 @@
     count = 2 * half
     span = index.shape[0] // sets * rank
     repeats = count // slot_sets[0].shape[0]
-    outs = [(s, first, some) for s in range(1, sets) for first, some in parts]
-    outs.append((0, 0, count))
+
+    outs = [(0, 0, count)] + [
+        (s, p * count // PARTS, count // PARTS) for s in range(1, sets) for p in range(PARTS)
+    ]
 
     def kernel(index_ref, low_ref, *refs):
         slot_refs, maps_ref, out_refs = refs[:sets], refs[sets], refs[sets + 1 : sets + 1 + len(outs)]
-        stages, (maps_buf, map_sems, out_sems) = (
-            refs[sets + 1 + len(outs) : sets + 1 + 2 * len(outs)], refs[sets + 1 + 2 * len(outs) :]
-        )
+        stage, maps_buf, map_sems, out_sems = refs[sets + 1 + len(outs) :]
         map_copies = block_copies(index_ref, maps_ref, maps_buf, map_sems, sets, rank)
-        writes = [pltpu.make_async_copy(stages[o], out_refs[o], out_sems.at[o]) for o in range(len(outs))]
+        writes = [
+            pltpu.make_async_copy(stage.at[s, pl.ds(first, some)], out_refs[o], out_sems.at[o])
+            for o, (s, first, some) in enumerate(outs)
+        ]
         order = list(range(1, sets)) + [0]
         for s in order:
             for copy in map_copies[s]:
@@ -314,33 +317,30 @@
             picked = jnp.where(pick, tiled, jnp.zeros_like(tiled))
             for copy in map_copies[s]:
                 copy.wait()
-            for o, (which, first, some) in enumerate(outs):
+            for at in range(0, width, CHUNK):
+                value = jnp.dot(
+                    picked, maps_buf[s * span : (s + 1) * span, at : at + CHUNK], preferred_element_type=jnp.float32
+                )
+                stage[s, :, at : at + CHUNK] = value.astype(stage.dtype)
+            for o, (which, _, _) in enumerate(outs):
                 if which == s:
-                    for at in range(0, width, CHUNK):
-                        value = jnp.dot(
-                            picked[first : first + some], maps_buf[s * span : (s + 1) * span, at : at + CHUNK],
-                            preferred_element_type=jnp.float32,
-                        )
-                        stages[o][:, at : at + CHUNK] = value.astype(stages[o].dtype)
                     writes[o].start()
         for write in writes:
             write.wait()
 
-    kinds = [jax.ShapeDtypeStruct((some, width), jnp.bfloat16 if s else jnp.float32) for s, _, some in outs]
-    done = call(
+    return call(
         kernel, [index, low, *slot_sets, maps], after, prefetch=1,
         in_specs=[pl.BlockSpec(memory_space=pltpu.VMEM)] * (1 + sets) + [ANY],
         out_specs=[ANY] * len(outs),
-        out_shape=kinds,
-        scratch=[pltpu.VMEM(kind.shape, kind.dtype) for kind in kinds]
-        + [
+        out_shape=[jax.ShapeDtypeStruct((some, width), jnp.bfloat16) for _, _, some in outs],
+        scratch=[
+            pltpu.VMEM((sets, count, width), jnp.bfloat16),
             pltpu.VMEM((sets * span, width), maps.dtype),
             pltpu.SemaphoreType.DMA((index.shape[0],)),
             pltpu.SemaphoreType.DMA((len(outs),)),
         ],
         name="expand",
     )
-    return [done[-1]] + [done[s * len(parts) : (s + 1) * len(parts)] for s in range(sets - 1)]
 
 
 def line_plan(nz):
@@ -417,7 +417,7 @@
     away_part, own_all, from_y, sums, arrived = {}, {}, {}, {}, {}
 
     def split(k):
-        return uneven if k == 0 else even
+        return uneven if k == 0 else [(0, count)]
 
     def add_up(span, terms, extra=(), dtype=jnp.bfloat16, into=None):
         low_row, high_row = span[0], span[0] + span[1]
@@ -437,35 +437,30 @@
     def whole(array):
         return [(0, count, array, 0)]
 
-    def parts_of(arrays, cut):
-        return [(at, some, array, 0) for (at, some), array in zip(cut, arrays)]
-
-    def multiply(aways, owns, tail=None):
+    def multiply(aways, owns, tail=None, chunk=1024):
         ks = sorted({k for k, _ in aways})
         starts = jnp.stack([away[k] for k in ks] + [own[k] for k in owns])
         outs = [(ks.index(k), *split(k)[p]) for k, p in aways]
         outs += [(len(ks) + i, 0, count) for i in range(len(owns))]
-        done = then(products, rows, projection_weight, starts, out_width, outs, tail)
+        done = then(products, rows, projection_weight, starts, out_width, outs, tail, chunk)
         away_part.update(zip(aways, done))
         own_all.update(zip(owns, done[len(aways) :]))
 
-    def start_y(i):
-        k, p = divmod(i, PARTS)
-        if k < nz:
-            value = away_part[k, p]
-            from_y[k, p] = swap_y(hold(value, last[0]) if i >= PARTS else value)
+    def start_y(k, p, after=None):
+        value = away_part[k, p]
+        from_y[k, p] = swap_y(value if after is None else hold(value, after))
 
     def y_parts(k):
-        return [(*split(k)[p], from_y[k, p], 0) for p in range(PARTS) if (k, p) in from_y]
+        return [(*cut, from_y[k, p], 0) for p, cut in enumerate(split(k)) if (k, p) in from_y]
 
     def sum_parts(k):
-        return [(*split(k)[p], sums[k, p], 0) for p in range(PARTS) if (k, p) in sums]
+        return [(*cut, sums[k, p], 0) for p, cut in enumerate(cut_of(0, k)) if (k, p) in sums]
 
     def cut_of(h, m):
-        return uneven if m == 0 and h <= 1 else even
+        return uneven if m == 0 and h <= 1 else [(0, count)]
 
     def arrived_parts(h, m):
-        return [(*cut_of(h, m)[p], arrived[h, m, p], 0) for p in range(PARTS) if (h, m, p) in arrived]
+        return [(*cut, arrived[h, m, p], 0) for p, cut in enumerate(cut_of(h, m)) if (h, m, p) in arrived]
 
     def line(h, m, p):
         k = slot_of(h, m)
@@ -481,34 +476,43 @@
 
     def line_order():
         ready, free = {}, {}
-        steps = [(h, m, p) for h in range(nz - 1) for m in range(nz - 1 - h) for p in range(PARTS)]
-        for h, m, p in sorted(steps, key=lambda step: (step[0], step[1] * PARTS + step[2])):
-            there = slot_of(h, m) * PARTS + p + 1.0
+        steps = [(h, m, p) for h in range(nz - 1) for m in range(nz - 1 - h) for p in range(len(cut_of(h, m)))]
+        for h, m, p in sorted(steps, key=lambda step: (step[0], step[1], step[2])):
+            k = slot_of(h, m)
+            there = (k + 1.0) * count if k or p else 1.0 * cut_of(0, 0)[0][1]
             if h:
-                there = max(there, ready[h - 1, m, p, "end"])
+                above = range(len(cut_of(h - 1, m)))
+                there = max(there, max(ready[h - 1, m, q, "end"] for q in above if q == p or len(above) != len(cut_of(h, m))))
             ready[h, m, p] = there
-            free[h] = max(there, free.get(h, 0.0)) + 1.0
+            free[h] = max(there, free.get(h, 0.0)) + cut_of(h, m)[p][1]
             ready[h, m, p, "end"] = free[h]
         return sorted(steps, key=lambda step: (ready[step], step[0]))
 
     row_ids = [tenant] + [pass_on(tenant, shift) for shift in range(1, owners)]
     row_sets = [rows] + [pass_on(rows, shift) for shift in range(1, owners)]
-    multiply([(0, p) for p in range(PARTS - 1)], [])
-    for i in range(PARTS - 1):
-        start_y(i)
+    multiply([(0, 0)], [], chunk=512)
+    start_y(0, 0)
     named = [slots(some_ids, me) for some_ids in row_ids]
     names = jnp.concatenate([which for which, _ in named])
     slot_sets = [row_slot for _, row_slot in named]
     low = then(low_rank, row_sets, slot_sets, adapter_down_maps, names, out_width)
-    multiply([LOW_WITH], [], low)
-    start_y(PARTS - 1)
-    multiply([(1, p) for p in range(PARTS)], [0])
-    low_sum = None
-
-    deltas = None
-    started = PARTS
+    multiply([LOW_WITH], [], low, chunk=512)
+    start_y(*LOW_WITH)
+    multiply([(1, 0)], [0])
+    start_y(1, 0)
     for h, m, p in line_order():
-        if h == 0 and (slot_of(0, m), p) == (2, 0) and nz > 2:
+        k = slot_of(h, m)
+        line(h, m, p)
+        if h == 0:
+            if k == 0 and p == 0:
+                multiply([(2, 0)] if nz > 2 else [], [1])
+            elif k == 0:
+                if nz > 2:
+                    start_y(2, 0, last[0])
+                multiply([(j, 0) for j in range(3, nz)], range(2, nz))
+            elif p == len(cut_of(h, m)) - 1 and k + 2 < nz:
+                start_y(k + 2, 0, last[0])
+        if (h, k) == (0, 1):
             low_at = uneven[LOW_WITH[1]][1]
             pieces = [(sums[LOW_WITH], low_at)]
             for step in range(nz - 1):
@@ -518,24 +522,14 @@
                 else:
                     pieces.append((arrived[step, 0, LOW_WITH[1]], low_at))
             low_sum = then(total, [(low_rows, pieces)])
-        line(h, m, p)
-        if h == 0:
-            start_y(started)
-            started += 1
-            if started == PARTS + 1:
-                multiply([(k, q) for k in range(2, nz) for q in range(PARTS)], range(1, nz))
-        if low_sum is not None and deltas is None:
-            deltas = then(expand, low_sum, slot_sets, adapter_up_maps, names, even)
-            back = {}
-            for shift in range(1, owners):
-                for q in range(PARTS):
-                    back[shift, q] = pass_on(deltas[shift][q], -shift)
-    head = [whole(own_all[nz - 1]), whole(deltas[0])]
-    head += [parts_of([back[shift, q] for q in range(PARTS)], even) for shift in range(1, owners)]
-    out = None
-    for span in even:
-        most = add_up(span, head + [arrived_parts(h, nz - 2 - h) for h in range(nz - 1)], dtype=jnp.float32)
-        out = add_up(span, [[(*span, most, 0)], y_parts(nz - 1)], into=(count, span[0], out))
+            deltas = then(expand, low_sum, slot_sets, adapter_up_maps, names)
+            back = [
+                [(*cut, pass_on(deltas[1 + (shift - 1) * PARTS + p], -shift), 0) for p, cut in enumerate(even)]
+                for shift in range(1, owners)
+            ]
+    span = (0, count)
+    most = add_up(span, [whole(own_all[nz - 1]), whole(deltas[0]), y_parts(nz - 1)] + back, dtype=jnp.float32)
+    out = add_up(span, [whole(most)] + [arrived_parts(h, nz - 2 - h) for h in range(nz - 1)])
     return out.reshape(steps, row_count, out_width)
 
 

time: 197 us -> 175 us (0.89)
  Pallas kernels: 90.8 us -> 69 us
  waiting for transfers between devices: 45.3 us -> 58.5 us
  starting transfers between devices: 43.2 us -> 30.6 us
    pallas_call x30 -> x21, Pallas kernels: 90.8 us -> 69 us  [call(): pl.pallas_call(body, grid_spec=pltpu.PrefetchScalarGridSpec(num_scalar_pr...]
    ppermute x8 -> x5, waiting for transfers between devices: 0.02 us -> 21.5 us  [swap_y(): return lax.ppermute(value, 'tensor', [(t, t ^ 1) for t in range(n)])]
    ppermute x13 -> x9, starting transfers between devices: 34.5 us -> 21.8 us  [hop(): return lax.ppermute(value, 'tensor', pairs)]
    ppermute x13 -> x9, waiting for transfers between devices: 45.3 us -> 34.6 us  [hop(): return lax.ppermute(value, 'tensor', pairs)]
    ppermute x4, waiting for transfers between devices: 0.01 us -> 2.28 us  [pass_on(): lax.ppermute(value, 'dp', [(i, (i + shift) % owners) for i in range(owner...]
    unnamed x46 -> x44, local copies, waits for them, and re-layouts: 10.1 us -> 9.1 us
    ppermute x8 -> x5, starting transfers between devices: 8.12 us -> 8.24 us  [swap_y(): return lax.ppermute(value, 'tensor', [(t, t ^ 1) for t in range(n)])]
  transfers between devices with their start and end apart: 25 -> 18, of which waited for: 5 -> 9; matrix products, arithmetic and copies ran while one was open for 1% -> 2% of each run, Pallas kernels for 46% -> 38%
where the time goes in v5:
time: 175 us; the launch traced here: 173 us
  Pallas kernels  69 us (39%)
  waiting for transfers between devices  58.5 us (33%)
  starting transfers between devices  30.6 us (17%)
  local copies, waits for them, and re-layouts  10.7 us (6%)
  between operations  3.25 us (2%)
    pallas_call x21, Pallas kernels, call(): pl.pallas_call(body, grid_spec=pltpu.PrefetchScalarGridSpec(num_scalar_pr...  69 us
    ppermute x9, waiting for transfers between devices, hop(): return lax.ppermute(value, 'tensor', pairs)  34.6 us
    ppermute x9, starting transfers between devices, hop(): return lax.ppermute(value, 'tensor', pairs)  21.8 us
    ppermute x5, waiting for transfers between devices, swap_y(): return lax.ppermute(value, 'tensor', [(t, t ^ 1) for t in range(n)])  21.5 us
    unnamed x44, local copies, waits for them, and re-layouts  9.1 us
    ppermute x5, starting transfers between devices, swap_y(): return lax.ppermute(value, 'tensor', [(t, t ^ 1) for t in range(n)])  8.24 us
  transfers between devices with their start and end apart: 18, of which 9 were waited for; matrix products, arithmetic and copies ran while one was open for 2% of the time, Pallas kernels for 38%

profile of v5, /device:TPU:0, one launch (start us, length us, event | category | flops | bytes accessed | tf_op | source)
XLA Modules:
  0.0 173.1 jit_solution(8826775354061491792)
XLA Ops:
  2.5 1.4 copy-done
  3.9 4.0 %products.5.refs_6_ = bf16[480,1024]{1,0:T(8,128)(2,1)} custom-call(s32[1]{0:T(128)} %bitcast.10.refs_0_, bf16[768,1024]{1,0:T(8,128)(2,1)S(1)} %bitcast.20, bf16[1024,8192]{1,0:T(8,128)(2,1)} %refs_2_.9), custom_call_target="tpu_custom_call" | custom-call | flops 1 | bytes 1 | tf_op jit(solution)/shard_map/products/pallas_call | solution.py:24
  7.9 3.0 %collective-permute-start.3 = (bf16[480,1024]{1,0:T(8,128)(2,1)}, bf16[480,1024]{1,0:T(8,128)(2,1)}, u32[]{:S(2)}, u32[]{:S(2)}) collective-permute-start(bf16[480,1024]{1,0:T(8,128)(2,1)} %products.5.refs_6_), channel_id=1, source_target_pairs={{0,2},{2,0},{4,6},{6,4},{8,10},{10,8},{12,14},{14,12},{1,3},{3,1},... | collective-permute-start | bytes 2949128 | tf_op jit(solution)/shard_map/ppermute | solution.py:372
  12.8 1.1 copy-done.20
  14.0 6.7 %low_rank.1.refs_3_.refs_4_.refs_2_ = bf16[96,1024]{1,0:T(8,128)(2,1)S(1)} custom-call(s32[32]{0:T(128)S(1)} %pad_add_fusion.2.refs_0_, bf16[768,1024]{1,0:T(8,128)(2,1)S(1)} %bitcast.21, bf16[768,1024]{1,0:T(8,128)(2,1)} %copy-done.20, s32[192,1]{1,0:T(8,128)S(1)} %copy.13.refs_3_.refs_2_, s32[192,1]{1,0:T(8,128)S(1)} %copy.14.refs_4_.refs_3_, ...), custom_call_target="tpu_custom_call" | custom-call | flops 1 | bytes 1 | tf_op jit(solution)/shard_map/low_rank/pallas_call | solution.py:24
  20.6 3.0 %products.6.refs_3_ = bf16[384,1024]{1,0:T(8,128)(2,1)} custom-call(s32[1]{0:T(128)} %bitcast.10.refs_0_, bf16[768,1024]{1,0:T(8,128)(2,1)S(1)} %bitcast.22, bf16[1024,8192]{1,0:T(8,128)(2,1)} %refs_2_.9, bf16[96,1024]{1,0:T(8,128)(2,1)S(1)} %low_rank.1.refs_3_.refs_4_.refs_2_, bf16[96,1024]{1,0:T(8,128)(2,1)S(1)} %low_rank.1.refs_3_.refs_4_.refs_2_), custom_call_target="tpu_custom_call" | custom-call | flops 1 | bytes 1 | tf_op jit(solution)/shard_map/products/pallas_call | solution.py:24
  23.9 6.3 %products.7 = (bf16[768,1024]{1,0:T(8,128)(2,1)}, bf16[768,1024]{1,0:T(8,128)(2,1)S(1)}) custom-call(s32[2]{0:T(128)S(1)} %pad_add_fusion.1.refs_0_, bf16[768,1024]{1,0:T(8,128)(2,1)} %bitcast.17, bf16[1024,8192]{1,0:T(8,128)(2,1)} %refs_2_.9, bf16[384,1024]{1,0:T(8,128)(2,1)} %products.6.refs_3_), custom_call_target="tpu_custom_call" | custom-call | flops 1 | bytes 1 | tf_op jit(solution)/shard_map/products/pallas_call | solution.py:24
  30.2 2.1 %collective-permute-start.7 = (bf16[768,1024]{1,0:T(8,128)(2,1)}, bf16[768,1024]{1,0:T(8,128)(2,1)}, u32[]{:S(2)}, u32[]{:S(2)}) collective-permute-start(bf16[768,1024]{1,0:T(8,128)(2,1)} %get-tuple-element.16.refs_2_), channel_id=1, source_target_pairs={{0,2},{2,0},{4,6},{6,4},{8,10},{10,8},{12,14},{14,12},{1,3},{3,1},... | collective-permute-start | bytes 4718600 | tf_op jit(solution)/shard_map/ppermute | solution.py:372
  32.3 1.6 collective-permute-done.3.refs_1_
  33.8 2.2 %total.12.refs_3_.refs_0_ = bf16[480,1024]{1,0:T(8,128)(2,1)S(1)} custom-call(bf16[768,1024]{1,0:T(8,128)(2,1)S(1)} %get-tuple-element.15.refs_0_, bf16[480,1024]{1,0:T(8,128)(2,1)} %collective-permute-done.3.refs_1_, bf16[768,1024]{1,0:T(8,128)(2,1)} %get-tuple-element.16.refs_2_), custom_call_target="tpu_custom_call" | custom-call | flops 1 | bytes 1 | tf_op jit(solution)/shard_map/total/pallas_call | solution.py:24
  36.1 5.0 %collective-permute-start.5 = (bf16[480,1024]{1,0:T(8,128)(2,1)S(1)}, bf16[480,1024]{1,0:T(8,128)(2,1)}, u32[]{:S(2)}, u32[]{:S(2)}) collective-permute-start(bf16[480,1024]{1,0:T(8,128)(2,1)S(1)} %total.12.refs_3_.refs_0_), channel_id=1, source_target_pairs={{0,4},{12,8},{2,6},{14,10},{1,5},{13,9},{3,7},{15,11},{16,20},{28,... | collective-permute-start | bytes 2949128 | tf_op jit(solution)/shard_map/ppermute | solution.py:379
  41.8 7.4 %products.8 = (bf16[768,1024]{1,0:T(8,128)(2,1)}, bf16[768,1024]{1,0:T(8,128)(2,1)}) custom-call(s32[2]{0:T(128)S(1)} %pad_add_fusion.3.refs_0_, bf16[768,1024]{1,0:T(8,128)(2,1)} %bitcast.18, bf16[1024,8192]{1,0:T(8,128)(2,1)} %refs_2_.9, bf16[480,1024]{1,0:T(8,128)(2,1)S(1)} %total.12.refs_3_.refs_0_), custom_call_target="tpu_custom_call" | custom-call | flops 1 | bytes 1 | tf_op jit(solution)/shard_map/products/pallas_call | solution.py:24
  49.2 1.4 collective-permute-done.2.refs_1_.refs_3_
  50.6 0.9 copy-done.10
  51.4 1.1 copy-done.11
  52.6 1.4 total.13.refs_3_.refs_0_.refs_2_.refs_1_
  54.0 4.2 %collective-permute-start.4 = (bf16[384,1024]{1,0:T(8,128)(2,1)S(1)}, bf16[384,1024]{1,0:T(8,128)(2,1)S(1)}, u32[]{:S(2)}, u32[]{:S(2)}) collective-permute-start(bf16[384,1024]{1,0:T(8,128)(2,1)S(1)} %total.13.refs_3_.refs_0_.refs_2_.refs_1_), channel_id=1, source_target_pairs={{0,4},{12,8},{2,6},{14,10},{1,5},{13,9},{3,7},{15,11},{16,20},{28,... | collective-permute-start | bytes 2359304 | tf_op jit(solution)/shard_map/ppermute | solution.py:379
  58.9 1.5 collective-permute-start.12
  60.5 10.0 %products.9 = (bf16[768,1024]{1,0:T(8,128)(2,1)S(1)}, bf16[768,1024]{1,0:T(8,128)(2,1)S(1)}, bf16[768,1024]{1,0:T(8,128)(2,1)}) custom-call(s32[3]{0:T(128)S(1)} %pad_add_fusion.refs_0_, bf16[768,1024]{1,0:T(8,128)(2,1)} %bitcast.19, bf16[1024,8192]{1,0:T(8,128)(2,1)} %refs_2_.9, bf16[384,1024]{1,0:T(8,128)(2,1)S(1)} %total.13.refs_3_.refs_0_.refs_2_.refs_1_), custom_call_target="tpu_custom_call" | custom-call | flops 1 | bytes 1 | tf_op jit(solution)/shard_map/products/pallas_call | solution.py:24
  70.5 1.2 copy-done.4
  71.8 2.2 %total.14.refs_4_ = bf16[480,1024]{1,0:T(8,128)(2,1)S(1)} custom-call(bf16[480,1024]{1,0:T(8,128)(2,1)S(1)} %total.12.refs_3_.refs_0_, bf16[480,1024]{1,0:T(8,128)(2,1)} %collective-permute-done.5.refs_1_, bf16[768,1024]{1,0:T(8,128)(2,1)} %copy-done.4), custom_call_target="tpu_custom_call" | custom-call | flops 1 | bytes 1 | tf_op jit(solution)/shard_map/total/pallas_call | solution.py:24
  74.0 2.3 %collective-permute-done.4.refs_1_.refs_3_ = bf16[384,1024]{1,0:T(8,128)(2,1)S(1)} collective-permute-done((bf16[384,1024]{1,0:T(8,128)(2,1)S(1)}, bf16[384,1024]{1,0:T(8,128)(2,1)S(1)}, u32[]{:S(2)}, u32[]{:S(2)}) %collective-permute-start.4) | collective-permute-done | bytes 786464 | tf_op jit(solution)/shard_map/ppermute | solution.py:379
  76.3 1.4 total.15.refs_2_
  77.7 6.7 %collective-permute-done.7.refs_1_ = bf16[768,1024]{1,0:T(8,128)(2,1)} collective-permute-done((bf16[768,1024]{1,0:T(8,128)(2,1)}, bf16[768,1024]{1,0:T(8,128)(2,1)}, u32[]{:S(2)}, u32[]{:S(2)}) %collective-permute-start.7) | collective-permute-done | bytes 1572896 | tf_op jit(solution)/shard_map/ppermute | solution.py:372
  84.4 1.8 %total.16.refs_2_.refs_1_.refs_0_ = bf16[768,1024]{1,0:T(8,128)(2,1)S(1)} custom-call(bf16[768,1024]{1,0:T(8,128)(2,1)S(1)} %copy-done.12, bf16[768,1024]{1,0:T(8,128)(2,1)} %collective-permute-done.7.refs_1_, bf16[384,1024]{1,0:T(8,128)(2,1)S(1)} %total.15.refs_2_), custom_call_target="tpu_custom_call" | custom-call | flops 1 | bytes 1 | tf_op jit(solution)/shard_map/total/pallas_call | solution.py:24
  86.2 5.2 %collective-permute-start.14 = (bf16[768,1024]{1,0:T(8,128)(2,1)S(1)}, bf16[768,1024]{1,0:T(8,128)(2,1)}, u32[]{:S(2)}, u32[]{:S(2)}) collective-permute-start(bf16[768,1024]{1,0:T(8,128)(2,1)S(1)} %total.16.refs_2_.refs_1_.refs_0_), channel_id=1, source_target_pairs={{0,4},{12,8},{2,6},{14,10},{1,5},{13,9},{3,7},{15,11},{16,20},{28,... | collective-permute-start | bytes 4718600 | tf_op jit(solution)/shard_map/ppermute | solution.py:379
  92.1 1.6 collective-permute-start.13
  93.8 1.5 collective-permute-start.9
  95.3 0.8 total.17.refs_4_
  96.1 1.4 collective-permute-start.8
  97.6 20.3 %collective-permute-done.8.refs_3_ = bf16[96,1024]{1,0:T(8,128)(2,1)S(1)} collective-permute-done((bf16[96,1024]{1,0:T(8,128)(2,1)S(1)}, bf16[96,1024]{1,0:T(8,128)(2,1)S(1)}, u32[]{:S(2)}, u32[]{:S(2)}) %collective-permute-start.8) | collective-permute-done | bytes 196640 | tf_op jit(solution)/shard_map/ppermute | solution.py:379
  117.9 1.4 total.18.refs_1_.refs_5_
  119.3 6.6 %expand.1 = (bf16[768,1024]{1,0:T(8,128)(2,1)S(1)}, bf16[384,1024]{1,0:T(8,128)(2,1)S(1)}, bf16[384,1024]{1,0:T(8,128)(2,1)S(1)}) custom-call(s32[32]{0:T(128)S(1)} %pad_add_fusion.2.refs_0_, bf16[96,1024]{1,0:T(8,128)(2,1)S(1)} %total.18.refs_1_.refs_5_, s32[192,1]{1,0:T(8,128)S(1)} %copy-done.14, s32[192,1]{1,0:T(8,128)S(1)} %copy-done.16, ...), custom_call_target="tpu_custom_call" | custom-call | flops 1 | bytes 1 | tf_op jit(solution)/shard_map/expand/pallas_call | solution.py:24
  125.9 1.1 copy-done.3
  127.0 0.9 copy-done.19
  128.0 2.0 %total.19.refs_2_.refs_0_ = bf16[768,1024]{1,0:T(8,128)(2,1)S(1)} custom-call(bf16[768,1024]{1,0:T(8,128)(2,1)S(1)} %get-tuple-element.24.refs_0_, bf16[768,1024]{1,0:T(8,128)(2,1)} %collective-permute-done.12.refs_1_, bf16[768,1024]{1,0:T(8,128)(2,1)} %copy-done.3), custom_call_target="tpu_custom_call" | custom-call | flops 1 | bytes 1 | tf_op jit(solution)/shard_map/total/pallas_call | solution.py:24
  130.0 1.6 collective-permute-start.15
  131.5 1.7 total.20.refs_4_
  133.3 1.2 copy-done.6
  134.5 2.6 %total.21.refs_8_ = bf16[768,1024]{1,0:T(8,128)(2,1)S(1)} custom-call(bf16[768,1024]{1,0:T(8,128)(2,1)} %copy-done.2, bf16[480,1024]{1,0:T(8,128)(2,1)} %collective-permute-done.13.refs_1_, bf16[768,1024]{1,0:T(8,128)(2,1)} %copy-done.2, bf16[384,1024]{1,0:T(8,128)(2,1)S(1)} %collective-permute-done.6.refs_1_.refs_2_.refs_3_, bf16[768,1024]{1,0:T(8,128)(2,1)} %copy-done.6), custom_call_target="tpu_custom_call" | custom-call | flops 1 | bytes 1 | tf_op jit(solution)/shard_map/total/pallas_call | solution.py:24
  137.0 1.3 collective-permute-start.17
  138.4 0.8 collective-permute-start.16
  139.2 11.9 %collective-permute-done.9.refs_2_.refs_6_ = bf16[768,1024]{1,0:T(8,128)(2,1)} collective-permute-done((bf16[768,1024]{1,0:T(8,128)(2,1)S(1)}, bf16[768,1024]{1,0:T(8,128)(2,1)}, u32[]{:S(2)}, u32[]{:S(2)}) %collective-permute-start.9) | collective-permute-done | bytes 1572896 | tf_op jit(solution)/shard_map/ppermute | solution.py:372
  151.2 2.3 %collective-permute-done.11.refs_7_ = bf16[384,1024]{1,0:T(8,128)(2,1)S(1)} collective-permute-done((bf16[384,1024]{1,0:T(8,128)(2,1)S(1)}, bf16[384,1024]{1,0:T(8,128)(2,1)S(1)}, u32[]{:S(2)}, u32[]{:S(2)}) %collective-permute-start.11) | collective-permute-done | bytes 786464 | tf_op jit(solution)/shard_map/ppermute | solution.py:385
  153.4 3.8 %total.22.refs_0_.refs_4_ = f32[768,1024]{1,0:T(8,128)} custom-call(bf16[768,1024]{1,0:T(8,128)(2,1)S(1)} %copy-done.9, bf16[768,1024]{1,0:T(8,128)(2,1)} %copy-done.3, bf16[768,1024]{1,0:T(8,128)(2,1)} %collective-permute-done.9.refs_2_.refs_6_, bf16[384,1024]{1,0:T(8,128)(2,1)S(1)} %collective-permute-done.10.refs_3_, bf16[768,1024]{1,0:T(8,128)(2,1)S(1)} %copy-done.9, ...), custom_call_target="tpu_custom_call" | custom-call | flops 1 | bytes 1 | tf_op jit(solution)/shard_map/total/pallas_call | solution.py:24
  157.2 2.2 %collective-permute-done.15.refs_1_ = bf16[768,1024]{1,0:T(8,128)(2,1)S(1)} collective-permute-done((bf16[768,1024]{1,0:T(8,128)(2,1)S(1)}, bf16[768,1024]{1,0:T(8,128)(2,1)S(1)}, u32[]{:S(2)}, u32[]{:S(2)}) %collective-permute-start.15) | collective-permute-done | bytes 1572896 | tf_op jit(solution)/shard_map/ppermute | solution.py:379
  159.4 9.8 %collective-permute-done.17.refs_3_ = bf16[768,1024]{1,0:T(8,128)(2,1)} collective-permute-done((bf16[768,1024]{1,0:T(8,128)(2,1)S(1)}, bf16[768,1024]{1,0:T(8,128)(2,1)}, u32[]{:S(2)}, u32[]{:S(2)}) %collective-permute-start.17) | collective-permute-done | bytes 1572896 | tf_op jit(solution)/shard_map/ppermute | solution.py:379
  169.3 3.7 %total.23 = bf16[768,1024]{1,0:T(8,128)(2,1)} custom-call(f32[768,1024]{1,0:T(8,128)} %total.22.refs_0_.refs_4_, bf16[768,1024]{1,0:T(8,128)(2,1)S(1)} %collective-permute-done.15.refs_1_, bf16[768,1024]{1,0:T(8,128)(2,1)S(1)} %collective-permute-done.16.refs_2_, bf16[768,1024]{1,0:T(8,128)(2,1)} %collective-permute-done.17.refs_3_, ...), custom_call_target="tpu_custom_call" | custom-call | flops 1 | bytes 1 | tf_op jit(solution)/shard_map/total/pallas_call | solution.py:24
  (74 shorter events, 4.2 us)
Async XLA Ops:
  0.0 12.1 %collective-permute-start = (s32[192]{0:T(256)}, s32[192]{0:T(256)S(1)}, u32[]{:S(2)}, u32[]{:S(2)}) collective-permute-start(s32[192]{0:T(256)} %param.7), channel_id=1, source_target_pairs={{0,1},{1,0},{2,3},{3,2},{4,5},{5,4},{6,7},{7,6},{8,9},{9,8},{10,11... | collective-permute-start | bytes 2312 | tf_op jit(solution)/shard_map/ppermute | solution.py:385
  0.5 12.4 %collective-permute-start.1 = (bf16[768,1024]{1,0:T(8,128)(2,1)}, bf16[768,1024]{1,0:T(8,128)(2,1)S(1)}, u32[]{:S(2)}, u32[]{:S(2)}) collective-permute-start(bf16[768,1024]{1,0:T(8,128)(2,1)} %bitcast.16), channel_id=1, source_target_pairs={{0,1},{1,0},{2,3},{3,2},{4,5},{5,4},{6,7},{7,6},{8,9},{9,8},{10,11... | collective-permute-start | bytes 4718600 | tf_op jit(solution)/shard_map/ppermute | solution.py:385
  2.5 1.4 copy-start
  3.9 7.0 %copy-start.21 = (s32[192]{0:T(256)S(1)}, s32[192]{0:T(256)}, u32[]{:S(2)}) copy-start(s32[192]{0:T(256)} %param.7) | copy-start | bytes 2308
  3.9 10.0 %copy-start.1 = (bf16[4,192,1024]{2,1,0:T(8,128)(2,1)S(1)}, bf16[4,192,1024]{2,1,0:T(8,128)(2,1)}, u32[]{:S(2)}) copy-start(bf16[4,192,1024]{2,1,0:T(8,128)(2,1)} %param.6) | copy-start | bytes 4718596
  7.9 25.9 %collective-permute-start.3 = (bf16[480,1024]{1,0:T(8,128)(2,1)}, bf16[480,1024]{1,0:T(8,128)(2,1)}, u32[]{:S(2)}, u32[]{:S(2)}) collective-permute-start(bf16[480,1024]{1,0:T(8,128)(2,1)} %products.5.refs_6_), channel_id=1, source_target_pairs={{0,2},{2,0},{4,6},{6,4},{8,10},{10,8},{12,14},{14,12},{1,3},{3,1},... | collective-permute-start | bytes 2949128 | tf_op jit(solution)/shard_map/ppermute | solution.py:372
  11.4 9.2 %copy-start.13 = (s32[192,1]{1,0:T(8,128)}, s32[192,1]{1,0:T(8,128)S(1)}, u32[]{:S(2)}) copy-start(s32[192,1]{1,0:T(8,128)S(1)} %copy.13.refs_3_.refs_2_) | copy-start | bytes 2308
  12.6 8.0 %copy-start.15 = (s32[192,1]{1,0:T(8,128)}, s32[192,1]{1,0:T(8,128)S(1)}, u32[]{:S(2)}) copy-start(s32[192,1]{1,0:T(8,128)S(1)} %copy.14.refs_4_.refs_3_) | copy-start | bytes 2308
  12.8 1.1 copy-start.20
  23.7 26.9 %collective-permute-start.2 = (bf16[384,1024]{1,0:T(8,128)(2,1)}, bf16[384,1024]{1,0:T(8,128)(2,1)S(1)}, u32[]{:S(2)}, u32[]{:S(2)}) collective-permute-start(bf16[384,1024]{1,0:T(8,128)(2,1)} %products.6.refs_3_), channel_id=1, source_target_pairs={{0,2},{2,0},{4,6},{6,4},{8,10},{10,8},{12,14},{14,12},{1,3},{3,1},... | collective-permute-start | bytes 2359304 | tf_op jit(solution)/shard_map/ppermute | solution.py:372
  30.2 54.2 %collective-permute-start.7 = (bf16[768,1024]{1,0:T(8,128)(2,1)}, bf16[768,1024]{1,0:T(8,128)(2,1)}, u32[]{:S(2)}, u32[]{:S(2)}) collective-permute-start(bf16[768,1024]{1,0:T(8,128)(2,1)} %get-tuple-element.16.refs_2_), channel_id=1, source_target_pairs={{0,2},{2,0},{4,6},{6,4},{8,10},{10,8},{12,14},{14,12},{1,3},{3,1},... | collective-permute-start | bytes 4718600 | tf_op jit(solution)/shard_map/ppermute | solution.py:372
  36.1 35.7 %collective-permute-start.5 = (bf16[480,1024]{1,0:T(8,128)(2,1)S(1)}, bf16[480,1024]{1,0:T(8,128)(2,1)}, u32[]{:S(2)}, u32[]{:S(2)}) collective-permute-start(bf16[480,1024]{1,0:T(8,128)(2,1)S(1)} %total.12.refs_3_.refs_0_), channel_id=1, source_target_pairs={{0,4},{12,8},{2,6},{14,10},{1,5},{13,9},{3,7},{15,11},{16,20},{28,... | collective-permute-start | bytes 2949128 | tf_op jit(solution)/shard_map/ppermute | solution.py:379
  50.6 0.9 copy-start.10
  51.4 1.1 copy-start.11
  54.0 22.3 %collective-permute-start.4 = (bf16[384,1024]{1,0:T(8,128)(2,1)S(1)}, bf16[384,1024]{1,0:T(8,128)(2,1)S(1)}, u32[]{:S(2)}, u32[]{:S(2)}) collective-permute-start(bf16[384,1024]{1,0:T(8,128)(2,1)S(1)} %total.13.refs_3_.refs_0_.refs_2_.refs_1_), channel_id=1, source_target_pairs={{0,4},{12,8},{2,6},{14,10},{1,5},{13,9},{3,7},{15,11},{16,20},{28,... | collective-permute-start | bytes 2359304 | tf_op jit(solution)/shard_map/ppermute | solution.py:379
  58.9 69.0 %collective-permute-start.12 = (bf16[768,1024]{1,0:T(8,128)(2,1)}, bf16[768,1024]{1,0:T(8,128)(2,1)}, u32[]{:S(2)}, u32[]{:S(2)}) collective-permute-start(bf16[768,1024]{1,0:T(8,128)(2,1)} %hold.3), channel_id=1, source_target_pairs={{0,2},{2,0},{4,6},{6,4},{8,10},{10,8},{12,14},{14,12},{1,3},{3,1},... | collective-permute-start | bytes 4718600 | tf_op jit(solution)/shard_map/ppermute | solution.py:372
  70.5 1.2 copy-start.4
  74.0 10.4 %copy-start.12 = (bf16[768,1024]{1,0:T(8,128)(2,1)S(1)}, bf16[768,1024]{1,0:T(8,128)(2,1)}, u32[]{:S(2)}) copy-start(bf16[768,1024]{1,0:T(8,128)(2,1)} %get-tuple-element.20.refs_0_) | copy-start | bytes 4718596
  84.4 9.4 %copy-start.5 = (bf16[768,1024]{1,0:T(8,128)(2,1)S(1)}, bf16[768,1024]{1,0:T(8,128)(2,1)}, u32[]{:S(2)}) copy-start(bf16[768,1024]{1,0:T(8,128)(2,1)} %copy-done.4) | copy-start | bytes 4718596
  86.2 45.3 %collective-permute-start.14 = (bf16[768,1024]{1,0:T(8,128)(2,1)S(1)}, bf16[768,1024]{1,0:T(8,128)(2,1)}, u32[]{:S(2)}, u32[]{:S(2)}) collective-permute-start(bf16[768,1024]{1,0:T(8,128)(2,1)S(1)} %total.16.refs_2_.refs_1_.refs_0_), channel_id=1, source_target_pairs={{0,4},{12,8},{2,6},{14,10},{1,5},{13,9},{3,7},{15,11},{16,20},{28,... | collective-permute-start | bytes 4718600 | tf_op jit(solution)/shard_map/ppermute | solution.py:379
  91.4 3.9 %collective-permute-start.6 = (bf16[384,1024]{1,0:T(8,128)(2,1)S(1)}, bf16[384,1024]{1,0:T(8,128)(2,1)S(1)}, u32[]{:S(2)}, u32[]{:S(2)}) collective-permute-start(bf16[384,1024]{1,0:T(8,128)(2,1)S(1)} %total.15.refs_2_), channel_id=1, source_target_pairs={{4,8},{8,4},{6,10},{10,6},{5,9},{9,5},{7,11},{11,7},{20,24},{24,20... | collective-permute-start | bytes 2359304 | tf_op jit(solution)/shard_map/ppermute | solution.py:379
  92.1 42.3 %collective-permute-start.13 = (bf16[480,1024]{1,0:T(8,128)(2,1)S(1)}, bf16[480,1024]{1,0:T(8,128)(2,1)}, u32[]{:S(2)}, u32[]{:S(2)}) collective-permute-start(bf16[480,1024]{1,0:T(8,128)(2,1)S(1)} %total.14.refs_4_), channel_id=1, source_target_pairs={{4,8},{8,4},{6,10},{10,6},{5,9},{9,5},{7,11},{11,7},{20,24},{24,20... | collective-permute-start | bytes 2949128 | tf_op jit(solution)/shard_map/ppermute | solution.py:379
  93.8 57.4 %collective-permute-start.9 = (bf16[768,1024]{1,0:T(8,128)(2,1)S(1)}, bf16[768,1024]{1,0:T(8,128)(2,1)}, u32[]{:S(2)}, u32[]{:S(2)}) collective-permute-start(bf16[768,1024]{1,0:T(8,128)(2,1)S(1)} %hold.2), channel_id=1, source_target_pairs={{0,2},{2,0},{4,6},{6,4},{8,10},{10,8},{12,14},{14,12},{1,3},{3,1},... | collective-permute-start | bytes 4718600 | tf_op jit(solution)/shard_map/ppermute | solution.py:372
  96.1 23.2 %copy-start.14 = (s32[192,1]{1,0:T(8,128)S(1)}, s32[192,1]{1,0:T(8,128)}, u32[]{:S(2)}) copy-start(s32[192,1]{1,0:T(8,128)} %copy-done.13) | copy-start | bytes 2308
  96.1 23.2 %copy-start.16 = (s32[192,1]{1,0:T(8,128)S(1)}, s32[192,1]{1,0:T(8,128)}, u32[]{:S(2)}) copy-start(s32[192,1]{1,0:T(8,128)} %copy-done.15) | copy-start | bytes 2308
  96.1 21.8 %collective-permute-start.8 = (bf16[96,1024]{1,0:T(8,128)(2,1)S(1)}, bf16[96,1024]{1,0:T(8,128)(2,1)S(1)}, u32[]{:S(2)}, u32[]{:S(2)}) collective-permute-start(bf16[96,1024]{1,0:T(8,128)(2,1)S(1)} %total.17.refs_4_), channel_id=1, source_target_pairs={{8,12},{4,0},{10,14},{6,2},{9,13},{5,1},{11,15},{7,3},{24,28},{20,... | collective-permute-start | bytes 589832 | tf_op jit(solution)/shard_map/ppermute | solution.py:379
  125.9 1.1 copy-start.3
  127.0 0.9 copy-start.19
  128.0 2.0 %copy-start.17 = (bf16[384,1024]{1,0:T(8,128)(2,1)}, bf16[384,1024]{1,0:T(8,128)(2,1)S(1)}, u32[]{:S(2)}) copy-start(bf16[384,1024]{1,0:T(8,128)(2,1)S(1)} %get-tuple-element.23) | copy-start | bytes 2359300
  130.0 1.6 copy-start.2
  130.0 29.4 %collective-permute-start.15 = (bf16[768,1024]{1,0:T(8,128)(2,1)S(1)}, bf16[768,1024]{1,0:T(8,128)(2,1)S(1)}, u32[]{:S(2)}, u32[]{:S(2)}) collective-permute-start(bf16[768,1024]{1,0:T(8,128)(2,1)S(1)} %total.19.refs_2_.refs_0_), channel_id=1, source_target_pairs={{0,4},{12,8},{2,6},{14,10},{1,5},{13,9},{3,7},{15,11},{16,20},{28,... | collective-permute-start | bytes 4718600 | tf_op jit(solution)/shard_map/ppermute | solution.py:379
  133.3 1.2 copy-start.6
  134.4 16.7 %copy-start.18 = (bf16[384,1024]{1,0:T(8,128)(2,1)S(1)}, bf16[384,1024]{1,0:T(8,128)(2,1)}, u32[]{:S(2)}) copy-start(bf16[384,1024]{1,0:T(8,128)(2,1)} %copy-done.17) | copy-start | bytes 2359300
  134.5 19.0 %copy-start.9 = (bf16[768,1024]{1,0:T(8,128)(2,1)S(1)}, bf16[768,1024]{1,0:T(8,128)(2,1)}, u32[]{:S(2)}) copy-start(bf16[768,1024]{1,0:T(8,128)(2,1)} %get-tuple-element.18.refs_0_.refs_4_) | copy-start | bytes 4718596
  134.5 3.9 %copy-start.7 = (bf16[768,1024]{1,0:T(8,128)(2,1)S(1)}, bf16[768,1024]{1,0:T(8,128)(2,1)}, u32[]{:S(2)}) copy-start(bf16[768,1024]{1,0:T(8,128)(2,1)} %copy-done.6) | copy-start | bytes 4718596
  137.0 16.4 %copy-start.8 = (bf16[768,1024]{1,0:T(8,128)(2,1)}, bf16[768,1024]{1,0:T(8,128)(2,1)S(1)}, u32[]{:S(2)}) copy-start(bf16[768,1024]{1,0:T(8,128)(2,1)S(1)} %total.21.refs_8_) | copy-start | bytes 4718596
  137.0 32.2 %collective-permute-start.17 = (bf16[768,1024]{1,0:T(8,128)(2,1)S(1)}, bf16[768,1024]{1,0:T(8,128)(2,1)}, u32[]{:S(2)}, u32[]{:S(2)}) collective-permute-start(bf16[768,1024]{1,0:T(8,128)(2,1)S(1)} %total.21.refs_8_), channel_id=1, source_target_pairs={{8,12},{4,0},{10,14},{6,2},{9,13},{5,1},{11,15},{7,3},{24,28},{20,... | collective-permute-start | bytes 4718600 | tf_op jit(solution)/shard_map/ppermute | solution.py:379
  138.4 30.9 %collective-permute-start.16 = (bf16[768,1024]{1,0:T(8,128)(2,1)S(1)}, bf16[768,1024]{1,0:T(8,128)(2,1)S(1)}, u32[]{:S(2)}, u32[]{:S(2)}) collective-permute-start(bf16[768,1024]{1,0:T(8,128)(2,1)S(1)} %copy-done.7), channel_id=1, source_target_pairs={{4,8},{8,4},{6,10},{10,6},{5,9},{9,5},{7,11},{11,7},{20,24},{24,20... | collective-permute-start | bytes 4718600 | tf_op jit(solution)/shard_map/ppermute | solution.py:379
  139.1 12.0 %collective-permute-start.10 = (bf16[384,1024]{1,0:T(8,128)(2,1)}, bf16[384,1024]{1,0:T(8,128)(2,1)S(1)}, u32[]{:S(2)}, u32[]{:S(2)}) collective-permute-start(bf16[384,1024]{1,0:T(8,128)(2,1)} %copy-done.19), channel_id=1, source_target_pairs={{0,1},{1,0},{2,3},{3,2},{4,5},{5,4},{6,7},{7,6},{8,9},{9,8},{10,11... | collective-permute-start | bytes 2359304 | tf_op jit(solution)/shard_map/ppermute | solution.py:385
  151.1 2.3 %collective-permute-start.11 = (bf16[384,1024]{1,0:T(8,128)(2,1)S(1)}, bf16[384,1024]{1,0:T(8,128)(2,1)S(1)}, u32[]{:S(2)}, u32[]{:S(2)}) collective-permute-start(bf16[384,1024]{1,0:T(8,128)(2,1)S(1)} %copy-done.18), channel_id=1, source_target_pairs={{0,1},{1,0},{2,3},{3,2},{4,5},{5,4},{6,7},{7,6},{8,9},{9,8},{10,11... | collective-permute-start | bytes 2359304 | tf_op jit(solution)/shard_map/ppermute | solution.py:385

commit v6 on v5

--- a/solution.py
+++ b/solution.py
@@ -11,7 +11,7 @@
 CHUNK = 512
 PARTS = 2
 LOW_WITH = (0, PARTS - 1)
-VMEM = 50 * 2**20
+VMEM = 63 * 2**20
 ANY = pl.BlockSpec(memory_space=pl.ANY)
 
 
@@ -38,7 +38,7 @@
     )(*operands, *after)
 
 
-def hold(value, after):
+def hold(value, after=()):
     def kernel(value_ref, out_ref):
         pass
 
@@ -52,14 +52,23 @@
     count, width = rows.shape
     blocks = starts.shape[0]
     chunks = [(at, min(chunk, size - at)) for at in range(0, size, chunk)]
-    low = min(first for _, first, _ in outs)
-    high = max(first + some for _, first, some in outs)
+    used = [segment for out in outs for segment in out if segment]
+    low = min(first for _, first, _ in used)
+    high = max(first + some for _, first, some in used)
     upper = (high - low) // 32 * 16
     row_parts = [(0, upper), (upper, high - low - upper)]
     tails = [] if tail is None else [tail]
-    heights = [some for _, _, some in outs]
-    for array in tails:
-        heights[-1] += array.shape[0]
+    heights, places, tail_places = [], [], []
+    for o, out in enumerate(outs):
+        at = 0
+        for segment in out:
+            if segment:
+                places.append((o, at, segment))
+                at += segment[2]
+            else:
+                tail_places.append((o, at))
+                at += tail.shape[0]
+        heights.append(at)
 
     def kernel(starts_ref, rows_ref, weight_ref, *refs):
         tail_refs, refs = refs[: len(tails)], refs[len(tails) :]
@@ -90,29 +99,29 @@
                 if b or c:
                     w_copies[b][c].start()
         stores = []
-        for ref in tail_refs:
-            below = pl.ds(outs[-1][2], ref.shape[0])
-            read = pltpu.make_async_copy(ref, stage[-1].at[below], tail_sems.at[0])
+        for i, (o, at) in enumerate(tail_places):
+            below = pl.ds(at, tail.shape[0])
+            read = pltpu.make_async_copy(tail_refs[0], stage[o].at[below], tail_sems.at[0, i])
             read.start()
             read.wait()
-            stores.append(pltpu.make_async_copy(stage[-1].at[below], out_refs[-1].at[below], tail_sems.at[1]))
+            stores.append(pltpu.make_async_copy(stage[o].at[below], out_refs[o].at[below], tail_sems.at[1, i]))
             stores[-1].start()
         for copy in x_copies:
             copy.wait()
         for b in range(blocks):
             for c, (at, extent) in enumerate(chunks):
                 w_copies[b][c].wait()
-                for o, (index, first, some) in enumerate(outs):
+                for n, (o, place, (index, first, some)) in enumerate(places):
                     if index == b:
                         value = jnp.dot(
                             x[first - low : first - low + some, :], w[b, :, at : at + extent],
                             preferred_element_type=jnp.float32,
                         )
-                        stage[o][:some, at : at + extent] = value.astype(rows.dtype)
+                        stage[o][place : place + some, at : at + extent] = value.astype(rows.dtype)
                         store = pltpu.make_async_copy(
-                            stage[o].at[pl.ds(0, some), pl.ds(at, extent)],
-                            out_refs[o].at[pl.ds(0, some), pl.ds(at, extent)],
-                            out_sems.at[o, c],
+                            stage[o].at[pl.ds(place, some), pl.ds(at, extent)],
+                            out_refs[o].at[pl.ds(place, some), pl.ds(at, extent)],
+                            out_sems.at[n, c],
                         )
                         store.start()
                         stores.append(store)
@@ -130,8 +139,8 @@
         + [
             pltpu.SemaphoreType.DMA((2,)),
             pltpu.SemaphoreType.DMA((blocks, len(chunks))),
-            pltpu.SemaphoreType.DMA((len(outs), len(chunks))),
-            pltpu.SemaphoreType.DMA((2,)),
+            pltpu.SemaphoreType.DMA((len(places), len(chunks))),
+            pltpu.SemaphoreType.DMA((2, max(1, len(tail_places)))),
         ],
         name="products",
     )
@@ -368,8 +377,9 @@
     my_order = jnp.asarray(order)[z]
     out_width = projection_weight.shape[1] // n
 
-    def swap_y(value):
-        return lax.ppermute(value, "tensor", [(t, t ^ 1) for t in range(n)])
+    def sum_y(value):
+        pairs = [[t, t + 1] for t in range(0, n, 2)]
+        return lax.psum_scatter(value, "tensor", scatter_dimension=0, axis_index_groups=pairs, tiled=True)
 
     def hop(value, h):
         pairs = []
@@ -409,12 +419,10 @@
         row_slot = jnp.sum(jnp.where(hit, position[None, :] + 1, 0), axis=1) - 1
         return names, row_slot[:, None]
 
-    away = [(my_order[k] * 2 + 1 - y) * out_width for k in range(nz)]
-    own = [(my_order[k] * 2 + y) * out_width for k in range(nz)]
     low_rows = 2 * (owners * count // 2) * adapter_down_maps.shape[1] // out_width
     even = [(p * count // PARTS, count // PARTS) for p in range(PARTS)]
     uneven = [(0, count // 2 + low_rows), (count // 2 + low_rows, count // 2 - low_rows)]
-    away_part, own_all, from_y, sums, arrived = {}, {}, {}, {}, {}
+    sums, arrived = {}, {}
 
     def split(k):
         return uneven if k == 0 else [(0, count)]
@@ -437,24 +445,15 @@
     def whole(array):
         return [(0, count, array, 0)]
 
-    def multiply(aways, owns, tail=None, chunk=1024):
-        ks = sorted({k for k, _ in aways})
-        starts = jnp.stack([away[k] for k in ks] + [own[k] for k in owns])
-        outs = [(ks.index(k), *split(k)[p]) for k, p in aways]
-        outs += [(len(ks) + i, 0, count) for i in range(len(owns))]
-        done = then(products, rows, projection_weight, starts, out_width, outs, tail, chunk)
-        away_part.update(zip(aways, done))
-        own_all.update(zip(owns, done[len(aways) :]))
-
-    def start_y(k, p, after=None):
-        value = away_part[k, p]
-        from_y[k, p] = swap_y(value if after is None else hold(value, after))
-
-    def y_parts(k):
-        return [(*cut, from_y[k, p], 0) for p, cut in enumerate(split(k)) if (k, p) in from_y]
+    def multiply(k, p, tail=None, chunk=1024):
+        first, some = split(k)[p]
+        starts = jnp.stack([(my_order[k] * 2 + side) * out_width for side in range(2)])
+        extra = [] if tail is None else [None]
+        outs = [[(0, first, some), *extra, (1, first, some), *extra]]
+        sums[k, p] = sum_y(then(products, rows, projection_weight, starts, out_width, outs, tail, chunk)[0])
 
     def sum_parts(k):
-        return [(*cut, sums[k, p], 0) for p, cut in enumerate(cut_of(0, k)) if (k, p) in sums]
+        return [(*cut, sums[k, p], 0) for p, cut in enumerate(split(k))]
 
     def cut_of(h, m):
         return uneven if m == 0 and h <= 1 else [(0, count)]
@@ -467,8 +466,7 @@
         span = cut_of(h, m)[p]
         low_too = m == 0 and h <= 1 and p == LOW_WITH[1]
         if h == 0:
-            extra = [(low_rows, [(low, 0), (from_y[k, p], span[1])])] if low_too else []
-            value = sums[k, p] = add_up(span, [whole(own_all[k]), y_parts(k)], extra)
+            value = then(hold, sums[k, p])
         else:
             extra = [(low_rows, [(sums[k, p], span[1]), (arrived[h - 1, m, p], span[1])])] if low_too else []
             value = add_up(span, [sum_parts(k), arrived_parts(h - 1, m)], extra)
@@ -490,28 +488,17 @@
 
     row_ids = [tenant] + [pass_on(tenant, shift) for shift in range(1, owners)]
     row_sets = [rows] + [pass_on(rows, shift) for shift in range(1, owners)]
-    multiply([(0, 0)], [], chunk=512)
-    start_y(0, 0)
+    multiply(0, 0, chunk=512)
     named = [slots(some_ids, me) for some_ids in row_ids]
     names = jnp.concatenate([which for which, _ in named])
     slot_sets = [row_slot for _, row_slot in named]
     low = then(low_rank, row_sets, slot_sets, adapter_down_maps, names, out_width)
-    multiply([LOW_WITH], [], low, chunk=512)
-    start_y(*LOW_WITH)
-    multiply([(1, 0)], [0])
-    start_y(1, 0)
+    multiply(*LOW_WITH, low, chunk=512)
+    for k in range(1, nz):
+        multiply(k, 0)
     for h, m, p in line_order():
         k = slot_of(h, m)
         line(h, m, p)
-        if h == 0:
-            if k == 0 and p == 0:
-                multiply([(2, 0)] if nz > 2 else [], [1])
-            elif k == 0:
-                if nz > 2:
-                    start_y(2, 0, last[0])
-                multiply([(j, 0) for j in range(3, nz)], range(2, nz))
-            elif p == len(cut_of(h, m)) - 1 and k + 2 < nz:
-                start_y(k + 2, 0, last[0])
         if (h, k) == (0, 1):
             low_at = uneven[LOW_WITH[1]][1]
             pieces = [(sums[LOW_WITH], low_at)]
@@ -528,8 +515,8 @@
                 for shift in range(1, owners)
             ]
     span = (0, count)
-    most = add_up(span, [whole(own_all[nz - 1]), whole(deltas[0]), y_parts(nz - 1)] + back, dtype=jnp.float32)
-    out = add_up(span, [whole(most)] + [arrived_parts(h, nz - 2 - h) for h in range(nz - 1)])
+    head = add_up(span, [whole(deltas[0]), sum_parts(nz - 1)] + back, dtype=jnp.float32)
+    out = add_up(span, [whole(head)] + [arrived_parts(h, nz - 2 - h) for h in range(nz - 1)])
     return out.reshape(steps, row_count, out_width)
 
 

time: 175 us -> 245 us (1.40)
  waiting for transfers between devices: 58.5 us -> 102 us
  between operations: 3.25 us -> 18.6 us
  Pallas kernels: 69 us -> 76.8 us
  local copies, waits for them, and re-layouts: 10.7 us -> 17.3 us
  starting transfers between devices: 30.6 us -> 25.9 us
  other arithmetic: 1.1 us -> 3.93 us
    reduce_scatter x0 -> x5, waiting for transfers between devices: none -> 57.9 us  [sum_y(): lax.psum_scatter(value, 'tensor', scatter_dimension=0, axis_index_groups=...]
    ppermute x5 -> x0, waiting for transfers between devices: 21.5 us -> none  [swap_y(): return lax.ppermute(value, 'tensor', [(t, t ^ 1) for t in range(n)])]
    ppermute x5 -> x0, starting transfers between devices: 8.24 us -> none  [swap_y(): return lax.ppermute(value, 'tensor', [(t, t ^ 1) for t in range(n)])]
    pallas_call x21 -> x19, Pallas kernels: 69 us -> 76.8 us  [call(): pl.pallas_call(body, grid_spec=pltpu.PrefetchScalarGridSpec(num_scalar_pr...]
    ppermute x9, waiting for transfers between devices: 34.6 us -> 41.8 us  [hop(): return lax.ppermute(value, 'tensor', pairs)]
    unnamed x44 -> x16, local copies, waits for them, and re-layouts: 9.1 us -> 14.5 us
    ppermute x9, starting transfers between devices: 21.8 us -> 24.5 us  [hop(): return lax.ppermute(value, 'tensor', pairs)]
  transfers between devices with their start and end apart: 18 -> 18, of which waited for: 9 -> 9; matrix products, arithmetic and copies ran while one was open for 2% -> 6% of each run, Pallas kernels for 38% -> 27%
where the time goes in v6:
time: 245 us; the launch traced here: 244 us
  waiting for transfers between devices  102 us (42%)
  Pallas kernels  76.8 us (31%)
  starting transfers between devices  25.9 us (11%)
  between operations  18.6 us (8%)
  local copies, waits for them, and re-layouts  17.3 us (7%)
  other arithmetic  3.93 us (2%)
    pallas_call x19, Pallas kernels, call(): pl.pallas_call(body, grid_spec=pltpu.PrefetchScalarGridSpec(num_scalar_pr...  76.8 us
    reduce_scatter x5, waiting for transfers between devices, sum_y(): lax.psum_scatter(value, 'tensor', scatter_dimension=0, axis_index_groups=...  57.9 us
    ppermute x9, waiting for transfers between devices, hop(): return lax.ppermute(value, 'tensor', pairs)  41.8 us
    ppermute x9, starting transfers between devices, hop(): return lax.ppermute(value, 'tensor', pairs)  24.5 us
    unnamed x16, local copies, waits for them, and re-layouts  14.5 us
  transfers between devices with their start and end apart: 18, of which 9 were waited for; matrix products, arithmetic and copies ran while one was open for 6% of the time, Pallas kernels for 27%

profile of v6, /device:TPU:0, one launch (start us, length us, event | category | flops | bytes accessed | tf_op | source)
XLA Modules:
  0.0 244.1 jit_solution(12303170731361094690)
XLA Ops:
  6.5 0.7 constant_dynamic-slice_fusion
  7.2 0.7 fusion.6
  9.8 6.1 %products.5.refs_6_ = bf16[960,1024]{1,0:T(8,128)(2,1)} custom-call(s32[2]{0:T(128)} %pad_add_fusion.1.refs_0_, bf16[768,1024]{1,0:T(8,128)(2,1)} %bitcast.12, bf16[1024,8192]{1,0:T(8,128)(2,1)} %refs_2_.9), custom_call_target="tpu_custom_call" | custom-call | flops 1 | bytes 1 | tf_op jit(solution)/shard_map/products/pallas_call | solution.py:24
  16.0 1.3 copy-done
  18.2 0.8 copy.15.refs_3_.refs_2_
  18.9 1.8 collective-permute-done
  21.1 0.8 copy.16.refs_4_.refs_3_
  21.9 0.7 pad_add_fusion.refs_0_
  22.6 9.8 %low_rank.1.refs_3_.refs_4_ = bf16[96,1024]{1,0:T(8,128)(2,1)} custom-call(s32[32]{0:T(128)} %pad_add_fusion.refs_0_, bf16[768,1024]{1,0:T(8,128)(2,1)} %bitcast.13, bf16[768,1024]{1,0:T(8,128)(2,1)} %collective-permute-done.1.refs_2_, s32[192,1]{1,0:T(8,128)} %copy.15.refs_3_.refs_2_, s32[192,1]{1,0:T(8,128)} %copy.16.refs_4_.refs_3_, ...), custom_call_target="tpu_custom_call" | custom-call | flops 1 | bytes 1 | tf_op jit(solution)/shard_map/low_rank/pallas_call | solution.py:24
  32.4 6.8 %products.6.refs_3_ = bf16[768,1024]{1,0:T(8,128)(2,1)} custom-call(s32[2]{0:T(128)} %pad_add_fusion.1.refs_0_, bf16[768,1024]{1,0:T(8,128)(2,1)} %bitcast.14, bf16[1024,8192]{1,0:T(8,128)(2,1)} %refs_2_.9, bf16[96,1024]{1,0:T(8,128)(2,1)} %low_rank.1.refs_3_.refs_4_, bf16[96,1024]{1,0:T(8,128)(2,1)} %low_rank.1.refs_3_.refs_4_), custom_call_target="tpu_custom_call" | custom-call | flops 1 | bytes 1 | tf_op jit(solution)/shard_map/products/pallas_call | solution.py:24
  41.2 7.5 %products.7.refs_3_ = bf16[1536,1024]{1,0:T(8,128)(2,1)} custom-call(s32[2]{0:T(128)} %pad_add_fusion.4.refs_0_, bf16[768,1024]{1,0:T(8,128)(2,1)} %bitcast.15, bf16[1024,8192]{1,0:T(8,128)(2,1)} %refs_2_.9, bf16[768,1024]{1,0:T(8,128)(2,1)} %products.6.refs_3_), custom_call_target="tpu_custom_call" | custom-call | flops 1 | bytes 1 | tf_op jit(solution)/shard_map/products/pallas_call | solution.py:24
  50.1 0.7 pad_add_fusion.3.refs_0_
  50.8 7.5 %products.8.refs_3_ = bf16[1536,1024]{1,0:T(8,128)(2,1)} custom-call(s32[2]{0:T(128)} %pad_add_fusion.3.refs_0_, bf16[768,1024]{1,0:T(8,128)(2,1)} %bitcast.16, bf16[1024,8192]{1,0:T(8,128)(2,1)} %refs_2_.9, bf16[1536,1024]{1,0:T(8,128)(2,1)} %products.7.refs_3_), custom_call_target="tpu_custom_call" | custom-call | flops 1 | bytes 1 | tf_op jit(solution)/shard_map/products/pallas_call | solution.py:24
  60.4 7.6 %products.9.refs_1_ = bf16[1536,1024]{1,0:T(8,128)(2,1)} custom-call(s32[2]{0:T(128)} %pad_add_fusion.2.refs_0_, bf16[768,1024]{1,0:T(8,128)(2,1)} %bitcast.17, bf16[1024,8192]{1,0:T(8,128)(2,1)} %refs_2_.9, bf16[1536,1024]{1,0:T(8,128)(2,1)} %products.8.refs_3_), custom_call_target="tpu_custom_call" | custom-call | flops 1 | bytes 1 | tf_op jit(solution)/shard_map/products/pallas_call | solution.py:24
  68.0 2.2 copy.19.refs_0_
  70.2 5.3 %collective-permute-start.3 = (bf16[480,1024]{1,0:T(8,128)(2,1)}, bf16[480,1024]{1,0:T(8,128)(2,1)}, u32[]{:S(2)}, u32[]{:S(2)}) collective-permute-start(bf16[480,1024]{1,0:T(8,128)(2,1)} %hold.4.refs_1_), channel_id=1, source_target_pairs={{0,4},{12,8},{2,6},{14,10},{1,5},{13,9},{3,7},{15,11},{16,20},{28,... | collective-permute-start | bytes 2949128 | tf_op jit(solution)/shard_map/ppermute | solution.py:389
  75.5 2.1 reduce-scatter.6.cloned.1.call-done.refs_0_.refs_2_
  77.6 2.1 copy.20.refs_0_
  79.7 3.4 %collective-permute-start.2 = (bf16[384,1024]{1,0:T(8,128)(2,1)}, bf16[384,1024]{1,0:T(8,128)(2,1)S(1)}, u32[]{:S(2)}, u32[]{:S(2)}) collective-permute-start(bf16[384,1024]{1,0:T(8,128)(2,1)} %hold.5.refs_2_), channel_id=1, source_target_pairs={{0,4},{12,8},{2,6},{14,10},{1,5},{13,9},{3,7},{15,11},{16,20},{28,... | collective-permute-start | bytes 2359304 | tf_op jit(solution)/shard_map/ppermute | solution.py:389
  83.1 13.9 %collective-permute-done.3.refs_1_ = bf16[480,1024]{1,0:T(8,128)(2,1)} collective-permute-done((bf16[480,1024]{1,0:T(8,128)(2,1)}, bf16[480,1024]{1,0:T(8,128)(2,1)}, u32[]{:S(2)}, u32[]{:S(2)}) %collective-permute-start.3) | collective-permute-done | bytes 983072 | tf_op jit(solution)/shard_map/ppermute | solution.py:389
  97.0 2.5 %total.8.refs_4_ = bf16[480,1024]{1,0:T(8,128)(2,1)} custom-call(bf16[480,1024]{1,0:T(8,128)(2,1)} %reduce-scatter.8.cloned.1.call-done.refs_0_, bf16[480,1024]{1,0:T(8,128)(2,1)} %collective-permute-done.3.refs_1_, bf16[384,1024]{1,0:T(8,128)(2,1)} %hold.5.refs_2_), custom_call_target="tpu_custom_call" | custom-call | flops 1 | bytes 1 | tf_op jit(solution)/shard_map/total/pallas_call | solution.py:24
  99.5 13.7 %collective-permute-done.2.refs_1_.refs_3_ = bf16[384,1024]{1,0:T(8,128)(2,1)S(1)} collective-permute-done((bf16[384,1024]{1,0:T(8,128)(2,1)}, bf16[384,1024]{1,0:T(8,128)(2,1)S(1)}, u32[]{:S(2)}, u32[]{:S(2)}) %collective-permute-start.2) | collective-permute-done | bytes 786464 | tf_op jit(solution)/shard_map/ppermute | solution.py:389
  113.2 0.9 copy-done.1
  114.1 2.3 total.9.refs_1_
  116.3 6.9 %reduce-scatter.10.cloned.1.call-done.refs_0_ = bf16[768,1024]{1,0:T(8,128)(2,1)} async-done(((bf16[1536,1024]{1,0:T(8,128)(2,1)}), bf16[768,1024]{1,0:T(8,128)(2,1)}) %reduce-scatter.10.cloned.1.call-update) | async-done | bytes 1572880 | tf_op jit(solution)/shard_map/reduce_scatter | solution.py:382
  123.3 2.7 %copy.21.refs_0_ = bf16[768,1024]{1,0:T(8,128)(2,1)} copy(bf16[768,1024]{1,0:T(8,128)(2,1)} %reduce-scatter.10.cloned.1.call-done.refs_0_) | data formatting | bytes 3145728
  125.9 4.5 %collective-permute-start.9 = (bf16[768,1024]{1,0:T(8,128)(2,1)}, bf16[768,1024]{1,0:T(8,128)(2,1)}, u32[]{:S(2)}, u32[]{:S(2)}) collective-permute-start(bf16[768,1024]{1,0:T(8,128)(2,1)} %hold.6.refs_2_), channel_id=1, source_target_pairs={{0,4},{12,8},{2,6},{14,10},{1,5},{13,9},{3,7},{15,11},{16,20},{28,... | collective-permute-start | bytes 4718600 | tf_op jit(solution)/shard_map/ppermute | solution.py:389
  130.5 0.7 collective-permute-start.4
  131.2 1.6 collective-permute-start.8
  132.8 0.9 copy-done.2
  133.7 1.8 total.10.refs_4_
  135.5 1.3 collective-permute-start.5
  136.8 32.0 %reduce-scatter.14.cloned.1.call-done.refs_0_.refs_2_ = bf16[768,1024]{1,0:T(8,128)(2,1)} async-done(((bf16[1536,1024]{1,0:T(8,128)(2,1)}), bf16[768,1024]{1,0:T(8,128)(2,1)}) %reduce-scatter.14.cloned.1.call-update) | async-done | bytes 1572880 | tf_op jit(solution)/shard_map/reduce_scatter | solution.py:382
  168.8 2.7 %copy.22.refs_0_ = bf16[768,1024]{1,0:T(8,128)(2,1)} copy(bf16[768,1024]{1,0:T(8,128)(2,1)} %reduce-scatter.14.cloned.1.call-done.refs_0_.refs_2_) | data formatting | bytes 3145728
  171.6 0.7 copy-done.4
  172.2 2.0 total.11.refs_1_.refs_5_
  174.3 9.1 %expand.1 = (bf16[768,1024]{1,0:T(8,128)(2,1)}, bf16[384,1024]{1,0:T(8,128)(2,1)}, bf16[384,1024]{1,0:T(8,128)(2,1)}) custom-call(s32[32]{0:T(128)} %pad_add_fusion.refs_0_, bf16[96,1024]{1,0:T(8,128)(2,1)} %total.11.refs_1_.refs_5_, s32[192,1]{1,0:T(8,128)} %copy.15.refs_3_.refs_2_, s32[192,1]{1,0:T(8,128)} %copy.16.refs_4_.refs_3_, ...), custom_call_target="tpu_custom_call" | custom-call | flops 1 | bytes 1 | tf_op jit(solution)/shard_map/expand/pallas_call | solution.py:24
  183.4 4.5 %collective-permute-start.10 = (bf16[768,1024]{1,0:T(8,128)(2,1)}, bf16[768,1024]{1,0:T(8,128)(2,1)}, u32[]{:S(2)}, u32[]{:S(2)}) collective-permute-start(bf16[768,1024]{1,0:T(8,128)(2,1)} %hold.7.refs_2_), channel_id=1, source_target_pairs={{0,4},{12,8},{2,6},{14,10},{1,5},{13,9},{3,7},{15,11},{16,20},{28,... | collective-permute-start | bytes 4718600 | tf_op jit(solution)/shard_map/ppermute | solution.py:389
  187.9 3.1 %total.12.refs_4_ = bf16[768,1024]{1,0:T(8,128)(2,1)} custom-call(bf16[768,1024]{1,0:T(8,128)(2,1)} %reduce-scatter.10.cloned.1.call-done.refs_0_, bf16[768,1024]{1,0:T(8,128)(2,1)} %collective-permute-done.9.refs_1_, bf16[768,1024]{1,0:T(8,128)(2,1)} %hold.7.refs_2_), custom_call_target="tpu_custom_call" | custom-call | flops 1 | bytes 1 | tf_op jit(solution)/shard_map/total/pallas_call | solution.py:24
  191.0 1.8 collective-permute-start.11
  192.9 2.7 %total.13.refs_6_ = bf16[768,1024]{1,0:T(8,128)(2,1)} custom-call(bf16[768,1024]{1,0:T(8,128)(2,1)} %reduce-scatter.14.cloned.1.call-done.refs_0_.refs_2_, bf16[480,1024]{1,0:T(8,128)(2,1)} %collective-permute-done.8.refs_1_, bf16[768,1024]{1,0:T(8,128)(2,1)} %reduce-scatter.14.cloned.1.call-done.refs_0_.refs_2_, bf16[384,1024]{1,0:T(8,128)(2,1)} %copy-done.2, ...), custom_call_target="tpu_custom_call" | custom-call | flops 1 | bytes 1 | tf_op jit(solution)/shard_map/total/pallas_call | solution.py:24
  195.6 1.3 collective-permute-start.12
  197.4 16.9 %reduce-scatter.12.cloned.1.call-done.refs_1_.refs_4_ = bf16[768,1024]{1,0:T(8,128)(2,1)} async-done(((bf16[1536,1024]{1,0:T(8,128)(2,1)}), bf16[768,1024]{1,0:T(8,128)(2,1)}) %reduce-scatter.12.cloned.1.call-update) | async-done | bytes 1572880 | tf_op jit(solution)/shard_map/reduce_scatter | solution.py:382
  214.3 1.0 copy-done.3
  215.3 3.5 %total.14.refs_0_.refs_4_ = f32[768,1024]{1,0:T(8,128)} custom-call(bf16[768,1024]{1,0:T(8,128)(2,1)} %get-tuple-element.8.refs_1_.refs_0_.refs_3_, bf16[768,1024]{1,0:T(8,128)(2,1)} %reduce-scatter.12.cloned.1.call-done.refs_1_.refs_4_, bf16[384,1024]{1,0:T(8,128)(2,1)} %copy-done.3, bf16[768,1024]{1,0:T(8,128)(2,1)} %get-tuple-element.8.refs_1_.refs_0_.refs_3_, ...), custom_call_target="tpu_custom_call" | custom-call | flops 1 | bytes 1 | tf_op jit(solution)/shard_map/total/pallas_call | solution.py:24
  218.8 1.4 collective-permute-done.10.refs_1_
  220.2 12.8 %collective-permute-done.12.refs_3_ = bf16[768,1024]{1,0:T(8,128)(2,1)} collective-permute-done((bf16[768,1024]{1,0:T(8,128)(2,1)}, bf16[768,1024]{1,0:T(8,128)(2,1)}, u32[]{:S(2)}, u32[]{:S(2)}) %collective-permute-start.12) | collective-permute-done | bytes 1572896 | tf_op jit(solution)/shard_map/ppermute | solution.py:389
  233.0 4.5 %total.15 = bf16[768,1024]{1,0:T(8,128)(2,1)} custom-call(f32[768,1024]{1,0:T(8,128)} %total.14.refs_0_.refs_4_, bf16[768,1024]{1,0:T(8,128)(2,1)} %collective-permute-done.10.refs_1_, bf16[768,1024]{1,0:T(8,128)(2,1)} %collective-permute-done.11.refs_2_, bf16[768,1024]{1,0:T(8,128)(2,1)} %collective-permute-done.12.refs_3_, f32[768,1024]{1,0:T(8,128)} %total.14.refs_0_.refs_4_), custom_call_target="tpu_custom_call" | custom-call | flops 1 | bytes 1 | tf_op jit(solution)/shard_map/total/pallas_call | solution.py:24
  (50 shorter events, 4.2 us)
Async XLA Ops:
  6.5 61.4 %reduce-scatter.8.cloned.1.call-start = ((), (), s32[]{:S(2)}) async-start(), calls=%async_computation.6 | async-start | bytes 2949120 | tf_op jit(solution)/shard_map/reduce_scatter | solution.py:382
  15.9 1.4 copy-start
  15.9 1.9 copy-start.5
  15.9 61.7 %reduce-scatter.6.cloned.1.call-start = ((), (), s32[]{:S(2)}) async-start(), calls=%async_computation.5 | async-start | bytes 2359296 | tf_op jit(solution)/shard_map/reduce_scatter | solution.py:382
  17.3 5.3 %collective-permute-start.1 = (bf16[768,1024]{1,0:T(8,128)(2,1)S(1)}, bf16[768,1024]{1,0:T(8,128)(2,1)}, u32[]{:S(2)}, u32[]{:S(2)}) collective-permute-start(bf16[768,1024]{1,0:T(8,128)(2,1)S(1)} %bitcast.18), channel_id=1, source_target_pairs={{0,1},{1,0},{2,3},{3,2},{4,5},{5,4},{6,7},{7,6},{8,9},{9,8},{10,11... | collective-permute-start | bytes 4718600 | tf_op jit(solution)/shard_map/ppermute | solution.py:395
  17.8 2.9 %collective-permute-start = (s32[192]{0:T(256)S(1)}, s32[192]{0:T(256)S(1)}, u32[]{:S(2)}, u32[]{:S(2)}) collective-permute-start(s32[192]{0:T(256)S(1)} %copy-done.5), channel_id=1, source_target_pairs={{0,1},{1,0},{2,3},{3,2},{4,5},{5,4},{6,7},{7,6},{8,9},{9,8},{10,11... | collective-permute-start | bytes 2312 | tf_op jit(solution)/shard_map/ppermute | solution.py:395
  39.2 84.0 %reduce-scatter.10.cloned.1.call-start = ((), (), s32[]{:S(2)}) async-start(), calls=%async_computation.7 | async-start | bytes 4718592 | tf_op jit(solution)/shard_map/reduce_scatter | solution.py:382
  48.7 120.1 %reduce-scatter.14.cloned.1.call-start = ((), (), s32[]{:S(2)}) async-start(), calls=%async_computation.9 | async-start | bytes 4718592 | tf_op jit(solution)/shard_map/reduce_scatter | solution.py:382
  58.3 156.0 %reduce-scatter.12.cloned.1.call-start = ((), (), s32[]{:S(2)}) async-start(), calls=%async_computation.8 | async-start | bytes 4718592 | tf_op jit(solution)/shard_map/reduce_scatter | solution.py:382
  70.2 26.7 %collective-permute-start.3 = (bf16[480,1024]{1,0:T(8,128)(2,1)}, bf16[480,1024]{1,0:T(8,128)(2,1)}, u32[]{:S(2)}, u32[]{:S(2)}) collective-permute-start(bf16[480,1024]{1,0:T(8,128)(2,1)} %hold.4.refs_1_), channel_id=1, source_target_pairs={{0,4},{12,8},{2,6},{14,10},{1,5},{13,9},{3,7},{15,11},{16,20},{28,... | collective-permute-start | bytes 2949128 | tf_op jit(solution)/shard_map/ppermute | solution.py:389
  79.7 33.5 %collective-permute-start.2 = (bf16[384,1024]{1,0:T(8,128)(2,1)}, bf16[384,1024]{1,0:T(8,128)(2,1)S(1)}, u32[]{:S(2)}, u32[]{:S(2)}) collective-permute-start(bf16[384,1024]{1,0:T(8,128)(2,1)} %hold.5.refs_2_), channel_id=1, source_target_pairs={{0,4},{12,8},{2,6},{14,10},{1,5},{13,9},{3,7},{15,11},{16,20},{28,... | collective-permute-start | bytes 2359304 | tf_op jit(solution)/shard_map/ppermute | solution.py:389
  113.2 0.9 copy-start.1
  125.9 62.0 %collective-permute-start.9 = (bf16[768,1024]{1,0:T(8,128)(2,1)}, bf16[768,1024]{1,0:T(8,128)(2,1)}, u32[]{:S(2)}, u32[]{:S(2)}) collective-permute-start(bf16[768,1024]{1,0:T(8,128)(2,1)} %hold.6.refs_2_), channel_id=1, source_target_pairs={{0,4},{12,8},{2,6},{14,10},{1,5},{13,9},{3,7},{15,11},{16,20},{28,... | collective-permute-start | bytes 4718600 | tf_op jit(solution)/shard_map/ppermute | solution.py:389
  130.5 2.3 collective-permute-start.4
  131.2 61.7 %collective-permute-start.8 = (bf16[480,1024]{1,0:T(8,128)(2,1)}, bf16[480,1024]{1,0:T(8,128)(2,1)}, u32[]{:S(2)}, u32[]{:S(2)}) collective-permute-start(bf16[480,1024]{1,0:T(8,128)(2,1)} %total.8.refs_4_), channel_id=1, source_target_pairs={{4,8},{8,4},{6,10},{10,6},{5,9},{9,5},{7,11},{11,7},{20,24},{24,20... | collective-permute-start | bytes 2949128 | tf_op jit(solution)/shard_map/ppermute | solution.py:389
  132.8 0.9 copy-start.2
  135.5 36.1 %collective-permute-start.5 = (bf16[96,1024]{1,0:T(8,128)(2,1)}, bf16[96,1024]{1,0:T(8,128)(2,1)S(1)}, u32[]{:S(2)}, u32[]{:S(2)}) collective-permute-start(bf16[96,1024]{1,0:T(8,128)(2,1)} %total.10.refs_4_), channel_id=1, source_target_pairs={{8,12},{4,0},{10,14},{6,2},{9,13},{5,1},{11,15},{7,3},{24,28},{20,... | collective-permute-start | bytes 589832 | tf_op jit(solution)/shard_map/ppermute | solution.py:389
  171.6 0.7 copy-start.4
  183.4 36.8 %collective-permute-start.10 = (bf16[768,1024]{1,0:T(8,128)(2,1)}, bf16[768,1024]{1,0:T(8,128)(2,1)}, u32[]{:S(2)}, u32[]{:S(2)}) collective-permute-start(bf16[768,1024]{1,0:T(8,128)(2,1)} %hold.7.refs_2_), channel_id=1, source_target_pairs={{0,4},{12,8},{2,6},{14,10},{1,5},{13,9},{3,7},{15,11},{16,20},{28,... | collective-permute-start | bytes 4718600 | tf_op jit(solution)/shard_map/ppermute | solution.py:389
  191.0 29.2 %collective-permute-start.11 = (bf16[768,1024]{1,0:T(8,128)(2,1)}, bf16[768,1024]{1,0:T(8,128)(2,1)}, u32[]{:S(2)}, u32[]{:S(2)}) collective-permute-start(bf16[768,1024]{1,0:T(8,128)(2,1)} %total.12.refs_4_), channel_id=1, source_target_pairs={{4,8},{8,4},{6,10},{10,6},{5,9},{9,5},{7,11},{11,7},{20,24},{24,20... | collective-permute-start | bytes 4718600 | tf_op jit(solution)/shard_map/ppermute | solution.py:389
  195.6 37.5 %collective-permute-start.12 = (bf16[768,1024]{1,0:T(8,128)(2,1)}, bf16[768,1024]{1,0:T(8,128)(2,1)}, u32[]{:S(2)}, u32[]{:S(2)}) collective-permute-start(bf16[768,1024]{1,0:T(8,128)(2,1)} %total.13.refs_6_), channel_id=1, source_target_pairs={{8,12},{4,0},{10,14},{6,2},{9,13},{5,1},{11,15},{7,3},{24,28},{20,... | collective-permute-start | bytes 4718600 | tf_op jit(solution)/shard_map/ppermute | solution.py:389
  196.9 17.4 %collective-permute-start.6 = (bf16[384,1024]{1,0:T(8,128)(2,1)}, bf16[384,1024]{1,0:T(8,128)(2,1)S(1)}, u32[]{:S(2)}, u32[]{:S(2)}) collective-permute-start(bf16[384,1024]{1,0:T(8,128)(2,1)} %get-tuple-element.9), channel_id=1, source_target_pairs={{0,1},{1,0},{2,3},{3,2},{4,5},{5,4},{6,7},{7,6},{8,9},{9,8},{10,11... | collective-permute-start | bytes 2359304 | tf_op jit(solution)/shard_map/ppermute | solution.py:395
  196.9 17.4 %collective-permute-start.7 = (bf16[384,1024]{1,0:T(8,128)(2,1)}, bf16[384,1024]{1,0:T(8,128)(2,1)}, u32[]{:S(2)}, u32[]{:S(2)}) collective-permute-start(bf16[384,1024]{1,0:T(8,128)(2,1)} %get-tuple-element.10), channel_id=1, source_target_pairs={{0,1},{1,0},{2,3},{3,2},{4,5},{5,4},{6,7},{7,6},{8,9},{9,8},{10,11... | collective-permute-start | bytes 2359304 | tf_op jit(solution)/shard_map/ppermute | solution.py:395
  214.3 1.0 copy-start.3
Sparse Core Ops, SparseCore 0:
  16.1 33.0 reduce-scatter.7
  51.5 26.0 reduce-scatter.5
  79.9 43.3 reduce-scatter.9
  125.4 43.3 reduce-scatter.13
  170.9 43.3 reduce-scatter.11

commit v7 on v5

--- a/solution.py
+++ b/solution.py
@@ -11,7 +11,8 @@
 CHUNK = 512
 PARTS = 2
 LOW_WITH = (0, PARTS - 1)
-VMEM = 50 * 2**20
+HEAD_AFTER = (2, 0)
+VMEM = 63 * 2**20
 ANY = pl.BlockSpec(memory_space=pl.ANY)
 
 
@@ -282,7 +283,7 @@
     )
 
 
-def expand(low, slot_sets, maps, index, after=()):
+def expand(low, slot_sets, maps, index, places, after=()):
     sets = len(slot_sets)
     rank, width = maps.shape[1:]
     tall = low.shape[0]
@@ -291,23 +292,20 @@
     span = index.shape[0] // sets * rank
     repeats = count // slot_sets[0].shape[0]
 
-    outs = [(0, 0, count)] + [
-        (s, p * count // PARTS, count // PARTS) for s in range(1, sets) for p in range(PARTS)
-    ]
-
-    def kernel(index_ref, low_ref, *refs):
-        slot_refs, maps_ref, out_refs = refs[:sets], refs[sets], refs[sets + 1 : sets + 1 + len(outs)]
-        stage, maps_buf, map_sems, out_sems = refs[sets + 1 + len(outs) :]
+    def kernel(index_ref, places_ref, low_ref, *refs):
+        slot_refs, maps_ref, out_ref = refs[:sets], refs[sets], refs[sets + 1]
+        stage, maps_buf, map_sems, out_sems = refs[sets + 2 :]
         map_copies = block_copies(index_ref, maps_ref, maps_buf, map_sems, sets, rank)
         writes = [
-            pltpu.make_async_copy(stage.at[s, pl.ds(first, some)], out_refs[o], out_sems.at[o])
-            for o, (s, first, some) in enumerate(outs)
+            pltpu.make_async_copy(
+                stage.at[s], out_ref.at[pl.ds(pl.multiple_of(places_ref[s] * count, count), count)], out_sems.at[s]
+            )
+            for s in range(sets)
         ]
-        order = list(range(1, sets)) + [0]
-        for s in order:
+        for s in range(sets):
             for copy in map_copies[s]:
                 copy.start()
-        for s in order:
+        for s in range(sets):
             lanes = [(s * half // tall + b) * 2 * rank for b in range(half // tall)]
             mine = jnp.concatenate(
                 [low_ref[:, at + side : at + side + rank] for side in (0, rank) for at in lanes], axis=0
@@ -322,22 +320,20 @@
                     picked, maps_buf[s * span : (s + 1) * span, at : at + CHUNK], preferred_element_type=jnp.float32
                 )
                 stage[s, :, at : at + CHUNK] = value.astype(stage.dtype)
-            for o, (which, _, _) in enumerate(outs):
-                if which == s:
-                    writes[o].start()
+            writes[s].start()
         for write in writes:
             write.wait()
 
     return call(
-        kernel, [index, low, *slot_sets, maps], after, prefetch=1,
+        kernel, [index, places, low, *slot_sets, maps], after, prefetch=2,
         in_specs=[pl.BlockSpec(memory_space=pltpu.VMEM)] * (1 + sets) + [ANY],
-        out_specs=[ANY] * len(outs),
-        out_shape=[jax.ShapeDtypeStruct((some, width), jnp.bfloat16) for _, _, some in outs],
+        out_specs=ANY,
+        out_shape=jax.ShapeDtypeStruct((sets * count, width), jnp.bfloat16),
         scratch=[
             pltpu.VMEM((sets, count, width), jnp.bfloat16),
             pltpu.VMEM((sets * span, width), maps.dtype),
             pltpu.SemaphoreType.DMA((index.shape[0],)),
-            pltpu.SemaphoreType.DMA((len(outs),)),
+            pltpu.SemaphoreType.DMA((sets,)),
         ],
         name="expand",
     )
@@ -457,7 +453,9 @@
         return [(*cut, sums[k, p], 0) for p, cut in enumerate(cut_of(0, k)) if (k, p) in sums]
 
     def cut_of(h, m):
-        return uneven if m == 0 and h <= 1 else [(0, count)]
+        if m == 0 and h <= 1:
+            return uneven
+        return even if m == 1 else [(0, count)]
 
     def arrived_parts(h, m):
         return [(*cut, arrived[h, m, p], 0) for p, cut in enumerate(cut_of(h, m)) if (h, m, p) in arrived]
@@ -512,7 +510,7 @@
                 multiply([(j, 0) for j in range(3, nz)], range(2, nz))
             elif p == len(cut_of(h, m)) - 1 and k + 2 < nz:
                 start_y(k + 2, 0, last[0])
-        if (h, k) == (0, 1):
+        if (h, k, p) == (0, 1, len(cut_of(h, m)) - 1):
             low_at = uneven[LOW_WITH[1]][1]
             pieces = [(sums[LOW_WITH], low_at)]
             for step in range(nz - 1):
@@ -521,15 +519,18 @@
                     pieces.append((hop(prefix, step), 0))
                 else:
                     pieces.append((arrived[step, 0, LOW_WITH[1]], low_at))
+        if (h, m, p) == (1, 1, 0):
             low_sum = then(total, [(low_rows, pieces)])
-            deltas = then(expand, low_sum, slot_sets, adapter_up_maps, names)
-            back = [
-                [(*cut, pass_on(deltas[1 + (shift - 1) * PARTS + p], -shift), 0) for p, cut in enumerate(even)]
-                for shift in range(1, owners)
-            ]
+            places = jnp.stack([(me - shift) % owners for shift in range(owners)])
+            deltas = then(expand, low_sum, slot_sets, adapter_up_maps, names, places)
+            delta = lax.psum_scatter(deltas, "dp", scatter_dimension=0, tiled=True)
+        if (h, m) == (HEAD_AFTER if nz > 2 else (0, 0)) and p == len(cut_of(h, m)) - 1:
+            head = add_up((0, count), [whole(own_all[nz - 1]), whole(delta)], dtype=jnp.float32)
     span = (0, count)
-    most = add_up(span, [whole(own_all[nz - 1]), whole(deltas[0]), y_parts(nz - 1)] + back, dtype=jnp.float32)
-    out = add_up(span, [whole(most)] + [arrived_parts(h, nz - 2 - h) for h in range(nz - 1)])
+    early = [arrived_parts(h, nz - 2 - h) for h in range(1, nz - 2)]
+    late = [arrived_parts(h, nz - 2 - h) for h in range(nz - 1) if not 1 <= h < nz - 2]
+    most = add_up(span, [whole(head), y_parts(nz - 1)] + early, dtype=jnp.float32)
+    out = add_up(span, [whole(most)] + late)
     return out.reshape(steps, row_count, out_width)
 
 

time: 175 us -> 227 us (1.30)
  the two profiles are of different devices: /device:TPU:0 before, /device:TPU:18 now
where the time goes in v7:
time: 227 us; the launch traced here: 226 us
  Pallas kernels  89.4 us (39%)
  waiting for transfers between devices  79.6 us (35%)
  starting transfers between devices  30.7 us (14%)
  between operations  16.5 us (7%)
  local copies, waits for them, and re-layouts  6.27 us (3%)
  other arithmetic  3.8 us (2%)
    pallas_call x24, Pallas kernels, call(): pl.pallas_call(body, grid_spec=pltpu.PrefetchScalarGridSpec(num_scalar_pr...  89.4 us
    ppermute x11, waiting for transfers between devices, hop(): return lax.ppermute(value, 'tensor', pairs)  47.2 us
    ppermute x5, waiting for transfers between devices, swap_y(): return lax.ppermute(value, 'tensor', [(t, t ^ 1) for t in range(n)])  32.4 us
    ppermute x11, starting transfers between devices, hop(): return lax.ppermute(value, 'tensor', pairs)  24.3 us
    ppermute x5, starting transfers between devices, swap_y(): return lax.ppermute(value, 'tensor', [(t, t ^ 1) for t in range(n)])  5.9 us
  transfers between devices with their start and end apart: 19, of which 8 were waited for; matrix products, arithmetic and copies ran while one was open for 3% of the time, Pallas kernels for 33%

profile of v7, /device:TPU:18, one launch (start us, length us, event | category | flops | bytes accessed | tf_op | source)
XLA Modules:
  0.0 226.3 jit_solution(8741782817848995596)
XLA Ops:
  7.0 0.7 constant_dynamic-slice_fusion
  9.0 3.8 %products.5.refs_6_ = bf16[480,1024]{1,0:T(8,128)(2,1)} custom-call(s32[1]{0:T(128)} %bitcast.10.refs_0_, bf16[768,1024]{1,0:T(8,128)(2,1)} %bitcast.19, bf16[1024,8192]{1,0:T(8,128)(2,1)} %refs_2_.9), custom_call_target="tpu_custom_call" | custom-call | flops 1 | bytes 1 | tf_op jit(solution)/shard_map/products/pallas_call | solution.py:25
  12.8 1.6 collective-permute-start.3
  14.8 0.8 copy.13.refs_3_
  15.9 0.8 copy.14.refs_4_
  17.4 9.3 %low_rank.1.refs_3_.refs_4_.refs_2_ = bf16[96,1024]{1,0:T(8,128)(2,1)} custom-call(s32[32]{0:T(128)} %pad_add_fusion.2.refs_0_, bf16[768,1024]{1,0:T(8,128)(2,1)} %bitcast.20, bf16[768,1024]{1,0:T(8,128)(2,1)} %collective-permute-done.1.refs_2_, s32[192,1]{1,0:T(8,128)} %copy.13.refs_3_, s32[192,1]{1,0:T(8,128)} %copy.14.refs_4_, ...), custom_call_target="tpu_custom_call" | custom-call | flops 1 | bytes 1 | tf_op jit(solution)/shard_map/low_rank/pallas_call | solution.py:25
  26.7 3.5 %products.6.refs_3_ = bf16[384,1024]{1,0:T(8,128)(2,1)} custom-call(s32[1]{0:T(128)} %bitcast.10.refs_0_, bf16[768,1024]{1,0:T(8,128)(2,1)} %bitcast.21, bf16[1024,8192]{1,0:T(8,128)(2,1)} %refs_2_.9, bf16[96,1024]{1,0:T(8,128)(2,1)} %low_rank.1.refs_3_.refs_4_.refs_2_, bf16[96,1024]{1,0:T(8,128)(2,1)} %low_rank.1.refs_3_.refs_4_.refs_2_), custom_call_target="tpu_custom_call" | custom-call | flops 1 | bytes 1 | tf_op jit(solution)/shard_map/products/pallas_call | solution.py:25
  32.1 7.5 %products.7 = (bf16[768,1024]{1,0:T(8,128)(2,1)}, bf16[768,1024]{1,0:T(8,128)(2,1)}) custom-call(s32[2]{0:T(128)} %pad_add_fusion.1.refs_0_, bf16[768,1024]{1,0:T(8,128)(2,1)} %bitcast.22, bf16[1024,8192]{1,0:T(8,128)(2,1)} %refs_2_.9, bf16[384,1024]{1,0:T(8,128)(2,1)} %products.6.refs_3_), custom_call_target="tpu_custom_call" | custom-call | flops 1 | bytes 1 | tf_op jit(solution)/shard_map/products/pallas_call | solution.py:25
  39.6 1.6 collective-permute-start.7
  41.2 2.4 %total.15.refs_3_.refs_0_ = bf16[480,1024]{1,0:T(8,128)(2,1)} custom-call(bf16[768,1024]{1,0:T(8,128)(2,1)} %get-tuple-element.12.refs_0_, bf16[480,1024]{1,0:T(8,128)(2,1)} %collective-permute-done.3.refs_1_, bf16[768,1024]{1,0:T(8,128)(2,1)} %get-tuple-element.13.refs_2_), custom_call_target="tpu_custom_call" | custom-call | flops 1 | bytes 1 | tf_op jit(solution)/shard_map/total/pallas_call | solution.py:25
  43.6 1.3 collective-permute-start.5
  46.2 7.5 %products.8 = (bf16[768,1024]{1,0:T(8,128)(2,1)}, bf16[768,1024]{1,0:T(8,128)(2,1)}) custom-call(s32[2]{0:T(128)} %pad_add_fusion.3.refs_0_, bf16[768,1024]{1,0:T(8,128)(2,1)} %bitcast.23, bf16[1024,8192]{1,0:T(8,128)(2,1)} %refs_2_.9, bf16[480,1024]{1,0:T(8,128)(2,1)} %total.15.refs_3_.refs_0_), custom_call_target="tpu_custom_call" | custom-call | flops 1 | bytes 1 | tf_op jit(solution)/shard_map/products/pallas_call | solution.py:25
  53.6 0.9 collective-permute-done.2.refs_1_.refs_3_
  54.6 0.9 copy-done.4
  55.5 2.2 total.16.refs_3_.refs_0_.refs_2_.refs_1_
  57.6 1.5 collective-permute-start.4
  60.4 9.9 %products.9 = (bf16[768,1024]{1,0:T(8,128)(2,1)}, bf16[768,1024]{1,0:T(8,128)(2,1)}, bf16[768,1024]{1,0:T(8,128)(2,1)}) custom-call(s32[3]{0:T(128)} %pad_add_fusion.refs_0_, bf16[768,1024]{1,0:T(8,128)(2,1)} %bitcast.24, bf16[1024,8192]{1,0:T(8,128)(2,1)} %refs_2_.9, bf16[384,1024]{1,0:T(8,128)(2,1)} %total.16.refs_3_.refs_0_.refs_2_.refs_1_), custom_call_target="tpu_custom_call" | custom-call | flops 1 | bytes 1 | tf_op jit(solution)/shard_map/products/pallas_call | solution.py:25
  70.5 2.4 %total.17.refs_4_ = bf16[480,1024]{1,0:T(8,128)(2,1)} custom-call(bf16[480,1024]{1,0:T(8,128)(2,1)} %total.15.refs_3_.refs_0_, bf16[480,1024]{1,0:T(8,128)(2,1)} %collective-permute-done.5.refs_1_, bf16[768,1024]{1,0:T(8,128)(2,1)} %get-tuple-element.16.refs_2_.refs_0_), custom_call_target="tpu_custom_call" | custom-call | flops 1 | bytes 1 | tf_op jit(solution)/shard_map/total/pallas_call | solution.py:25
  73.0 12.4 %collective-permute-done.4.refs_1_.refs_3_ = bf16[384,1024]{1,0:T(8,128)(2,1)S(1)} collective-permute-done((bf16[384,1024]{1,0:T(8,128)(2,1)}, bf16[384,1024]{1,0:T(8,128)(2,1)S(1)}, u32[]{:S(2)}, u32[]{:S(2)}) %collective-permute-start.4) | collective-permute-done | bytes 786464 | tf_op jit(solution)/shard_map/ppermute | solution.py:375
  85.4 0.9 copy-done.1
  86.3 2.2 total.18.refs_2_
  88.5 2.4 %collective-permute-start.6 = (bf16[384,1024]{1,0:T(8,128)(2,1)}, bf16[384,1024]{1,0:T(8,128)(2,1)S(1)}, u32[]{:S(2)}, u32[]{:S(2)}) collective-permute-start(bf16[384,1024]{1,0:T(8,128)(2,1)} %total.18.refs_2_), channel_id=1, source_target_pairs={{4,8},{8,4},{6,10},{10,6},{5,9},{9,5},{7,11},{11,7},{20,24},{24,20... | collective-permute-start | bytes 2359304 | tf_op jit(solution)/shard_map/ppermute | solution.py:375
  90.9 2.2 total.19.refs_2_.refs_0_
  93.1 1.3 collective-permute-start.9
  94.4 2.3 total.20.refs_2_.refs_0_.refs_1_
  96.7 11.7 %collective-permute-done.6.refs_1_.refs_2_.refs_3_ = bf16[384,1024]{1,0:T(8,128)(2,1)S(1)} collective-permute-done((bf16[384,1024]{1,0:T(8,128)(2,1)}, bf16[384,1024]{1,0:T(8,128)(2,1)S(1)}, u32[]{:S(2)}, u32[]{:S(2)}) %collective-permute-start.6) | collective-permute-done | bytes 786464 | tf_op jit(solution)/shard_map/ppermute | solution.py:375
  108.4 0.9 copy-done.2
  109.3 1.8 total.21.refs_2_
  111.1 1.3 collective-permute-start.8
  113.0 2.3 total.22.refs_4_
  116.5 2.0 total.23.refs_2_.refs_6_
  118.6 8.5 %expand.1.refs_2_ = bf16[1536,1024]{1,0:T(8,128)(2,1)} custom-call(s32[32]{0:T(128)} %pad_add_fusion.2.refs_0_, s32[2]{0:T(128)} %pad_add_fusion.4.refs_1_, bf16[96,1024]{1,0:T(8,128)(2,1)} %total.23.refs_2_.refs_6_, s32[192,1]{1,0:T(8,128)} %copy.13.refs_3_, s32[192,1]{1,0:T(8,128)} %copy.14.refs_4_, bf16[64,64,1024]{2,1,0:T(8,128)(2,1)} %refs_5_.3, ...), custom_call_target="tpu_custom_call" | custom-call | flops 1 | bytes 1 | tf_op jit(solution)/shard_map/expand/pallas_call | solution.py:25
  127.7 2.8 %collective-permute-start.11 = (bf16[480,1024]{1,0:T(8,128)(2,1)}, bf16[480,1024]{1,0:T(8,128)(2,1)}, u32[]{:S(2)}, u32[]{:S(2)}) collective-permute-start(bf16[480,1024]{1,0:T(8,128)(2,1)} %total.17.refs_4_), channel_id=1, source_target_pairs={{4,8},{8,4},{6,10},{10,6},{5,9},{9,5},{7,11},{11,7},{20,24},{24,20... | collective-permute-start | bytes 2949128 | tf_op jit(solution)/shard_map/ppermute | solution.py:375
  130.4 1.3 collective-permute-start.12
  131.7 1.6 collective-permute-start.13
  133.3 31.5 %collective-permute-done.10.refs_1_ = bf16[768,1024]{1,0:T(8,128)(2,1)} collective-permute-done((bf16[768,1024]{1,0:T(8,128)(2,1)}, bf16[768,1024]{1,0:T(8,128)(2,1)}, u32[]{:S(2)}, u32[]{:S(2)}) %collective-permute-start.10) | collective-permute-done | bytes 1572896 | tf_op jit(solution)/shard_map/ppermute | solution.py:368
  164.8 3.0 %total.24.refs_2_.refs_0_ = bf16[768,1024]{1,0:T(8,128)(2,1)} custom-call(bf16[768,1024]{1,0:T(8,128)(2,1)} %get-tuple-element.18.refs_0_, bf16[768,1024]{1,0:T(8,128)(2,1)} %collective-permute-done.10.refs_1_, bf16[1536,1024]{1,0:T(8,128)(2,1)} %expand.1.refs_2_), custom_call_target="tpu_custom_call" | custom-call | flops 1 | bytes 1 | tf_op jit(solution)/shard_map/total/pallas_call | solution.py:25
  167.8 2.2 total.25.refs_4_
  170.0 2.8 %total.26.refs_2_ = bf16[768,1024]{1,0:T(8,128)(2,1)} custom-call(bf16[768,1024]{1,0:T(8,128)(2,1)} %total.24.refs_2_.refs_0_, bf16[480,1024]{1,0:T(8,128)(2,1)} %collective-permute-done.11.refs_1_, bf16[768,1024]{1,0:T(8,128)(2,1)} %total.24.refs_2_.refs_0_, bf16[384,1024]{1,0:T(8,128)(2,1)} %copy-done.2, bf16[384,1024]{1,0:T(8,128)(2,1)} %total.25.refs_4_), custom_call_target="tpu_custom_call" | custom-call | flops 1 | bytes 1 | tf_op jit(solution)/shard_map/total/pallas_call | solution.py:25
  172.8 5.4 %collective-permute-start.17 = (bf16[768,1024]{1,0:T(8,128)(2,1)}, bf16[768,1024]{1,0:T(8,128)(2,1)}, u32[]{:S(2)}, u32[]{:S(2)}) collective-permute-start(bf16[768,1024]{1,0:T(8,128)(2,1)} %total.26.refs_2_), channel_id=1, source_target_pairs={{8,12},{4,0},{10,14},{6,2},{9,13},{5,1},{11,15},{7,3},{24,28},{20,... | collective-permute-start | bytes 4718600 | tf_op jit(solution)/shard_map/ppermute | solution.py:375
  178.3 1.3 collective-permute-start.16
  179.6 2.4 %collective-permute-start.14 = (bf16[384,1024]{1,0:T(8,128)(2,1)S(1)}, bf16[384,1024]{1,0:T(8,128)(2,1)}, u32[]{:S(2)}, u32[]{:S(2)}) collective-permute-start(bf16[384,1024]{1,0:T(8,128)(2,1)S(1)} %copy-done.3), channel_id=1, source_target_pairs={{4,8},{8,4},{6,10},{10,6},{5,9},{9,5},{7,11},{11,7},{20,24},{24,20... | collective-permute-start | bytes 2359304 | tf_op jit(solution)/shard_map/ppermute | solution.py:375
  181.9 3.5 %collective-permute-start.15 = (bf16[384,1024]{1,0:T(8,128)(2,1)}, bf16[384,1024]{1,0:T(8,128)(2,1)}, u32[]{:S(2)}, u32[]{:S(2)}) collective-permute-start(bf16[384,1024]{1,0:T(8,128)(2,1)} %total.25.refs_4_), channel_id=1, source_target_pairs={{4,8},{8,4},{6,10},{10,6},{5,9},{9,5},{7,11},{11,7},{20,24},{24,20... | collective-permute-start | bytes 2359304 | tf_op jit(solution)/shard_map/ppermute | solution.py:375
  185.5 3.2 %total.27.refs_0_.refs_3_.refs_6_ = f32[768,1024]{1,0:T(8,128)} custom-call(bf16[768,1024]{1,0:T(8,128)(2,1)} %get-tuple-element.15.refs_0_, bf16[768,1024]{1,0:T(8,128)(2,1)} %reduce-scatter.2.cloned.1.call-done.refs_1_, bf16[768,1024]{1,0:T(8,128)(2,1)} %total.26.refs_2_), custom_call_target="tpu_custom_call" | custom-call | flops 1 | bytes 1 | tf_op jit(solution)/shard_map/total/pallas_call | solution.py:25
  188.7 13.4 %collective-permute-done.14.refs_2_ = bf16[384,1024]{1,0:T(8,128)(2,1)} collective-permute-done((bf16[384,1024]{1,0:T(8,128)(2,1)S(1)}, bf16[384,1024]{1,0:T(8,128)(2,1)}, u32[]{:S(2)}, u32[]{:S(2)}) %collective-permute-start.14) | collective-permute-done | bytes 786464 | tf_op jit(solution)/shard_map/ppermute | solution.py:375
  202.0 8.9 %collective-permute-done.15.refs_5_ = bf16[384,1024]{1,0:T(8,128)(2,1)} collective-permute-done((bf16[384,1024]{1,0:T(8,128)(2,1)}, bf16[384,1024]{1,0:T(8,128)(2,1)}, u32[]{:S(2)}, u32[]{:S(2)}) %collective-permute-start.15) | collective-permute-done | bytes 786464 | tf_op jit(solution)/shard_map/ppermute | solution.py:375
  210.9 4.5 %total.28.refs_0_.refs_3_ = f32[768,1024]{1,0:T(8,128)} custom-call(f32[768,1024]{1,0:T(8,128)} %total.27.refs_0_.refs_3_.refs_6_, bf16[768,1024]{1,0:T(8,128)(2,1)} %collective-permute-done.13.refs_1_.refs_4_, bf16[384,1024]{1,0:T(8,128)(2,1)} %collective-permute-done.14.refs_2_, f32[768,1024]{1,0:T(8,128)} %total.27.refs_0_.refs_3_.refs_6_, ...), custom_call_target="tpu_custom_call" | custom-call | flops 1 | bytes 1 | tf_op jit(solution)/shard_map/total/pallas_call | solution.py:25
  215.5 4.0 %total.29 = bf16[768,1024]{1,0:T(8,128)(2,1)} custom-call(f32[768,1024]{1,0:T(8,128)} %total.28.refs_0_.refs_3_, bf16[768,1024]{1,0:T(8,128)(2,1)} %collective-permute-done.16.refs_1_, bf16[768,1024]{1,0:T(8,128)(2,1)} %collective-permute-done.17.refs_2_, f32[768,1024]{1,0:T(8,128)} %total.28.refs_0_.refs_3_), custom_call_target="tpu_custom_call" | custom-call | flops 1 | bytes 1 | tf_op jit(solution)/shard_map/total/pallas_call | solution.py:25
  (51 shorter events, 7.6 us)
Async XLA Ops:
  6.5 178.9 %reduce-scatter.2.cloned.1.call-start = ((), (), s32[]{:S(2)}) async-start(), calls=%async_computation.1 | async-start | bytes 4718592 | tf_op jit(solution)/shard_map/reduce_scatter | solution.py:526
  6.5 9.0 %collective-permute-start = (s32[192]{0:T(256)}, s32[192]{0:T(256)S(1)}, u32[]{:S(2)}, u32[]{:S(2)}) collective-permute-start(s32[192]{0:T(256)} %param.7), channel_id=1, source_target_pairs={{0,1},{1,0},{2,3},{3,2},{4,5},{5,4},{6,7},{7,6},{8,9},{9,8},{10,11... | collective-permute-start | bytes 2312 | tf_op jit(solution)/shard_map/ppermute | solution.py:381
  6.5 10.8 %collective-permute-start.1 = (bf16[768,1024]{1,0:T(8,128)(2,1)}, bf16[768,1024]{1,0:T(8,128)(2,1)}, u32[]{:S(2)}, u32[]{:S(2)}) collective-permute-start(bf16[768,1024]{1,0:T(8,128)(2,1)} %bitcast.18), channel_id=1, source_target_pairs={{0,1},{1,0},{2,3},{3,2},{4,5},{5,4},{6,7},{7,6},{8,9},{9,8},{10,11... | collective-permute-start | bytes 4718600 | tf_op jit(solution)/shard_map/ppermute | solution.py:381
  9.0 5.4 %copy-start.6 = (s32[192]{0:T(256)S(1)}, s32[192]{0:T(256)}, u32[]{:S(2)}) copy-start(s32[192]{0:T(256)} %param.7) | copy-start | bytes 2308
  12.8 28.4 %collective-permute-start.3 = (bf16[480,1024]{1,0:T(8,128)(2,1)}, bf16[480,1024]{1,0:T(8,128)(2,1)}, u32[]{:S(2)}, u32[]{:S(2)}) collective-permute-start(bf16[480,1024]{1,0:T(8,128)(2,1)} %products.5.refs_6_), channel_id=1, source_target_pairs={{0,2},{2,0},{4,6},{6,4},{8,10},{10,8},{12,14},{14,12},{1,3},{3,1},... | collective-permute-start | bytes 2949128 | tf_op jit(solution)/shard_map/ppermute | solution.py:368
  30.2 24.3 %collective-permute-start.2 = (bf16[384,1024]{1,0:T(8,128)(2,1)}, bf16[384,1024]{1,0:T(8,128)(2,1)S(1)}, u32[]{:S(2)}, u32[]{:S(2)}) collective-permute-start(bf16[384,1024]{1,0:T(8,128)(2,1)} %products.6.refs_3_), channel_id=1, source_target_pairs={{0,2},{2,0},{4,6},{6,4},{8,10},{10,8},{12,14},{14,12},{1,3},{3,1},... | collective-permute-start | bytes 2359304 | tf_op jit(solution)/shard_map/ppermute | solution.py:368
  39.6 51.2 %collective-permute-start.7 = (bf16[768,1024]{1,0:T(8,128)(2,1)}, bf16[768,1024]{1,0:T(8,128)(2,1)}, u32[]{:S(2)}, u32[]{:S(2)}) collective-permute-start(bf16[768,1024]{1,0:T(8,128)(2,1)} %get-tuple-element.13.refs_2_), channel_id=1, source_target_pairs={{0,2},{2,0},{4,6},{6,4},{8,10},{10,8},{12,14},{14,12},{1,3},{3,1},... | collective-permute-start | bytes 4718600 | tf_op jit(solution)/shard_map/ppermute | solution.py:368
  43.6 26.9 %collective-permute-start.5 = (bf16[480,1024]{1,0:T(8,128)(2,1)}, bf16[480,1024]{1,0:T(8,128)(2,1)}, u32[]{:S(2)}, u32[]{:S(2)}) collective-permute-start(bf16[480,1024]{1,0:T(8,128)(2,1)} %total.15.refs_3_.refs_0_), channel_id=1, source_target_pairs={{0,4},{12,8},{2,6},{14,10},{1,5},{13,9},{3,7},{15,11},{16,20},{28,... | collective-permute-start | bytes 2949128 | tf_op jit(solution)/shard_map/ppermute | solution.py:375
  54.6 0.9 copy-start.4
  57.6 27.8 %collective-permute-start.4 = (bf16[384,1024]{1,0:T(8,128)(2,1)}, bf16[384,1024]{1,0:T(8,128)(2,1)S(1)}, u32[]{:S(2)}, u32[]{:S(2)}) collective-permute-start(bf16[384,1024]{1,0:T(8,128)(2,1)} %total.16.refs_3_.refs_0_.refs_2_.refs_1_), channel_id=1, source_target_pairs={{0,4},{12,8},{2,6},{14,10},{1,5},{13,9},{3,7},{15,11},{16,20},{28,... | collective-permute-start | bytes 2359304 | tf_op jit(solution)/shard_map/ppermute | solution.py:375
  85.4 0.9 copy-start.1
  88.5 19.9 %collective-permute-start.6 = (bf16[384,1024]{1,0:T(8,128)(2,1)}, bf16[384,1024]{1,0:T(8,128)(2,1)S(1)}, u32[]{:S(2)}, u32[]{:S(2)}) collective-permute-start(bf16[384,1024]{1,0:T(8,128)(2,1)} %total.18.refs_2_), channel_id=1, source_target_pairs={{4,8},{8,4},{6,10},{10,6},{5,9},{9,5},{7,11},{11,7},{20,24},{24,20... | collective-permute-start | bytes 2359304 | tf_op jit(solution)/shard_map/ppermute | solution.py:375
  93.1 19.9 %collective-permute-start.9 = (bf16[384,1024]{1,0:T(8,128)(2,1)}, bf16[384,1024]{1,0:T(8,128)(2,1)}, u32[]{:S(2)}, u32[]{:S(2)}) collective-permute-start(bf16[384,1024]{1,0:T(8,128)(2,1)} %total.19.refs_2_.refs_0_), channel_id=1, source_target_pairs={{0,4},{12,8},{2,6},{14,10},{1,5},{13,9},{3,7},{15,11},{16,20},{28,... | collective-permute-start | bytes 2359304 | tf_op jit(solution)/shard_map/ppermute | solution.py:375
  108.4 0.9 copy-start.2
  111.1 4.8 %collective-permute-start.8 = (bf16[96,1024]{1,0:T(8,128)(2,1)}, bf16[96,1024]{1,0:T(8,128)(2,1)S(1)}, u32[]{:S(2)}, u32[]{:S(2)}) collective-permute-start(bf16[96,1024]{1,0:T(8,128)(2,1)} %total.21.refs_2_), channel_id=1, source_target_pairs={{8,12},{4,0},{10,14},{6,2},{9,13},{5,1},{11,15},{7,3},{24,28},{20,... | collective-permute-start | bytes 589832 | tf_op jit(solution)/shard_map/ppermute | solution.py:375
  115.8 0.7 copy-start.5
  127.1 3.4 %copy-start = (bf16[384,1024]{1,0:T(8,128)(2,1)S(1)}, bf16[384,1024]{1,0:T(8,128)(2,1)}, u32[]{:S(2)}) copy-start(bf16[384,1024]{1,0:T(8,128)(2,1)} %total.20.refs_2_.refs_0_.refs_1_) | copy-start | bytes 2359300
  127.1 37.7 %collective-permute-start.10 = (bf16[768,1024]{1,0:T(8,128)(2,1)}, bf16[768,1024]{1,0:T(8,128)(2,1)}, u32[]{:S(2)}, u32[]{:S(2)}) collective-permute-start(bf16[768,1024]{1,0:T(8,128)(2,1)} %hold.2), channel_id=1, source_target_pairs={{0,2},{2,0},{4,6},{6,4},{8,10},{10,8},{12,14},{14,12},{1,3},{3,1},... | collective-permute-start | bytes 4718600 | tf_op jit(solution)/shard_map/ppermute | solution.py:368
  127.7 42.4 %collective-permute-start.11 = (bf16[480,1024]{1,0:T(8,128)(2,1)}, bf16[480,1024]{1,0:T(8,128)(2,1)}, u32[]{:S(2)}, u32[]{:S(2)}) collective-permute-start(bf16[480,1024]{1,0:T(8,128)(2,1)} %total.17.refs_4_), channel_id=1, source_target_pairs={{4,8},{8,4},{6,10},{10,6},{5,9},{9,5},{7,11},{11,7},{20,24},{24,20... | collective-permute-start | bytes 2949128 | tf_op jit(solution)/shard_map/ppermute | solution.py:375
  130.4 37.3 %collective-permute-start.12 = (bf16[384,1024]{1,0:T(8,128)(2,1)S(1)}, bf16[384,1024]{1,0:T(8,128)(2,1)}, u32[]{:S(2)}, u32[]{:S(2)}) collective-permute-start(bf16[384,1024]{1,0:T(8,128)(2,1)S(1)} %copy-done), channel_id=1, source_target_pairs={{0,4},{12,8},{2,6},{14,10},{1,5},{13,9},{3,7},{15,11},{16,20},{28,... | collective-permute-start | bytes 2359304 | tf_op jit(solution)/shard_map/ppermute | solution.py:375
  131.7 70.3 %collective-permute-start.13 = (bf16[768,1024]{1,0:T(8,128)(2,1)}, bf16[768,1024]{1,0:T(8,128)(2,1)}, u32[]{:S(2)}, u32[]{:S(2)}) collective-permute-start(bf16[768,1024]{1,0:T(8,128)(2,1)} %hold.3), channel_id=1, source_target_pairs={{0,2},{2,0},{4,6},{6,4},{8,10},{10,8},{12,14},{14,12},{1,3},{3,1},... | collective-permute-start | bytes 4718600 | tf_op jit(solution)/shard_map/ppermute | solution.py:368
  170.0 9.5 %copy-start.3 = (bf16[384,1024]{1,0:T(8,128)(2,1)S(1)}, bf16[384,1024]{1,0:T(8,128)(2,1)}, u32[]{:S(2)}) copy-start(bf16[384,1024]{1,0:T(8,128)(2,1)} %total.22.refs_4_) | copy-start | bytes 2359300
  172.8 42.7 %collective-permute-start.17 = (bf16[768,1024]{1,0:T(8,128)(2,1)}, bf16[768,1024]{1,0:T(8,128)(2,1)}, u32[]{:S(2)}, u32[]{:S(2)}) collective-permute-start(bf16[768,1024]{1,0:T(8,128)(2,1)} %total.26.refs_2_), channel_id=1, source_target_pairs={{8,12},{4,0},{10,14},{6,2},{9,13},{5,1},{11,15},{7,3},{24,28},{20,... | collective-permute-start | bytes 4718600 | tf_op jit(solution)/shard_map/ppermute | solution.py:375
  178.3 37.2 %collective-permute-start.16 = (bf16[768,1024]{1,0:T(8,128)(2,1)}, bf16[768,1024]{1,0:T(8,128)(2,1)}, u32[]{:S(2)}, u32[]{:S(2)}) collective-permute-start(bf16[768,1024]{1,0:T(8,128)(2,1)} %total.24.refs_2_.refs_0_), channel_id=1, source_target_pairs={{0,4},{12,8},{2,6},{14,10},{1,5},{13,9},{3,7},{15,11},{16,20},{28,... | collective-permute-start | bytes 4718600 | tf_op jit(solution)/shard_map/ppermute | solution.py:375
  179.6 22.5 %collective-permute-start.14 = (bf16[384,1024]{1,0:T(8,128)(2,1)S(1)}, bf16[384,1024]{1,0:T(8,128)(2,1)}, u32[]{:S(2)}, u32[]{:S(2)}) collective-permute-start(bf16[384,1024]{1,0:T(8,128)(2,1)S(1)} %copy-done.3), channel_id=1, source_target_pairs={{4,8},{8,4},{6,10},{10,6},{5,9},{9,5},{7,11},{11,7},{20,24},{24,20... | collective-permute-start | bytes 2359304 | tf_op jit(solution)/shard_map/ppermute | solution.py:375
  181.9 29.0 %collective-permute-start.15 = (bf16[384,1024]{1,0:T(8,128)(2,1)}, bf16[384,1024]{1,0:T(8,128)(2,1)}, u32[]{:S(2)}, u32[]{:S(2)}) collective-permute-start(bf16[384,1024]{1,0:T(8,128)(2,1)} %total.25.refs_4_), channel_id=1, source_target_pairs={{4,8},{8,4},{6,10},{10,6},{5,9},{9,5},{7,11},{11,7},{20,24},{24,20... | collective-permute-start | bytes 2359304 | tf_op jit(solution)/shard_map/ppermute | solution.py:375
Sparse Core Ops, SparseCore 0:
  127.2 12.0 reduce-scatter.1

commit v8 on v6

--- a/solution.py
+++ b/solution.py
@@ -10,7 +10,6 @@
 LANES = 128
 CHUNK = 512
 PARTS = 2
-LOW_WITH = (0, PARTS - 1)
 VMEM = 63 * 2**20
 ANY = pl.BlockSpec(memory_space=pl.ANY)
 
@@ -38,7 +37,7 @@
     )(*operands, *after)
 
 
-def hold(value, after=()):
+def hold(value, after):
     def kernel(value_ref, out_ref):
         pass
 
@@ -48,9 +47,9 @@
     )
 
 
-def products(rows, weight, starts, size, outs, tail=None, chunk=1024, after=()):
+def products(rows, weight, starts, names, size, outs, tail=None, chunk=1024, after=()):
     count, width = rows.shape
-    blocks = starts.shape[0]
+    blocks = len(names)
     chunks = [(at, min(chunk, size - at)) for at in range(0, size, chunk)]
     used = [segment for out in outs for segment in out if segment]
     low = min(first for _, first, _ in used)
@@ -83,7 +82,7 @@
         w_copies = [
             [
                 pltpu.make_async_copy(
-                    weight_ref.at[:, pl.ds(pl.multiple_of(starts_ref[b] + at, LANES), extent)],
+                    weight_ref.at[:, pl.ds(pl.multiple_of(starts_ref[names[b]] + at, LANES), extent)],
                     w.at[b, :, pl.ds(at, extent)],
                     w_sems.at[b, c],
                 )
@@ -372,14 +371,11 @@
     n = lax.axis_size("tensor")
     nz = n // 2
     place = lax.axis_index("tensor")
-    z, y = place // 2, place % 2
     order = line_plan(nz)
-    my_order = jnp.asarray(order)[z]
     out_width = projection_weight.shape[1] // n
 
-    def sum_y(value):
-        pairs = [[t, t + 1] for t in range(0, n, 2)]
-        return lax.psum_scatter(value, "tensor", scatter_dimension=0, axis_index_groups=pairs, tiled=True)
+    def swap_y(value):
+        return lax.ppermute(value, "tensor", [(t, t ^ 1) for t in range(n)])
 
     def hop(value, h):
         pairs = []
@@ -419,13 +415,11 @@
         row_slot = jnp.sum(jnp.where(hit, position[None, :] + 1, 0), axis=1) - 1
         return names, row_slot[:, None]
 
+    blocks = [[(order[t // 2][k] * 2 + side) for side in (1 - t % 2, t % 2) for k in range(nz)] for t in range(n)]
+    starts = jnp.asarray(np.asarray(blocks, np.int32) * out_width)[place]
     low_rows = 2 * (owners * count // 2) * adapter_down_maps.shape[1] // out_width
     even = [(p * count // PARTS, count // PARTS) for p in range(PARTS)]
-    uneven = [(0, count // 2 + low_rows), (count // 2 + low_rows, count // 2 - low_rows)]
-    sums, arrived = {}, {}
-
-    def split(k):
-        return uneven if k == 0 else [(0, count)]
+    away_all, own_all, from_y, sums, arrived = {}, {}, {}, {}, {}
 
     def add_up(span, terms, extra=(), dtype=jnp.bfloat16, into=None):
         low_row, high_row = span[0], span[0] + span[1]
@@ -445,18 +439,26 @@
     def whole(array):
         return [(0, count, array, 0)]
 
-    def multiply(k, p, tail=None, chunk=1024):
-        first, some = split(k)[p]
-        starts = jnp.stack([(my_order[k] * 2 + side) * out_width for side in range(2)])
-        extra = [] if tail is None else [None]
-        outs = [[(0, first, some), *extra, (1, first, some), *extra]]
-        sums[k, p] = sum_y(then(products, rows, projection_weight, starts, out_width, outs, tail, chunk)[0])
+    def multiply(outs, tail=None, chunk=1024):
+        names = sorted({segment[0] for out in outs for segment in out if segment}, key=str)
+        outs = [[segment and (names.index(segment[0]), *segment[1:]) for segment in out] for out in outs]
+        columns = [k + (nz if kind == "own" else 0) for kind, k in names]
+        return then(products, rows, projection_weight, starts, columns, out_width, outs, tail, chunk)
+
+    def all_of(kind, k):
+        return [((kind, k), 0, count)]
+
+    def start_y(k):
+        from_y[k] = swap_y(hold(away_all[k], last[0]) if k else away_all[k])
+
+    def y_parts(k):
+        return whole(from_y[k])
 
     def sum_parts(k):
-        return [(*cut, sums[k, p], 0) for p, cut in enumerate(split(k))]
+        return [(*cut, sums[k, p], 0) for p, cut in enumerate(cut_of(0, k)) if (k, p) in sums]
 
     def cut_of(h, m):
-        return uneven if m == 0 and h <= 1 else [(0, count)]
+        return even if m <= 1 and h <= 1 else [(0, count)]
 
     def arrived_parts(h, m):
         return [(*cut, arrived[h, m, p], 0) for p, cut in enumerate(cut_of(h, m)) if (h, m, p) in arrived]
@@ -464,12 +466,10 @@
     def line(h, m, p):
         k = slot_of(h, m)
         span = cut_of(h, m)[p]
-        low_too = m == 0 and h <= 1 and p == LOW_WITH[1]
         if h == 0:
-            value = then(hold, sums[k, p])
+            value = sums[k, p] = add_up(span, [whole(own_all[k]), y_parts(k)])
         else:
-            extra = [(low_rows, [(sums[k, p], span[1]), (arrived[h - 1, m, p], span[1])])] if low_too else []
-            value = add_up(span, [sum_parts(k), arrived_parts(h - 1, m)], extra)
+            value = add_up(span, [sum_parts(k), arrived_parts(h - 1, m)])
         arrived[h, m, p] = hop(value, h)
 
     def line_order():
@@ -477,46 +477,68 @@
         steps = [(h, m, p) for h in range(nz - 1) for m in range(nz - 1 - h) for p in range(len(cut_of(h, m)))]
         for h, m, p in sorted(steps, key=lambda step: (step[0], step[1], step[2])):
             k = slot_of(h, m)
-            there = (k + 1.0) * count if k or p else 1.0 * cut_of(0, 0)[0][1]
+            there = (k + 1.0) * count
             if h:
                 above = range(len(cut_of(h - 1, m)))
                 there = max(there, max(ready[h - 1, m, q, "end"] for q in above if q == p or len(above) != len(cut_of(h, m))))
             ready[h, m, p] = there
             free[h] = max(there, free.get(h, 0.0)) + cut_of(h, m)[p][1]
             ready[h, m, p, "end"] = free[h]
-        return sorted(steps, key=lambda step: (ready[step], step[0]))
+        return sorted(steps, key=lambda step: (ready[step], step[0] and nz - step[0]))
 
     row_ids = [tenant] + [pass_on(tenant, shift) for shift in range(1, owners)]
     row_sets = [rows] + [pass_on(rows, shift) for shift in range(1, owners)]
-    multiply(0, 0, chunk=512)
+    away_all[0] = multiply([all_of("away", 0)], chunk=512)[0]
+    start_y(0)
     named = [slots(some_ids, me) for some_ids in row_ids]
     names = jnp.concatenate([which for which, _ in named])
     slot_sets = [row_slot for _, row_slot in named]
     low = then(low_rank, row_sets, slot_sets, adapter_down_maps, names, out_width)
-    multiply(*LOW_WITH, low, chunk=512)
-    for k in range(1, nz):
-        multiply(k, 0)
+    bits = [1 << i for i in range(1, 16) if 1 << i < n] + [1]
+
+    def send_low():
+        bit = bits.pop(0)
+        return lax.ppermute(low, "tensor", [(t, t ^ bit) for t in range(n)])
+
+    def add_low(other):
+        return then(total, [(low_rows, [(low, 0), (other, 0)])])
+
+    k = 0
+    while len(bits) > 1:
+        other = send_low()
+        if k < 2:
+            own_all[k] = multiply([all_of("own", k)])[0]
+            k += 1
+        low = add_low(other)
+    other = send_low()
+    away_all[1], *rest = multiply([all_of("away", 1)] + [all_of("own", j) for j in range(k, 2)])
+    own_all.update(zip(range(k, 2), rest))
+    if nz > 2:
+        away_all[2], own_all[2] = multiply([all_of("away", 2), all_of("own", 2)])
+    low = add_low(other)
+    start_y(1)
     for h, m, p in line_order():
         k = slot_of(h, m)
+        if (h, m, p) == (1, 1, 1):
+            last[0] += (arrived[1, 1, 0],)
         line(h, m, p)
-        if (h, k) == (0, 1):
-            low_at = uneven[LOW_WITH[1]][1]
-            pieces = [(sums[LOW_WITH], low_at)]
-            for step in range(nz - 1):
-                if step >= 2:
-                    prefix = then(total, [(low_rows, [pieces[0], pieces[-1]])])
-                    pieces.append((hop(prefix, step), 0))
-                else:
-                    pieces.append((arrived[step, 0, LOW_WITH[1]], low_at))
-            low_sum = then(total, [(low_rows, pieces)])
-            deltas = then(expand, low_sum, slot_sets, adapter_up_maps, names)
+        if h == 0 and p == len(cut_of(h, m)) - 1 and k + 2 < nz:
+            start_y(k + 2)
+        if (h, k, p) == (0, 0, len(cut_of(h, m)) - 1):
+            for j in range(3, nz):
+                away_all[j], own_all[j] = multiply([all_of("away", j), all_of("own", j)])
+            deltas = then(expand, low, slot_sets, adapter_up_maps, names)
             back = [
                 [(*cut, pass_on(deltas[1 + (shift - 1) * PARTS + p], -shift), 0) for p, cut in enumerate(even)]
                 for shift in range(1, owners)
             ]
+        if (h, m, p) == (1, 0, 0) or nz == 2:
+            head = add_up((0, count), [whole(own_all[nz - 1]), whole(deltas[0])] + back, dtype=jnp.float32)
     span = (0, count)
-    head = add_up(span, [whole(deltas[0]), sum_parts(nz - 1)] + back, dtype=jnp.float32)
-    out = add_up(span, [whole(head)] + [arrived_parts(h, nz - 2 - h) for h in range(nz - 1)])
+    early = [arrived_parts(h, nz - 2 - h) for h in range(1, nz - 2)]
+    late = [arrived_parts(h, nz - 2 - h) for h in range(nz - 1) if not 1 <= h < nz - 2]
+    most = add_up(span, [whole(head), y_parts(nz - 1)] + early, dtype=jnp.float32)
+    out = add_up(span, [whole(most)] + late)
     return out.reshape(steps, row_count, out_width)
 
 

time: 245 us -> 185 us (0.76)
  waiting for transfers between devices: 102 us -> 39.6 us
  Pallas kernels: 76.8 us -> 96.6 us
  between operations: 18.6 us -> 0.54 us
  starting transfers between devices: 25.9 us -> 40 us
  local copies, waits for them, and re-layouts: 17.3 us -> 5.77 us
  other arithmetic: 3.93 us -> 1.42 us
    reduce_scatter x5 -> x0, waiting for transfers between devices: 57.9 us -> none  [sum_y(): lax.psum_scatter(value, 'tensor', scatter_dimension=0, axis_index_groups=...]
    ppermute x9 -> x10, waiting for transfers between devices: 41.8 us -> 14 us  [hop(): return lax.ppermute(value, 'tensor', pairs)]
    ppermute x0 -> x7, waiting for transfers between devices: none -> 25.6 us  [the longest x4 22.4 us: swap_y(): return lax.ppermute(value, 'tensor', [(t, t ^ 1) for t in range(n)])]
    pallas_call x19 -> x27, Pallas kernels: 76.8 us -> 96.6 us  [call(): pl.pallas_call(body, grid_spec=pltpu.PrefetchScalarGridSpec(num_scalar_pr...]
    unnamed x16 -> x14, local copies, waits for them, and re-layouts: 14.5 us -> 3.04 us
    ppermute x0 -> x7, starting transfers between devices: none -> 11.4 us  [the longest x4 6.49 us: swap_y(): return lax.ppermute(value, 'tensor', [(t, t ^ 1) for t in range(n)])]
    ppermute x9 -> x10, starting transfers between devices: 24.5 us -> 27.5 us  [hop(): return lax.ppermute(value, 'tensor', pairs)]
    another operation x4 -> x0, other arithmetic: 2.49 us -> none  [multiply(): jnp.stack([(my_order[k] * 2 + side) * out_width for side in range(2)])]
  transfers between devices with their start and end apart: 18 -> 21, of which waited for: 9 -> 7; matrix products, arithmetic and copies ran while one was open for 6% -> 2% of each run, Pallas kernels for 27% -> 50%
where the time goes in v8:
time: 185 us; the launch traced here: 184 us
  Pallas kernels  96.6 us (52%)
  starting transfers between devices  40 us (22%)
  waiting for transfers between devices  39.6 us (21%)
  local copies, waits for them, and re-layouts  5.77 us (3%)
    pallas_call x27, Pallas kernels, call(): pl.pallas_call(body, grid_spec=pltpu.PrefetchScalarGridSpec(num_scalar_pr...  96.6 us
    ppermute x10, starting transfers between devices, hop(): return lax.ppermute(value, 'tensor', pairs)  27.5 us
    ppermute x4, waiting for transfers between devices, swap_y(): return lax.ppermute(value, 'tensor', [(t, t ^ 1) for t in range(n)])  22.4 us
    ppermute x10, waiting for transfers between devices, hop(): return lax.ppermute(value, 'tensor', pairs)  14 us
    ppermute x4, starting transfers between devices, swap_y(): return lax.ppermute(value, 'tensor', [(t, t ^ 1) for t in range(n)])  6.49 us
    ppermute x3, starting transfers between devices, send_low(): return lax.ppermute(low, 'tensor', [(t, t ^ bit) for t in range(n)])  4.88 us
  transfers between devices with their start and end apart: 21, of which 7 were waited for; matrix products, arithmetic and copies ran while one was open for 2% of the time, Pallas kernels for 50%

profile of v8, /device:TPU:0, one launch (start us, length us, event | category | flops | bytes accessed | tf_op | source)
XLA Modules:
  0.0 184.0 jit_solution(9307604149853475555)
XLA Ops:
  0.5 1.2 dynamic-slice_bitcast_fusion.refs_0_
  1.7 5.4 %products.6.refs_6_ = bf16[768,1024]{1,0:T(8,128)(2,1)} custom-call(s32[8]{0:T(128)} %dynamic-slice_bitcast_fusion.refs_0_, bf16[768,1024]{1,0:T(8,128)(2,1)} %bitcast.7, bf16[1024,8192]{1,0:T(8,128)(2,1)} %refs_2_.11), custom_call_target="tpu_custom_call" | custom-call | flops 1 | bytes 1 | tf_op jit(solution)/shard_map/products/pallas_call | solution.py:23
  7.1 3.0 %collective-permute-start.2 = (bf16[768,1024]{1,0:T(8,128)(2,1)}, bf16[768,1024]{1,0:T(8,128)(2,1)}, u32[]{:S(2)}, u32[]{:S(2)}) collective-permute-start(bf16[768,1024]{1,0:T(8,128)(2,1)} %products.6.refs_6_), channel_id=1, source_target_pairs={{0,2},{2,0},{4,6},{6,4},{8,10},{10,8},{12,14},{14,12},{1,3},{3,1},... | collective-permute-start | bytes 4718600 | tf_op jit(solution)/shard_map/ppermute | solution.py:378
  10.5 0.8 copy.14.refs_3_.refs_2_
  13.2 9.3 %low_rank.1.refs_3_.refs_0_ = bf16[96,1024]{1,0:T(8,128)(2,1)} custom-call(s32[32]{0:T(128)} %pad_add_fusion.refs_0_, bf16[768,1024]{1,0:T(8,128)(2,1)} %bitcast.8, bf16[768,1024]{1,0:T(8,128)(2,1)} %collective-permute-done.1.refs_2_, s32[192,1]{1,0:T(8,128)} %copy.14.refs_3_.refs_2_, s32[192,1]{1,0:T(8,128)} %copy.15.refs_4_.refs_3_, ...), custom_call_target="tpu_custom_call" | custom-call | flops 1 | bytes 1 | tf_op jit(solution)/shard_map/low_rank/pallas_call | solution.py:23
  22.5 1.6 collective-permute-start.3
  24.2 5.8 %products.7.refs_2_.refs_0_ = bf16[768,1024]{1,0:T(8,128)(2,1)} custom-call(s32[8]{0:T(128)} %dynamic-slice_bitcast_fusion.refs_0_, bf16[768,1024]{1,0:T(8,128)(2,1)} %bitcast.9, bf16[1024,8192]{1,0:T(8,128)(2,1)} %refs_2_.11, bf16[96,1024]{1,0:T(8,128)(2,1)} %low_rank.1.refs_3_.refs_0_), custom_call_target="tpu_custom_call" | custom-call | flops 1 | bytes 1 | tf_op jit(solution)/shard_map/products/pallas_call | solution.py:23
  30.6 1.8 total.16.refs_3_.refs_0_
  32.4 2.7 %collective-permute-start.4 = (bf16[96,1024]{1,0:T(8,128)(2,1)}, bf16[96,1024]{1,0:T(8,128)(2,1)S(1)}, u32[]{:S(2)}, u32[]{:S(2)}) collective-permute-start(bf16[96,1024]{1,0:T(8,128)(2,1)} %total.16.refs_3_.refs_0_), channel_id=1, source_target_pairs={{0,8},{2,10},{4,12},{6,14},{8,0},{10,2},{12,4},{14,6},{1,9},{3,11}... | collective-permute-start | bytes 589832 | tf_op jit(solution)/shard_map/ppermute | solution.py:501
  35.1 5.7 %products.8.refs_2_.refs_0_ = bf16[768,1024]{1,0:T(8,128)(2,1)} custom-call(s32[8]{0:T(128)} %dynamic-slice_bitcast_fusion.refs_0_, bf16[768,1024]{1,0:T(8,128)(2,1)} %bitcast.10, bf16[1024,8192]{1,0:T(8,128)(2,1)} %refs_2_.11, bf16[96,1024]{1,0:T(8,128)(2,1)} %total.16.refs_3_.refs_0_), custom_call_target="tpu_custom_call" | custom-call | flops 1 | bytes 1 | tf_op jit(solution)/shard_map/products/pallas_call | solution.py:23
  40.7 3.2 %collective-permute-done.4.refs_1_ = bf16[96,1024]{1,0:T(8,128)(2,1)S(1)} collective-permute-done((bf16[96,1024]{1,0:T(8,128)(2,1)}, bf16[96,1024]{1,0:T(8,128)(2,1)S(1)}, u32[]{:S(2)}, u32[]{:S(2)}) %collective-permute-start.4) | collective-permute-done | bytes 196640 | tf_op jit(solution)/shard_map/ppermute | solution.py:501
  44.6 1.8 total.17.refs_3_.refs_0_
  47.0 5.7 %products.9.refs_3_.refs_0_ = bf16[768,1024]{1,0:T(8,128)(2,1)} custom-call(s32[8]{0:T(128)} %dynamic-slice_bitcast_fusion.refs_0_, bf16[768,1024]{1,0:T(8,128)(2,1)} %bitcast.11, bf16[1024,8192]{1,0:T(8,128)(2,1)} %refs_2_.11, bf16[96,1024]{1,0:T(8,128)(2,1)} %total.17.refs_3_.refs_0_), custom_call_target="tpu_custom_call" | custom-call | flops 1 | bytes 1 | tf_op jit(solution)/shard_map/products/pallas_call | solution.py:23
  52.7 7.5 %products.10 = (bf16[768,1024]{1,0:T(8,128)(2,1)}, bf16[768,1024]{1,0:T(8,128)(2,1)}) custom-call(s32[8]{0:T(128)} %dynamic-slice_bitcast_fusion.refs_0_, bf16[768,1024]{1,0:T(8,128)(2,1)} %bitcast.12, bf16[1024,8192]{1,0:T(8,128)(2,1)} %refs_2_.11, bf16[768,1024]{1,0:T(8,128)(2,1)} %products.9.refs_3_.refs_0_), custom_call_target="tpu_custom_call" | custom-call | flops 1 | bytes 1 | tf_op jit(solution)/shard_map/products/pallas_call | solution.py:23
  60.9 1.8 total.18.refs_2_.refs_1_
  62.7 1.6 collective-permute-start.9
  64.3 2.3 %total.19.refs_2_.refs_0_ = bf16[384,1024]{1,0:T(8,128)(2,1)} custom-call(bf16[768,1024]{1,0:T(8,128)(2,1)} %products.7.refs_2_.refs_0_, bf16[768,1024]{1,0:T(8,128)(2,1)} %collective-permute-done.2.refs_1_, bf16[96,1024]{1,0:T(8,128)(2,1)} %total.18.refs_2_.refs_1_), custom_call_target="tpu_custom_call" | custom-call | flops 1 | bytes 1 | tf_op jit(solution)/shard_map/total/pallas_call | solution.py:23
  66.5 2.7 %collective-permute-start.8 = (bf16[384,1024]{1,0:T(8,128)(2,1)}, bf16[384,1024]{1,0:T(8,128)(2,1)}, u32[]{:S(2)}, u32[]{:S(2)}) collective-permute-start(bf16[384,1024]{1,0:T(8,128)(2,1)} %total.19.refs_2_.refs_0_), channel_id=1, source_target_pairs={{0,4},{12,8},{2,6},{14,10},{1,5},{13,9},{3,7},{15,11},{16,20},{28,... | collective-permute-start | bytes 2359304 | tf_op jit(solution)/shard_map/ppermute | solution.py:385
  69.2 2.2 %total.20.refs_3_.refs_0_.refs_1_ = bf16[384,1024]{1,0:T(8,128)(2,1)} custom-call(bf16[768,1024]{1,0:T(8,128)(2,1)} %products.7.refs_2_.refs_0_, bf16[768,1024]{1,0:T(8,128)(2,1)} %collective-permute-done.2.refs_1_, bf16[384,1024]{1,0:T(8,128)(2,1)} %total.19.refs_2_.refs_0_), custom_call_target="tpu_custom_call" | custom-call | flops 1 | bytes 1 | tf_op jit(solution)/shard_map/total/pallas_call | solution.py:23
  71.5 7.5 %products.11 = (bf16[768,1024]{1,0:T(8,128)(2,1)}, bf16[768,1024]{1,0:T(8,128)(2,1)}) custom-call(s32[8]{0:T(128)} %dynamic-slice_bitcast_fusion.refs_0_, bf16[768,1024]{1,0:T(8,128)(2,1)} %bitcast.13, bf16[1024,8192]{1,0:T(8,128)(2,1)} %refs_2_.11, bf16[384,1024]{1,0:T(8,128)(2,1)} %total.20.refs_3_.refs_0_.refs_1_), custom_call_target="tpu_custom_call" | custom-call | flops 1 | bytes 1 | tf_op jit(solution)/shard_map/products/pallas_call | solution.py:23
  78.9 8.5 %expand.1 = (bf16[768,1024]{1,0:T(8,128)(2,1)}, bf16[384,1024]{1,0:T(8,128)(2,1)}, bf16[384,1024]{1,0:T(8,128)(2,1)}) custom-call(s32[32]{0:T(128)} %pad_add_fusion.refs_0_, bf16[96,1024]{1,0:T(8,128)(2,1)} %total.18.refs_2_.refs_1_, s32[192,1]{1,0:T(8,128)} %copy.14.refs_3_.refs_2_, s32[192,1]{1,0:T(8,128)} %copy.15.refs_4_.refs_3_, ...), custom_call_target="tpu_custom_call" | custom-call | flops 1 | bytes 1 | tf_op jit(solution)/shard_map/expand/pallas_call | solution.py:23
  88.7 2.2 %collective-permute-start.12 = (bf16[384,1024]{1,0:T(8,128)(2,1)S(1)}, bf16[384,1024]{1,0:T(8,128)(2,1)}, u32[]{:S(2)}, u32[]{:S(2)}) collective-permute-start(bf16[384,1024]{1,0:T(8,128)(2,1)S(1)} %copy-done), channel_id=1, source_target_pairs={{0,4},{12,8},{2,6},{14,10},{1,5},{13,9},{3,7},{15,11},{16,20},{28,... | collective-permute-start | bytes 2359304 | tf_op jit(solution)/shard_map/ppermute | solution.py:385
  90.8 2.2 %total.21.refs_6_ = bf16[384,1024]{1,0:T(8,128)(2,1)} custom-call(bf16[384,1024]{1,0:T(8,128)(2,1)} %total.19.refs_2_.refs_0_, bf16[384,1024]{1,0:T(8,128)(2,1)} %collective-permute-done.8.refs_1_, bf16[768,1024]{1,0:T(8,128)(2,1)} %get-tuple-element.15.refs_2_.refs_1_.refs_4_), custom_call_target="tpu_custom_call" | custom-call | flops 1 | bytes 1 | tf_op jit(solution)/shard_map/total/pallas_call | solution.py:23
  93.1 3.6 %total.22.refs_2_.refs_0_.refs_3_ = f32[768,1024]{1,0:T(8,128)} custom-call(bf16[768,1024]{1,0:T(8,128)(2,1)} %get-tuple-element.13.refs_0_.refs_3_, bf16[768,1024]{1,0:T(8,128)(2,1)} %get-tuple-element.15.refs_2_.refs_1_.refs_4_, bf16[384,1024]{1,0:T(8,128)(2,1)} %collective-permute-done.6.refs_2_, bf16[768,1024]{1,0:T(8,128)(2,1)} %get-tuple-element.13.refs_0_.refs_3_, ...), custom_call_target="tpu_custom_call" | custom-call | flops 1 | bytes 1 | tf_op jit(solution)/shard_map/total/pallas_call | solution.py:23
  96.8 3.6 %collective-permute-done.9.refs_1_ = bf16[768,1024]{1,0:T(8,128)(2,1)} collective-permute-done((bf16[768,1024]{1,0:T(8,128)(2,1)}, bf16[768,1024]{1,0:T(8,128)(2,1)}, u32[]{:S(2)}, u32[]{:S(2)}) %collective-permute-start.9) | collective-permute-done | bytes 1572896 | tf_op jit(solution)/shard_map/ppermute | solution.py:378
  100.4 2.2 %total.23.refs_2_.refs_0_ = bf16[384,1024]{1,0:T(8,128)(2,1)} custom-call(bf16[768,1024]{1,0:T(8,128)(2,1)} %products.8.refs_2_.refs_0_, bf16[768,1024]{1,0:T(8,128)(2,1)} %collective-permute-done.9.refs_1_, f32[768,1024]{1,0:T(8,128)} %total.22.refs_2_.refs_0_.refs_3_), custom_call_target="tpu_custom_call" | custom-call | flops 1 | bytes 1 | tf_op jit(solution)/shard_map/total/pallas_call | solution.py:23
  102.6 2.7 %collective-permute-start.11 = (bf16[384,1024]{1,0:T(8,128)(2,1)}, bf16[384,1024]{1,0:T(8,128)(2,1)}, u32[]{:S(2)}, u32[]{:S(2)}) collective-permute-start(bf16[384,1024]{1,0:T(8,128)(2,1)} %total.23.refs_2_.refs_0_), channel_id=1, source_target_pairs={{0,4},{12,8},{2,6},{14,10},{1,5},{13,9},{3,7},{15,11},{16,20},{28,... | collective-permute-start | bytes 2359304 | tf_op jit(solution)/shard_map/ppermute | solution.py:385
  105.3 1.5 collective-permute-start.16
  106.8 2.3 %total.24.refs_1_.refs_2_.refs_0_ = bf16[384,1024]{1,0:T(8,128)(2,1)} custom-call(bf16[768,1024]{1,0:T(8,128)(2,1)} %products.8.refs_2_.refs_0_, bf16[768,1024]{1,0:T(8,128)(2,1)} %collective-permute-done.9.refs_1_, bf16[384,1024]{1,0:T(8,128)(2,1)} %total.23.refs_2_.refs_0_), custom_call_target="tpu_custom_call" | custom-call | flops 1 | bytes 1 | tf_op jit(solution)/shard_map/total/pallas_call | solution.py:23
  109.1 2.3 %total.25.refs_2_ = bf16[384,1024]{1,0:T(8,128)(2,1)} custom-call(bf16[384,1024]{1,0:T(8,128)(2,1)} %total.20.refs_3_.refs_0_.refs_1_, bf16[384,1024]{1,0:T(8,128)(2,1)} %collective-permute-done.12.refs_1_, bf16[384,1024]{1,0:T(8,128)(2,1)} %total.24.refs_1_.refs_2_.refs_0_), custom_call_target="tpu_custom_call" | custom-call | flops 1 | bytes 1 | tf_op jit(solution)/shard_map/total/pallas_call | solution.py:23
  111.5 1.6 collective-permute-start.17
  113.1 5.7 %collective-permute-start.14 = (bf16[384,1024]{1,0:T(8,128)(2,1)S(1)}, bf16[384,1024]{1,0:T(8,128)(2,1)}, u32[]{:S(2)}, u32[]{:S(2)}) collective-permute-start(bf16[384,1024]{1,0:T(8,128)(2,1)S(1)} %copy-done.1), channel_id=1, source_target_pairs={{0,4},{12,8},{2,6},{14,10},{1,5},{13,9},{3,7},{15,11},{16,20},{28,... | collective-permute-start | bytes 2359304 | tf_op jit(solution)/shard_map/ppermute | solution.py:385
  118.7 6.1 %collective-permute-done.11.refs_1_ = bf16[384,1024]{1,0:T(8,128)(2,1)} collective-permute-done((bf16[384,1024]{1,0:T(8,128)(2,1)}, bf16[384,1024]{1,0:T(8,128)(2,1)}, u32[]{:S(2)}, u32[]{:S(2)}) %collective-permute-start.11) | collective-permute-done | bytes 786464 | tf_op jit(solution)/shard_map/ppermute | solution.py:385
  124.8 1.4 collective-permute-start.10
  126.2 2.2 %total.26.refs_2_ = bf16[384,1024]{1,0:T(8,128)(2,1)} custom-call(bf16[384,1024]{1,0:T(8,128)(2,1)} %total.23.refs_2_.refs_0_, bf16[384,1024]{1,0:T(8,128)(2,1)} %collective-permute-done.11.refs_1_, bf16[384,1024]{1,0:T(8,128)(2,1)} %total.25.refs_2_), custom_call_target="tpu_custom_call" | custom-call | flops 1 | bytes 1 | tf_op jit(solution)/shard_map/total/pallas_call | solution.py:23
  128.5 5.6 %collective-permute-done.15.refs_1_ = bf16[768,1024]{1,0:T(8,128)(2,1)} collective-permute-done((bf16[768,1024]{1,0:T(8,128)(2,1)}, bf16[768,1024]{1,0:T(8,128)(2,1)}, u32[]{:S(2)}, u32[]{:S(2)}) %collective-permute-start.15) | collective-permute-done | bytes 1572896 | tf_op jit(solution)/shard_map/ppermute | solution.py:378
  134.1 1.6 collective-permute-start.13
  135.6 3.0 %total.27.refs_0_.refs_2_.refs_4_ = bf16[768,1024]{1,0:T(8,128)(2,1)} custom-call(bf16[768,1024]{1,0:T(8,128)(2,1)} %get-tuple-element.18.refs_0_, bf16[768,1024]{1,0:T(8,128)(2,1)} %collective-permute-done.15.refs_1_, bf16[384,1024]{1,0:T(8,128)(2,1)} %total.26.refs_2_), custom_call_target="tpu_custom_call" | custom-call | flops 1 | bytes 1 | tf_op jit(solution)/shard_map/total/pallas_call | solution.py:23
  138.6 2.8 %total.28.refs_2_ = bf16[768,1024]{1,0:T(8,128)(2,1)} custom-call(bf16[768,1024]{1,0:T(8,128)(2,1)} %total.27.refs_0_.refs_2_.refs_4_, bf16[384,1024]{1,0:T(8,128)(2,1)} %collective-permute-done.16.refs_1_, bf16[768,1024]{1,0:T(8,128)(2,1)} %total.27.refs_0_.refs_2_.refs_4_, bf16[384,1024]{1,0:T(8,128)(2,1)} %collective-permute-done.17.refs_3_, ...), custom_call_target="tpu_custom_call" | custom-call | flops 1 | bytes 1 | tf_op jit(solution)/shard_map/total/pallas_call | solution.py:23
  141.4 1.3 collective-permute-start.20
  142.7 7.6 %collective-permute-start.19 = (bf16[768,1024]{1,0:T(8,128)(2,1)}, bf16[768,1024]{1,0:T(8,128)(2,1)}, u32[]{:S(2)}, u32[]{:S(2)}) collective-permute-start(bf16[768,1024]{1,0:T(8,128)(2,1)} %total.27.refs_0_.refs_2_.refs_4_), channel_id=1, source_target_pairs={{0,4},{12,8},{2,6},{14,10},{1,5},{13,9},{3,7},{15,11},{16,20},{28,... | collective-permute-start | bytes 4718600 | tf_op jit(solution)/shard_map/ppermute | solution.py:385
  150.3 2.2 %total.29.refs_6_ = bf16[384,1024]{1,0:T(8,128)(2,1)} custom-call(bf16[384,1024]{1,0:T(8,128)(2,1)} %total.24.refs_1_.refs_2_.refs_0_, bf16[384,1024]{1,0:T(8,128)(2,1)} %collective-permute-done.14.refs_1_, bf16[768,1024]{1,0:T(8,128)(2,1)} %total.28.refs_2_, bf16[384,1024]{1,0:T(8,128)(2,1)} %collective-permute-done.13.refs_3_.refs_2_), custom_call_target="tpu_custom_call" | custom-call | flops 1 | bytes 1 | tf_op jit(solution)/shard_map/total/pallas_call | solution.py:23
  153.3 13.2 %collective-permute-done.10.refs_1_.refs_4_ = bf16[768,1024]{1,0:T(8,128)(2,1)} collective-permute-done((bf16[768,1024]{1,0:T(8,128)(2,1)}, bf16[768,1024]{1,0:T(8,128)(2,1)}, u32[]{:S(2)}, u32[]{:S(2)}) %collective-permute-start.10) | collective-permute-done | bytes 1572896 | tf_op jit(solution)/shard_map/ppermute | solution.py:378
  166.5 0.9 copy-done.2
  167.4 4.5 %total.30.refs_0_.refs_3_ = f32[768,1024]{1,0:T(8,128)} custom-call(f32[768,1024]{1,0:T(8,128)} %total.22.refs_2_.refs_0_.refs_3_, bf16[768,1024]{1,0:T(8,128)(2,1)} %collective-permute-done.10.refs_1_.refs_4_, bf16[384,1024]{1,0:T(8,128)(2,1)} %collective-permute-done.13.refs_3_.refs_2_, f32[768,1024]{1,0:T(8,128)} %total.22.refs_2_.refs_0_.refs_3_, ...), custom_call_target="tpu_custom_call" | custom-call | flops 1 | bytes 1 | tf_op jit(solution)/shard_map/total/pallas_call | solution.py:23
  171.9 5.6 %collective-permute-done.20.refs_2_ = bf16[768,1024]{1,0:T(8,128)(2,1)} collective-permute-done((bf16[768,1024]{1,0:T(8,128)(2,1)}, bf16[768,1024]{1,0:T(8,128)(2,1)}, u32[]{:S(2)}, u32[]{:S(2)}) %collective-permute-start.20) | collective-permute-done | bytes 1572896 | tf_op jit(solution)/shard_map/ppermute | solution.py:385
  177.5 2.3 %collective-permute-done.19.refs_1_ = bf16[768,1024]{1,0:T(8,128)(2,1)} collective-permute-done((bf16[768,1024]{1,0:T(8,128)(2,1)}, bf16[768,1024]{1,0:T(8,128)(2,1)}, u32[]{:S(2)}, u32[]{:S(2)}) %collective-permute-start.19) | collective-permute-done | bytes 1572896 | tf_op jit(solution)/shard_map/ppermute | solution.py:385
  179.8 4.0 %total.31 = bf16[768,1024]{1,0:T(8,128)(2,1)} custom-call(f32[768,1024]{1,0:T(8,128)} %total.30.refs_0_.refs_3_, bf16[768,1024]{1,0:T(8,128)(2,1)} %collective-permute-done.19.refs_1_, bf16[768,1024]{1,0:T(8,128)(2,1)} %collective-permute-done.20.refs_2_, f32[768,1024]{1,0:T(8,128)} %total.30.refs_0_.refs_3_), custom_call_target="tpu_custom_call" | custom-call | flops 1 | bytes 1 | tf_op jit(solution)/shard_map/total/pallas_call | solution.py:23
  (52 shorter events, 7.3 us)
Async XLA Ops:
  0.0 11.3 %collective-permute-start = (s32[192]{0:T(256)}, s32[192]{0:T(256)S(1)}, u32[]{:S(2)}, u32[]{:S(2)}) collective-permute-start(s32[192]{0:T(256)} %param.7), channel_id=1, source_target_pairs={{0,1},{1,0},{2,3},{3,2},{4,5},{5,4},{6,7},{7,6},{8,9},{9,8},{10,11... | collective-permute-start | bytes 2312 | tf_op jit(solution)/shard_map/ppermute | solution.py:391
  0.5 12.7 %collective-permute-start.1 = (bf16[768,1024]{1,0:T(8,128)(2,1)}, bf16[768,1024]{1,0:T(8,128)(2,1)}, u32[]{:S(2)}, u32[]{:S(2)}) collective-permute-start(bf16[768,1024]{1,0:T(8,128)(2,1)} %bitcast.6), channel_id=1, source_target_pairs={{0,1},{1,0},{2,3},{3,2},{4,5},{5,4},{6,7},{7,6},{8,9},{9,8},{10,11... | collective-permute-start | bytes 4718600 | tf_op jit(solution)/shard_map/ppermute | solution.py:391
  1.7 8.5 %copy-start.6 = (s32[192]{0:T(256)S(1)}, s32[192]{0:T(256)}, u32[]{:S(2)}) copy-start(s32[192]{0:T(256)} %param.7) | copy-start | bytes 2308
  7.1 57.1 %collective-permute-start.2 = (bf16[768,1024]{1,0:T(8,128)(2,1)}, bf16[768,1024]{1,0:T(8,128)(2,1)}, u32[]{:S(2)}, u32[]{:S(2)}) collective-permute-start(bf16[768,1024]{1,0:T(8,128)(2,1)} %products.6.refs_6_), channel_id=1, source_target_pairs={{0,2},{2,0},{4,6},{6,4},{8,10},{10,8},{12,14},{14,12},{1,3},{3,1},... | collective-permute-start | bytes 4718600 | tf_op jit(solution)/shard_map/ppermute | solution.py:378
  22.5 7.4 %collective-permute-start.3 = (bf16[96,1024]{1,0:T(8,128)(2,1)}, bf16[96,1024]{1,0:T(8,128)(2,1)S(1)}, u32[]{:S(2)}, u32[]{:S(2)}) collective-permute-start(bf16[96,1024]{1,0:T(8,128)(2,1)} %low_rank.1.refs_3_.refs_0_), channel_id=1, source_target_pairs={{0,4},{2,6},{4,0},{6,2},{8,12},{10,14},{12,8},{14,10},{1,5},{3,7},... | collective-permute-start | bytes 589832 | tf_op jit(solution)/shard_map/ppermute | solution.py:501
  29.9 0.7 copy-start.4
  32.4 11.5 %collective-permute-start.4 = (bf16[96,1024]{1,0:T(8,128)(2,1)}, bf16[96,1024]{1,0:T(8,128)(2,1)S(1)}, u32[]{:S(2)}, u32[]{:S(2)}) collective-permute-start(bf16[96,1024]{1,0:T(8,128)(2,1)} %total.16.refs_3_.refs_0_), channel_id=1, source_target_pairs={{0,8},{2,10},{4,12},{6,14},{8,0},{10,2},{12,4},{14,6},{1,9},{3,11}... | collective-permute-start | bytes 589832 | tf_op jit(solution)/shard_map/ppermute | solution.py:501
  43.9 0.7 copy-start.5
  46.4 13.8 %collective-permute-start.5 = (bf16[96,1024]{1,0:T(8,128)(2,1)}, bf16[96,1024]{1,0:T(8,128)(2,1)S(1)}, u32[]{:S(2)}, u32[]{:S(2)}) collective-permute-start(bf16[96,1024]{1,0:T(8,128)(2,1)} %total.17.refs_3_.refs_0_), channel_id=1, source_target_pairs={{0,2},{2,0},{4,6},{6,4},{8,10},{10,8},{12,14},{14,12},{1,3},{3,1},... | collective-permute-start | bytes 589832 | tf_op jit(solution)/shard_map/ppermute | solution.py:501
  60.2 0.7 copy-start.3
  62.7 37.7 %collective-permute-start.9 = (bf16[768,1024]{1,0:T(8,128)(2,1)}, bf16[768,1024]{1,0:T(8,128)(2,1)}, u32[]{:S(2)}, u32[]{:S(2)}) collective-permute-start(bf16[768,1024]{1,0:T(8,128)(2,1)} %hold.3), channel_id=1, source_target_pairs={{0,2},{2,0},{4,6},{6,4},{8,10},{10,8},{12,14},{14,12},{1,3},{3,1},... | collective-permute-start | bytes 4718600 | tf_op jit(solution)/shard_map/ppermute | solution.py:378
  66.5 22.0 %collective-permute-start.8 = (bf16[384,1024]{1,0:T(8,128)(2,1)}, bf16[384,1024]{1,0:T(8,128)(2,1)}, u32[]{:S(2)}, u32[]{:S(2)}) collective-permute-start(bf16[384,1024]{1,0:T(8,128)(2,1)} %total.19.refs_2_.refs_0_), channel_id=1, source_target_pairs={{0,4},{12,8},{2,6},{14,10},{1,5},{13,9},{3,7},{15,11},{16,20},{28,... | collective-permute-start | bytes 2359304 | tf_op jit(solution)/shard_map/ppermute | solution.py:385
  87.4 5.7 %collective-permute-start.6 = (bf16[384,1024]{1,0:T(8,128)(2,1)}, bf16[384,1024]{1,0:T(8,128)(2,1)}, u32[]{:S(2)}, u32[]{:S(2)}) collective-permute-start(bf16[384,1024]{1,0:T(8,128)(2,1)} %get-tuple-element.16), channel_id=1, source_target_pairs={{0,1},{1,0},{2,3},{3,2},{4,5},{5,4},{6,7},{7,6},{8,9},{9,8},{10,11... | collective-permute-start | bytes 2359304 | tf_op jit(solution)/shard_map/ppermute | solution.py:391
  87.5 1.1 copy-start
  87.5 5.6 %collective-permute-start.7 = (bf16[384,1024]{1,0:T(8,128)(2,1)}, bf16[384,1024]{1,0:T(8,128)(2,1)}, u32[]{:S(2)}, u32[]{:S(2)}) collective-permute-start(bf16[384,1024]{1,0:T(8,128)(2,1)} %get-tuple-element.17), channel_id=1, source_target_pairs={{0,1},{1,0},{2,3},{3,2},{4,5},{5,4},{6,7},{7,6},{8,9},{9,8},{10,11... | collective-permute-start | bytes 2359304 | tf_op jit(solution)/shard_map/ppermute | solution.py:391
  88.0 46.0 %collective-permute-start.15 = (bf16[768,1024]{1,0:T(8,128)(2,1)}, bf16[768,1024]{1,0:T(8,128)(2,1)}, u32[]{:S(2)}, u32[]{:S(2)}) collective-permute-start(bf16[768,1024]{1,0:T(8,128)(2,1)} %hold.5), channel_id=1, source_target_pairs={{0,2},{2,0},{4,6},{6,4},{8,10},{10,8},{12,14},{14,12},{1,3},{3,1},... | collective-permute-start | bytes 4718600 | tf_op jit(solution)/shard_map/ppermute | solution.py:378
  88.7 20.5 %collective-permute-start.12 = (bf16[384,1024]{1,0:T(8,128)(2,1)S(1)}, bf16[384,1024]{1,0:T(8,128)(2,1)}, u32[]{:S(2)}, u32[]{:S(2)}) collective-permute-start(bf16[384,1024]{1,0:T(8,128)(2,1)S(1)} %copy-done), channel_id=1, source_target_pairs={{0,4},{12,8},{2,6},{14,10},{1,5},{13,9},{3,7},{15,11},{16,20},{28,... | collective-permute-start | bytes 2359304 | tf_op jit(solution)/shard_map/ppermute | solution.py:385
  102.6 22.2 %collective-permute-start.11 = (bf16[384,1024]{1,0:T(8,128)(2,1)}, bf16[384,1024]{1,0:T(8,128)(2,1)}, u32[]{:S(2)}, u32[]{:S(2)}) collective-permute-start(bf16[384,1024]{1,0:T(8,128)(2,1)} %total.23.refs_2_.refs_0_), channel_id=1, source_target_pairs={{0,4},{12,8},{2,6},{14,10},{1,5},{13,9},{3,7},{15,11},{16,20},{28,... | collective-permute-start | bytes 2359304 | tf_op jit(solution)/shard_map/ppermute | solution.py:385
  105.3 33.3 %collective-permute-start.16 = (bf16[384,1024]{1,0:T(8,128)(2,1)}, bf16[384,1024]{1,0:T(8,128)(2,1)}, u32[]{:S(2)}, u32[]{:S(2)}) collective-permute-start(bf16[384,1024]{1,0:T(8,128)(2,1)} %total.21.refs_6_), channel_id=1, source_target_pairs={{4,8},{8,4},{6,10},{10,6},{5,9},{9,5},{7,11},{11,7},{20,24},{24,20... | collective-permute-start | bytes 2359304 | tf_op jit(solution)/shard_map/ppermute | solution.py:385
  109.1 3.9 %copy-start.1 = (bf16[384,1024]{1,0:T(8,128)(2,1)S(1)}, bf16[384,1024]{1,0:T(8,128)(2,1)}, u32[]{:S(2)}) copy-start(bf16[384,1024]{1,0:T(8,128)(2,1)} %total.24.refs_1_.refs_2_.refs_0_) | copy-start | bytes 2359300
  111.5 27.1 %collective-permute-start.17 = (bf16[384,1024]{1,0:T(8,128)(2,1)}, bf16[384,1024]{1,0:T(8,128)(2,1)}, u32[]{:S(2)}, u32[]{:S(2)}) collective-permute-start(bf16[384,1024]{1,0:T(8,128)(2,1)} %total.25.refs_2_), channel_id=1, source_target_pairs={{4,8},{8,4},{6,10},{10,6},{5,9},{9,5},{7,11},{11,7},{20,24},{24,20... | collective-permute-start | bytes 2359304 | tf_op jit(solution)/shard_map/ppermute | solution.py:385
  113.1 37.3 %collective-permute-start.14 = (bf16[384,1024]{1,0:T(8,128)(2,1)S(1)}, bf16[384,1024]{1,0:T(8,128)(2,1)}, u32[]{:S(2)}, u32[]{:S(2)}) collective-permute-start(bf16[384,1024]{1,0:T(8,128)(2,1)S(1)} %copy-done.1), channel_id=1, source_target_pairs={{0,4},{12,8},{2,6},{14,10},{1,5},{13,9},{3,7},{15,11},{16,20},{28,... | collective-permute-start | bytes 2359304 | tf_op jit(solution)/shard_map/ppermute | solution.py:385
  124.8 41.7 %collective-permute-start.10 = (bf16[768,1024]{1,0:T(8,128)(2,1)}, bf16[768,1024]{1,0:T(8,128)(2,1)}, u32[]{:S(2)}, u32[]{:S(2)}) collective-permute-start(bf16[768,1024]{1,0:T(8,128)(2,1)} %hold.4), channel_id=1, source_target_pairs={{0,2},{2,0},{4,6},{6,4},{8,10},{10,8},{12,14},{14,12},{1,3},{3,1},... | collective-permute-start | bytes 4718600 | tf_op jit(solution)/shard_map/ppermute | solution.py:378
  134.1 16.3 %collective-permute-start.13 = (bf16[384,1024]{1,0:T(8,128)(2,1)}, bf16[384,1024]{1,0:T(8,128)(2,1)}, u32[]{:S(2)}, u32[]{:S(2)}) collective-permute-start(bf16[384,1024]{1,0:T(8,128)(2,1)} %total.26.refs_2_), channel_id=1, source_target_pairs={{4,8},{8,4},{6,10},{10,6},{5,9},{9,5},{7,11},{11,7},{20,24},{24,20... | collective-permute-start | bytes 2359304 | tf_op jit(solution)/shard_map/ppermute | solution.py:385
  141.4 36.1 %collective-permute-start.20 = (bf16[768,1024]{1,0:T(8,128)(2,1)}, bf16[768,1024]{1,0:T(8,128)(2,1)}, u32[]{:S(2)}, u32[]{:S(2)}) collective-permute-start(bf16[768,1024]{1,0:T(8,128)(2,1)} %total.28.refs_2_), channel_id=1, source_target_pairs={{8,12},{4,0},{10,14},{6,2},{9,13},{5,1},{11,15},{7,3},{24,28},{20,... | collective-permute-start | bytes 4718600 | tf_op jit(solution)/shard_map/ppermute | solution.py:385
  142.7 37.1 %collective-permute-start.19 = (bf16[768,1024]{1,0:T(8,128)(2,1)}, bf16[768,1024]{1,0:T(8,128)(2,1)}, u32[]{:S(2)}, u32[]{:S(2)}) collective-permute-start(bf16[768,1024]{1,0:T(8,128)(2,1)} %total.27.refs_0_.refs_2_.refs_4_), channel_id=1, source_target_pairs={{0,4},{12,8},{2,6},{14,10},{1,5},{13,9},{3,7},{15,11},{16,20},{28,... | collective-permute-start | bytes 4718600 | tf_op jit(solution)/shard_map/ppermute | solution.py:385
  152.6 13.9 %collective-permute-start.18 = (bf16[384,1024]{1,0:T(8,128)(2,1)}, bf16[384,1024]{1,0:T(8,128)(2,1)S(1)}, u32[]{:S(2)}, u32[]{:S(2)}) collective-permute-start(bf16[384,1024]{1,0:T(8,128)(2,1)} %total.29.refs_6_), channel_id=1, source_target_pairs={{4,8},{8,4},{6,10},{10,6},{5,9},{9,5},{7,11},{11,7},{20,24},{24,20... | collective-permute-start | bytes 2359304 | tf_op jit(solution)/shard_map/ppermute | solution.py:385
  166.5 0.9 copy-start.2

commit v9 on v5

--- a/solution.py
+++ b/solution.py
@@ -11,6 +11,7 @@
 CHUNK = 512
 PARTS = 2
 LOW_WITH = (0, PARTS - 1)
+HEAD_AFTER = (2, 0)
 VMEM = 50 * 2**20
 ANY = pl.BlockSpec(memory_space=pl.ANY)
 
@@ -48,9 +49,9 @@
     )
 
 
-def products(rows, weight, starts, size, outs, tail=None, chunk=1024, after=()):
+def products(rows, weight, starts, names, size, outs, tail=None, chunk=1024, after=()):
     count, width = rows.shape
-    blocks = starts.shape[0]
+    blocks = len(names)
     chunks = [(at, min(chunk, size - at)) for at in range(0, size, chunk)]
     low = min(first for _, first, _ in outs)
     high = max(first + some for _, first, some in outs)
@@ -74,7 +75,7 @@
         w_copies = [
             [
                 pltpu.make_async_copy(
-                    weight_ref.at[:, pl.ds(pl.multiple_of(starts_ref[b] + at, LANES), extent)],
+                    weight_ref.at[:, pl.ds(pl.multiple_of(starts_ref[names[b]] + at, LANES), extent)],
                     w.at[b, :, pl.ds(at, extent)],
                     w_sems.at[b, c],
                 )
@@ -363,9 +364,7 @@
     n = lax.axis_size("tensor")
     nz = n // 2
     place = lax.axis_index("tensor")
-    z, y = place // 2, place % 2
     order = line_plan(nz)
-    my_order = jnp.asarray(order)[z]
     out_width = projection_weight.shape[1] // n
 
     def swap_y(value):
@@ -409,8 +408,8 @@
         row_slot = jnp.sum(jnp.where(hit, position[None, :] + 1, 0), axis=1) - 1
         return names, row_slot[:, None]
 
-    away = [(my_order[k] * 2 + 1 - y) * out_width for k in range(nz)]
-    own = [(my_order[k] * 2 + y) * out_width for k in range(nz)]
+    blocks = [[(order[t // 2][k] * 2 + side) for side in (1 - t % 2, t % 2) for k in range(nz)] for t in range(n)]
+    starts = jnp.asarray(np.asarray(blocks, np.int32) * out_width)[place]
     low_rows = 2 * (owners * count // 2) * adapter_down_maps.shape[1] // out_width
     even = [(p * count // PARTS, count // PARTS) for p in range(PARTS)]
     uneven = [(0, count // 2 + low_rows), (count // 2 + low_rows, count // 2 - low_rows)]
@@ -439,10 +438,10 @@
 
     def multiply(aways, owns, tail=None, chunk=1024):
         ks = sorted({k for k, _ in aways})
-        starts = jnp.stack([away[k] for k in ks] + [own[k] for k in owns])
+        names = ks + [nz + k for k in owns]
         outs = [(ks.index(k), *split(k)[p]) for k, p in aways]
         outs += [(len(ks) + i, 0, count) for i in range(len(owns))]
-        done = then(products, rows, projection_weight, starts, out_width, outs, tail, chunk)
+        done = then(products, rows, projection_weight, starts, names, out_width, outs, tail, chunk)
         away_part.update(zip(aways, done))
         own_all.update(zip(owns, done[len(aways) :]))
 
@@ -457,7 +456,9 @@
         return [(*cut, sums[k, p], 0) for p, cut in enumerate(cut_of(0, k)) if (k, p) in sums]
 
     def cut_of(h, m):
-        return uneven if m == 0 and h <= 1 else [(0, count)]
+        if m == 0 and h <= 1:
+            return uneven
+        return even if m == 1 else [(0, count)]
 
     def arrived_parts(h, m):
         return [(*cut, arrived[h, m, p], 0) for p, cut in enumerate(cut_of(h, m)) if (h, m, p) in arrived]
@@ -502,6 +503,8 @@
     start_y(1, 0)
     for h, m, p in line_order():
         k = slot_of(h, m)
+        if (h, m, p) == (1, 1, 1):
+            last[0] += (arrived[1, 1, 0],)
         line(h, m, p)
         if h == 0:
             if k == 0 and p == 0:
@@ -510,9 +513,9 @@
                 if nz > 2:
                     start_y(2, 0, last[0])
                 multiply([(j, 0) for j in range(3, nz)], range(2, nz))
-            elif p == len(cut_of(h, m)) - 1 and k + 2 < nz:
-                start_y(k + 2, 0, last[0])
-        if (h, k) == (0, 1):
+            elif p == len(cut_of(h, m)) - 1 and 1 < k < nz - 1:
+                start_y(k + 1, 0, last[0])
+        if (h, k, p) == (0, 1, len(cut_of(h, m)) - 1):
             low_at = uneven[LOW_WITH[1]][1]
             pieces = [(sums[LOW_WITH], low_at)]
             for step in range(nz - 1):
@@ -521,15 +524,20 @@
                     pieces.append((hop(prefix, step), 0))
                 else:
                     pieces.append((arrived[step, 0, LOW_WITH[1]], low_at))
+        if (h, m, p) == (1, 1, 0):
             low_sum = then(total, [(low_rows, pieces)])
             deltas = then(expand, low_sum, slot_sets, adapter_up_maps, names)
             back = [
                 [(*cut, pass_on(deltas[1 + (shift - 1) * PARTS + p], -shift), 0) for p, cut in enumerate(even)]
                 for shift in range(1, owners)
             ]
+        if (h, m) == (HEAD_AFTER if nz > 2 else (0, 0)) and p == len(cut_of(h, m)) - 1:
+            head = add_up((0, count), [whole(own_all[nz - 1]), whole(deltas[0])] + back, dtype=jnp.float32)
     span = (0, count)
-    most = add_up(span, [whole(own_all[nz - 1]), whole(deltas[0]), y_parts(nz - 1)] + back, dtype=jnp.float32)
-    out = add_up(span, [whole(most)] + [arrived_parts(h, nz - 2 - h) for h in range(nz - 1)])
+    early = [arrived_parts(h, nz - 2 - h) for h in range(1, nz - 2)]
+    late = [arrived_parts(h, nz - 2 - h) for h in range(nz - 1) if not 1 <= h < nz - 2]
+    most = add_up(span, [whole(head), y_parts(nz - 1)] + early, dtype=jnp.float32)
+    out = add_up(span, [whole(most)] + late)
     return out.reshape(steps, row_count, out_width)
 
 

time: 175 us -> 186 us (1.063)
  local copies, waits for them, and re-layouts: 10.7 us -> 17.6 us
  Pallas kernels: 69 us -> 75 us
  starting transfers between devices: 30.6 us -> 34 us
  between operations: 3.25 us -> 0.59 us
  waiting for transfers between devices: 58.5 us -> 56.4 us
    unnamed x44 -> x52, local copies, waits for them, and re-layouts: 9.1 us -> 15.4 us
    pallas_call x21 -> x24, Pallas kernels: 69 us -> 75 us  [call(): pl.pallas_call(body, grid_spec=pltpu.PrefetchScalarGridSpec(num_scalar_pr...]
    ppermute x9 -> x11, waiting for transfers between devices: 34.6 us -> 29.4 us  [hop(): return lax.ppermute(value, 'tensor', pairs)]
    ppermute x5, waiting for transfers between devices: 21.5 us -> 26.6 us  [swap_y(): return lax.ppermute(value, 'tensor', [(t, t ^ 1) for t in range(n)])]
    ppermute x9 -> x11, starting transfers between devices: 21.8 us -> 24.9 us  [hop(): return lax.ppermute(value, 'tensor', pairs)]
  transfers between devices with their start and end apart: 18 -> 20, of which waited for: 9 -> 8; matrix products, arithmetic and copies ran while one was open for 2% -> 2% of each run, Pallas kernels for 38% -> 39%
where the time goes in v9:
time: 186 us; the launch traced here: 185 us
  Pallas kernels  75 us (40%)
  waiting for transfers between devices  56.4 us (30%)
  starting transfers between devices  34 us (18%)
  local copies, waits for them, and re-layouts  17.6 us (9%)
    pallas_call x24, Pallas kernels, call(): pl.pallas_call(body, grid_spec=pltpu.PrefetchScalarGridSpec(num_scalar_pr...  75 us
    ppermute x11, waiting for transfers between devices, hop(): return lax.ppermute(value, 'tensor', pairs)  29.4 us
    ppermute x5, waiting for transfers between devices, swap_y(): return lax.ppermute(value, 'tensor', [(t, t ^ 1) for t in range(n)])  26.6 us
    ppermute x11, starting transfers between devices, hop(): return lax.ppermute(value, 'tensor', pairs)  24.9 us
    unnamed x52, local copies, waits for them, and re-layouts  15.4 us
    ppermute x5, starting transfers between devices, swap_y(): return lax.ppermute(value, 'tensor', [(t, t ^ 1) for t in range(n)])  8.23 us
  transfers between devices with their start and end apart: 20, of which 8 were waited for; matrix products, arithmetic and copies ran while one was open for 2% of the time, Pallas kernels for 39%

profile of v9, /device:TPU:0, one launch (start us, length us, event | category | flops | bytes accessed | tf_op | source)
XLA Modules:
  0.0 185.1 jit_solution(8940662304624341336)
XLA Ops:
  1.2 1.4 copy-done
  2.6 3.6 %products.5.refs_6_ = bf16[480,1024]{1,0:T(8,128)(2,1)S(1)} custom-call(s32[8]{0:T(128)S(1)} %dynamic-slice_bitcast_fusion.refs_0_, bf16[768,1024]{1,0:T(8,128)(2,1)S(1)} %bitcast.10, bf16[1024,8192]{1,0:T(8,128)(2,1)} %refs_2_.9), custom_call_target="tpu_custom_call" | custom-call | flops 1 | bytes 1 | tf_op jit(solution)/shard_map/products/pallas_call | solution.py:25
  6.2 3.0 %collective-permute-start.3 = (bf16[480,1024]{1,0:T(8,128)(2,1)S(1)}, bf16[480,1024]{1,0:T(8,128)(2,1)S(1)}, u32[]{:S(2)}, u32[]{:S(2)}) collective-permute-start(bf16[480,1024]{1,0:T(8,128)(2,1)S(1)} %products.5.refs_6_), channel_id=1, source_target_pairs={{0,2},{2,0},{4,6},{6,4},{8,10},{10,8},{12,14},{14,12},{1,3},{3,1},... | collective-permute-start | bytes 2949128 | tf_op jit(solution)/shard_map/ppermute | solution.py:371
  15.2 6.6 %low_rank.1.refs_3_.refs_4_.refs_2_ = bf16[96,1024]{1,0:T(8,128)(2,1)S(1)} custom-call(s32[32]{0:T(128)S(1)} %pad_add_fusion.refs_0_, bf16[768,1024]{1,0:T(8,128)(2,1)S(1)} %bitcast.11, bf16[768,1024]{1,0:T(8,128)(2,1)} %collective-permute-done.1.refs_2_, s32[192,1]{1,0:T(8,128)S(1)} %copy-done.15, s32[192,1]{1,0:T(8,128)S(1)} %copy-done.17, ...), custom_call_target="tpu_custom_call" | custom-call | flops 1 | bytes 1 | tf_op jit(solution)/shard_map/low_rank/pallas_call | solution.py:25
  21.8 2.9 %products.6.refs_3_ = bf16[384,1024]{1,0:T(8,128)(2,1)S(1)} custom-call(s32[8]{0:T(128)S(1)} %dynamic-slice_bitcast_fusion.refs_0_, bf16[768,1024]{1,0:T(8,128)(2,1)S(1)} %bitcast.12, bf16[1024,8192]{1,0:T(8,128)(2,1)} %refs_2_.9, bf16[96,1024]{1,0:T(8,128)(2,1)S(1)} %low_rank.1.refs_3_.refs_4_.refs_2_, bf16[96,1024]{1,0:T(8,128)(2,1)S(1)} %low_rank.1.refs_3_.refs_4_.refs_2_), custom_call_target="tpu_custom_call" | custom-call | flops 1 | bytes 1 | tf_op jit(solution)/shard_map/products/pallas_call | solution.py:25
  24.8 6.3 %products.7 = (bf16[768,1024]{1,0:T(8,128)(2,1)}, bf16[768,1024]{1,0:T(8,128)(2,1)S(1)}) custom-call(s32[8]{0:T(128)S(1)} %dynamic-slice_bitcast_fusion.refs_0_, bf16[768,1024]{1,0:T(8,128)(2,1)} %bitcast.7, bf16[1024,8192]{1,0:T(8,128)(2,1)} %refs_2_.9, bf16[384,1024]{1,0:T(8,128)(2,1)S(1)} %products.6.refs_3_), custom_call_target="tpu_custom_call" | custom-call | flops 1 | bytes 1 | tf_op jit(solution)/shard_map/products/pallas_call | solution.py:25
  31.1 2.1 %collective-permute-start.7 = (bf16[768,1024]{1,0:T(8,128)(2,1)}, bf16[768,1024]{1,0:T(8,128)(2,1)}, u32[]{:S(2)}, u32[]{:S(2)}) collective-permute-start(bf16[768,1024]{1,0:T(8,128)(2,1)} %get-tuple-element.16.refs_2_), channel_id=1, source_target_pairs={{0,2},{2,0},{4,6},{6,4},{8,10},{10,8},{12,14},{14,12},{1,3},{3,1},... | collective-permute-start | bytes 4718600 | tf_op jit(solution)/shard_map/ppermute | solution.py:371
  33.2 2.2 %total.15.refs_3_.refs_0_ = bf16[480,1024]{1,0:T(8,128)(2,1)S(1)} custom-call(bf16[768,1024]{1,0:T(8,128)(2,1)S(1)} %get-tuple-element.15.refs_0_, bf16[480,1024]{1,0:T(8,128)(2,1)S(1)} %collective-permute-done.3.refs_1_, bf16[768,1024]{1,0:T(8,128)(2,1)} %get-tuple-element.16.refs_2_), custom_call_target="tpu_custom_call" | custom-call | flops 1 | bytes 1 | tf_op jit(solution)/shard_map/total/pallas_call | solution.py:25
  35.4 3.5 %collective-permute-start.5 = (bf16[480,1024]{1,0:T(8,128)(2,1)S(1)}, bf16[480,1024]{1,0:T(8,128)(2,1)S(1)}, u32[]{:S(2)}, u32[]{:S(2)}) collective-permute-start(bf16[480,1024]{1,0:T(8,128)(2,1)S(1)} %total.15.refs_3_.refs_0_), channel_id=1, source_target_pairs={{0,4},{12,8},{2,6},{14,10},{1,5},{13,9},{3,7},{15,11},{16,20},{28,... | collective-permute-start | bytes 2949128 | tf_op jit(solution)/shard_map/ppermute | solution.py:378
  38.9 7.6 %products.8 = (bf16[768,1024]{1,0:T(8,128)(2,1)S(1)}, bf16[768,1024]{1,0:T(8,128)(2,1)}) custom-call(s32[8]{0:T(128)S(1)} %dynamic-slice_bitcast_fusion.refs_0_, bf16[768,1024]{1,0:T(8,128)(2,1)} %bitcast.8, bf16[1024,8192]{1,0:T(8,128)(2,1)} %refs_2_.9, bf16[480,1024]{1,0:T(8,128)(2,1)S(1)} %total.15.refs_3_.refs_0_), custom_call_target="tpu_custom_call" | custom-call | flops 1 | bytes 1 | tf_op jit(solution)/shard_map/products/pallas_call | solution.py:25
  46.5 1.2 copy-done.9
  47.7 1.0 collective-permute-done.2.refs_1_.refs_3_
  48.6 1.4 total.16.refs_3_.refs_0_.refs_2_.refs_1_
  50.0 4.2 %collective-permute-start.4 = (bf16[384,1024]{1,0:T(8,128)(2,1)S(1)}, bf16[384,1024]{1,0:T(8,128)(2,1)S(1)}, u32[]{:S(2)}, u32[]{:S(2)}) collective-permute-start(bf16[384,1024]{1,0:T(8,128)(2,1)S(1)} %total.16.refs_3_.refs_0_.refs_2_.refs_1_), channel_id=1, source_target_pairs={{0,4},{12,8},{2,6},{14,10},{1,5},{13,9},{3,7},{15,11},{16,20},{28,... | collective-permute-start | bytes 2359304 | tf_op jit(solution)/shard_map/ppermute | solution.py:378
  54.3 10.1 %products.9 = (bf16[768,1024]{1,0:T(8,128)(2,1)S(1)}, bf16[768,1024]{1,0:T(8,128)(2,1)S(1)}, bf16[768,1024]{1,0:T(8,128)(2,1)}) custom-call(s32[8]{0:T(128)S(1)} %dynamic-slice_bitcast_fusion.refs_0_, bf16[768,1024]{1,0:T(8,128)(2,1)} %bitcast.9, bf16[1024,8192]{1,0:T(8,128)(2,1)} %refs_2_.9, bf16[384,1024]{1,0:T(8,128)(2,1)S(1)} %total.16.refs_3_.refs_0_.refs_2_.refs_1_), custom_call_target="tpu_custom_call" | custom-call | flops 1 | bytes 1 | tf_op jit(solution)/shard_map/products/pallas_call | solution.py:25
  64.4 1.1 copy-done.6
  65.6 1.2 copy-done.13
  66.8 1.5 collective-permute-start.12
  68.3 2.2 %total.17.refs_4_ = bf16[480,1024]{1,0:T(8,128)(2,1)S(1)} custom-call(bf16[480,1024]{1,0:T(8,128)(2,1)S(1)} %total.15.refs_3_.refs_0_, bf16[480,1024]{1,0:T(8,128)(2,1)S(1)} %collective-permute-done.5.refs_1_, bf16[768,1024]{1,0:T(8,128)(2,1)} %copy-done.6), custom_call_target="tpu_custom_call" | custom-call | flops 1 | bytes 1 | tf_op jit(solution)/shard_map/total/pallas_call | solution.py:25
  70.5 5.9 %collective-permute-done.4.refs_1_.refs_3_ = bf16[384,1024]{1,0:T(8,128)(2,1)S(1)} collective-permute-done((bf16[384,1024]{1,0:T(8,128)(2,1)S(1)}, bf16[384,1024]{1,0:T(8,128)(2,1)S(1)}, u32[]{:S(2)}, u32[]{:S(2)}) %collective-permute-start.4) | collective-permute-done | bytes 786464 | tf_op jit(solution)/shard_map/ppermute | solution.py:378
  76.4 1.4 total.18.refs_2_
  78.5 4.0 %collective-permute-done.7.refs_1_ = bf16[768,1024]{1,0:T(8,128)(2,1)} collective-permute-done((bf16[768,1024]{1,0:T(8,128)(2,1)}, bf16[768,1024]{1,0:T(8,128)(2,1)}, u32[]{:S(2)}, u32[]{:S(2)}) %collective-permute-start.7) | collective-permute-done | bytes 1572896 | tf_op jit(solution)/shard_map/ppermute | solution.py:371
  82.5 1.8 total.19.refs_2_.refs_0_
  84.3 4.1 %collective-permute-start.9 = (bf16[384,1024]{1,0:T(8,128)(2,1)S(1)}, bf16[384,1024]{1,0:T(8,128)(2,1)S(1)}, u32[]{:S(2)}, u32[]{:S(2)}) collective-permute-start(bf16[384,1024]{1,0:T(8,128)(2,1)S(1)} %total.19.refs_2_.refs_0_), channel_id=1, source_target_pairs={{0,4},{12,8},{2,6},{14,10},{1,5},{13,9},{3,7},{15,11},{16,20},{28,... | collective-permute-start | bytes 2359304 | tf_op jit(solution)/shard_map/ppermute | solution.py:378
  88.3 1.7 collective-permute-start.13
  90.0 1.8 total.20.refs_2_.refs_0_
  91.8 4.0 %collective-permute-start.14 = (bf16[384,1024]{1,0:T(8,128)(2,1)S(1)}, bf16[384,1024]{1,0:T(8,128)(2,1)}, u32[]{:S(2)}, u32[]{:S(2)}) collective-permute-start(bf16[384,1024]{1,0:T(8,128)(2,1)S(1)} %total.20.refs_2_.refs_0_), channel_id=1, source_target_pairs={{0,4},{12,8},{2,6},{14,10},{1,5},{13,9},{3,7},{15,11},{16,20},{28,... | collective-permute-start | bytes 2359304 | tf_op jit(solution)/shard_map/ppermute | solution.py:378
  96.6 9.7 %collective-permute-done.9.refs_1_ = bf16[384,1024]{1,0:T(8,128)(2,1)S(1)} collective-permute-done((bf16[384,1024]{1,0:T(8,128)(2,1)S(1)}, bf16[384,1024]{1,0:T(8,128)(2,1)S(1)}, u32[]{:S(2)}, u32[]{:S(2)}) %collective-permute-start.9) | collective-permute-done | bytes 786464 | tf_op jit(solution)/shard_map/ppermute | solution.py:378
  106.3 1.4 total.22.refs_4_
  108.5 1.3 collective-permute-start.8
  109.8 8.9 %collective-permute-done.8.refs_3_ = bf16[96,1024]{1,0:T(8,128)(2,1)S(1)} collective-permute-done((bf16[96,1024]{1,0:T(8,128)(2,1)S(1)}, bf16[96,1024]{1,0:T(8,128)(2,1)S(1)}, u32[]{:S(2)}, u32[]{:S(2)}) %collective-permute-start.8) | collective-permute-done | bytes 196640 | tf_op jit(solution)/shard_map/ppermute | solution.py:378
  118.7 1.4 total.23.refs_1_.refs_5_
  120.1 7.1 %expand.1 = (bf16[768,1024]{1,0:T(8,128)(2,1)S(1)}, bf16[384,1024]{1,0:T(8,128)(2,1)}, bf16[384,1024]{1,0:T(8,128)(2,1)S(1)}) custom-call(s32[32]{0:T(128)S(1)} %pad_add_fusion.refs_0_, bf16[96,1024]{1,0:T(8,128)(2,1)S(1)} %total.23.refs_1_.refs_5_, s32[192,1]{1,0:T(8,128)S(1)} %copy-done.16, s32[192,1]{1,0:T(8,128)S(1)} %copy-done.18, ...), custom_call_target="tpu_custom_call" | custom-call | flops 1 | bytes 1 | tf_op jit(solution)/shard_map/expand/pallas_call | solution.py:25
  127.2 1.1 copy-done.3
  129.2 1.4 copy-done.14
  130.6 1.8 total.24.refs_2_.refs_0_.refs_1_
  132.5 1.1 copy-done.2
  133.6 2.6 %collective-permute-start.18 = (bf16[768,1024]{1,0:T(8,128)(2,1)S(1)}, bf16[768,1024]{1,0:T(8,128)(2,1)}, u32[]{:S(2)}, u32[]{:S(2)}) collective-permute-start(bf16[768,1024]{1,0:T(8,128)(2,1)S(1)} %total.24.refs_2_.refs_0_.refs_1_), channel_id=1, source_target_pairs={{0,4},{12,8},{2,6},{14,10},{1,5},{13,9},{3,7},{15,11},{16,20},{28,... | collective-permute-start | bytes 4718600 | tf_op jit(solution)/shard_map/ppermute | solution.py:378
  136.2 1.5 collective-permute-start.16
  137.8 1.8 total.25.refs_4_
  140.5 2.6 %total.26.refs_6_ = bf16[768,1024]{1,0:T(8,128)(2,1)S(1)} custom-call(bf16[768,1024]{1,0:T(8,128)(2,1)} %copy-done.2, bf16[480,1024]{1,0:T(8,128)(2,1)} %collective-permute-done.13.refs_1_, bf16[768,1024]{1,0:T(8,128)(2,1)} %copy-done.2, bf16[384,1024]{1,0:T(8,128)(2,1)S(1)} %collective-permute-done.6.refs_1_.refs_2_.refs_3_, ...), custom_call_target="tpu_custom_call" | custom-call | flops 1 | bytes 1 | tf_op jit(solution)/shard_map/total/pallas_call | solution.py:25
  143.1 1.3 collective-permute-start.19
  146.7 1.1 copy-done.20
  147.9 3.5 %total.27.refs_0_.refs_3_.refs_6_ = f32[768,1024]{1,0:T(8,128)} custom-call(bf16[768,1024]{1,0:T(8,128)(2,1)S(1)} %copy-done.4, bf16[768,1024]{1,0:T(8,128)(2,1)} %copy-done.3, bf16[384,1024]{1,0:T(8,128)(2,1)S(1)} %copy-done.20, bf16[768,1024]{1,0:T(8,128)(2,1)S(1)} %copy-done.4, bf16[768,1024]{1,0:T(8,128)(2,1)} %copy-done.3, ...), custom_call_target="tpu_custom_call" | custom-call | flops 1 | bytes 1 | tf_op jit(solution)/shard_map/total/pallas_call | solution.py:25
  151.4 21.6 %collective-permute-done.16.refs_1_.refs_4_ = bf16[768,1024]{1,0:T(8,128)(2,1)S(1)} collective-permute-done((bf16[768,1024]{1,0:T(8,128)(2,1)S(1)}, bf16[768,1024]{1,0:T(8,128)(2,1)S(1)}, u32[]{:S(2)}, u32[]{:S(2)}) %collective-permute-start.16) | collective-permute-done | bytes 1572896 | tf_op jit(solution)/shard_map/ppermute | solution.py:371
  173.1 3.5 %total.28.refs_0_.refs_3_ = f32[768,1024]{1,0:T(8,128)} custom-call(f32[768,1024]{1,0:T(8,128)} %total.27.refs_0_.refs_3_.refs_6_, bf16[768,1024]{1,0:T(8,128)(2,1)S(1)} %collective-permute-done.16.refs_1_.refs_4_, bf16[384,1024]{1,0:T(8,128)(2,1)S(1)} %copy-done.12, f32[768,1024]{1,0:T(8,128)} %total.27.refs_0_.refs_3_.refs_6_, ...), custom_call_target="tpu_custom_call" | custom-call | flops 1 | bytes 1 | tf_op jit(solution)/shard_map/total/pallas_call | solution.py:25
  176.6 4.9 %collective-permute-done.19.refs_2_ = bf16[768,1024]{1,0:T(8,128)(2,1)S(1)} collective-permute-done((bf16[768,1024]{1,0:T(8,128)(2,1)S(1)}, bf16[768,1024]{1,0:T(8,128)(2,1)S(1)}, u32[]{:S(2)}, u32[]{:S(2)}) %collective-permute-start.19) | collective-permute-done | bytes 1572896 | tf_op jit(solution)/shard_map/ppermute | solution.py:378
  181.5 3.5 %total.29 = bf16[768,1024]{1,0:T(8,128)(2,1)} custom-call(f32[768,1024]{1,0:T(8,128)} %total.28.refs_0_.refs_3_, bf16[768,1024]{1,0:T(8,128)(2,1)} %collective-permute-done.18.refs_1_, bf16[768,1024]{1,0:T(8,128)(2,1)S(1)} %collective-permute-done.19.refs_2_, f32[768,1024]{1,0:T(8,128)} %total.28.refs_0_.refs_3_), custom_call_target="tpu_custom_call" | custom-call | flops 1 | bytes 1 | tf_op jit(solution)/shard_map/total/pallas_call | solution.py:25
  (85 shorter events, 13.9 us)
Async XLA Ops:
  0.0 10.9 %collective-permute-start = (s32[192]{0:T(256)}, s32[192]{0:T(256)S(1)}, u32[]{:S(2)}, u32[]{:S(2)}) collective-permute-start(s32[192]{0:T(256)} %param.7), channel_id=1, source_target_pairs={{0,1},{1,0},{2,3},{3,2},{4,5},{5,4},{6,7},{7,6},{8,9},{9,8},{10,11... | collective-permute-start | bytes 2312 | tf_op jit(solution)/shard_map/ppermute | solution.py:384
  0.5 13.0 %collective-permute-start.1 = (bf16[768,1024]{1,0:T(8,128)(2,1)}, bf16[768,1024]{1,0:T(8,128)(2,1)}, u32[]{:S(2)}, u32[]{:S(2)}) collective-permute-start(bf16[768,1024]{1,0:T(8,128)(2,1)} %bitcast.6), channel_id=1, source_target_pairs={{0,1},{1,0},{2,3},{3,2},{4,5},{5,4},{6,7},{7,6},{8,9},{9,8},{10,11... | collective-permute-start | bytes 4718600 | tf_op jit(solution)/shard_map/ppermute | solution.py:384
  1.2 1.4 copy-start
  2.6 6.6 %copy-start.23 = (s32[192]{0:T(256)S(1)}, s32[192]{0:T(256)}, u32[]{:S(2)}) copy-start(s32[192]{0:T(256)} %param.7) | copy-start | bytes 2308
  2.6 10.8 %copy-start.1 = (bf16[4,192,1024]{2,1,0:T(8,128)(2,1)S(1)}, bf16[4,192,1024]{2,1,0:T(8,128)(2,1)}, u32[]{:S(2)}) copy-start(bf16[4,192,1024]{2,1,0:T(8,128)(2,1)} %param.6) | copy-start | bytes 4718596
  6.2 27.0 %collective-permute-start.3 = (bf16[480,1024]{1,0:T(8,128)(2,1)S(1)}, bf16[480,1024]{1,0:T(8,128)(2,1)S(1)}, u32[]{:S(2)}, u32[]{:S(2)}) collective-permute-start(bf16[480,1024]{1,0:T(8,128)(2,1)S(1)} %products.5.refs_6_), channel_id=1, source_target_pairs={{0,2},{2,0},{4,6},{6,4},{8,10},{10,8},{12,14},{14,12},{1,3},{3,1},... | collective-permute-start | bytes 2949128 | tf_op jit(solution)/shard_map/ppermute | solution.py:371
  9.5 0.6 copy-start.24
  11.2 0.5 copy-start.25
  13.4 0.9 copy-start.15
  14.3 0.9 copy-start.17
  24.7 23.9 %collective-permute-start.2 = (bf16[384,1024]{1,0:T(8,128)(2,1)S(1)}, bf16[384,1024]{1,0:T(8,128)(2,1)S(1)}, u32[]{:S(2)}, u32[]{:S(2)}) collective-permute-start(bf16[384,1024]{1,0:T(8,128)(2,1)S(1)} %products.6.refs_3_), channel_id=1, source_target_pairs={{0,2},{2,0},{4,6},{6,4},{8,10},{10,8},{12,14},{14,12},{1,3},{3,1},... | collective-permute-start | bytes 2359304 | tf_op jit(solution)/shard_map/ppermute | solution.py:371
  31.1 51.3 %collective-permute-start.7 = (bf16[768,1024]{1,0:T(8,128)(2,1)}, bf16[768,1024]{1,0:T(8,128)(2,1)}, u32[]{:S(2)}, u32[]{:S(2)}) collective-permute-start(bf16[768,1024]{1,0:T(8,128)(2,1)} %get-tuple-element.16.refs_2_), channel_id=1, source_target_pairs={{0,2},{2,0},{4,6},{6,4},{8,10},{10,8},{12,14},{14,12},{1,3},{3,1},... | collective-permute-start | bytes 4718600 | tf_op jit(solution)/shard_map/ppermute | solution.py:371
  35.4 32.9 %collective-permute-start.5 = (bf16[480,1024]{1,0:T(8,128)(2,1)S(1)}, bf16[480,1024]{1,0:T(8,128)(2,1)S(1)}, u32[]{:S(2)}, u32[]{:S(2)}) collective-permute-start(bf16[480,1024]{1,0:T(8,128)(2,1)S(1)} %total.15.refs_3_.refs_0_), channel_id=1, source_target_pairs={{0,4},{12,8},{2,6},{14,10},{1,5},{13,9},{3,7},{15,11},{16,20},{28,... | collective-permute-start | bytes 2949128 | tf_op jit(solution)/shard_map/ppermute | solution.py:378
  46.5 1.2 copy-start.9
  48.6 5.7 %copy-start.10 = (bf16[768,1024]{1,0:T(8,128)(2,1)S(1)}, bf16[768,1024]{1,0:T(8,128)(2,1)}, u32[]{:S(2)}) copy-start(bf16[768,1024]{1,0:T(8,128)(2,1)} %copy-done.9) | copy-start | bytes 4718596
  50.0 26.3 %collective-permute-start.4 = (bf16[384,1024]{1,0:T(8,128)(2,1)S(1)}, bf16[384,1024]{1,0:T(8,128)(2,1)S(1)}, u32[]{:S(2)}, u32[]{:S(2)}) collective-permute-start(bf16[384,1024]{1,0:T(8,128)(2,1)S(1)} %total.16.refs_3_.refs_0_.refs_2_.refs_1_), channel_id=1, source_target_pairs={{0,4},{12,8},{2,6},{14,10},{1,5},{13,9},{3,7},{15,11},{16,20},{28,... | collective-permute-start | bytes 2359304 | tf_op jit(solution)/shard_map/ppermute | solution.py:378
  64.4 1.2 copy-start.6
  65.6 1.2 copy-start.13
  66.8 62.5 %collective-permute-start.12 = (bf16[768,1024]{1,0:T(8,128)(2,1)S(1)}, bf16[768,1024]{1,0:T(8,128)(2,1)}, u32[]{:S(2)}, u32[]{:S(2)}) collective-permute-start(bf16[768,1024]{1,0:T(8,128)(2,1)S(1)} %hold.2), channel_id=1, source_target_pairs={{0,2},{2,0},{4,6},{6,4},{8,10},{10,8},{12,14},{14,12},{1,3},{3,1},... | collective-permute-start | bytes 4718600 | tf_op jit(solution)/shard_map/ppermute | solution.py:371
  70.4 12.0 %copy-start.8 = (bf16[768,1024]{1,0:T(8,128)(2,1)S(1)}, bf16[768,1024]{1,0:T(8,128)(2,1)}, u32[]{:S(2)}) copy-start(bf16[768,1024]{1,0:T(8,128)(2,1)} %get-tuple-element.20.refs_0_) | copy-start | bytes 4718596
  77.8 18.0 %collective-permute-start.6 = (bf16[384,1024]{1,0:T(8,128)(2,1)S(1)}, bf16[384,1024]{1,0:T(8,128)(2,1)S(1)}, u32[]{:S(2)}, u32[]{:S(2)}) collective-permute-start(bf16[384,1024]{1,0:T(8,128)(2,1)S(1)} %total.18.refs_2_), channel_id=1, source_target_pairs={{4,8},{8,4},{6,10},{10,6},{5,9},{9,5},{7,11},{11,7},{20,24},{24,20... | collective-permute-start | bytes 2359304 | tf_op jit(solution)/shard_map/ppermute | solution.py:378
  84.3 22.0 %collective-permute-start.9 = (bf16[384,1024]{1,0:T(8,128)(2,1)S(1)}, bf16[384,1024]{1,0:T(8,128)(2,1)S(1)}, u32[]{:S(2)}, u32[]{:S(2)}) collective-permute-start(bf16[384,1024]{1,0:T(8,128)(2,1)S(1)} %total.19.refs_2_.refs_0_), channel_id=1, source_target_pairs={{0,4},{12,8},{2,6},{14,10},{1,5},{13,9},{3,7},{15,11},{16,20},{28,... | collective-permute-start | bytes 2359304 | tf_op jit(solution)/shard_map/ppermute | solution.py:378
  88.3 52.1 %collective-permute-start.13 = (bf16[480,1024]{1,0:T(8,128)(2,1)S(1)}, bf16[480,1024]{1,0:T(8,128)(2,1)}, u32[]{:S(2)}, u32[]{:S(2)}) collective-permute-start(bf16[480,1024]{1,0:T(8,128)(2,1)S(1)} %total.17.refs_4_), channel_id=1, source_target_pairs={{4,8},{8,4},{6,10},{10,6},{5,9},{9,5},{7,11},{11,7},{20,24},{24,20... | collective-permute-start | bytes 2949128 | tf_op jit(solution)/shard_map/ppermute | solution.py:378
  91.8 44.4 %collective-permute-start.14 = (bf16[384,1024]{1,0:T(8,128)(2,1)S(1)}, bf16[384,1024]{1,0:T(8,128)(2,1)}, u32[]{:S(2)}, u32[]{:S(2)}) collective-permute-start(bf16[384,1024]{1,0:T(8,128)(2,1)S(1)} %total.20.refs_2_.refs_0_), channel_id=1, source_target_pairs={{0,4},{12,8},{2,6},{14,10},{1,5},{13,9},{3,7},{15,11},{16,20},{28,... | collective-permute-start | bytes 2359304 | tf_op jit(solution)/shard_map/ppermute | solution.py:378
  107.6 12.4 %copy-start.16 = (s32[192,1]{1,0:T(8,128)S(1)}, s32[192,1]{1,0:T(8,128)}, u32[]{:S(2)}) copy-start(s32[192,1]{1,0:T(8,128)} %copy.13.refs_3_.refs_2_) | copy-start | bytes 2308
  107.6 12.4 %copy-start.18 = (s32[192,1]{1,0:T(8,128)S(1)}, s32[192,1]{1,0:T(8,128)}, u32[]{:S(2)}) copy-start(s32[192,1]{1,0:T(8,128)} %copy.14.refs_4_.refs_3_) | copy-start | bytes 2308
  107.7 30.1 %collective-permute-start.15 = (bf16[384,1024]{1,0:T(8,128)(2,1)S(1)}, bf16[384,1024]{1,0:T(8,128)(2,1)S(1)}, u32[]{:S(2)}, u32[]{:S(2)}) collective-permute-start(bf16[384,1024]{1,0:T(8,128)(2,1)S(1)} %total.22.refs_4_), channel_id=1, source_target_pairs={{4,8},{8,4},{6,10},{10,6},{5,9},{9,5},{7,11},{11,7},{20,24},{24,20... | collective-permute-start | bytes 2359304 | tf_op jit(solution)/shard_map/ppermute | solution.py:378
  108.5 10.2 %collective-permute-start.8 = (bf16[96,1024]{1,0:T(8,128)(2,1)S(1)}, bf16[96,1024]{1,0:T(8,128)(2,1)S(1)}, u32[]{:S(2)}, u32[]{:S(2)}) collective-permute-start(bf16[96,1024]{1,0:T(8,128)(2,1)S(1)} %total.21.refs_2_), channel_id=1, source_target_pairs={{8,12},{4,0},{10,14},{6,2},{9,13},{5,1},{11,15},{7,3},{24,28},{20,... | collective-permute-start | bytes 589832 | tf_op jit(solution)/shard_map/ppermute | solution.py:378
  127.2 1.1 copy-start.3
  128.3 0.9 copy-start.21
  129.2 1.4 copy-start.14
  130.6 1.9 %copy-start.7 = (bf16[768,1024]{1,0:T(8,128)(2,1)S(1)}, bf16[768,1024]{1,0:T(8,128)(2,1)}, u32[]{:S(2)}) copy-start(bf16[768,1024]{1,0:T(8,128)(2,1)} %copy-done.6) | copy-start | bytes 4718596
  132.5 1.2 copy-start.2
  133.6 42.9 %collective-permute-start.18 = (bf16[768,1024]{1,0:T(8,128)(2,1)S(1)}, bf16[768,1024]{1,0:T(8,128)(2,1)}, u32[]{:S(2)}, u32[]{:S(2)}) collective-permute-start(bf16[768,1024]{1,0:T(8,128)(2,1)S(1)} %total.24.refs_2_.refs_0_.refs_1_), channel_id=1, source_target_pairs={{0,4},{12,8},{2,6},{14,10},{1,5},{13,9},{3,7},{15,11},{16,20},{28,... | collective-permute-start | bytes 4718600 | tf_op jit(solution)/shard_map/ppermute | solution.py:378
  136.2 8.4 %collective-permute-start.10 = (bf16[384,1024]{1,0:T(8,128)(2,1)}, bf16[384,1024]{1,0:T(8,128)(2,1)S(1)}, u32[]{:S(2)}, u32[]{:S(2)}) collective-permute-start(bf16[384,1024]{1,0:T(8,128)(2,1)} %get-tuple-element.22), channel_id=1, source_target_pairs={{0,1},{1,0},{2,3},{3,2},{4,5},{5,4},{6,7},{7,6},{8,9},{9,8},{10,11... | collective-permute-start | bytes 2359304 | tf_op jit(solution)/shard_map/ppermute | solution.py:384
  136.2 36.8 %collective-permute-start.16 = (bf16[768,1024]{1,0:T(8,128)(2,1)S(1)}, bf16[768,1024]{1,0:T(8,128)(2,1)S(1)}, u32[]{:S(2)}, u32[]{:S(2)}) collective-permute-start(bf16[768,1024]{1,0:T(8,128)(2,1)S(1)} %hold.3), channel_id=1, source_target_pairs={{0,2},{2,0},{4,6},{6,4},{8,10},{10,8},{12,14},{14,12},{1,3},{3,1},... | collective-permute-start | bytes 4718600 | tf_op jit(solution)/shard_map/ppermute | solution.py:371
  139.6 0.9 copy-start.11
  140.5 3.9 %copy-start.22 = (bf16[384,1024]{1,0:T(8,128)(2,1)S(1)}, bf16[384,1024]{1,0:T(8,128)(2,1)}, u32[]{:S(2)}) copy-start(bf16[384,1024]{1,0:T(8,128)(2,1)} %copy-done.21) | copy-start | bytes 2359300
  140.5 6.2 %copy-start.4 = (bf16[768,1024]{1,0:T(8,128)(2,1)S(1)}, bf16[768,1024]{1,0:T(8,128)(2,1)}, u32[]{:S(2)}) copy-start(bf16[768,1024]{1,0:T(8,128)(2,1)} %get-tuple-element.18.refs_0_.refs_3_) | copy-start | bytes 4718596
  143.1 3.7 %copy-start.5 = (bf16[768,1024]{1,0:T(8,128)(2,1)}, bf16[768,1024]{1,0:T(8,128)(2,1)S(1)}, u32[]{:S(2)}) copy-start(bf16[768,1024]{1,0:T(8,128)(2,1)S(1)} %total.26.refs_6_) | copy-start | bytes 4718596
  143.1 38.4 %collective-permute-start.19 = (bf16[768,1024]{1,0:T(8,128)(2,1)S(1)}, bf16[768,1024]{1,0:T(8,128)(2,1)S(1)}, u32[]{:S(2)}, u32[]{:S(2)}) collective-permute-start(bf16[768,1024]{1,0:T(8,128)(2,1)S(1)} %total.26.refs_6_), channel_id=1, source_target_pairs={{8,12},{4,0},{10,14},{6,2},{9,13},{5,1},{11,15},{7,3},{24,28},{20,... | collective-permute-start | bytes 4718600 | tf_op jit(solution)/shard_map/ppermute | solution.py:378
  144.4 2.4 %collective-permute-start.11 = (bf16[384,1024]{1,0:T(8,128)(2,1)S(1)}, bf16[384,1024]{1,0:T(8,128)(2,1)S(1)}, u32[]{:S(2)}, u32[]{:S(2)}) collective-permute-start(bf16[384,1024]{1,0:T(8,128)(2,1)S(1)} %copy-done.22), channel_id=1, source_target_pairs={{0,1},{1,0},{2,3},{3,2},{4,5},{5,4},{6,7},{7,6},{8,9},{9,8},{10,11... | collective-permute-start | bytes 2359304 | tf_op jit(solution)/shard_map/ppermute | solution.py:384
  144.7 0.9 copy-start.19
  145.6 5.9 %collective-permute-start.17 = (bf16[384,1024]{1,0:T(8,128)(2,1)S(1)}, bf16[384,1024]{1,0:T(8,128)(2,1)S(1)}, u32[]{:S(2)}, u32[]{:S(2)}) collective-permute-start(bf16[384,1024]{1,0:T(8,128)(2,1)S(1)} %total.25.refs_4_), channel_id=1, source_target_pairs={{4,8},{8,4},{6,10},{10,6},{5,9},{9,5},{7,11},{11,7},{20,24},{24,20... | collective-permute-start | bytes 2359304 | tf_op jit(solution)/shard_map/ppermute | solution.py:378
  146.7 1.1 copy-start.20
  147.9 25.2 %copy-start.12 = (bf16[384,1024]{1,0:T(8,128)(2,1)S(1)}, bf16[384,1024]{1,0:T(8,128)(2,1)}, u32[]{:S(2)}) copy-start(bf16[384,1024]{1,0:T(8,128)(2,1)} %copy-done.11) | copy-start | bytes 2359300

commit v10 on v9

--- a/solution.py
+++ b/solution.py
@@ -11,7 +11,8 @@
 CHUNK = 512
 PARTS = 2
 LOW_WITH = (0, PARTS - 1)
-HEAD_AFTER = (2, 0)
+LOW_SUM_AFTER = (0, 2, 0)
+EXPAND_AFTER = (2, 0, 0)
 VMEM = 50 * 2**20
 ANY = pl.BlockSpec(memory_space=pl.ANY)
 
@@ -501,6 +502,7 @@
     start_y(*LOW_WITH)
     multiply([(1, 0)], [0])
     start_y(1, 0)
+    low_sum = deltas = None
     for h, m, p in line_order():
         k = slot_of(h, m)
         if (h, m, p) == (1, 1, 1):
@@ -513,8 +515,8 @@
                 if nz > 2:
                     start_y(2, 0, last[0])
                 multiply([(j, 0) for j in range(3, nz)], range(2, nz))
-            elif p == len(cut_of(h, m)) - 1 and 1 < k < nz - 1:
-                start_y(k + 1, 0, last[0])
+            elif p == len(cut_of(h, m)) - 1 and k + 2 < nz:
+                start_y(k + 2, 0, last[0])
         if (h, k, p) == (0, 1, len(cut_of(h, m)) - 1):
             low_at = uneven[LOW_WITH[1]][1]
             pieces = [(sums[LOW_WITH], low_at)]
@@ -524,20 +526,19 @@
                     pieces.append((hop(prefix, step), 0))
                 else:
                     pieces.append((arrived[step, 0, LOW_WITH[1]], low_at))
-        if (h, m, p) == (1, 1, 0):
+        if (h, m, p) == LOW_SUM_AFTER:
             low_sum = then(total, [(low_rows, pieces)])
+        if deltas is None and low_sum is not None and EXPAND_AFTER in arrived:
             deltas = then(expand, low_sum, slot_sets, adapter_up_maps, names)
             back = [
                 [(*cut, pass_on(deltas[1 + (shift - 1) * PARTS + p], -shift), 0) for p, cut in enumerate(even)]
                 for shift in range(1, owners)
             ]
-        if (h, m) == (HEAD_AFTER if nz > 2 else (0, 0)) and p == len(cut_of(h, m)) - 1:
-            head = add_up((0, count), [whole(own_all[nz - 1]), whole(deltas[0])] + back, dtype=jnp.float32)
     span = (0, count)
     early = [arrived_parts(h, nz - 2 - h) for h in range(1, nz - 2)]
     late = [arrived_parts(h, nz - 2 - h) for h in range(nz - 1) if not 1 <= h < nz - 2]
-    most = add_up(span, [whole(head), y_parts(nz - 1)] + early, dtype=jnp.float32)
-    out = add_up(span, [whole(most)] + late)
+    most = add_up(span, [whole(own_all[nz - 1]), whole(deltas[0]), y_parts(nz - 1)] + early, dtype=jnp.float32)
+    out = add_up(span, [whole(most)] + back + late)
     return out.reshape(steps, row_count, out_width)
 
 

time: 186 us -> 182 us (0.978)
  local copies, waits for them, and re-layouts: 17.6 us -> 12.6 us
  waiting for transfers between devices: 56.4 us -> 61.3 us
  Pallas kernels: 75 us -> 72.1 us
    ppermute x11, waiting for transfers between devices: 29.4 us -> 43.8 us  [hop(): return lax.ppermute(value, 'tensor', pairs)]
    ppermute x5, waiting for transfers between devices: 26.6 us -> 17.5 us  [swap_y(): return lax.ppermute(value, 'tensor', [(t, t ^ 1) for t in range(n)])]
    unnamed x52 -> x40, local copies, waits for them, and re-layouts: 15.4 us -> 10.4 us
    pallas_call x24 -> x23, Pallas kernels: 75 us -> 72.1 us  [call(): pl.pallas_call(body, grid_spec=pltpu.PrefetchScalarGridSpec(num_scalar_pr...]
  transfers between devices with their start and end apart: 20 -> 20, of which waited for: 8 -> 9; matrix products, arithmetic and copies ran while one was open for 2% -> 2% of each run, Pallas kernels for 39% -> 38%
where the time goes in v10:
time: 182 us
  Pallas kernels  72.1 us (40%)
  waiting for transfers between devices  61.3 us (34%)
  starting transfers between devices  34 us (19%)
  local copies, waits for them, and re-layouts  12.6 us (7%)
    pallas_call x23, Pallas kernels, call(): pl.pallas_call(body, grid_spec=pltpu.PrefetchScalarGridSpec(num_scalar_pr...  72.1 us
    ppermute x11, waiting for transfers between devices, hop(): return lax.ppermute(value, 'tensor', pairs)  43.8 us
    ppermute x11, starting transfers between devices, hop(): return lax.ppermute(value, 'tensor', pairs)  25.1 us
    ppermute x5, waiting for transfers between devices, swap_y(): return lax.ppermute(value, 'tensor', [(t, t ^ 1) for t in range(n)])  17.5 us
    unnamed x40, local copies, waits for them, and re-layouts  10.4 us
    ppermute x5, starting transfers between devices, swap_y(): return lax.ppermute(value, 'tensor', [(t, t ^ 1) for t in range(n)])  8.35 us
  transfers between devices with their start and end apart: 20, of which 9 were waited for; matrix products, arithmetic and copies ran while one was open for 2% of the time, Pallas kernels for 38%

profile of v10, /device:TPU:0, one launch (start us, length us, event | category | flops | bytes accessed | tf_op | source)
XLA Modules:
  0.0 182.1 jit_solution(9416230787304295606)
XLA Ops:
  1.2 1.4 copy-done
  2.6 3.6 %products.5.refs_6_ = bf16[480,1024]{1,0:T(8,128)(2,1)S(1)} custom-call(s32[8]{0:T(128)S(1)} %dynamic-slice_bitcast_fusion.refs_0_, bf16[768,1024]{1,0:T(8,128)(2,1)S(1)} %bitcast.10, bf16[1024,8192]{1,0:T(8,128)(2,1)} %refs_2_.9), custom_call_target="tpu_custom_call" | custom-call | flops 1 | bytes 1 | tf_op jit(solution)/shard_map/products/pallas_call | solution.py:26
  6.2 3.0 %collective-permute-start.3 = (bf16[480,1024]{1,0:T(8,128)(2,1)S(1)}, bf16[480,1024]{1,0:T(8,128)(2,1)S(1)}, u32[]{:S(2)}, u32[]{:S(2)}) collective-permute-start(bf16[480,1024]{1,0:T(8,128)(2,1)S(1)} %products.5.refs_6_), channel_id=1, source_target_pairs={{0,2},{2,0},{4,6},{6,4},{8,10},{10,8},{12,14},{14,12},{1,3},{3,1},... | collective-permute-start | bytes 2949128 | tf_op jit(solution)/shard_map/ppermute | solution.py:372
  15.2 6.8 %low_rank.1.refs_3_.refs_4_.refs_2_ = bf16[96,1024]{1,0:T(8,128)(2,1)S(1)} custom-call(s32[32]{0:T(128)S(1)} %pad_add_fusion.refs_0_, bf16[768,1024]{1,0:T(8,128)(2,1)S(1)} %bitcast.11, bf16[768,1024]{1,0:T(8,128)(2,1)} %collective-permute-done.1.refs_2_, s32[192,1]{1,0:T(8,128)S(1)} %copy-done.13, s32[192,1]{1,0:T(8,128)S(1)} %copy-done.15, ...), custom_call_target="tpu_custom_call" | custom-call | flops 1 | bytes 1 | tf_op jit(solution)/shard_map/low_rank/pallas_call | solution.py:26
  21.9 2.9 %products.6.refs_3_ = bf16[384,1024]{1,0:T(8,128)(2,1)S(1)} custom-call(s32[8]{0:T(128)S(1)} %dynamic-slice_bitcast_fusion.refs_0_, bf16[768,1024]{1,0:T(8,128)(2,1)S(1)} %bitcast.12, bf16[1024,8192]{1,0:T(8,128)(2,1)} %refs_2_.9, bf16[96,1024]{1,0:T(8,128)(2,1)S(1)} %low_rank.1.refs_3_.refs_4_.refs_2_, bf16[96,1024]{1,0:T(8,128)(2,1)S(1)} %low_rank.1.refs_3_.refs_4_.refs_2_), custom_call_target="tpu_custom_call" | custom-call | flops 1 | bytes 1 | tf_op jit(solution)/shard_map/products/pallas_call | solution.py:26
  24.9 6.3 %products.7 = (bf16[768,1024]{1,0:T(8,128)(2,1)}, bf16[768,1024]{1,0:T(8,128)(2,1)S(1)}) custom-call(s32[8]{0:T(128)S(1)} %dynamic-slice_bitcast_fusion.refs_0_, bf16[768,1024]{1,0:T(8,128)(2,1)} %bitcast.7, bf16[1024,8192]{1,0:T(8,128)(2,1)} %refs_2_.9, bf16[384,1024]{1,0:T(8,128)(2,1)S(1)} %products.6.refs_3_), custom_call_target="tpu_custom_call" | custom-call | flops 1 | bytes 1 | tf_op jit(solution)/shard_map/products/pallas_call | solution.py:26
  31.2 2.1 %collective-permute-start.7 = (bf16[768,1024]{1,0:T(8,128)(2,1)}, bf16[768,1024]{1,0:T(8,128)(2,1)}, u32[]{:S(2)}, u32[]{:S(2)}) collective-permute-start(bf16[768,1024]{1,0:T(8,128)(2,1)} %get-tuple-element.16.refs_2_), channel_id=1, source_target_pairs={{0,2},{2,0},{4,6},{6,4},{8,10},{10,8},{12,14},{14,12},{1,3},{3,1},... | collective-permute-start | bytes 4718600 | tf_op jit(solution)/shard_map/ppermute | solution.py:372
  33.3 2.2 %total.14.refs_3_.refs_0_ = bf16[480,1024]{1,0:T(8,128)(2,1)S(1)} custom-call(bf16[768,1024]{1,0:T(8,128)(2,1)S(1)} %get-tuple-element.15.refs_0_, bf16[480,1024]{1,0:T(8,128)(2,1)S(1)} %collective-permute-done.3.refs_1_, bf16[768,1024]{1,0:T(8,128)(2,1)} %get-tuple-element.16.refs_2_), custom_call_target="tpu_custom_call" | custom-call | flops 1 | bytes 1 | tf_op jit(solution)/shard_map/total/pallas_call | solution.py:26
  35.5 3.5 %collective-permute-start.5 = (bf16[480,1024]{1,0:T(8,128)(2,1)S(1)}, bf16[480,1024]{1,0:T(8,128)(2,1)S(1)}, u32[]{:S(2)}, u32[]{:S(2)}) collective-permute-start(bf16[480,1024]{1,0:T(8,128)(2,1)S(1)} %total.14.refs_3_.refs_0_), channel_id=1, source_target_pairs={{0,4},{12,8},{2,6},{14,10},{1,5},{13,9},{3,7},{15,11},{16,20},{28,... | collective-permute-start | bytes 2949128 | tf_op jit(solution)/shard_map/ppermute | solution.py:379
  39.0 7.5 %products.8 = (bf16[768,1024]{1,0:T(8,128)(2,1)S(1)}, bf16[768,1024]{1,0:T(8,128)(2,1)}) custom-call(s32[8]{0:T(128)S(1)} %dynamic-slice_bitcast_fusion.refs_0_, bf16[768,1024]{1,0:T(8,128)(2,1)} %bitcast.8, bf16[1024,8192]{1,0:T(8,128)(2,1)} %refs_2_.9, bf16[480,1024]{1,0:T(8,128)(2,1)S(1)} %total.14.refs_3_.refs_0_), custom_call_target="tpu_custom_call" | custom-call | flops 1 | bytes 1 | tf_op jit(solution)/shard_map/products/pallas_call | solution.py:26
  46.6 1.2 copy-done.8
  47.7 0.9 collective-permute-done.2.refs_1_.refs_3_
  48.6 1.4 total.15.refs_3_.refs_0_.refs_2_.refs_1_
  50.0 4.2 %collective-permute-start.4 = (bf16[384,1024]{1,0:T(8,128)(2,1)S(1)}, bf16[384,1024]{1,0:T(8,128)(2,1)S(1)}, u32[]{:S(2)}, u32[]{:S(2)}) collective-permute-start(bf16[384,1024]{1,0:T(8,128)(2,1)S(1)} %total.15.refs_3_.refs_0_.refs_2_.refs_1_), channel_id=1, source_target_pairs={{0,4},{12,8},{2,6},{14,10},{1,5},{13,9},{3,7},{15,11},{16,20},{28,... | collective-permute-start | bytes 2359304 | tf_op jit(solution)/shard_map/ppermute | solution.py:379
  54.3 1.6 collective-permute-start.9
  55.9 10.0 %products.9 = (bf16[768,1024]{1,0:T(8,128)(2,1)S(1)}, bf16[768,1024]{1,0:T(8,128)(2,1)S(1)}, bf16[768,1024]{1,0:T(8,128)(2,1)}) custom-call(s32[8]{0:T(128)S(1)} %dynamic-slice_bitcast_fusion.refs_0_, bf16[768,1024]{1,0:T(8,128)(2,1)} %bitcast.9, bf16[1024,8192]{1,0:T(8,128)(2,1)} %refs_2_.9, bf16[384,1024]{1,0:T(8,128)(2,1)S(1)} %total.15.refs_3_.refs_0_.refs_2_.refs_1_), custom_call_target="tpu_custom_call" | custom-call | flops 1 | bytes 1 | tf_op jit(solution)/shard_map/products/pallas_call | solution.py:26
  66.0 1.2 copy-done.4
  67.2 1.1 copy-done.11
  68.4 2.2 %total.16.refs_4_ = bf16[480,1024]{1,0:T(8,128)(2,1)S(1)} custom-call(bf16[480,1024]{1,0:T(8,128)(2,1)S(1)} %total.14.refs_3_.refs_0_, bf16[480,1024]{1,0:T(8,128)(2,1)S(1)} %collective-permute-done.5.refs_1_, bf16[768,1024]{1,0:T(8,128)(2,1)} %copy-done.4), custom_call_target="tpu_custom_call" | custom-call | flops 1 | bytes 1 | tf_op jit(solution)/shard_map/total/pallas_call | solution.py:26
  70.5 6.4 %collective-permute-done.4.refs_1_.refs_3_ = bf16[384,1024]{1,0:T(8,128)(2,1)S(1)} collective-permute-done((bf16[384,1024]{1,0:T(8,128)(2,1)S(1)}, bf16[384,1024]{1,0:T(8,128)(2,1)S(1)}, u32[]{:S(2)}, u32[]{:S(2)}) %collective-permute-start.4) | collective-permute-done | bytes 786464 | tf_op jit(solution)/shard_map/ppermute | solution.py:379
  76.9 1.4 total.17.refs_2_
  79.0 3.4 %collective-permute-done.7.refs_1_ = bf16[768,1024]{1,0:T(8,128)(2,1)} collective-permute-done((bf16[768,1024]{1,0:T(8,128)(2,1)}, bf16[768,1024]{1,0:T(8,128)(2,1)}, u32[]{:S(2)}, u32[]{:S(2)}) %collective-permute-start.7) | collective-permute-done | bytes 1572896 | tf_op jit(solution)/shard_map/ppermute | solution.py:372
  82.5 1.8 total.18.refs_2_.refs_0_
  84.3 4.2 %collective-permute-start.10 = (bf16[384,1024]{1,0:T(8,128)(2,1)S(1)}, bf16[384,1024]{1,0:T(8,128)(2,1)S(1)}, u32[]{:S(2)}, u32[]{:S(2)}) collective-permute-start(bf16[384,1024]{1,0:T(8,128)(2,1)S(1)} %total.18.refs_2_.refs_0_), channel_id=1, source_target_pairs={{0,4},{12,8},{2,6},{14,10},{1,5},{13,9},{3,7},{15,11},{16,20},{28,... | collective-permute-start | bytes 2359304 | tf_op jit(solution)/shard_map/ppermute | solution.py:379
  88.5 1.6 collective-permute-start.11
  90.1 1.8 total.19.refs_2_.refs_0_.refs_1_
  91.9 4.1 %collective-permute-start.12 = (bf16[384,1024]{1,0:T(8,128)(2,1)S(1)}, bf16[384,1024]{1,0:T(8,128)(2,1)}, u32[]{:S(2)}, u32[]{:S(2)}) collective-permute-start(bf16[384,1024]{1,0:T(8,128)(2,1)S(1)} %total.19.refs_2_.refs_0_.refs_1_), channel_id=1, source_target_pairs={{0,4},{12,8},{2,6},{14,10},{1,5},{13,9},{3,7},{15,11},{16,20},{28,... | collective-permute-start | bytes 2359304 | tf_op jit(solution)/shard_map/ppermute | solution.py:379
  96.8 9.6 %collective-permute-done.10.refs_1_ = bf16[384,1024]{1,0:T(8,128)(2,1)S(1)} collective-permute-done((bf16[384,1024]{1,0:T(8,128)(2,1)S(1)}, bf16[384,1024]{1,0:T(8,128)(2,1)S(1)}, u32[]{:S(2)}, u32[]{:S(2)}) %collective-permute-start.10) | collective-permute-done | bytes 786464 | tf_op jit(solution)/shard_map/ppermute | solution.py:379
  106.4 1.4 total.21.refs_2_
  108.5 1.6 collective-permute-start.14
  110.1 6.1 %collective-permute-done.9.refs_1_ = bf16[768,1024]{1,0:T(8,128)(2,1)} collective-permute-done((bf16[768,1024]{1,0:T(8,128)(2,1)S(1)}, bf16[768,1024]{1,0:T(8,128)(2,1)}, u32[]{:S(2)}, u32[]{:S(2)}) %collective-permute-start.9) | collective-permute-done | bytes 1572896 | tf_op jit(solution)/shard_map/ppermute | solution.py:372
  116.2 1.3 collective-permute-start.8
  117.5 1.4 copy-done.12
  118.9 1.7 total.22.refs_4_.refs_0_.refs_2_
  120.6 3.1 %collective-permute-done.8.refs_3_ = bf16[96,1024]{1,0:T(8,128)(2,1)S(1)} collective-permute-done((bf16[96,1024]{1,0:T(8,128)(2,1)S(1)}, bf16[96,1024]{1,0:T(8,128)(2,1)S(1)}, u32[]{:S(2)}, u32[]{:S(2)}) %collective-permute-start.8) | collective-permute-done | bytes 196640 | tf_op jit(solution)/shard_map/ppermute | solution.py:379
  123.7 1.6 collective-permute-start.17
  125.3 1.4 total.23.refs_2_.refs_1_
  126.7 1.8 total.24.refs_4_
  128.6 2.5 %total.25.refs_5_ = bf16[768,1024]{1,0:T(8,128)(2,1)S(1)} custom-call(bf16[768,1024]{1,0:T(8,128)(2,1)} %copy-done.2, bf16[480,1024]{1,0:T(8,128)(2,1)} %collective-permute-done.11.refs_1_, bf16[768,1024]{1,0:T(8,128)(2,1)} %copy-done.2, bf16[384,1024]{1,0:T(8,128)(2,1)S(1)} %collective-permute-done.6.refs_1_.refs_2_.refs_3_, ...), custom_call_target="tpu_custom_call" | custom-call | flops 1 | bytes 1 | tf_op jit(solution)/shard_map/total/pallas_call | solution.py:26
  131.1 1.6 collective-permute-start.18
  132.6 1.6 collective-permute-start.15
  134.2 6.8 %expand.1 = (bf16[768,1024]{1,0:T(8,128)(2,1)S(1)}, bf16[384,1024]{1,0:T(8,128)(2,1)}, bf16[384,1024]{1,0:T(8,128)(2,1)}) custom-call(s32[32]{0:T(128)S(1)} %pad_add_fusion.refs_0_, bf16[96,1024]{1,0:T(8,128)(2,1)S(1)} %total.23.refs_2_.refs_1_, s32[192,1]{1,0:T(8,128)S(1)} %copy-done.14, s32[192,1]{1,0:T(8,128)S(1)} %copy-done.16, ...), custom_call_target="tpu_custom_call" | custom-call | flops 1 | bytes 1 | tf_op jit(solution)/shard_map/expand/pallas_call | solution.py:26
  141.1 1.1 copy-done.3
  142.2 7.0 %collective-permute-done.14.refs_2_.refs_6_ = bf16[768,1024]{1,0:T(8,128)(2,1)} collective-permute-done((bf16[768,1024]{1,0:T(8,128)(2,1)S(1)}, bf16[768,1024]{1,0:T(8,128)(2,1)}, u32[]{:S(2)}, u32[]{:S(2)}) %collective-permute-start.14) | collective-permute-done | bytes 1572896 | tf_op jit(solution)/shard_map/ppermute | solution.py:372
  149.2 4.2 %total.26.refs_0_.refs_4_.refs_8_ = f32[768,1024]{1,0:T(8,128)} custom-call(bf16[768,1024]{1,0:T(8,128)(2,1)S(1)} %copy-done.10, bf16[768,1024]{1,0:T(8,128)(2,1)} %copy-done.3, bf16[768,1024]{1,0:T(8,128)(2,1)} %collective-permute-done.14.refs_2_.refs_6_, bf16[384,1024]{1,0:T(8,128)(2,1)S(1)} %collective-permute-done.13.refs_3_, ...), custom_call_target="tpu_custom_call" | custom-call | flops 1 | bytes 1 | tf_op jit(solution)/shard_map/total/pallas_call | solution.py:26
  153.4 4.1 %collective-permute-done.17.refs_2_.refs_6_ = bf16[768,1024]{1,0:T(8,128)(2,1)S(1)} collective-permute-done((bf16[768,1024]{1,0:T(8,128)(2,1)S(1)}, bf16[768,1024]{1,0:T(8,128)(2,1)S(1)}, u32[]{:S(2)}, u32[]{:S(2)}) %collective-permute-start.17) | collective-permute-done | bytes 1572896 | tf_op jit(solution)/shard_map/ppermute | solution.py:379
  157.5 20.6 %collective-permute-done.18.refs_3_.refs_7_ = bf16[768,1024]{1,0:T(8,128)(2,1)} collective-permute-done((bf16[768,1024]{1,0:T(8,128)(2,1)S(1)}, bf16[768,1024]{1,0:T(8,128)(2,1)}, u32[]{:S(2)}, u32[]{:S(2)}) %collective-permute-start.18) | collective-permute-done | bytes 1572896 | tf_op jit(solution)/shard_map/ppermute | solution.py:379
  178.2 3.8 %total.27 = bf16[768,1024]{1,0:T(8,128)(2,1)} custom-call(f32[768,1024]{1,0:T(8,128)} %total.26.refs_0_.refs_4_.refs_8_, bf16[384,1024]{1,0:T(8,128)(2,1)S(1)} %collective-permute-done.16.refs_1_, bf16[768,1024]{1,0:T(8,128)(2,1)S(1)} %collective-permute-done.17.refs_2_.refs_6_, bf16[768,1024]{1,0:T(8,128)(2,1)} %collective-permute-done.18.refs_3_.refs_7_, ...), custom_call_target="tpu_custom_call" | custom-call | flops 1 | bytes 1 | tf_op jit(solution)/shard_map/total/pallas_call | solution.py:26
  (72 shorter events, 9.5 us)
Async XLA Ops:
  0.0 10.9 %collective-permute-start = (s32[192]{0:T(256)}, s32[192]{0:T(256)S(1)}, u32[]{:S(2)}, u32[]{:S(2)}) collective-permute-start(s32[192]{0:T(256)} %param.7), channel_id=1, source_target_pairs={{0,1},{1,0},{2,3},{3,2},{4,5},{5,4},{6,7},{7,6},{8,9},{9,8},{10,11... | collective-permute-start | bytes 2312 | tf_op jit(solution)/shard_map/ppermute | solution.py:385
  0.5 12.9 %collective-permute-start.1 = (bf16[768,1024]{1,0:T(8,128)(2,1)}, bf16[768,1024]{1,0:T(8,128)(2,1)}, u32[]{:S(2)}, u32[]{:S(2)}) collective-permute-start(bf16[768,1024]{1,0:T(8,128)(2,1)} %bitcast.6), channel_id=1, source_target_pairs={{0,1},{1,0},{2,3},{3,2},{4,5},{5,4},{6,7},{7,6},{8,9},{9,8},{10,11... | collective-permute-start | bytes 4718600 | tf_op jit(solution)/shard_map/ppermute | solution.py:385
  1.2 1.4 copy-start
  2.6 6.6 %copy-start.17 = (s32[192]{0:T(256)S(1)}, s32[192]{0:T(256)}, u32[]{:S(2)}) copy-start(s32[192]{0:T(256)} %param.7) | copy-start | bytes 2308
  2.6 10.8 %copy-start.1 = (bf16[4,192,1024]{2,1,0:T(8,128)(2,1)S(1)}, bf16[4,192,1024]{2,1,0:T(8,128)(2,1)}, u32[]{:S(2)}) copy-start(bf16[4,192,1024]{2,1,0:T(8,128)(2,1)} %param.6) | copy-start | bytes 4718596
  6.2 27.1 %collective-permute-start.3 = (bf16[480,1024]{1,0:T(8,128)(2,1)S(1)}, bf16[480,1024]{1,0:T(8,128)(2,1)S(1)}, u32[]{:S(2)}, u32[]{:S(2)}) collective-permute-start(bf16[480,1024]{1,0:T(8,128)(2,1)S(1)} %products.5.refs_6_), channel_id=1, source_target_pairs={{0,2},{2,0},{4,6},{6,4},{8,10},{10,8},{12,14},{14,12},{1,3},{3,1},... | collective-permute-start | bytes 2949128 | tf_op jit(solution)/shard_map/ppermute | solution.py:372
  9.5 0.5 copy-start.18
  11.1 0.5 copy-start.19
  13.4 0.9 copy-start.13
  14.3 0.9 copy-start.15
  24.8 23.8 %collective-permute-start.2 = (bf16[384,1024]{1,0:T(8,128)(2,1)S(1)}, bf16[384,1024]{1,0:T(8,128)(2,1)S(1)}, u32[]{:S(2)}, u32[]{:S(2)}) collective-permute-start(bf16[384,1024]{1,0:T(8,128)(2,1)S(1)} %products.6.refs_3_), channel_id=1, source_target_pairs={{0,2},{2,0},{4,6},{6,4},{8,10},{10,8},{12,14},{14,12},{1,3},{3,1},... | collective-permute-start | bytes 2359304 | tf_op jit(solution)/shard_map/ppermute | solution.py:372
  31.2 51.2 %collective-permute-start.7 = (bf16[768,1024]{1,0:T(8,128)(2,1)}, bf16[768,1024]{1,0:T(8,128)(2,1)}, u32[]{:S(2)}, u32[]{:S(2)}) collective-permute-start(bf16[768,1024]{1,0:T(8,128)(2,1)} %get-tuple-element.16.refs_2_), channel_id=1, source_target_pairs={{0,2},{2,0},{4,6},{6,4},{8,10},{10,8},{12,14},{14,12},{1,3},{3,1},... | collective-permute-start | bytes 4718600 | tf_op jit(solution)/shard_map/ppermute | solution.py:372
  35.5 32.9 %collective-permute-start.5 = (bf16[480,1024]{1,0:T(8,128)(2,1)S(1)}, bf16[480,1024]{1,0:T(8,128)(2,1)S(1)}, u32[]{:S(2)}, u32[]{:S(2)}) collective-permute-start(bf16[480,1024]{1,0:T(8,128)(2,1)S(1)} %total.14.refs_3_.refs_0_), channel_id=1, source_target_pairs={{0,4},{12,8},{2,6},{14,10},{1,5},{13,9},{3,7},{15,11},{16,20},{28,... | collective-permute-start | bytes 2949128 | tf_op jit(solution)/shard_map/ppermute | solution.py:379
  46.5 1.2 copy-start.8
  48.6 5.7 %copy-start.9 = (bf16[768,1024]{1,0:T(8,128)(2,1)S(1)}, bf16[768,1024]{1,0:T(8,128)(2,1)}, u32[]{:S(2)}) copy-start(bf16[768,1024]{1,0:T(8,128)(2,1)} %copy-done.8) | copy-start | bytes 4718596
  50.0 26.9 %collective-permute-start.4 = (bf16[384,1024]{1,0:T(8,128)(2,1)S(1)}, bf16[384,1024]{1,0:T(8,128)(2,1)S(1)}, u32[]{:S(2)}, u32[]{:S(2)}) collective-permute-start(bf16[384,1024]{1,0:T(8,128)(2,1)S(1)} %total.15.refs_3_.refs_0_.refs_2_.refs_1_), channel_id=1, source_target_pairs={{0,4},{12,8},{2,6},{14,10},{1,5},{13,9},{3,7},{15,11},{16,20},{28,... | collective-permute-start | bytes 2359304 | tf_op jit(solution)/shard_map/ppermute | solution.py:379
  54.3 61.8 %collective-permute-start.9 = (bf16[768,1024]{1,0:T(8,128)(2,1)S(1)}, bf16[768,1024]{1,0:T(8,128)(2,1)}, u32[]{:S(2)}, u32[]{:S(2)}) collective-permute-start(bf16[768,1024]{1,0:T(8,128)(2,1)S(1)} %hold.2), channel_id=1, source_target_pairs={{0,2},{2,0},{4,6},{6,4},{8,10},{10,8},{12,14},{14,12},{1,3},{3,1},... | collective-permute-start | bytes 4718600 | tf_op jit(solution)/shard_map/ppermute | solution.py:372
  66.0 1.2 copy-start.4
  67.2 1.1 copy-start.11
  70.5 11.9 %copy-start.7 = (bf16[768,1024]{1,0:T(8,128)(2,1)S(1)}, bf16[768,1024]{1,0:T(8,128)(2,1)}, u32[]{:S(2)}) copy-start(bf16[768,1024]{1,0:T(8,128)(2,1)} %get-tuple-element.20.refs_0_) | copy-start | bytes 4718596
  78.3 17.7 %collective-permute-start.6 = (bf16[384,1024]{1,0:T(8,128)(2,1)S(1)}, bf16[384,1024]{1,0:T(8,128)(2,1)S(1)}, u32[]{:S(2)}, u32[]{:S(2)}) collective-permute-start(bf16[384,1024]{1,0:T(8,128)(2,1)S(1)} %total.17.refs_2_), channel_id=1, source_target_pairs={{4,8},{8,4},{6,10},{10,6},{5,9},{9,5},{7,11},{11,7},{20,24},{24,20... | collective-permute-start | bytes 2359304 | tf_op jit(solution)/shard_map/ppermute | solution.py:379
  84.3 7.7 %copy-start.5 = (bf16[768,1024]{1,0:T(8,128)(2,1)S(1)}, bf16[768,1024]{1,0:T(8,128)(2,1)}, u32[]{:S(2)}) copy-start(bf16[768,1024]{1,0:T(8,128)(2,1)} %copy-done.4) | copy-start | bytes 4718596
  84.3 22.1 %collective-permute-start.10 = (bf16[384,1024]{1,0:T(8,128)(2,1)S(1)}, bf16[384,1024]{1,0:T(8,128)(2,1)S(1)}, u32[]{:S(2)}, u32[]{:S(2)}) collective-permute-start(bf16[384,1024]{1,0:T(8,128)(2,1)S(1)} %total.18.refs_2_.refs_0_), channel_id=1, source_target_pairs={{0,4},{12,8},{2,6},{14,10},{1,5},{13,9},{3,7},{15,11},{16,20},{28,... | collective-permute-start | bytes 2359304 | tf_op jit(solution)/shard_map/ppermute | solution.py:379
  88.5 40.1 %collective-permute-start.11 = (bf16[480,1024]{1,0:T(8,128)(2,1)S(1)}, bf16[480,1024]{1,0:T(8,128)(2,1)}, u32[]{:S(2)}, u32[]{:S(2)}) collective-permute-start(bf16[480,1024]{1,0:T(8,128)(2,1)S(1)} %total.16.refs_4_), channel_id=1, source_target_pairs={{4,8},{8,4},{6,10},{10,6},{5,9},{9,5},{7,11},{11,7},{20,24},{24,20... | collective-permute-start | bytes 2949128 | tf_op jit(solution)/shard_map/ppermute | solution.py:379
  91.9 34.8 %collective-permute-start.12 = (bf16[384,1024]{1,0:T(8,128)(2,1)S(1)}, bf16[384,1024]{1,0:T(8,128)(2,1)}, u32[]{:S(2)}, u32[]{:S(2)}) collective-permute-start(bf16[384,1024]{1,0:T(8,128)(2,1)S(1)} %total.19.refs_2_.refs_0_.refs_1_), channel_id=1, source_target_pairs={{0,4},{12,8},{2,6},{14,10},{1,5},{13,9},{3,7},{15,11},{16,20},{28,... | collective-permute-start | bytes 2359304 | tf_op jit(solution)/shard_map/ppermute | solution.py:379
  107.8 18.9 %collective-permute-start.13 = (bf16[384,1024]{1,0:T(8,128)(2,1)S(1)}, bf16[384,1024]{1,0:T(8,128)(2,1)S(1)}, u32[]{:S(2)}, u32[]{:S(2)}) collective-permute-start(bf16[384,1024]{1,0:T(8,128)(2,1)S(1)} %total.21.refs_2_), channel_id=1, source_target_pairs={{4,8},{8,4},{6,10},{10,6},{5,9},{9,5},{7,11},{11,7},{20,24},{24,20... | collective-permute-start | bytes 2359304 | tf_op jit(solution)/shard_map/ppermute | solution.py:379
  108.5 40.7 %collective-permute-start.14 = (bf16[768,1024]{1,0:T(8,128)(2,1)S(1)}, bf16[768,1024]{1,0:T(8,128)(2,1)}, u32[]{:S(2)}, u32[]{:S(2)}) collective-permute-start(bf16[768,1024]{1,0:T(8,128)(2,1)S(1)} %hold.3), channel_id=1, source_target_pairs={{0,2},{2,0},{4,6},{6,4},{8,10},{10,8},{12,14},{14,12},{1,3},{3,1},... | collective-permute-start | bytes 4718600 | tf_op jit(solution)/shard_map/ppermute | solution.py:372
  116.2 7.6 %collective-permute-start.8 = (bf16[96,1024]{1,0:T(8,128)(2,1)S(1)}, bf16[96,1024]{1,0:T(8,128)(2,1)S(1)}, u32[]{:S(2)}, u32[]{:S(2)}) collective-permute-start(bf16[96,1024]{1,0:T(8,128)(2,1)S(1)} %total.20.refs_2_), channel_id=1, source_target_pairs={{8,12},{4,0},{10,14},{6,2},{9,13},{5,1},{11,15},{7,3},{24,28},{20,... | collective-permute-start | bytes 589832 | tf_op jit(solution)/shard_map/ppermute | solution.py:379
  117.5 1.4 copy-start.12
  120.6 4.7 %copy-start.2 = (bf16[768,1024]{1,0:T(8,128)(2,1)}, bf16[768,1024]{1,0:T(8,128)(2,1)S(1)}, u32[]{:S(2)}) copy-start(bf16[768,1024]{1,0:T(8,128)(2,1)S(1)} %total.22.refs_4_.refs_0_.refs_2_) | copy-start | bytes 4718596
  123.7 33.8 %collective-permute-start.17 = (bf16[768,1024]{1,0:T(8,128)(2,1)S(1)}, bf16[768,1024]{1,0:T(8,128)(2,1)S(1)}, u32[]{:S(2)}, u32[]{:S(2)}) collective-permute-start(bf16[768,1024]{1,0:T(8,128)(2,1)S(1)} %total.22.refs_4_.refs_0_.refs_2_), channel_id=1, source_target_pairs={{0,4},{12,8},{2,6},{14,10},{1,5},{13,9},{3,7},{15,11},{16,20},{28,... | collective-permute-start | bytes 4718600 | tf_op jit(solution)/shard_map/ppermute | solution.py:379
  128.5 5.7 %copy-start.14 = (s32[192,1]{1,0:T(8,128)S(1)}, s32[192,1]{1,0:T(8,128)}, u32[]{:S(2)}) copy-start(s32[192,1]{1,0:T(8,128)} %copy.13.refs_3_.refs_2_) | copy-start | bytes 2308
  128.6 5.7 %copy-start.16 = (s32[192,1]{1,0:T(8,128)S(1)}, s32[192,1]{1,0:T(8,128)}, u32[]{:S(2)}) copy-start(s32[192,1]{1,0:T(8,128)} %copy.14.refs_4_.refs_3_) | copy-start | bytes 2308
  131.1 3.2 %copy-start.6 = (bf16[768,1024]{1,0:T(8,128)(2,1)}, bf16[768,1024]{1,0:T(8,128)(2,1)S(1)}, u32[]{:S(2)}) copy-start(bf16[768,1024]{1,0:T(8,128)(2,1)S(1)} %total.25.refs_5_) | copy-start | bytes 4718596
  131.1 18.2 %copy-start.10 = (bf16[768,1024]{1,0:T(8,128)(2,1)S(1)}, bf16[768,1024]{1,0:T(8,128)(2,1)}, u32[]{:S(2)}) copy-start(bf16[768,1024]{1,0:T(8,128)(2,1)} %get-tuple-element.18.refs_0_.refs_4_) | copy-start | bytes 4718596
  131.1 47.1 %collective-permute-start.18 = (bf16[768,1024]{1,0:T(8,128)(2,1)S(1)}, bf16[768,1024]{1,0:T(8,128)(2,1)}, u32[]{:S(2)}, u32[]{:S(2)}) collective-permute-start(bf16[768,1024]{1,0:T(8,128)(2,1)S(1)} %total.25.refs_5_), channel_id=1, source_target_pairs={{8,12},{4,0},{10,14},{6,2},{9,13},{5,1},{11,15},{7,3},{24,28},{20,... | collective-permute-start | bytes 4718600 | tf_op jit(solution)/shard_map/ppermute | solution.py:379
  132.6 16.6 %collective-permute-start.15 = (bf16[384,1024]{1,0:T(8,128)(2,1)S(1)}, bf16[384,1024]{1,0:T(8,128)(2,1)}, u32[]{:S(2)}, u32[]{:S(2)}) collective-permute-start(bf16[384,1024]{1,0:T(8,128)(2,1)S(1)} %total.24.refs_4_), channel_id=1, source_target_pairs={{4,8},{8,4},{6,10},{10,6},{5,9},{9,5},{7,11},{11,7},{20,24},{24,20... | collective-permute-start | bytes 2359304 | tf_op jit(solution)/shard_map/ppermute | solution.py:379
  141.0 1.1 copy-start.3
  142.2 15.3 %collective-permute-start.16 = (bf16[384,1024]{1,0:T(8,128)(2,1)}, bf16[384,1024]{1,0:T(8,128)(2,1)S(1)}, u32[]{:S(2)}, u32[]{:S(2)}) collective-permute-start(bf16[384,1024]{1,0:T(8,128)(2,1)} %get-tuple-element.23), channel_id=1, source_target_pairs={{0,1},{1,0},{2,3},{3,2},{4,5},{5,4},{6,7},{7,6},{8,9},{9,8},{10,11... | collective-permute-start | bytes 2359304 | tf_op jit(solution)/shard_map/ppermute | solution.py:385
  149.2 8.3 %collective-permute-start.19 = (bf16[384,1024]{1,0:T(8,128)(2,1)}, bf16[384,1024]{1,0:T(8,128)(2,1)S(1)}, u32[]{:S(2)}, u32[]{:S(2)}) collective-permute-start(bf16[384,1024]{1,0:T(8,128)(2,1)} %get-tuple-element.24), channel_id=1, source_target_pairs={{0,1},{1,0},{2,3},{3,2},{4,5},{5,4},{6,7},{7,6},{8,9},{9,8},{10,11... | collective-permute-start | bytes 2359304 | tf_op jit(solution)/shard_map/ppermute | solution.py:385

commit v11 on v10

--- a/solution.py
+++ b/solution.py
@@ -413,7 +413,7 @@
     starts = jnp.asarray(np.asarray(blocks, np.int32) * out_width)[place]
     low_rows = 2 * (owners * count // 2) * adapter_down_maps.shape[1] // out_width
     even = [(p * count // PARTS, count // PARTS) for p in range(PARTS)]
-    uneven = [(0, count // 2 + low_rows), (count // 2 + low_rows, count // 2 - low_rows)]
+    uneven = [(0, (count + low_rows) // 2), ((count + low_rows) // 2, (count - low_rows) // 2)]
     away_part, own_all, from_y, sums, arrived = {}, {}, {}, {}, {}
 
     def split(k):
@@ -505,8 +505,6 @@
     low_sum = deltas = None
     for h, m, p in line_order():
         k = slot_of(h, m)
-        if (h, m, p) == (1, 1, 1):
-            last[0] += (arrived[1, 1, 0],)
         line(h, m, p)
         if h == 0:
             if k == 0 and p == 0:
@@ -520,6 +518,7 @@
         if (h, k, p) == (0, 1, len(cut_of(h, m)) - 1):
             low_at = uneven[LOW_WITH[1]][1]
             pieces = [(sums[LOW_WITH], low_at)]
+            last[0] += (arrived[1, 0, 0],) if nz > 2 else ()
             for step in range(nz - 1):
                 if step >= 2:
                     prefix = then(total, [(low_rows, [pieces[0], pieces[-1]])])
@@ -529,6 +528,7 @@
         if (h, m, p) == LOW_SUM_AFTER:
             low_sum = then(total, [(low_rows, pieces)])
         if deltas is None and low_sum is not None and EXPAND_AFTER in arrived:
+            last[0] += (arrived[1, 1, 0],) if nz > 2 else ()
             deltas = then(expand, low_sum, slot_sets, adapter_up_maps, names)
             back = [
                 [(*cut, pass_on(deltas[1 + (shift - 1) * PARTS + p], -shift), 0) for p, cut in enumerate(even)]

time: 182 us -> 169 us (0.929)
  waiting for transfers between devices: 61.3 us -> 51.7 us
  local copies, waits for them, and re-layouts: 12.6 us -> 8.99 us
    ppermute x11, waiting for transfers between devices: 43.8 us -> 22.7 us  [hop(): return lax.ppermute(value, 'tensor', pairs)]
    ppermute x5, waiting for transfers between devices: 17.5 us -> 28.9 us  [swap_y(): return lax.ppermute(value, 'tensor', [(t, t ^ 1) for t in range(n)])]
    unnamed x40 -> x46, local copies, waits for them, and re-layouts: 10.4 us -> 8.06 us
  transfers between devices with their start and end apart: 20 -> 20, of which waited for: 9 -> 9; matrix products, arithmetic and copies ran while one was open for 2% -> 1% of each run, Pallas kernels for 38% -> 40%
where the time goes in v11:
time: 169 us; the launch traced here: 168 us
  Pallas kernels  71.7 us (42%)
  waiting for transfers between devices  51.7 us (31%)
  starting transfers between devices  33.3 us (20%)
  local copies, waits for them, and re-layouts  8.99 us (5%)
    pallas_call x23, Pallas kernels, call(): pl.pallas_call(body, grid_spec=pltpu.PrefetchScalarGridSpec(num_scalar_pr...  71.7 us
    ppermute x5, waiting for transfers between devices, swap_y(): return lax.ppermute(value, 'tensor', [(t, t ^ 1) for t in range(n)])  28.9 us
    ppermute x11, starting transfers between devices, hop(): return lax.ppermute(value, 'tensor', pairs)  24.9 us
    ppermute x11, waiting for transfers between devices, hop(): return lax.ppermute(value, 'tensor', pairs)  22.7 us
    unnamed x46, local copies, waits for them, and re-layouts  8.06 us
    ppermute x5, starting transfers between devices, swap_y(): return lax.ppermute(value, 'tensor', [(t, t ^ 1) for t in range(n)])  7.81 us
  transfers between devices with their start and end apart: 20, of which 9 were waited for; matrix products, arithmetic and copies ran while one was open for 1% of the time, Pallas kernels for 40%

profile of v11, /device:TPU:0, one launch (start us, length us, event | category | flops | bytes accessed | tf_op | source)
XLA Modules:
  0.0 167.9 jit_solution(137773091225247314)
XLA Ops:
  1.2 1.4 copy-done
  2.6 3.4 %products.5.refs_6_ = bf16[432,1024]{1,0:T(8,128)(2,1)S(1)} custom-call(s32[8]{0:T(128)S(1)} %dynamic-slice_bitcast_fusion.refs_0_, bf16[768,1024]{1,0:T(8,128)(2,1)S(1)} %bitcast.10, bf16[1024,8192]{1,0:T(8,128)(2,1)} %refs_2_.9), custom_call_target="tpu_custom_call" | custom-call | flops 1 | bytes 1 | tf_op jit(solution)/shard_map/products/pallas_call | solution.py:26
  6.0 3.0 %collective-permute-start.3 = (bf16[432,1024]{1,0:T(8,128)(2,1)S(1)}, bf16[432,1024]{1,0:T(8,128)(2,1)S(1)}, u32[]{:S(2)}, u32[]{:S(2)}) collective-permute-start(bf16[432,1024]{1,0:T(8,128)(2,1)S(1)} %products.5.refs_6_), channel_id=1, source_target_pairs={{0,2},{2,0},{4,6},{6,4},{8,10},{10,8},{12,14},{14,12},{1,3},{3,1},... | collective-permute-start | bytes 2654216 | tf_op jit(solution)/shard_map/ppermute | solution.py:372
  12.0 6.6 %low_rank.1.refs_3_.refs_4_.refs_2_ = bf16[96,1024]{1,0:T(8,128)(2,1)S(1)} custom-call(s32[32]{0:T(128)S(1)} %pad_add_fusion.refs_0_, bf16[768,1024]{1,0:T(8,128)(2,1)S(1)} %bitcast.11, bf16[768,1024]{1,0:T(8,128)(2,1)} %collective-permute-done.1.refs_2_, s32[192,1]{1,0:T(8,128)S(1)} %copy.13.refs_3_.refs_2_, s32[192,1]{1,0:T(8,128)S(1)} %copy.14.refs_4_.refs_3_, ...), custom_call_target="tpu_custom_call" | custom-call | flops 1 | bytes 1 | tf_op jit(solution)/shard_map/low_rank/pallas_call | solution.py:26
  18.6 3.0 %products.6.refs_3_ = bf16[432,1024]{1,0:T(8,128)(2,1)S(1)} custom-call(s32[8]{0:T(128)S(1)} %dynamic-slice_bitcast_fusion.refs_0_, bf16[768,1024]{1,0:T(8,128)(2,1)S(1)} %bitcast.12, bf16[1024,8192]{1,0:T(8,128)(2,1)} %refs_2_.9, bf16[96,1024]{1,0:T(8,128)(2,1)S(1)} %low_rank.1.refs_3_.refs_4_.refs_2_, bf16[96,1024]{1,0:T(8,128)(2,1)S(1)} %low_rank.1.refs_3_.refs_4_.refs_2_), custom_call_target="tpu_custom_call" | custom-call | flops 1 | bytes 1 | tf_op jit(solution)/shard_map/products/pallas_call | solution.py:26
  21.7 6.4 %products.7 = (bf16[768,1024]{1,0:T(8,128)(2,1)S(1)}, bf16[768,1024]{1,0:T(8,128)(2,1)S(1)}) custom-call(s32[8]{0:T(128)S(1)} %dynamic-slice_bitcast_fusion.refs_0_, bf16[768,1024]{1,0:T(8,128)(2,1)} %bitcast.7, bf16[1024,8192]{1,0:T(8,128)(2,1)} %refs_2_.9, bf16[432,1024]{1,0:T(8,128)(2,1)S(1)} %products.6.refs_3_), custom_call_target="tpu_custom_call" | custom-call | flops 1 | bytes 1 | tf_op jit(solution)/shard_map/products/pallas_call | solution.py:26
  28.2 1.3 collective-permute-done.3.refs_1_
  29.5 1.8 %total.14.refs_3_.refs_0_ = bf16[432,1024]{1,0:T(8,128)(2,1)S(1)} custom-call(bf16[768,1024]{1,0:T(8,128)(2,1)S(1)} %get-tuple-element.15.refs_0_, bf16[432,1024]{1,0:T(8,128)(2,1)S(1)} %collective-permute-done.3.refs_1_, bf16[768,1024]{1,0:T(8,128)(2,1)} %copy-done.15), custom_call_target="tpu_custom_call" | custom-call | flops 1 | bytes 1 | tf_op jit(solution)/shard_map/total/pallas_call | solution.py:26
  31.3 4.1 %collective-permute-start.5 = (bf16[432,1024]{1,0:T(8,128)(2,1)S(1)}, bf16[432,1024]{1,0:T(8,128)(2,1)S(1)}, u32[]{:S(2)}, u32[]{:S(2)}) collective-permute-start(bf16[432,1024]{1,0:T(8,128)(2,1)S(1)} %total.14.refs_3_.refs_0_), channel_id=1, source_target_pairs={{0,4},{12,8},{2,6},{14,10},{1,5},{13,9},{3,7},{15,11},{16,20},{28,... | collective-permute-start | bytes 2654216 | tf_op jit(solution)/shard_map/ppermute | solution.py:379
  35.3 1.6 collective-permute-start.7
  36.9 6.4 %products.8 = (bf16[768,1024]{1,0:T(8,128)(2,1)S(1)}, bf16[768,1024]{1,0:T(8,128)(2,1)S(1)}) custom-call(s32[8]{0:T(128)S(1)} %dynamic-slice_bitcast_fusion.refs_0_, bf16[768,1024]{1,0:T(8,128)(2,1)} %bitcast.8, bf16[1024,8192]{1,0:T(8,128)(2,1)} %refs_2_.9, bf16[432,1024]{1,0:T(8,128)(2,1)S(1)} %total.14.refs_3_.refs_0_), custom_call_target="tpu_custom_call" | custom-call | flops 1 | bytes 1 | tf_op jit(solution)/shard_map/products/pallas_call | solution.py:26
  43.4 1.2 copy-done.6
  44.6 3.9 %collective-permute-done.2.refs_1_.refs_3_ = bf16[432,1024]{1,0:T(8,128)(2,1)S(1)} collective-permute-done((bf16[432,1024]{1,0:T(8,128)(2,1)S(1)}, bf16[432,1024]{1,0:T(8,128)(2,1)S(1)}, u32[]{:S(2)}, u32[]{:S(2)}) %collective-permute-start.2) | collective-permute-done | bytes 884768 | tf_op jit(solution)/shard_map/ppermute | solution.py:372
  48.5 1.8 %total.15.refs_3_.refs_0_.refs_2_.refs_1_ = bf16[432,1024]{1,0:T(8,128)(2,1)S(1)} custom-call(bf16[768,1024]{1,0:T(8,128)(2,1)S(1)} %get-tuple-element.15.refs_0_, bf16[432,1024]{1,0:T(8,128)(2,1)S(1)} %collective-permute-done.2.refs_1_.refs_3_, bf16[96,1024]{1,0:T(8,128)(2,1)S(1)} %low_rank.1.refs_3_.refs_4_.refs_2_, ...), custom_call_target="tpu_custom_call" | custom-call | flops 1 | bytes 1 | tf_op jit(solution)/shard_map/total/pallas_call | solution.py:26
  50.3 4.3 %collective-permute-start.4 = (bf16[432,1024]{1,0:T(8,128)(2,1)S(1)}, bf16[432,1024]{1,0:T(8,128)(2,1)S(1)}, u32[]{:S(2)}, u32[]{:S(2)}) collective-permute-start(bf16[432,1024]{1,0:T(8,128)(2,1)S(1)} %total.15.refs_3_.refs_0_.refs_2_.refs_1_), channel_id=1, source_target_pairs={{0,4},{12,8},{2,6},{14,10},{1,5},{13,9},{3,7},{15,11},{16,20},{28,... | collective-permute-start | bytes 2654216 | tf_op jit(solution)/shard_map/ppermute | solution.py:379
  54.5 10.1 %products.9 = (bf16[768,1024]{1,0:T(8,128)(2,1)S(1)}, bf16[768,1024]{1,0:T(8,128)(2,1)S(1)}, bf16[768,1024]{1,0:T(8,128)(2,1)}) custom-call(s32[8]{0:T(128)S(1)} %dynamic-slice_bitcast_fusion.refs_0_, bf16[768,1024]{1,0:T(8,128)(2,1)} %bitcast.9, bf16[1024,8192]{1,0:T(8,128)(2,1)} %refs_2_.9, bf16[432,1024]{1,0:T(8,128)(2,1)S(1)} %total.15.refs_3_.refs_0_.refs_2_.refs_1_), custom_call_target="tpu_custom_call" | custom-call | flops 1 | bytes 1 | tf_op jit(solution)/shard_map/products/pallas_call | solution.py:26
  64.6 1.1 copy-done.3
  65.7 1.2 copy-done.13
  66.9 2.1 %total.16.refs_4_ = bf16[432,1024]{1,0:T(8,128)(2,1)} custom-call(bf16[432,1024]{1,0:T(8,128)(2,1)S(1)} %total.14.refs_3_.refs_0_, bf16[432,1024]{1,0:T(8,128)(2,1)S(1)} %collective-permute-done.5.refs_1_, bf16[768,1024]{1,0:T(8,128)(2,1)} %copy-done.3), custom_call_target="tpu_custom_call" | custom-call | flops 1 | bytes 1 | tf_op jit(solution)/shard_map/total/pallas_call | solution.py:26
  69.8 1.6 collective-permute-start.10
  71.4 1.5 collective-permute-done.4.refs_1_.refs_3_
  72.8 1.8 %total.17.refs_2_ = bf16[432,1024]{1,0:T(8,128)(2,1)S(1)} custom-call(bf16[432,1024]{1,0:T(8,128)(2,1)S(1)} %total.15.refs_3_.refs_0_.refs_2_.refs_1_, bf16[432,1024]{1,0:T(8,128)(2,1)S(1)} %collective-permute-done.4.refs_1_.refs_3_, bf16[432,1024]{1,0:T(8,128)(2,1)S(1)} %total.15.refs_3_.refs_0_.refs_2_.refs_1_, ...), custom_call_target="tpu_custom_call" | custom-call | flops 1 | bytes 1 | tf_op jit(solution)/shard_map/total/pallas_call | solution.py:26
  75.3 6.9 %collective-permute-done.7.refs_1_ = bf16[768,1024]{1,0:T(8,128)(2,1)} collective-permute-done((bf16[768,1024]{1,0:T(8,128)(2,1)}, bf16[768,1024]{1,0:T(8,128)(2,1)}, u32[]{:S(2)}, u32[]{:S(2)}) %collective-permute-start.7) | collective-permute-done | bytes 1572896 | tf_op jit(solution)/shard_map/ppermute | solution.py:372
  82.3 1.8 %total.18.refs_2_.refs_0_ = bf16[384,1024]{1,0:T(8,128)(2,1)S(1)} custom-call(bf16[768,1024]{1,0:T(8,128)(2,1)S(1)} %get-tuple-element.20.refs_0_, bf16[768,1024]{1,0:T(8,128)(2,1)} %collective-permute-done.7.refs_1_, bf16[432,1024]{1,0:T(8,128)(2,1)S(1)} %total.17.refs_2_), custom_call_target="tpu_custom_call" | custom-call | flops 1 | bytes 1 | tf_op jit(solution)/shard_map/total/pallas_call | solution.py:26
  84.1 4.2 %collective-permute-start.11 = (bf16[384,1024]{1,0:T(8,128)(2,1)S(1)}, bf16[384,1024]{1,0:T(8,128)(2,1)S(1)}, u32[]{:S(2)}, u32[]{:S(2)}) collective-permute-start(bf16[384,1024]{1,0:T(8,128)(2,1)S(1)} %total.18.refs_2_.refs_0_), channel_id=1, source_target_pairs={{0,4},{12,8},{2,6},{14,10},{1,5},{13,9},{3,7},{15,11},{16,20},{28,... | collective-permute-start | bytes 2359304 | tf_op jit(solution)/shard_map/ppermute | solution.py:379
  88.3 1.8 %total.19.refs_2_.refs_0_.refs_1_ = bf16[384,1024]{1,0:T(8,128)(2,1)S(1)} custom-call(bf16[768,1024]{1,0:T(8,128)(2,1)S(1)} %get-tuple-element.20.refs_0_, bf16[768,1024]{1,0:T(8,128)(2,1)} %collective-permute-done.7.refs_1_, bf16[384,1024]{1,0:T(8,128)(2,1)S(1)} %total.18.refs_2_.refs_0_), custom_call_target="tpu_custom_call" | custom-call | flops 1 | bytes 1 | tf_op jit(solution)/shard_map/total/pallas_call | solution.py:26
  90.1 2.2 %collective-permute-start.12 = (bf16[384,1024]{1,0:T(8,128)(2,1)S(1)}, bf16[384,1024]{1,0:T(8,128)(2,1)}, u32[]{:S(2)}, u32[]{:S(2)}) collective-permute-start(bf16[384,1024]{1,0:T(8,128)(2,1)S(1)} %total.19.refs_2_.refs_0_.refs_1_), channel_id=1, source_target_pairs={{0,4},{12,8},{2,6},{14,10},{1,5},{13,9},{3,7},{15,11},{16,20},{28,... | collective-permute-start | bytes 2359304 | tf_op jit(solution)/shard_map/ppermute | solution.py:379
  92.3 1.5 collective-permute-start.14
  93.8 0.8 total.20.refs_2_
  94.7 1.4 collective-permute-start.9
  96.1 10.1 %collective-permute-done.11.refs_1_ = bf16[384,1024]{1,0:T(8,128)(2,1)S(1)} collective-permute-done((bf16[384,1024]{1,0:T(8,128)(2,1)S(1)}, bf16[384,1024]{1,0:T(8,128)(2,1)S(1)}, u32[]{:S(2)}, u32[]{:S(2)}) %collective-permute-start.11) | collective-permute-done | bytes 786464 | tf_op jit(solution)/shard_map/ppermute | solution.py:379
  106.2 1.4 total.21.refs_2_
  108.3 7.7 %collective-permute-done.10.refs_1_ = bf16[768,1024]{1,0:T(8,128)(2,1)} collective-permute-done((bf16[768,1024]{1,0:T(8,128)(2,1)S(1)}, bf16[768,1024]{1,0:T(8,128)(2,1)}, u32[]{:S(2)}, u32[]{:S(2)}) %collective-permute-start.10) | collective-permute-done | bytes 1572896 | tf_op jit(solution)/shard_map/ppermute | solution.py:372
  116.0 1.7 %total.22.refs_4_.refs_0_.refs_2_ = bf16[768,1024]{1,0:T(8,128)(2,1)S(1)} custom-call(bf16[768,1024]{1,0:T(8,128)(2,1)S(1)} %copy-done.14, bf16[768,1024]{1,0:T(8,128)(2,1)} %collective-permute-done.10.refs_1_, bf16[384,1024]{1,0:T(8,128)(2,1)S(1)} %total.21.refs_2_), custom_call_target="tpu_custom_call" | custom-call | flops 1 | bytes 1 | tf_op jit(solution)/shard_map/total/pallas_call | solution.py:26
  117.7 4.1 %collective-permute-start.17 = (bf16[768,1024]{1,0:T(8,128)(2,1)S(1)}, bf16[768,1024]{1,0:T(8,128)(2,1)S(1)}, u32[]{:S(2)}, u32[]{:S(2)}) collective-permute-start(bf16[768,1024]{1,0:T(8,128)(2,1)S(1)} %total.22.refs_4_.refs_0_.refs_2_), channel_id=1, source_target_pairs={{0,4},{12,8},{2,6},{14,10},{1,5},{13,9},{3,7},{15,11},{16,20},{28,... | collective-permute-start | bytes 4718600 | tf_op jit(solution)/shard_map/ppermute | solution.py:379
  121.9 1.4 total.23.refs_2_.refs_1_
  123.3 1.9 %total.24.refs_4_ = bf16[384,1024]{1,0:T(8,128)(2,1)S(1)} custom-call(bf16[384,1024]{1,0:T(8,128)(2,1)S(1)} %total.19.refs_2_.refs_0_.refs_1_, bf16[384,1024]{1,0:T(8,128)(2,1)} %collective-permute-done.12.refs_1_, bf16[96,1024]{1,0:T(8,128)(2,1)S(1)} %total.23.refs_2_.refs_1_), custom_call_target="tpu_custom_call" | custom-call | flops 1 | bytes 1 | tf_op jit(solution)/shard_map/total/pallas_call | solution.py:26
  125.2 2.3 %total.25.refs_5_ = bf16[768,1024]{1,0:T(8,128)(2,1)S(1)} custom-call(bf16[768,1024]{1,0:T(8,128)(2,1)} %copy-done.2, bf16[432,1024]{1,0:T(8,128)(2,1)S(1)} %copy-done.10, bf16[768,1024]{1,0:T(8,128)(2,1)} %copy-done.2, bf16[432,1024]{1,0:T(8,128)(2,1)S(1)} %collective-permute-done.6.refs_1_.refs_2_.refs_3_, bf16[384,1024]{1,0:T(8,128)(2,1)S(1)} %total.24.refs_4_), custom_call_target="tpu_custom_call" | custom-call | flops 1 | bytes 1 | tf_op jit(solution)/shard_map/total/pallas_call | solution.py:26
  127.5 1.6 collective-permute-start.18
  129.1 0.9 collective-permute-start.15
  130.1 0.9 copy-done.11
  131.0 1.1 copy-done.12
  132.1 7.7 %expand.1 = (bf16[768,1024]{1,0:T(8,128)(2,1)}, bf16[384,1024]{1,0:T(8,128)(2,1)S(1)}, bf16[384,1024]{1,0:T(8,128)(2,1)S(1)}) custom-call(s32[32]{0:T(128)S(1)} %pad_add_fusion.refs_0_, bf16[96,1024]{1,0:T(8,128)(2,1)S(1)} %total.23.refs_2_.refs_1_, s32[192,1]{1,0:T(8,128)S(1)} %copy-done.17, s32[192,1]{1,0:T(8,128)S(1)} %copy-done.19, ...), custom_call_target="tpu_custom_call" | custom-call | flops 1 | bytes 1 | tf_op jit(solution)/shard_map/expand/pallas_call | solution.py:26
  139.9 9.2 %collective-permute-done.14.refs_2_.refs_6_ = bf16[768,1024]{1,0:T(8,128)(2,1)} collective-permute-done((bf16[768,1024]{1,0:T(8,128)(2,1)S(1)}, bf16[768,1024]{1,0:T(8,128)(2,1)}, u32[]{:S(2)}, u32[]{:S(2)}) %collective-permute-start.14) | collective-permute-done | bytes 1572896 | tf_op jit(solution)/shard_map/ppermute | solution.py:372
  149.0 3.8 %total.26.refs_0_.refs_4_.refs_8_ = f32[768,1024]{1,0:T(8,128)} custom-call(bf16[768,1024]{1,0:T(8,128)(2,1)S(1)} %copy-done.8, bf16[768,1024]{1,0:T(8,128)(2,1)} %get-tuple-element.22.refs_1_.refs_5_.refs_8_, bf16[768,1024]{1,0:T(8,128)(2,1)} %collective-permute-done.14.refs_2_.refs_6_, bf16[384,1024]{1,0:T(8,128)(2,1)S(1)} %copy-done.12, ...), custom_call_target="tpu_custom_call" | custom-call | flops 1 | bytes 1 | tf_op jit(solution)/shard_map/total/pallas_call | solution.py:26
  152.9 1.1 collective-permute-done.17.refs_2_.refs_6_
  153.9 10.1 %collective-permute-done.18.refs_3_.refs_7_ = bf16[768,1024]{1,0:T(8,128)(2,1)} collective-permute-done((bf16[768,1024]{1,0:T(8,128)(2,1)S(1)}, bf16[768,1024]{1,0:T(8,128)(2,1)}, u32[]{:S(2)}, u32[]{:S(2)}) %collective-permute-start.18) | collective-permute-done | bytes 1572896 | tf_op jit(solution)/shard_map/ppermute | solution.py:379
  164.0 3.8 %total.27 = bf16[768,1024]{1,0:T(8,128)(2,1)} custom-call(f32[768,1024]{1,0:T(8,128)} %total.26.refs_0_.refs_4_.refs_8_, bf16[384,1024]{1,0:T(8,128)(2,1)S(1)} %collective-permute-done.16.refs_1_, bf16[768,1024]{1,0:T(8,128)(2,1)S(1)} %collective-permute-done.17.refs_2_.refs_6_, bf16[768,1024]{1,0:T(8,128)(2,1)} %collective-permute-done.18.refs_3_.refs_7_, ...), custom_call_target="tpu_custom_call" | custom-call | flops 1 | bytes 1 | tf_op jit(solution)/shard_map/total/pallas_call | solution.py:26
  (78 shorter events, 6.4 us)
Async XLA Ops:
  0.0 9.5 %collective-permute-start = (s32[192]{0:T(256)}, s32[192]{0:T(256)S(1)}, u32[]{:S(2)}, u32[]{:S(2)}) collective-permute-start(s32[192]{0:T(256)} %param.7), channel_id=1, source_target_pairs={{0,1},{1,0},{2,3},{3,2},{4,5},{5,4},{6,7},{7,6},{8,9},{9,8},{10,11... | collective-permute-start | bytes 2312 | tf_op jit(solution)/shard_map/ppermute | solution.py:385
  0.5 11.5 %collective-permute-start.1 = (bf16[768,1024]{1,0:T(8,128)(2,1)}, bf16[768,1024]{1,0:T(8,128)(2,1)}, u32[]{:S(2)}, u32[]{:S(2)}) collective-permute-start(bf16[768,1024]{1,0:T(8,128)(2,1)} %bitcast.6), channel_id=1, source_target_pairs={{0,1},{1,0},{2,3},{3,2},{4,5},{5,4},{6,7},{7,6},{8,9},{9,8},{10,11... | collective-permute-start | bytes 4718600 | tf_op jit(solution)/shard_map/ppermute | solution.py:385
  1.2 1.4 copy-start
  2.6 6.4 %copy-start.20 = (s32[192]{0:T(256)S(1)}, s32[192]{0:T(256)}, u32[]{:S(2)}) copy-start(s32[192]{0:T(256)} %param.7) | copy-start | bytes 2308
  2.6 9.3 %copy-start.1 = (bf16[4,192,1024]{2,1,0:T(8,128)(2,1)S(1)}, bf16[4,192,1024]{2,1,0:T(8,128)(2,1)}, u32[]{:S(2)}) copy-start(bf16[4,192,1024]{2,1,0:T(8,128)(2,1)} %param.6) | copy-start | bytes 4718596
  6.0 23.5 %collective-permute-start.3 = (bf16[432,1024]{1,0:T(8,128)(2,1)S(1)}, bf16[432,1024]{1,0:T(8,128)(2,1)S(1)}, u32[]{:S(2)}, u32[]{:S(2)}) collective-permute-start(bf16[432,1024]{1,0:T(8,128)(2,1)S(1)} %products.5.refs_6_), channel_id=1, source_target_pairs={{0,2},{2,0},{4,6},{6,4},{8,10},{10,8},{12,14},{14,12},{1,3},{3,1},... | collective-permute-start | bytes 2654216 | tf_op jit(solution)/shard_map/ppermute | solution.py:372
  9.5 9.0 %copy-start.16 = (s32[192,1]{1,0:T(8,128)}, s32[192,1]{1,0:T(8,128)S(1)}, u32[]{:S(2)}) copy-start(s32[192,1]{1,0:T(8,128)S(1)} %copy.13.refs_3_.refs_2_) | copy-start | bytes 2308
  9.7 0.5 copy-start.21
  10.3 0.5 copy-start.22
  11.1 7.5 %copy-start.18 = (s32[192,1]{1,0:T(8,128)}, s32[192,1]{1,0:T(8,128)S(1)}, u32[]{:S(2)}) copy-start(s32[192,1]{1,0:T(8,128)S(1)} %copy.14.refs_4_.refs_3_) | copy-start | bytes 2308
  21.6 26.8 %collective-permute-start.2 = (bf16[432,1024]{1,0:T(8,128)(2,1)S(1)}, bf16[432,1024]{1,0:T(8,128)(2,1)S(1)}, u32[]{:S(2)}, u32[]{:S(2)}) collective-permute-start(bf16[432,1024]{1,0:T(8,128)(2,1)S(1)} %products.6.refs_3_), channel_id=1, source_target_pairs={{0,2},{2,0},{4,6},{6,4},{8,10},{10,8},{12,14},{14,12},{1,3},{3,1},... | collective-permute-start | bytes 2654216 | tf_op jit(solution)/shard_map/ppermute | solution.py:372
  28.2 1.3 copy-start.15
  31.3 35.6 %collective-permute-start.5 = (bf16[432,1024]{1,0:T(8,128)(2,1)S(1)}, bf16[432,1024]{1,0:T(8,128)(2,1)S(1)}, u32[]{:S(2)}, u32[]{:S(2)}) collective-permute-start(bf16[432,1024]{1,0:T(8,128)(2,1)S(1)} %total.14.refs_3_.refs_0_), channel_id=1, source_target_pairs={{0,4},{12,8},{2,6},{14,10},{1,5},{13,9},{3,7},{15,11},{16,20},{28,... | collective-permute-start | bytes 2654216 | tf_op jit(solution)/shard_map/ppermute | solution.py:379
  35.3 46.9 %collective-permute-start.7 = (bf16[768,1024]{1,0:T(8,128)(2,1)}, bf16[768,1024]{1,0:T(8,128)(2,1)}, u32[]{:S(2)}, u32[]{:S(2)}) collective-permute-start(bf16[768,1024]{1,0:T(8,128)(2,1)} %copy-done.15), channel_id=1, source_target_pairs={{0,2},{2,0},{4,6},{6,4},{8,10},{10,8},{12,14},{14,12},{1,3},{3,1},... | collective-permute-start | bytes 4718600 | tf_op jit(solution)/shard_map/ppermute | solution.py:372
  43.4 1.2 copy-start.6
  50.3 22.6 %collective-permute-start.4 = (bf16[432,1024]{1,0:T(8,128)(2,1)S(1)}, bf16[432,1024]{1,0:T(8,128)(2,1)S(1)}, u32[]{:S(2)}, u32[]{:S(2)}) collective-permute-start(bf16[432,1024]{1,0:T(8,128)(2,1)S(1)} %total.15.refs_3_.refs_0_.refs_2_.refs_1_), channel_id=1, source_target_pairs={{0,4},{12,8},{2,6},{14,10},{1,5},{13,9},{3,7},{15,11},{16,20},{28,... | collective-permute-start | bytes 2654216 | tf_op jit(solution)/shard_map/ppermute | solution.py:379
  64.6 1.2 copy-start.3
  65.7 1.2 copy-start.13
  66.9 2.9 %copy-start.7 = (bf16[768,1024]{1,0:T(8,128)(2,1)S(1)}, bf16[768,1024]{1,0:T(8,128)(2,1)}, u32[]{:S(2)}) copy-start(bf16[768,1024]{1,0:T(8,128)(2,1)} %copy-done.6) | copy-start | bytes 4718596
  69.0 23.3 %collective-permute-start.8 = (bf16[432,1024]{1,0:T(8,128)(2,1)}, bf16[432,1024]{1,0:T(8,128)(2,1)S(1)}, u32[]{:S(2)}, u32[]{:S(2)}) collective-permute-start(bf16[432,1024]{1,0:T(8,128)(2,1)} %total.16.refs_4_), channel_id=1, source_target_pairs={{4,8},{8,4},{6,10},{10,6},{5,9},{9,5},{7,11},{11,7},{20,24},{24,20... | collective-permute-start | bytes 2654216 | tf_op jit(solution)/shard_map/ppermute | solution.py:379
  69.8 46.2 %collective-permute-start.10 = (bf16[768,1024]{1,0:T(8,128)(2,1)S(1)}, bf16[768,1024]{1,0:T(8,128)(2,1)}, u32[]{:S(2)}, u32[]{:S(2)}) collective-permute-start(bf16[768,1024]{1,0:T(8,128)(2,1)S(1)} %hold.2), channel_id=1, source_target_pairs={{0,2},{2,0},{4,6},{6,4},{8,10},{10,8},{12,14},{14,12},{1,3},{3,1},... | collective-permute-start | bytes 4718600 | tf_op jit(solution)/shard_map/ppermute | solution.py:372
  74.6 19.2 %collective-permute-start.6 = (bf16[432,1024]{1,0:T(8,128)(2,1)S(1)}, bf16[432,1024]{1,0:T(8,128)(2,1)S(1)}, u32[]{:S(2)}, u32[]{:S(2)}) collective-permute-start(bf16[432,1024]{1,0:T(8,128)(2,1)S(1)} %total.17.refs_2_), channel_id=1, source_target_pairs={{4,8},{8,4},{6,10},{10,6},{5,9},{9,5},{7,11},{11,7},{20,24},{24,20... | collective-permute-start | bytes 2654216 | tf_op jit(solution)/shard_map/ppermute | solution.py:379
  84.1 6.0 %copy-start.4 = (bf16[768,1024]{1,0:T(8,128)(2,1)S(1)}, bf16[768,1024]{1,0:T(8,128)(2,1)}, u32[]{:S(2)}) copy-start(bf16[768,1024]{1,0:T(8,128)(2,1)} %copy-done.3) | copy-start | bytes 4718596
  84.1 22.1 %collective-permute-start.11 = (bf16[384,1024]{1,0:T(8,128)(2,1)S(1)}, bf16[384,1024]{1,0:T(8,128)(2,1)S(1)}, u32[]{:S(2)}, u32[]{:S(2)}) collective-permute-start(bf16[384,1024]{1,0:T(8,128)(2,1)S(1)} %total.18.refs_2_.refs_0_), channel_id=1, source_target_pairs={{0,4},{12,8},{2,6},{14,10},{1,5},{13,9},{3,7},{15,11},{16,20},{28,... | collective-permute-start | bytes 2359304 | tf_op jit(solution)/shard_map/ppermute | solution.py:379
  90.1 33.2 %collective-permute-start.12 = (bf16[384,1024]{1,0:T(8,128)(2,1)S(1)}, bf16[384,1024]{1,0:T(8,128)(2,1)}, u32[]{:S(2)}, u32[]{:S(2)}) collective-permute-start(bf16[384,1024]{1,0:T(8,128)(2,1)S(1)} %total.19.refs_2_.refs_0_.refs_1_), channel_id=1, source_target_pairs={{0,4},{12,8},{2,6},{14,10},{1,5},{13,9},{3,7},{15,11},{16,20},{28,... | collective-permute-start | bytes 2359304 | tf_op jit(solution)/shard_map/ppermute | solution.py:379
  92.3 2.3 %copy-start.9 = (bf16[432,1024]{1,0:T(8,128)(2,1)}, bf16[432,1024]{1,0:T(8,128)(2,1)S(1)}, u32[]{:S(2)}) copy-start(bf16[432,1024]{1,0:T(8,128)(2,1)S(1)} %collective-permute-done.8.refs_3_.refs_1_) | copy-start | bytes 2654212
  92.3 56.7 %collective-permute-start.14 = (bf16[768,1024]{1,0:T(8,128)(2,1)S(1)}, bf16[768,1024]{1,0:T(8,128)(2,1)}, u32[]{:S(2)}, u32[]{:S(2)}) collective-permute-start(bf16[768,1024]{1,0:T(8,128)(2,1)S(1)} %hold.3), channel_id=1, source_target_pairs={{0,2},{2,0},{4,6},{6,4},{8,10},{10,8},{12,14},{14,12},{1,3},{3,1},... | collective-permute-start | bytes 4718600 | tf_op jit(solution)/shard_map/ppermute | solution.py:372
  94.6 21.3 %copy-start.14 = (bf16[768,1024]{1,0:T(8,128)(2,1)S(1)}, bf16[768,1024]{1,0:T(8,128)(2,1)}, u32[]{:S(2)}) copy-start(bf16[768,1024]{1,0:T(8,128)(2,1)} %copy-done.13) | copy-start | bytes 4718596
  94.7 27.2 %collective-permute-start.9 = (bf16[96,1024]{1,0:T(8,128)(2,1)S(1)}, bf16[96,1024]{1,0:T(8,128)(2,1)S(1)}, u32[]{:S(2)}, u32[]{:S(2)}) collective-permute-start(bf16[96,1024]{1,0:T(8,128)(2,1)S(1)} %total.20.refs_2_), channel_id=1, source_target_pairs={{8,12},{4,0},{10,14},{6,2},{9,13},{5,1},{11,15},{7,3},{24,28},{20,... | collective-permute-start | bytes 589832 | tf_op jit(solution)/shard_map/ppermute | solution.py:379
  107.6 22.5 %collective-permute-start.13 = (bf16[384,1024]{1,0:T(8,128)(2,1)S(1)}, bf16[384,1024]{1,0:T(8,128)(2,1)S(1)}, u32[]{:S(2)}, u32[]{:S(2)}) collective-permute-start(bf16[384,1024]{1,0:T(8,128)(2,1)S(1)} %total.21.refs_2_), channel_id=1, source_target_pairs={{4,8},{8,4},{6,10},{10,6},{5,9},{9,5},{7,11},{11,7},{20,24},{24,20... | collective-permute-start | bytes 2359304 | tf_op jit(solution)/shard_map/ppermute | solution.py:379
  117.7 4.2 %copy-start.2 = (bf16[768,1024]{1,0:T(8,128)(2,1)}, bf16[768,1024]{1,0:T(8,128)(2,1)S(1)}, u32[]{:S(2)}) copy-start(bf16[768,1024]{1,0:T(8,128)(2,1)S(1)} %total.22.refs_4_.refs_0_.refs_2_) | copy-start | bytes 4718596
  117.7 36.2 %collective-permute-start.17 = (bf16[768,1024]{1,0:T(8,128)(2,1)S(1)}, bf16[768,1024]{1,0:T(8,128)(2,1)S(1)}, u32[]{:S(2)}, u32[]{:S(2)}) collective-permute-start(bf16[768,1024]{1,0:T(8,128)(2,1)S(1)} %total.22.refs_4_.refs_0_.refs_2_), channel_id=1, source_target_pairs={{0,4},{12,8},{2,6},{14,10},{1,5},{13,9},{3,7},{15,11},{16,20},{28,... | collective-permute-start | bytes 4718600 | tf_op jit(solution)/shard_map/ppermute | solution.py:379
  123.3 1.9 %copy-start.10 = (bf16[432,1024]{1,0:T(8,128)(2,1)S(1)}, bf16[432,1024]{1,0:T(8,128)(2,1)}, u32[]{:S(2)}) copy-start(bf16[432,1024]{1,0:T(8,128)(2,1)} %copy-done.9) | copy-start | bytes 2654212
  125.2 5.8 %copy-start.17 = (s32[192,1]{1,0:T(8,128)S(1)}, s32[192,1]{1,0:T(8,128)}, u32[]{:S(2)}) copy-start(s32[192,1]{1,0:T(8,128)} %copy-done.16) | copy-start | bytes 2308
  125.2 5.8 %copy-start.19 = (s32[192,1]{1,0:T(8,128)S(1)}, s32[192,1]{1,0:T(8,128)}, u32[]{:S(2)}) copy-start(s32[192,1]{1,0:T(8,128)} %copy-done.18) | copy-start | bytes 2308
  127.5 2.5 %copy-start.5 = (bf16[768,1024]{1,0:T(8,128)(2,1)}, bf16[768,1024]{1,0:T(8,128)(2,1)S(1)}, u32[]{:S(2)}) copy-start(bf16[768,1024]{1,0:T(8,128)(2,1)S(1)} %total.25.refs_5_) | copy-start | bytes 4718596
  127.5 21.5 %copy-start.8 = (bf16[768,1024]{1,0:T(8,128)(2,1)S(1)}, bf16[768,1024]{1,0:T(8,128)(2,1)}, u32[]{:S(2)}) copy-start(bf16[768,1024]{1,0:T(8,128)(2,1)} %get-tuple-element.18.refs_0_.refs_4_) | copy-start | bytes 4718596
  127.5 36.5 %collective-permute-start.18 = (bf16[768,1024]{1,0:T(8,128)(2,1)S(1)}, bf16[768,1024]{1,0:T(8,128)(2,1)}, u32[]{:S(2)}, u32[]{:S(2)}) collective-permute-start(bf16[768,1024]{1,0:T(8,128)(2,1)S(1)} %total.25.refs_5_), channel_id=1, source_target_pairs={{8,12},{4,0},{10,14},{6,2},{9,13},{5,1},{11,15},{7,3},{24,28},{20,... | collective-permute-start | bytes 4718600 | tf_op jit(solution)/shard_map/ppermute | solution.py:379
  129.1 20.0 %collective-permute-start.15 = (bf16[384,1024]{1,0:T(8,128)(2,1)S(1)}, bf16[384,1024]{1,0:T(8,128)(2,1)S(1)}, u32[]{:S(2)}, u32[]{:S(2)}) collective-permute-start(bf16[384,1024]{1,0:T(8,128)(2,1)S(1)} %total.24.refs_4_), channel_id=1, source_target_pairs={{4,8},{8,4},{6,10},{10,6},{5,9},{9,5},{7,11},{11,7},{20,24},{24,20... | collective-permute-start | bytes 2359304 | tf_op jit(solution)/shard_map/ppermute | solution.py:379
  130.0 0.9 copy-start.11
  131.0 1.1 copy-start.12
  139.8 14.1 %collective-permute-start.16 = (bf16[384,1024]{1,0:T(8,128)(2,1)S(1)}, bf16[384,1024]{1,0:T(8,128)(2,1)S(1)}, u32[]{:S(2)}, u32[]{:S(2)}) collective-permute-start(bf16[384,1024]{1,0:T(8,128)(2,1)S(1)} %get-tuple-element.23), channel_id=1, source_target_pairs={{0,1},{1,0},{2,3},{3,2},{4,5},{5,4},{6,7},{7,6},{8,9},{9,8},{10,11... | collective-permute-start | bytes 2359304 | tf_op jit(solution)/shard_map/ppermute | solution.py:385
  149.0 4.9 %collective-permute-start.19 = (bf16[384,1024]{1,0:T(8,128)(2,1)S(1)}, bf16[384,1024]{1,0:T(8,128)(2,1)S(1)}, u32[]{:S(2)}, u32[]{:S(2)}) collective-permute-start(bf16[384,1024]{1,0:T(8,128)(2,1)S(1)} %get-tuple-element.24), channel_id=1, source_target_pairs={{0,1},{1,0},{2,3},{3,2},{4,5},{5,4},{6,7},{7,6},{8,9},{9,8},{10,11... | collective-permute-start | bytes 2359304 | tf_op jit(solution)/shard_map/ppermute | solution.py:385

commit v12 on v11

--- a/solution.py
+++ b/solution.py
@@ -12,7 +12,7 @@
 PARTS = 2
 LOW_WITH = (0, PARTS - 1)
 LOW_SUM_AFTER = (0, 2, 0)
-EXPAND_AFTER = (2, 0, 0)
+EXPAND_AFTER = (1, 1, 1)
 VMEM = 50 * 2**20
 ANY = pl.BlockSpec(memory_space=pl.ANY)
 
@@ -146,7 +146,8 @@
     tiles = []
     at = 0
     for r, (some, terms) in enumerate(runs):
-        size = -(-some // 32) * 16 if some * width > 2**17 else some
+        split = 4 if some * len(terms) > 2000 else 2 if some * width > 2**17 else 1
+        size = -(-some // (16 * split)) * 16
         for skip in range(0, some, size):
             tiles.append((r, skip, min(size, some - skip), at + skip))
         at += some
@@ -488,7 +489,7 @@
             ready[h, m, p] = there
             free[h] = max(there, free.get(h, 0.0)) + cut_of(h, m)[p][1]
             ready[h, m, p, "end"] = free[h]
-        return sorted(steps, key=lambda step: (ready[step], step[0]))
+        return sorted(steps, key=lambda step: (ready[step], step[0] and nz - step[0]))
 
     row_ids = [tenant] + [pass_on(tenant, shift) for shift in range(1, owners)]
     row_sets = [rows] + [pass_on(rows, shift) for shift in range(1, owners)]
@@ -537,7 +538,7 @@
     span = (0, count)
     early = [arrived_parts(h, nz - 2 - h) for h in range(1, nz - 2)]
     late = [arrived_parts(h, nz - 2 - h) for h in range(nz - 1) if not 1 <= h < nz - 2]
-    most = add_up(span, [whole(own_all[nz - 1]), whole(deltas[0]), y_parts(nz - 1)] + early, dtype=jnp.float32)
+    most = add_up(span, [whole(own_all[nz - 1]), whole(deltas[0]), y_parts(nz - 1)] + early)
     out = add_up(span, [whole(most)] + back + late)
     return out.reshape(steps, row_count, out_width)
 

time: 169 us -> 169 us (level)
  starting transfers between devices: 33.3 us -> 52.1 us
  waiting for transfers between devices: 51.7 us -> 36.1 us
  local copies, waits for them, and re-layouts: 8.99 us -> 6.94 us
    ppermute x11, starting transfers between devices: 24.9 us -> 43.1 us  [hop(): return lax.ppermute(value, 'tensor', pairs)]
    ppermute x5, waiting for transfers between devices: 28.9 us -> 19.5 us  [swap_y(): return lax.ppermute(value, 'tensor', [(t, t ^ 1) for t in range(n)])]
    ppermute x11, waiting for transfers between devices: 22.7 us -> 16.7 us  [hop(): return lax.ppermute(value, 'tensor', pairs)]
    unnamed x46 -> x38, local copies, waits for them, and re-layouts: 8.06 us -> 6.02 us
  transfers between devices with their start and end apart: 20 -> 20, of which waited for: 9 -> 7; matrix products, arithmetic and copies ran while one was open for 1% -> 1% of each run, Pallas kernels for 40% -> 40%
where the time goes in v12:
time: 169 us; the launch traced here: 168 us
  Pallas kernels  70.9 us (42%)
  starting transfers between devices  52.1 us (31%)
  waiting for transfers between devices  36.1 us (21%)
  local copies, waits for them, and re-layouts  6.94 us (4%)
    pallas_call x23, Pallas kernels, call(): pl.pallas_call(body, grid_spec=pltpu.PrefetchScalarGridSpec(num_scalar_pr...  70.9 us
    ppermute x11, starting transfers between devices, hop(): return lax.ppermute(value, 'tensor', pairs)  43.1 us
    ppermute x5, waiting for transfers between devices, swap_y(): return lax.ppermute(value, 'tensor', [(t, t ^ 1) for t in range(n)])  19.5 us
    ppermute x11, waiting for transfers between devices, hop(): return lax.ppermute(value, 'tensor', pairs)  16.7 us
    ppermute x5, starting transfers between devices, swap_y(): return lax.ppermute(value, 'tensor', [(t, t ^ 1) for t in range(n)])  8.36 us
    unnamed x38, local copies, waits for them, and re-layouts  6.02 us
  transfers between devices with their start and end apart: 20, of which 7 were waited for; matrix products, arithmetic and copies ran while one was open for 1% of the time, Pallas kernels for 40%

profile of v12, /device:TPU:0, one launch (start us, length us, event | category | flops | bytes accessed | tf_op | source)
XLA Modules:
  0.0 168.3 jit_solution(4574751156233340367)
XLA Ops:
  1.2 1.4 copy-done
  2.6 3.4 %products.5.refs_6_ = bf16[432,1024]{1,0:T(8,128)(2,1)S(1)} custom-call(s32[8]{0:T(128)S(1)} %dynamic-slice_bitcast_fusion.refs_0_, bf16[768,1024]{1,0:T(8,128)(2,1)S(1)} %bitcast.10, bf16[1024,8192]{1,0:T(8,128)(2,1)} %refs_2_.9), custom_call_target="tpu_custom_call" | custom-call | flops 1 | bytes 1 | tf_op jit(solution)/shard_map/products/pallas_call | solution.py:26
  6.0 3.0 %collective-permute-start.3 = (bf16[432,1024]{1,0:T(8,128)(2,1)S(1)}, bf16[432,1024]{1,0:T(8,128)(2,1)S(1)}, u32[]{:S(2)}, u32[]{:S(2)}) collective-permute-start(bf16[432,1024]{1,0:T(8,128)(2,1)S(1)} %products.5.refs_6_), channel_id=1, source_target_pairs={{0,2},{2,0},{4,6},{6,4},{8,10},{10,8},{12,14},{14,12},{1,3},{3,1},... | collective-permute-start | bytes 2654216 | tf_op jit(solution)/shard_map/ppermute | solution.py:373
  11.0 0.8 select_reduce_fusion.2
  11.9 6.6 %low_rank.1.refs_3_.refs_4_.refs_2_ = bf16[96,1024]{1,0:T(8,128)(2,1)S(1)} custom-call(s32[32]{0:T(128)S(1)} %pad_add_fusion.refs_0_, bf16[768,1024]{1,0:T(8,128)(2,1)S(1)} %bitcast.11, bf16[768,1024]{1,0:T(8,128)(2,1)} %collective-permute-done.1.refs_2_, s32[192,1]{1,0:T(8,128)S(1)} %copy.13.refs_3_.refs_2_, s32[192,1]{1,0:T(8,128)S(1)} %copy.14.refs_4_.refs_3_, ...), custom_call_target="tpu_custom_call" | custom-call | flops 1 | bytes 1 | tf_op jit(solution)/shard_map/low_rank/pallas_call | solution.py:26
  18.5 3.0 %products.6.refs_3_ = bf16[432,1024]{1,0:T(8,128)(2,1)S(1)} custom-call(s32[8]{0:T(128)S(1)} %dynamic-slice_bitcast_fusion.refs_0_, bf16[768,1024]{1,0:T(8,128)(2,1)S(1)} %bitcast.12, bf16[1024,8192]{1,0:T(8,128)(2,1)} %refs_2_.9, bf16[96,1024]{1,0:T(8,128)(2,1)S(1)} %low_rank.1.refs_3_.refs_4_.refs_2_, bf16[96,1024]{1,0:T(8,128)(2,1)S(1)} %low_rank.1.refs_3_.refs_4_.refs_2_), custom_call_target="tpu_custom_call" | custom-call | flops 1 | bytes 1 | tf_op jit(solution)/shard_map/products/pallas_call | solution.py:26
  21.7 6.3 %products.7 = (bf16[768,1024]{1,0:T(8,128)(2,1)}, bf16[768,1024]{1,0:T(8,128)(2,1)S(1)}) custom-call(s32[8]{0:T(128)S(1)} %dynamic-slice_bitcast_fusion.refs_0_, bf16[768,1024]{1,0:T(8,128)(2,1)} %bitcast.7, bf16[1024,8192]{1,0:T(8,128)(2,1)} %refs_2_.9, bf16[432,1024]{1,0:T(8,128)(2,1)S(1)} %products.6.refs_3_), custom_call_target="tpu_custom_call" | custom-call | flops 1 | bytes 1 | tf_op jit(solution)/shard_map/products/pallas_call | solution.py:26
  28.0 2.1 %collective-permute-start.7 = (bf16[768,1024]{1,0:T(8,128)(2,1)}, bf16[768,1024]{1,0:T(8,128)(2,1)}, u32[]{:S(2)}, u32[]{:S(2)}) collective-permute-start(bf16[768,1024]{1,0:T(8,128)(2,1)} %get-tuple-element.16.refs_2_), channel_id=1, source_target_pairs={{0,2},{2,0},{4,6},{6,4},{8,10},{10,8},{12,14},{14,12},{1,3},{3,1},... | collective-permute-start | bytes 4718600 | tf_op jit(solution)/shard_map/ppermute | solution.py:373
  30.1 1.8 %total.14.refs_3_.refs_0_ = bf16[432,1024]{1,0:T(8,128)(2,1)S(1)} custom-call(bf16[768,1024]{1,0:T(8,128)(2,1)S(1)} %get-tuple-element.15.refs_0_, bf16[432,1024]{1,0:T(8,128)(2,1)S(1)} %collective-permute-done.3.refs_1_, bf16[768,1024]{1,0:T(8,128)(2,1)} %get-tuple-element.16.refs_2_), custom_call_target="tpu_custom_call" | custom-call | flops 1 | bytes 1 | tf_op jit(solution)/shard_map/total/pallas_call | solution.py:26
  31.8 3.5 %collective-permute-start.5 = (bf16[432,1024]{1,0:T(8,128)(2,1)S(1)}, bf16[432,1024]{1,0:T(8,128)(2,1)S(1)}, u32[]{:S(2)}, u32[]{:S(2)}) collective-permute-start(bf16[432,1024]{1,0:T(8,128)(2,1)S(1)} %total.14.refs_3_.refs_0_), channel_id=1, source_target_pairs={{0,4},{12,8},{2,6},{14,10},{1,5},{13,9},{3,7},{15,11},{16,20},{28,... | collective-permute-start | bytes 2654216 | tf_op jit(solution)/shard_map/ppermute | solution.py:380
  35.4 6.4 %products.8 = (bf16[768,1024]{1,0:T(8,128)(2,1)S(1)}, bf16[768,1024]{1,0:T(8,128)(2,1)S(1)}) custom-call(s32[8]{0:T(128)S(1)} %dynamic-slice_bitcast_fusion.refs_0_, bf16[768,1024]{1,0:T(8,128)(2,1)} %bitcast.8, bf16[1024,8192]{1,0:T(8,128)(2,1)} %refs_2_.9, bf16[432,1024]{1,0:T(8,128)(2,1)S(1)} %total.14.refs_3_.refs_0_), custom_call_target="tpu_custom_call" | custom-call | flops 1 | bytes 1 | tf_op jit(solution)/shard_map/products/pallas_call | solution.py:26
  41.8 1.2 copy-done.5
  43.0 5.5 %collective-permute-done.2.refs_1_.refs_3_ = bf16[432,1024]{1,0:T(8,128)(2,1)S(1)} collective-permute-done((bf16[432,1024]{1,0:T(8,128)(2,1)S(1)}, bf16[432,1024]{1,0:T(8,128)(2,1)S(1)}, u32[]{:S(2)}, u32[]{:S(2)}) %collective-permute-start.2) | collective-permute-done | bytes 884768 | tf_op jit(solution)/shard_map/ppermute | solution.py:373
  48.5 1.8 %total.15.refs_3_.refs_0_.refs_2_.refs_1_ = bf16[432,1024]{1,0:T(8,128)(2,1)S(1)} custom-call(bf16[768,1024]{1,0:T(8,128)(2,1)S(1)} %get-tuple-element.15.refs_0_, bf16[432,1024]{1,0:T(8,128)(2,1)S(1)} %collective-permute-done.2.refs_1_.refs_3_, bf16[96,1024]{1,0:T(8,128)(2,1)S(1)} %low_rank.1.refs_3_.refs_4_.refs_2_, ...), custom_call_target="tpu_custom_call" | custom-call | flops 1 | bytes 1 | tf_op jit(solution)/shard_map/total/pallas_call | solution.py:26
  50.3 4.3 %collective-permute-start.4 = (bf16[432,1024]{1,0:T(8,128)(2,1)S(1)}, bf16[432,1024]{1,0:T(8,128)(2,1)S(1)}, u32[]{:S(2)}, u32[]{:S(2)}) collective-permute-start(bf16[432,1024]{1,0:T(8,128)(2,1)S(1)} %total.15.refs_3_.refs_0_.refs_2_.refs_1_), channel_id=1, source_target_pairs={{0,4},{12,8},{2,6},{14,10},{1,5},{13,9},{3,7},{15,11},{16,20},{28,... | collective-permute-start | bytes 2654216 | tf_op jit(solution)/shard_map/ppermute | solution.py:380
  54.5 1.6 collective-permute-start.10
  56.1 10.1 %products.9 = (bf16[768,1024]{1,0:T(8,128)(2,1)S(1)}, bf16[768,1024]{1,0:T(8,128)(2,1)S(1)}, bf16[768,1024]{1,0:T(8,128)(2,1)}) custom-call(s32[8]{0:T(128)S(1)} %dynamic-slice_bitcast_fusion.refs_0_, bf16[768,1024]{1,0:T(8,128)(2,1)} %bitcast.9, bf16[1024,8192]{1,0:T(8,128)(2,1)} %refs_2_.9, bf16[432,1024]{1,0:T(8,128)(2,1)S(1)} %total.15.refs_3_.refs_0_.refs_2_.refs_1_), custom_call_target="tpu_custom_call" | custom-call | flops 1 | bytes 1 | tf_op jit(solution)/shard_map/products/pallas_call | solution.py:26
  66.2 1.1 copy-done.3
  67.3 2.1 %total.16.refs_4_ = bf16[432,1024]{1,0:T(8,128)(2,1)} custom-call(bf16[432,1024]{1,0:T(8,128)(2,1)S(1)} %total.14.refs_3_.refs_0_, bf16[432,1024]{1,0:T(8,128)(2,1)S(1)} %collective-permute-done.5.refs_1_, bf16[768,1024]{1,0:T(8,128)(2,1)} %copy-done.3), custom_call_target="tpu_custom_call" | custom-call | flops 1 | bytes 1 | tf_op jit(solution)/shard_map/total/pallas_call | solution.py:26
  69.5 0.7 collective-permute-start.8
  70.2 2.5 %collective-permute-done.4.refs_1_.refs_3_ = bf16[432,1024]{1,0:T(8,128)(2,1)S(1)} collective-permute-done((bf16[432,1024]{1,0:T(8,128)(2,1)S(1)}, bf16[432,1024]{1,0:T(8,128)(2,1)S(1)}, u32[]{:S(2)}, u32[]{:S(2)}) %collective-permute-start.4) | collective-permute-done | bytes 884768 | tf_op jit(solution)/shard_map/ppermute | solution.py:380
  72.8 1.8 %total.17.refs_2_ = bf16[432,1024]{1,0:T(8,128)(2,1)S(1)} custom-call(bf16[432,1024]{1,0:T(8,128)(2,1)S(1)} %total.15.refs_3_.refs_0_.refs_2_.refs_1_, bf16[432,1024]{1,0:T(8,128)(2,1)S(1)} %collective-permute-done.4.refs_1_.refs_3_, bf16[432,1024]{1,0:T(8,128)(2,1)S(1)} %total.15.refs_3_.refs_0_.refs_2_.refs_1_, ...), custom_call_target="tpu_custom_call" | custom-call | flops 1 | bytes 1 | tf_op jit(solution)/shard_map/total/pallas_call | solution.py:26
  74.6 0.7 collective-permute-start.6
  75.3 7.0 %collective-permute-done.7.refs_1_ = bf16[768,1024]{1,0:T(8,128)(2,1)} collective-permute-done((bf16[768,1024]{1,0:T(8,128)(2,1)}, bf16[768,1024]{1,0:T(8,128)(2,1)}, u32[]{:S(2)}, u32[]{:S(2)}) %collective-permute-start.7) | collective-permute-done | bytes 1572896 | tf_op jit(solution)/shard_map/ppermute | solution.py:373
  82.3 1.8 %total.18.refs_2_.refs_0_ = bf16[384,1024]{1,0:T(8,128)(2,1)S(1)} custom-call(bf16[768,1024]{1,0:T(8,128)(2,1)S(1)} %get-tuple-element.20.refs_0_, bf16[768,1024]{1,0:T(8,128)(2,1)} %collective-permute-done.7.refs_1_, bf16[432,1024]{1,0:T(8,128)(2,1)S(1)} %total.17.refs_2_), custom_call_target="tpu_custom_call" | custom-call | flops 1 | bytes 1 | tf_op jit(solution)/shard_map/total/pallas_call | solution.py:26
  84.1 4.2 %collective-permute-start.11 = (bf16[384,1024]{1,0:T(8,128)(2,1)S(1)}, bf16[384,1024]{1,0:T(8,128)(2,1)S(1)}, u32[]{:S(2)}, u32[]{:S(2)}) collective-permute-start(bf16[384,1024]{1,0:T(8,128)(2,1)S(1)} %total.18.refs_2_.refs_0_), channel_id=1, source_target_pairs={{0,4},{12,8},{2,6},{14,10},{1,5},{13,9},{3,7},{15,11},{16,20},{28,... | collective-permute-start | bytes 2359304 | tf_op jit(solution)/shard_map/ppermute | solution.py:380
  88.3 1.8 %total.19.refs_2_.refs_0_.refs_1_ = bf16[384,1024]{1,0:T(8,128)(2,1)S(1)} custom-call(bf16[768,1024]{1,0:T(8,128)(2,1)S(1)} %get-tuple-element.20.refs_0_, bf16[768,1024]{1,0:T(8,128)(2,1)} %collective-permute-done.7.refs_1_, bf16[384,1024]{1,0:T(8,128)(2,1)S(1)} %total.18.refs_2_.refs_0_), custom_call_target="tpu_custom_call" | custom-call | flops 1 | bytes 1 | tf_op jit(solution)/shard_map/total/pallas_call | solution.py:26
  90.1 1.6 collective-permute-start.14
  91.7 0.8 total.20.refs_2_
  92.6 1.4 collective-permute-start.9
  94.1 19.5 %collective-permute-start.12 = (bf16[384,1024]{1,0:T(8,128)(2,1)S(1)}, bf16[384,1024]{1,0:T(8,128)(2,1)S(1)}, u32[]{:S(2)}, u32[]{:S(2)}) collective-permute-start(bf16[384,1024]{1,0:T(8,128)(2,1)S(1)} %total.19.refs_2_.refs_0_.refs_1_), channel_id=1, source_target_pairs={{0,4},{12,8},{2,6},{14,10},{1,5},{13,9},{3,7},{15,11},{16,20},{28,... | collective-permute-start | bytes 2359304 | tf_op jit(solution)/shard_map/ppermute | solution.py:380
  113.6 1.4 total.21.refs_2_
  115.0 1.6 collective-permute-start.13
  116.5 1.7 %total.22.refs_4_.refs_0_.refs_2_ = bf16[768,1024]{1,0:T(8,128)(2,1)S(1)} custom-call(bf16[768,1024]{1,0:T(8,128)(2,1)S(1)} %copy-done.10, bf16[768,1024]{1,0:T(8,128)(2,1)} %collective-permute-done.10.refs_1_, bf16[384,1024]{1,0:T(8,128)(2,1)S(1)} %total.21.refs_2_), custom_call_target="tpu_custom_call" | custom-call | flops 1 | bytes 1 | tf_op jit(solution)/shard_map/total/pallas_call | solution.py:26
  118.3 4.9 %collective-permute-start.17 = (bf16[768,1024]{1,0:T(8,128)(2,1)S(1)}, bf16[768,1024]{1,0:T(8,128)(2,1)}, u32[]{:S(2)}, u32[]{:S(2)}) collective-permute-start(bf16[768,1024]{1,0:T(8,128)(2,1)S(1)} %total.22.refs_4_.refs_0_.refs_2_), channel_id=1, source_target_pairs={{0,4},{12,8},{2,6},{14,10},{1,5},{13,9},{3,7},{15,11},{16,20},{28,... | collective-permute-start | bytes 4718600 | tf_op jit(solution)/shard_map/ppermute | solution.py:380
  123.2 1.4 total.23.refs_4_.refs_1_
  124.6 2.3 %total.24.refs_2_ = bf16[768,1024]{1,0:T(8,128)(2,1)S(1)} custom-call(bf16[768,1024]{1,0:T(8,128)(2,1)} %copy-done.2, bf16[432,1024]{1,0:T(8,128)(2,1)S(1)} %copy-done.8, bf16[768,1024]{1,0:T(8,128)(2,1)} %copy-done.2, bf16[432,1024]{1,0:T(8,128)(2,1)S(1)} %collective-permute-done.6.refs_1_.refs_2_.refs_3_, bf16[96,1024]{1,0:T(8,128)(2,1)S(1)} %total.23.refs_4_.refs_1_), custom_call_target="tpu_custom_call" | custom-call | flops 1 | bytes 1 | tf_op jit(solution)/shard_map/total/pallas_call | solution.py:26
  126.9 1.4 collective-permute-start.18
  128.3 3.2 %collective-permute-done.12.refs_1_ = bf16[384,1024]{1,0:T(8,128)(2,1)S(1)} collective-permute-done((bf16[384,1024]{1,0:T(8,128)(2,1)S(1)}, bf16[384,1024]{1,0:T(8,128)(2,1)S(1)}, u32[]{:S(2)}, u32[]{:S(2)}) %collective-permute-start.12) | collective-permute-done | bytes 786464 | tf_op jit(solution)/shard_map/ppermute | solution.py:380
  131.5 1.4 total.25.refs_5_
  132.9 0.9 collective-permute-start.15
  133.9 8.0 %expand.1 = (bf16[768,1024]{1,0:T(8,128)(2,1)}, bf16[384,1024]{1,0:T(8,128)(2,1)S(1)}, bf16[384,1024]{1,0:T(8,128)(2,1)S(1)}) custom-call(s32[32]{0:T(128)S(1)} %pad_add_fusion.refs_0_, bf16[96,1024]{1,0:T(8,128)(2,1)S(1)} %total.23.refs_4_.refs_1_, s32[192,1]{1,0:T(8,128)S(1)} %copy-done.12, s32[192,1]{1,0:T(8,128)S(1)} %copy-done.14, ...), custom_call_target="tpu_custom_call" | custom-call | flops 1 | bytes 1 | tf_op jit(solution)/shard_map/expand/pallas_call | solution.py:26
  142.0 7.0 %collective-permute-done.14.refs_2_.refs_6_ = bf16[768,1024]{1,0:T(8,128)(2,1)} collective-permute-done((bf16[768,1024]{1,0:T(8,128)(2,1)S(1)}, bf16[768,1024]{1,0:T(8,128)(2,1)}, u32[]{:S(2)}, u32[]{:S(2)}) %collective-permute-start.14) | collective-permute-done | bytes 1572896 | tf_op jit(solution)/shard_map/ppermute | solution.py:373
  149.0 3.2 %total.26.refs_0_.refs_4_.refs_8_ = bf16[768,1024]{1,0:T(8,128)(2,1)S(1)} custom-call(bf16[768,1024]{1,0:T(8,128)(2,1)} %get-tuple-element.18.refs_0_.refs_4_, bf16[768,1024]{1,0:T(8,128)(2,1)} %get-tuple-element.22.refs_1_.refs_5_.refs_8_, bf16[768,1024]{1,0:T(8,128)(2,1)} %collective-permute-done.14.refs_2_.refs_6_, ...), custom_call_target="tpu_custom_call" | custom-call | flops 1 | bytes 1 | tf_op jit(solution)/shard_map/total/pallas_call | solution.py:26
  152.2 9.1 %collective-permute-done.17.refs_2_.refs_6_ = bf16[768,1024]{1,0:T(8,128)(2,1)} collective-permute-done((bf16[768,1024]{1,0:T(8,128)(2,1)S(1)}, bf16[768,1024]{1,0:T(8,128)(2,1)}, u32[]{:S(2)}, u32[]{:S(2)}) %collective-permute-start.17) | collective-permute-done | bytes 1572896 | tf_op jit(solution)/shard_map/ppermute | solution.py:380
  161.3 1.8 %collective-permute-done.18.refs_3_.refs_7_ = bf16[768,1024]{1,0:T(8,128)(2,1)S(1)} collective-permute-done((bf16[768,1024]{1,0:T(8,128)(2,1)S(1)}, bf16[768,1024]{1,0:T(8,128)(2,1)S(1)}, u32[]{:S(2)}, u32[]{:S(2)}) %collective-permute-start.18) | collective-permute-done | bytes 1572896 | tf_op jit(solution)/shard_map/ppermute | solution.py:380
  163.1 1.2 copy-done.15
  164.3 3.9 %total.27 = bf16[768,1024]{1,0:T(8,128)(2,1)} custom-call(bf16[768,1024]{1,0:T(8,128)(2,1)S(1)} %total.26.refs_0_.refs_4_.refs_8_, bf16[384,1024]{1,0:T(8,128)(2,1)S(1)} %collective-permute-done.16.refs_1_, bf16[768,1024]{1,0:T(8,128)(2,1)} %collective-permute-done.17.refs_2_.refs_6_, bf16[768,1024]{1,0:T(8,128)(2,1)} %copy-done.15, ...), custom_call_target="tpu_custom_call" | custom-call | flops 1 | bytes 1 | tf_op jit(solution)/shard_map/total/pallas_call | solution.py:26
  (70 shorter events, 3.5 us)
Async XLA Ops:
  0.0 9.5 %collective-permute-start = (s32[192]{0:T(256)}, s32[192]{0:T(256)S(1)}, u32[]{:S(2)}, u32[]{:S(2)}) collective-permute-start(s32[192]{0:T(256)} %param.7), channel_id=1, source_target_pairs={{0,1},{1,0},{2,3},{3,2},{4,5},{5,4},{6,7},{7,6},{8,9},{9,8},{10,11... | collective-permute-start | bytes 2312 | tf_op jit(solution)/shard_map/ppermute | solution.py:386
  0.5 11.5 %collective-permute-start.1 = (bf16[768,1024]{1,0:T(8,128)(2,1)}, bf16[768,1024]{1,0:T(8,128)(2,1)}, u32[]{:S(2)}, u32[]{:S(2)}) collective-permute-start(bf16[768,1024]{1,0:T(8,128)(2,1)} %bitcast.6), channel_id=1, source_target_pairs={{0,1},{1,0},{2,3},{3,2},{4,5},{5,4},{6,7},{7,6},{8,9},{9,8},{10,11... | collective-permute-start | bytes 4718600 | tf_op jit(solution)/shard_map/ppermute | solution.py:386
  1.2 1.4 copy-start
  2.6 6.4 %copy-start.16 = (s32[192]{0:T(256)S(1)}, s32[192]{0:T(256)}, u32[]{:S(2)}) copy-start(s32[192]{0:T(256)} %param.7) | copy-start | bytes 2308
  2.6 9.3 %copy-start.1 = (bf16[4,192,1024]{2,1,0:T(8,128)(2,1)S(1)}, bf16[4,192,1024]{2,1,0:T(8,128)(2,1)}, u32[]{:S(2)}) copy-start(bf16[4,192,1024]{2,1,0:T(8,128)(2,1)} %param.6) | copy-start | bytes 4718596
  6.0 24.1 %collective-permute-start.3 = (bf16[432,1024]{1,0:T(8,128)(2,1)S(1)}, bf16[432,1024]{1,0:T(8,128)(2,1)S(1)}, u32[]{:S(2)}, u32[]{:S(2)}) collective-permute-start(bf16[432,1024]{1,0:T(8,128)(2,1)S(1)} %products.5.refs_6_), channel_id=1, source_target_pairs={{0,2},{2,0},{4,6},{6,4},{8,10},{10,8},{12,14},{14,12},{1,3},{3,1},... | collective-permute-start | bytes 2654216 | tf_op jit(solution)/shard_map/ppermute | solution.py:373
  9.5 9.0 %copy-start.11 = (s32[192,1]{1,0:T(8,128)}, s32[192,1]{1,0:T(8,128)S(1)}, u32[]{:S(2)}) copy-start(s32[192,1]{1,0:T(8,128)S(1)} %copy.13.refs_3_.refs_2_) | copy-start | bytes 2308
  9.7 0.5 copy-start.17
  10.3 0.5 copy-start.18
  11.0 7.5 %copy-start.13 = (s32[192,1]{1,0:T(8,128)}, s32[192,1]{1,0:T(8,128)S(1)}, u32[]{:S(2)}) copy-start(s32[192,1]{1,0:T(8,128)S(1)} %copy.14.refs_4_.refs_3_) | copy-start | bytes 2308
  21.6 26.9 %collective-permute-start.2 = (bf16[432,1024]{1,0:T(8,128)(2,1)S(1)}, bf16[432,1024]{1,0:T(8,128)(2,1)S(1)}, u32[]{:S(2)}, u32[]{:S(2)}) collective-permute-start(bf16[432,1024]{1,0:T(8,128)(2,1)S(1)} %products.6.refs_3_), channel_id=1, source_target_pairs={{0,2},{2,0},{4,6},{6,4},{8,10},{10,8},{12,14},{14,12},{1,3},{3,1},... | collective-permute-start | bytes 2654216 | tf_op jit(solution)/shard_map/ppermute | solution.py:373
  28.0 54.3 %collective-permute-start.7 = (bf16[768,1024]{1,0:T(8,128)(2,1)}, bf16[768,1024]{1,0:T(8,128)(2,1)}, u32[]{:S(2)}, u32[]{:S(2)}) collective-permute-start(bf16[768,1024]{1,0:T(8,128)(2,1)} %get-tuple-element.16.refs_2_), channel_id=1, source_target_pairs={{0,2},{2,0},{4,6},{6,4},{8,10},{10,8},{12,14},{14,12},{1,3},{3,1},... | collective-permute-start | bytes 4718600 | tf_op jit(solution)/shard_map/ppermute | solution.py:373
  31.8 35.5 %collective-permute-start.5 = (bf16[432,1024]{1,0:T(8,128)(2,1)S(1)}, bf16[432,1024]{1,0:T(8,128)(2,1)S(1)}, u32[]{:S(2)}, u32[]{:S(2)}) collective-permute-start(bf16[432,1024]{1,0:T(8,128)(2,1)S(1)} %total.14.refs_3_.refs_0_), channel_id=1, source_target_pairs={{0,4},{12,8},{2,6},{14,10},{1,5},{13,9},{3,7},{15,11},{16,20},{28,... | collective-permute-start | bytes 2654216 | tf_op jit(solution)/shard_map/ppermute | solution.py:380
  41.8 1.2 copy-start.5
  48.5 6.1 %copy-start.6 = (bf16[768,1024]{1,0:T(8,128)(2,1)S(1)}, bf16[768,1024]{1,0:T(8,128)(2,1)}, u32[]{:S(2)}) copy-start(bf16[768,1024]{1,0:T(8,128)(2,1)} %copy-done.5) | copy-start | bytes 4718596
  50.3 22.5 %collective-permute-start.4 = (bf16[432,1024]{1,0:T(8,128)(2,1)S(1)}, bf16[432,1024]{1,0:T(8,128)(2,1)S(1)}, u32[]{:S(2)}, u32[]{:S(2)}) collective-permute-start(bf16[432,1024]{1,0:T(8,128)(2,1)S(1)} %total.15.refs_3_.refs_0_.refs_2_.refs_1_), channel_id=1, source_target_pairs={{0,4},{12,8},{2,6},{14,10},{1,5},{13,9},{3,7},{15,11},{16,20},{28,... | collective-permute-start | bytes 2654216 | tf_op jit(solution)/shard_map/ppermute | solution.py:380
  54.5 62.0 %collective-permute-start.10 = (bf16[768,1024]{1,0:T(8,128)(2,1)S(1)}, bf16[768,1024]{1,0:T(8,128)(2,1)}, u32[]{:S(2)}, u32[]{:S(2)}) collective-permute-start(bf16[768,1024]{1,0:T(8,128)(2,1)S(1)} %hold.2), channel_id=1, source_target_pairs={{0,2},{2,0},{4,6},{6,4},{8,10},{10,8},{12,14},{14,12},{1,3},{3,1},... | collective-permute-start | bytes 4718600 | tf_op jit(solution)/shard_map/ppermute | solution.py:373
  66.2 1.1 copy-start.3
  67.3 2.2 %copy-start.9 = (bf16[768,1024]{1,0:T(8,128)(2,1)}, bf16[768,1024]{1,0:T(8,128)(2,1)S(1)}, u32[]{:S(2)}) copy-start(bf16[768,1024]{1,0:T(8,128)(2,1)S(1)} %get-tuple-element.21.refs_0_) | copy-start | bytes 4718596
  69.5 22.2 %collective-permute-start.8 = (bf16[432,1024]{1,0:T(8,128)(2,1)}, bf16[432,1024]{1,0:T(8,128)(2,1)S(1)}, u32[]{:S(2)}, u32[]{:S(2)}) collective-permute-start(bf16[432,1024]{1,0:T(8,128)(2,1)} %total.16.refs_4_), channel_id=1, source_target_pairs={{4,8},{8,4},{6,10},{10,6},{5,9},{9,5},{7,11},{11,7},{20,24},{24,20... | collective-permute-start | bytes 2654216 | tf_op jit(solution)/shard_map/ppermute | solution.py:380
  74.6 17.1 %collective-permute-start.6 = (bf16[432,1024]{1,0:T(8,128)(2,1)S(1)}, bf16[432,1024]{1,0:T(8,128)(2,1)S(1)}, u32[]{:S(2)}, u32[]{:S(2)}) collective-permute-start(bf16[432,1024]{1,0:T(8,128)(2,1)S(1)} %total.17.refs_2_), channel_id=1, source_target_pairs={{4,8},{8,4},{6,10},{10,6},{5,9},{9,5},{7,11},{11,7},{20,24},{24,20... | collective-permute-start | bytes 2654216 | tf_op jit(solution)/shard_map/ppermute | solution.py:380
  84.1 6.0 %copy-start.4 = (bf16[768,1024]{1,0:T(8,128)(2,1)S(1)}, bf16[768,1024]{1,0:T(8,128)(2,1)}, u32[]{:S(2)}) copy-start(bf16[768,1024]{1,0:T(8,128)(2,1)} %copy-done.3) | copy-start | bytes 4718596
  84.1 29.5 %collective-permute-start.11 = (bf16[384,1024]{1,0:T(8,128)(2,1)S(1)}, bf16[384,1024]{1,0:T(8,128)(2,1)S(1)}, u32[]{:S(2)}, u32[]{:S(2)}) collective-permute-start(bf16[384,1024]{1,0:T(8,128)(2,1)S(1)} %total.18.refs_2_.refs_0_), channel_id=1, source_target_pairs={{0,4},{12,8},{2,6},{14,10},{1,5},{13,9},{3,7},{15,11},{16,20},{28,... | collective-permute-start | bytes 2359304 | tf_op jit(solution)/shard_map/ppermute | solution.py:380
  90.1 58.9 %collective-permute-start.14 = (bf16[768,1024]{1,0:T(8,128)(2,1)S(1)}, bf16[768,1024]{1,0:T(8,128)(2,1)}, u32[]{:S(2)}, u32[]{:S(2)}) collective-permute-start(bf16[768,1024]{1,0:T(8,128)(2,1)S(1)} %hold.3), channel_id=1, source_target_pairs={{0,2},{2,0},{4,6},{6,4},{8,10},{10,8},{12,14},{14,12},{1,3},{3,1},... | collective-permute-start | bytes 4718600 | tf_op jit(solution)/shard_map/ppermute | solution.py:373
  91.7 0.9 copy-start.7
  92.6 23.9 %copy-start.10 = (bf16[768,1024]{1,0:T(8,128)(2,1)S(1)}, bf16[768,1024]{1,0:T(8,128)(2,1)}, u32[]{:S(2)}) copy-start(bf16[768,1024]{1,0:T(8,128)(2,1)} %copy-done.9) | copy-start | bytes 4718596
  92.6 30.5 %collective-permute-start.9 = (bf16[96,1024]{1,0:T(8,128)(2,1)S(1)}, bf16[96,1024]{1,0:T(8,128)(2,1)S(1)}, u32[]{:S(2)}, u32[]{:S(2)}) collective-permute-start(bf16[96,1024]{1,0:T(8,128)(2,1)S(1)} %total.20.refs_2_), channel_id=1, source_target_pairs={{8,12},{4,0},{10,14},{6,2},{9,13},{5,1},{11,15},{7,3},{24,28},{20,... | collective-permute-start | bytes 589832 | tf_op jit(solution)/shard_map/ppermute | solution.py:380
  94.1 37.5 %collective-permute-start.12 = (bf16[384,1024]{1,0:T(8,128)(2,1)S(1)}, bf16[384,1024]{1,0:T(8,128)(2,1)S(1)}, u32[]{:S(2)}, u32[]{:S(2)}) collective-permute-start(bf16[384,1024]{1,0:T(8,128)(2,1)S(1)} %total.19.refs_2_.refs_0_.refs_1_), channel_id=1, source_target_pairs={{0,4},{12,8},{2,6},{14,10},{1,5},{13,9},{3,7},{15,11},{16,20},{28,... | collective-permute-start | bytes 2359304 | tf_op jit(solution)/shard_map/ppermute | solution.py:380
  115.0 18.9 %collective-permute-start.13 = (bf16[384,1024]{1,0:T(8,128)(2,1)S(1)}, bf16[384,1024]{1,0:T(8,128)(2,1)}, u32[]{:S(2)}, u32[]{:S(2)}) collective-permute-start(bf16[384,1024]{1,0:T(8,128)(2,1)S(1)} %total.21.refs_2_), channel_id=1, source_target_pairs={{4,8},{8,4},{6,10},{10,6},{5,9},{9,5},{7,11},{11,7},{20,24},{24,20... | collective-permute-start | bytes 2359304 | tf_op jit(solution)/shard_map/ppermute | solution.py:380
  118.3 4.9 %copy-start.2 = (bf16[768,1024]{1,0:T(8,128)(2,1)}, bf16[768,1024]{1,0:T(8,128)(2,1)S(1)}, u32[]{:S(2)}) copy-start(bf16[768,1024]{1,0:T(8,128)(2,1)S(1)} %total.22.refs_4_.refs_0_.refs_2_) | copy-start | bytes 4718596
  118.3 6.3 %copy-start.8 = (bf16[432,1024]{1,0:T(8,128)(2,1)S(1)}, bf16[432,1024]{1,0:T(8,128)(2,1)}, u32[]{:S(2)}) copy-start(bf16[432,1024]{1,0:T(8,128)(2,1)} %copy-done.7) | copy-start | bytes 2654212
  118.3 43.0 %collective-permute-start.17 = (bf16[768,1024]{1,0:T(8,128)(2,1)S(1)}, bf16[768,1024]{1,0:T(8,128)(2,1)}, u32[]{:S(2)}, u32[]{:S(2)}) collective-permute-start(bf16[768,1024]{1,0:T(8,128)(2,1)S(1)} %total.22.refs_4_.refs_0_.refs_2_), channel_id=1, source_target_pairs={{0,4},{12,8},{2,6},{14,10},{1,5},{13,9},{3,7},{15,11},{16,20},{28,... | collective-permute-start | bytes 4718600 | tf_op jit(solution)/shard_map/ppermute | solution.py:380
  126.8 7.0 %copy-start.12 = (s32[192,1]{1,0:T(8,128)S(1)}, s32[192,1]{1,0:T(8,128)}, u32[]{:S(2)}) copy-start(s32[192,1]{1,0:T(8,128)} %copy-done.11) | copy-start | bytes 2308
  126.9 7.0 %copy-start.14 = (s32[192,1]{1,0:T(8,128)S(1)}, s32[192,1]{1,0:T(8,128)}, u32[]{:S(2)}) copy-start(s32[192,1]{1,0:T(8,128)} %copy-done.13) | copy-start | bytes 2308
  126.9 36.2 %collective-permute-start.18 = (bf16[768,1024]{1,0:T(8,128)(2,1)S(1)}, bf16[768,1024]{1,0:T(8,128)(2,1)S(1)}, u32[]{:S(2)}, u32[]{:S(2)}) collective-permute-start(bf16[768,1024]{1,0:T(8,128)(2,1)S(1)} %total.24.refs_2_), channel_id=1, source_target_pairs={{8,12},{4,0},{10,14},{6,2},{9,13},{5,1},{11,15},{7,3},{24,28},{20,... | collective-permute-start | bytes 4718600 | tf_op jit(solution)/shard_map/ppermute | solution.py:380
  132.9 16.1 %collective-permute-start.15 = (bf16[384,1024]{1,0:T(8,128)(2,1)S(1)}, bf16[384,1024]{1,0:T(8,128)(2,1)S(1)}, u32[]{:S(2)}, u32[]{:S(2)}) collective-permute-start(bf16[384,1024]{1,0:T(8,128)(2,1)S(1)} %total.25.refs_5_), channel_id=1, source_target_pairs={{4,8},{8,4},{6,10},{10,6},{5,9},{9,5},{7,11},{11,7},{20,24},{24,20... | collective-permute-start | bytes 2359304 | tf_op jit(solution)/shard_map/ppermute | solution.py:380
  141.9 19.4 %collective-permute-start.16 = (bf16[384,1024]{1,0:T(8,128)(2,1)S(1)}, bf16[384,1024]{1,0:T(8,128)(2,1)S(1)}, u32[]{:S(2)}, u32[]{:S(2)}) collective-permute-start(bf16[384,1024]{1,0:T(8,128)(2,1)S(1)} %get-tuple-element.23), channel_id=1, source_target_pairs={{0,1},{1,0},{2,3},{3,2},{4,5},{5,4},{6,7},{7,6},{8,9},{9,8},{10,11... | collective-permute-start | bytes 2359304 | tf_op jit(solution)/shard_map/ppermute | solution.py:386
  149.0 12.3 %collective-permute-start.19 = (bf16[384,1024]{1,0:T(8,128)(2,1)S(1)}, bf16[384,1024]{1,0:T(8,128)(2,1)S(1)}, u32[]{:S(2)}, u32[]{:S(2)}) collective-permute-start(bf16[384,1024]{1,0:T(8,128)(2,1)S(1)} %get-tuple-element.24), channel_id=1, source_target_pairs={{0,1},{1,0},{2,3},{3,2},{4,5},{5,4},{6,7},{7,6},{8,9},{9,8},{10,11... | collective-permute-start | bytes 2359304 | tf_op jit(solution)/shard_map/ppermute | solution.py:386
  163.1 1.2 copy-start.15

commit v13 on v12

--- a/solution.py
+++ b/solution.py
@@ -460,7 +460,7 @@
     def cut_of(h, m):
         if m == 0 and h <= 1:
             return uneven
-        return even if m == 1 else [(0, count)]
+        return [(0, count * 7 // 16), (count * 7 // 16, count * 9 // 16)] if m == 1 else [(0, count)]
 
     def arrived_parts(h, m):
         return [(*cut, arrived[h, m, p], 0) for p, cut in enumerate(cut_of(h, m)) if (h, m, p) in arrived]

time: 169 us -> 174 us (1.030)
  the two profiles are of different devices: /device:TPU:0 before, /device:TPU:14 now
where the time goes in v13:
time: 174 us; the launch traced here: 173 us
  Pallas kernels  71 us (41%)
  waiting for transfers between devices  59.4 us (34%)
  starting transfers between devices  33 us (19%)
  local copies, waits for them, and re-layouts  8.07 us (5%)
    pallas_call x23, Pallas kernels, call(): pl.pallas_call(body, grid_spec=pltpu.PrefetchScalarGridSpec(num_scalar_pr...  71 us
    ppermute x11, waiting for transfers between devices, hop(): return lax.ppermute(value, 'tensor', pairs)  38.6 us
    ppermute x11, starting transfers between devices, hop(): return lax.ppermute(value, 'tensor', pairs)  28.1 us
    ppermute x5, waiting for transfers between devices, swap_y(): return lax.ppermute(value, 'tensor', [(t, t ^ 1) for t in range(n)])  20.8 us
    unnamed x40, local copies, waits for them, and re-layouts  7.15 us
    ppermute x5, starting transfers between devices, swap_y(): return lax.ppermute(value, 'tensor', [(t, t ^ 1) for t in range(n)])  3.87 us
  transfers between devices with their start and end apart: 20, of which 9 were waited for; matrix products, arithmetic and copies ran while one was open for 1% of the time, Pallas kernels for 39%

profile of v13, /device:TPU:14, one launch (start us, length us, event | category | flops | bytes accessed | tf_op | source)
XLA Modules:
  0.0 173.1 jit_solution(1132733974761718778)
XLA Ops:
  1.2 1.4 copy-done
  2.6 3.4 %products.5.refs_6_ = bf16[432,1024]{1,0:T(8,128)(2,1)S(1)} custom-call(s32[8]{0:T(128)S(1)} %dynamic-slice_bitcast_fusion.refs_0_, bf16[768,1024]{1,0:T(8,128)(2,1)S(1)} %bitcast.10, bf16[1024,8192]{1,0:T(8,128)(2,1)} %refs_2_.9), custom_call_target="tpu_custom_call" | custom-call | flops 1 | bytes 1 | tf_op jit(solution)/shard_map/products/pallas_call | solution.py:26
  7.8 6.7 %low_rank.1.refs_3_.refs_4_.refs_2_ = bf16[96,1024]{1,0:T(8,128)(2,1)S(1)} custom-call(s32[32]{0:T(128)S(1)} %pad_add_fusion.refs_0_, bf16[768,1024]{1,0:T(8,128)(2,1)S(1)} %bitcast.11, bf16[768,1024]{1,0:T(8,128)(2,1)} %collective-permute-done.1.refs_2_, s32[192,1]{1,0:T(8,128)S(1)} %copy.13.refs_3_.refs_2_, s32[192,1]{1,0:T(8,128)S(1)} %copy.14.refs_4_.refs_3_, ...), custom_call_target="tpu_custom_call" | custom-call | flops 1 | bytes 1 | tf_op jit(solution)/shard_map/low_rank/pallas_call | solution.py:26
  14.5 3.0 %products.6.refs_3_ = bf16[432,1024]{1,0:T(8,128)(2,1)S(1)} custom-call(s32[8]{0:T(128)S(1)} %dynamic-slice_bitcast_fusion.refs_0_, bf16[768,1024]{1,0:T(8,128)(2,1)S(1)} %bitcast.12, bf16[1024,8192]{1,0:T(8,128)(2,1)} %refs_2_.9, bf16[96,1024]{1,0:T(8,128)(2,1)S(1)} %low_rank.1.refs_3_.refs_4_.refs_2_, bf16[96,1024]{1,0:T(8,128)(2,1)S(1)} %low_rank.1.refs_3_.refs_4_.refs_2_), custom_call_target="tpu_custom_call" | custom-call | flops 1 | bytes 1 | tf_op jit(solution)/shard_map/products/pallas_call | solution.py:26
  17.5 1.6 collective-permute-start.2
  19.1 6.3 %products.7 = (bf16[768,1024]{1,0:T(8,128)(2,1)}, bf16[768,1024]{1,0:T(8,128)(2,1)S(1)}) custom-call(s32[8]{0:T(128)S(1)} %dynamic-slice_bitcast_fusion.refs_0_, bf16[768,1024]{1,0:T(8,128)(2,1)} %bitcast.7, bf16[1024,8192]{1,0:T(8,128)(2,1)} %refs_2_.9, bf16[432,1024]{1,0:T(8,128)(2,1)S(1)} %products.6.refs_3_), custom_call_target="tpu_custom_call" | custom-call | flops 1 | bytes 1 | tf_op jit(solution)/shard_map/products/pallas_call | solution.py:26
  26.0 2.6 %collective-permute-done.3.refs_1_ = bf16[432,1024]{1,0:T(8,128)(2,1)S(1)} collective-permute-done((bf16[432,1024]{1,0:T(8,128)(2,1)S(1)}, bf16[432,1024]{1,0:T(8,128)(2,1)S(1)}, u32[]{:S(2)}, u32[]{:S(2)}) %collective-permute-start.3) | collective-permute-done | bytes 884768 | tf_op jit(solution)/shard_map/ppermute | solution.py:373
  28.6 1.8 %total.14.refs_3_.refs_0_ = bf16[432,1024]{1,0:T(8,128)(2,1)S(1)} custom-call(bf16[768,1024]{1,0:T(8,128)(2,1)S(1)} %get-tuple-element.15.refs_0_, bf16[432,1024]{1,0:T(8,128)(2,1)S(1)} %collective-permute-done.3.refs_1_, bf16[768,1024]{1,0:T(8,128)(2,1)} %get-tuple-element.16.refs_2_), custom_call_target="tpu_custom_call" | custom-call | flops 1 | bytes 1 | tf_op jit(solution)/shard_map/total/pallas_call | solution.py:26
  30.4 1.3 collective-permute-start.5
  31.7 6.4 %products.8 = (bf16[768,1024]{1,0:T(8,128)(2,1)S(1)}, bf16[768,1024]{1,0:T(8,128)(2,1)S(1)}) custom-call(s32[8]{0:T(128)S(1)} %dynamic-slice_bitcast_fusion.refs_0_, bf16[768,1024]{1,0:T(8,128)(2,1)} %bitcast.8, bf16[1024,8192]{1,0:T(8,128)(2,1)} %refs_2_.9, bf16[432,1024]{1,0:T(8,128)(2,1)S(1)} %total.14.refs_3_.refs_0_), custom_call_target="tpu_custom_call" | custom-call | flops 1 | bytes 1 | tf_op jit(solution)/shard_map/products/pallas_call | solution.py:26
  38.1 1.2 copy-done.7
  39.3 8.3 %collective-permute-done.2.refs_1_.refs_3_ = bf16[432,1024]{1,0:T(8,128)(2,1)S(1)} collective-permute-done((bf16[432,1024]{1,0:T(8,128)(2,1)S(1)}, bf16[432,1024]{1,0:T(8,128)(2,1)S(1)}, u32[]{:S(2)}, u32[]{:S(2)}) %collective-permute-start.2) | collective-permute-done | bytes 884768 | tf_op jit(solution)/shard_map/ppermute | solution.py:373
  47.5 1.8 %total.15.refs_3_.refs_0_.refs_2_.refs_1_ = bf16[432,1024]{1,0:T(8,128)(2,1)S(1)} custom-call(bf16[768,1024]{1,0:T(8,128)(2,1)S(1)} %get-tuple-element.15.refs_0_, bf16[432,1024]{1,0:T(8,128)(2,1)S(1)} %collective-permute-done.2.refs_1_.refs_3_, bf16[96,1024]{1,0:T(8,128)(2,1)S(1)} %low_rank.1.refs_3_.refs_4_.refs_2_, ...), custom_call_target="tpu_custom_call" | custom-call | flops 1 | bytes 1 | tf_op jit(solution)/shard_map/total/pallas_call | solution.py:26
  49.3 1.5 collective-permute-start.4
  51.4 10.1 %products.9 = (bf16[768,1024]{1,0:T(8,128)(2,1)S(1)}, bf16[768,1024]{1,0:T(8,128)(2,1)S(1)}, bf16[768,1024]{1,0:T(8,128)(2,1)}) custom-call(s32[8]{0:T(128)S(1)} %dynamic-slice_bitcast_fusion.refs_0_, bf16[768,1024]{1,0:T(8,128)(2,1)} %bitcast.9, bf16[1024,8192]{1,0:T(8,128)(2,1)} %refs_2_.9, bf16[432,1024]{1,0:T(8,128)(2,1)S(1)} %total.15.refs_3_.refs_0_.refs_2_.refs_1_), custom_call_target="tpu_custom_call" | custom-call | flops 1 | bytes 1 | tf_op jit(solution)/shard_map/products/pallas_call | solution.py:26
  61.5 1.1 copy-done.5
  62.6 1.0 copy-done.13
  63.6 1.2 copy-done.14
  64.8 1.8 %total.16.refs_4_ = bf16[432,1024]{1,0:T(8,128)(2,1)S(1)} custom-call(bf16[432,1024]{1,0:T(8,128)(2,1)S(1)} %total.14.refs_3_.refs_0_, bf16[432,1024]{1,0:T(8,128)(2,1)S(1)} %copy-done.14, bf16[768,1024]{1,0:T(8,128)(2,1)} %copy-done.5), custom_call_target="tpu_custom_call" | custom-call | flops 1 | bytes 1 | tf_op jit(solution)/shard_map/total/pallas_call | solution.py:26
  66.6 3.5 %collective-permute-start.8 = (bf16[432,1024]{1,0:T(8,128)(2,1)S(1)}, bf16[432,1024]{1,0:T(8,128)(2,1)S(1)}, u32[]{:S(2)}, u32[]{:S(2)}) collective-permute-start(bf16[432,1024]{1,0:T(8,128)(2,1)S(1)} %total.16.refs_4_), channel_id=1, source_target_pairs={{4,8},{8,4},{6,10},{10,6},{5,9},{9,5},{7,11},{11,7},{20,24},{24,20... | collective-permute-start | bytes 2654216 | tf_op jit(solution)/shard_map/ppermute | solution.py:380
  70.1 0.9 collective-permute-done.4.refs_1_.refs_3_
  71.0 1.8 %total.17.refs_2_ = bf16[432,1024]{1,0:T(8,128)(2,1)S(1)} custom-call(bf16[432,1024]{1,0:T(8,128)(2,1)S(1)} %total.15.refs_3_.refs_0_.refs_2_.refs_1_, bf16[432,1024]{1,0:T(8,128)(2,1)S(1)} %collective-permute-done.4.refs_1_.refs_3_, bf16[432,1024]{1,0:T(8,128)(2,1)S(1)} %total.15.refs_3_.refs_0_.refs_2_.refs_1_, ...), custom_call_target="tpu_custom_call" | custom-call | flops 1 | bytes 1 | tf_op jit(solution)/shard_map/total/pallas_call | solution.py:26
  72.8 3.5 %collective-permute-start.6 = (bf16[432,1024]{1,0:T(8,128)(2,1)S(1)}, bf16[432,1024]{1,0:T(8,128)(2,1)S(1)}, u32[]{:S(2)}, u32[]{:S(2)}) collective-permute-start(bf16[432,1024]{1,0:T(8,128)(2,1)S(1)} %total.17.refs_2_), channel_id=1, source_target_pairs={{4,8},{8,4},{6,10},{10,6},{5,9},{9,5},{7,11},{11,7},{20,24},{24,20... | collective-permute-start | bytes 2654216 | tf_op jit(solution)/shard_map/ppermute | solution.py:380
  76.3 5.1 %collective-permute-done.7.refs_1_ = bf16[768,1024]{1,0:T(8,128)(2,1)} collective-permute-done((bf16[768,1024]{1,0:T(8,128)(2,1)}, bf16[768,1024]{1,0:T(8,128)(2,1)}, u32[]{:S(2)}, u32[]{:S(2)}) %collective-permute-start.7) | collective-permute-done | bytes 1572896 | tf_op jit(solution)/shard_map/ppermute | solution.py:373
  81.4 1.6 total.18.refs_2_.refs_0_
  83.0 2.2 %total.19.refs_2_.refs_0_.refs_1_ = bf16[432,1024]{1,0:T(8,128)(2,1)S(1)} custom-call(bf16[768,1024]{1,0:T(8,128)(2,1)S(1)} %get-tuple-element.20.refs_0_, bf16[768,1024]{1,0:T(8,128)(2,1)} %collective-permute-done.7.refs_1_, bf16[336,1024]{1,0:T(8,128)(2,1)S(1)} %total.18.refs_2_.refs_0_), custom_call_target="tpu_custom_call" | custom-call | flops 1 | bytes 1 | tf_op jit(solution)/shard_map/total/pallas_call | solution.py:26
  85.8 1.3 collective-permute-start.11
  87.0 4.0 %collective-permute-done.8.refs_3_.refs_1_ = bf16[432,1024]{1,0:T(8,128)(2,1)S(1)} collective-permute-done((bf16[432,1024]{1,0:T(8,128)(2,1)S(1)}, bf16[432,1024]{1,0:T(8,128)(2,1)S(1)}, u32[]{:S(2)}, u32[]{:S(2)}) %collective-permute-start.8) | collective-permute-done | bytes 884768 | tf_op jit(solution)/shard_map/ppermute | solution.py:380
  91.1 1.3 collective-permute-start.12
  92.4 14.5 %collective-permute-done.6.refs_1_.refs_2_.refs_3_ = bf16[432,1024]{1,0:T(8,128)(2,1)S(1)} collective-permute-done((bf16[432,1024]{1,0:T(8,128)(2,1)S(1)}, bf16[432,1024]{1,0:T(8,128)(2,1)S(1)}, u32[]{:S(2)}, u32[]{:S(2)}) %collective-permute-start.6) | collective-permute-done | bytes 884768 | tf_op jit(solution)/shard_map/ppermute | solution.py:380
  106.9 0.8 total.20.refs_2_
  107.7 1.4 collective-permute-start.9
  109.2 1.0 total.21.refs_2_
  110.2 4.9 %collective-permute-done.10.refs_1_ = bf16[768,1024]{1,0:T(8,128)(2,1)} collective-permute-done((bf16[768,1024]{1,0:T(8,128)(2,1)S(1)}, bf16[768,1024]{1,0:T(8,128)(2,1)}, u32[]{:S(2)}, u32[]{:S(2)}) %collective-permute-start.10) | collective-permute-done | bytes 1572896 | tf_op jit(solution)/shard_map/ppermute | solution.py:373
  115.1 1.7 total.22.refs_4_.refs_0_.refs_2_
  116.8 1.1 copy-done.2
  118.0 1.4 total.23.refs_4_.refs_1_
  119.4 1.3 collective-permute-start.17
  120.7 2.3 %total.24.refs_2_ = bf16[768,1024]{1,0:T(8,128)(2,1)S(1)} custom-call(bf16[768,1024]{1,0:T(8,128)(2,1)} %copy-done.2, bf16[432,1024]{1,0:T(8,128)(2,1)S(1)} %copy-done.10, bf16[768,1024]{1,0:T(8,128)(2,1)} %copy-done.2, bf16[432,1024]{1,0:T(8,128)(2,1)S(1)} %collective-permute-done.6.refs_1_.refs_2_.refs_3_, bf16[96,1024]{1,0:T(8,128)(2,1)S(1)} %total.23.refs_4_.refs_1_), custom_call_target="tpu_custom_call" | custom-call | flops 1 | bytes 1 | tf_op jit(solution)/shard_map/total/pallas_call | solution.py:26
  123.0 7.0 %collective-permute-start.18 = (bf16[768,1024]{1,0:T(8,128)(2,1)S(1)}, bf16[768,1024]{1,0:T(8,128)(2,1)}, u32[]{:S(2)}, u32[]{:S(2)}) collective-permute-start(bf16[768,1024]{1,0:T(8,128)(2,1)S(1)} %total.24.refs_2_), channel_id=1, source_target_pairs={{8,12},{4,0},{10,14},{6,2},{9,13},{5,1},{11,15},{7,3},{24,28},{20,... | collective-permute-start | bytes 4718600 | tf_op jit(solution)/shard_map/ppermute | solution.py:380
  130.0 3.5 %collective-permute-start.13 = (bf16[336,1024]{1,0:T(8,128)(2,1)S(1)}, bf16[336,1024]{1,0:T(8,128)(2,1)S(1)}, u32[]{:S(2)}, u32[]{:S(2)}) collective-permute-start(bf16[336,1024]{1,0:T(8,128)(2,1)S(1)} %total.21.refs_2_), channel_id=1, source_target_pairs={{4,8},{8,4},{6,10},{10,6},{5,9},{9,5},{7,11},{11,7},{20,24},{24,20... | collective-permute-start | bytes 2064392 | tf_op jit(solution)/shard_map/ppermute | solution.py:380
  133.5 2.1 %total.25.refs_5_ = bf16[432,1024]{1,0:T(8,128)(2,1)S(1)} custom-call(bf16[432,1024]{1,0:T(8,128)(2,1)S(1)} %total.19.refs_2_.refs_0_.refs_1_, bf16[432,1024]{1,0:T(8,128)(2,1)} %collective-permute-done.12.refs_1_, bf16[768,1024]{1,0:T(8,128)(2,1)} %copy-done.4), custom_call_target="tpu_custom_call" | custom-call | flops 1 | bytes 1 | tf_op jit(solution)/shard_map/total/pallas_call | solution.py:26
  135.6 2.6 %collective-permute-start.15 = (bf16[432,1024]{1,0:T(8,128)(2,1)S(1)}, bf16[432,1024]{1,0:T(8,128)(2,1)S(1)}, u32[]{:S(2)}, u32[]{:S(2)}) collective-permute-start(bf16[432,1024]{1,0:T(8,128)(2,1)S(1)} %total.25.refs_5_), channel_id=1, source_target_pairs={{4,8},{8,4},{6,10},{10,6},{5,9},{9,5},{7,11},{11,7},{20,24},{24,20... | collective-permute-start | bytes 2654216 | tf_op jit(solution)/shard_map/ppermute | solution.py:380
  138.2 12.1 %collective-permute-done.13.refs_6_.refs_3_ = bf16[336,1024]{1,0:T(8,128)(2,1)S(1)} collective-permute-done((bf16[336,1024]{1,0:T(8,128)(2,1)S(1)}, bf16[336,1024]{1,0:T(8,128)(2,1)S(1)}, u32[]{:S(2)}, u32[]{:S(2)}) %collective-permute-start.13) | collective-permute-done | bytes 688160 | tf_op jit(solution)/shard_map/ppermute | solution.py:380
  150.3 8.0 %expand.1 = (bf16[768,1024]{1,0:T(8,128)(2,1)}, bf16[384,1024]{1,0:T(8,128)(2,1)S(1)}, bf16[384,1024]{1,0:T(8,128)(2,1)S(1)}) custom-call(s32[32]{0:T(128)S(1)} %pad_add_fusion.refs_0_, bf16[96,1024]{1,0:T(8,128)(2,1)S(1)} %total.23.refs_4_.refs_1_, s32[192,1]{1,0:T(8,128)S(1)} %copy-done.16, s32[192,1]{1,0:T(8,128)S(1)} %copy-done.18, ...), custom_call_target="tpu_custom_call" | custom-call | flops 1 | bytes 1 | tf_op jit(solution)/shard_map/expand/pallas_call | solution.py:26
  158.8 7.0 %collective-permute-done.15.refs_7_ = bf16[432,1024]{1,0:T(8,128)(2,1)S(1)} collective-permute-done((bf16[432,1024]{1,0:T(8,128)(2,1)S(1)}, bf16[432,1024]{1,0:T(8,128)(2,1)S(1)}, u32[]{:S(2)}, u32[]{:S(2)}) %collective-permute-start.15) | collective-permute-done | bytes 884768 | tf_op jit(solution)/shard_map/ppermute | solution.py:380
  165.8 3.1 %total.26.refs_0_.refs_4_.refs_8_ = bf16[768,1024]{1,0:T(8,128)(2,1)S(1)} custom-call(bf16[768,1024]{1,0:T(8,128)(2,1)} %get-tuple-element.18.refs_0_.refs_4_, bf16[768,1024]{1,0:T(8,128)(2,1)} %get-tuple-element.22.refs_1_.refs_5_.refs_8_, bf16[768,1024]{1,0:T(8,128)(2,1)} %collective-permute-done.14.refs_2_.refs_6_, ...), custom_call_target="tpu_custom_call" | custom-call | flops 1 | bytes 1 | tf_op jit(solution)/shard_map/total/pallas_call | solution.py:26
  169.0 3.9 %total.27 = bf16[768,1024]{1,0:T(8,128)(2,1)} custom-call(bf16[768,1024]{1,0:T(8,128)(2,1)S(1)} %total.26.refs_0_.refs_4_.refs_8_, bf16[384,1024]{1,0:T(8,128)(2,1)S(1)} %collective-permute-done.16.refs_1_, bf16[768,1024]{1,0:T(8,128)(2,1)} %collective-permute-done.17.refs_2_.refs_6_, bf16[768,1024]{1,0:T(8,128)(2,1)} %collective-permute-done.18.refs_3_.refs_7_, ...), custom_call_target="tpu_custom_call" | custom-call | flops 1 | bytes 1 | tf_op jit(solution)/shard_map/total/pallas_call | solution.py:26
  (72 shorter events, 5.3 us)
Async XLA Ops:
  0.0 7.1 %collective-permute-start = (s32[192]{0:T(256)}, s32[192]{0:T(256)S(1)}, u32[]{:S(2)}, u32[]{:S(2)}) collective-permute-start(s32[192]{0:T(256)} %param.7), channel_id=1, source_target_pairs={{0,1},{1,0},{2,3},{3,2},{4,5},{5,4},{6,7},{7,6},{8,9},{9,8},{10,11... | collective-permute-start | bytes 2312 | tf_op jit(solution)/shard_map/ppermute | solution.py:386
  0.0 7.8 %collective-permute-start.1 = (bf16[768,1024]{1,0:T(8,128)(2,1)}, bf16[768,1024]{1,0:T(8,128)(2,1)}, u32[]{:S(2)}, u32[]{:S(2)}) collective-permute-start(bf16[768,1024]{1,0:T(8,128)(2,1)} %bitcast.6), channel_id=1, source_target_pairs={{0,1},{1,0},{2,3},{3,2},{4,5},{5,4},{6,7},{7,6},{8,9},{9,8},{10,11... | collective-permute-start | bytes 4718600 | tf_op jit(solution)/shard_map/ppermute | solution.py:386
  1.2 1.4 copy-start
  2.6 4.0 %copy-start.19 = (s32[192]{0:T(256)S(1)}, s32[192]{0:T(256)}, u32[]{:S(2)}) copy-start(s32[192]{0:T(256)} %param.7) | copy-start | bytes 2308
  2.6 5.2 %copy-start.1 = (bf16[4,192,1024]{2,1,0:T(8,128)(2,1)S(1)}, bf16[4,192,1024]{2,1,0:T(8,128)(2,1)}, u32[]{:S(2)}) copy-start(bf16[4,192,1024]{2,1,0:T(8,128)(2,1)} %param.6) | copy-start | bytes 4718596
  6.0 22.6 %collective-permute-start.3 = (bf16[432,1024]{1,0:T(8,128)(2,1)S(1)}, bf16[432,1024]{1,0:T(8,128)(2,1)S(1)}, u32[]{:S(2)}, u32[]{:S(2)}) collective-permute-start(bf16[432,1024]{1,0:T(8,128)(2,1)S(1)} %products.5.refs_6_), channel_id=1, source_target_pairs={{0,2},{2,0},{4,6},{6,4},{8,10},{10,8},{12,14},{14,12},{1,3},{3,1},... | collective-permute-start | bytes 2654216 | tf_op jit(solution)/shard_map/ppermute | solution.py:373
  7.1 7.4 %copy-start.15 = (s32[192,1]{1,0:T(8,128)}, s32[192,1]{1,0:T(8,128)S(1)}, u32[]{:S(2)}) copy-start(s32[192,1]{1,0:T(8,128)S(1)} %copy.13.refs_3_.refs_2_) | copy-start | bytes 2308
  7.8 6.7 %copy-start.17 = (s32[192,1]{1,0:T(8,128)}, s32[192,1]{1,0:T(8,128)S(1)}, u32[]{:S(2)}) copy-start(s32[192,1]{1,0:T(8,128)S(1)} %copy.14.refs_4_.refs_3_) | copy-start | bytes 2308
  17.5 30.0 %collective-permute-start.2 = (bf16[432,1024]{1,0:T(8,128)(2,1)S(1)}, bf16[432,1024]{1,0:T(8,128)(2,1)S(1)}, u32[]{:S(2)}, u32[]{:S(2)}) collective-permute-start(bf16[432,1024]{1,0:T(8,128)(2,1)S(1)} %products.6.refs_3_), channel_id=1, source_target_pairs={{0,2},{2,0},{4,6},{6,4},{8,10},{10,8},{12,14},{14,12},{1,3},{3,1},... | collective-permute-start | bytes 2654216 | tf_op jit(solution)/shard_map/ppermute | solution.py:373
  25.5 55.9 %collective-permute-start.7 = (bf16[768,1024]{1,0:T(8,128)(2,1)}, bf16[768,1024]{1,0:T(8,128)(2,1)}, u32[]{:S(2)}, u32[]{:S(2)}) collective-permute-start(bf16[768,1024]{1,0:T(8,128)(2,1)} %get-tuple-element.16.refs_2_), channel_id=1, source_target_pairs={{0,2},{2,0},{4,6},{6,4},{8,10},{10,8},{12,14},{14,12},{1,3},{3,1},... | collective-permute-start | bytes 4718600 | tf_op jit(solution)/shard_map/ppermute | solution.py:373
  30.4 32.3 %collective-permute-start.5 = (bf16[432,1024]{1,0:T(8,128)(2,1)S(1)}, bf16[432,1024]{1,0:T(8,128)(2,1)S(1)}, u32[]{:S(2)}, u32[]{:S(2)}) collective-permute-start(bf16[432,1024]{1,0:T(8,128)(2,1)S(1)} %total.14.refs_3_.refs_0_), channel_id=1, source_target_pairs={{0,4},{12,8},{2,6},{14,10},{1,5},{13,9},{3,7},{15,11},{16,20},{28,... | collective-permute-start | bytes 2654216 | tf_op jit(solution)/shard_map/ppermute | solution.py:380
  38.1 1.2 copy-start.7
  47.5 3.3 %copy-start.8 = (bf16[768,1024]{1,0:T(8,128)(2,1)S(1)}, bf16[768,1024]{1,0:T(8,128)(2,1)}, u32[]{:S(2)}) copy-start(bf16[768,1024]{1,0:T(8,128)(2,1)} %copy-done.7) | copy-start | bytes 4718596
  49.3 21.6 %collective-permute-start.4 = (bf16[432,1024]{1,0:T(8,128)(2,1)S(1)}, bf16[432,1024]{1,0:T(8,128)(2,1)S(1)}, u32[]{:S(2)}, u32[]{:S(2)}) collective-permute-start(bf16[432,1024]{1,0:T(8,128)(2,1)S(1)} %total.15.refs_3_.refs_0_.refs_2_.refs_1_), channel_id=1, source_target_pairs={{0,4},{12,8},{2,6},{14,10},{1,5},{13,9},{3,7},{15,11},{16,20},{28,... | collective-permute-start | bytes 2654216 | tf_op jit(solution)/shard_map/ppermute | solution.py:380
  50.8 64.2 %collective-permute-start.10 = (bf16[768,1024]{1,0:T(8,128)(2,1)S(1)}, bf16[768,1024]{1,0:T(8,128)(2,1)}, u32[]{:S(2)}, u32[]{:S(2)}) collective-permute-start(bf16[768,1024]{1,0:T(8,128)(2,1)S(1)} %hold.2), channel_id=1, source_target_pairs={{0,2},{2,0},{4,6},{6,4},{8,10},{10,8},{12,14},{14,12},{1,3},{3,1},... | collective-permute-start | bytes 4718600 | tf_op jit(solution)/shard_map/ppermute | solution.py:373
  61.5 1.1 copy-start.5
  62.6 4.0 %copy-start.11 = (bf16[768,1024]{1,0:T(8,128)(2,1)}, bf16[768,1024]{1,0:T(8,128)(2,1)S(1)}, u32[]{:S(2)}) copy-start(bf16[768,1024]{1,0:T(8,128)(2,1)S(1)} %get-tuple-element.21.refs_0_) | copy-start | bytes 4718596
  62.6 1.0 copy-start.13
  63.6 1.2 copy-start.14
  66.6 24.5 %collective-permute-start.8 = (bf16[432,1024]{1,0:T(8,128)(2,1)S(1)}, bf16[432,1024]{1,0:T(8,128)(2,1)S(1)}, u32[]{:S(2)}, u32[]{:S(2)}) collective-permute-start(bf16[432,1024]{1,0:T(8,128)(2,1)S(1)} %total.16.refs_4_), channel_id=1, source_target_pairs={{4,8},{8,4},{6,10},{10,6},{5,9},{9,5},{7,11},{11,7},{20,24},{24,20... | collective-permute-start | bytes 2654216 | tf_op jit(solution)/shard_map/ppermute | solution.py:380
  72.8 34.1 %collective-permute-start.6 = (bf16[432,1024]{1,0:T(8,128)(2,1)S(1)}, bf16[432,1024]{1,0:T(8,128)(2,1)S(1)}, u32[]{:S(2)}, u32[]{:S(2)}) collective-permute-start(bf16[432,1024]{1,0:T(8,128)(2,1)S(1)} %total.17.refs_2_), channel_id=1, source_target_pairs={{4,8},{8,4},{6,10},{10,6},{5,9},{9,5},{7,11},{11,7},{20,24},{24,20... | collective-permute-start | bytes 2654216 | tf_op jit(solution)/shard_map/ppermute | solution.py:380
  83.0 2.2 %copy-start.6 = (bf16[768,1024]{1,0:T(8,128)(2,1)S(1)}, bf16[768,1024]{1,0:T(8,128)(2,1)}, u32[]{:S(2)}) copy-start(bf16[768,1024]{1,0:T(8,128)(2,1)} %copy-done.5) | copy-start | bytes 4718596
  85.2 73.2 %collective-permute-start.14 = (bf16[768,1024]{1,0:T(8,128)(2,1)S(1)}, bf16[768,1024]{1,0:T(8,128)(2,1)}, u32[]{:S(2)}, u32[]{:S(2)}) collective-permute-start(bf16[768,1024]{1,0:T(8,128)(2,1)S(1)} %hold.3), channel_id=1, source_target_pairs={{0,2},{2,0},{4,6},{6,4},{8,10},{10,8},{12,14},{14,12},{1,3},{3,1},... | collective-permute-start | bytes 4718600 | tf_op jit(solution)/shard_map/ppermute | solution.py:373
  85.8 23.4 %collective-permute-start.11 = (bf16[336,1024]{1,0:T(8,128)(2,1)S(1)}, bf16[336,1024]{1,0:T(8,128)(2,1)S(1)}, u32[]{:S(2)}, u32[]{:S(2)}) collective-permute-start(bf16[336,1024]{1,0:T(8,128)(2,1)S(1)} %total.18.refs_2_.refs_0_), channel_id=1, source_target_pairs={{0,4},{12,8},{2,6},{14,10},{1,5},{13,9},{3,7},{15,11},{16,20},{28,... | collective-permute-start | bytes 2064392 | tf_op jit(solution)/shard_map/ppermute | solution.py:380
  91.1 16.7 %copy-start.9 = (bf16[432,1024]{1,0:T(8,128)(2,1)}, bf16[432,1024]{1,0:T(8,128)(2,1)S(1)}, u32[]{:S(2)}) copy-start(bf16[432,1024]{1,0:T(8,128)(2,1)S(1)} %collective-permute-done.8.refs_3_.refs_1_) | copy-start | bytes 2654212
  91.1 42.4 %collective-permute-start.12 = (bf16[432,1024]{1,0:T(8,128)(2,1)S(1)}, bf16[432,1024]{1,0:T(8,128)(2,1)}, u32[]{:S(2)}, u32[]{:S(2)}) collective-permute-start(bf16[432,1024]{1,0:T(8,128)(2,1)S(1)} %total.19.refs_2_.refs_0_.refs_1_), channel_id=1, source_target_pairs={{0,4},{12,8},{2,6},{14,10},{1,5},{13,9},{3,7},{15,11},{16,20},{28,... | collective-permute-start | bytes 2654216 | tf_op jit(solution)/shard_map/ppermute | solution.py:380
  107.7 7.3 %copy-start.12 = (bf16[768,1024]{1,0:T(8,128)(2,1)S(1)}, bf16[768,1024]{1,0:T(8,128)(2,1)}, u32[]{:S(2)}) copy-start(bf16[768,1024]{1,0:T(8,128)(2,1)} %copy-done.11) | copy-start | bytes 4718596
  107.7 10.2 %collective-permute-start.9 = (bf16[96,1024]{1,0:T(8,128)(2,1)S(1)}, bf16[96,1024]{1,0:T(8,128)(2,1)S(1)}, u32[]{:S(2)}, u32[]{:S(2)}) collective-permute-start(bf16[96,1024]{1,0:T(8,128)(2,1)S(1)} %total.20.refs_2_), channel_id=1, source_target_pairs={{8,12},{4,0},{10,14},{6,2},{9,13},{5,1},{11,15},{7,3},{24,28},{20,... | collective-permute-start | bytes 589832 | tf_op jit(solution)/shard_map/ppermute | solution.py:380
  116.8 1.1 copy-start.2
  117.9 2.8 %copy-start.10 = (bf16[432,1024]{1,0:T(8,128)(2,1)S(1)}, bf16[432,1024]{1,0:T(8,128)(2,1)}, u32[]{:S(2)}) copy-start(bf16[432,1024]{1,0:T(8,128)(2,1)} %copy-done.9) | copy-start | bytes 2654212
  118.0 1.5 copy-start.3
  119.4 49.5 %collective-permute-start.17 = (bf16[768,1024]{1,0:T(8,128)(2,1)S(1)}, bf16[768,1024]{1,0:T(8,128)(2,1)}, u32[]{:S(2)}, u32[]{:S(2)}) collective-permute-start(bf16[768,1024]{1,0:T(8,128)(2,1)S(1)} %copy-done.3), channel_id=1, source_target_pairs={{0,4},{12,8},{2,6},{14,10},{1,5},{13,9},{3,7},{15,11},{16,20},{28,... | collective-permute-start | bytes 4718600 | tf_op jit(solution)/shard_map/ppermute | solution.py:380
  123.0 10.5 %copy-start.4 = (bf16[768,1024]{1,0:T(8,128)(2,1)}, bf16[768,1024]{1,0:T(8,128)(2,1)S(1)}, u32[]{:S(2)}) copy-start(bf16[768,1024]{1,0:T(8,128)(2,1)S(1)} %total.24.refs_2_) | copy-start | bytes 4718596
  123.0 27.3 %copy-start.16 = (s32[192,1]{1,0:T(8,128)S(1)}, s32[192,1]{1,0:T(8,128)}, u32[]{:S(2)}) copy-start(s32[192,1]{1,0:T(8,128)} %copy-done.15) | copy-start | bytes 2308
  123.0 27.3 %copy-start.18 = (s32[192,1]{1,0:T(8,128)S(1)}, s32[192,1]{1,0:T(8,128)}, u32[]{:S(2)}) copy-start(s32[192,1]{1,0:T(8,128)} %copy-done.17) | copy-start | bytes 2308
  123.0 45.9 %collective-permute-start.18 = (bf16[768,1024]{1,0:T(8,128)(2,1)S(1)}, bf16[768,1024]{1,0:T(8,128)(2,1)}, u32[]{:S(2)}, u32[]{:S(2)}) collective-permute-start(bf16[768,1024]{1,0:T(8,128)(2,1)S(1)} %total.24.refs_2_), channel_id=1, source_target_pairs={{8,12},{4,0},{10,14},{6,2},{9,13},{5,1},{11,15},{7,3},{24,28},{20,... | collective-permute-start | bytes 4718600 | tf_op jit(solution)/shard_map/ppermute | solution.py:380
  130.0 20.3 %collective-permute-start.13 = (bf16[336,1024]{1,0:T(8,128)(2,1)S(1)}, bf16[336,1024]{1,0:T(8,128)(2,1)S(1)}, u32[]{:S(2)}, u32[]{:S(2)}) collective-permute-start(bf16[336,1024]{1,0:T(8,128)(2,1)S(1)} %total.21.refs_2_), channel_id=1, source_target_pairs={{4,8},{8,4},{6,10},{10,6},{5,9},{9,5},{7,11},{11,7},{20,24},{24,20... | collective-permute-start | bytes 2064392 | tf_op jit(solution)/shard_map/ppermute | solution.py:380
  135.6 30.3 %collective-permute-start.15 = (bf16[432,1024]{1,0:T(8,128)(2,1)S(1)}, bf16[432,1024]{1,0:T(8,128)(2,1)S(1)}, u32[]{:S(2)}, u32[]{:S(2)}) collective-permute-start(bf16[432,1024]{1,0:T(8,128)(2,1)S(1)} %total.25.refs_5_), channel_id=1, source_target_pairs={{4,8},{8,4},{6,10},{10,6},{5,9},{9,5},{7,11},{11,7},{20,24},{24,20... | collective-permute-start | bytes 2654216 | tf_op jit(solution)/shard_map/ppermute | solution.py:380
  158.3 10.7 %collective-permute-start.16 = (bf16[384,1024]{1,0:T(8,128)(2,1)S(1)}, bf16[384,1024]{1,0:T(8,128)(2,1)S(1)}, u32[]{:S(2)}, u32[]{:S(2)}) collective-permute-start(bf16[384,1024]{1,0:T(8,128)(2,1)S(1)} %get-tuple-element.23), channel_id=1, source_target_pairs={{0,1},{1,0},{2,3},{3,2},{4,5},{5,4},{6,7},{7,6},{8,9},{9,8},{10,11... | collective-permute-start | bytes 2359304 | tf_op jit(solution)/shard_map/ppermute | solution.py:386
  158.3 10.6 %collective-permute-start.19 = (bf16[384,1024]{1,0:T(8,128)(2,1)S(1)}, bf16[384,1024]{1,0:T(8,128)(2,1)S(1)}, u32[]{:S(2)}, u32[]{:S(2)}) collective-permute-start(bf16[384,1024]{1,0:T(8,128)(2,1)S(1)} %get-tuple-element.24), channel_id=1, source_target_pairs={{0,1},{1,0},{2,3},{3,2},{4,5},{5,4},{6,7},{7,6},{8,9},{9,8},{10,11... | collective-permute-start | bytes 2359304 | tf_op jit(solution)/shard_map/ppermute | solution.py:386

commit v14 on v13

--- a/solution.py
+++ b/solution.py
@@ -17,7 +17,7 @@
 ANY = pl.BlockSpec(memory_space=pl.ANY)
 
 
-def call(kernel, operands, after, *, in_specs, out_specs, out_shape, name, prefetch=0, scratch=(), alias=None):
+def call(kernel, operands, after, *, in_specs, out_specs, out_shape, name, prefetch=0, scratch=(), alias=None, vmem=VMEM):
     inputs, extra = len(operands), len(after)
 
     def body(*refs):
@@ -34,7 +34,7 @@
         ),
         out_shape=out_shape,
         input_output_aliases=alias or {},
-        compiler_params=pltpu.CompilerParams(vmem_limit_bytes=VMEM),
+        compiler_params=pltpu.CompilerParams(vmem_limit_bytes=vmem),
         cost_estimate=pl.CostEstimate(flops=1, transcendentals=0, bytes_accessed=1),
         name=name,
     )(*operands, *after)
@@ -50,7 +50,7 @@
     )
 
 
-def products(rows, weight, starts, names, size, outs, tail=None, chunk=1024, after=()):
+def products(rows, weight, starts, names, size, outs, tail=None, chunk=1024, vmem=VMEM, after=()):
     count, width = rows.shape
     blocks = len(names)
     chunks = [(at, min(chunk, size - at)) for at in range(0, size, chunk)]
@@ -135,7 +135,7 @@
             pltpu.SemaphoreType.DMA((len(outs), len(chunks))),
             pltpu.SemaphoreType.DMA((2,)),
         ],
-        name="products",
+        name="products", vmem=vmem,
     )
 
 
@@ -438,12 +438,12 @@
     def whole(array):
         return [(0, count, array, 0)]
 
-    def multiply(aways, owns, tail=None, chunk=1024):
+    def multiply(aways, owns, tail=None, chunk=1024, vmem=VMEM):
         ks = sorted({k for k, _ in aways})
         names = ks + [nz + k for k in owns]
         outs = [(ks.index(k), *split(k)[p]) for k, p in aways]
         outs += [(len(ks) + i, 0, count) for i in range(len(owns))]
-        done = then(products, rows, projection_weight, starts, names, out_width, outs, tail, chunk)
+        done = then(products, rows, projection_weight, starts, names, out_width, outs, tail, chunk, vmem)
         away_part.update(zip(aways, done))
         own_all.update(zip(owns, done[len(aways) :]))
 
@@ -460,7 +460,7 @@
     def cut_of(h, m):
         if m == 0 and h <= 1:
             return uneven
-        return [(0, count * 7 // 16), (count * 7 // 16, count * 9 // 16)] if m == 1 else [(0, count)]
+        return [(0, count * 8 // 16), (count * 8 // 16, count * 8 // 16)] if m == 1 else [(0, count)]
 
     def arrived_parts(h, m):
         return [(*cut, arrived[h, m, p], 0) for p, cut in enumerate(cut_of(h, m)) if (h, m, p) in arrived]
@@ -493,7 +493,7 @@
 
     row_ids = [tenant] + [pass_on(tenant, shift) for shift in range(1, owners)]
     row_sets = [rows] + [pass_on(rows, shift) for shift in range(1, owners)]
-    multiply([(0, 0)], [], chunk=512)
+    multiply([(0, 0)], [], chunk=512, vmem=VMEM + 13 * 2**20)
     start_y(0, 0)
     named = [slots(some_ids, me) for some_ids in row_ids]
     names = jnp.concatenate([which for which, _ in named])
@@ -506,6 +506,8 @@
     low_sum = deltas = None
     for h, m, p in line_order():
         k = slot_of(h, m)
+        if (h, m, p) == (2, 0, 0) and nz == 4:
+            last[0] += (arrived[0, 1, 1],)
         line(h, m, p)
         if h == 0:
             if k == 0 and p == 0:

time: 174 us -> 167 us (0.960)
  the two profiles are of different devices: /device:TPU:14 before, /device:TPU:0 now
where the time goes in v14:
time: 167 us
  Pallas kernels  72.1 us (43%)
  waiting for transfers between devices  52.3 us (31%)
  starting transfers between devices  33 us (20%)
  local copies, waits for them, and re-layouts  7.76 us (5%)
    pallas_call x23, Pallas kernels, call(): pl.pallas_call(body, grid_spec=pltpu.PrefetchScalarGridSpec(num_scalar_pr...  72.1 us
    ppermute x5, waiting for transfers between devices, swap_y(): return lax.ppermute(value, 'tensor', [(t, t ^ 1) for t in range(n)])  29.2 us
    ppermute x11, starting transfers between devices, hop(): return lax.ppermute(value, 'tensor', pairs)  24.5 us
    ppermute x11, waiting for transfers between devices, hop(): return lax.ppermute(value, 'tensor', pairs)  23.1 us
    ppermute x5, starting transfers between devices, swap_y(): return lax.ppermute(value, 'tensor', [(t, t ^ 1) for t in range(n)])  7.88 us
    unnamed x24, local copies, waits for them, and re-layouts  6.33 us
  transfers between devices with their start and end apart: 20, of which 9 were waited for; matrix products, arithmetic and copies ran while one was open for 1% of the time, Pallas kernels for 41%

profile of v14, /device:TPU:0, one launch (start us, length us, event | category | flops | bytes accessed | tf_op | source)
XLA Modules:
  0.0 166.7 jit_solution(9634657422730915284)
XLA Ops:
  0.5 1.2 dynamic-slice_bitcast_fusion.refs_0_
  1.7 4.4 %products.5.refs_6_ = bf16[432,1024]{1,0:T(8,128)(2,1)} custom-call(s32[8]{0:T(128)} %dynamic-slice_bitcast_fusion.refs_0_, bf16[768,1024]{1,0:T(8,128)(2,1)} %bitcast.7, bf16[1024,8192]{1,0:T(8,128)(2,1)} %refs_2_.9), custom_call_target="tpu_custom_call" | custom-call | flops 1 | bytes 1 | tf_op jit(solution)/shard_map/products/pallas_call | solution.py:26
  6.1 3.0 %collective-permute-start.3 = (bf16[432,1024]{1,0:T(8,128)(2,1)}, bf16[432,1024]{1,0:T(8,128)(2,1)S(1)}, u32[]{:S(2)}, u32[]{:S(2)}) collective-permute-start(bf16[432,1024]{1,0:T(8,128)(2,1)} %products.5.refs_6_), channel_id=1, source_target_pairs={{0,2},{2,0},{4,6},{6,4},{8,10},{10,8},{12,14},{14,12},{1,3},{3,1},... | collective-permute-start | bytes 2654216 | tf_op jit(solution)/shard_map/ppermute | solution.py:373
  10.3 1.4 copy-done
  11.7 1.2 copy-done.8
  12.9 6.6 %low_rank.1.refs_3_.refs_4_.refs_2_ = bf16[96,1024]{1,0:T(8,128)(2,1)S(1)} custom-call(s32[32]{0:T(128)S(1)} %pad_add_fusion.refs_0_, bf16[768,1024]{1,0:T(8,128)(2,1)S(1)} %bitcast.11, bf16[768,1024]{1,0:T(8,128)(2,1)} %collective-permute-done.1.refs_2_, s32[192,1]{1,0:T(8,128)S(1)} %copy.13.refs_3_.refs_2_, s32[192,1]{1,0:T(8,128)S(1)} %copy.14.refs_4_.refs_3_, ...), custom_call_target="tpu_custom_call" | custom-call | flops 1 | bytes 1 | tf_op jit(solution)/shard_map/low_rank/pallas_call | solution.py:26
  19.5 3.0 %products.6.refs_3_ = bf16[432,1024]{1,0:T(8,128)(2,1)S(1)} custom-call(s32[8]{0:T(128)S(1)} %copy-done.9, bf16[768,1024]{1,0:T(8,128)(2,1)S(1)} %bitcast.12, bf16[1024,8192]{1,0:T(8,128)(2,1)} %refs_2_.9, bf16[96,1024]{1,0:T(8,128)(2,1)S(1)} %low_rank.1.refs_3_.refs_4_.refs_2_, bf16[96,1024]{1,0:T(8,128)(2,1)S(1)} %low_rank.1.refs_3_.refs_4_.refs_2_), custom_call_target="tpu_custom_call" | custom-call | flops 1 | bytes 1 | tf_op jit(solution)/shard_map/products/pallas_call | solution.py:26
  22.7 6.3 %products.7 = (bf16[768,1024]{1,0:T(8,128)(2,1)}, bf16[768,1024]{1,0:T(8,128)(2,1)S(1)}) custom-call(s32[8]{0:T(128)S(1)} %copy-done.9, bf16[768,1024]{1,0:T(8,128)(2,1)} %bitcast.8, bf16[1024,8192]{1,0:T(8,128)(2,1)} %refs_2_.9, bf16[432,1024]{1,0:T(8,128)(2,1)S(1)} %products.6.refs_3_), custom_call_target="tpu_custom_call" | custom-call | flops 1 | bytes 1 | tf_op jit(solution)/shard_map/products/pallas_call | solution.py:26
  29.0 0.8 collective-permute-done.3.refs_1_
  29.8 1.8 %total.14.refs_3_.refs_0_ = bf16[432,1024]{1,0:T(8,128)(2,1)S(1)} custom-call(bf16[768,1024]{1,0:T(8,128)(2,1)S(1)} %get-tuple-element.15.refs_0_, bf16[432,1024]{1,0:T(8,128)(2,1)S(1)} %collective-permute-done.3.refs_1_, bf16[768,1024]{1,0:T(8,128)(2,1)} %get-tuple-element.16.refs_2_), custom_call_target="tpu_custom_call" | custom-call | flops 1 | bytes 1 | tf_op jit(solution)/shard_map/total/pallas_call | solution.py:26
  31.6 4.1 %collective-permute-start.5 = (bf16[432,1024]{1,0:T(8,128)(2,1)S(1)}, bf16[432,1024]{1,0:T(8,128)(2,1)S(1)}, u32[]{:S(2)}, u32[]{:S(2)}) collective-permute-start(bf16[432,1024]{1,0:T(8,128)(2,1)S(1)} %total.14.refs_3_.refs_0_), channel_id=1, source_target_pairs={{0,4},{12,8},{2,6},{14,10},{1,5},{13,9},{3,7},{15,11},{16,20},{28,... | collective-permute-start | bytes 2654216 | tf_op jit(solution)/shard_map/ppermute | solution.py:380
  35.7 1.6 collective-permute-start.7
  37.2 6.4 %products.8 = (bf16[768,1024]{1,0:T(8,128)(2,1)S(1)}, bf16[768,1024]{1,0:T(8,128)(2,1)S(1)}) custom-call(s32[8]{0:T(128)S(1)} %copy-done.9, bf16[768,1024]{1,0:T(8,128)(2,1)} %bitcast.9, bf16[1024,8192]{1,0:T(8,128)(2,1)} %refs_2_.9, bf16[432,1024]{1,0:T(8,128)(2,1)S(1)} %total.14.refs_3_.refs_0_), custom_call_target="tpu_custom_call" | custom-call | flops 1 | bytes 1 | tf_op jit(solution)/shard_map/products/pallas_call | solution.py:26
  43.7 1.2 copy-done.6
  44.8 3.9 %collective-permute-done.2.refs_1_.refs_3_ = bf16[432,1024]{1,0:T(8,128)(2,1)S(1)} collective-permute-done((bf16[432,1024]{1,0:T(8,128)(2,1)S(1)}, bf16[432,1024]{1,0:T(8,128)(2,1)S(1)}, u32[]{:S(2)}, u32[]{:S(2)}) %collective-permute-start.2) | collective-permute-done | bytes 884768 | tf_op jit(solution)/shard_map/ppermute | solution.py:373
  48.8 1.8 %total.15.refs_3_.refs_0_.refs_2_.refs_1_ = bf16[432,1024]{1,0:T(8,128)(2,1)S(1)} custom-call(bf16[768,1024]{1,0:T(8,128)(2,1)S(1)} %get-tuple-element.15.refs_0_, bf16[432,1024]{1,0:T(8,128)(2,1)S(1)} %collective-permute-done.2.refs_1_.refs_3_, bf16[96,1024]{1,0:T(8,128)(2,1)S(1)} %low_rank.1.refs_3_.refs_4_.refs_2_, ...), custom_call_target="tpu_custom_call" | custom-call | flops 1 | bytes 1 | tf_op jit(solution)/shard_map/total/pallas_call | solution.py:26
  50.6 4.3 %collective-permute-start.4 = (bf16[432,1024]{1,0:T(8,128)(2,1)S(1)}, bf16[432,1024]{1,0:T(8,128)(2,1)S(1)}, u32[]{:S(2)}, u32[]{:S(2)}) collective-permute-start(bf16[432,1024]{1,0:T(8,128)(2,1)S(1)} %total.15.refs_3_.refs_0_.refs_2_.refs_1_), channel_id=1, source_target_pairs={{0,4},{12,8},{2,6},{14,10},{1,5},{13,9},{3,7},{15,11},{16,20},{28,... | collective-permute-start | bytes 2654216 | tf_op jit(solution)/shard_map/ppermute | solution.py:380
  54.8 10.0 %products.9 = (bf16[768,1024]{1,0:T(8,128)(2,1)S(1)}, bf16[768,1024]{1,0:T(8,128)(2,1)S(1)}, bf16[768,1024]{1,0:T(8,128)(2,1)}) custom-call(s32[8]{0:T(128)S(1)} %copy-done.9, bf16[768,1024]{1,0:T(8,128)(2,1)} %bitcast.10, bf16[1024,8192]{1,0:T(8,128)(2,1)} %refs_2_.9, bf16[432,1024]{1,0:T(8,128)(2,1)S(1)} %total.15.refs_3_.refs_0_.refs_2_.refs_1_), custom_call_target="tpu_custom_call" | custom-call | flops 1 | bytes 1 | tf_op jit(solution)/shard_map/products/pallas_call | solution.py:26
  64.9 1.2 copy-done.4
  66.1 1.8 %total.16.refs_4_ = bf16[432,1024]{1,0:T(8,128)(2,1)S(1)} custom-call(bf16[432,1024]{1,0:T(8,128)(2,1)S(1)} %total.14.refs_3_.refs_0_, bf16[432,1024]{1,0:T(8,128)(2,1)S(1)} %collective-permute-done.5.refs_1_, bf16[768,1024]{1,0:T(8,128)(2,1)} %copy-done.4), custom_call_target="tpu_custom_call" | custom-call | flops 1 | bytes 1 | tf_op jit(solution)/shard_map/total/pallas_call | solution.py:26
  68.6 1.6 collective-permute-start.10
  70.2 2.6 %collective-permute-done.4.refs_1_.refs_3_ = bf16[432,1024]{1,0:T(8,128)(2,1)S(1)} collective-permute-done((bf16[432,1024]{1,0:T(8,128)(2,1)S(1)}, bf16[432,1024]{1,0:T(8,128)(2,1)S(1)}, u32[]{:S(2)}, u32[]{:S(2)}) %collective-permute-start.4) | collective-permute-done | bytes 884768 | tf_op jit(solution)/shard_map/ppermute | solution.py:380
  72.8 1.8 %total.17.refs_2_ = bf16[432,1024]{1,0:T(8,128)(2,1)S(1)} custom-call(bf16[432,1024]{1,0:T(8,128)(2,1)S(1)} %total.15.refs_3_.refs_0_.refs_2_.refs_1_, bf16[432,1024]{1,0:T(8,128)(2,1)S(1)} %collective-permute-done.4.refs_1_.refs_3_, bf16[432,1024]{1,0:T(8,128)(2,1)S(1)} %total.15.refs_3_.refs_0_.refs_2_.refs_1_, ...), custom_call_target="tpu_custom_call" | custom-call | flops 1 | bytes 1 | tf_op jit(solution)/shard_map/total/pallas_call | solution.py:26
  75.3 7.3 %collective-permute-done.7.refs_1_ = bf16[768,1024]{1,0:T(8,128)(2,1)} collective-permute-done((bf16[768,1024]{1,0:T(8,128)(2,1)}, bf16[768,1024]{1,0:T(8,128)(2,1)}, u32[]{:S(2)}, u32[]{:S(2)}) %collective-permute-start.7) | collective-permute-done | bytes 1572896 | tf_op jit(solution)/shard_map/ppermute | solution.py:373
  82.6 1.8 %total.18.refs_2_.refs_0_ = bf16[384,1024]{1,0:T(8,128)(2,1)S(1)} custom-call(bf16[768,1024]{1,0:T(8,128)(2,1)S(1)} %get-tuple-element.20.refs_0_, bf16[768,1024]{1,0:T(8,128)(2,1)} %collective-permute-done.7.refs_1_, bf16[432,1024]{1,0:T(8,128)(2,1)S(1)} %total.17.refs_2_), custom_call_target="tpu_custom_call" | custom-call | flops 1 | bytes 1 | tf_op jit(solution)/shard_map/total/pallas_call | solution.py:26
  84.4 5.1 %collective-permute-start.11 = (bf16[384,1024]{1,0:T(8,128)(2,1)S(1)}, bf16[384,1024]{1,0:T(8,128)(2,1)}, u32[]{:S(2)}, u32[]{:S(2)}) collective-permute-start(bf16[384,1024]{1,0:T(8,128)(2,1)S(1)} %total.18.refs_2_.refs_0_), channel_id=1, source_target_pairs={{0,4},{12,8},{2,6},{14,10},{1,5},{13,9},{3,7},{15,11},{16,20},{28,... | collective-permute-start | bytes 2359304 | tf_op jit(solution)/shard_map/ppermute | solution.py:380
  89.4 1.8 %total.19.refs_2_.refs_0_.refs_1_ = bf16[384,1024]{1,0:T(8,128)(2,1)S(1)} custom-call(bf16[768,1024]{1,0:T(8,128)(2,1)S(1)} %get-tuple-element.20.refs_0_, bf16[768,1024]{1,0:T(8,128)(2,1)} %collective-permute-done.7.refs_1_, bf16[384,1024]{1,0:T(8,128)(2,1)S(1)} %total.18.refs_2_.refs_0_), custom_call_target="tpu_custom_call" | custom-call | flops 1 | bytes 1 | tf_op jit(solution)/shard_map/total/pallas_call | solution.py:26
  91.3 1.6 collective-permute-start.14
  92.8 1.3 collective-permute-start.12
  94.2 0.8 total.20.refs_2_
  95.0 1.3 collective-permute-start.9
  96.3 10.2 %collective-permute-done.11.refs_1_ = bf16[384,1024]{1,0:T(8,128)(2,1)} collective-permute-done((bf16[384,1024]{1,0:T(8,128)(2,1)S(1)}, bf16[384,1024]{1,0:T(8,128)(2,1)}, u32[]{:S(2)}, u32[]{:S(2)}) %collective-permute-start.11) | collective-permute-done | bytes 786464 | tf_op jit(solution)/shard_map/ppermute | solution.py:380
  106.5 1.8 %total.21.refs_2_ = bf16[384,1024]{1,0:T(8,128)(2,1)S(1)} custom-call(bf16[384,1024]{1,0:T(8,128)(2,1)S(1)} %total.18.refs_2_.refs_0_, bf16[384,1024]{1,0:T(8,128)(2,1)} %collective-permute-done.11.refs_1_, bf16[96,1024]{1,0:T(8,128)(2,1)S(1)} %total.20.refs_2_), custom_call_target="tpu_custom_call" | custom-call | flops 1 | bytes 1 | tf_op jit(solution)/shard_map/total/pallas_call | solution.py:26
  109.0 7.2 %collective-permute-done.10.refs_1_ = bf16[768,1024]{1,0:T(8,128)(2,1)} collective-permute-done((bf16[768,1024]{1,0:T(8,128)(2,1)S(1)}, bf16[768,1024]{1,0:T(8,128)(2,1)}, u32[]{:S(2)}, u32[]{:S(2)}) %collective-permute-start.10) | collective-permute-done | bytes 1572896 | tf_op jit(solution)/shard_map/ppermute | solution.py:373
  116.3 1.7 %total.22.refs_4_.refs_0_.refs_2_ = bf16[768,1024]{1,0:T(8,128)(2,1)S(1)} custom-call(bf16[768,1024]{1,0:T(8,128)(2,1)S(1)} %get-tuple-element.21.refs_0_, bf16[768,1024]{1,0:T(8,128)(2,1)} %collective-permute-done.10.refs_1_, bf16[384,1024]{1,0:T(8,128)(2,1)S(1)} %total.21.refs_2_), custom_call_target="tpu_custom_call" | custom-call | flops 1 | bytes 1 | tf_op jit(solution)/shard_map/total/pallas_call | solution.py:26
  118.0 4.1 %collective-permute-start.17 = (bf16[768,1024]{1,0:T(8,128)(2,1)S(1)}, bf16[768,1024]{1,0:T(8,128)(2,1)S(1)}, u32[]{:S(2)}, u32[]{:S(2)}) collective-permute-start(bf16[768,1024]{1,0:T(8,128)(2,1)S(1)} %total.22.refs_4_.refs_0_.refs_2_), channel_id=1, source_target_pairs={{0,4},{12,8},{2,6},{14,10},{1,5},{13,9},{3,7},{15,11},{16,20},{28,... | collective-permute-start | bytes 4718600 | tf_op jit(solution)/shard_map/ppermute | solution.py:380
  122.2 1.4 total.23.refs_4_.refs_1_
  123.6 2.6 %total.24.refs_2_ = bf16[768,1024]{1,0:T(8,128)(2,1)} custom-call(bf16[768,1024]{1,0:T(8,128)(2,1)} %copy-done.2, bf16[432,1024]{1,0:T(8,128)(2,1)S(1)} %collective-permute-done.8.refs_3_.refs_1_, bf16[768,1024]{1,0:T(8,128)(2,1)} %copy-done.2, bf16[432,1024]{1,0:T(8,128)(2,1)S(1)} %collective-permute-done.6.refs_1_.refs_2_.refs_3_, ...), custom_call_target="tpu_custom_call" | custom-call | flops 1 | bytes 1 | tf_op jit(solution)/shard_map/total/pallas_call | solution.py:26
  126.2 1.3 collective-permute-start.18
  127.5 1.4 copy-done.3
  128.9 1.4 total.25.refs_5_
  130.3 0.9 collective-permute-start.15
  131.3 8.0 %expand.1 = (bf16[768,1024]{1,0:T(8,128)(2,1)}, bf16[384,1024]{1,0:T(8,128)(2,1)S(1)}, bf16[384,1024]{1,0:T(8,128)(2,1)S(1)}) custom-call(s32[32]{0:T(128)S(1)} %pad_add_fusion.refs_0_, bf16[96,1024]{1,0:T(8,128)(2,1)S(1)} %total.23.refs_4_.refs_1_, s32[192,1]{1,0:T(8,128)S(1)} %copy.13.refs_3_.refs_2_, s32[192,1]{1,0:T(8,128)S(1)} %copy.14.refs_4_.refs_3_, ...), custom_call_target="tpu_custom_call" | custom-call | flops 1 | bytes 1 | tf_op jit(solution)/shard_map/expand/pallas_call | solution.py:26
  139.4 10.0 %collective-permute-done.14.refs_2_.refs_6_ = bf16[768,1024]{1,0:T(8,128)(2,1)} collective-permute-done((bf16[768,1024]{1,0:T(8,128)(2,1)S(1)}, bf16[768,1024]{1,0:T(8,128)(2,1)}, u32[]{:S(2)}, u32[]{:S(2)}) %collective-permute-start.14) | collective-permute-done | bytes 1572896 | tf_op jit(solution)/shard_map/ppermute | solution.py:373
  149.3 3.0 %total.26.refs_0_.refs_4_.refs_8_ = bf16[768,1024]{1,0:T(8,128)(2,1)S(1)} custom-call(bf16[768,1024]{1,0:T(8,128)(2,1)} %get-tuple-element.18.refs_0_.refs_4_, bf16[768,1024]{1,0:T(8,128)(2,1)} %get-tuple-element.22.refs_1_.refs_5_.refs_8_, bf16[768,1024]{1,0:T(8,128)(2,1)} %collective-permute-done.14.refs_2_.refs_6_, ...), custom_call_target="tpu_custom_call" | custom-call | flops 1 | bytes 1 | tf_op jit(solution)/shard_map/total/pallas_call | solution.py:26
  152.3 1.9 %collective-permute-done.17.refs_2_.refs_6_ = bf16[768,1024]{1,0:T(8,128)(2,1)S(1)} collective-permute-done((bf16[768,1024]{1,0:T(8,128)(2,1)S(1)}, bf16[768,1024]{1,0:T(8,128)(2,1)S(1)}, u32[]{:S(2)}, u32[]{:S(2)}) %collective-permute-start.17) | collective-permute-done | bytes 1572896 | tf_op jit(solution)/shard_map/ppermute | solution.py:380
  154.2 8.4 %collective-permute-done.18.refs_3_.refs_7_ = bf16[768,1024]{1,0:T(8,128)(2,1)} collective-permute-done((bf16[768,1024]{1,0:T(8,128)(2,1)}, bf16[768,1024]{1,0:T(8,128)(2,1)}, u32[]{:S(2)}, u32[]{:S(2)}) %collective-permute-start.18) | collective-permute-done | bytes 1572896 | tf_op jit(solution)/shard_map/ppermute | solution.py:380
  162.7 3.9 %total.27 = bf16[768,1024]{1,0:T(8,128)(2,1)} custom-call(bf16[768,1024]{1,0:T(8,128)(2,1)S(1)} %total.26.refs_0_.refs_4_.refs_8_, bf16[384,1024]{1,0:T(8,128)(2,1)S(1)} %collective-permute-done.16.refs_1_, bf16[768,1024]{1,0:T(8,128)(2,1)} %copy-done.10, bf16[768,1024]{1,0:T(8,128)(2,1)} %collective-permute-done.18.refs_3_.refs_7_, ...), custom_call_target="tpu_custom_call" | custom-call | flops 1 | bytes 1 | tf_op jit(solution)/shard_map/total/pallas_call | solution.py:26
  (56 shorter events, 4.0 us)
Async XLA Ops:
  0.0 9.6 %collective-permute-start = (s32[192]{0:T(256)}, s32[192]{0:T(256)S(1)}, u32[]{:S(2)}, u32[]{:S(2)}) collective-permute-start(s32[192]{0:T(256)} %param.7), channel_id=1, source_target_pairs={{0,1},{1,0},{2,3},{3,2},{4,5},{5,4},{6,7},{7,6},{8,9},{9,8},{10,11... | collective-permute-start | bytes 2312 | tf_op jit(solution)/shard_map/ppermute | solution.py:386
  0.5 9.9 %collective-permute-start.1 = (bf16[768,1024]{1,0:T(8,128)(2,1)}, bf16[768,1024]{1,0:T(8,128)(2,1)}, u32[]{:S(2)}, u32[]{:S(2)}) collective-permute-start(bf16[768,1024]{1,0:T(8,128)(2,1)} %bitcast.6), channel_id=1, source_target_pairs={{0,1},{1,0},{2,3},{3,2},{4,5},{5,4},{6,7},{7,6},{8,9},{9,8},{10,11... | collective-permute-start | bytes 4718600 | tf_op jit(solution)/shard_map/ppermute | solution.py:386
  1.7 7.4 %copy-start.11 = (s32[192]{0:T(256)S(1)}, s32[192]{0:T(256)}, u32[]{:S(2)}) copy-start(s32[192]{0:T(256)} %param.7) | copy-start | bytes 2308
  6.1 23.7 %collective-permute-start.3 = (bf16[432,1024]{1,0:T(8,128)(2,1)}, bf16[432,1024]{1,0:T(8,128)(2,1)S(1)}, u32[]{:S(2)}, u32[]{:S(2)}) collective-permute-start(bf16[432,1024]{1,0:T(8,128)(2,1)} %products.5.refs_6_), channel_id=1, source_target_pairs={{0,2},{2,0},{4,6},{6,4},{8,10},{10,8},{12,14},{14,12},{1,3},{3,1},... | collective-permute-start | bytes 2654216 | tf_op jit(solution)/shard_map/ppermute | solution.py:373
  10.3 1.4 copy-start
  11.7 1.2 copy-start.8
  12.9 6.6 %copy-start.1 = (bf16[4,192,1024]{2,1,0:T(8,128)(2,1)S(1)}, bf16[4,192,1024]{2,1,0:T(8,128)(2,1)}, u32[]{:S(2)}) copy-start(bf16[4,192,1024]{2,1,0:T(8,128)(2,1)} %param.6) | copy-start | bytes 4718596
  12.9 6.6 %copy-start.9 = (s32[8]{0:T(128)S(1)}, s32[8]{0:T(128)}, u32[]{:S(2)}) copy-start(s32[8]{0:T(128)} %dynamic-slice_bitcast_fusion.refs_0_) | copy-start | bytes 100
  22.6 26.2 %collective-permute-start.2 = (bf16[432,1024]{1,0:T(8,128)(2,1)S(1)}, bf16[432,1024]{1,0:T(8,128)(2,1)S(1)}, u32[]{:S(2)}, u32[]{:S(2)}) collective-permute-start(bf16[432,1024]{1,0:T(8,128)(2,1)S(1)} %products.6.refs_3_), channel_id=1, source_target_pairs={{0,2},{2,0},{4,6},{6,4},{8,10},{10,8},{12,14},{14,12},{1,3},{3,1},... | collective-permute-start | bytes 2654216 | tf_op jit(solution)/shard_map/ppermute | solution.py:373
  31.6 34.5 %collective-permute-start.5 = (bf16[432,1024]{1,0:T(8,128)(2,1)S(1)}, bf16[432,1024]{1,0:T(8,128)(2,1)S(1)}, u32[]{:S(2)}, u32[]{:S(2)}) collective-permute-start(bf16[432,1024]{1,0:T(8,128)(2,1)S(1)} %total.14.refs_3_.refs_0_), channel_id=1, source_target_pairs={{0,4},{12,8},{2,6},{14,10},{1,5},{13,9},{3,7},{15,11},{16,20},{28,... | collective-permute-start | bytes 2654216 | tf_op jit(solution)/shard_map/ppermute | solution.py:380
  35.7 46.9 %collective-permute-start.7 = (bf16[768,1024]{1,0:T(8,128)(2,1)}, bf16[768,1024]{1,0:T(8,128)(2,1)}, u32[]{:S(2)}, u32[]{:S(2)}) collective-permute-start(bf16[768,1024]{1,0:T(8,128)(2,1)} %get-tuple-element.16.refs_2_), channel_id=1, source_target_pairs={{0,2},{2,0},{4,6},{6,4},{8,10},{10,8},{12,14},{14,12},{1,3},{3,1},... | collective-permute-start | bytes 4718600 | tf_op jit(solution)/shard_map/ppermute | solution.py:373
  43.7 1.2 copy-start.6
  50.6 22.2 %collective-permute-start.4 = (bf16[432,1024]{1,0:T(8,128)(2,1)S(1)}, bf16[432,1024]{1,0:T(8,128)(2,1)S(1)}, u32[]{:S(2)}, u32[]{:S(2)}) collective-permute-start(bf16[432,1024]{1,0:T(8,128)(2,1)S(1)} %total.15.refs_3_.refs_0_.refs_2_.refs_1_), channel_id=1, source_target_pairs={{0,4},{12,8},{2,6},{14,10},{1,5},{13,9},{3,7},{15,11},{16,20},{28,... | collective-permute-start | bytes 2654216 | tf_op jit(solution)/shard_map/ppermute | solution.py:380
  64.9 1.2 copy-start.4
  66.1 2.5 %copy-start.7 = (bf16[768,1024]{1,0:T(8,128)(2,1)S(1)}, bf16[768,1024]{1,0:T(8,128)(2,1)}, u32[]{:S(2)}) copy-start(bf16[768,1024]{1,0:T(8,128)(2,1)} %copy-done.6) | copy-start | bytes 4718596
  67.8 25.0 %collective-permute-start.8 = (bf16[432,1024]{1,0:T(8,128)(2,1)S(1)}, bf16[432,1024]{1,0:T(8,128)(2,1)S(1)}, u32[]{:S(2)}, u32[]{:S(2)}) collective-permute-start(bf16[432,1024]{1,0:T(8,128)(2,1)S(1)} %total.16.refs_4_), channel_id=1, source_target_pairs={{4,8},{8,4},{6,10},{10,6},{5,9},{9,5},{7,11},{11,7},{20,24},{24,20... | collective-permute-start | bytes 2654216 | tf_op jit(solution)/shard_map/ppermute | solution.py:380
  68.6 47.7 %collective-permute-start.10 = (bf16[768,1024]{1,0:T(8,128)(2,1)S(1)}, bf16[768,1024]{1,0:T(8,128)(2,1)}, u32[]{:S(2)}, u32[]{:S(2)}) collective-permute-start(bf16[768,1024]{1,0:T(8,128)(2,1)S(1)} %hold.2), channel_id=1, source_target_pairs={{0,2},{2,0},{4,6},{6,4},{8,10},{10,8},{12,14},{14,12},{1,3},{3,1},... | collective-permute-start | bytes 4718600 | tf_op jit(solution)/shard_map/ppermute | solution.py:373
  74.6 19.6 %collective-permute-start.6 = (bf16[432,1024]{1,0:T(8,128)(2,1)S(1)}, bf16[432,1024]{1,0:T(8,128)(2,1)S(1)}, u32[]{:S(2)}, u32[]{:S(2)}) collective-permute-start(bf16[432,1024]{1,0:T(8,128)(2,1)S(1)} %total.17.refs_2_), channel_id=1, source_target_pairs={{4,8},{8,4},{6,10},{10,6},{5,9},{9,5},{7,11},{11,7},{20,24},{24,20... | collective-permute-start | bytes 2654216 | tf_op jit(solution)/shard_map/ppermute | solution.py:380
  84.4 6.9 %copy-start.5 = (bf16[768,1024]{1,0:T(8,128)(2,1)S(1)}, bf16[768,1024]{1,0:T(8,128)(2,1)}, u32[]{:S(2)}) copy-start(bf16[768,1024]{1,0:T(8,128)(2,1)} %copy-done.4) | copy-start | bytes 4718596
  84.4 22.1 %collective-permute-start.11 = (bf16[384,1024]{1,0:T(8,128)(2,1)S(1)}, bf16[384,1024]{1,0:T(8,128)(2,1)}, u32[]{:S(2)}, u32[]{:S(2)}) collective-permute-start(bf16[384,1024]{1,0:T(8,128)(2,1)S(1)} %total.18.refs_2_.refs_0_), channel_id=1, source_target_pairs={{0,4},{12,8},{2,6},{14,10},{1,5},{13,9},{3,7},{15,11},{16,20},{28,... | collective-permute-start | bytes 2359304 | tf_op jit(solution)/shard_map/ppermute | solution.py:380
  91.3 58.1 %collective-permute-start.14 = (bf16[768,1024]{1,0:T(8,128)(2,1)S(1)}, bf16[768,1024]{1,0:T(8,128)(2,1)}, u32[]{:S(2)}, u32[]{:S(2)}) collective-permute-start(bf16[768,1024]{1,0:T(8,128)(2,1)S(1)} %hold.3), channel_id=1, source_target_pairs={{0,2},{2,0},{4,6},{6,4},{8,10},{10,8},{12,14},{14,12},{1,3},{3,1},... | collective-permute-start | bytes 4718600 | tf_op jit(solution)/shard_map/ppermute | solution.py:373
  92.8 30.8 %collective-permute-start.12 = (bf16[384,1024]{1,0:T(8,128)(2,1)S(1)}, bf16[384,1024]{1,0:T(8,128)(2,1)S(1)}, u32[]{:S(2)}, u32[]{:S(2)}) collective-permute-start(bf16[384,1024]{1,0:T(8,128)(2,1)S(1)} %total.19.refs_2_.refs_0_.refs_1_), channel_id=1, source_target_pairs={{0,4},{12,8},{2,6},{14,10},{1,5},{13,9},{3,7},{15,11},{16,20},{28,... | collective-permute-start | bytes 2359304 | tf_op jit(solution)/shard_map/ppermute | solution.py:380
  95.0 27.1 %collective-permute-start.9 = (bf16[96,1024]{1,0:T(8,128)(2,1)S(1)}, bf16[96,1024]{1,0:T(8,128)(2,1)S(1)}, u32[]{:S(2)}, u32[]{:S(2)}) collective-permute-start(bf16[96,1024]{1,0:T(8,128)(2,1)S(1)} %total.20.refs_2_), channel_id=1, source_target_pairs={{8,12},{4,0},{10,14},{6,2},{9,13},{5,1},{11,15},{7,3},{24,28},{20,... | collective-permute-start | bytes 589832 | tf_op jit(solution)/shard_map/ppermute | solution.py:380
  108.3 22.9 %collective-permute-start.13 = (bf16[384,1024]{1,0:T(8,128)(2,1)S(1)}, bf16[384,1024]{1,0:T(8,128)(2,1)S(1)}, u32[]{:S(2)}, u32[]{:S(2)}) collective-permute-start(bf16[384,1024]{1,0:T(8,128)(2,1)S(1)} %total.21.refs_2_), channel_id=1, source_target_pairs={{4,8},{8,4},{6,10},{10,6},{5,9},{9,5},{7,11},{11,7},{20,24},{24,20... | collective-permute-start | bytes 2359304 | tf_op jit(solution)/shard_map/ppermute | solution.py:380
  118.0 4.2 %copy-start.2 = (bf16[768,1024]{1,0:T(8,128)(2,1)}, bf16[768,1024]{1,0:T(8,128)(2,1)S(1)}, u32[]{:S(2)}) copy-start(bf16[768,1024]{1,0:T(8,128)(2,1)S(1)} %total.22.refs_4_.refs_0_.refs_2_) | copy-start | bytes 4718596
  118.0 36.2 %collective-permute-start.17 = (bf16[768,1024]{1,0:T(8,128)(2,1)S(1)}, bf16[768,1024]{1,0:T(8,128)(2,1)S(1)}, u32[]{:S(2)}, u32[]{:S(2)}) collective-permute-start(bf16[768,1024]{1,0:T(8,128)(2,1)S(1)} %total.22.refs_4_.refs_0_.refs_2_), channel_id=1, source_target_pairs={{0,4},{12,8},{2,6},{14,10},{1,5},{13,9},{3,7},{15,11},{16,20},{28,... | collective-permute-start | bytes 4718600 | tf_op jit(solution)/shard_map/ppermute | solution.py:380
  126.2 36.4 %collective-permute-start.18 = (bf16[768,1024]{1,0:T(8,128)(2,1)}, bf16[768,1024]{1,0:T(8,128)(2,1)}, u32[]{:S(2)}, u32[]{:S(2)}) collective-permute-start(bf16[768,1024]{1,0:T(8,128)(2,1)} %total.24.refs_2_), channel_id=1, source_target_pairs={{8,12},{4,0},{10,14},{6,2},{9,13},{5,1},{11,15},{7,3},{24,28},{20,... | collective-permute-start | bytes 4718600 | tf_op jit(solution)/shard_map/ppermute | solution.py:380
  127.5 1.4 copy-start.3
  130.3 19.0 %collective-permute-start.15 = (bf16[384,1024]{1,0:T(8,128)(2,1)S(1)}, bf16[384,1024]{1,0:T(8,128)(2,1)S(1)}, u32[]{:S(2)}, u32[]{:S(2)}) collective-permute-start(bf16[384,1024]{1,0:T(8,128)(2,1)S(1)} %total.25.refs_5_), channel_id=1, source_target_pairs={{4,8},{8,4},{6,10},{10,6},{5,9},{9,5},{7,11},{11,7},{20,24},{24,20... | collective-permute-start | bytes 2359304 | tf_op jit(solution)/shard_map/ppermute | solution.py:380
  139.3 14.9 %collective-permute-start.16 = (bf16[384,1024]{1,0:T(8,128)(2,1)S(1)}, bf16[384,1024]{1,0:T(8,128)(2,1)S(1)}, u32[]{:S(2)}, u32[]{:S(2)}) collective-permute-start(bf16[384,1024]{1,0:T(8,128)(2,1)S(1)} %get-tuple-element.23), channel_id=1, source_target_pairs={{0,1},{1,0},{2,3},{3,2},{4,5},{5,4},{6,7},{7,6},{8,9},{9,8},{10,11... | collective-permute-start | bytes 2359304 | tf_op jit(solution)/shard_map/ppermute | solution.py:386
  149.3 4.9 %collective-permute-start.19 = (bf16[384,1024]{1,0:T(8,128)(2,1)S(1)}, bf16[384,1024]{1,0:T(8,128)(2,1)S(1)}, u32[]{:S(2)}, u32[]{:S(2)}) collective-permute-start(bf16[384,1024]{1,0:T(8,128)(2,1)S(1)} %get-tuple-element.24), channel_id=1, source_target_pairs={{0,1},{1,0},{2,3},{3,2},{4,5},{5,4},{6,7},{7,6},{8,9},{9,8},{10,11... | collective-permute-start | bytes 2359304 | tf_op jit(solution)/shard_map/ppermute | solution.py:386
  154.2 8.4 %copy-start.10 = (bf16[768,1024]{1,0:T(8,128)(2,1)}, bf16[768,1024]{1,0:T(8,128)(2,1)S(1)}, u32[]{:S(2)}) copy-start(bf16[768,1024]{1,0:T(8,128)(2,1)S(1)} %collective-permute-done.17.refs_2_.refs_6_) | copy-start | bytes 4718596

commit v15 on v14

--- a/solution.py
+++ b/solution.py
@@ -235,11 +235,11 @@
     repeats = count // slot_sets[0].shape[0]
     half = count // 2
     group = 256
-    tall = sets * half * 2 * rank // wide
+    tall = half * 2 * rank // wide
 
     def kernel(index_ref, *refs):
-        row_refs, slot_refs, maps_ref, out_ref = refs[:sets], refs[sets : 2 * sets], refs[2 * sets], refs[2 * sets + 1]
-        rows_buf, maps_buf, row_sems, map_sems = refs[2 * sets + 2 :]
+        row_refs, slot_refs, maps_ref = refs[:sets], refs[sets : 2 * sets], refs[2 * sets]
+        out_refs, (rows_buf, maps_buf, row_sems, map_sems) = refs[2 * sets + 1 : 3 * sets + 1], refs[3 * sets + 1 :]
         row_copies = [
             pltpu.make_async_copy(row_refs[s], rows_buf.at[s], row_sems.at[s]) for s in range(sets)
         ]
@@ -264,17 +264,17 @@
             summed = acc[:, 0:rank]
             for g in range(1, group // rank):
                 summed += acc[:, g * rank : (g + 1) * rank]
-            summed = summed.astype(out_ref.dtype)
+            summed = summed.astype(out_refs[s].dtype)
             for b in range(half // tall):
-                lanes = slice((s * half // tall + b) * 2 * rank, (s * half // tall + b + 1) * 2 * rank)
+                lanes = slice(b * 2 * rank, (b + 1) * 2 * rank)
                 both = [summed[start + b * tall : start + (b + 1) * tall] for start in (0, half)]
-                out_ref[:, lanes] = jnp.concatenate(both, axis=1)
+                out_refs[s][:, lanes] = jnp.concatenate(both, axis=1)
 
     return call(
         kernel, [index, *row_sets, *slot_sets, maps], after, prefetch=1,
         in_specs=[ANY] * sets + [pl.BlockSpec(memory_space=pltpu.VMEM)] * sets + [ANY],
-        out_specs=pl.BlockSpec(memory_space=pltpu.VMEM),
-        out_shape=jax.ShapeDtypeStruct((tall, wide), jnp.bfloat16),
+        out_specs=[pl.BlockSpec(memory_space=pltpu.VMEM)] * sets,
+        out_shape=[jax.ShapeDtypeStruct((tall, wide), jnp.bfloat16)] * sets,
         scratch=[
             pltpu.VMEM((sets, count, width), row_sets[0].dtype),
             pltpu.VMEM((sets * span, width), maps.dtype),
@@ -285,11 +285,11 @@
     )
 
 
-def expand(low, slot_sets, maps, index, after=()):
+def expand(low_sets, slot_sets, maps, index, after=()):
     sets = len(slot_sets)
     rank, width = maps.shape[1:]
-    tall = low.shape[0]
-    half = low.size // sets // (2 * rank)
+    tall = low_sets[0].shape[0]
+    half = low_sets[0].size // (2 * rank)
     count = 2 * half
     span = index.shape[0] // sets * rank
     repeats = count // slot_sets[0].shape[0]
@@ -298,7 +298,8 @@
         (s, p * count // PARTS, count // PARTS) for s in range(1, sets) for p in range(PARTS)
     ]
 
-    def kernel(index_ref, low_ref, *refs):
+    def kernel(index_ref, *refs):
+        low_refs, refs = refs[:sets], refs[sets:]
         slot_refs, maps_ref, out_refs = refs[:sets], refs[sets], refs[sets + 1 : sets + 1 + len(outs)]
         stage, maps_buf, map_sems, out_sems = refs[sets + 1 + len(outs) :]
         map_copies = block_copies(index_ref, maps_ref, maps_buf, map_sems, sets, rank)
@@ -311,9 +312,9 @@
             for copy in map_copies[s]:
                 copy.start()
         for s in order:
-            lanes = [(s * half // tall + b) * 2 * rank for b in range(half // tall)]
+            lanes = [b * 2 * rank for b in range(half // tall)]
             mine = jnp.concatenate(
-                [low_ref[:, at + side : at + side + rank] for side in (0, rank) for at in lanes], axis=0
+                [low_refs[s][:, at + side : at + side + rank] for side in (0, rank) for at in lanes], axis=0
             )
             tiled = jnp.concatenate([mine] * (span // rank), axis=1)
             pick = lane_pick(slot_refs[s], repeats, (count, span), rank, 0)
@@ -332,8 +333,8 @@
             write.wait()
 
     return call(
-        kernel, [index, low, *slot_sets, maps], after, prefetch=1,
-        in_specs=[pl.BlockSpec(memory_space=pltpu.VMEM)] * (1 + sets) + [ANY],
+        kernel, [index, *low_sets, *slot_sets, maps], after, prefetch=1,
+        in_specs=[pl.BlockSpec(memory_space=pltpu.VMEM)] * (2 * sets) + [ANY],
         out_specs=[ANY] * len(outs),
         out_shape=[jax.ShapeDtypeStruct((some, width), jnp.bfloat16) for _, _, some in outs],
         scratch=[
@@ -412,9 +413,10 @@
 
     blocks = [[(order[t // 2][k] * 2 + side) for side in (1 - t % 2, t % 2) for k in range(nz)] for t in range(n)]
     starts = jnp.asarray(np.asarray(blocks, np.int32) * out_width)[place]
-    low_rows = 2 * (owners * count // 2) * adapter_down_maps.shape[1] // out_width
+    low_rows = count * adapter_down_maps.shape[1] // out_width
     even = [(p * count // PARTS, count // PARTS) for p in range(PARTS)]
-    uneven = [(0, (count + low_rows) // 2), ((count + low_rows) // 2, (count - low_rows) // 2)]
+    high_part = -(-(count + low_rows) // 32) * 16
+    uneven = [(0, high_part), (high_part, count - high_part)]
     away_part, own_all, from_y, sums, arrived = {}, {}, {}, {}, {}
 
     def split(k):
@@ -498,7 +500,9 @@
     named = [slots(some_ids, me) for some_ids in row_ids]
     names = jnp.concatenate([which for which, _ in named])
     slot_sets = [row_slot for _, row_slot in named]
-    low = then(low_rank, row_sets, slot_sets, adapter_down_maps, names, out_width)
+    low_sets = then(low_rank, row_sets, slot_sets, adapter_down_maps, names, out_width)
+    low_terms = [(low_sets[0], 0)] + [(pass_on(low_sets[s], -s), 0) for s in range(1, owners)]
+    low = then(total, [(low_rows, low_terms)])
     multiply([LOW_WITH], [], low, chunk=512)
     start_y(*LOW_WITH)
     multiply([(1, 0)], [0])
@@ -530,9 +534,10 @@
                     pieces.append((arrived[step, 0, LOW_WITH[1]], low_at))
         if (h, m, p) == LOW_SUM_AFTER:
             low_sum = then(total, [(low_rows, pieces)])
+            low_back = [low_sum] + [pass_on(low_sum, shift) for shift in range(1, owners)]
         if deltas is None and low_sum is not None and EXPAND_AFTER in arrived:
             last[0] += (arrived[1, 1, 0],) if nz > 2 else ()
-            deltas = then(expand, low_sum, slot_sets, adapter_up_maps, names)
+            deltas = then(expand, low_back, slot_sets, adapter_up_maps, names)
             back = [
                 [(*cut, pass_on(deltas[1 + (shift - 1) * PARTS + p], -shift), 0) for p, cut in enumerate(even)]
                 for shift in range(1, owners)
@@ -541,7 +546,8 @@
     early = [arrived_parts(h, nz - 2 - h) for h in range(1, nz - 2)]
     late = [arrived_parts(h, nz - 2 - h) for h in range(nz - 1) if not 1 <= h < nz - 2]
     most = add_up(span, [whole(own_all[nz - 1]), whole(deltas[0]), y_parts(nz - 1)] + early)
-    out = add_up(span, [whole(most)] + back + late)
+    most = add_up(span, [whole(most)] + back + late[:-1])
+    out = add_up(span, [whole(most)] + late[-1:])
     return out.reshape(steps, row_count, out_width)
 
 

time: 167 us -> 163 us (0.976)
  waiting for transfers between devices: 52.3 us -> 50.1 us
    ppermute x5, waiting for transfers between devices: 29.2 us -> 26 us  [swap_y(): return lax.ppermute(value, 'tensor', [(t, t ^ 1) for t in range(n)])]
    unnamed x24 -> x18, local copies, waits for them, and re-layouts: 6.33 us -> 4.88 us
    pallas_call x23 -> x25, Pallas kernels: 72.1 us -> 70.7 us  [call(): pl.pallas_call(body, grid_spec=pltpu.PrefetchScalarGridSpec(num_scalar_pr...]
  transfers between devices with their start and end apart: 20 -> 22, of which waited for: 9 -> 9; matrix products, arithmetic and copies ran while one was open for 1% -> 1% of each run, Pallas kernels for 41% -> 43%
where the time goes in v15:
time: 163 us; the launch traced here: 162 us
  Pallas kernels  70.7 us (43%)
  waiting for transfers between devices  50.1 us (31%)
  starting transfers between devices  33.2 us (20%)
  local copies, waits for them, and re-layouts  6.31 us (4%)
    pallas_call x25, Pallas kernels, call(): pl.pallas_call(body, grid_spec=pltpu.PrefetchScalarGridSpec(num_scalar_pr...  70.7 us
    ppermute x5, waiting for transfers between devices, swap_y(): return lax.ppermute(value, 'tensor', [(t, t ^ 1) for t in range(n)])  26 us
    ppermute x11, starting transfers between devices, hop(): return lax.ppermute(value, 'tensor', pairs)  24.5 us
    ppermute x11, waiting for transfers between devices, hop(): return lax.ppermute(value, 'tensor', pairs)  23 us
    ppermute x5, starting transfers between devices, swap_y(): return lax.ppermute(value, 'tensor', [(t, t ^ 1) for t in range(n)])  7.91 us
    unnamed x18, local copies, waits for them, and re-layouts  4.88 us
  transfers between devices with their start and end apart: 22, of which 9 were waited for; matrix products, arithmetic and copies ran while one was open for 1% of the time, Pallas kernels for 43%

profile of v15, /device:TPU:0, one launch (start us, length us, event | category | flops | bytes accessed | tf_op | source)
XLA Modules:
  0.0 161.9 jit_solution(1116273172654527921)
XLA Ops:
  0.5 1.2 dynamic-slice_bitcast_fusion.refs_0_
  1.7 4.3 %products.5.refs_6_ = bf16[416,1024]{1,0:T(8,128)(2,1)} custom-call(s32[8]{0:T(128)} %dynamic-slice_bitcast_fusion.refs_0_, bf16[768,1024]{1,0:T(8,128)(2,1)} %bitcast.7, bf16[1024,8192]{1,0:T(8,128)(2,1)} %refs_2_.9), custom_call_target="tpu_custom_call" | custom-call | flops 1 | bytes 1 | tf_op jit(solution)/shard_map/products/pallas_call | solution.py:26
  6.1 3.0 %collective-permute-start.4 = (bf16[416,1024]{1,0:T(8,128)(2,1)}, bf16[416,1024]{1,0:T(8,128)(2,1)S(1)}, u32[]{:S(2)}, u32[]{:S(2)}) collective-permute-start(bf16[416,1024]{1,0:T(8,128)(2,1)} %products.5.refs_6_), channel_id=1, source_target_pairs={{0,2},{2,0},{4,6},{6,4},{8,10},{10,8},{12,14},{14,12},{1,3},{3,1},... | collective-permute-start | bytes 2555912 | tf_op jit(solution)/shard_map/ppermute | solution.py:374
  10.3 1.4 copy-done
  11.7 1.2 copy-done.6
  12.9 6.6 %low_rank.1 = (bf16[48,1024]{1,0:T(8,128)(2,1)S(1)}, bf16[48,1024]{1,0:T(8,128)(2,1)S(1)}) custom-call(s32[32]{0:T(128)S(1)} %pad_add_fusion.refs_0_, bf16[768,1024]{1,0:T(8,128)(2,1)S(1)} %bitcast.11, bf16[768,1024]{1,0:T(8,128)(2,1)} %collective-permute-done.1.refs_2_, s32[192,1]{1,0:T(8,128)S(1)} %copy.13.refs_3_, s32[192,1]{1,0:T(8,128)S(1)} %copy.14.refs_4_, ...), custom_call_target="tpu_custom_call" | custom-call | flops 1 | bytes 1 | tf_op jit(solution)/shard_map/low_rank/pallas_call | solution.py:26
  19.6 1.2 collective-permute-done.2.refs_1_
  21.2 3.1 %products.6.refs_3_ = bf16[400,1024]{1,0:T(8,128)(2,1)S(1)} custom-call(s32[8]{0:T(128)S(1)} %copy-done.7, bf16[768,1024]{1,0:T(8,128)(2,1)S(1)} %bitcast.12, bf16[1024,8192]{1,0:T(8,128)(2,1)} %refs_2_.9, bf16[48,1024]{1,0:T(8,128)(2,1)S(1)} %total.16.refs_3_.refs_4_.refs_2_, bf16[48,1024]{1,0:T(8,128)(2,1)S(1)} %total.16.refs_3_.refs_4_.refs_2_), custom_call_target="tpu_custom_call" | custom-call | flops 1 | bytes 1 | tf_op jit(solution)/shard_map/products/pallas_call | solution.py:26
  24.5 6.3 %products.7 = (bf16[768,1024]{1,0:T(8,128)(2,1)}, bf16[768,1024]{1,0:T(8,128)(2,1)S(1)}) custom-call(s32[8]{0:T(128)S(1)} %copy-done.7, bf16[768,1024]{1,0:T(8,128)(2,1)} %bitcast.8, bf16[1024,8192]{1,0:T(8,128)(2,1)} %refs_2_.9, bf16[400,1024]{1,0:T(8,128)(2,1)S(1)} %products.6.refs_3_), custom_call_target="tpu_custom_call" | custom-call | flops 1 | bytes 1 | tf_op jit(solution)/shard_map/products/pallas_call | solution.py:26
  30.8 1.6 %total.17.refs_3_.refs_0_ = bf16[416,1024]{1,0:T(8,128)(2,1)S(1)} custom-call(bf16[768,1024]{1,0:T(8,128)(2,1)S(1)} %get-tuple-element.19.refs_0_, bf16[416,1024]{1,0:T(8,128)(2,1)S(1)} %collective-permute-done.4.refs_1_, bf16[768,1024]{1,0:T(8,128)(2,1)} %get-tuple-element.20.refs_2_), custom_call_target="tpu_custom_call" | custom-call | flops 1 | bytes 1 | tf_op jit(solution)/shard_map/total/pallas_call | solution.py:26
  32.5 4.0 %collective-permute-start.6 = (bf16[416,1024]{1,0:T(8,128)(2,1)S(1)}, bf16[416,1024]{1,0:T(8,128)(2,1)S(1)}, u32[]{:S(2)}, u32[]{:S(2)}) collective-permute-start(bf16[416,1024]{1,0:T(8,128)(2,1)S(1)} %total.17.refs_3_.refs_0_), channel_id=1, source_target_pairs={{0,4},{12,8},{2,6},{14,10},{1,5},{13,9},{3,7},{15,11},{16,20},{28,... | collective-permute-start | bytes 2555912 | tf_op jit(solution)/shard_map/ppermute | solution.py:381
  36.5 1.6 collective-permute-start.8
  38.1 6.4 %products.8 = (bf16[768,1024]{1,0:T(8,128)(2,1)S(1)}, bf16[768,1024]{1,0:T(8,128)(2,1)S(1)}) custom-call(s32[8]{0:T(128)S(1)} %copy-done.7, bf16[768,1024]{1,0:T(8,128)(2,1)} %bitcast.9, bf16[1024,8192]{1,0:T(8,128)(2,1)} %refs_2_.9, bf16[416,1024]{1,0:T(8,128)(2,1)S(1)} %total.17.refs_3_.refs_0_), custom_call_target="tpu_custom_call" | custom-call | flops 1 | bytes 1 | tf_op jit(solution)/shard_map/products/pallas_call | solution.py:26
  44.5 1.2 copy-done.4
  45.7 0.9 collective-permute-done.3.refs_1_.refs_3_
  46.6 1.5 total.18.refs_3_.refs_0_.refs_2_.refs_1_
  48.1 4.3 %collective-permute-start.5 = (bf16[400,1024]{1,0:T(8,128)(2,1)S(1)}, bf16[400,1024]{1,0:T(8,128)(2,1)S(1)}, u32[]{:S(2)}, u32[]{:S(2)}) collective-permute-start(bf16[400,1024]{1,0:T(8,128)(2,1)S(1)} %total.18.refs_3_.refs_0_.refs_2_.refs_1_), channel_id=1, source_target_pairs={{0,4},{12,8},{2,6},{14,10},{1,5},{13,9},{3,7},{15,11},{16,20},{28,... | collective-permute-start | bytes 2457608 | tf_op jit(solution)/shard_map/ppermute | solution.py:381
  52.4 10.0 %products.9 = (bf16[768,1024]{1,0:T(8,128)(2,1)S(1)}, bf16[768,1024]{1,0:T(8,128)(2,1)S(1)}, bf16[768,1024]{1,0:T(8,128)(2,1)}) custom-call(s32[8]{0:T(128)S(1)} %copy-done.7, bf16[768,1024]{1,0:T(8,128)(2,1)} %bitcast.10, bf16[1024,8192]{1,0:T(8,128)(2,1)} %refs_2_.9, bf16[400,1024]{1,0:T(8,128)(2,1)S(1)} %total.18.refs_3_.refs_0_.refs_2_.refs_1_), custom_call_target="tpu_custom_call" | custom-call | flops 1 | bytes 1 | tf_op jit(solution)/shard_map/products/pallas_call | solution.py:26
  62.5 2.0 %total.19.refs_4_ = bf16[416,1024]{1,0:T(8,128)(2,1)} custom-call(bf16[416,1024]{1,0:T(8,128)(2,1)S(1)} %total.17.refs_3_.refs_0_, bf16[416,1024]{1,0:T(8,128)(2,1)S(1)} %collective-permute-done.6.refs_1_, bf16[768,1024]{1,0:T(8,128)(2,1)S(1)} %get-tuple-element.23.refs_2_.refs_0_), custom_call_target="tpu_custom_call" | custom-call | flops 1 | bytes 1 | tf_op jit(solution)/shard_map/total/pallas_call | solution.py:26
  64.5 0.7 collective-permute-start.9
  65.2 1.6 collective-permute-start.11
  66.8 5.4 %collective-permute-done.5.refs_1_.refs_3_ = bf16[400,1024]{1,0:T(8,128)(2,1)S(1)} collective-permute-done((bf16[400,1024]{1,0:T(8,128)(2,1)S(1)}, bf16[400,1024]{1,0:T(8,128)(2,1)S(1)}, u32[]{:S(2)}, u32[]{:S(2)}) %collective-permute-start.5) | collective-permute-done | bytes 819232 | tf_op jit(solution)/shard_map/ppermute | solution.py:381
  72.2 1.5 total.20.refs_2_
  73.7 0.7 collective-permute-start.7
  74.4 6.0 %collective-permute-done.8.refs_1_ = bf16[768,1024]{1,0:T(8,128)(2,1)} collective-permute-done((bf16[768,1024]{1,0:T(8,128)(2,1)}, bf16[768,1024]{1,0:T(8,128)(2,1)}, u32[]{:S(2)}, u32[]{:S(2)}) %collective-permute-start.8) | collective-permute-done | bytes 1572896 | tf_op jit(solution)/shard_map/ppermute | solution.py:374
  80.4 1.8 %total.21.refs_2_.refs_0_ = bf16[384,1024]{1,0:T(8,128)(2,1)S(1)} custom-call(bf16[768,1024]{1,0:T(8,128)(2,1)S(1)} %get-tuple-element.24.refs_0_, bf16[768,1024]{1,0:T(8,128)(2,1)} %collective-permute-done.8.refs_1_, bf16[400,1024]{1,0:T(8,128)(2,1)S(1)} %total.20.refs_2_), custom_call_target="tpu_custom_call" | custom-call | flops 1 | bytes 1 | tf_op jit(solution)/shard_map/total/pallas_call | solution.py:26
  82.2 4.1 %collective-permute-start.12 = (bf16[384,1024]{1,0:T(8,128)(2,1)S(1)}, bf16[384,1024]{1,0:T(8,128)(2,1)S(1)}, u32[]{:S(2)}, u32[]{:S(2)}) collective-permute-start(bf16[384,1024]{1,0:T(8,128)(2,1)S(1)} %total.21.refs_2_.refs_0_), channel_id=1, source_target_pairs={{0,4},{12,8},{2,6},{14,10},{1,5},{13,9},{3,7},{15,11},{16,20},{28,... | collective-permute-start | bytes 2359304 | tf_op jit(solution)/shard_map/ppermute | solution.py:381
  86.3 1.8 %total.22.refs_2_.refs_0_.refs_1_ = bf16[384,1024]{1,0:T(8,128)(2,1)S(1)} custom-call(bf16[768,1024]{1,0:T(8,128)(2,1)S(1)} %get-tuple-element.24.refs_0_, bf16[768,1024]{1,0:T(8,128)(2,1)} %collective-permute-done.8.refs_1_, bf16[384,1024]{1,0:T(8,128)(2,1)S(1)} %total.21.refs_2_.refs_0_), custom_call_target="tpu_custom_call" | custom-call | flops 1 | bytes 1 | tf_op jit(solution)/shard_map/total/pallas_call | solution.py:26
  88.1 1.6 collective-permute-start.16
  89.7 1.3 collective-permute-start.14
  91.5 1.3 collective-permute-start.10
  92.8 11.4 %collective-permute-done.12.refs_1_ = bf16[384,1024]{1,0:T(8,128)(2,1)S(1)} collective-permute-done((bf16[384,1024]{1,0:T(8,128)(2,1)S(1)}, bf16[384,1024]{1,0:T(8,128)(2,1)S(1)}, u32[]{:S(2)}, u32[]{:S(2)}) %collective-permute-start.12) | collective-permute-done | bytes 786464 | tf_op jit(solution)/shard_map/ppermute | solution.py:381
  104.2 1.4 total.24.refs_2_
  106.3 7.8 %collective-permute-done.11.refs_1_ = bf16[768,1024]{1,0:T(8,128)(2,1)} collective-permute-done((bf16[768,1024]{1,0:T(8,128)(2,1)S(1)}, bf16[768,1024]{1,0:T(8,128)(2,1)}, u32[]{:S(2)}, u32[]{:S(2)}) %collective-permute-start.11) | collective-permute-done | bytes 1572896 | tf_op jit(solution)/shard_map/ppermute | solution.py:374
  114.1 1.7 %total.25.refs_4_.refs_0_.refs_2_ = bf16[768,1024]{1,0:T(8,128)(2,1)S(1)} custom-call(bf16[768,1024]{1,0:T(8,128)(2,1)S(1)} %get-tuple-element.25.refs_0_, bf16[768,1024]{1,0:T(8,128)(2,1)} %collective-permute-done.11.refs_1_, bf16[384,1024]{1,0:T(8,128)(2,1)S(1)} %total.24.refs_2_), custom_call_target="tpu_custom_call" | custom-call | flops 1 | bytes 1 | tf_op jit(solution)/shard_map/total/pallas_call | solution.py:26
  115.9 5.2 %collective-permute-start.19 = (bf16[768,1024]{1,0:T(8,128)(2,1)S(1)}, bf16[768,1024]{1,0:T(8,128)(2,1)}, u32[]{:S(2)}, u32[]{:S(2)}) collective-permute-start(bf16[768,1024]{1,0:T(8,128)(2,1)S(1)} %total.25.refs_4_.refs_0_.refs_2_), channel_id=1, source_target_pairs={{0,4},{12,8},{2,6},{14,10},{1,5},{13,9},{3,7},{15,11},{16,20},{28,... | collective-permute-start | bytes 4718600 | tf_op jit(solution)/shard_map/ppermute | solution.py:381
  121.1 0.7 total.26.refs_4_.refs_1_
  121.8 2.2 %total.27.refs_2_ = bf16[768,1024]{1,0:T(8,128)(2,1)S(1)} custom-call(bf16[768,1024]{1,0:T(8,128)(2,1)} %copy-done.2, bf16[416,1024]{1,0:T(8,128)(2,1)S(1)} %collective-permute-done.9.refs_3_.refs_1_, bf16[768,1024]{1,0:T(8,128)(2,1)} %copy-done.2, bf16[400,1024]{1,0:T(8,128)(2,1)S(1)} %collective-permute-done.7.refs_1_.refs_2_.refs_3_, ...), custom_call_target="tpu_custom_call" | custom-call | flops 1 | bytes 1 | tf_op jit(solution)/shard_map/total/pallas_call | solution.py:26
  124.1 1.3 collective-permute-start.21
  125.4 1.4 total.28.refs_6_
  126.8 0.9 collective-permute-start.17
  127.8 8.1 %expand.1 = (bf16[768,1024]{1,0:T(8,128)(2,1)}, bf16[384,1024]{1,0:T(8,128)(2,1)S(1)}, bf16[384,1024]{1,0:T(8,128)(2,1)S(1)}) custom-call(s32[32]{0:T(128)S(1)} %pad_add_fusion.refs_0_, bf16[48,1024]{1,0:T(8,128)(2,1)S(1)} %total.26.refs_4_.refs_1_, bf16[48,1024]{1,0:T(8,128)(2,1)S(1)} %collective-permute-done.13.refs_2_, s32[192,1]{1,0:T(8,128)S(1)} %copy.13.refs_3_, ...), custom_call_target="tpu_custom_call" | custom-call | flops 1 | bytes 1 | tf_op jit(solution)/shard_map/expand/pallas_call | solution.py:26
  136.0 11.2 %collective-permute-done.16.refs_2_.refs_6_ = bf16[768,1024]{1,0:T(8,128)(2,1)} collective-permute-done((bf16[768,1024]{1,0:T(8,128)(2,1)S(1)}, bf16[768,1024]{1,0:T(8,128)(2,1)}, u32[]{:S(2)}, u32[]{:S(2)}) %collective-permute-start.16) | collective-permute-done | bytes 1572896 | tf_op jit(solution)/shard_map/ppermute | solution.py:374
  147.2 3.0 %total.29.refs_0_.refs_3_.refs_6_ = bf16[768,1024]{1,0:T(8,128)(2,1)S(1)} custom-call(bf16[768,1024]{1,0:T(8,128)(2,1)} %get-tuple-element.22.refs_0_.refs_4_, bf16[768,1024]{1,0:T(8,128)(2,1)} %get-tuple-element.26.refs_1_.refs_5_.refs_8_, bf16[768,1024]{1,0:T(8,128)(2,1)} %collective-permute-done.16.refs_2_.refs_6_, ...), custom_call_target="tpu_custom_call" | custom-call | flops 1 | bytes 1 | tf_op jit(solution)/shard_map/total/pallas_call | solution.py:26
  150.2 1.1 copy-done.3
  151.9 2.7 %total.30.refs_0_.refs_2_ = bf16[768,1024]{1,0:T(8,128)(2,1)S(1)} custom-call(bf16[768,1024]{1,0:T(8,128)(2,1)} %copy-done.3, bf16[384,1024]{1,0:T(8,128)(2,1)S(1)} %collective-permute-done.18.refs_1_, bf16[768,1024]{1,0:T(8,128)(2,1)} %collective-permute-done.19.refs_2_.refs_5_, bf16[768,1024]{1,0:T(8,128)(2,1)} %copy-done.3, ...), custom_call_target="tpu_custom_call" | custom-call | flops 1 | bytes 1 | tf_op jit(solution)/shard_map/total/pallas_call | solution.py:26
  154.6 5.5 %collective-permute-done.21.refs_1_ = bf16[768,1024]{1,0:T(8,128)(2,1)S(1)} collective-permute-done((bf16[768,1024]{1,0:T(8,128)(2,1)S(1)}, bf16[768,1024]{1,0:T(8,128)(2,1)S(1)}, u32[]{:S(2)}, u32[]{:S(2)}) %collective-permute-start.21) | collective-permute-done | bytes 1572896 | tf_op jit(solution)/shard_map/ppermute | solution.py:381
  160.2 1.6 total.31
  (56 shorter events, 4.3 us)
Async XLA Ops:
  0.0 9.6 %collective-permute-start = (s32[192]{0:T(256)}, s32[192]{0:T(256)S(1)}, u32[]{:S(2)}, u32[]{:S(2)}) collective-permute-start(s32[192]{0:T(256)} %param.7), channel_id=1, source_target_pairs={{0,1},{1,0},{2,3},{3,2},{4,5},{5,4},{6,7},{7,6},{8,9},{9,8},{10,11... | collective-permute-start | bytes 2312 | tf_op jit(solution)/shard_map/ppermute | solution.py:387
  0.5 9.8 %collective-permute-start.1 = (bf16[768,1024]{1,0:T(8,128)(2,1)}, bf16[768,1024]{1,0:T(8,128)(2,1)}, u32[]{:S(2)}, u32[]{:S(2)}) collective-permute-start(bf16[768,1024]{1,0:T(8,128)(2,1)} %bitcast.6), channel_id=1, source_target_pairs={{0,1},{1,0},{2,3},{3,2},{4,5},{5,4},{6,7},{7,6},{8,9},{9,8},{10,11... | collective-permute-start | bytes 4718600 | tf_op jit(solution)/shard_map/ppermute | solution.py:387
  1.7 7.4 %copy-start.8 = (s32[192]{0:T(256)S(1)}, s32[192]{0:T(256)}, u32[]{:S(2)}) copy-start(s32[192]{0:T(256)} %param.7) | copy-start | bytes 2308
  6.1 24.8 %collective-permute-start.4 = (bf16[416,1024]{1,0:T(8,128)(2,1)}, bf16[416,1024]{1,0:T(8,128)(2,1)S(1)}, u32[]{:S(2)}, u32[]{:S(2)}) collective-permute-start(bf16[416,1024]{1,0:T(8,128)(2,1)} %products.5.refs_6_), channel_id=1, source_target_pairs={{0,2},{2,0},{4,6},{6,4},{8,10},{10,8},{12,14},{14,12},{1,3},{3,1},... | collective-permute-start | bytes 2555912 | tf_op jit(solution)/shard_map/ppermute | solution.py:374
  10.3 1.4 copy-start
  11.7 1.2 copy-start.6
  12.9 8.4 %copy-start.1 = (bf16[4,192,1024]{2,1,0:T(8,128)(2,1)S(1)}, bf16[4,192,1024]{2,1,0:T(8,128)(2,1)}, u32[]{:S(2)}) copy-start(bf16[4,192,1024]{2,1,0:T(8,128)(2,1)} %param.6) | copy-start | bytes 4718596
  12.9 8.4 %copy-start.7 = (s32[8]{0:T(128)S(1)}, s32[8]{0:T(128)}, u32[]{:S(2)}) copy-start(s32[8]{0:T(128)} %dynamic-slice_bitcast_fusion.refs_0_) | copy-start | bytes 100
  19.4 1.4 collective-permute-start.2
  24.4 22.2 %collective-permute-start.3 = (bf16[400,1024]{1,0:T(8,128)(2,1)S(1)}, bf16[400,1024]{1,0:T(8,128)(2,1)S(1)}, u32[]{:S(2)}, u32[]{:S(2)}) collective-permute-start(bf16[400,1024]{1,0:T(8,128)(2,1)S(1)} %products.6.refs_3_), channel_id=1, source_target_pairs={{0,2},{2,0},{4,6},{6,4},{8,10},{10,8},{12,14},{14,12},{1,3},{3,1},... | collective-permute-start | bytes 2457608 | tf_op jit(solution)/shard_map/ppermute | solution.py:374
  32.5 30.0 %collective-permute-start.6 = (bf16[416,1024]{1,0:T(8,128)(2,1)S(1)}, bf16[416,1024]{1,0:T(8,128)(2,1)S(1)}, u32[]{:S(2)}, u32[]{:S(2)}) collective-permute-start(bf16[416,1024]{1,0:T(8,128)(2,1)S(1)} %total.17.refs_3_.refs_0_), channel_id=1, source_target_pairs={{0,4},{12,8},{2,6},{14,10},{1,5},{13,9},{3,7},{15,11},{16,20},{28,... | collective-permute-start | bytes 2555912 | tf_op jit(solution)/shard_map/ppermute | solution.py:381
  36.5 44.0 %collective-permute-start.8 = (bf16[768,1024]{1,0:T(8,128)(2,1)}, bf16[768,1024]{1,0:T(8,128)(2,1)}, u32[]{:S(2)}, u32[]{:S(2)}) collective-permute-start(bf16[768,1024]{1,0:T(8,128)(2,1)} %get-tuple-element.20.refs_2_), channel_id=1, source_target_pairs={{0,2},{2,0},{4,6},{6,4},{8,10},{10,8},{12,14},{14,12},{1,3},{3,1},... | collective-permute-start | bytes 4718600 | tf_op jit(solution)/shard_map/ppermute | solution.py:374
  44.5 1.2 copy-start.4
  48.1 24.0 %collective-permute-start.5 = (bf16[400,1024]{1,0:T(8,128)(2,1)S(1)}, bf16[400,1024]{1,0:T(8,128)(2,1)S(1)}, u32[]{:S(2)}, u32[]{:S(2)}) collective-permute-start(bf16[400,1024]{1,0:T(8,128)(2,1)S(1)} %total.18.refs_3_.refs_0_.refs_2_.refs_1_), channel_id=1, source_target_pairs={{0,4},{12,8},{2,6},{14,10},{1,5},{13,9},{3,7},{15,11},{16,20},{28,... | collective-permute-start | bytes 2457608 | tf_op jit(solution)/shard_map/ppermute | solution.py:381
  62.5 2.8 %copy-start.5 = (bf16[768,1024]{1,0:T(8,128)(2,1)S(1)}, bf16[768,1024]{1,0:T(8,128)(2,1)}, u32[]{:S(2)}) copy-start(bf16[768,1024]{1,0:T(8,128)(2,1)} %copy-done.4) | copy-start | bytes 4718596
  64.5 25.2 %collective-permute-start.9 = (bf16[416,1024]{1,0:T(8,128)(2,1)}, bf16[416,1024]{1,0:T(8,128)(2,1)S(1)}, u32[]{:S(2)}, u32[]{:S(2)}) collective-permute-start(bf16[416,1024]{1,0:T(8,128)(2,1)} %total.19.refs_4_), channel_id=1, source_target_pairs={{4,8},{8,4},{6,10},{10,6},{5,9},{9,5},{7,11},{11,7},{20,24},{24,20... | collective-permute-start | bytes 2555912 | tf_op jit(solution)/shard_map/ppermute | solution.py:381
  65.2 48.9 %collective-permute-start.11 = (bf16[768,1024]{1,0:T(8,128)(2,1)S(1)}, bf16[768,1024]{1,0:T(8,128)(2,1)}, u32[]{:S(2)}, u32[]{:S(2)}) collective-permute-start(bf16[768,1024]{1,0:T(8,128)(2,1)S(1)} %hold.2), channel_id=1, source_target_pairs={{0,2},{2,0},{4,6},{6,4},{8,10},{10,8},{12,14},{14,12},{1,3},{3,1},... | collective-permute-start | bytes 4718600 | tf_op jit(solution)/shard_map/ppermute | solution.py:374
  73.7 17.3 %collective-permute-start.7 = (bf16[400,1024]{1,0:T(8,128)(2,1)S(1)}, bf16[400,1024]{1,0:T(8,128)(2,1)S(1)}, u32[]{:S(2)}, u32[]{:S(2)}) collective-permute-start(bf16[400,1024]{1,0:T(8,128)(2,1)S(1)} %total.20.refs_2_), channel_id=1, source_target_pairs={{4,8},{8,4},{6,10},{10,6},{5,9},{9,5},{7,11},{11,7},{20,24},{24,20... | collective-permute-start | bytes 2457608 | tf_op jit(solution)/shard_map/ppermute | solution.py:381
  82.2 22.0 %collective-permute-start.12 = (bf16[384,1024]{1,0:T(8,128)(2,1)S(1)}, bf16[384,1024]{1,0:T(8,128)(2,1)S(1)}, u32[]{:S(2)}, u32[]{:S(2)}) collective-permute-start(bf16[384,1024]{1,0:T(8,128)(2,1)S(1)} %total.21.refs_2_.refs_0_), channel_id=1, source_target_pairs={{0,4},{12,8},{2,6},{14,10},{1,5},{13,9},{3,7},{15,11},{16,20},{28,... | collective-permute-start | bytes 2359304 | tf_op jit(solution)/shard_map/ppermute | solution.py:381
  88.1 59.1 %collective-permute-start.16 = (bf16[768,1024]{1,0:T(8,128)(2,1)S(1)}, bf16[768,1024]{1,0:T(8,128)(2,1)}, u32[]{:S(2)}, u32[]{:S(2)}) collective-permute-start(bf16[768,1024]{1,0:T(8,128)(2,1)S(1)} %hold.3), channel_id=1, source_target_pairs={{0,2},{2,0},{4,6},{6,4},{8,10},{10,8},{12,14},{14,12},{1,3},{3,1},... | collective-permute-start | bytes 4718600 | tf_op jit(solution)/shard_map/ppermute | solution.py:374
  89.7 32.1 %collective-permute-start.14 = (bf16[384,1024]{1,0:T(8,128)(2,1)S(1)}, bf16[384,1024]{1,0:T(8,128)(2,1)S(1)}, u32[]{:S(2)}, u32[]{:S(2)}) collective-permute-start(bf16[384,1024]{1,0:T(8,128)(2,1)S(1)} %total.22.refs_2_.refs_0_.refs_1_), channel_id=1, source_target_pairs={{0,4},{12,8},{2,6},{14,10},{1,5},{13,9},{3,7},{15,11},{16,20},{28,... | collective-permute-start | bytes 2359304 | tf_op jit(solution)/shard_map/ppermute | solution.py:381
  91.5 29.6 %collective-permute-start.10 = (bf16[48,1024]{1,0:T(8,128)(2,1)S(1)}, bf16[48,1024]{1,0:T(8,128)(2,1)S(1)}, u32[]{:S(2)}, u32[]{:S(2)}) collective-permute-start(bf16[48,1024]{1,0:T(8,128)(2,1)S(1)} %total.23.refs_2_), channel_id=1, source_target_pairs={{8,12},{4,0},{10,14},{6,2},{9,13},{5,1},{11,15},{7,3},{24,28},{20,... | collective-permute-start | bytes 294920 | tf_op jit(solution)/shard_map/ppermute | solution.py:381
  105.6 22.2 %collective-permute-start.15 = (bf16[384,1024]{1,0:T(8,128)(2,1)S(1)}, bf16[384,1024]{1,0:T(8,128)(2,1)S(1)}, u32[]{:S(2)}, u32[]{:S(2)}) collective-permute-start(bf16[384,1024]{1,0:T(8,128)(2,1)S(1)} %total.24.refs_2_), channel_id=1, source_target_pairs={{4,8},{8,4},{6,10},{10,6},{5,9},{9,5},{7,11},{11,7},{20,24},{24,20... | collective-permute-start | bytes 2359304 | tf_op jit(solution)/shard_map/ppermute | solution.py:381
  115.9 5.2 %copy-start.2 = (bf16[768,1024]{1,0:T(8,128)(2,1)}, bf16[768,1024]{1,0:T(8,128)(2,1)S(1)}, u32[]{:S(2)}) copy-start(bf16[768,1024]{1,0:T(8,128)(2,1)S(1)} %total.25.refs_4_.refs_0_.refs_2_) | copy-start | bytes 4718596
  115.9 36.1 %collective-permute-start.19 = (bf16[768,1024]{1,0:T(8,128)(2,1)S(1)}, bf16[768,1024]{1,0:T(8,128)(2,1)}, u32[]{:S(2)}, u32[]{:S(2)}) collective-permute-start(bf16[768,1024]{1,0:T(8,128)(2,1)S(1)} %total.25.refs_4_.refs_0_.refs_2_), channel_id=1, source_target_pairs={{0,4},{12,8},{2,6},{14,10},{1,5},{13,9},{3,7},{15,11},{16,20},{28,... | collective-permute-start | bytes 4718600 | tf_op jit(solution)/shard_map/ppermute | solution.py:381
  124.1 36.1 %collective-permute-start.21 = (bf16[768,1024]{1,0:T(8,128)(2,1)S(1)}, bf16[768,1024]{1,0:T(8,128)(2,1)S(1)}, u32[]{:S(2)}, u32[]{:S(2)}) collective-permute-start(bf16[768,1024]{1,0:T(8,128)(2,1)S(1)} %total.27.refs_2_), channel_id=1, source_target_pairs={{8,12},{4,0},{10,14},{6,2},{9,13},{5,1},{11,15},{7,3},{24,28},{20,... | collective-permute-start | bytes 4718600 | tf_op jit(solution)/shard_map/ppermute | solution.py:381
  125.4 1.5 collective-permute-start.13
  126.8 20.4 %collective-permute-start.17 = (bf16[384,1024]{1,0:T(8,128)(2,1)S(1)}, bf16[384,1024]{1,0:T(8,128)(2,1)S(1)}, u32[]{:S(2)}, u32[]{:S(2)}) collective-permute-start(bf16[384,1024]{1,0:T(8,128)(2,1)S(1)} %total.28.refs_6_), channel_id=1, source_target_pairs={{4,8},{8,4},{6,10},{10,6},{5,9},{9,5},{7,11},{11,7},{20,24},{24,20... | collective-permute-start | bytes 2359304 | tf_op jit(solution)/shard_map/ppermute | solution.py:381
  135.9 16.1 %collective-permute-start.18 = (bf16[384,1024]{1,0:T(8,128)(2,1)S(1)}, bf16[384,1024]{1,0:T(8,128)(2,1)S(1)}, u32[]{:S(2)}, u32[]{:S(2)}) collective-permute-start(bf16[384,1024]{1,0:T(8,128)(2,1)S(1)} %get-tuple-element.27), channel_id=1, source_target_pairs={{0,1},{1,0},{2,3},{3,2},{4,5},{5,4},{6,7},{7,6},{8,9},{9,8},{10,11... | collective-permute-start | bytes 2359304 | tf_op jit(solution)/shard_map/ppermute | solution.py:387
  147.2 4.8 %collective-permute-start.20 = (bf16[384,1024]{1,0:T(8,128)(2,1)S(1)}, bf16[384,1024]{1,0:T(8,128)(2,1)S(1)}, u32[]{:S(2)}, u32[]{:S(2)}) collective-permute-start(bf16[384,1024]{1,0:T(8,128)(2,1)S(1)} %get-tuple-element.28), channel_id=1, source_target_pairs={{0,1},{1,0},{2,3},{3,2},{4,5},{5,4},{6,7},{7,6},{8,9},{9,8},{10,11... | collective-permute-start | bytes 2359304 | tf_op jit(solution)/shard_map/ppermute | solution.py:387
  150.2 1.1 copy-start.3

commit v16 on v15

--- a/solution.py
+++ b/solution.py
@@ -11,7 +11,7 @@
 CHUNK = 512
 PARTS = 2
 LOW_WITH = (0, PARTS - 1)
-LOW_SUM_AFTER = (0, 2, 0)
+LOW_SUM_AFTER = (2, 0, 0)
 EXPAND_AFTER = (1, 1, 1)
 VMEM = 50 * 2**20
 ANY = pl.BlockSpec(memory_space=pl.ANY)
@@ -139,7 +139,7 @@
     )
 
 
-def total(runs, dtype=jnp.bfloat16, into=None, after=()):
+def total(runs, dtype=jnp.bfloat16, into=None, only=None, after=()):
     width = runs[0][1][0][0].shape[1]
     height = sum(some for some, _ in runs)
     rows_in_all, first, so_far = into or (height, 0, None)
@@ -156,7 +156,15 @@
     most_terms = max(len(terms) for _, terms in runs)
     of_run = np.cumsum([0] + [len(terms) for _, terms in runs])
 
+    flags = [] if only is None else [only[0]]
+
     def kernel(*refs):
+        if only is None:
+            add(*refs)
+        else:
+            pl.when(refs[0][only[1]] != 0)(lambda: add(*refs[1:]))
+
+    def add(*refs):
         term_refs, out_ref = refs[: len(operands)], refs[len(operands) + len(before)]
         refs = refs[len(operands) + len(before) + 1 :]
         bufs, (stage, in_sems, out_sems) = refs[: len(operands)], refs[len(operands) :]
@@ -193,7 +201,7 @@
             write.wait()
 
     return call(
-        kernel, operands + before, after,
+        kernel, flags + operands + before, after, prefetch=len(flags),
         in_specs=[ANY] * (len(operands) + len(before)),
         out_specs=ANY,
         out_shape=jax.ShapeDtypeStruct((rows_in_all, width), dtype),
@@ -203,7 +211,7 @@
             pltpu.SemaphoreType.DMA((most_terms, len(tiles))),
             pltpu.SemaphoreType.DMA((len(tiles),)),
         ],
-        alias={len(operands): 0} if before else None,
+        alias={len(flags) + len(operands): 0} if before else None,
         name="total",
     )
 
@@ -412,7 +420,9 @@
         return names, row_slot[:, None]
 
     blocks = [[(order[t // 2][k] * 2 + side) for side in (1 - t % 2, t % 2) for k in range(nz)] for t in range(n)]
-    starts = jnp.asarray(np.asarray(blocks, np.int32) * out_width)[place]
+    sends = [[int(t // 2 in (h, nz - 1 - h)) for h in range(nz - 1)] for t in range(n)]
+    table = np.concatenate([np.asarray(blocks, np.int32) * out_width, np.asarray(sends, np.int32)], axis=1)
+    starts = jnp.asarray(table)[place]
     low_rows = count * adapter_down_maps.shape[1] // out_width
     even = [(p * count // PARTS, count // PARTS) for p in range(PARTS)]
     high_part = -(-(count + low_rows) // 32) * 16
@@ -422,7 +432,7 @@
     def split(k):
         return uneven if k == 0 else [(0, count)]
 
-    def add_up(span, terms, extra=(), dtype=jnp.bfloat16, into=None):
+    def add_up(span, terms, extra=(), dtype=jnp.bfloat16, only=None):
         low_row, high_row = span[0], span[0] + span[1]
         cuts = {low_row, high_row}
         for term in terms:
@@ -435,7 +445,7 @@
                 (array, row + begin - at) for term in terms for at, some, array, row in term if at <= begin < at + some
             ]
             runs.append((end - begin, here))
-        return then(total, runs + list(extra), dtype, into)
+        return then(total, runs + list(extra), dtype, None, only)
 
     def whole(array):
         return [(0, count, array, 0)]
@@ -476,7 +486,7 @@
             value = sums[k, p] = add_up(span, [whole(own_all[k]), y_parts(k)], extra)
         else:
             extra = [(low_rows, [(sums[k, p], span[1]), (arrived[h - 1, m, p], span[1])])] if low_too else []
-            value = add_up(span, [sum_parts(k), arrived_parts(h - 1, m)], extra)
+            value = add_up(span, [sum_parts(k), arrived_parts(h - 1, m)], extra, only=(starts, 2 * nz + h))
         arrived[h, m, p] = hop(value, h)
 
     def line_order():
@@ -511,7 +521,7 @@
     for h, m, p in line_order():
         k = slot_of(h, m)
         if (h, m, p) == (2, 0, 0) and nz == 4:
-            last[0] += (arrived[0, 1, 1],)
+            last[0] += (arrived[0, 1, 1], pieces[-1][0])
         line(h, m, p)
         if h == 0:
             if k == 0 and p == 0:
@@ -528,7 +538,7 @@
             last[0] += (arrived[1, 0, 0],) if nz > 2 else ()
             for step in range(nz - 1):
                 if step >= 2:
-                    prefix = then(total, [(low_rows, [pieces[0], pieces[-1]])])
+                    prefix = then(total, [(low_rows, [pieces[0], pieces[-1]])], only=(starts, 2 * nz + step))
                     pieces.append((hop(prefix, step), 0))
                 else:
                     pieces.append((arrived[step, 0, LOW_WITH[1]], low_at))

time: 163 us -> 160 us (0.982)
  Pallas kernels: 70.7 us -> 65.5 us
  local copies, waits for them, and re-layouts: 6.31 us -> 11 us
    pallas_call x25, Pallas kernels: 70.7 us -> 65.5 us  [call(): pl.pallas_call(body, grid_spec=pltpu.PrefetchScalarGridSpec(num_scalar_pr...]
    unnamed x18 -> x30, local copies, waits for them, and re-layouts: 4.88 us -> 9.55 us
    ppermute x11, waiting for transfers between devices: 23 us -> 21 us  [hop(): return lax.ppermute(value, 'tensor', pairs)]
  transfers between devices with their start and end apart: 22 -> 22, of which waited for: 9 -> 9; matrix products, arithmetic and copies ran while one was open for 1% -> 1% of each run, Pallas kernels for 43% -> 40%
where the time goes in v16:
time: 160 us
  Pallas kernels  65.5 us (41%)
  waiting for transfers between devices  49.9 us (31%)
  starting transfers between devices  31.9 us (20%)
  local copies, waits for them, and re-layouts  11 us (7%)
    pallas_call x25, Pallas kernels, call(): pl.pallas_call(body, grid_spec=pltpu.PrefetchScalarGridSpec(num_scalar_pr...  65.5 us
    ppermute x5, waiting for transfers between devices, swap_y(): return lax.ppermute(value, 'tensor', [(t, t ^ 1) for t in range(n)])  26.9 us
    ppermute x11, starting transfers between devices, hop(): return lax.ppermute(value, 'tensor', pairs)  23.3 us
    ppermute x11, waiting for transfers between devices, hop(): return lax.ppermute(value, 'tensor', pairs)  21 us
    unnamed x30, local copies, waits for them, and re-layouts  9.55 us
    ppermute x5, starting transfers between devices, swap_y(): return lax.ppermute(value, 'tensor', [(t, t ^ 1) for t in range(n)])  7.82 us
  transfers between devices with their start and end apart: 22, of which 9 were waited for; matrix products, arithmetic and copies ran while one was open for 1% of the time, Pallas kernels for 40%

profile of v16, /device:TPU:0, one launch (start us, length us, event | category | flops | bytes accessed | tf_op | source)
XLA Modules:
  0.0 159.8 jit_solution(5351674348582155791)
XLA Ops:
  0.5 1.2 dynamic-slice_bitcast_fusion.refs_0_
  1.7 4.3 %products.5.refs_6_ = bf16[416,1024]{1,0:T(8,128)(2,1)} custom-call(s32[11]{0:T(128)} %dynamic-slice_bitcast_fusion.refs_0_, bf16[768,1024]{1,0:T(8,128)(2,1)} %bitcast.7, bf16[1024,8192]{1,0:T(8,128)(2,1)} %refs_2_.9), custom_call_target="tpu_custom_call" | custom-call | flops 1 | bytes 1 | tf_op jit(solution)/shard_map/products/pallas_call | solution.py:26
  6.1 3.0 %collective-permute-start.4 = (bf16[416,1024]{1,0:T(8,128)(2,1)}, bf16[416,1024]{1,0:T(8,128)(2,1)S(1)}, u32[]{:S(2)}, u32[]{:S(2)}) collective-permute-start(bf16[416,1024]{1,0:T(8,128)(2,1)} %products.5.refs_6_), channel_id=1, source_target_pairs={{0,2},{2,0},{4,6},{6,4},{8,10},{10,8},{12,14},{14,12},{1,3},{3,1},... | collective-permute-start | bytes 2555912 | tf_op jit(solution)/shard_map/ppermute | solution.py:382
  10.3 1.4 copy-done
  11.7 1.2 copy-done.8
  12.9 6.8 %low_rank.1 = (bf16[48,1024]{1,0:T(8,128)(2,1)S(1)}, bf16[48,1024]{1,0:T(8,128)(2,1)S(1)}) custom-call(s32[32]{0:T(128)S(1)} %pad_add_fusion.refs_0_, bf16[768,1024]{1,0:T(8,128)(2,1)S(1)} %bitcast.11, bf16[768,1024]{1,0:T(8,128)(2,1)} %collective-permute-done.1.refs_2_, s32[192,1]{1,0:T(8,128)S(1)} %copy.13.refs_3_, s32[192,1]{1,0:T(8,128)S(1)} %copy.14.refs_4_, ...), custom_call_target="tpu_custom_call" | custom-call | flops 1 | bytes 1 | tf_op jit(solution)/shard_map/low_rank/pallas_call | solution.py:26
  19.7 1.3 collective-permute-done.2.refs_1_
  21.4 3.1 %products.6.refs_3_ = bf16[400,1024]{1,0:T(8,128)(2,1)S(1)} custom-call(s32[11]{0:T(128)S(1)} %copy-done.11, bf16[768,1024]{1,0:T(8,128)(2,1)S(1)} %bitcast.12, bf16[1024,8192]{1,0:T(8,128)(2,1)} %refs_2_.9, bf16[48,1024]{1,0:T(8,128)(2,1)S(1)} %total.16.refs_3_.refs_4_.refs_2_, bf16[48,1024]{1,0:T(8,128)(2,1)S(1)} %total.16.refs_3_.refs_4_.refs_2_), custom_call_target="tpu_custom_call" | custom-call | flops 1 | bytes 1 | tf_op jit(solution)/shard_map/products/pallas_call | solution.py:26
  24.7 6.4 %products.7 = (bf16[768,1024]{1,0:T(8,128)(2,1)S(1)}, bf16[768,1024]{1,0:T(8,128)(2,1)S(1)}) custom-call(s32[11]{0:T(128)S(1)} %copy-done.11, bf16[768,1024]{1,0:T(8,128)(2,1)} %bitcast.8, bf16[1024,8192]{1,0:T(8,128)(2,1)} %refs_2_.9, bf16[400,1024]{1,0:T(8,128)(2,1)S(1)} %products.6.refs_3_), custom_call_target="tpu_custom_call" | custom-call | flops 1 | bytes 1 | tf_op jit(solution)/shard_map/products/pallas_call | solution.py:26
  31.1 1.1 copy-done.9
  32.3 1.6 %total.17.refs_3_.refs_1_ = bf16[416,1024]{1,0:T(8,128)(2,1)S(1)} custom-call(bf16[768,1024]{1,0:T(8,128)(2,1)S(1)} %get-tuple-element.19.refs_0_, bf16[416,1024]{1,0:T(8,128)(2,1)S(1)} %collective-permute-done.4.refs_1_, bf16[768,1024]{1,0:T(8,128)(2,1)} %copy-done.9), custom_call_target="tpu_custom_call" | custom-call | flops 1 | bytes 1 | tf_op jit(solution)/shard_map/total/pallas_call | solution.py:26
  33.9 4.0 %collective-permute-start.6 = (bf16[416,1024]{1,0:T(8,128)(2,1)S(1)}, bf16[416,1024]{1,0:T(8,128)(2,1)S(1)}, u32[]{:S(2)}, u32[]{:S(2)}) collective-permute-start(bf16[416,1024]{1,0:T(8,128)(2,1)S(1)} %total.17.refs_3_.refs_1_), channel_id=1, source_target_pairs={{0,4},{12,8},{2,6},{14,10},{1,5},{13,9},{3,7},{15,11},{16,20},{28,... | collective-permute-start | bytes 2555912 | tf_op jit(solution)/shard_map/ppermute | solution.py:389
  37.9 1.6 collective-permute-start.8
  39.5 6.4 %products.8 = (bf16[768,1024]{1,0:T(8,128)(2,1)S(1)}, bf16[768,1024]{1,0:T(8,128)(2,1)S(1)}) custom-call(s32[11]{0:T(128)S(1)} %copy-done.11, bf16[768,1024]{1,0:T(8,128)(2,1)} %bitcast.9, bf16[1024,8192]{1,0:T(8,128)(2,1)} %refs_2_.9, bf16[416,1024]{1,0:T(8,128)(2,1)S(1)} %total.17.refs_3_.refs_1_), custom_call_target="tpu_custom_call" | custom-call | flops 1 | bytes 1 | tf_op jit(solution)/shard_map/products/pallas_call | solution.py:26
  46.0 1.1 copy-done.6
  47.1 1.5 total.18.refs_3_.refs_1_.refs_0_
  48.6 3.8 %collective-permute-start.5 = (bf16[400,1024]{1,0:T(8,128)(2,1)S(1)}, bf16[400,1024]{1,0:T(8,128)(2,1)S(1)}, u32[]{:S(2)}, u32[]{:S(2)}) collective-permute-start(bf16[400,1024]{1,0:T(8,128)(2,1)S(1)} %total.18.refs_3_.refs_1_.refs_0_), channel_id=1, source_target_pairs={{0,4},{12,8},{2,6},{14,10},{1,5},{13,9},{3,7},{15,11},{16,20},{28,... | collective-permute-start | bytes 2457608 | tf_op jit(solution)/shard_map/ppermute | solution.py:389
  52.4 10.1 %products.9 = (bf16[768,1024]{1,0:T(8,128)(2,1)S(1)}, bf16[768,1024]{1,0:T(8,128)(2,1)S(1)}, bf16[768,1024]{1,0:T(8,128)(2,1)}) custom-call(s32[11]{0:T(128)S(1)} %copy-done.11, bf16[768,1024]{1,0:T(8,128)(2,1)} %bitcast.10, bf16[1024,8192]{1,0:T(8,128)(2,1)} %refs_2_.9, bf16[400,1024]{1,0:T(8,128)(2,1)S(1)} %total.18.refs_3_.refs_1_.refs_0_), custom_call_target="tpu_custom_call" | custom-call | flops 1 | bytes 1 | tf_op jit(solution)/shard_map/products/pallas_call | solution.py:26
  62.5 1.1 copy-done.4
  64.3 0.7 collective-permute-start.9
  65.1 1.5 collective-permute-start.11
  66.6 7.1 %collective-permute-done.5.refs_2_.refs_4_.refs_1_ = bf16[400,1024]{1,0:T(8,128)(2,1)S(1)} collective-permute-done((bf16[400,1024]{1,0:T(8,128)(2,1)S(1)}, bf16[400,1024]{1,0:T(8,128)(2,1)S(1)}, u32[]{:S(2)}, u32[]{:S(2)}) %collective-permute-start.5) | collective-permute-done | bytes 819232 | tf_op jit(solution)/shard_map/ppermute | solution.py:389
  74.3 0.7 collective-permute-start.7
  75.0 5.4 %collective-permute-done.8.refs_1_ = bf16[768,1024]{1,0:T(8,128)(2,1)} collective-permute-done((bf16[768,1024]{1,0:T(8,128)(2,1)S(1)}, bf16[768,1024]{1,0:T(8,128)(2,1)}, u32[]{:S(2)}, u32[]{:S(2)}) %collective-permute-start.8) | collective-permute-done | bytes 1572896 | tf_op jit(solution)/shard_map/ppermute | solution.py:382
  80.4 1.8 %total.21.refs_2_.refs_1_ = bf16[384,1024]{1,0:T(8,128)(2,1)S(1)} custom-call(bf16[768,1024]{1,0:T(8,128)(2,1)S(1)} %get-tuple-element.24.refs_0_, bf16[768,1024]{1,0:T(8,128)(2,1)} %collective-permute-done.8.refs_1_, bf16[400,1024]{1,0:T(8,128)(2,1)S(1)} %total.20.refs_2_), custom_call_target="tpu_custom_call" | custom-call | flops 1 | bytes 1 | tf_op jit(solution)/shard_map/total/pallas_call | solution.py:26
  82.2 4.2 %collective-permute-start.12 = (bf16[384,1024]{1,0:T(8,128)(2,1)S(1)}, bf16[384,1024]{1,0:T(8,128)(2,1)S(1)}, u32[]{:S(2)}, u32[]{:S(2)}) collective-permute-start(bf16[384,1024]{1,0:T(8,128)(2,1)S(1)} %total.21.refs_2_.refs_1_), channel_id=1, source_target_pairs={{0,4},{12,8},{2,6},{14,10},{1,5},{13,9},{3,7},{15,11},{16,20},{28,... | collective-permute-start | bytes 2359304 | tf_op jit(solution)/shard_map/ppermute | solution.py:389
  86.4 1.8 %total.22.refs_3_.refs_1_ = bf16[384,1024]{1,0:T(8,128)(2,1)S(1)} custom-call(bf16[768,1024]{1,0:T(8,128)(2,1)S(1)} %get-tuple-element.24.refs_0_, bf16[768,1024]{1,0:T(8,128)(2,1)} %collective-permute-done.8.refs_1_, bf16[384,1024]{1,0:T(8,128)(2,1)S(1)} %total.21.refs_2_.refs_1_), custom_call_target="tpu_custom_call" | custom-call | flops 1 | bytes 1 | tf_op jit(solution)/shard_map/total/pallas_call | solution.py:26
  88.3 1.6 collective-permute-start.16
  89.8 1.6 collective-permute-start.13
  92.0 1.3 collective-permute-start.10
  93.3 11.0 %collective-permute-done.12.refs_2_ = bf16[384,1024]{1,0:T(8,128)(2,1)S(1)} collective-permute-done((bf16[384,1024]{1,0:T(8,128)(2,1)S(1)}, bf16[384,1024]{1,0:T(8,128)(2,1)S(1)}, u32[]{:S(2)}, u32[]{:S(2)}) %collective-permute-start.12) | collective-permute-done | bytes 786464 | tf_op jit(solution)/shard_map/ppermute | solution.py:389
  105.0 0.7 collective-permute-start.15
  105.7 8.3 %collective-permute-done.11.refs_1_ = bf16[768,1024]{1,0:T(8,128)(2,1)S(1)} collective-permute-done((bf16[768,1024]{1,0:T(8,128)(2,1)S(1)}, bf16[768,1024]{1,0:T(8,128)(2,1)S(1)}, u32[]{:S(2)}, u32[]{:S(2)}) %collective-permute-start.11) | collective-permute-done | bytes 1572896 | tf_op jit(solution)/shard_map/ppermute | solution.py:382
  114.0 1.1 copy-done.13
  115.2 1.7 %total.25.refs_1_.refs_3_.refs_5_ = bf16[768,1024]{1,0:T(8,128)(2,1)S(1)} custom-call(bf16[768,1024]{1,0:T(8,128)(2,1)S(1)} %get-tuple-element.25.refs_0_, bf16[768,1024]{1,0:T(8,128)(2,1)} %copy-done.13, bf16[384,1024]{1,0:T(8,128)(2,1)S(1)} %total.24.refs_2_), custom_call_target="tpu_custom_call" | custom-call | flops 1 | bytes 1 | tf_op jit(solution)/shard_map/total/pallas_call | solution.py:26
  116.9 4.1 %collective-permute-start.19 = (bf16[768,1024]{1,0:T(8,128)(2,1)S(1)}, bf16[768,1024]{1,0:T(8,128)(2,1)S(1)}, u32[]{:S(2)}, u32[]{:S(2)}) collective-permute-start(bf16[768,1024]{1,0:T(8,128)(2,1)S(1)} %total.25.refs_1_.refs_3_.refs_5_), channel_id=1, source_target_pairs={{0,4},{12,8},{2,6},{14,10},{1,5},{13,9},{3,7},{15,11},{16,20},{28,... | collective-permute-start | bytes 4718600 | tf_op jit(solution)/shard_map/ppermute | solution.py:389
  121.7 1.3 collective-permute-start.21
  123.0 0.7 total.27.refs_3_.refs_1_
  125.2 0.9 collective-permute-start.17
  126.1 7.8 %expand.1 = (bf16[768,1024]{1,0:T(8,128)(2,1)}, bf16[384,1024]{1,0:T(8,128)(2,1)S(1)}, bf16[384,1024]{1,0:T(8,128)(2,1)S(1)}) custom-call(s32[32]{0:T(128)S(1)} %pad_add_fusion.refs_0_, bf16[48,1024]{1,0:T(8,128)(2,1)S(1)} %total.27.refs_3_.refs_1_, bf16[48,1024]{1,0:T(8,128)(2,1)S(1)} %collective-permute-done.14.refs_2_, s32[192,1]{1,0:T(8,128)S(1)} %copy.13.refs_3_, ...), custom_call_target="tpu_custom_call" | custom-call | flops 1 | bytes 1 | tf_op jit(solution)/shard_map/expand/pallas_call | solution.py:26
  134.0 13.2 %collective-permute-done.16.refs_2_.refs_6_ = bf16[768,1024]{1,0:T(8,128)(2,1)} collective-permute-done((bf16[768,1024]{1,0:T(8,128)(2,1)S(1)}, bf16[768,1024]{1,0:T(8,128)(2,1)}, u32[]{:S(2)}, u32[]{:S(2)}) %collective-permute-start.16) | collective-permute-done | bytes 1572896 | tf_op jit(solution)/shard_map/ppermute | solution.py:382
  147.2 3.0 %total.29.refs_0_.refs_3_.refs_6_ = bf16[768,1024]{1,0:T(8,128)(2,1)S(1)} custom-call(bf16[768,1024]{1,0:T(8,128)(2,1)} %get-tuple-element.22.refs_0_.refs_4_, bf16[768,1024]{1,0:T(8,128)(2,1)} %get-tuple-element.26.refs_1_.refs_5_.refs_8_, bf16[768,1024]{1,0:T(8,128)(2,1)} %collective-permute-done.16.refs_2_.refs_6_, ...), custom_call_target="tpu_custom_call" | custom-call | flops 1 | bytes 1 | tf_op jit(solution)/shard_map/total/pallas_call | solution.py:26
  150.2 1.1 copy-done.2
  151.3 1.6 collective-permute-done.19.refs_2_.refs_5_
  152.9 1.2 copy-done.12
  154.1 2.7 %total.30.refs_0_.refs_2_ = bf16[768,1024]{1,0:T(8,128)(2,1)S(1)} custom-call(bf16[768,1024]{1,0:T(8,128)(2,1)} %copy-done.2, bf16[384,1024]{1,0:T(8,128)(2,1)S(1)} %collective-permute-done.18.refs_1_, bf16[768,1024]{1,0:T(8,128)(2,1)} %copy-done.12, bf16[768,1024]{1,0:T(8,128)(2,1)} %copy-done.2, bf16[384,1024]{1,0:T(8,128)(2,1)S(1)} %collective-permute-done.20.refs_4_, ...), custom_call_target="tpu_custom_call" | custom-call | flops 1 | bytes 1 | tf_op jit(solution)/shard_map/total/pallas_call | solution.py:26
  156.8 1.3 collective-permute-done.21.refs_1_
  158.1 1.6 total.31
  (68 shorter events, 6.8 us)
Async XLA Ops:
  0.0 9.6 %collective-permute-start = (s32[192]{0:T(256)}, s32[192]{0:T(256)S(1)}, u32[]{:S(2)}, u32[]{:S(2)}) collective-permute-start(s32[192]{0:T(256)} %param.7), channel_id=1, source_target_pairs={{0,1},{1,0},{2,3},{3,2},{4,5},{5,4},{6,7},{7,6},{8,9},{9,8},{10,11... | collective-permute-start | bytes 2312 | tf_op jit(solution)/shard_map/ppermute | solution.py:395
  0.5 9.8 %collective-permute-start.1 = (bf16[768,1024]{1,0:T(8,128)(2,1)}, bf16[768,1024]{1,0:T(8,128)(2,1)}, u32[]{:S(2)}, u32[]{:S(2)}) collective-permute-start(bf16[768,1024]{1,0:T(8,128)(2,1)} %bitcast.6), channel_id=1, source_target_pairs={{0,1},{1,0},{2,3},{3,2},{4,5},{5,4},{6,7},{7,6},{8,9},{9,8},{10,11... | collective-permute-start | bytes 4718600 | tf_op jit(solution)/shard_map/ppermute | solution.py:395
  1.7 7.4 %copy-start.14 = (s32[192]{0:T(256)S(1)}, s32[192]{0:T(256)}, u32[]{:S(2)}) copy-start(s32[192]{0:T(256)} %param.7) | copy-start | bytes 2308
  6.1 26.2 %collective-permute-start.4 = (bf16[416,1024]{1,0:T(8,128)(2,1)}, bf16[416,1024]{1,0:T(8,128)(2,1)S(1)}, u32[]{:S(2)}, u32[]{:S(2)}) collective-permute-start(bf16[416,1024]{1,0:T(8,128)(2,1)} %products.5.refs_6_), channel_id=1, source_target_pairs={{0,2},{2,0},{4,6},{6,4},{8,10},{10,8},{12,14},{14,12},{1,3},{3,1},... | collective-permute-start | bytes 2555912 | tf_op jit(solution)/shard_map/ppermute | solution.py:382
  10.3 1.4 copy-start
  11.7 1.2 copy-start.8
  12.9 8.6 %copy-start.1 = (bf16[4,192,1024]{2,1,0:T(8,128)(2,1)S(1)}, bf16[4,192,1024]{2,1,0:T(8,128)(2,1)}, u32[]{:S(2)}) copy-start(bf16[4,192,1024]{2,1,0:T(8,128)(2,1)} %param.6) | copy-start | bytes 4718596
  12.9 8.6 %copy-start.11 = (s32[11]{0:T(128)S(1)}, s32[11]{0:T(128)}, u32[]{:S(2)}) copy-start(s32[11]{0:T(128)} %dynamic-slice_bitcast_fusion.refs_0_) | copy-start | bytes 136
  19.6 1.4 collective-permute-start.2
  24.6 22.5 %collective-permute-start.3 = (bf16[400,1024]{1,0:T(8,128)(2,1)S(1)}, bf16[400,1024]{1,0:T(8,128)(2,1)S(1)}, u32[]{:S(2)}, u32[]{:S(2)}) collective-permute-start(bf16[400,1024]{1,0:T(8,128)(2,1)S(1)} %products.6.refs_3_), channel_id=1, source_target_pairs={{0,2},{2,0},{4,6},{6,4},{8,10},{10,8},{12,14},{14,12},{1,3},{3,1},... | collective-permute-start | bytes 2457608 | tf_op jit(solution)/shard_map/ppermute | solution.py:382
  31.1 1.1 copy-start.9
  32.3 5.7 %copy-start.10 = (bf16[768,1024]{1,0:T(8,128)(2,1)S(1)}, bf16[768,1024]{1,0:T(8,128)(2,1)}, u32[]{:S(2)}) copy-start(bf16[768,1024]{1,0:T(8,128)(2,1)} %copy-done.9) | copy-start | bytes 4718596
  33.9 29.7 %collective-permute-start.6 = (bf16[416,1024]{1,0:T(8,128)(2,1)S(1)}, bf16[416,1024]{1,0:T(8,128)(2,1)S(1)}, u32[]{:S(2)}, u32[]{:S(2)}) collective-permute-start(bf16[416,1024]{1,0:T(8,128)(2,1)S(1)} %total.17.refs_3_.refs_1_), channel_id=1, source_target_pairs={{0,4},{12,8},{2,6},{14,10},{1,5},{13,9},{3,7},{15,11},{16,20},{28,... | collective-permute-start | bytes 2555912 | tf_op jit(solution)/shard_map/ppermute | solution.py:389
  37.9 42.5 %collective-permute-start.8 = (bf16[768,1024]{1,0:T(8,128)(2,1)S(1)}, bf16[768,1024]{1,0:T(8,128)(2,1)}, u32[]{:S(2)}, u32[]{:S(2)}) collective-permute-start(bf16[768,1024]{1,0:T(8,128)(2,1)S(1)} %copy-done.10), channel_id=1, source_target_pairs={{0,2},{2,0},{4,6},{6,4},{8,10},{10,8},{12,14},{14,12},{1,3},{3,1},... | collective-permute-start | bytes 4718600 | tf_op jit(solution)/shard_map/ppermute | solution.py:382
  46.0 1.1 copy-start.6
  48.6 25.0 %collective-permute-start.5 = (bf16[400,1024]{1,0:T(8,128)(2,1)S(1)}, bf16[400,1024]{1,0:T(8,128)(2,1)S(1)}, u32[]{:S(2)}, u32[]{:S(2)}) collective-permute-start(bf16[400,1024]{1,0:T(8,128)(2,1)S(1)} %total.18.refs_3_.refs_1_.refs_0_), channel_id=1, source_target_pairs={{0,4},{12,8},{2,6},{14,10},{1,5},{13,9},{3,7},{15,11},{16,20},{28,... | collective-permute-start | bytes 2457608 | tf_op jit(solution)/shard_map/ppermute | solution.py:389
  62.5 1.2 copy-start.4
  63.6 1.4 copy-start.7
  64.3 25.6 %collective-permute-start.9 = (bf16[416,1024]{1,0:T(8,128)(2,1)}, bf16[416,1024]{1,0:T(8,128)(2,1)S(1)}, u32[]{:S(2)}, u32[]{:S(2)}) collective-permute-start(bf16[416,1024]{1,0:T(8,128)(2,1)} %total.19.refs_5_), channel_id=1, source_target_pairs={{4,8},{8,4},{6,10},{10,6},{5,9},{9,5},{7,11},{11,7},{20,24},{24,20... | collective-permute-start | bytes 2555912 | tf_op jit(solution)/shard_map/ppermute | solution.py:389
  65.1 49.0 %collective-permute-start.11 = (bf16[768,1024]{1,0:T(8,128)(2,1)S(1)}, bf16[768,1024]{1,0:T(8,128)(2,1)S(1)}, u32[]{:S(2)}, u32[]{:S(2)}) collective-permute-start(bf16[768,1024]{1,0:T(8,128)(2,1)S(1)} %hold.2), channel_id=1, source_target_pairs={{0,2},{2,0},{4,6},{6,4},{8,10},{10,8},{12,14},{14,12},{1,3},{3,1},... | collective-permute-start | bytes 4718600 | tf_op jit(solution)/shard_map/ppermute | solution.py:382
  74.3 17.2 %collective-permute-start.7 = (bf16[400,1024]{1,0:T(8,128)(2,1)S(1)}, bf16[400,1024]{1,0:T(8,128)(2,1)S(1)}, u32[]{:S(2)}, u32[]{:S(2)}) collective-permute-start(bf16[400,1024]{1,0:T(8,128)(2,1)S(1)} %total.20.refs_2_), channel_id=1, source_target_pairs={{4,8},{8,4},{6,10},{10,6},{5,9},{9,5},{7,11},{11,7},{20,24},{24,20... | collective-permute-start | bytes 2457608 | tf_op jit(solution)/shard_map/ppermute | solution.py:389
  82.2 6.0 %copy-start.5 = (bf16[768,1024]{1,0:T(8,128)(2,1)S(1)}, bf16[768,1024]{1,0:T(8,128)(2,1)}, u32[]{:S(2)}) copy-start(bf16[768,1024]{1,0:T(8,128)(2,1)} %copy-done.4) | copy-start | bytes 4718596
  82.2 22.1 %collective-permute-start.12 = (bf16[384,1024]{1,0:T(8,128)(2,1)S(1)}, bf16[384,1024]{1,0:T(8,128)(2,1)S(1)}, u32[]{:S(2)}, u32[]{:S(2)}) collective-permute-start(bf16[384,1024]{1,0:T(8,128)(2,1)S(1)} %total.21.refs_2_.refs_1_), channel_id=1, source_target_pairs={{0,4},{12,8},{2,6},{14,10},{1,5},{13,9},{3,7},{15,11},{16,20},{28,... | collective-permute-start | bytes 2359304 | tf_op jit(solution)/shard_map/ppermute | solution.py:389
  88.3 58.9 %collective-permute-start.16 = (bf16[768,1024]{1,0:T(8,128)(2,1)S(1)}, bf16[768,1024]{1,0:T(8,128)(2,1)}, u32[]{:S(2)}, u32[]{:S(2)}) collective-permute-start(bf16[768,1024]{1,0:T(8,128)(2,1)S(1)} %hold.3), channel_id=1, source_target_pairs={{0,2},{2,0},{4,6},{6,4},{8,10},{10,8},{12,14},{14,12},{1,3},{3,1},... | collective-permute-start | bytes 4718600 | tf_op jit(solution)/shard_map/ppermute | solution.py:382
  89.8 31.2 %collective-permute-start.13 = (bf16[384,1024]{1,0:T(8,128)(2,1)S(1)}, bf16[384,1024]{1,0:T(8,128)(2,1)S(1)}, u32[]{:S(2)}, u32[]{:S(2)}) collective-permute-start(bf16[384,1024]{1,0:T(8,128)(2,1)S(1)} %total.22.refs_3_.refs_1_), channel_id=1, source_target_pairs={{0,4},{12,8},{2,6},{14,10},{1,5},{13,9},{3,7},{15,11},{16,20},{28,... | collective-permute-start | bytes 2359304 | tf_op jit(solution)/shard_map/ppermute | solution.py:389
  92.0 29.0 %collective-permute-start.10 = (bf16[48,1024]{1,0:T(8,128)(2,1)S(1)}, bf16[48,1024]{1,0:T(8,128)(2,1)S(1)}, u32[]{:S(2)}, u32[]{:S(2)}) collective-permute-start(bf16[48,1024]{1,0:T(8,128)(2,1)S(1)} %total.23.refs_3_), channel_id=1, source_target_pairs={{8,12},{4,0},{10,14},{6,2},{9,13},{5,1},{11,15},{7,3},{24,28},{20,... | collective-permute-start | bytes 294920 | tf_op jit(solution)/shard_map/ppermute | solution.py:389
  105.0 21.1 %collective-permute-start.15 = (bf16[384,1024]{1,0:T(8,128)(2,1)S(1)}, bf16[384,1024]{1,0:T(8,128)(2,1)S(1)}, u32[]{:S(2)}, u32[]{:S(2)}) collective-permute-start(bf16[384,1024]{1,0:T(8,128)(2,1)S(1)} %total.24.refs_2_), channel_id=1, source_target_pairs={{4,8},{8,4},{6,10},{10,6},{5,9},{9,5},{7,11},{11,7},{20,24},{24,20... | collective-permute-start | bytes 2359304 | tf_op jit(solution)/shard_map/ppermute | solution.py:389
  114.0 1.1 copy-start.13
  116.9 4.2 %copy-start.3 = (bf16[768,1024]{1,0:T(8,128)(2,1)}, bf16[768,1024]{1,0:T(8,128)(2,1)S(1)}, u32[]{:S(2)}) copy-start(bf16[768,1024]{1,0:T(8,128)(2,1)S(1)} %total.25.refs_1_.refs_3_.refs_5_) | copy-start | bytes 4718596
  116.9 36.0 %collective-permute-start.19 = (bf16[768,1024]{1,0:T(8,128)(2,1)S(1)}, bf16[768,1024]{1,0:T(8,128)(2,1)S(1)}, u32[]{:S(2)}, u32[]{:S(2)}) collective-permute-start(bf16[768,1024]{1,0:T(8,128)(2,1)S(1)} %total.25.refs_1_.refs_3_.refs_5_), channel_id=1, source_target_pairs={{0,4},{12,8},{2,6},{14,10},{1,5},{13,9},{3,7},{15,11},{16,20},{28,... | collective-permute-start | bytes 4718600 | tf_op jit(solution)/shard_map/ppermute | solution.py:389
  121.7 36.3 %collective-permute-start.21 = (bf16[768,1024]{1,0:T(8,128)(2,1)}, bf16[768,1024]{1,0:T(8,128)(2,1)S(1)}, u32[]{:S(2)}, u32[]{:S(2)}) collective-permute-start(bf16[768,1024]{1,0:T(8,128)(2,1)} %total.26.refs_4_), channel_id=1, source_target_pairs={{8,12},{4,0},{10,14},{6,2},{9,13},{5,1},{11,15},{7,3},{24,28},{20,... | collective-permute-start | bytes 4718600 | tf_op jit(solution)/shard_map/ppermute | solution.py:389
  123.8 1.4 collective-permute-start.14
  125.2 22.0 %collective-permute-start.17 = (bf16[384,1024]{1,0:T(8,128)(2,1)S(1)}, bf16[384,1024]{1,0:T(8,128)(2,1)S(1)}, u32[]{:S(2)}, u32[]{:S(2)}) collective-permute-start(bf16[384,1024]{1,0:T(8,128)(2,1)S(1)} %total.28.refs_6_), channel_id=1, source_target_pairs={{4,8},{8,4},{6,10},{10,6},{5,9},{9,5},{7,11},{11,7},{20,24},{24,20... | collective-permute-start | bytes 2359304 | tf_op jit(solution)/shard_map/ppermute | solution.py:389
  133.9 19.0 %collective-permute-start.18 = (bf16[384,1024]{1,0:T(8,128)(2,1)S(1)}, bf16[384,1024]{1,0:T(8,128)(2,1)S(1)}, u32[]{:S(2)}, u32[]{:S(2)}) collective-permute-start(bf16[384,1024]{1,0:T(8,128)(2,1)S(1)} %get-tuple-element.27), channel_id=1, source_target_pairs={{0,1},{1,0},{2,3},{3,2},{4,5},{5,4},{6,7},{7,6},{8,9},{9,8},{10,11... | collective-permute-start | bytes 2359304 | tf_op jit(solution)/shard_map/ppermute | solution.py:395
  147.2 5.7 %collective-permute-start.20 = (bf16[384,1024]{1,0:T(8,128)(2,1)S(1)}, bf16[384,1024]{1,0:T(8,128)(2,1)S(1)}, u32[]{:S(2)}, u32[]{:S(2)}) collective-permute-start(bf16[384,1024]{1,0:T(8,128)(2,1)S(1)} %get-tuple-element.28), channel_id=1, source_target_pairs={{0,1},{1,0},{2,3},{3,2},{4,5},{5,4},{6,7},{7,6},{8,9},{9,8},{10,11... | collective-permute-start | bytes 2359304 | tf_op jit(solution)/shard_map/ppermute | solution.py:395
  150.2 1.1 copy-start.2
  152.9 1.2 copy-start.12

commit v17 on v16

--- a/solution.py
+++ b/solution.py
@@ -13,7 +13,7 @@
 LOW_WITH = (0, PARTS - 1)
 LOW_SUM_AFTER = (2, 0, 0)
 EXPAND_AFTER = (1, 1, 1)
-VMEM = 50 * 2**20
+VMEM = 47 * 2**20
 ANY = pl.BlockSpec(memory_space=pl.ANY)
 
 
@@ -505,7 +505,7 @@
 
     row_ids = [tenant] + [pass_on(tenant, shift) for shift in range(1, owners)]
     row_sets = [rows] + [pass_on(rows, shift) for shift in range(1, owners)]
-    multiply([(0, 0)], [], chunk=512, vmem=VMEM + 13 * 2**20)
+    multiply([(0, 0)], [], chunk=512, vmem=VMEM + 16 * 2**20)
     start_y(0, 0)
     named = [slots(some_ids, me) for some_ids in row_ids]
     names = jnp.concatenate([which for which, _ in named])

time: 160 us -> 159 us (level)
  waiting for transfers between devices: 49.9 us -> 57.2 us
  local copies, waits for them, and re-layouts: 11 us -> 5.16 us
  Pallas kernels: 65.5 us -> 60.6 us
  starting transfers between devices: 31.9 us -> 34 us
    ppermute x5, waiting for transfers between devices: 26.9 us -> 33.4 us  [swap_y(): return lax.ppermute(value, 'tensor', [(t, t ^ 1) for t in range(n)])]
    unnamed x30 -> x14, local copies, waits for them, and re-layouts: 9.55 us -> 3.73 us
    pallas_call x25, Pallas kernels: 65.5 us -> 60.6 us  [call(): pl.pallas_call(body, grid_spec=pltpu.PrefetchScalarGridSpec(num_scalar_pr...]
    ppermute x11, starting transfers between devices: 23.3 us -> 25.3 us  [hop(): return lax.ppermute(value, 'tensor', pairs)]
  transfers between devices with their start and end apart: 22 -> 22, of which waited for: 9 -> 10; matrix products, arithmetic and copies ran while one was open for 1% -> 1% of each run, Pallas kernels for 40% -> 37%
where the time goes in v17:
time: 159 us
  Pallas kernels  60.6 us (38%)
  waiting for transfers between devices  57.2 us (36%)
  starting transfers between devices  34 us (21%)
  local copies, waits for them, and re-layouts  5.16 us (3%)
    pallas_call x25, Pallas kernels, call(): pl.pallas_call(body, grid_spec=pltpu.PrefetchScalarGridSpec(num_scalar_pr...  60.6 us
    ppermute x5, waiting for transfers between devices, swap_y(): return lax.ppermute(value, 'tensor', [(t, t ^ 1) for t in range(n)])  33.4 us
    ppermute x11, starting transfers between devices, hop(): return lax.ppermute(value, 'tensor', pairs)  25.3 us
    ppermute x11, waiting for transfers between devices, hop(): return lax.ppermute(value, 'tensor', pairs)  21.9 us
    ppermute x5, starting transfers between devices, swap_y(): return lax.ppermute(value, 'tensor', [(t, t ^ 1) for t in range(n)])  7.87 us
    unnamed x14, local copies, waits for them, and re-layouts  3.73 us
  transfers between devices with their start and end apart: 22, of which 10 were waited for; matrix products, arithmetic and copies ran while one was open for 1% of the time, Pallas kernels for 37%

profile of v17, /device:TPU:0, one launch (start us, length us, event | category | flops | bytes accessed | tf_op | source)
XLA Modules:
  0.0 158.5 jit_solution(13253347257921544900)
XLA Ops:
  0.5 1.2 dynamic-slice_bitcast_fusion.refs_0_
  1.7 4.3 %products.5.refs_6_ = bf16[416,1024]{1,0:T(8,128)(2,1)} custom-call(s32[11]{0:T(128)} %dynamic-slice_bitcast_fusion.refs_0_, bf16[768,1024]{1,0:T(8,128)(2,1)} %bitcast.7, bf16[1024,8192]{1,0:T(8,128)(2,1)} %refs_2_.9), custom_call_target="tpu_custom_call" | custom-call | flops 1 | bytes 1 | tf_op jit(solution)/shard_map/products/pallas_call | solution.py:26
  6.1 3.0 %collective-permute-start.4 = (bf16[416,1024]{1,0:T(8,128)(2,1)}, bf16[416,1024]{1,0:T(8,128)(2,1)S(1)}, u32[]{:S(2)}, u32[]{:S(2)}) collective-permute-start(bf16[416,1024]{1,0:T(8,128)(2,1)} %products.5.refs_6_), channel_id=1, source_target_pairs={{0,2},{2,0},{4,6},{6,4},{8,10},{10,8},{12,14},{14,12},{1,3},{3,1},... | collective-permute-start | bytes 2555912 | tf_op jit(solution)/shard_map/ppermute | solution.py:382
  10.3 1.4 copy-done
  11.7 1.2 copy-done.4
  12.9 6.6 %low_rank.1 = (bf16[48,1024]{1,0:T(8,128)(2,1)S(1)}, bf16[48,1024]{1,0:T(8,128)(2,1)S(1)}) custom-call(s32[32]{0:T(128)S(1)} %pad_add_fusion.refs_0_, bf16[768,1024]{1,0:T(8,128)(2,1)S(1)} %bitcast.8, bf16[768,1024]{1,0:T(8,128)(2,1)} %collective-permute-done.1.refs_2_, s32[192,1]{1,0:T(8,128)S(1)} %copy.13.refs_3_, s32[192,1]{1,0:T(8,128)S(1)} %copy.14.refs_4_, ...), custom_call_target="tpu_custom_call" | custom-call | flops 1 | bytes 1 | tf_op jit(solution)/shard_map/low_rank/pallas_call | solution.py:26
  19.5 1.3 collective-permute-done.2.refs_1_
  21.2 3.1 %products.6.refs_3_ = bf16[400,1024]{1,0:T(8,128)(2,1)S(1)} custom-call(s32[11]{0:T(128)S(1)} %copy-done.5, bf16[768,1024]{1,0:T(8,128)(2,1)S(1)} %bitcast.9, bf16[1024,8192]{1,0:T(8,128)(2,1)} %refs_2_.9, bf16[48,1024]{1,0:T(8,128)(2,1)S(1)} %total.16.refs_3_.refs_4_.refs_2_, bf16[48,1024]{1,0:T(8,128)(2,1)S(1)} %total.16.refs_3_.refs_4_.refs_2_), custom_call_target="tpu_custom_call" | custom-call | flops 1 | bytes 1 | tf_op jit(solution)/shard_map/products/pallas_call | solution.py:26
  24.5 6.0 %products.7 = (bf16[768,1024]{1,0:T(8,128)(2,1)}, bf16[768,1024]{1,0:T(8,128)(2,1)S(1)}) custom-call(s32[11]{0:T(128)S(1)} %copy-done.5, bf16[768,1024]{1,0:T(8,128)(2,1)S(1)} %bitcast.10, bf16[1024,8192]{1,0:T(8,128)(2,1)} %refs_2_.9, bf16[400,1024]{1,0:T(8,128)(2,1)S(1)} %products.6.refs_3_), custom_call_target="tpu_custom_call" | custom-call | flops 1 | bytes 1 | tf_op jit(solution)/shard_map/products/pallas_call | solution.py:26
  30.4 1.6 %total.17.refs_3_.refs_1_ = bf16[416,1024]{1,0:T(8,128)(2,1)S(1)} custom-call(bf16[768,1024]{1,0:T(8,128)(2,1)S(1)} %get-tuple-element.19.refs_0_, bf16[416,1024]{1,0:T(8,128)(2,1)S(1)} %collective-permute-done.4.refs_1_, bf16[768,1024]{1,0:T(8,128)(2,1)} %get-tuple-element.20.refs_2_), custom_call_target="tpu_custom_call" | custom-call | flops 1 | bytes 1 | tf_op jit(solution)/shard_map/total/pallas_call | solution.py:26
  32.1 4.0 %collective-permute-start.6 = (bf16[416,1024]{1,0:T(8,128)(2,1)S(1)}, bf16[416,1024]{1,0:T(8,128)(2,1)S(1)}, u32[]{:S(2)}, u32[]{:S(2)}) collective-permute-start(bf16[416,1024]{1,0:T(8,128)(2,1)S(1)} %total.17.refs_3_.refs_1_), channel_id=1, source_target_pairs={{0,4},{12,8},{2,6},{14,10},{1,5},{13,9},{3,7},{15,11},{16,20},{28,... | collective-permute-start | bytes 2555912 | tf_op jit(solution)/shard_map/ppermute | solution.py:389
  36.1 1.6 collective-permute-start.8
  37.7 6.0 %products.8 = (bf16[768,1024]{1,0:T(8,128)(2,1)}, bf16[768,1024]{1,0:T(8,128)(2,1)S(1)}) custom-call(s32[11]{0:T(128)S(1)} %copy-done.5, bf16[768,1024]{1,0:T(8,128)(2,1)S(1)} %bitcast.11, bf16[1024,8192]{1,0:T(8,128)(2,1)} %refs_2_.9, bf16[416,1024]{1,0:T(8,128)(2,1)S(1)} %total.17.refs_3_.refs_1_), custom_call_target="tpu_custom_call" | custom-call | flops 1 | bytes 1 | tf_op jit(solution)/shard_map/products/pallas_call | solution.py:26
  43.7 1.1 copy-done.2
  44.8 1.8 %collective-permute-done.3.refs_1_.refs_3_ = bf16[400,1024]{1,0:T(8,128)(2,1)S(1)} collective-permute-done((bf16[400,1024]{1,0:T(8,128)(2,1)S(1)}, bf16[400,1024]{1,0:T(8,128)(2,1)S(1)}, u32[]{:S(2)}, u32[]{:S(2)}) %collective-permute-start.3) | collective-permute-done | bytes 819232 | tf_op jit(solution)/shard_map/ppermute | solution.py:382
  46.6 1.5 total.18.refs_3_.refs_1_.refs_0_
  48.1 4.3 %collective-permute-start.5 = (bf16[400,1024]{1,0:T(8,128)(2,1)S(1)}, bf16[400,1024]{1,0:T(8,128)(2,1)S(1)}, u32[]{:S(2)}, u32[]{:S(2)}) collective-permute-start(bf16[400,1024]{1,0:T(8,128)(2,1)S(1)} %total.18.refs_3_.refs_1_.refs_0_), channel_id=1, source_target_pairs={{0,4},{12,8},{2,6},{14,10},{1,5},{13,9},{3,7},{15,11},{16,20},{28,... | collective-permute-start | bytes 2457608 | tf_op jit(solution)/shard_map/ppermute | solution.py:389
  52.4 8.0 %products.9 = (bf16[768,1024]{1,0:T(8,128)(2,1)S(1)}, bf16[768,1024]{1,0:T(8,128)(2,1)S(1)}, bf16[768,1024]{1,0:T(8,128)(2,1)S(1)}) custom-call(s32[11]{0:T(128)S(1)} %copy-done.5, bf16[768,1024]{1,0:T(8,128)(2,1)S(1)} %bitcast.12, bf16[1024,8192]{1,0:T(8,128)(2,1)} %refs_2_.9, bf16[400,1024]{1,0:T(8,128)(2,1)S(1)} %total.18.refs_3_.refs_1_.refs_0_), custom_call_target="tpu_custom_call" | custom-call | flops 1 | bytes 1 | tf_op jit(solution)/shard_map/products/pallas_call | solution.py:26
  60.4 0.6 total.19.refs_5_
  61.0 0.7 collective-permute-start.9
  61.8 1.6 collective-permute-start.11
  63.4 8.5 %collective-permute-done.5.refs_2_.refs_4_.refs_1_ = bf16[400,1024]{1,0:T(8,128)(2,1)S(1)} collective-permute-done((bf16[400,1024]{1,0:T(8,128)(2,1)S(1)}, bf16[400,1024]{1,0:T(8,128)(2,1)S(1)}, u32[]{:S(2)}, u32[]{:S(2)}) %collective-permute-start.5) | collective-permute-done | bytes 819232 | tf_op jit(solution)/shard_map/ppermute | solution.py:389
  71.8 0.6 total.20.refs_2_
  72.5 0.7 collective-permute-start.7
  73.2 7.1 %collective-permute-done.8.refs_1_ = bf16[768,1024]{1,0:T(8,128)(2,1)S(1)} collective-permute-done((bf16[768,1024]{1,0:T(8,128)(2,1)}, bf16[768,1024]{1,0:T(8,128)(2,1)S(1)}, u32[]{:S(2)}, u32[]{:S(2)}) %collective-permute-start.8) | collective-permute-done | bytes 1572896 | tf_op jit(solution)/shard_map/ppermute | solution.py:382
  80.3 1.4 total.21.refs_2_.refs_1_
  81.7 4.9 %collective-permute-start.12 = (bf16[384,1024]{1,0:T(8,128)(2,1)S(1)}, bf16[384,1024]{1,0:T(8,128)(2,1)}, u32[]{:S(2)}, u32[]{:S(2)}) collective-permute-start(bf16[384,1024]{1,0:T(8,128)(2,1)S(1)} %total.21.refs_2_.refs_1_), channel_id=1, source_target_pairs={{0,4},{12,8},{2,6},{14,10},{1,5},{13,9},{3,7},{15,11},{16,20},{28,... | collective-permute-start | bytes 2359304 | tf_op jit(solution)/shard_map/ppermute | solution.py:389
  86.6 1.4 total.22.refs_3_.refs_1_
  88.0 1.6 collective-permute-start.16
  89.6 1.3 collective-permute-start.13
  91.5 1.3 collective-permute-start.10
  92.8 10.9 %collective-permute-done.12.refs_2_ = bf16[384,1024]{1,0:T(8,128)(2,1)} collective-permute-done((bf16[384,1024]{1,0:T(8,128)(2,1)S(1)}, bf16[384,1024]{1,0:T(8,128)(2,1)}, u32[]{:S(2)}, u32[]{:S(2)}) %collective-permute-start.12) | collective-permute-done | bytes 786464 | tf_op jit(solution)/shard_map/ppermute | solution.py:389
  104.3 0.7 collective-permute-start.15
  105.0 9.0 %collective-permute-done.11.refs_1_ = bf16[768,1024]{1,0:T(8,128)(2,1)S(1)} collective-permute-done((bf16[768,1024]{1,0:T(8,128)(2,1)}, bf16[768,1024]{1,0:T(8,128)(2,1)S(1)}, u32[]{:S(2)}, u32[]{:S(2)}) %collective-permute-start.11) | collective-permute-done | bytes 1572896 | tf_op jit(solution)/shard_map/ppermute | solution.py:382
  114.0 0.8 total.25.refs_1_.refs_3_.refs_5_
  114.8 5.2 %collective-permute-start.19 = (bf16[768,1024]{1,0:T(8,128)(2,1)S(1)}, bf16[768,1024]{1,0:T(8,128)(2,1)}, u32[]{:S(2)}, u32[]{:S(2)}) collective-permute-start(bf16[768,1024]{1,0:T(8,128)(2,1)S(1)} %total.25.refs_1_.refs_3_.refs_5_), channel_id=1, source_target_pairs={{0,4},{12,8},{2,6},{14,10},{1,5},{13,9},{3,7},{15,11},{16,20},{28,... | collective-permute-start | bytes 4718600 | tf_op jit(solution)/shard_map/ppermute | solution.py:389
  120.0 0.7 total.26.refs_4_
  120.6 1.3 collective-permute-start.21
  121.9 0.7 total.27.refs_3_.refs_1_
  122.8 0.6 total.28.refs_6_
  123.4 0.7 collective-permute-done.14.refs_2_
  124.0 0.9 collective-permute-start.17
  125.0 6.7 %expand.1 = (bf16[768,1024]{1,0:T(8,128)(2,1)S(1)}, bf16[384,1024]{1,0:T(8,128)(2,1)S(1)}, bf16[384,1024]{1,0:T(8,128)(2,1)S(1)}) custom-call(s32[32]{0:T(128)S(1)} %pad_add_fusion.refs_0_, bf16[48,1024]{1,0:T(8,128)(2,1)S(1)} %total.27.refs_3_.refs_1_, bf16[48,1024]{1,0:T(8,128)(2,1)S(1)} %collective-permute-done.14.refs_2_, s32[192,1]{1,0:T(8,128)S(1)} %copy.13.refs_3_, ...), custom_call_target="tpu_custom_call" | custom-call | flops 1 | bytes 1 | tf_op jit(solution)/shard_map/expand/pallas_call | solution.py:26
  131.8 15.4 %collective-permute-done.16.refs_2_.refs_6_ = bf16[768,1024]{1,0:T(8,128)(2,1)} collective-permute-done((bf16[768,1024]{1,0:T(8,128)(2,1)S(1)}, bf16[768,1024]{1,0:T(8,128)(2,1)}, u32[]{:S(2)}, u32[]{:S(2)}) %collective-permute-start.16) | collective-permute-done | bytes 1572896 | tf_op jit(solution)/shard_map/ppermute | solution.py:382
  147.2 4.0 %total.29.refs_0_.refs_3_.refs_6_ = bf16[768,1024]{1,0:T(8,128)(2,1)S(1)} custom-call(bf16[768,1024]{1,0:T(8,128)(2,1)S(1)} %get-tuple-element.22.refs_0_.refs_4_, bf16[768,1024]{1,0:T(8,128)(2,1)S(1)} %get-tuple-element.26.refs_1_.refs_5_.refs_8_, bf16[768,1024]{1,0:T(8,128)(2,1)} %collective-permute-done.16.refs_2_.refs_6_, ...), custom_call_target="tpu_custom_call" | custom-call | flops 1 | bytes 1 | tf_op jit(solution)/shard_map/total/pallas_call | solution.py:26
  151.4 3.0 %total.30.refs_0_.refs_2_ = bf16[768,1024]{1,0:T(8,128)(2,1)S(1)} custom-call(bf16[768,1024]{1,0:T(8,128)(2,1)S(1)} %total.29.refs_0_.refs_3_.refs_6_, bf16[384,1024]{1,0:T(8,128)(2,1)S(1)} %collective-permute-done.18.refs_1_, bf16[768,1024]{1,0:T(8,128)(2,1)} %collective-permute-done.19.refs_2_.refs_5_, ...), custom_call_target="tpu_custom_call" | custom-call | flops 1 | bytes 1 | tf_op jit(solution)/shard_map/total/pallas_call | solution.py:26
  154.4 2.3 %collective-permute-done.21.refs_1_ = bf16[768,1024]{1,0:T(8,128)(2,1)S(1)} collective-permute-done((bf16[768,1024]{1,0:T(8,128)(2,1)S(1)}, bf16[768,1024]{1,0:T(8,128)(2,1)S(1)}, u32[]{:S(2)}, u32[]{:S(2)}) %collective-permute-start.21) | collective-permute-done | bytes 1572896 | tf_op jit(solution)/shard_map/ppermute | solution.py:389
  156.7 1.6 total.31
  (52 shorter events, 3.9 us)
Async XLA Ops:
  0.0 9.6 %collective-permute-start = (s32[192]{0:T(256)}, s32[192]{0:T(256)S(1)}, u32[]{:S(2)}, u32[]{:S(2)}) collective-permute-start(s32[192]{0:T(256)} %param.7), channel_id=1, source_target_pairs={{0,1},{1,0},{2,3},{3,2},{4,5},{5,4},{6,7},{7,6},{8,9},{9,8},{10,11... | collective-permute-start | bytes 2312 | tf_op jit(solution)/shard_map/ppermute | solution.py:395
  0.5 9.8 %collective-permute-start.1 = (bf16[768,1024]{1,0:T(8,128)(2,1)}, bf16[768,1024]{1,0:T(8,128)(2,1)}, u32[]{:S(2)}, u32[]{:S(2)}) collective-permute-start(bf16[768,1024]{1,0:T(8,128)(2,1)} %bitcast.6), channel_id=1, source_target_pairs={{0,1},{1,0},{2,3},{3,2},{4,5},{5,4},{6,7},{7,6},{8,9},{9,8},{10,11... | collective-permute-start | bytes 4718600 | tf_op jit(solution)/shard_map/ppermute | solution.py:395
  1.7 7.4 %copy-start.6 = (s32[192]{0:T(256)S(1)}, s32[192]{0:T(256)}, u32[]{:S(2)}) copy-start(s32[192]{0:T(256)} %param.7) | copy-start | bytes 2308
  6.1 24.4 %collective-permute-start.4 = (bf16[416,1024]{1,0:T(8,128)(2,1)}, bf16[416,1024]{1,0:T(8,128)(2,1)S(1)}, u32[]{:S(2)}, u32[]{:S(2)}) collective-permute-start(bf16[416,1024]{1,0:T(8,128)(2,1)} %products.5.refs_6_), channel_id=1, source_target_pairs={{0,2},{2,0},{4,6},{6,4},{8,10},{10,8},{12,14},{14,12},{1,3},{3,1},... | collective-permute-start | bytes 2555912 | tf_op jit(solution)/shard_map/ppermute | solution.py:382
  10.3 1.4 copy-start
  11.7 1.2 copy-start.4
  12.9 8.4 %copy-start.1 = (bf16[4,192,1024]{2,1,0:T(8,128)(2,1)S(1)}, bf16[4,192,1024]{2,1,0:T(8,128)(2,1)}, u32[]{:S(2)}) copy-start(bf16[4,192,1024]{2,1,0:T(8,128)(2,1)} %param.6) | copy-start | bytes 4718596
  12.9 8.4 %copy-start.5 = (s32[11]{0:T(128)S(1)}, s32[11]{0:T(128)}, u32[]{:S(2)}) copy-start(s32[11]{0:T(128)} %dynamic-slice_bitcast_fusion.refs_0_) | copy-start | bytes 136
  19.4 1.4 collective-permute-start.2
  24.4 22.2 %collective-permute-start.3 = (bf16[400,1024]{1,0:T(8,128)(2,1)S(1)}, bf16[400,1024]{1,0:T(8,128)(2,1)S(1)}, u32[]{:S(2)}, u32[]{:S(2)}) collective-permute-start(bf16[400,1024]{1,0:T(8,128)(2,1)S(1)} %products.6.refs_3_), channel_id=1, source_target_pairs={{0,2},{2,0},{4,6},{6,4},{8,10},{10,8},{12,14},{14,12},{1,3},{3,1},... | collective-permute-start | bytes 2457608 | tf_op jit(solution)/shard_map/ppermute | solution.py:382
  32.1 28.3 %collective-permute-start.6 = (bf16[416,1024]{1,0:T(8,128)(2,1)S(1)}, bf16[416,1024]{1,0:T(8,128)(2,1)S(1)}, u32[]{:S(2)}, u32[]{:S(2)}) collective-permute-start(bf16[416,1024]{1,0:T(8,128)(2,1)S(1)} %total.17.refs_3_.refs_1_), channel_id=1, source_target_pairs={{0,4},{12,8},{2,6},{14,10},{1,5},{13,9},{3,7},{15,11},{16,20},{28,... | collective-permute-start | bytes 2555912 | tf_op jit(solution)/shard_map/ppermute | solution.py:389
  36.1 44.2 %collective-permute-start.8 = (bf16[768,1024]{1,0:T(8,128)(2,1)}, bf16[768,1024]{1,0:T(8,128)(2,1)S(1)}, u32[]{:S(2)}, u32[]{:S(2)}) collective-permute-start(bf16[768,1024]{1,0:T(8,128)(2,1)} %get-tuple-element.20.refs_2_), channel_id=1, source_target_pairs={{0,2},{2,0},{4,6},{6,4},{8,10},{10,8},{12,14},{14,12},{1,3},{3,1},... | collective-permute-start | bytes 4718600 | tf_op jit(solution)/shard_map/ppermute | solution.py:382
  43.7 1.2 copy-start.2
  48.1 23.7 %collective-permute-start.5 = (bf16[400,1024]{1,0:T(8,128)(2,1)S(1)}, bf16[400,1024]{1,0:T(8,128)(2,1)S(1)}, u32[]{:S(2)}, u32[]{:S(2)}) collective-permute-start(bf16[400,1024]{1,0:T(8,128)(2,1)S(1)} %total.18.refs_3_.refs_1_.refs_0_), channel_id=1, source_target_pairs={{0,4},{12,8},{2,6},{14,10},{1,5},{13,9},{3,7},{15,11},{16,20},{28,... | collective-permute-start | bytes 2457608 | tf_op jit(solution)/shard_map/ppermute | solution.py:389
  61.0 28.5 %collective-permute-start.9 = (bf16[416,1024]{1,0:T(8,128)(2,1)S(1)}, bf16[416,1024]{1,0:T(8,128)(2,1)S(1)}, u32[]{:S(2)}, u32[]{:S(2)}) collective-permute-start(bf16[416,1024]{1,0:T(8,128)(2,1)S(1)} %total.19.refs_5_), channel_id=1, source_target_pairs={{4,8},{8,4},{6,10},{10,6},{5,9},{9,5},{7,11},{11,7},{20,24},{24,20... | collective-permute-start | bytes 2555912 | tf_op jit(solution)/shard_map/ppermute | solution.py:389
  61.8 18.5 %copy-start.3 = (bf16[768,1024]{1,0:T(8,128)(2,1)S(1)}, bf16[768,1024]{1,0:T(8,128)(2,1)}, u32[]{:S(2)}) copy-start(bf16[768,1024]{1,0:T(8,128)(2,1)} %copy-done.2) | copy-start | bytes 4718596
  61.8 52.2 %collective-permute-start.11 = (bf16[768,1024]{1,0:T(8,128)(2,1)}, bf16[768,1024]{1,0:T(8,128)(2,1)S(1)}, u32[]{:S(2)}, u32[]{:S(2)}) collective-permute-start(bf16[768,1024]{1,0:T(8,128)(2,1)} %hold.2), channel_id=1, source_target_pairs={{0,2},{2,0},{4,6},{6,4},{8,10},{10,8},{12,14},{14,12},{1,3},{3,1},... | collective-permute-start | bytes 4718600 | tf_op jit(solution)/shard_map/ppermute | solution.py:382
  72.5 18.4 %collective-permute-start.7 = (bf16[400,1024]{1,0:T(8,128)(2,1)S(1)}, bf16[400,1024]{1,0:T(8,128)(2,1)S(1)}, u32[]{:S(2)}, u32[]{:S(2)}) collective-permute-start(bf16[400,1024]{1,0:T(8,128)(2,1)S(1)} %total.20.refs_2_), channel_id=1, source_target_pairs={{4,8},{8,4},{6,10},{10,6},{5,9},{9,5},{7,11},{11,7},{20,24},{24,20... | collective-permute-start | bytes 2457608 | tf_op jit(solution)/shard_map/ppermute | solution.py:389
  81.7 22.0 %collective-permute-start.12 = (bf16[384,1024]{1,0:T(8,128)(2,1)S(1)}, bf16[384,1024]{1,0:T(8,128)(2,1)}, u32[]{:S(2)}, u32[]{:S(2)}) collective-permute-start(bf16[384,1024]{1,0:T(8,128)(2,1)S(1)} %total.21.refs_2_.refs_1_), channel_id=1, source_target_pairs={{0,4},{12,8},{2,6},{14,10},{1,5},{13,9},{3,7},{15,11},{16,20},{28,... | collective-permute-start | bytes 2359304 | tf_op jit(solution)/shard_map/ppermute | solution.py:389
  88.0 59.2 %collective-permute-start.16 = (bf16[768,1024]{1,0:T(8,128)(2,1)S(1)}, bf16[768,1024]{1,0:T(8,128)(2,1)}, u32[]{:S(2)}, u32[]{:S(2)}) collective-permute-start(bf16[768,1024]{1,0:T(8,128)(2,1)S(1)} %hold.3), channel_id=1, source_target_pairs={{0,2},{2,0},{4,6},{6,4},{8,10},{10,8},{12,14},{14,12},{1,3},{3,1},... | collective-permute-start | bytes 4718600 | tf_op jit(solution)/shard_map/ppermute | solution.py:382
  89.6 30.4 %collective-permute-start.13 = (bf16[384,1024]{1,0:T(8,128)(2,1)S(1)}, bf16[384,1024]{1,0:T(8,128)(2,1)S(1)}, u32[]{:S(2)}, u32[]{:S(2)}) collective-permute-start(bf16[384,1024]{1,0:T(8,128)(2,1)S(1)} %total.22.refs_3_.refs_1_), channel_id=1, source_target_pairs={{0,4},{12,8},{2,6},{14,10},{1,5},{13,9},{3,7},{15,11},{16,20},{28,... | collective-permute-start | bytes 2359304 | tf_op jit(solution)/shard_map/ppermute | solution.py:389
  91.5 28.5 %collective-permute-start.10 = (bf16[48,1024]{1,0:T(8,128)(2,1)S(1)}, bf16[48,1024]{1,0:T(8,128)(2,1)S(1)}, u32[]{:S(2)}, u32[]{:S(2)}) collective-permute-start(bf16[48,1024]{1,0:T(8,128)(2,1)S(1)} %total.23.refs_3_), channel_id=1, source_target_pairs={{8,12},{4,0},{10,14},{6,2},{9,13},{5,1},{11,15},{7,3},{24,28},{20,... | collective-permute-start | bytes 294920 | tf_op jit(solution)/shard_map/ppermute | solution.py:389
  104.3 20.7 %collective-permute-start.15 = (bf16[384,1024]{1,0:T(8,128)(2,1)S(1)}, bf16[384,1024]{1,0:T(8,128)(2,1)S(1)}, u32[]{:S(2)}, u32[]{:S(2)}) collective-permute-start(bf16[384,1024]{1,0:T(8,128)(2,1)S(1)} %total.24.refs_2_), channel_id=1, source_target_pairs={{4,8},{8,4},{6,10},{10,6},{5,9},{9,5},{7,11},{11,7},{20,24},{24,20... | collective-permute-start | bytes 2359304 | tf_op jit(solution)/shard_map/ppermute | solution.py:389
  114.8 36.6 %collective-permute-start.19 = (bf16[768,1024]{1,0:T(8,128)(2,1)S(1)}, bf16[768,1024]{1,0:T(8,128)(2,1)}, u32[]{:S(2)}, u32[]{:S(2)}) collective-permute-start(bf16[768,1024]{1,0:T(8,128)(2,1)S(1)} %total.25.refs_1_.refs_3_.refs_5_), channel_id=1, source_target_pairs={{0,4},{12,8},{2,6},{14,10},{1,5},{13,9},{3,7},{15,11},{16,20},{28,... | collective-permute-start | bytes 4718600 | tf_op jit(solution)/shard_map/ppermute | solution.py:389
  120.6 36.1 %collective-permute-start.21 = (bf16[768,1024]{1,0:T(8,128)(2,1)S(1)}, bf16[768,1024]{1,0:T(8,128)(2,1)S(1)}, u32[]{:S(2)}, u32[]{:S(2)}) collective-permute-start(bf16[768,1024]{1,0:T(8,128)(2,1)S(1)} %total.26.refs_4_), channel_id=1, source_target_pairs={{8,12},{4,0},{10,14},{6,2},{9,13},{5,1},{11,15},{7,3},{24,28},{20,... | collective-permute-start | bytes 4718600 | tf_op jit(solution)/shard_map/ppermute | solution.py:389
  122.7 1.4 collective-permute-start.14
  124.0 23.2 %collective-permute-start.17 = (bf16[384,1024]{1,0:T(8,128)(2,1)S(1)}, bf16[384,1024]{1,0:T(8,128)(2,1)S(1)}, u32[]{:S(2)}, u32[]{:S(2)}) collective-permute-start(bf16[384,1024]{1,0:T(8,128)(2,1)S(1)} %total.28.refs_6_), channel_id=1, source_target_pairs={{4,8},{8,4},{6,10},{10,6},{5,9},{9,5},{7,11},{11,7},{20,24},{24,20... | collective-permute-start | bytes 2359304 | tf_op jit(solution)/shard_map/ppermute | solution.py:389
  131.7 19.8 %collective-permute-start.18 = (bf16[384,1024]{1,0:T(8,128)(2,1)S(1)}, bf16[384,1024]{1,0:T(8,128)(2,1)S(1)}, u32[]{:S(2)}, u32[]{:S(2)}) collective-permute-start(bf16[384,1024]{1,0:T(8,128)(2,1)S(1)} %get-tuple-element.27), channel_id=1, source_target_pairs={{0,1},{1,0},{2,3},{3,2},{4,5},{5,4},{6,7},{7,6},{8,9},{9,8},{10,11... | collective-permute-start | bytes 2359304 | tf_op jit(solution)/shard_map/ppermute | solution.py:395
  147.2 4.2 %collective-permute-start.20 = (bf16[384,1024]{1,0:T(8,128)(2,1)S(1)}, bf16[384,1024]{1,0:T(8,128)(2,1)S(1)}, u32[]{:S(2)}, u32[]{:S(2)}) collective-permute-start(bf16[384,1024]{1,0:T(8,128)(2,1)S(1)} %get-tuple-element.28), channel_id=1, source_target_pairs={{0,1},{1,0},{2,3},{3,2},{4,5},{5,4},{6,7},{7,6},{8,9},{9,8},{10,11... | collective-permute-start | bytes 2359304 | tf_op jit(solution)/shard_map/ppermute | solution.py:395

commit v18 on v17

--- a/solution.py
+++ b/solution.py
@@ -521,7 +521,7 @@
     for h, m, p in line_order():
         k = slot_of(h, m)
         if (h, m, p) == (2, 0, 0) and nz == 4:
-            last[0] += (arrived[0, 1, 1], pieces[-1][0])
+            last[0] += (pieces[-1][0],)
         line(h, m, p)
         if h == 0:
             if k == 0 and p == 0:
@@ -546,7 +546,6 @@
             low_sum = then(total, [(low_rows, pieces)])
             low_back = [low_sum] + [pass_on(low_sum, shift) for shift in range(1, owners)]
         if deltas is None and low_sum is not None and EXPAND_AFTER in arrived:
-            last[0] += (arrived[1, 1, 0],) if nz > 2 else ()
             deltas = then(expand, low_back, slot_sets, adapter_up_maps, names)
             back = [
                 [(*cut, pass_on(deltas[1 + (shift - 1) * PARTS + p], -shift), 0) for p, cut in enumerate(even)]

time: 159 us -> 159 us (level)
  waiting for transfers between devices: 57.2 us -> 54.9 us
  local copies, waits for them, and re-layouts: 5.16 us -> 7.17 us
    ppermute x5, waiting for transfers between devices: 33.4 us -> 28.5 us  [swap_y(): return lax.ppermute(value, 'tensor', [(t, t ^ 1) for t in range(n)])]
    ppermute x11, waiting for transfers between devices: 21.9 us -> 25.1 us  [hop(): return lax.ppermute(value, 'tensor', pairs)]
    unnamed x14 -> x18, local copies, waits for them, and re-layouts: 3.73 us -> 5.73 us
  transfers between devices with their start and end apart: 22 -> 22, of which waited for: 10 -> 9; matrix products, arithmetic and copies ran while one was open for 1% -> 1% of each run, Pallas kernels for 37% -> 37%
where the time goes in v18:
time: 159 us; the launch traced here: 158 us
  Pallas kernels  60.4 us (38%)
  waiting for transfers between devices  54.9 us (35%)
  starting transfers between devices  34.5 us (22%)
  local copies, waits for them, and re-layouts  7.17 us (5%)
    pallas_call x25, Pallas kernels, call(): pl.pallas_call(body, grid_spec=pltpu.PrefetchScalarGridSpec(num_scalar_pr...  60.4 us
    ppermute x5, waiting for transfers between devices, swap_y(): return lax.ppermute(value, 'tensor', [(t, t ^ 1) for t in range(n)])  28.5 us
    ppermute x11, waiting for transfers between devices, hop(): return lax.ppermute(value, 'tensor', pairs)  25.1 us
    ppermute x11, starting transfers between devices, hop(): return lax.ppermute(value, 'tensor', pairs)  25 us
    ppermute x5, starting transfers between devices, swap_y(): return lax.ppermute(value, 'tensor', [(t, t ^ 1) for t in range(n)])  8.35 us
    unnamed x18, local copies, waits for them, and re-layouts  5.73 us
  transfers between devices with their start and end apart: 22, of which 9 were waited for; matrix products, arithmetic and copies ran while one was open for 1% of the time, Pallas kernels for 37%

profile of v18, /device:TPU:0, one launch (start us, length us, event | category | flops | bytes accessed | tf_op | source)
XLA Modules:
  0.0 158.5 jit_solution(12641988068188468135)
XLA Ops:
  0.5 1.2 dynamic-slice_bitcast_fusion.refs_0_
  1.7 4.3 %products.5.refs_6_ = bf16[416,1024]{1,0:T(8,128)(2,1)} custom-call(s32[11]{0:T(128)} %dynamic-slice_bitcast_fusion.refs_0_, bf16[768,1024]{1,0:T(8,128)(2,1)} %bitcast.7, bf16[1024,8192]{1,0:T(8,128)(2,1)} %refs_2_.9), custom_call_target="tpu_custom_call" | custom-call | flops 1 | bytes 1 | tf_op jit(solution)/shard_map/products/pallas_call | solution.py:26
  6.1 3.0 %collective-permute-start.4 = (bf16[416,1024]{1,0:T(8,128)(2,1)}, bf16[416,1024]{1,0:T(8,128)(2,1)S(1)}, u32[]{:S(2)}, u32[]{:S(2)}) collective-permute-start(bf16[416,1024]{1,0:T(8,128)(2,1)} %products.5.refs_6_), channel_id=1, source_target_pairs={{0,2},{2,0},{4,6},{6,4},{8,10},{10,8},{12,14},{14,12},{1,3},{3,1},... | collective-permute-start | bytes 2555912 | tf_op jit(solution)/shard_map/ppermute | solution.py:382
  10.3 1.4 copy-done
  11.7 1.2 copy-done.4
  12.9 6.6 %low_rank.1 = (bf16[48,1024]{1,0:T(8,128)(2,1)S(1)}, bf16[48,1024]{1,0:T(8,128)(2,1)S(1)}) custom-call(s32[32]{0:T(128)S(1)} %pad_add_fusion.refs_0_, bf16[768,1024]{1,0:T(8,128)(2,1)S(1)} %bitcast.8, bf16[768,1024]{1,0:T(8,128)(2,1)} %collective-permute-done.1.refs_2_, s32[192,1]{1,0:T(8,128)S(1)} %copy.13.refs_3_, s32[192,1]{1,0:T(8,128)S(1)} %copy.14.refs_4_, ...), custom_call_target="tpu_custom_call" | custom-call | flops 1 | bytes 1 | tf_op jit(solution)/shard_map/low_rank/pallas_call | solution.py:26
  19.6 1.2 collective-permute-done.2.refs_1_
  21.2 3.1 %products.6.refs_3_ = bf16[400,1024]{1,0:T(8,128)(2,1)S(1)} custom-call(s32[11]{0:T(128)S(1)} %copy-done.7, bf16[768,1024]{1,0:T(8,128)(2,1)S(1)} %bitcast.9, bf16[1024,8192]{1,0:T(8,128)(2,1)} %refs_2_.9, bf16[48,1024]{1,0:T(8,128)(2,1)S(1)} %total.16.refs_3_.refs_4_.refs_2_, bf16[48,1024]{1,0:T(8,128)(2,1)S(1)} %total.16.refs_3_.refs_4_.refs_2_), custom_call_target="tpu_custom_call" | custom-call | flops 1 | bytes 1 | tf_op jit(solution)/shard_map/products/pallas_call | solution.py:26
  24.5 6.0 %products.7 = (bf16[768,1024]{1,0:T(8,128)(2,1)}, bf16[768,1024]{1,0:T(8,128)(2,1)S(1)}) custom-call(s32[11]{0:T(128)S(1)} %copy-done.7, bf16[768,1024]{1,0:T(8,128)(2,1)S(1)} %bitcast.10, bf16[1024,8192]{1,0:T(8,128)(2,1)} %refs_2_.9, bf16[400,1024]{1,0:T(8,128)(2,1)S(1)} %products.6.refs_3_), custom_call_target="tpu_custom_call" | custom-call | flops 1 | bytes 1 | tf_op jit(solution)/shard_map/products/pallas_call | solution.py:26
  30.5 2.0 %collective-permute-start.8 = (bf16[768,1024]{1,0:T(8,128)(2,1)}, bf16[768,1024]{1,0:T(8,128)(2,1)S(1)}, u32[]{:S(2)}, u32[]{:S(2)}) collective-permute-start(bf16[768,1024]{1,0:T(8,128)(2,1)} %get-tuple-element.20.refs_2_), channel_id=1, source_target_pairs={{0,2},{2,0},{4,6},{6,4},{8,10},{10,8},{12,14},{14,12},{1,3},{3,1},... | collective-permute-start | bytes 4718600 | tf_op jit(solution)/shard_map/ppermute | solution.py:382
  32.5 1.6 %total.17.refs_3_.refs_1_ = bf16[416,1024]{1,0:T(8,128)(2,1)S(1)} custom-call(bf16[768,1024]{1,0:T(8,128)(2,1)S(1)} %get-tuple-element.19.refs_0_, bf16[416,1024]{1,0:T(8,128)(2,1)S(1)} %collective-permute-done.4.refs_1_, bf16[768,1024]{1,0:T(8,128)(2,1)} %get-tuple-element.20.refs_2_), custom_call_target="tpu_custom_call" | custom-call | flops 1 | bytes 1 | tf_op jit(solution)/shard_map/total/pallas_call | solution.py:26
  34.1 3.5 %collective-permute-start.6 = (bf16[416,1024]{1,0:T(8,128)(2,1)S(1)}, bf16[416,1024]{1,0:T(8,128)(2,1)S(1)}, u32[]{:S(2)}, u32[]{:S(2)}) collective-permute-start(bf16[416,1024]{1,0:T(8,128)(2,1)S(1)} %total.17.refs_3_.refs_1_), channel_id=1, source_target_pairs={{0,4},{12,8},{2,6},{14,10},{1,5},{13,9},{3,7},{15,11},{16,20},{28,... | collective-permute-start | bytes 2555912 | tf_op jit(solution)/shard_map/ppermute | solution.py:389
  37.7 6.0 %products.8 = (bf16[768,1024]{1,0:T(8,128)(2,1)}, bf16[768,1024]{1,0:T(8,128)(2,1)S(1)}) custom-call(s32[11]{0:T(128)S(1)} %copy-done.7, bf16[768,1024]{1,0:T(8,128)(2,1)S(1)} %bitcast.11, bf16[1024,8192]{1,0:T(8,128)(2,1)} %refs_2_.9, bf16[416,1024]{1,0:T(8,128)(2,1)S(1)} %total.17.refs_3_.refs_1_), custom_call_target="tpu_custom_call" | custom-call | flops 1 | bytes 1 | tf_op jit(solution)/shard_map/products/pallas_call | solution.py:26
  43.7 1.2 copy-done.2
  44.8 1.8 %collective-permute-done.3.refs_1_.refs_3_ = bf16[400,1024]{1,0:T(8,128)(2,1)S(1)} collective-permute-done((bf16[400,1024]{1,0:T(8,128)(2,1)S(1)}, bf16[400,1024]{1,0:T(8,128)(2,1)S(1)}, u32[]{:S(2)}, u32[]{:S(2)}) %collective-permute-start.3) | collective-permute-done | bytes 819232 | tf_op jit(solution)/shard_map/ppermute | solution.py:382
  46.6 1.5 total.18.refs_3_.refs_1_.refs_0_
  48.1 4.3 %collective-permute-start.5 = (bf16[400,1024]{1,0:T(8,128)(2,1)S(1)}, bf16[400,1024]{1,0:T(8,128)(2,1)S(1)}, u32[]{:S(2)}, u32[]{:S(2)}) collective-permute-start(bf16[400,1024]{1,0:T(8,128)(2,1)S(1)} %total.18.refs_3_.refs_1_.refs_0_), channel_id=1, source_target_pairs={{0,4},{12,8},{2,6},{14,10},{1,5},{13,9},{3,7},{15,11},{16,20},{28,... | collective-permute-start | bytes 2457608 | tf_op jit(solution)/shard_map/ppermute | solution.py:389
  52.4 1.6 collective-permute-start.11
  54.0 8.0 %products.9 = (bf16[768,1024]{1,0:T(8,128)(2,1)S(1)}, bf16[768,1024]{1,0:T(8,128)(2,1)S(1)}, bf16[768,1024]{1,0:T(8,128)(2,1)S(1)}) custom-call(s32[11]{0:T(128)S(1)} %copy-done.7, bf16[768,1024]{1,0:T(8,128)(2,1)S(1)} %bitcast.12, bf16[1024,8192]{1,0:T(8,128)(2,1)} %refs_2_.9, bf16[400,1024]{1,0:T(8,128)(2,1)S(1)} %total.18.refs_3_.refs_1_.refs_0_), custom_call_target="tpu_custom_call" | custom-call | flops 1 | bytes 1 | tf_op jit(solution)/shard_map/products/pallas_call | solution.py:26
  62.6 0.8 collective-permute-start.9
  63.5 9.6 %collective-permute-done.5.refs_2_.refs_4_.refs_1_ = bf16[400,1024]{1,0:T(8,128)(2,1)S(1)} collective-permute-done((bf16[400,1024]{1,0:T(8,128)(2,1)S(1)}, bf16[400,1024]{1,0:T(8,128)(2,1)S(1)}, u32[]{:S(2)}, u32[]{:S(2)}) %collective-permute-start.5) | collective-permute-done | bytes 819232 | tf_op jit(solution)/shard_map/ppermute | solution.py:389
  73.1 0.6 total.20.refs_2_
  73.7 0.7 collective-permute-start.7
  74.5 5.8 %collective-permute-done.8.refs_1_ = bf16[768,1024]{1,0:T(8,128)(2,1)S(1)} collective-permute-done((bf16[768,1024]{1,0:T(8,128)(2,1)}, bf16[768,1024]{1,0:T(8,128)(2,1)S(1)}, u32[]{:S(2)}, u32[]{:S(2)}) %collective-permute-start.8) | collective-permute-done | bytes 1572896 | tf_op jit(solution)/shard_map/ppermute | solution.py:382
  80.3 1.4 total.21.refs_2_.refs_1_
  81.7 1.4 total.22.refs_3_.refs_1_
  83.1 4.1 %collective-permute-start.12 = (bf16[384,1024]{1,0:T(8,128)(2,1)S(1)}, bf16[384,1024]{1,0:T(8,128)(2,1)S(1)}, u32[]{:S(2)}, u32[]{:S(2)}) collective-permute-start(bf16[384,1024]{1,0:T(8,128)(2,1)S(1)} %total.21.refs_2_.refs_1_), channel_id=1, source_target_pairs={{0,4},{12,8},{2,6},{14,10},{1,5},{13,9},{3,7},{15,11},{16,20},{28,... | collective-permute-start | bytes 2359304 | tf_op jit(solution)/shard_map/ppermute | solution.py:389
  87.1 1.6 collective-permute-start.15
  88.7 1.3 collective-permute-start.14
  90.7 1.3 collective-permute-start.10
  92.0 13.1 %collective-permute-done.12.refs_2_ = bf16[384,1024]{1,0:T(8,128)(2,1)S(1)} collective-permute-done((bf16[384,1024]{1,0:T(8,128)(2,1)S(1)}, bf16[384,1024]{1,0:T(8,128)(2,1)S(1)}, u32[]{:S(2)}, u32[]{:S(2)}) %collective-permute-start.12) | collective-permute-done | bytes 786464 | tf_op jit(solution)/shard_map/ppermute | solution.py:389
  105.7 1.6 collective-permute-start.16
  107.3 6.8 %collective-permute-done.11.refs_1_ = bf16[768,1024]{1,0:T(8,128)(2,1)S(1)} collective-permute-done((bf16[768,1024]{1,0:T(8,128)(2,1)}, bf16[768,1024]{1,0:T(8,128)(2,1)S(1)}, u32[]{:S(2)}, u32[]{:S(2)}) %collective-permute-start.11) | collective-permute-done | bytes 1572896 | tf_op jit(solution)/shard_map/ppermute | solution.py:382
  114.0 0.8 total.25.refs_1_.refs_3_.refs_5_
  114.8 5.2 %collective-permute-start.19 = (bf16[768,1024]{1,0:T(8,128)(2,1)S(1)}, bf16[768,1024]{1,0:T(8,128)(2,1)}, u32[]{:S(2)}, u32[]{:S(2)}) collective-permute-start(bf16[768,1024]{1,0:T(8,128)(2,1)S(1)} %total.25.refs_1_.refs_3_.refs_5_), channel_id=1, source_target_pairs={{0,4},{12,8},{2,6},{14,10},{1,5},{13,9},{3,7},{15,11},{16,20},{28,... | collective-permute-start | bytes 4718600 | tf_op jit(solution)/shard_map/ppermute | solution.py:389
  120.0 0.7 total.26.refs_4_
  120.6 1.3 collective-permute-start.21
  121.9 0.7 total.27.refs_3_.refs_1_
  122.7 0.9 copy-done.5
  123.6 1.1 copy-done.6
  125.3 0.9 collective-permute-start.17
  126.3 6.8 %expand.1 = (bf16[768,1024]{1,0:T(8,128)(2,1)S(1)}, bf16[384,1024]{1,0:T(8,128)(2,1)S(1)}, bf16[384,1024]{1,0:T(8,128)(2,1)S(1)}) custom-call(s32[32]{0:T(128)S(1)} %pad_add_fusion.refs_0_, bf16[48,1024]{1,0:T(8,128)(2,1)S(1)} %total.27.refs_3_.refs_1_, bf16[48,1024]{1,0:T(8,128)(2,1)S(1)} %collective-permute-done.13.refs_2_, s32[192,1]{1,0:T(8,128)S(1)} %copy.13.refs_3_, ...), custom_call_target="tpu_custom_call" | custom-call | flops 1 | bytes 1 | tf_op jit(solution)/shard_map/expand/pallas_call | solution.py:26
  133.1 14.1 %collective-permute-done.15.refs_2_.refs_6_ = bf16[768,1024]{1,0:T(8,128)(2,1)} collective-permute-done((bf16[768,1024]{1,0:T(8,128)(2,1)S(1)}, bf16[768,1024]{1,0:T(8,128)(2,1)}, u32[]{:S(2)}, u32[]{:S(2)}) %collective-permute-start.15) | collective-permute-done | bytes 1572896 | tf_op jit(solution)/shard_map/ppermute | solution.py:382
  147.7 3.6 %total.29.refs_0_.refs_3_.refs_6_ = bf16[768,1024]{1,0:T(8,128)(2,1)S(1)} custom-call(bf16[768,1024]{1,0:T(8,128)(2,1)S(1)} %get-tuple-element.22.refs_0_.refs_4_, bf16[768,1024]{1,0:T(8,128)(2,1)S(1)} %get-tuple-element.26.refs_1_.refs_5_.refs_8_, bf16[768,1024]{1,0:T(8,128)(2,1)} %collective-permute-done.15.refs_2_.refs_6_, ...), custom_call_target="tpu_custom_call" | custom-call | flops 1 | bytes 1 | tf_op jit(solution)/shard_map/total/pallas_call | solution.py:26
  151.3 1.5 collective-permute-done.19.refs_2_.refs_5_
  152.8 3.0 %total.30.refs_0_.refs_2_ = bf16[768,1024]{1,0:T(8,128)(2,1)S(1)} custom-call(bf16[768,1024]{1,0:T(8,128)(2,1)S(1)} %total.29.refs_0_.refs_3_.refs_6_, bf16[384,1024]{1,0:T(8,128)(2,1)S(1)} %collective-permute-done.18.refs_1_, bf16[768,1024]{1,0:T(8,128)(2,1)} %collective-permute-done.19.refs_2_.refs_5_, ...), custom_call_target="tpu_custom_call" | custom-call | flops 1 | bytes 1 | tf_op jit(solution)/shard_map/total/pallas_call | solution.py:26
  155.8 0.9 collective-permute-done.21.refs_1_
  156.7 1.6 total.31
  (56 shorter events, 5.2 us)
Async XLA Ops:
  0.0 9.6 %collective-permute-start = (s32[192]{0:T(256)}, s32[192]{0:T(256)S(1)}, u32[]{:S(2)}, u32[]{:S(2)}) collective-permute-start(s32[192]{0:T(256)} %param.7), channel_id=1, source_target_pairs={{0,1},{1,0},{2,3},{3,2},{4,5},{5,4},{6,7},{7,6},{8,9},{9,8},{10,11... | collective-permute-start | bytes 2312 | tf_op jit(solution)/shard_map/ppermute | solution.py:395
  0.5 9.8 %collective-permute-start.1 = (bf16[768,1024]{1,0:T(8,128)(2,1)}, bf16[768,1024]{1,0:T(8,128)(2,1)}, u32[]{:S(2)}, u32[]{:S(2)}) collective-permute-start(bf16[768,1024]{1,0:T(8,128)(2,1)} %bitcast.6), channel_id=1, source_target_pairs={{0,1},{1,0},{2,3},{3,2},{4,5},{5,4},{6,7},{7,6},{8,9},{9,8},{10,11... | collective-permute-start | bytes 4718600 | tf_op jit(solution)/shard_map/ppermute | solution.py:395
  1.7 7.4 %copy-start.8 = (s32[192]{0:T(256)S(1)}, s32[192]{0:T(256)}, u32[]{:S(2)}) copy-start(s32[192]{0:T(256)} %param.7) | copy-start | bytes 2308
  6.1 26.4 %collective-permute-start.4 = (bf16[416,1024]{1,0:T(8,128)(2,1)}, bf16[416,1024]{1,0:T(8,128)(2,1)S(1)}, u32[]{:S(2)}, u32[]{:S(2)}) collective-permute-start(bf16[416,1024]{1,0:T(8,128)(2,1)} %products.5.refs_6_), channel_id=1, source_target_pairs={{0,2},{2,0},{4,6},{6,4},{8,10},{10,8},{12,14},{14,12},{1,3},{3,1},... | collective-permute-start | bytes 2555912 | tf_op jit(solution)/shard_map/ppermute | solution.py:382
  10.3 1.4 copy-start
  11.7 1.2 copy-start.4
  12.9 8.4 %copy-start.1 = (bf16[4,192,1024]{2,1,0:T(8,128)(2,1)S(1)}, bf16[4,192,1024]{2,1,0:T(8,128)(2,1)}, u32[]{:S(2)}) copy-start(bf16[4,192,1024]{2,1,0:T(8,128)(2,1)} %param.6) | copy-start | bytes 4718596
  12.9 8.4 %copy-start.7 = (s32[11]{0:T(128)S(1)}, s32[11]{0:T(128)}, u32[]{:S(2)}) copy-start(s32[11]{0:T(128)} %dynamic-slice_bitcast_fusion.refs_0_) | copy-start | bytes 136
  19.5 1.4 collective-permute-start.2
  24.4 22.2 %collective-permute-start.3 = (bf16[400,1024]{1,0:T(8,128)(2,1)S(1)}, bf16[400,1024]{1,0:T(8,128)(2,1)S(1)}, u32[]{:S(2)}, u32[]{:S(2)}) collective-permute-start(bf16[400,1024]{1,0:T(8,128)(2,1)S(1)} %products.6.refs_3_), channel_id=1, source_target_pairs={{0,2},{2,0},{4,6},{6,4},{8,10},{10,8},{12,14},{14,12},{1,3},{3,1},... | collective-permute-start | bytes 2457608 | tf_op jit(solution)/shard_map/ppermute | solution.py:382
  30.5 49.9 %collective-permute-start.8 = (bf16[768,1024]{1,0:T(8,128)(2,1)}, bf16[768,1024]{1,0:T(8,128)(2,1)S(1)}, u32[]{:S(2)}, u32[]{:S(2)}) collective-permute-start(bf16[768,1024]{1,0:T(8,128)(2,1)} %get-tuple-element.20.refs_2_), channel_id=1, source_target_pairs={{0,2},{2,0},{4,6},{6,4},{8,10},{10,8},{12,14},{14,12},{1,3},{3,1},... | collective-permute-start | bytes 4718600 | tf_op jit(solution)/shard_map/ppermute | solution.py:382
  34.1 27.9 %collective-permute-start.6 = (bf16[416,1024]{1,0:T(8,128)(2,1)S(1)}, bf16[416,1024]{1,0:T(8,128)(2,1)S(1)}, u32[]{:S(2)}, u32[]{:S(2)}) collective-permute-start(bf16[416,1024]{1,0:T(8,128)(2,1)S(1)} %total.17.refs_3_.refs_1_), channel_id=1, source_target_pairs={{0,4},{12,8},{2,6},{14,10},{1,5},{13,9},{3,7},{15,11},{16,20},{28,... | collective-permute-start | bytes 2555912 | tf_op jit(solution)/shard_map/ppermute | solution.py:389
  43.6 1.2 copy-start.2
  48.1 25.0 %collective-permute-start.5 = (bf16[400,1024]{1,0:T(8,128)(2,1)S(1)}, bf16[400,1024]{1,0:T(8,128)(2,1)S(1)}, u32[]{:S(2)}, u32[]{:S(2)}) collective-permute-start(bf16[400,1024]{1,0:T(8,128)(2,1)S(1)} %total.18.refs_3_.refs_1_.refs_0_), channel_id=1, source_target_pairs={{0,4},{12,8},{2,6},{14,10},{1,5},{13,9},{3,7},{15,11},{16,20},{28,... | collective-permute-start | bytes 2457608 | tf_op jit(solution)/shard_map/ppermute | solution.py:389
  52.4 61.6 %collective-permute-start.11 = (bf16[768,1024]{1,0:T(8,128)(2,1)}, bf16[768,1024]{1,0:T(8,128)(2,1)S(1)}, u32[]{:S(2)}, u32[]{:S(2)}) collective-permute-start(bf16[768,1024]{1,0:T(8,128)(2,1)} %hold.2), channel_id=1, source_target_pairs={{0,2},{2,0},{4,6},{6,4},{8,10},{10,8},{12,14},{14,12},{1,3},{3,1},... | collective-permute-start | bytes 4718600 | tf_op jit(solution)/shard_map/ppermute | solution.py:382
  62.6 17.7 %copy-start.3 = (bf16[768,1024]{1,0:T(8,128)(2,1)S(1)}, bf16[768,1024]{1,0:T(8,128)(2,1)}, u32[]{:S(2)}) copy-start(bf16[768,1024]{1,0:T(8,128)(2,1)} %copy-done.2) | copy-start | bytes 4718596
  62.6 26.1 %collective-permute-start.9 = (bf16[416,1024]{1,0:T(8,128)(2,1)S(1)}, bf16[416,1024]{1,0:T(8,128)(2,1)S(1)}, u32[]{:S(2)}, u32[]{:S(2)}) collective-permute-start(bf16[416,1024]{1,0:T(8,128)(2,1)S(1)} %total.19.refs_5_), channel_id=1, source_target_pairs={{4,8},{8,4},{6,10},{10,6},{5,9},{9,5},{7,11},{11,7},{20,24},{24,20... | collective-permute-start | bytes 2555912 | tf_op jit(solution)/shard_map/ppermute | solution.py:389
  73.7 16.3 %collective-permute-start.7 = (bf16[400,1024]{1,0:T(8,128)(2,1)S(1)}, bf16[400,1024]{1,0:T(8,128)(2,1)S(1)}, u32[]{:S(2)}, u32[]{:S(2)}) collective-permute-start(bf16[400,1024]{1,0:T(8,128)(2,1)S(1)} %total.20.refs_2_), channel_id=1, source_target_pairs={{4,8},{8,4},{6,10},{10,6},{5,9},{9,5},{7,11},{11,7},{20,24},{24,20... | collective-permute-start | bytes 2457608 | tf_op jit(solution)/shard_map/ppermute | solution.py:389
  83.1 22.0 %collective-permute-start.12 = (bf16[384,1024]{1,0:T(8,128)(2,1)S(1)}, bf16[384,1024]{1,0:T(8,128)(2,1)S(1)}, u32[]{:S(2)}, u32[]{:S(2)}) collective-permute-start(bf16[384,1024]{1,0:T(8,128)(2,1)S(1)} %total.21.refs_2_.refs_1_), channel_id=1, source_target_pairs={{0,4},{12,8},{2,6},{14,10},{1,5},{13,9},{3,7},{15,11},{16,20},{28,... | collective-permute-start | bytes 2359304 | tf_op jit(solution)/shard_map/ppermute | solution.py:389
  87.1 60.0 %collective-permute-start.15 = (bf16[768,1024]{1,0:T(8,128)(2,1)S(1)}, bf16[768,1024]{1,0:T(8,128)(2,1)}, u32[]{:S(2)}, u32[]{:S(2)}) collective-permute-start(bf16[768,1024]{1,0:T(8,128)(2,1)S(1)} %hold.3), channel_id=1, source_target_pairs={{0,2},{2,0},{4,6},{6,4},{8,10},{10,8},{12,14},{14,12},{1,3},{3,1},... | collective-permute-start | bytes 4718600 | tf_op jit(solution)/shard_map/ppermute | solution.py:382
  88.7 33.9 %collective-permute-start.14 = (bf16[384,1024]{1,0:T(8,128)(2,1)S(1)}, bf16[384,1024]{1,0:T(8,128)(2,1)S(1)}, u32[]{:S(2)}, u32[]{:S(2)}) collective-permute-start(bf16[384,1024]{1,0:T(8,128)(2,1)S(1)} %total.22.refs_3_.refs_1_), channel_id=1, source_target_pairs={{0,4},{12,8},{2,6},{14,10},{1,5},{13,9},{3,7},{15,11},{16,20},{28,... | collective-permute-start | bytes 2359304 | tf_op jit(solution)/shard_map/ppermute | solution.py:389
  90.7 29.3 %collective-permute-start.10 = (bf16[48,1024]{1,0:T(8,128)(2,1)S(1)}, bf16[48,1024]{1,0:T(8,128)(2,1)S(1)}, u32[]{:S(2)}, u32[]{:S(2)}) collective-permute-start(bf16[48,1024]{1,0:T(8,128)(2,1)S(1)} %total.23.refs_3_), channel_id=1, source_target_pairs={{8,12},{4,0},{10,14},{6,2},{9,13},{5,1},{11,15},{7,3},{24,28},{20,... | collective-permute-start | bytes 294920 | tf_op jit(solution)/shard_map/ppermute | solution.py:389
  105.7 41.5 %collective-permute-start.16 = (bf16[384,1024]{1,0:T(8,128)(2,1)S(1)}, bf16[384,1024]{1,0:T(8,128)(2,1)}, u32[]{:S(2)}, u32[]{:S(2)}) collective-permute-start(bf16[384,1024]{1,0:T(8,128)(2,1)S(1)} %total.24.refs_2_), channel_id=1, source_target_pairs={{4,8},{8,4},{6,10},{10,6},{5,9},{9,5},{7,11},{11,7},{20,24},{24,20... | collective-permute-start | bytes 2359304 | tf_op jit(solution)/shard_map/ppermute | solution.py:389
  114.8 38.0 %collective-permute-start.19 = (bf16[768,1024]{1,0:T(8,128)(2,1)S(1)}, bf16[768,1024]{1,0:T(8,128)(2,1)}, u32[]{:S(2)}, u32[]{:S(2)}) collective-permute-start(bf16[768,1024]{1,0:T(8,128)(2,1)S(1)} %total.25.refs_1_.refs_3_.refs_5_), channel_id=1, source_target_pairs={{0,4},{12,8},{2,6},{14,10},{1,5},{13,9},{3,7},{15,11},{16,20},{28,... | collective-permute-start | bytes 4718600 | tf_op jit(solution)/shard_map/ppermute | solution.py:389
  120.6 36.1 %collective-permute-start.21 = (bf16[768,1024]{1,0:T(8,128)(2,1)S(1)}, bf16[768,1024]{1,0:T(8,128)(2,1)S(1)}, u32[]{:S(2)}, u32[]{:S(2)}) collective-permute-start(bf16[768,1024]{1,0:T(8,128)(2,1)S(1)} %total.26.refs_4_), channel_id=1, source_target_pairs={{8,12},{4,0},{10,14},{6,2},{9,13},{5,1},{11,15},{7,3},{24,28},{20,... | collective-permute-start | bytes 4718600 | tf_op jit(solution)/shard_map/ppermute | solution.py:389
  122.7 0.9 copy-start.5
  123.6 1.7 %collective-permute-start.13 = (bf16[48,1024]{1,0:T(8,128)(2,1)S(1)}, bf16[48,1024]{1,0:T(8,128)(2,1)S(1)}, u32[]{:S(2)}, u32[]{:S(2)}) collective-permute-start(bf16[48,1024]{1,0:T(8,128)(2,1)S(1)} %total.27.refs_3_.refs_1_), channel_id=1, source_target_pairs={{0,1},{1,0},{2,3},{3,2},{4,5},{5,4},{6,7},{7,6},{8,9},{9,8},{10,11... | collective-permute-start | bytes 294920 | tf_op jit(solution)/shard_map/ppermute | solution.py:395
  123.6 1.1 copy-start.6
  125.3 22.4 %collective-permute-start.17 = (bf16[384,1024]{1,0:T(8,128)(2,1)S(1)}, bf16[384,1024]{1,0:T(8,128)(2,1)S(1)}, u32[]{:S(2)}, u32[]{:S(2)}) collective-permute-start(bf16[384,1024]{1,0:T(8,128)(2,1)S(1)} %total.28.refs_6_), channel_id=1, source_target_pairs={{4,8},{8,4},{6,10},{10,6},{5,9},{9,5},{7,11},{11,7},{20,24},{24,20... | collective-permute-start | bytes 2359304 | tf_op jit(solution)/shard_map/ppermute | solution.py:389
  147.2 4.1 %collective-permute-start.18 = (bf16[384,1024]{1,0:T(8,128)(2,1)S(1)}, bf16[384,1024]{1,0:T(8,128)(2,1)S(1)}, u32[]{:S(2)}, u32[]{:S(2)}) collective-permute-start(bf16[384,1024]{1,0:T(8,128)(2,1)S(1)} %get-tuple-element.27), channel_id=1, source_target_pairs={{0,1},{1,0},{2,3},{3,2},{4,5},{5,4},{6,7},{7,6},{8,9},{9,8},{10,11... | collective-permute-start | bytes 2359304 | tf_op jit(solution)/shard_map/ppermute | solution.py:395
  147.2 4.1 %collective-permute-start.20 = (bf16[384,1024]{1,0:T(8,128)(2,1)S(1)}, bf16[384,1024]{1,0:T(8,128)(2,1)S(1)}, u32[]{:S(2)}, u32[]{:S(2)}) collective-permute-start(bf16[384,1024]{1,0:T(8,128)(2,1)S(1)} %get-tuple-element.28), channel_id=1, source_target_pairs={{0,1},{1,0},{2,3},{3,2},{4,5},{5,4},{6,7},{7,6},{8,9},{9,8},{10,11... | collective-permute-start | bytes 2359304 | tf_op jit(solution)/shard_map/ppermute | solution.py:395

commit v19 on v18

--- a/solution.py
+++ b/solution.py
@@ -293,7 +293,7 @@
     )
 
 
-def expand(low_sets, slot_sets, maps, index, after=()):
+def expand(low_sets, slot_sets, maps, index, base, after=()):
     sets = len(slot_sets)
     rank, width = maps.shape[1:]
     tall = low_sets[0].shape[0]
@@ -308,8 +308,8 @@
 
     def kernel(index_ref, *refs):
         low_refs, refs = refs[:sets], refs[sets:]
-        slot_refs, maps_ref, out_refs = refs[:sets], refs[sets], refs[sets + 1 : sets + 1 + len(outs)]
-        stage, maps_buf, map_sems, out_sems = refs[sets + 1 + len(outs) :]
+        slot_refs, maps_ref, base_ref, *refs = refs[:sets], refs[sets], refs[sets + 1], *refs[sets + 2 :]
+        out_refs, (stage, maps_buf, map_sems, out_sems) = refs[: len(outs)], refs[len(outs) :]
         map_copies = block_copies(index_ref, maps_ref, maps_buf, map_sems, sets, rank)
         writes = [
             pltpu.make_async_copy(stage.at[s, pl.ds(first, some)], out_refs[o], out_sems.at[o])
@@ -333,6 +333,8 @@
                 value = jnp.dot(
                     picked, maps_buf[s * span : (s + 1) * span, at : at + CHUNK], preferred_element_type=jnp.float32
                 )
+                if s == 0:
+                    value += base_ref[:, at : at + CHUNK].astype(jnp.float32)
                 stage[s, :, at : at + CHUNK] = value.astype(stage.dtype)
             for o, (which, _, _) in enumerate(outs):
                 if which == s:
@@ -341,8 +343,8 @@
             write.wait()
 
     return call(
-        kernel, [index, *low_sets, *slot_sets, maps], after, prefetch=1,
-        in_specs=[pl.BlockSpec(memory_space=pltpu.VMEM)] * (2 * sets) + [ANY],
+        kernel, [index, *low_sets, *slot_sets, maps, base], after, prefetch=1,
+        in_specs=[pl.BlockSpec(memory_space=pltpu.VMEM)] * (2 * sets) + [ANY, pl.BlockSpec(memory_space=pltpu.VMEM)],
         out_specs=[ANY] * len(outs),
         out_shape=[jax.ShapeDtypeStruct((some, width), jnp.bfloat16) for _, _, some in outs],
         scratch=[
@@ -546,7 +548,7 @@
             low_sum = then(total, [(low_rows, pieces)])
             low_back = [low_sum] + [pass_on(low_sum, shift) for shift in range(1, owners)]
         if deltas is None and low_sum is not None and EXPAND_AFTER in arrived:
-            deltas = then(expand, low_back, slot_sets, adapter_up_maps, names)
+            deltas = then(expand, low_back, slot_sets, adapter_up_maps, names, own_all[nz - 1])
             back = [
                 [(*cut, pass_on(deltas[1 + (shift - 1) * PARTS + p], -shift), 0) for p, cut in enumerate(even)]
                 for shift in range(1, owners)
@@ -554,7 +556,7 @@
     span = (0, count)
     early = [arrived_parts(h, nz - 2 - h) for h in range(1, nz - 2)]
     late = [arrived_parts(h, nz - 2 - h) for h in range(nz - 1) if not 1 <= h < nz - 2]
-    most = add_up(span, [whole(own_all[nz - 1]), whole(deltas[0]), y_parts(nz - 1)] + early)
+    most = add_up(span, [whole(deltas[0]), y_parts(nz - 1)] + early)
     most = add_up(span, [whole(most)] + back + late[:-1])
     out = add_up(span, [whole(most)] + late[-1:])
     return out.reshape(steps, row_count, out_width)

time: 159 us -> 160 us (level)
  waiting for transfers between devices: 54.9 us -> 51.4 us
  local copies, waits for them, and re-layouts: 7.17 us -> 9.11 us
    ppermute x11, waiting for transfers between devices: 25.1 us -> 20.8 us  [hop(): return lax.ppermute(value, 'tensor', pairs)]
    unnamed x18, local copies, waits for them, and re-layouts: 5.73 us -> 7.68 us
  transfers between devices with their start and end apart: 22 -> 22, of which waited for: 9 -> 10; matrix products, arithmetic and copies ran while one was open for 1% -> 1% of each run, Pallas kernels for 37% -> 38%
where the time goes in v19:
time: 160 us; the launch traced here: 159 us
  Pallas kernels  61.3 us (38%)
  waiting for transfers between devices  51.4 us (32%)
  starting transfers between devices  35.6 us (22%)
  local copies, waits for them, and re-layouts  9.11 us (6%)
    pallas_call x25, Pallas kernels, call(): pl.pallas_call(body, grid_spec=pltpu.PrefetchScalarGridSpec(num_scalar_pr...  61.3 us
    ppermute x5, waiting for transfers between devices, swap_y(): return lax.ppermute(value, 'tensor', [(t, t ^ 1) for t in range(n)])  28.6 us
    ppermute x11, starting transfers between devices, hop(): return lax.ppermute(value, 'tensor', pairs)  26.1 us
    ppermute x11, waiting for transfers between devices, hop(): return lax.ppermute(value, 'tensor', pairs)  20.8 us
    ppermute x5, starting transfers between devices, swap_y(): return lax.ppermute(value, 'tensor', [(t, t ^ 1) for t in range(n)])  8.35 us
    unnamed x18, local copies, waits for them, and re-layouts  7.68 us
  transfers between devices with their start and end apart: 22, of which 10 were waited for; matrix products, arithmetic and copies ran while one was open for 1% of the time, Pallas kernels for 38%

profile of v19, /device:TPU:0, one launch (start us, length us, event | category | flops | bytes accessed | tf_op | source)
XLA Modules:
  0.0 159.0 jit_solution(3800518917148238190)
XLA Ops:
  0.5 1.2 dynamic-slice_bitcast_fusion.refs_0_
  1.7 4.3 %products.5.refs_6_ = bf16[416,1024]{1,0:T(8,128)(2,1)} custom-call(s32[11]{0:T(128)} %dynamic-slice_bitcast_fusion.refs_0_, bf16[768,1024]{1,0:T(8,128)(2,1)} %bitcast.7, bf16[1024,8192]{1,0:T(8,128)(2,1)} %refs_2_.9), custom_call_target="tpu_custom_call" | custom-call | flops 1 | bytes 1 | tf_op jit(solution)/shard_map/products/pallas_call | solution.py:26
  6.1 3.0 %collective-permute-start.4 = (bf16[416,1024]{1,0:T(8,128)(2,1)}, bf16[416,1024]{1,0:T(8,128)(2,1)S(1)}, u32[]{:S(2)}, u32[]{:S(2)}) collective-permute-start(bf16[416,1024]{1,0:T(8,128)(2,1)} %products.5.refs_6_), channel_id=1, source_target_pairs={{0,2},{2,0},{4,6},{6,4},{8,10},{10,8},{12,14},{14,12},{1,3},{3,1},... | collective-permute-start | bytes 2555912 | tf_op jit(solution)/shard_map/ppermute | solution.py:384
  10.3 1.4 copy-done
  11.7 1.2 copy-done.2
  12.9 6.6 %low_rank.1 = (bf16[48,1024]{1,0:T(8,128)(2,1)S(1)}, bf16[48,1024]{1,0:T(8,128)(2,1)S(1)}) custom-call(s32[32]{0:T(128)S(1)} %pad_add_fusion.refs_0_, bf16[768,1024]{1,0:T(8,128)(2,1)S(1)} %bitcast.8, bf16[768,1024]{1,0:T(8,128)(2,1)} %collective-permute-done.1.refs_2_, s32[192,1]{1,0:T(8,128)S(1)} %copy.13.refs_3_, s32[192,1]{1,0:T(8,128)S(1)} %copy.14.refs_4_, ...), custom_call_target="tpu_custom_call" | custom-call | flops 1 | bytes 1 | tf_op jit(solution)/shard_map/low_rank/pallas_call | solution.py:26
  19.5 1.3 collective-permute-done.2.refs_1_
  21.3 3.1 %products.6.refs_3_ = bf16[400,1024]{1,0:T(8,128)(2,1)S(1)} custom-call(s32[11]{0:T(128)S(1)} %copy-done.7, bf16[768,1024]{1,0:T(8,128)(2,1)S(1)} %bitcast.9, bf16[1024,8192]{1,0:T(8,128)(2,1)} %refs_2_.9, bf16[48,1024]{1,0:T(8,128)(2,1)S(1)} %total.16.refs_3_.refs_4_.refs_2_, bf16[48,1024]{1,0:T(8,128)(2,1)S(1)} %total.16.refs_3_.refs_4_.refs_2_), custom_call_target="tpu_custom_call" | custom-call | flops 1 | bytes 1 | tf_op jit(solution)/shard_map/products/pallas_call | solution.py:26
  24.5 6.0 %products.7 = (bf16[768,1024]{1,0:T(8,128)(2,1)}, bf16[768,1024]{1,0:T(8,128)(2,1)S(1)}) custom-call(s32[11]{0:T(128)S(1)} %copy-done.7, bf16[768,1024]{1,0:T(8,128)(2,1)S(1)} %bitcast.10, bf16[1024,8192]{1,0:T(8,128)(2,1)} %refs_2_.9, bf16[400,1024]{1,0:T(8,128)(2,1)S(1)} %products.6.refs_3_), custom_call_target="tpu_custom_call" | custom-call | flops 1 | bytes 1 | tf_op jit(solution)/shard_map/products/pallas_call | solution.py:26
  30.5 2.1 %collective-permute-start.8 = (bf16[768,1024]{1,0:T(8,128)(2,1)}, bf16[768,1024]{1,0:T(8,128)(2,1)S(1)}, u32[]{:S(2)}, u32[]{:S(2)}) collective-permute-start(bf16[768,1024]{1,0:T(8,128)(2,1)} %get-tuple-element.20.refs_2_), channel_id=1, source_target_pairs={{0,2},{2,0},{4,6},{6,4},{8,10},{10,8},{12,14},{14,12},{1,3},{3,1},... | collective-permute-start | bytes 4718600 | tf_op jit(solution)/shard_map/ppermute | solution.py:384
  32.5 1.6 %total.17.refs_3_.refs_1_ = bf16[416,1024]{1,0:T(8,128)(2,1)S(1)} custom-call(bf16[768,1024]{1,0:T(8,128)(2,1)S(1)} %get-tuple-element.19.refs_0_, bf16[416,1024]{1,0:T(8,128)(2,1)S(1)} %collective-permute-done.4.refs_1_, bf16[768,1024]{1,0:T(8,128)(2,1)} %get-tuple-element.20.refs_2_), custom_call_target="tpu_custom_call" | custom-call | flops 1 | bytes 1 | tf_op jit(solution)/shard_map/total/pallas_call | solution.py:26
  34.2 3.5 %collective-permute-start.6 = (bf16[416,1024]{1,0:T(8,128)(2,1)S(1)}, bf16[416,1024]{1,0:T(8,128)(2,1)S(1)}, u32[]{:S(2)}, u32[]{:S(2)}) collective-permute-start(bf16[416,1024]{1,0:T(8,128)(2,1)S(1)} %total.17.refs_3_.refs_1_), channel_id=1, source_target_pairs={{0,4},{12,8},{2,6},{14,10},{1,5},{13,9},{3,7},{15,11},{16,20},{28,... | collective-permute-start | bytes 2555912 | tf_op jit(solution)/shard_map/ppermute | solution.py:391
  37.7 6.1 %products.8 = (bf16[768,1024]{1,0:T(8,128)(2,1)S(1)}, bf16[768,1024]{1,0:T(8,128)(2,1)S(1)}) custom-call(s32[11]{0:T(128)S(1)} %copy-done.7, bf16[768,1024]{1,0:T(8,128)(2,1)S(1)} %bitcast.11, bf16[1024,8192]{1,0:T(8,128)(2,1)} %refs_2_.9, bf16[416,1024]{1,0:T(8,128)(2,1)S(1)} %total.17.refs_3_.refs_1_), custom_call_target="tpu_custom_call" | custom-call | flops 1 | bytes 1 | tf_op jit(solution)/shard_map/products/pallas_call | solution.py:26
  43.8 2.8 %collective-permute-done.3.refs_1_.refs_3_ = bf16[400,1024]{1,0:T(8,128)(2,1)S(1)} collective-permute-done((bf16[400,1024]{1,0:T(8,128)(2,1)S(1)}, bf16[400,1024]{1,0:T(8,128)(2,1)S(1)}, u32[]{:S(2)}, u32[]{:S(2)}) %collective-permute-start.3) | collective-permute-done | bytes 819232 | tf_op jit(solution)/shard_map/ppermute | solution.py:384
  46.6 1.5 total.18.refs_3_.refs_1_.refs_0_
  48.1 4.3 %collective-permute-start.5 = (bf16[400,1024]{1,0:T(8,128)(2,1)S(1)}, bf16[400,1024]{1,0:T(8,128)(2,1)S(1)}, u32[]{:S(2)}, u32[]{:S(2)}) collective-permute-start(bf16[400,1024]{1,0:T(8,128)(2,1)S(1)} %total.18.refs_3_.refs_1_.refs_0_), channel_id=1, source_target_pairs={{0,4},{12,8},{2,6},{14,10},{1,5},{13,9},{3,7},{15,11},{16,20},{28,... | collective-permute-start | bytes 2457608 | tf_op jit(solution)/shard_map/ppermute | solution.py:391
  52.4 1.6 collective-permute-start.11
  54.0 8.0 %products.9 = (bf16[768,1024]{1,0:T(8,128)(2,1)S(1)}, bf16[768,1024]{1,0:T(8,128)(2,1)S(1)}, bf16[768,1024]{1,0:T(8,128)(2,1)S(1)}) custom-call(s32[11]{0:T(128)S(1)} %copy-done.7, bf16[768,1024]{1,0:T(8,128)(2,1)S(1)} %bitcast.12, bf16[1024,8192]{1,0:T(8,128)(2,1)} %refs_2_.9, bf16[400,1024]{1,0:T(8,128)(2,1)S(1)} %total.18.refs_3_.refs_1_.refs_0_), custom_call_target="tpu_custom_call" | custom-call | flops 1 | bytes 1 | tf_op jit(solution)/shard_map/products/pallas_call | solution.py:26
  62.0 1.1 copy-done.3
  63.2 1.2 copy-done.5
  64.9 0.7 collective-permute-start.9
  65.6 7.5 %collective-permute-done.5.refs_2_.refs_4_.refs_1_ = bf16[400,1024]{1,0:T(8,128)(2,1)S(1)} collective-permute-done((bf16[400,1024]{1,0:T(8,128)(2,1)S(1)}, bf16[400,1024]{1,0:T(8,128)(2,1)S(1)}, u32[]{:S(2)}, u32[]{:S(2)}) %collective-permute-start.5) | collective-permute-done | bytes 819232 | tf_op jit(solution)/shard_map/ppermute | solution.py:391
  73.8 0.7 collective-permute-start.7
  74.5 5.8 %collective-permute-done.8.refs_1_ = bf16[768,1024]{1,0:T(8,128)(2,1)S(1)} collective-permute-done((bf16[768,1024]{1,0:T(8,128)(2,1)}, bf16[768,1024]{1,0:T(8,128)(2,1)S(1)}, u32[]{:S(2)}, u32[]{:S(2)}) %collective-permute-start.8) | collective-permute-done | bytes 1572896 | tf_op jit(solution)/shard_map/ppermute | solution.py:384
  80.3 1.4 total.21.refs_2_.refs_1_
  81.7 1.4 total.22.refs_3_.refs_1_
  83.1 4.1 %collective-permute-start.12 = (bf16[384,1024]{1,0:T(8,128)(2,1)S(1)}, bf16[384,1024]{1,0:T(8,128)(2,1)S(1)}, u32[]{:S(2)}, u32[]{:S(2)}) collective-permute-start(bf16[384,1024]{1,0:T(8,128)(2,1)S(1)} %total.21.refs_2_.refs_1_), channel_id=1, source_target_pairs={{0,4},{12,8},{2,6},{14,10},{1,5},{13,9},{3,7},{15,11},{16,20},{28,... | collective-permute-start | bytes 2359304 | tf_op jit(solution)/shard_map/ppermute | solution.py:391
  87.1 1.6 collective-permute-start.15
  88.7 3.7 %collective-permute-start.14 = (bf16[384,1024]{1,0:T(8,128)(2,1)S(1)}, bf16[384,1024]{1,0:T(8,128)(2,1)}, u32[]{:S(2)}, u32[]{:S(2)}) collective-permute-start(bf16[384,1024]{1,0:T(8,128)(2,1)S(1)} %total.22.refs_3_.refs_1_), channel_id=1, source_target_pairs={{0,4},{12,8},{2,6},{14,10},{1,5},{13,9},{3,7},{15,11},{16,20},{28,... | collective-permute-start | bytes 2359304 | tf_op jit(solution)/shard_map/ppermute | solution.py:391
  93.0 1.3 collective-permute-start.10
  94.3 10.8 %collective-permute-done.12.refs_2_ = bf16[384,1024]{1,0:T(8,128)(2,1)S(1)} collective-permute-done((bf16[384,1024]{1,0:T(8,128)(2,1)S(1)}, bf16[384,1024]{1,0:T(8,128)(2,1)S(1)}, u32[]{:S(2)}, u32[]{:S(2)}) %collective-permute-start.12) | collective-permute-done | bytes 786464 | tf_op jit(solution)/shard_map/ppermute | solution.py:391
  105.7 1.6 collective-permute-start.16
  107.2 6.8 %collective-permute-done.11.refs_1_ = bf16[768,1024]{1,0:T(8,128)(2,1)S(1)} collective-permute-done((bf16[768,1024]{1,0:T(8,128)(2,1)S(1)}, bf16[768,1024]{1,0:T(8,128)(2,1)S(1)}, u32[]{:S(2)}, u32[]{:S(2)}) %collective-permute-start.11) | collective-permute-done | bytes 1572896 | tf_op jit(solution)/shard_map/ppermute | solution.py:384
  114.0 1.4 copy-done.4
  115.4 0.8 total.25.refs_1_.refs_3_.refs_5_
  116.2 4.1 %collective-permute-start.19 = (bf16[768,1024]{1,0:T(8,128)(2,1)S(1)}, bf16[768,1024]{1,0:T(8,128)(2,1)S(1)}, u32[]{:S(2)}, u32[]{:S(2)}) collective-permute-start(bf16[768,1024]{1,0:T(8,128)(2,1)S(1)} %total.25.refs_1_.refs_3_.refs_5_), channel_id=1, source_target_pairs={{0,4},{12,8},{2,6},{14,10},{1,5},{13,9},{3,7},{15,11},{16,20},{28,... | collective-permute-start | bytes 4718600 | tf_op jit(solution)/shard_map/ppermute | solution.py:391
  121.0 1.3 collective-permute-start.21
  122.3 0.7 total.27.refs_3_.refs_1_
  123.7 0.7 collective-permute-done.13.refs_2_
  124.4 0.9 collective-permute-start.17
  125.4 1.4 copy-done.6
  126.8 7.1 %expand.1 = (bf16[768,1024]{1,0:T(8,128)(2,1)S(1)}, bf16[384,1024]{1,0:T(8,128)(2,1)S(1)}, bf16[384,1024]{1,0:T(8,128)(2,1)S(1)}) custom-call(s32[32]{0:T(128)S(1)} %pad_add_fusion.refs_0_, bf16[48,1024]{1,0:T(8,128)(2,1)S(1)} %total.27.refs_3_.refs_1_, bf16[48,1024]{1,0:T(8,128)(2,1)S(1)} %collective-permute-done.13.refs_2_, s32[192,1]{1,0:T(8,128)S(1)} %copy.13.refs_3_, ...), custom_call_target="tpu_custom_call" | custom-call | flops 1 | bytes 1 | tf_op jit(solution)/shard_map/expand/pallas_call | solution.py:26
  133.9 13.2 %collective-permute-done.15.refs_1_.refs_4_ = bf16[768,1024]{1,0:T(8,128)(2,1)S(1)} collective-permute-done((bf16[768,1024]{1,0:T(8,128)(2,1)S(1)}, bf16[768,1024]{1,0:T(8,128)(2,1)S(1)}, u32[]{:S(2)}, u32[]{:S(2)}) %collective-permute-start.15) | collective-permute-done | bytes 1572896 | tf_op jit(solution)/shard_map/ppermute | solution.py:384
  147.6 3.3 %total.29.refs_0_.refs_3_.refs_6_ = bf16[768,1024]{1,0:T(8,128)(2,1)S(1)} custom-call(bf16[768,1024]{1,0:T(8,128)(2,1)S(1)} %get-tuple-element.26.refs_0_.refs_3_.refs_6_, bf16[768,1024]{1,0:T(8,128)(2,1)S(1)} %collective-permute-done.15.refs_1_.refs_4_, bf16[384,1024]{1,0:T(8,128)(2,1)} %collective-permute-done.16.refs_2_, ...), custom_call_target="tpu_custom_call" | custom-call | flops 1 | bytes 1 | tf_op jit(solution)/shard_map/total/pallas_call | solution.py:26
  151.0 1.8 %collective-permute-done.19.refs_2_.refs_5_ = bf16[768,1024]{1,0:T(8,128)(2,1)S(1)} collective-permute-done((bf16[768,1024]{1,0:T(8,128)(2,1)S(1)}, bf16[768,1024]{1,0:T(8,128)(2,1)S(1)}, u32[]{:S(2)}, u32[]{:S(2)}) %collective-permute-start.19) | collective-permute-done | bytes 1572896 | tf_op jit(solution)/shard_map/ppermute | solution.py:391
  152.8 3.7 %total.30.refs_0_.refs_2_ = bf16[768,1024]{1,0:T(8,128)(2,1)S(1)} custom-call(bf16[768,1024]{1,0:T(8,128)(2,1)S(1)} %total.29.refs_0_.refs_3_.refs_6_, bf16[384,1024]{1,0:T(8,128)(2,1)S(1)} %collective-permute-done.18.refs_1_, bf16[768,1024]{1,0:T(8,128)(2,1)S(1)} %collective-permute-done.19.refs_2_.refs_5_, ...), custom_call_target="tpu_custom_call" | custom-call | flops 1 | bytes 1 | tf_op jit(solution)/shard_map/total/pallas_call | solution.py:26
  156.5 0.7 collective-permute-done.21.refs_1_
  157.2 1.6 total.31
  (56 shorter events, 6.5 us)
Async XLA Ops:
  0.0 9.6 %collective-permute-start = (s32[192]{0:T(256)}, s32[192]{0:T(256)S(1)}, u32[]{:S(2)}, u32[]{:S(2)}) collective-permute-start(s32[192]{0:T(256)} %param.7), channel_id=1, source_target_pairs={{0,1},{1,0},{2,3},{3,2},{4,5},{5,4},{6,7},{7,6},{8,9},{9,8},{10,11... | collective-permute-start | bytes 2312 | tf_op jit(solution)/shard_map/ppermute | solution.py:397
  0.5 9.8 %collective-permute-start.1 = (bf16[768,1024]{1,0:T(8,128)(2,1)}, bf16[768,1024]{1,0:T(8,128)(2,1)}, u32[]{:S(2)}, u32[]{:S(2)}) collective-permute-start(bf16[768,1024]{1,0:T(8,128)(2,1)} %bitcast.6), channel_id=1, source_target_pairs={{0,1},{1,0},{2,3},{3,2},{4,5},{5,4},{6,7},{7,6},{8,9},{9,8},{10,11... | collective-permute-start | bytes 4718600 | tf_op jit(solution)/shard_map/ppermute | solution.py:397
  1.7 7.4 %copy-start.8 = (s32[192]{0:T(256)S(1)}, s32[192]{0:T(256)}, u32[]{:S(2)}) copy-start(s32[192]{0:T(256)} %param.7) | copy-start | bytes 2308
  6.1 26.5 %collective-permute-start.4 = (bf16[416,1024]{1,0:T(8,128)(2,1)}, bf16[416,1024]{1,0:T(8,128)(2,1)S(1)}, u32[]{:S(2)}, u32[]{:S(2)}) collective-permute-start(bf16[416,1024]{1,0:T(8,128)(2,1)} %products.5.refs_6_), channel_id=1, source_target_pairs={{0,2},{2,0},{4,6},{6,4},{8,10},{10,8},{12,14},{14,12},{1,3},{3,1},... | collective-permute-start | bytes 2555912 | tf_op jit(solution)/shard_map/ppermute | solution.py:384
  10.3 1.4 copy-start
  11.7 1.2 copy-start.2
  12.9 8.4 %copy-start.1 = (bf16[4,192,1024]{2,1,0:T(8,128)(2,1)S(1)}, bf16[4,192,1024]{2,1,0:T(8,128)(2,1)}, u32[]{:S(2)}) copy-start(bf16[4,192,1024]{2,1,0:T(8,128)(2,1)} %param.6) | copy-start | bytes 4718596
  12.9 8.4 %copy-start.7 = (s32[11]{0:T(128)S(1)}, s32[11]{0:T(128)}, u32[]{:S(2)}) copy-start(s32[11]{0:T(128)} %dynamic-slice_bitcast_fusion.refs_0_) | copy-start | bytes 136
  19.5 1.4 collective-permute-start.2
  24.4 22.2 %collective-permute-start.3 = (bf16[400,1024]{1,0:T(8,128)(2,1)S(1)}, bf16[400,1024]{1,0:T(8,128)(2,1)S(1)}, u32[]{:S(2)}, u32[]{:S(2)}) collective-permute-start(bf16[400,1024]{1,0:T(8,128)(2,1)S(1)} %products.6.refs_3_), channel_id=1, source_target_pairs={{0,2},{2,0},{4,6},{6,4},{8,10},{10,8},{12,14},{14,12},{1,3},{3,1},... | collective-permute-start | bytes 2457608 | tf_op jit(solution)/shard_map/ppermute | solution.py:384
  30.5 49.9 %collective-permute-start.8 = (bf16[768,1024]{1,0:T(8,128)(2,1)}, bf16[768,1024]{1,0:T(8,128)(2,1)S(1)}, u32[]{:S(2)}, u32[]{:S(2)}) collective-permute-start(bf16[768,1024]{1,0:T(8,128)(2,1)} %get-tuple-element.20.refs_2_), channel_id=1, source_target_pairs={{0,2},{2,0},{4,6},{6,4},{8,10},{10,8},{12,14},{14,12},{1,3},{3,1},... | collective-permute-start | bytes 4718600 | tf_op jit(solution)/shard_map/ppermute | solution.py:384
  34.2 30.2 %collective-permute-start.6 = (bf16[416,1024]{1,0:T(8,128)(2,1)S(1)}, bf16[416,1024]{1,0:T(8,128)(2,1)S(1)}, u32[]{:S(2)}, u32[]{:S(2)}) collective-permute-start(bf16[416,1024]{1,0:T(8,128)(2,1)S(1)} %total.17.refs_3_.refs_1_), channel_id=1, source_target_pairs={{0,4},{12,8},{2,6},{14,10},{1,5},{13,9},{3,7},{15,11},{16,20},{28,... | collective-permute-start | bytes 2555912 | tf_op jit(solution)/shard_map/ppermute | solution.py:391
  48.1 25.0 %collective-permute-start.5 = (bf16[400,1024]{1,0:T(8,128)(2,1)S(1)}, bf16[400,1024]{1,0:T(8,128)(2,1)S(1)}, u32[]{:S(2)}, u32[]{:S(2)}) collective-permute-start(bf16[400,1024]{1,0:T(8,128)(2,1)S(1)} %total.18.refs_3_.refs_1_.refs_0_), channel_id=1, source_target_pairs={{0,4},{12,8},{2,6},{14,10},{1,5},{13,9},{3,7},{15,11},{16,20},{28,... | collective-permute-start | bytes 2457608 | tf_op jit(solution)/shard_map/ppermute | solution.py:391
  52.4 61.6 %collective-permute-start.11 = (bf16[768,1024]{1,0:T(8,128)(2,1)S(1)}, bf16[768,1024]{1,0:T(8,128)(2,1)S(1)}, u32[]{:S(2)}, u32[]{:S(2)}) collective-permute-start(bf16[768,1024]{1,0:T(8,128)(2,1)S(1)} %hold.2), channel_id=1, source_target_pairs={{0,2},{2,0},{4,6},{6,4},{8,10},{10,8},{12,14},{14,12},{1,3},{3,1},... | collective-permute-start | bytes 4718600 | tf_op jit(solution)/shard_map/ppermute | solution.py:384
  62.0 1.1 copy-start.3
  63.1 1.2 copy-start.5
  64.9 23.8 %collective-permute-start.9 = (bf16[416,1024]{1,0:T(8,128)(2,1)S(1)}, bf16[416,1024]{1,0:T(8,128)(2,1)S(1)}, u32[]{:S(2)}, u32[]{:S(2)}) collective-permute-start(bf16[416,1024]{1,0:T(8,128)(2,1)S(1)} %total.19.refs_5_), channel_id=1, source_target_pairs={{4,8},{8,4},{6,10},{10,6},{5,9},{9,5},{7,11},{11,7},{20,24},{24,20... | collective-permute-start | bytes 2555912 | tf_op jit(solution)/shard_map/ppermute | solution.py:391
  73.8 18.6 %collective-permute-start.7 = (bf16[400,1024]{1,0:T(8,128)(2,1)S(1)}, bf16[400,1024]{1,0:T(8,128)(2,1)S(1)}, u32[]{:S(2)}, u32[]{:S(2)}) collective-permute-start(bf16[400,1024]{1,0:T(8,128)(2,1)S(1)} %total.20.refs_2_), channel_id=1, source_target_pairs={{4,8},{8,4},{6,10},{10,6},{5,9},{9,5},{7,11},{11,7},{20,24},{24,20... | collective-permute-start | bytes 2457608 | tf_op jit(solution)/shard_map/ppermute | solution.py:391
  83.1 22.0 %collective-permute-start.12 = (bf16[384,1024]{1,0:T(8,128)(2,1)S(1)}, bf16[384,1024]{1,0:T(8,128)(2,1)S(1)}, u32[]{:S(2)}, u32[]{:S(2)}) collective-permute-start(bf16[384,1024]{1,0:T(8,128)(2,1)S(1)} %total.21.refs_2_.refs_1_), channel_id=1, source_target_pairs={{0,4},{12,8},{2,6},{14,10},{1,5},{13,9},{3,7},{15,11},{16,20},{28,... | collective-permute-start | bytes 2359304 | tf_op jit(solution)/shard_map/ppermute | solution.py:391
  87.1 59.9 %collective-permute-start.15 = (bf16[768,1024]{1,0:T(8,128)(2,1)S(1)}, bf16[768,1024]{1,0:T(8,128)(2,1)S(1)}, u32[]{:S(2)}, u32[]{:S(2)}) collective-permute-start(bf16[768,1024]{1,0:T(8,128)(2,1)S(1)} %hold.3), channel_id=1, source_target_pairs={{0,2},{2,0},{4,6},{6,4},{8,10},{10,8},{12,14},{14,12},{1,3},{3,1},... | collective-permute-start | bytes 4718600 | tf_op jit(solution)/shard_map/ppermute | solution.py:384
  88.7 34.3 %collective-permute-start.14 = (bf16[384,1024]{1,0:T(8,128)(2,1)S(1)}, bf16[384,1024]{1,0:T(8,128)(2,1)}, u32[]{:S(2)}, u32[]{:S(2)}) collective-permute-start(bf16[384,1024]{1,0:T(8,128)(2,1)S(1)} %total.22.refs_3_.refs_1_), channel_id=1, source_target_pairs={{0,4},{12,8},{2,6},{14,10},{1,5},{13,9},{3,7},{15,11},{16,20},{28,... | collective-permute-start | bytes 2359304 | tf_op jit(solution)/shard_map/ppermute | solution.py:391
  93.0 27.3 %collective-permute-start.10 = (bf16[48,1024]{1,0:T(8,128)(2,1)S(1)}, bf16[48,1024]{1,0:T(8,128)(2,1)S(1)}, u32[]{:S(2)}, u32[]{:S(2)}) collective-permute-start(bf16[48,1024]{1,0:T(8,128)(2,1)S(1)} %total.23.refs_3_), channel_id=1, source_target_pairs={{8,12},{4,0},{10,14},{6,2},{9,13},{5,1},{11,15},{7,3},{24,28},{20,... | collective-permute-start | bytes 294920 | tf_op jit(solution)/shard_map/ppermute | solution.py:391
  105.7 41.4 %collective-permute-start.16 = (bf16[384,1024]{1,0:T(8,128)(2,1)S(1)}, bf16[384,1024]{1,0:T(8,128)(2,1)}, u32[]{:S(2)}, u32[]{:S(2)}) collective-permute-start(bf16[384,1024]{1,0:T(8,128)(2,1)S(1)} %total.24.refs_2_), channel_id=1, source_target_pairs={{4,8},{8,4},{6,10},{10,6},{5,9},{9,5},{7,11},{11,7},{20,24},{24,20... | collective-permute-start | bytes 2359304 | tf_op jit(solution)/shard_map/ppermute | solution.py:391
  114.0 1.4 copy-start.4
  116.2 36.6 %collective-permute-start.19 = (bf16[768,1024]{1,0:T(8,128)(2,1)S(1)}, bf16[768,1024]{1,0:T(8,128)(2,1)S(1)}, u32[]{:S(2)}, u32[]{:S(2)}) collective-permute-start(bf16[768,1024]{1,0:T(8,128)(2,1)S(1)} %total.25.refs_1_.refs_3_.refs_5_), channel_id=1, source_target_pairs={{0,4},{12,8},{2,6},{14,10},{1,5},{13,9},{3,7},{15,11},{16,20},{28,... | collective-permute-start | bytes 4718600 | tf_op jit(solution)/shard_map/ppermute | solution.py:391
  121.0 36.2 %collective-permute-start.21 = (bf16[768,1024]{1,0:T(8,128)(2,1)S(1)}, bf16[768,1024]{1,0:T(8,128)(2,1)S(1)}, u32[]{:S(2)}, u32[]{:S(2)}) collective-permute-start(bf16[768,1024]{1,0:T(8,128)(2,1)S(1)} %total.26.refs_4_), channel_id=1, source_target_pairs={{8,12},{4,0},{10,14},{6,2},{9,13},{5,1},{11,15},{7,3},{24,28},{20,... | collective-permute-start | bytes 4718600 | tf_op jit(solution)/shard_map/ppermute | solution.py:391
  123.0 1.4 collective-permute-start.13
  124.4 23.2 %collective-permute-start.17 = (bf16[384,1024]{1,0:T(8,128)(2,1)S(1)}, bf16[384,1024]{1,0:T(8,128)(2,1)S(1)}, u32[]{:S(2)}, u32[]{:S(2)}) collective-permute-start(bf16[384,1024]{1,0:T(8,128)(2,1)S(1)} %total.28.refs_7_), channel_id=1, source_target_pairs={{4,8},{8,4},{6,10},{10,6},{5,9},{9,5},{7,11},{11,7},{20,24},{24,20... | collective-permute-start | bytes 2359304 | tf_op jit(solution)/shard_map/ppermute | solution.py:391
  125.3 1.4 copy-start.6
  147.1 3.9 %collective-permute-start.18 = (bf16[384,1024]{1,0:T(8,128)(2,1)S(1)}, bf16[384,1024]{1,0:T(8,128)(2,1)S(1)}, u32[]{:S(2)}, u32[]{:S(2)}) collective-permute-start(bf16[384,1024]{1,0:T(8,128)(2,1)S(1)} %get-tuple-element.27), channel_id=1, source_target_pairs={{0,1},{1,0},{2,3},{3,2},{4,5},{5,4},{6,7},{7,6},{8,9},{9,8},{10,11... | collective-permute-start | bytes 2359304 | tf_op jit(solution)/shard_map/ppermute | solution.py:397
  147.1 3.9 %collective-permute-start.20 = (bf16[384,1024]{1,0:T(8,128)(2,1)S(1)}, bf16[384,1024]{1,0:T(8,128)(2,1)S(1)}, u32[]{:S(2)}, u32[]{:S(2)}) collective-permute-start(bf16[384,1024]{1,0:T(8,128)(2,1)S(1)} %get-tuple-element.28), channel_id=1, source_target_pairs={{0,1},{1,0},{2,3},{3,2},{4,5},{5,4},{6,7},{7,6},{8,9},{9,8},{10,11... | collective-permute-start | bytes 2359304 | tf_op jit(solution)/shard_map/ppermute | solution.py:397
